TPU v7x, 32 devices: a whole 2x2x4 slice. The times are simulated.
32 devices in a mesh: groups: 2 (over y), markov: 4 (over z), storage: 2 (over x), sub: 2 (over core).
Axes of the slice: x: 2, y: 2, z: 4, core: 2. Of those that a mesh axis runs over, the one named last changes fastest.
Arguments:
- expected_cot: bfloat16 [8192, 2048], P(('groups', 'markov'), ('storage', 'sub')), parts along dimension 0, may hold values from -192 to 192
- value_next: bfloat16 [8192, 2048], P(('groups', 'markov'), ('storage', 'sub')), parts along dimension 0, may hold values from -0.0024414062 to 0.0024414062
- transition: bfloat16 [8192, 4096], P(('groups', 'storage', 'sub'), 'markov'), parts along dimension 0, may hold values from 6.1035156e-05 to 0.0009765625
- section: int32 [2], P('groups'), parts along dimension 0, may hold values from 0 to 51
Outputs:
- section_adjoint: float32 [8192, 2048], P(('groups', 'markov'), ('storage', 'sub')), parts along dimension 0
- transition_grad: float32 [8192, 4096], P(('groups', 'storage', 'sub'), 'markov'), parts along dimension 0
There are 2 independent parts, one for each index of `groups`. A program takes and returns all parts, laid end to end along the dimension named above; each array names one. Nothing has to cross between parts.
All inputs are finite; a program needn't handle non-finite values.
Results may differ from a plain program's by a relative error of at most 0.0003.
Values may be sent and summed in bfloat16 or wider, within the bound.
No kernel may reach another device: no remote copies, remote signals or barrier semaphores. Data moves between devices by JAX's collectives and lax.ppermute only.
A program may use at most 64 MiB of HBM per device.

v0:
```python
import jax
import jax.numpy as jnp
from jax import lax
from jax.sharding import PartitionSpec as P

discount_rate = 0.97


def shards(expected_cot, value_next, transition, section):
    discount_factor = jnp.exp(section[0].astype(jnp.float32) * jnp.log(jnp.float32(discount_rate)))
    cotangent_all = lax.all_gather(expected_cot, "markov", axis=0, tiled=True)
    adjoint_sum = lax.dot_general(
        lax.all_gather(transition, ("storage", "sub"), axis=0, tiled=True),
        cotangent_all,
        (((0,), (0,)), ((), ())),
        preferred_element_type=jnp.float32,
    )
    own_states = lax.all_to_all(
        cotangent_all, ("storage", "sub"), split_axis=0, concat_axis=1, tiled=True
    )
    gathered_values = lax.all_gather(value_next, ("storage", "sub"), axis=1, tiled=True)
    gradient_sum = lax.dot_general(
        own_states, gathered_values, (((1,), (1,)), ((), ())), preferred_element_type=jnp.float32
    )
    return (discount_factor * adjoint_sum, discount_factor * gradient_sum)


def solution(mesh):
    return jax.shard_map(
        shards,
        mesh=mesh,
        in_specs=(
            P(("groups", "markov"), ("storage", "sub")),
            P(("groups", "markov"), ("storage", "sub")),
            P(("groups", "storage", "sub"), "markov"),
            P("groups"),
        ),
        out_specs=(
            P(("groups", "markov"), ("storage", "sub")),
            P(("groups", "storage", "sub"), "markov"),
        ),
        check_vma=False,
    )
```

profile of v0, /device:TPU:0, one launch (start us, length us, event | category | flops | bytes accessed | tf_op | source)
XLA Modules:
  0.0 232.2 jit_solution(16197326605313307399)
XLA Ops:
  7.2 0.0 all-gather.6.cloned.1.call-start
  7.2 0.7 all-gather.6.cloned.1.call-update
  7.9 0.0 all-gather.8.cloned.1.call-start
  7.9 0.7 all-gather.8.cloned.1.call-update
  8.6 0.0 all-gather.4.cloned.1.call-start
  8.7 0.7 all-gather.4.cloned.1.call-update
  9.4 83.7 %all-gather.6.cloned.1.call-done = bf16[4096,512]{1,0:T(8,128)(2,1)} async-done(((bf16[1024,512]{1,0:T(8,128)(2,1)}), bf16[4096,512]{1,0:T(8,128)(2,1)}) %all-gather.6.cloned.1.call-update) | async-done | bytes 4194320 | tf_op jit(solution)/shard_map/all_gather | solution.py:11
  93.1 4.9 %all-to-all-start = ((bf16[4,1024,512]{2,1,0:T(8,128)(2,1)}), bf16[4,1024,512]{2,1,0:T(8,128)(2,1)}, u32[]{:S(2)}, u32[]{:S(2)}) async-start(bf16[4,1024,512]{2,1,0:T(8,128)(2,1)} %bitcast.8), calls=%async_computation | async-start | bytes 8388608 | tf_op jit(solution)/shard_map/all_to_all | solution.py:18
  98.6 75.5 %all-to-all-done = bf16[4,1024,512]{2,1,0:T(8,128)(2,1)} async-done(((bf16[4,1024,512]{2,1,0:T(8,128)(2,1)}), bf16[4,1024,512]{2,1,0:T(8,128)(2,1)}, u32[]{:S(2)}, u32[]{:S(2)}) %all-to-all-start) | async-done | bytes 4194336 | tf_op jit(solution)/shard_map/all_to_all | solution.py:18
  174.2 6.3 %copy.6 = bf16[1024,4,512]{0,2,1:T(8,128)(2,1)} copy(bf16[1024,4,512]{2,0,1:T(8,128)(2,1)} %bitcast.2) | data formatting | bytes 8388608 | tf_op jit(solution)/shard_map/all_to_all | solution.py:18
  180.5 0.0 all-gather.8.cloned.1.call-done
  180.5 10.0 %convolution_multiply_fusion = f32[1024,1024]{1,0:T(8,128)} fusion(bf16[1024,2048]{0,1:T(8,128)(2,1)} %bitcast.9, bf16[1024,2048]{1,0:T(8,128)(2,1)} %all-gather.8.cloned.1.call-done, f32[]{:T(128)} %bitcast), kind=kOutput, calls=%fused_computation | convolution fusion | flops 4296015872 | bytes 12582916 | tf_op jit(solution)/shard_map/dot_general | solution.py:22
  190.5 24.8 %all-gather.4.cloned.1.call-done = bf16[4096,1024]{1,0:T(8,128)(2,1)} async-done(((bf16[1024,1024]{1,0:T(8,128)(2,1)}), bf16[4096,1024]{1,0:T(8,128)(2,1)}) %all-gather.4.cloned.1.call-update) | async-done | bytes 8388624 | tf_op jit(solution)/shard_map/all_gather | solution.py:13
  215.3 10.4 %convolution_multiply_fusion.1 = f32[1024,512]{1,0:T(8,128)} fusion(bf16[4096,1024]{1,0:T(8,128)(2,1)} %all-gather.4.cloned.1.call-done, bf16[4096,512]{1,0:T(8,128)(2,1)} %all-gather.6.cloned.1.call-done, f32[]{:T(128)} %bitcast), kind=kOutput, calls=%fused_computation.1 | convolution fusion | flops 4295491584 | bytes 14680068 | tf_op jit(solution)/shard_map/dot_general | solution.py:12
Async XLA Ops:
  7.2 85.9 %all-gather.6.cloned.1.call-start = ((), (), s32[]{:S(2)}) async-start(), calls=%async_computation.2 | async-start | bytes 5242880 | tf_op jit(solution)/shard_map/all_gather | solution.py:11
  7.9 172.6 %all-gather.8.cloned.1.call-start = ((), (), s32[]{:S(2)}) async-start(), calls=%async_computation.3 | async-start | bytes 5242880 | tf_op jit(solution)/shard_map/all_gather | solution.py:21
  8.6 206.6 %all-gather.4.cloned.1.call-start = ((), (), s32[]{:S(2)}) async-start(), calls=%async_computation.1 | async-start | bytes 10485760 | tf_op jit(solution)/shard_map/all_gather | solution.py:13
  93.1 81.1 %all-to-all-start = ((bf16[4,1024,512]{2,1,0:T(8,128)(2,1)}), bf16[4,1024,512]{2,1,0:T(8,128)(2,1)}, u32[]{:S(2)}, u32[]{:S(2)}) async-start(bf16[4,1024,512]{2,1,0:T(8,128)(2,1)} %bitcast.8), calls=%async_computation | async-start | bytes 8388608 | tf_op jit(solution)/shard_map/all_to_all | solution.py:18
Sparse Core Ops, SparseCore 0:
  9.6 83.4 all-gather.5
  94.6 55.5 all-gather.7
  151.8 63.4 all-gather.3
where the time goes:
time: 233 us; the launch traced here: 232 us
  waiting for transfers between devices  186 us (80%)
  matrix products  20.4 us (9%)
  between operations  14.4 us (6%)
  local copies, waits for them, and re-layouts  6.34 us (3%)
  starting transfers between devices  4.97 us (2%)
    all_gather x1, waiting for transfers between devices, shards(): cotangent_all = lax.all_gather(expected_cot, 'markov', axis=0, tiled=True)  83.7 us
    all_to_all x1, waiting for transfers between devices, shards(): lax.all_to_all(cotangent_all, ('storage', 'sub'), split_axis=0, concat_ax...  75.5 us
    all_gather x1, waiting for transfers between devices, shards(): lax.all_gather(transition, ('storage', 'sub'), axis=0, tiled=True)  24.8 us
    dot_general x1, matrix products, shards(): lax.dot_general(lax.all_gather(transition, ('storage', 'sub'), axis=0, ti...  10.4 us
    dot_general x1, matrix products, shards(): lax.dot_general(own_states, gathered_values, (((1,), (1,)), ((), ())), pr...  10 us
    all_to_all x1, local copies, waits for them, and re-layouts, shards(): lax.all_to_all(cotangent_all, ('storage', 'sub'), split_axis=0, concat_ax...  6.34 us
    all_to_all x1, starting transfers between devices, shards(): lax.all_to_all(cotangent_all, ('storage', 'sub'), split_axis=0, concat_ax...  4.85 us
  transfers between devices with their start and end apart: 4, of which 3 were waited for; matrix products, arithmetic and copies ran while one was open for 7% of the time, Pallas kernels for 0%

commit v1 on v0

--- a/solution.py
+++ b/solution.py
@@ -4,10 +4,15 @@
 from jax.sharding import PartitionSpec as P
 
 discount_rate = 0.97
+AXES = ("groups", "markov", "storage", "sub")
 
 
-def shards(expected_cot, value_next, transition, section):
-    discount_factor = jnp.exp(section[0].astype(jnp.float32) * jnp.log(jnp.float32(discount_rate)))
+def factor_of(section):
+    return jnp.exp(section[0].astype(jnp.float32) * jnp.log(jnp.float32(discount_rate)))
+
+
+def plain_shards(expected_cot, value_next, transition, section):
+    discount_factor = factor_of(section)
     cotangent_all = lax.all_gather(expected_cot, "markov", axis=0, tiled=True)
     adjoint_sum = lax.dot_general(
         lax.all_gather(transition, ("storage", "sub"), axis=0, tiled=True),
@@ -25,7 +30,109 @@
     return (discount_factor * adjoint_sum, discount_factor * gradient_sum)
 
 
+def tdot(a, b):
+    return lax.dot_general(a, b, (((0,), (0,)), ((), ())), preferred_element_type=jnp.float32)
+
+
+def dott(a, b):
+    return lax.dot_general(a, b, (((1,), (1,)), ((), ())), preferred_element_type=jnp.float32)
+
+
+def two_line_shards(sizes):
+    groups, layers, sides, cores = sizes
+
+    def index(g, z, s, c):
+        return ((g * layers + z) * sides + s) * cores + c
+
+    def level_moves(moves):
+        at = lambda s, level: level if s == 0 else layers - 1 - level
+        return [
+            (index(g, at(s, a), s, c), index(g, at(s, b), s, c))
+            for g in range(groups) for s in range(sides) for c in range(cores) for a, b in moves
+        ]
+
+    cross_pairs = [
+        (index(g, z, s, c), index(g, z, 1 - s, c))
+        for g in range(groups) for z in range(layers) for s in range(sides) for c in range(cores)
+    ]
+    core_pairs = [
+        (index(g, z, s, c), index(g, z, s, 1 - c))
+        for g in range(groups) for z in range(layers) for s in range(sides) for c in range(cores)
+    ]
+
+    def send(array, pairs):
+        return lax.ppermute(array, AXES, pairs)
+
+    def shards(expected_cot, value_next, transition, section):
+        df = factor_of(section)
+        z, s, c = lax.axis_index("markov"), lax.axis_index("storage"), lax.axis_index("sub")
+        level = jnp.where(s == 0, z, layers - 1 - z)
+        first = (c + s) % 2 == 0
+        half = expected_cot.shape[1] // 2
+        ep, eq = expected_cot[:, :half], expected_cot[:, half:]
+        vp, vq = value_next[:, :half], value_next[:, half:]
+        far = level >= 2
+
+        def pick(l0, l1, l2, l3):
+            return jnp.where(level < 2, jnp.where(level == 0, l0, l1), jnp.where(level == 2, l2, l3))
+
+        up = lambda a, *levels: send(a, level_moves([(i, i + 1) for i in levels]))
+        down = lambda a, *levels: send(a, level_moves([(i, i - 1) for i in levels]))
+        cross = lambda a: send(a, cross_pairs)
+        swap = lambda a: send(a, core_pairs)
+
+        t_other = swap(transition)
+        v_other = swap(value_next)
+        x0 = cross(jnp.where(far, ep, vp))
+        u0 = up(ep, 0, 1)
+        d0 = down(eq, 3, 2)
+        x1 = cross(jnp.where(far, eq, vq))
+        u1 = up(jnp.where(level == 2, u0, x0), 0, 1, 2)
+        d1 = down(d0, 2, 1)
+        x2 = cross(jnp.where(far, vp, jnp.where(level == 1, d0, d1)))
+        u2 = up(jnp.where(level == 0, x1, u1), 0, 1, 2)
+        d2 = down(d1, 1)
+        x3 = cross(jnp.where(far, vq, jnp.where(level == 1, d1, d2)))
+        u3 = up(pick(eq, u0, u2, u2), 0, 1, 2)
+        d3 = down(x0, 1)
+        b0p, b1p = pick(x0, u1, u2, u3), pick(d3, x0, u1, u2)
+        bp_own, bp_other = jnp.where(first, b0p, b1p), jnp.where(first, b1p, b0p)
+        part_p = cross(tdot(transition, bp_own) + tdot(t_other, bp_other))
+        u4 = up(jnp.where(level == 1, eq, u3), 1, 2)
+        d4 = down(x1, 1)
+        b0q, b1q = pick(x1, u2, x3, x3), pick(d4, x1, x2, x2)
+        bq_own, bq_other = jnp.where(first, b0q, b1q), jnp.where(first, b1q, b0q)
+        part_q = cross(tdot(transition, bq_own) + tdot(t_other, bq_other))
+        u5 = up(jnp.where(level == 1, u3, u4), 1, 2)
+        d5 = down(expected_cot, 1)
+        u6 = up(u5, 2)
+
+        vfar = jnp.concatenate([jnp.where(far, x0, x2), jnp.where(far, x1, x3)], 1)
+        vfar_other = swap(vfar)
+        bp_swapped, bq_swapped = swap(bp_other), swap(bq_other)
+        b_all = jnp.concatenate([bp_own, bq_own, bp_swapped, bq_swapped], 1)
+        grad = dott(b_all, jnp.concatenate([vfar, vfar_other], 1))
+
+        a0p, a1p = pick(ep, u0, u3, u4), pick(d5[:, :half], ep, u0, u1)
+        ap_own, ap_other = jnp.where(first, a0p, a1p), jnp.where(first, a1p, a0p)
+        a0q, a1q = pick(eq, u3, u5, u6), pick(d5[:, half:], eq, u4, u5)
+        aq_own, aq_other = jnp.where(first, a0q, a1q), jnp.where(first, a1q, a0q)
+        a_own = jnp.concatenate([ap_own, aq_own], 1)
+        a_other = jnp.concatenate([ap_other, aq_other], 1)
+        a_swapped = jnp.concatenate([swap(ap_other), swap(aq_other)], 1)
+        grad = grad + dott(
+            jnp.concatenate([a_own, a_swapped], 1), jnp.concatenate([value_next, v_other], 1)
+        )
+        adjoint = tdot(transition, a_own) + tdot(t_other, a_other)
+        adjoint = adjoint + jnp.concatenate([part_p, part_q], 1)
+        return df * adjoint, df * grad
+
+    return shards
+
+
 def solution(mesh):
+    sizes = tuple(mesh.shape[a] for a in AXES)
+    shards = two_line_shards(sizes) if sizes[1:] == (4, 2, 2) else plain_shards
     return jax.shard_map(
         shards,
         mesh=mesh,

time: 233 us -> 220 us (0.944)
  waiting for transfers between devices: 186 us -> 143 us
  starting transfers between devices: 4.97 us -> 35.2 us
  between operations: 14.4 us -> 1.73 us
  other arithmetic: 0 us -> 10.4 us
  matrix products: 20.4 us -> 23.8 us
    ppermute x0 -> x26, waiting for transfers between devices: none -> 143 us  [send(): return lax.ppermute(array, AXES, pairs)]
    all_gather x3 -> x0, waiting for transfers between devices: 108 us -> none  [the longest x1 83.7 us: shards(): cotangent_all = lax.all_gather(expected_cot, 'markov', axis=0, tiled=True)]
    all_to_all x1 -> x0, waiting for transfers between devices: 75.5 us -> none  [shards(): lax.all_to_all(cotangent_all, ('storage', 'sub'), split_axis=0, concat_ax...]
    ppermute x0 -> x26, starting transfers between devices: none -> 35.2 us  [send(): return lax.ppermute(array, AXES, pairs)]
    select_n x0 -> x12, other arithmetic: none -> 9.37 us  [the longest x1 3.15 us: shards(): ap_own, ap_other = (jnp.where(first, a0p, a1p), jnp.where(first, a1p, a0p))]
    all_to_all x1 -> x0, local copies, waits for them, and re-layouts: 6.34 us -> none  [shards(): lax.all_to_all(cotangent_all, ('storage', 'sub'), split_axis=0, concat_ax...]
    all_to_all x1 -> x0, starting transfers between devices: 4.85 us -> none  [shards(): lax.all_to_all(cotangent_all, ('storage', 'sub'), split_axis=0, concat_ax...]
    unnamed x0 -> x37, local copies, waits for them, and re-layouts: none -> 4.69 us
  transfers between devices with their start and end apart: 4 -> 26, of which waited for: 3 -> 15; matrix products, arithmetic and copies ran while one was open for 7% -> 12% of each run, Pallas kernels for 0% -> 0%
where the time goes in v1:
time: 220 us; the launch traced here: 219 us
  waiting for transfers between devices  143 us (65%)
  starting transfers between devices  35.2 us (16%)
  matrix products  23.8 us (11%)
  other arithmetic  10.4 us (5%)
  local copies, waits for them, and re-layouts  4.69 us (2%)
    ppermute x26, waiting for transfers between devices, send(): return lax.ppermute(array, AXES, pairs)  143 us
    ppermute x26, starting transfers between devices, send(): return lax.ppermute(array, AXES, pairs)  35.2 us
    dot_general x6, matrix products, tdot(): lax.dot_general(a, b, (((0,), (0,)), ((), ())), preferred_element_type=jn...  12.2 us
    dot_general x2, matrix products, dott(): lax.dot_general(a, b, (((1,), (1,)), ((), ())), preferred_element_type=jn...  11.6 us
    unnamed x37, local copies, waits for them, and re-layouts  4.69 us
  transfers between devices with their start and end apart: 26, of which 15 were waited for; matrix products, arithmetic and copies ran while one was open for 12% of the time, Pallas kernels for 0%

profile of v1, /device:TPU:0, one launch (start us, length us, event | category | flops | bytes accessed | tf_op | source)
XLA Modules:
  0.0 219.2 jit_solution(3701995566943312186)
XLA Ops:
  0.6 2.4 %broadcast_select_fusion.4 = (bf16[1024,256]{1,0:T(8,128)(2,1)S(1)}, bf16[1024,256]{1,0:T(8,128)(2,1)}, bf16[1024,256]{1,0:T(8,128)(2,1)S(1)}) fusion(pred[]{:T(512)S(6)} %ge.3, bf16[1024,512]{1,0:T(8,128)(2,1)} %param.5, bf16[1024,512]{1,0:T(8,128)(2,1)} %param.4), kind=kLoop, calls=%fused_computation.56 | loop fusion | flops 524288 | bytes 3670017 | tf_op jit(solution)/shard_map/jit(_where)/select_n | solution.py:86
  3.1 5.1 %collective-permute-start = (bf16[1024,256]{1,0:T(8,128)(2,1)S(1)}, bf16[1024,256]{1,0:T(8,128)(2,1)S(1)}, u32[]{:S(2)}, u32[]{:S(2)}) collective-permute-start(bf16[1024,256]{1,0:T(8,128)(2,1)S(1)} %get-tuple-element.28), channel_id=1, source_target_pairs={{0,4},{4,8},{1,5},{5,9},{14,10},{10,6},{15,11},{11,7},{16,20},{20,... | collective-permute-start | bytes 1572872 | tf_op jit(solution)/shard_map/ppermute | solution.py:64
  8.2 0.1 collective-permute-start.2
  8.2 2.0 collective-permute-start.1
  10.3 9.0 %collective-permute-done = bf16[1024,256]{1,0:T(8,128)(2,1)S(1)} collective-permute-done((bf16[1024,256]{1,0:T(8,128)(2,1)S(1)}, bf16[1024,256]{1,0:T(8,128)(2,1)S(1)}, u32[]{:S(2)}, u32[]{:S(2)}) %collective-permute-start) | collective-permute-done | bytes 524320 | tf_op jit(solution)/shard_map/ppermute | solution.py:64
  19.3 3.9 %collective-permute-done.2 = bf16[1024,256]{1,0:T(8,128)(2,1)} collective-permute-done((bf16[1024,256]{1,0:T(8,128)(2,1)S(1)}, bf16[1024,256]{1,0:T(8,128)(2,1)}, u32[]{:S(2)}, u32[]{:S(2)}) %collective-permute-start.2) | collective-permute-done | bytes 524320 | tf_op jit(solution)/shard_map/ppermute | solution.py:64
  23.2 1.1 broadcast_select_fusion.6
  24.3 3.5 %collective-permute-start.3 = (bf16[1024,256]{1,0:T(8,128)(2,1)S(1)}, bf16[1024,256]{1,0:T(8,128)(2,1)S(1)}, u32[]{:S(2)}, u32[]{:S(2)}) collective-permute-start(bf16[1024,256]{1,0:T(8,128)(2,1)S(1)} %broadcast_select_fusion.6), channel_id=1, source_target_pairs={{0,4},{4,8},{8,12},{1,5},{5,9},{9,13},{14,10},{10,6},{6,2},{15,11}... | collective-permute-start | bytes 1572872 | tf_op jit(solution)/shard_map/ppermute | solution.py:64
  27.8 5.1 %collective-permute-done.1 = bf16[1024,256]{1,0:T(8,128)(2,1)S(1)} collective-permute-done((bf16[1024,256]{1,0:T(8,128)(2,1)}, bf16[1024,256]{1,0:T(8,128)(2,1)S(1)}, u32[]{:S(2)}, u32[]{:S(2)}) %collective-permute-start.1) | collective-permute-done | bytes 524320 | tf_op jit(solution)/shard_map/ppermute | solution.py:64
  32.9 3.4 %collective-permute-done.3 = bf16[1024,256]{1,0:T(8,128)(2,1)S(1)} collective-permute-done((bf16[1024,256]{1,0:T(8,128)(2,1)S(1)}, bf16[1024,256]{1,0:T(8,128)(2,1)S(1)}, u32[]{:S(2)}, u32[]{:S(2)}) %collective-permute-start.3) | collective-permute-done | bytes 524320 | tf_op jit(solution)/shard_map/ppermute | solution.py:64
  36.3 0.8 copy-done.8
  37.1 0.1 broadcast_select_fusion.7
  37.1 4.4 %collective-permute-start.4 = (bf16[1024,256]{1,0:T(8,128)(2,1)S(1)}, bf16[1024,256]{1,0:T(8,128)(2,1)S(1)}, u32[]{:S(2)}, u32[]{:S(2)}) collective-permute-start(bf16[1024,256]{1,0:T(8,128)(2,1)S(1)} %broadcast_select_fusion.7), channel_id=1, source_target_pairs={{0,4},{4,8},{8,12},{1,5},{5,9},{9,13},{14,10},{10,6},{6,2},{15,11}... | collective-permute-start | bytes 1572872 | tf_op jit(solution)/shard_map/ppermute | solution.py:64
  41.5 7.5 %collective-permute-done.4 = bf16[1024,256]{1,0:T(8,128)(2,1)S(1)} collective-permute-done((bf16[1024,256]{1,0:T(8,128)(2,1)S(1)}, bf16[1024,256]{1,0:T(8,128)(2,1)S(1)}, u32[]{:S(2)}, u32[]{:S(2)}) %collective-permute-start.4) | collective-permute-done | bytes 524320 | tf_op jit(solution)/shard_map/ppermute | solution.py:64
  49.1 0.8 copy-done.3
  49.9 0.9 select_select_fusion.8
  50.8 5.3 %collective-permute-start.5 = (bf16[1024,256]{1,0:T(8,128)(2,1)}, bf16[1024,256]{1,0:T(8,128)(2,1)}, u32[]{:S(2)}, u32[]{:S(2)}) collective-permute-start(bf16[1024,256]{1,0:T(8,128)(2,1)} %select_select_fusion.8), channel_id=1, source_target_pairs={{0,4},{4,8},{8,12},{1,5},{5,9},{9,13},{14,10},{10,6},{6,2},{15,11}... | collective-permute-start | bytes 1572872 | tf_op jit(solution)/shard_map/ppermute | solution.py:64
  56.1 6.2 %collective-permute-done.5 = bf16[1024,256]{1,0:T(8,128)(2,1)} collective-permute-done((bf16[1024,256]{1,0:T(8,128)(2,1)}, bf16[1024,256]{1,0:T(8,128)(2,1)}, u32[]{:S(2)}, u32[]{:S(2)}) %collective-permute-start.5) | collective-permute-done | bytes 524320 | tf_op jit(solution)/shard_map/ppermute | solution.py:64
  62.3 1.1 broadcast_select_fusion.1
  63.4 0.7 collective-permute-start.6
  64.1 1.3 collective-permute-start.7
  65.4 0.0 collective-permute-done.6
  65.4 0.1 broadcast_select_fusion
  65.5 1.5 collective-permute-start.8
  67.0 1.3 collective-permute-start.11
  68.3 1.5 collective-permute-start.9
  69.7 0.0 collective-permute-start.10
  69.8 24.1 %collective-permute-done.7 = bf16[1024,512]{1,0:T(8,128)(2,1)} collective-permute-done((bf16[1024,512]{1,0:T(8,128)(2,1)S(1)}, bf16[1024,512]{1,0:T(8,128)(2,1)}, u32[]{:S(2)}, u32[]{:S(2)}) %collective-permute-start.7) | collective-permute-done | bytes 1048608 | tf_op jit(solution)/shard_map/ppermute | solution.py:64
  93.8 5.6 %collective-permute-done.11 = bf16[1024,256]{1,0:T(8,128)(2,1)} collective-permute-done((bf16[1024,256]{1,0:T(8,128)(2,1)}, bf16[1024,256]{1,0:T(8,128)(2,1)}, u32[]{:S(2)}, u32[]{:S(2)}) %collective-permute-start.11) | collective-permute-done | bytes 524320 | tf_op jit(solution)/shard_map/ppermute | solution.py:64
  99.4 3.1 %broadcast_select_fusion.13 = (bf16[1024,256]{1,0:T(8,128)(2,1)S(1)}, bf16[1024,256]{1,0:T(8,128)(2,1)S(1)}, bf16[1024,256]{1,0:T(8,128)(2,1)S(1)}, bf16[1024,25...) fusion(pred[]{:T(512)S(6)} %eq.12, ...), kind=kLoop, calls=%fused_computation.65 | loop fusion | flops 5505024 | bytes 12058628 | tf_op jit(solution)/shard_map/jit(_where)/select_n | solution.py:117
  102.6 0.7 collective-permute-start.13
  103.3 1.3 collective-permute-start.14
  104.6 25.8 %collective-permute-done.14 = bf16[1024,256]{1,0:T(8,128)(2,1)S(1)} collective-permute-done((bf16[1024,256]{1,0:T(8,128)(2,1)S(1)}, bf16[1024,256]{1,0:T(8,128)(2,1)S(1)}, u32[]{:S(2)}, u32[]{:S(2)}) %collective-permute-start.14) | collective-permute-done | bytes 524320 | tf_op jit(solution)/shard_map/ppermute | solution.py:64
  130.4 1.3 collective-permute-start.15
  131.7 0.1 collective-permute-start.25
  132.5 1.3 collective-permute-start.17
  133.8 0.1 broadcast_select_fusion.10
  133.9 11.2 %collective-permute-done.15 = bf16[1024,256]{1,0:T(8,128)(2,1)S(1)} collective-permute-done((bf16[1024,256]{1,0:T(8,128)(2,1)S(1)}, bf16[1024,256]{1,0:T(8,128)(2,1)S(1)}, u32[]{:S(2)}, u32[]{:S(2)}) %collective-permute-start.15) | collective-permute-done | bytes 524320 | tf_op jit(solution)/shard_map/ppermute | solution.py:64
  145.1 0.2 select_select_fusion
  145.3 0.1 collective-permute-start.16
  145.3 2.0 collective-permute-start.18
  147.3 0.0 collective-permute-done.10
  147.3 2.3 %fusion.46 = f32[256,1024]{1,0:T(8,128)S(1)} fusion(bf16[1024,256]{1,0:T(8,128)(2,1)S(1)} %broadcast_select_fusion.10, bf16[1024,1024]{1,0:T(8,128)(2,1)} %collective-permute-done.10), kind=kOutput, calls=%fused_computation.72 | convolution fusion | flops 536870912 | bytes 3670016 | tf_op jit(solution)/shard_map/dot_general | solution.py:34
  149.7 0.7 fusion.26
  150.4 0.1 collective-permute-start.12
  150.6 2.1 collective-permute-done.17
  152.7 7.5 %collective-permute-done.16 = bf16[1024,256]{1,0:T(8,128)(2,1)S(1)} collective-permute-done((bf16[1024,256]{1,0:T(8,128)(2,1)S(1)}, bf16[1024,256]{1,0:T(8,128)(2,1)S(1)}, u32[]{:S(2)}, u32[]{:S(2)}) %collective-permute-start.16) | collective-permute-done | bytes 524320 | tf_op jit(solution)/shard_map/ppermute | solution.py:64
  160.2 11.2 %collective-permute-done.18 = bf16[1024,256]{1,0:T(8,128)(2,1)S(1)} collective-permute-done((bf16[1024,256]{1,0:T(8,128)(2,1)S(1)}, bf16[1024,256]{1,0:T(8,128)(2,1)S(1)}, u32[]{:S(2)}, u32[]{:S(2)}) %collective-permute-start.18) | collective-permute-done | bytes 524320 | tf_op jit(solution)/shard_map/ppermute | solution.py:64
  171.4 0.2 broadcast_select_fusion.9
  171.7 0.1 broadcast_select_fusion.8
  171.7 2.8 %fusion.47 = f32[256,1024]{1,0:T(8,128)S(1)} fusion(bf16[1024,256]{1,0:T(8,128)(2,1)S(1)} %broadcast_select_fusion.8, bf16[1024,1024]{1,0:T(8,128)(2,1)} %collective-permute-done.10), kind=kOutput, calls=%fused_computation.73 | convolution fusion | flops 536870912 | bytes 3670016 | tf_op jit(solution)/shard_map/dot_general | solution.py:34
  174.6 0.7 fusion.25
  175.3 1.1 collective-permute-start.19
  176.4 0.1 broadcast_select_fusion.14
  176.5 1.0 pad_maximum_fusion
  177.6 1.3 fusion.31
  178.9 0.6 collective-permute-start.20
  179.4 0.1 collective-permute-start.21
  179.5 4.4 %fusion.14 = f32[1024,1024]{1,0:T(8,128)} fusion(bf16[1024,256]{1,0:T(8,128)(2,1)S(1)} %collective-permute-done.24, bf16[1024,256]{1,0:T(8,128)(2,1)S(1)} %collective-permute-done.23, bf16[1024,256]{1,0:T(8,128)(2,1)S(1)} %get-tuple-element.30, bf16[1024,256]{1,0:T(8,128)(2,1)S(1)} %get-tuple-element.31, bf16[1024,512]{1,0:T(8,128)(2,1)S(1)} %collective-permute-done.25, ...), kind=kOutput, calls=%fused_computation.16 | convolution fusion | flops 2160066560 | bytes 8388608 | tf_op jit(solution)/shard_map/dot_general | solution.py:38
  183.9 9.5 %collective-permute-done.12 = f32[1024,256]{0,1:T(8,128)S(1)} collective-permute-done((f32[1024,256]{0,1:T(8,128)S(1)}, f32[1024,256]{0,1:T(8,128)S(1)}, u32[]{:S(2)}, u32[]{:S(2)}) %collective-permute-start.12) | collective-permute-done | bytes 1048608 | tf_op jit(solution)/shard_map/ppermute | solution.py:64
  193.4 11.2 %collective-permute-done.19 = f32[1024,256]{0,1:T(8,128)S(1)} collective-permute-done((f32[1024,256]{0,1:T(8,128)S(1)}, f32[1024,256]{0,1:T(8,128)S(1)}, u32[]{:S(2)}, u32[]{:S(2)}) %collective-permute-start.19) | collective-permute-done | bytes 1048608 | tf_op jit(solution)/shard_map/ppermute | solution.py:64
  204.6 4.3 %fusion = f32[1024,512]{0,1:T(8,128)} fusion(f32[1024,256]{0,1:T(8,128)S(1)} %collective-permute-done.19, f32[1024,256]{0,1:T(8,128)S(1)} %collective-permute-done.12, f32[512,1024]{1,0:T(8,128)S(1)} %fusion.31, bf16[1024,1024]{1,0:T(8,128)(2,1)} %collective-permute-done.10, bf16[1024,256]{1,0:T(8,128)(2,1)S(1)} %get-tuple-element.16, ...), kind=kOutput, calls=%fused_computation.2 | convolution fusion | flops 1077936128 | bytes 9437188 | tf_op jit(solution)/shard_map/dot_general | solution.py:34
  208.9 3.0 %copy.6 = f32[1024,512]{1,0:T(8,128)} copy(f32[1024,512]{0,1:T(8,128)} %fusion) | data formatting | bytes 4194304
  212.0 7.2 %add_multiply_fusion = f32[1024,1024]{1,0:T(8,128)} fusion(f32[1024,1024]{1,0:T(8,128)} %fusion.14, f32[]{:T(128)} %bitcast, bf16[1024,512]{1,0:T(8,128)(2,1)} %collective-permute-done.22, bf16[1024,256]{1,0:T(8,128)(2,1)S(1)} %copy-done.15, bf16[1024,256]{1,0:T(8,128)(2,1)S(1)} %copy-done.17, bf16[1024,256]{1,0:T(8,128)(2,1)} %collective-permute-done.21, ...), kind=kOutput, calls=%fused_computation | convolution fusion | flops 2164260864 | bytes 12582916 | tf_op jit(solution)/shard_map/dot_general | solution.py:38
  (46 shorter events, 0.1 us)
Async XLA Ops:
  3.1 46.8 %copy-start.1 = (bf16[1024,512]{1,0:T(8,128)(2,1)S(1)}, bf16[1024,512]{1,0:T(8,128)(2,1)}, u32[]{:S(2)}) copy-start(bf16[1024,512]{1,0:T(8,128)(2,1)} %param.4) | copy-start | bytes 3145732
  3.1 16.2 %collective-permute-start = (bf16[1024,256]{1,0:T(8,128)(2,1)S(1)}, bf16[1024,256]{1,0:T(8,128)(2,1)S(1)}, u32[]{:S(2)}, u32[]{:S(2)}) collective-permute-start(bf16[1024,256]{1,0:T(8,128)(2,1)S(1)} %get-tuple-element.28), channel_id=1, source_target_pairs={{0,4},{4,8},{1,5},{5,9},{14,10},{10,6},{15,11},{11,7},{16,20},{20,... | collective-permute-start | bytes 1572872 | tf_op jit(solution)/shard_map/ppermute | solution.py:64
  8.2 15.0 %collective-permute-start.2 = (bf16[1024,256]{1,0:T(8,128)(2,1)S(1)}, bf16[1024,256]{1,0:T(8,128)(2,1)}, u32[]{:S(2)}, u32[]{:S(2)}) collective-permute-start(bf16[1024,256]{1,0:T(8,128)(2,1)S(1)} %get-tuple-element.19), channel_id=1, source_target_pairs={{0,2},{1,3},{2,0},{3,1},{4,6},{5,7},{6,4},{7,5},{8,10},{9,11},{10,... | collective-permute-start | bytes 1572872 | tf_op jit(solution)/shard_map/ppermute | solution.py:64
  8.2 24.6 %collective-permute-start.1 = (bf16[1024,256]{1,0:T(8,128)(2,1)}, bf16[1024,256]{1,0:T(8,128)(2,1)S(1)}, u32[]{:S(2)}, u32[]{:S(2)}) collective-permute-start(bf16[1024,256]{1,0:T(8,128)(2,1)} %get-tuple-element.20), channel_id=1, source_target_pairs={{0,2},{1,3},{2,0},{3,1},{4,6},{5,7},{6,4},{7,5},{8,10},{9,11},{10,... | collective-permute-start | bytes 1572872 | tf_op jit(solution)/shard_map/ppermute | solution.py:64
  19.3 29.8 %copy-start.2 = (bf16[1024,256]{1,0:T(8,128)(2,1)}, bf16[1024,256]{1,0:T(8,128)(2,1)S(1)}, u32[]{:S(2)}) copy-start(bf16[1024,256]{1,0:T(8,128)(2,1)S(1)} %collective-permute-done) | copy-start | bytes 1572868
  24.3 12.0 %collective-permute-start.3 = (bf16[1024,256]{1,0:T(8,128)(2,1)S(1)}, bf16[1024,256]{1,0:T(8,128)(2,1)S(1)}, u32[]{:S(2)}, u32[]{:S(2)}) collective-permute-start(bf16[1024,256]{1,0:T(8,128)(2,1)S(1)} %broadcast_select_fusion.6), channel_id=1, source_target_pairs={{0,4},{4,8},{8,12},{1,5},{5,9},{9,13},{14,10},{10,6},{6,2},{15,11}... | collective-permute-start | bytes 1572872 | tf_op jit(solution)/shard_map/ppermute | solution.py:64
  32.9 16.2 %copy-start.12 = (bf16[1024,256]{1,0:T(8,128)(2,1)}, bf16[1024,256]{1,0:T(8,128)(2,1)S(1)}, u32[]{:S(2)}) copy-start(bf16[1024,256]{1,0:T(8,128)(2,1)S(1)} %collective-permute-done.1) | copy-start | bytes 1572868
  36.3 0.8 copy-start.8
  37.1 12.0 %collective-permute-start.4 = (bf16[1024,256]{1,0:T(8,128)(2,1)S(1)}, bf16[1024,256]{1,0:T(8,128)(2,1)S(1)}, u32[]{:S(2)}, u32[]{:S(2)}) collective-permute-start(bf16[1024,256]{1,0:T(8,128)(2,1)S(1)} %broadcast_select_fusion.7), channel_id=1, source_target_pairs={{0,4},{4,8},{8,12},{1,5},{5,9},{9,13},{14,10},{10,6},{6,2},{15,11}... | collective-permute-start | bytes 1572872 | tf_op jit(solution)/shard_map/ppermute | solution.py:64
  49.1 0.8 copy-start.3
  50.8 19.0 %copy-start = (bf16[1024,1024]{1,0:T(8,128)(2,1)S(1)}, bf16[1024,1024]{1,0:T(8,128)(2,1)}, u32[]{:S(2)}) copy-start(bf16[1024,1024]{1,0:T(8,128)(2,1)} %param.6) | copy-start | bytes 6291460
  50.8 11.5 %collective-permute-start.5 = (bf16[1024,256]{1,0:T(8,128)(2,1)}, bf16[1024,256]{1,0:T(8,128)(2,1)}, u32[]{:S(2)}, u32[]{:S(2)}) collective-permute-start(bf16[1024,256]{1,0:T(8,128)(2,1)} %select_select_fusion.8), channel_id=1, source_target_pairs={{0,4},{4,8},{8,12},{1,5},{5,9},{9,13},{14,10},{10,6},{6,2},{15,11}... | collective-permute-start | bytes 1572872 | tf_op jit(solution)/shard_map/ppermute | solution.py:64
  63.4 2.0 collective-permute-start.6
  64.1 29.7 %collective-permute-start.7 = (bf16[1024,512]{1,0:T(8,128)(2,1)S(1)}, bf16[1024,512]{1,0:T(8,128)(2,1)}, u32[]{:S(2)}, u32[]{:S(2)}) collective-permute-start(bf16[1024,512]{1,0:T(8,128)(2,1)S(1)} %copy-done.1), channel_id=1, source_target_pairs={{4,0},{5,1},{10,14},{11,15},{20,16},{21,17},{26,30},{27,31}} | collective-permute-start | bytes 3145736 | tf_op jit(solution)/shard_map/ppermute | solution.py:64
  65.4 2.9 %copy-start.9 = (bf16[1024,256]{1,0:T(8,128)(2,1)}, bf16[1024,256]{1,0:T(8,128)(2,1)S(1)}, u32[]{:S(2)}) copy-start(bf16[1024,256]{1,0:T(8,128)(2,1)S(1)} %collective-permute-done.6) | copy-start | bytes 1572868
  65.5 2.8 %collective-permute-start.8 = (bf16[1024,256]{1,0:T(8,128)(2,1)S(1)}, bf16[1024,256]{1,0:T(8,128)(2,1)}, u32[]{:S(2)}, u32[]{:S(2)}) collective-permute-start(bf16[1024,256]{1,0:T(8,128)(2,1)S(1)} %broadcast_select_fusion), channel_id=1, source_target_pairs={{4,8},{8,12},{5,9},{9,13},{10,6},{6,2},{11,7},{7,3},{20,24},{24,28... | collective-permute-start | bytes 1572872 | tf_op jit(solution)/shard_map/ppermute | solution.py:64
  67.0 32.5 %collective-permute-start.11 = (bf16[1024,256]{1,0:T(8,128)(2,1)}, bf16[1024,256]{1,0:T(8,128)(2,1)}, u32[]{:S(2)}, u32[]{:S(2)}) collective-permute-start(bf16[1024,256]{1,0:T(8,128)(2,1)} %collective-permute-done.2), channel_id=1, source_target_pairs={{4,0},{5,1},{10,14},{11,15},{20,16},{21,17},{26,30},{27,31}} | collective-permute-start | bytes 1572872 | tf_op jit(solution)/shard_map/ppermute | solution.py:64
  68.3 31.2 %collective-permute-start.9 = (bf16[1024,256]{1,0:T(8,128)(2,1)}, bf16[1024,256]{1,0:T(8,128)(2,1)}, u32[]{:S(2)}, u32[]{:S(2)}) collective-permute-start(bf16[1024,256]{1,0:T(8,128)(2,1)} %collective-permute-done.8), channel_id=1, source_target_pairs={{8,12},{9,13},{6,2},{7,3},{24,28},{25,29},{22,18},{23,19}} | collective-permute-start | bytes 1572872 | tf_op jit(solution)/shard_map/ppermute | solution.py:64
  69.7 77.6 %collective-permute-start.10 = (bf16[1024,1024]{1,0:T(8,128)(2,1)S(1)}, bf16[1024,1024]{1,0:T(8,128)(2,1)}, u32[]{:S(2)}, u32[]{:S(2)}) collective-permute-start(bf16[1024,1024]{1,0:T(8,128)(2,1)S(1)} %copy-done), channel_id=1, source_target_pairs={{0,1},{1,0},{2,3},{3,2},{4,5},{5,4},{6,7},{7,6},{8,9},{9,8},{10,11... | collective-permute-start | bytes 6291464 | tf_op jit(solution)/shard_map/ppermute | solution.py:64
  69.7 62.0 %copy-start.5 = (bf16[1024,512]{1,0:T(8,128)(2,1)S(1)}, bf16[1024,512]{1,0:T(8,128)(2,1)}, u32[]{:S(2)}) copy-start(bf16[1024,512]{1,0:T(8,128)(2,1)} %param.5) | copy-start | bytes 3145732
  69.7 62.7 %copy-start.13 = (bf16[1024,256]{1,0:T(8,128)(2,1)S(1)}, bf16[1024,256]{1,0:T(8,128)(2,1)}, u32[]{:S(2)}) copy-start(bf16[1024,256]{1,0:T(8,128)(2,1)} %copy-done.12) | copy-start | bytes 1572868
  102.6 47.1 %copy-start.6 = (bf16[1024,256]{1,0:T(8,128)(2,1)}, bf16[1024,256]{1,0:T(8,128)(2,1)S(1)}, u32[]{:S(2)}) copy-start(bf16[1024,256]{1,0:T(8,128)(2,1)S(1)} %get-tuple-element.25) | copy-start | bytes 1572868
  102.6 0.7 collective-permute-start.13
  103.3 27.1 %collective-permute-start.14 = (bf16[1024,256]{1,0:T(8,128)(2,1)S(1)}, bf16[1024,256]{1,0:T(8,128)(2,1)S(1)}, u32[]{:S(2)}, u32[]{:S(2)}) collective-permute-start(bf16[1024,256]{1,0:T(8,128)(2,1)S(1)} %collective-permute-done.13), channel_id=1, source_target_pairs={{8,4},{4,0},{9,5},{5,1},{6,10},{10,14},{7,11},{11,15},{24,20},{20,... | collective-permute-start | bytes 1572872 | tf_op jit(solution)/shard_map/ppermute | solution.py:64
  130.4 14.7 %collective-permute-start.15 = (bf16[1024,256]{1,0:T(8,128)(2,1)S(1)}, bf16[1024,256]{1,0:T(8,128)(2,1)S(1)}, u32[]{:S(2)}, u32[]{:S(2)}) collective-permute-start(bf16[1024,256]{1,0:T(8,128)(2,1)S(1)} %collective-permute-done.14), channel_id=1, source_target_pairs={{4,0},{5,1},{10,14},{11,15},{20,16},{21,17},{26,30},{27,31}} | collective-permute-start | bytes 1572872 | tf_op jit(solution)/shard_map/ppermute | solution.py:64
  131.7 45.9 %collective-permute-start.25 = (bf16[1024,512]{1,0:T(8,128)(2,1)S(1)}, bf16[1024,512]{1,0:T(8,128)(2,1)S(1)}, u32[]{:S(2)}, u32[]{:S(2)}) collective-permute-start(bf16[1024,512]{1,0:T(8,128)(2,1)S(1)} %copy-done.5), channel_id=1, source_target_pairs={{0,1},{1,0},{2,3},{3,2},{4,5},{5,4},{6,7},{7,6},{8,9},{9,8},{10,11... | collective-permute-start | bytes 3145736 | tf_op jit(solution)/shard_map/ppermute | solution.py:64
  132.5 20.2 %collective-permute-start.17 = (bf16[1024,256]{1,0:T(8,128)(2,1)S(1)}, bf16[1024,256]{1,0:T(8,128)(2,1)S(1)}, u32[]{:S(2)}, u32[]{:S(2)}) collective-permute-start(bf16[1024,256]{1,0:T(8,128)(2,1)S(1)} %copy-done.13), channel_id=1, source_target_pairs={{4,0},{5,1},{10,14},{11,15},{20,16},{21,17},{26,30},{27,31}} | collective-permute-start | bytes 1572872 | tf_op jit(solution)/shard_map/ppermute | solution.py:64
  145.3 14.9 %collective-permute-start.16 = (bf16[1024,256]{1,0:T(8,128)(2,1)S(1)}, bf16[1024,256]{1,0:T(8,128)(2,1)S(1)}, u32[]{:S(2)}, u32[]{:S(2)}) collective-permute-start(bf16[1024,256]{1,0:T(8,128)(2,1)S(1)} %get-tuple-element.22), channel_id=1, source_target_pairs={{0,2},{1,3},{2,0},{3,1},{4,6},{5,7},{6,4},{7,5},{8,10},{9,11},{10,... | collective-permute-start | bytes 1572872 | tf_op jit(solution)/shard_map/ppermute | solution.py:64
  145.3 26.1 %collective-permute-start.18 = (bf16[1024,256]{1,0:T(8,128)(2,1)S(1)}, bf16[1024,256]{1,0:T(8,128)(2,1)S(1)}, u32[]{:S(2)}, u32[]{:S(2)}) collective-permute-start(bf16[1024,256]{1,0:T(8,128)(2,1)S(1)} %get-tuple-element.21), channel_id=1, source_target_pairs={{0,2},{1,3},{2,0},{3,1},{4,6},{5,7},{6,4},{7,5},{8,10},{9,11},{10,... | collective-permute-start | bytes 1572872 | tf_op jit(solution)/shard_map/ppermute | solution.py:64
  149.7 21.7 %copy-start.4 = (bf16[1024,256]{1,0:T(8,128)(2,1)S(1)}, bf16[1024,256]{1,0:T(8,128)(2,1)}, u32[]{:S(2)}) copy-start(bf16[1024,256]{1,0:T(8,128)(2,1)} %copy-done.3) | copy-start | bytes 1572868
  150.4 42.9 %collective-permute-start.12 = (f32[1024,256]{0,1:T(8,128)S(1)}, f32[1024,256]{0,1:T(8,128)S(1)}, u32[]{:S(2)}, u32[]{:S(2)}) collective-permute-start(f32[1024,256]{0,1:T(8,128)S(1)} %fusion.26), channel_id=1, source_target_pairs={{0,2},{1,3},{2,0},{3,1},{4,6},{5,7},{6,4},{7,5},{8,10},{9,11},{10,... | collective-permute-start | bytes 3145736 | tf_op jit(solution)/shard_map/ppermute | solution.py:64
  152.7 26.2 %collective-permute-start.24 = (bf16[1024,256]{1,0:T(8,128)(2,1)S(1)}, bf16[1024,256]{1,0:T(8,128)(2,1)S(1)}, u32[]{:S(2)}, u32[]{:S(2)}) collective-permute-start(bf16[1024,256]{1,0:T(8,128)(2,1)S(1)} %get-tuple-element.16), channel_id=1, source_target_pairs={{0,1},{1,0},{2,3},{3,2},{4,5},{5,4},{6,7},{7,6},{8,9},{9,8},{10,11... | collective-permute-start | bytes 1572872 | tf_op jit(solution)/shard_map/ppermute | solution.py:64
  160.2 19.3 %collective-permute-start.23 = (bf16[1024,256]{1,0:T(8,128)(2,1)S(1)}, bf16[1024,256]{1,0:T(8,128)(2,1)S(1)}, u32[]{:S(2)}, u32[]{:S(2)}) collective-permute-start(bf16[1024,256]{1,0:T(8,128)(2,1)S(1)} %get-tuple-element.4), channel_id=1, source_target_pairs={{0,1},{1,0},{2,3},{3,2},{4,5},{5,4},{6,7},{7,6},{8,9},{9,8},{10,11... | collective-permute-start | bytes 1572872 | tf_op jit(solution)/shard_map/ppermute | solution.py:64
  171.6 2.9 %copy-start.10 = (bf16[1024,256]{1,0:T(8,128)(2,1)}, bf16[1024,256]{1,0:T(8,128)(2,1)S(1)}, u32[]{:S(2)}) copy-start(bf16[1024,256]{1,0:T(8,128)(2,1)S(1)} %get-tuple-element.13) | copy-start | bytes 1572868
  171.7 4.9 %copy-start.14 = (bf16[1024,256]{1,0:T(8,128)(2,1)}, bf16[1024,256]{1,0:T(8,128)(2,1)S(1)}, u32[]{:S(2)}) copy-start(bf16[1024,256]{1,0:T(8,128)(2,1)S(1)} %get-tuple-element.23) | copy-start | bytes 1572868
  171.7 4.9 %copy-start.16 = (bf16[1024,256]{1,0:T(8,128)(2,1)}, bf16[1024,256]{1,0:T(8,128)(2,1)S(1)}, u32[]{:S(2)}) copy-start(bf16[1024,256]{1,0:T(8,128)(2,1)S(1)} %get-tuple-element.29) | copy-start | bytes 1572868
  175.3 29.3 %collective-permute-start.19 = (f32[1024,256]{0,1:T(8,128)S(1)}, f32[1024,256]{0,1:T(8,128)S(1)}, u32[]{:S(2)}, u32[]{:S(2)}) collective-permute-start(f32[1024,256]{0,1:T(8,128)S(1)} %fusion.25), channel_id=1, source_target_pairs={{0,2},{1,3},{2,0},{3,1},{4,6},{5,7},{6,4},{7,5},{8,10},{9,11},{10,... | collective-permute-start | bytes 3145736 | tf_op jit(solution)/shard_map/ppermute | solution.py:64
  177.6 34.4 %collective-permute-start.22 = (bf16[1024,512]{1,0:T(8,128)(2,1)}, bf16[1024,512]{1,0:T(8,128)(2,1)}, u32[]{:S(2)}, u32[]{:S(2)}) collective-permute-start(bf16[1024,512]{1,0:T(8,128)(2,1)} %pad_maximum_fusion), channel_id=1, source_target_pairs={{0,1},{1,0},{2,3},{3,2},{4,5},{5,4},{6,7},{7,6},{8,9},{9,8},{10,11... | collective-permute-start | bytes 3145736 | tf_op jit(solution)/shard_map/ppermute | solution.py:64
  178.9 33.1 %collective-permute-start.20 = (bf16[1024,256]{1,0:T(8,128)(2,1)S(1)}, bf16[1024,256]{1,0:T(8,128)(2,1)}, u32[]{:S(2)}, u32[]{:S(2)}) collective-permute-start(bf16[1024,256]{1,0:T(8,128)(2,1)S(1)} %broadcast_select_fusion.10), channel_id=1, source_target_pairs={{0,1},{1,0},{2,3},{3,2},{4,5},{5,4},{6,7},{7,6},{8,9},{9,8},{10,11... | collective-permute-start | bytes 1572872 | tf_op jit(solution)/shard_map/ppermute | solution.py:64
  179.4 32.5 %collective-permute-start.21 = (bf16[1024,256]{1,0:T(8,128)(2,1)S(1)}, bf16[1024,256]{1,0:T(8,128)(2,1)}, u32[]{:S(2)}, u32[]{:S(2)}) collective-permute-start(bf16[1024,256]{1,0:T(8,128)(2,1)S(1)} %broadcast_select_fusion.8), channel_id=1, source_target_pairs={{0,1},{1,0},{2,3},{3,2},{4,5},{5,4},{6,7},{7,6},{8,9},{9,8},{10,11... | collective-permute-start | bytes 1572872 | tf_op jit(solution)/shard_map/ppermute | solution.py:64
  208.9 3.1 %copy-start.7 = (bf16[1024,256]{1,0:T(8,128)(2,1)S(1)}, bf16[1024,256]{1,0:T(8,128)(2,1)}, u32[]{:S(2)}) copy-start(bf16[1024,256]{1,0:T(8,128)(2,1)} %copy-done.6) | copy-start | bytes 1572868
  208.9 3.1 %copy-start.11 = (bf16[1024,256]{1,0:T(8,128)(2,1)S(1)}, bf16[1024,256]{1,0:T(8,128)(2,1)}, u32[]{:S(2)}) copy-start(bf16[1024,256]{1,0:T(8,128)(2,1)} %copy-done.10) | copy-start | bytes 1572868
  208.9 3.1 %copy-start.15 = (bf16[1024,256]{1,0:T(8,128)(2,1)S(1)}, bf16[1024,256]{1,0:T(8,128)(2,1)}, u32[]{:S(2)}) copy-start(bf16[1024,256]{1,0:T(8,128)(2,1)} %copy-done.14) | copy-start | bytes 1572868
  208.9 3.1 %copy-start.17 = (bf16[1024,256]{1,0:T(8,128)(2,1)S(1)}, bf16[1024,256]{1,0:T(8,128)(2,1)}, u32[]{:S(2)}) copy-start(bf16[1024,256]{1,0:T(8,128)(2,1)} %copy-done.16) | copy-start | bytes 1572868

commit v2 on v0

--- a/solution.py
+++ b/solution.py
@@ -4,10 +4,15 @@
 from jax.sharding import PartitionSpec as P
 
 discount_rate = 0.97
+AXES = ("groups", "markov", "storage", "sub")
 
 
-def shards(expected_cot, value_next, transition, section):
-    discount_factor = jnp.exp(section[0].astype(jnp.float32) * jnp.log(jnp.float32(discount_rate)))
+def factor_of(section):
+    return jnp.exp(section[0].astype(jnp.float32) * jnp.log(jnp.float32(discount_rate)))
+
+
+def plain_shards(expected_cot, value_next, transition, section):
+    discount_factor = factor_of(section)
     cotangent_all = lax.all_gather(expected_cot, "markov", axis=0, tiled=True)
     adjoint_sum = lax.dot_general(
         lax.all_gather(transition, ("storage", "sub"), axis=0, tiled=True),
@@ -25,7 +30,116 @@
     return (discount_factor * adjoint_sum, discount_factor * gradient_sum)
 
 
+def tdot(a, b):
+    return lax.dot_general(a, b, (((0,), (0,)), ((), ())), preferred_element_type=jnp.float32)
+
+
+def dott(a, b):
+    return lax.dot_general(a, b, (((1,), (1,)), ((), ())), preferred_element_type=jnp.float32)
+
+
+def after(array, *others):
+    return lax.optimization_barrier((array,) + others)[0]
+
+
+def two_side_shards(sizes):
+    groups, layers, sides, cores = sizes
+    places = [(g, z, s, c) for g in range(groups) for z in range(layers) for s in range(sides) for c in range(cores)]
+    index = {place: i for i, place in enumerate(places)}
+
+    def pairs(move, chosen=lambda g, z, s, c: True):
+        return [(index[p], index[move(*p)]) for p in places if chosen(*p)]
+
+    def is_home(g, z, s, c):
+        return z // 2 == s
+
+    def is_away(g, z, s, c):
+        return z // 2 != s
+
+    def jumped(g, z, s, c):
+        return (g, z ^ 2, s, c)
+
+    cross_pairs = pairs(lambda g, z, s, c: (g, z, 1 - s, c))
+    step_pairs = pairs(lambda g, z, s, c: (g, z ^ 1, s, c))
+    core_pairs = pairs(lambda g, z, s, c: (g, z, s, 1 - c))
+    home_jump_pairs, away_jump_pairs = pairs(jumped, is_home), pairs(jumped, is_away)
+
+    def cross(a):
+        return lax.ppermute(a, AXES, cross_pairs)
+
+    def step(a):
+        return lax.ppermute(a, AXES, step_pairs)
+
+    def swap(a):
+        return lax.ppermute(a, AXES, core_pairs)
+
+    def home_jump(a):
+        return lax.ppermute(a, AXES, home_jump_pairs)
+
+    def away_jump(a):
+        return lax.ppermute(a, AXES, away_jump_pairs)
+
+    def shards(expected_cot, value_next, transition, section):
+        df = factor_of(section)
+        z, s, c = lax.axis_index("markov"), lax.axis_index("storage"), lax.axis_index("sub")
+        home = z // 2 == s
+        mine = z % 2 == c
+        half = expected_cot.shape[1] // 2
+        ep, eq = expected_cot[:, :half], expected_cot[:, half:]
+        vp, vq = value_next[:, :half], value_next[:, half:]
+
+        x1 = cross(jnp.where(home, vp, ep))
+        jq = away_jump(eq)
+        t_other = swap(transition)
+        v_other = swap(value_next)
+        t_near, t_next = jnp.where(mine, transition, t_other), jnp.where(mine, t_other, transition)
+
+        def adjoint_of(near, far):
+            return tdot(t_near, near) + tdot(t_next, far)
+
+        def own_and_swapped(near, far):
+            return jnp.where(mine, near, far), swap(jnp.where(mine, far, near))
+
+        x2 = cross(after(jnp.where(home, vq, vp), x1))
+        jp = home_jump(x1)
+        x3 = cross(after(jnp.where(home, jq, vq), x2))
+        jq2 = away_jump(x3)
+        bp = jnp.where(home, x1, jp)
+        bp_next = step(bp)
+        jap = home_jump(after(ep, jp))
+        part_p = cross(adjoint_of(bp, bp_next))
+        bq = jnp.where(home, jq2, x3)
+        bq_next = step(after(bq, bp_next))
+        part_q = cross(adjoint_of(bq, bq_next))
+        ap = jnp.where(home, ep, jap)
+        ap_next = step(after(ap, bq_next))
+        jaq = home_jump(after(eq, jap))
+        aq = jnp.where(home, eq, jaq)
+        aq_next = step(after(aq, ap_next))
+
+        v_across = jnp.concatenate([jnp.where(home, x2, x1), jnp.where(home, x3, x2)], 1)
+        v_across_other = swap(v_across)
+        bp_own, bp_swapped = own_and_swapped(bp, bp_next)
+        bq_own, bq_swapped = own_and_swapped(bq, bq_next)
+        grad = dott(
+            jnp.concatenate([bp_own, bq_own, bp_swapped, bq_swapped], 1),
+            jnp.concatenate([v_across, v_across_other], 1),
+        )
+        ap_own, ap_swapped = own_and_swapped(ap, ap_next)
+        aq_own, aq_swapped = own_and_swapped(aq, aq_next)
+        grad = grad + dott(
+            jnp.concatenate([ap_own, aq_own, ap_swapped, aq_swapped], 1),
+            jnp.concatenate([value_next, v_other], 1),
+        )
+        adjoint = jnp.concatenate([adjoint_of(ap, ap_next) + part_p, adjoint_of(aq, aq_next) + part_q], 1)
+        return df * adjoint, df * grad
+
+    return shards
+
+
 def solution(mesh):
+    sizes = tuple(mesh.shape[a] for a in AXES)
+    shards = two_side_shards(sizes) if sizes[1:] == (4, 2, 2) else plain_shards
     return jax.shard_map(
         shards,
         mesh=mesh,

time: 233 us -> 198 us (0.85)
  waiting for transfers between devices: 186 us -> 92.5 us
  starting transfers between devices: 4.97 us -> 71.3 us
  between operations: 14.4 us -> 1.66 us
  other arithmetic: 0 us -> 11.1 us
  matrix products: 20.4 us -> 16.6 us
    all_gather x3 -> x0, waiting for transfers between devices: 108 us -> none  [the longest x1 83.7 us: shards(): cotangent_all = lax.all_gather(expected_cot, 'markov', axis=0, tiled=True)]
    ppermute x0 -> x21, waiting for transfers between devices: none -> 92.5 us  [the longest x5 48.4 us: cross(): return lax.ppermute(a, AXES, cross_pairs)]
    all_to_all x1 -> x0, waiting for transfers between devices: 75.5 us -> none  [shards(): lax.all_to_all(cotangent_all, ('storage', 'sub'), split_axis=0, concat_ax...]
    ppermute x0 -> x21, starting transfers between devices: none -> 71.3 us  [the longest x4 37.8 us: step(): return lax.ppermute(a, AXES, step_pairs)]
    select_n x0 -> x8, other arithmetic: none -> 9.59 us  [the longest x4 4.45 us: own_and_swapped(): return (jnp.where(mine, near, far), swap(jnp.where(mine, far, near)))]
    all_to_all x1 -> x0, local copies, waits for them, and re-layouts: 6.34 us -> none  [shards(): lax.all_to_all(cotangent_all, ('storage', 'sub'), split_axis=0, concat_ax...]
    all_to_all x1 -> x0, starting transfers between devices: 4.85 us -> none  [shards(): lax.all_to_all(cotangent_all, ('storage', 'sub'), split_axis=0, concat_ax...]
    dot_general x2 -> x10, matrix products: 20.4 us -> 16.6 us  [the longest x2 10.6 us: dott(): lax.dot_general(a, b, (((1,), (1,)), ((), ())), preferred_element_type=jn...]
  transfers between devices with their start and end apart: 4 -> 21, of which waited for: 3 -> 10; matrix products, arithmetic and copies ran while one was open for 7% -> 11% of each run, Pallas kernels for 0% -> 0%
where the time goes in v2:
time: 198 us; the launch traced here: 197 us
  waiting for transfers between devices  92.5 us (47%)
  starting transfers between devices  71.3 us (36%)
  matrix products  16.6 us (8%)
  other arithmetic  11.1 us (6%)
  local copies, waits for them, and re-layouts  4.1 us (2%)
    ppermute x5, waiting for transfers between devices, cross(): return lax.ppermute(a, AXES, cross_pairs)  48.4 us
    ppermute x4, starting transfers between devices, step(): return lax.ppermute(a, AXES, step_pairs)  37.8 us
    ppermute x2, waiting for transfers between devices, away_jump(): return lax.ppermute(a, AXES, away_jump_pairs)  32.3 us
    ppermute x5, starting transfers between devices, cross(): return lax.ppermute(a, AXES, cross_pairs)  18.5 us
    ppermute x3, starting transfers between devices, home_jump(): return lax.ppermute(a, AXES, home_jump_pairs)  11.7 us
    ppermute x4, waiting for transfers between devices, step(): return lax.ppermute(a, AXES, step_pairs)  11.1 us
    dot_general x2, matrix products, dott(): lax.dot_general(a, b, (((1,), (1,)), ((), ())), preferred_element_type=jn...  10.6 us
    dot_general x8, matrix products, tdot(): lax.dot_general(a, b, (((0,), (0,)), ((), ())), preferred_element_type=jn...  6.06 us
  transfers between devices with their start and end apart: 21, of which 10 were waited for; matrix products, arithmetic and copies ran while one was open for 11% of the time, Pallas kernels for 0%

profile of v2, /device:TPU:0, one launch (start us, length us, event | category | flops | bytes accessed | tf_op | source)
XLA Modules:
  0.0 197.3 jit_solution(7139451917651305681)
XLA Ops:
  0.6 1.1 slice.14
  1.7 1.3 collective-permute-start.4
  3.0 0.0 copy-start.1
  3.1 27.1 %collective-permute-done.4 = bf16[1024,256]{1,0:T(8,128)(2,1)S(1)} collective-permute-done((bf16[1024,256]{1,0:T(8,128)(2,1)S(1)}, bf16[1024,256]{1,0:T(8,128)(2,1)S(1)}, u32[]{:S(2)}, u32[]{:S(2)}) %collective-permute-start.4) | collective-permute-done | bytes 524320 | tf_op jit(solution)/shard_map/ppermute | solution.py:80
  30.2 1.5 broadcast_select_fusion.15
  31.7 0.1 collective-permute-start.1
  31.8 0.1 collective-permute-start
  31.9 13.0 %collective-permute-done.1 = bf16[1024,256]{1,0:T(8,128)(2,1)S(1)} collective-permute-done((bf16[1024,256]{1,0:T(8,128)(2,1)S(1)}, bf16[1024,256]{1,0:T(8,128)(2,1)S(1)}, u32[]{:S(2)}, u32[]{:S(2)}) %collective-permute-start.1) | collective-permute-done | bytes 524320 | tf_op jit(solution)/shard_map/ppermute | solution.py:68
  44.9 0.3 collective-permute-start.5
  45.2 0.5 copy-done.4
  45.7 1.5 collective-permute-start.2
  47.1 9.9 %collective-permute-done.5 = bf16[1024,256]{1,0:T(8,128)(2,1)S(1)} collective-permute-done((bf16[1024,256]{1,0:T(8,128)(2,1)S(1)}, bf16[1024,256]{1,0:T(8,128)(2,1)S(1)}, u32[]{:S(2)}, u32[]{:S(2)}) %collective-permute-start.5) | collective-permute-done | bytes 524320 | tf_op jit(solution)/shard_map/ppermute | solution.py:68
  57.1 0.6 collective-permute-start.6
  57.6 4.7 %collective-permute-start.3 = (bf16[1024,256]{1,0:T(8,128)(2,1)S(1)}, bf16[1024,256]{1,0:T(8,128)(2,1)S(1)}, u32[]{:S(2)}, u32[]{:S(2)}) collective-permute-start(bf16[1024,256]{1,0:T(8,128)(2,1)S(1)} %get-tuple-element.9), channel_id=1, source_target_pairs={{0,8},{1,9},{4,12},{5,13},{10,2},{11,3},{14,6},{15,7},{16,24},{17,... | collective-permute-start | bytes 1572872 | tf_op jit(solution)/shard_map/ppermute | solution.py:77
  62.3 6.1 %collective-permute-done.6 = bf16[1024,256]{1,0:T(8,128)(2,1)} collective-permute-done((bf16[1024,256]{1,0:T(8,128)(2,1)S(1)}, bf16[1024,256]{1,0:T(8,128)(2,1)}, u32[]{:S(2)}, u32[]{:S(2)}) %collective-permute-start.6) | collective-permute-done | bytes 524320 | tf_op jit(solution)/shard_map/ppermute | solution.py:68
  68.4 1.3 collective-permute-start.7
  69.7 0.1 collective-permute-start.20
  70.5 0.7 collective-permute-done.3
  71.2 5.5 %collective-permute-start.12 = (bf16[1024,256]{1,0:T(8,128)(2,1)}, bf16[1024,256]{1,0:T(8,128)(2,1)S(1)}, u32[]{:S(2)}, u32[]{:S(2)}) collective-permute-start(bf16[1024,256]{1,0:T(8,128)(2,1)} %copy-done.7), channel_id=1, source_target_pairs={{0,8},{1,9},{4,12},{5,13},{10,2},{11,3},{14,6},{15,7},{16,24},{17,... | collective-permute-start | bytes 1572872 | tf_op jit(solution)/shard_map/ppermute | solution.py:77
  76.7 5.1 %collective-permute-done.7 = bf16[1024,256]{1,0:T(8,128)(2,1)} collective-permute-done((bf16[1024,256]{1,0:T(8,128)(2,1)}, bf16[1024,256]{1,0:T(8,128)(2,1)}, u32[]{:S(2)}, u32[]{:S(2)}) %collective-permute-start.7) | collective-permute-done | bytes 524320 | tf_op jit(solution)/shard_map/ppermute | solution.py:80
  81.9 1.7 broadcast_select_fusion.11
  83.6 32.3 %collective-permute-start.8 = (bf16[1024,256]{1,0:T(8,128)(2,1)S(1)}, bf16[1024,256]{1,0:T(8,128)(2,1)S(1)}, u32[]{:S(2)}, u32[]{:S(2)}) collective-permute-start(bf16[1024,256]{1,0:T(8,128)(2,1)S(1)} %get-tuple-element.35), channel_id=1, source_target_pairs={{0,4},{1,5},{2,6},{3,7},{4,0},{5,1},{6,2},{7,3},{8,12},{9,13},{10,... | collective-permute-start | bytes 1572872 | tf_op jit(solution)/shard_map/ppermute | solution.py:71
  115.9 0.0 collective-permute-done
  115.9 1.9 broadcast_select_fusion.1
  117.7 0.0 copy-start
  117.7 0.0 copy-start.9
  117.7 1.1 pad_maximum_fusion
  118.8 0.0 collective-permute-start.17
  118.8 0.0 collective-permute-done.12
  118.8 0.5 copy-done
  119.3 0.1 copy-done.9
  119.5 0.1 broadcast_select_fusion.17
  119.6 7.2 %collective-permute-done.8 = bf16[1024,256]{1,0:T(8,128)(2,1)S(1)} collective-permute-done((bf16[1024,256]{1,0:T(8,128)(2,1)S(1)}, bf16[1024,256]{1,0:T(8,128)(2,1)S(1)}, u32[]{:S(2)}, u32[]{:S(2)}) %collective-permute-start.8) | collective-permute-done | bytes 524320 | tf_op jit(solution)/shard_map/ppermute | solution.py:71
  126.8 1.7 collective-permute-start.9
  128.5 0.7 fusion.31
  129.3 0.8 convolution_add_fusion.2
  130.1 8.1 %collective-permute-start.11 = (f32[1024,256]{0,1:T(8,128)S(1)}, f32[1024,256]{0,1:T(8,128)S(1)}, u32[]{:S(2)}, u32[]{:S(2)}) collective-permute-start(f32[1024,256]{0,1:T(8,128)S(1)} %convolution_add_fusion.2), channel_id=1, source_target_pairs={{0,2},{1,3},{2,0},{3,1},{4,6},{5,7},{6,4},{7,5},{8,10},{9,11},{10,... | collective-permute-start | bytes 3145736 | tf_op jit(solution)/shard_map/ppermute | solution.py:68
  138.1 1.1 broadcast_select_fusion.9
  139.2 0.0 collective-permute-done.9
  139.2 2.0 %collective-permute-start.10 = (bf16[1024,256]{1,0:T(8,128)(2,1)S(1)}, bf16[1024,256]{1,0:T(8,128)(2,1)S(1)}, u32[]{:S(2)}, u32[]{:S(2)}) collective-permute-start(bf16[1024,256]{1,0:T(8,128)(2,1)S(1)} %get-tuple-element.13), channel_id=1, source_target_pairs={{0,4},{1,5},{2,6},{3,7},{4,0},{5,1},{6,2},{7,3},{8,12},{9,13},{10,... | collective-permute-start | bytes 1572872 | tf_op jit(solution)/shard_map/ppermute | solution.py:71
  141.2 0.8 fusion.33
  142.0 0.8 convolution_add_fusion
  142.7 9.5 %collective-permute-start.14 = (f32[1024,256]{0,1:T(8,128)S(1)}, f32[1024,256]{0,1:T(8,128)S(1)}, u32[]{:S(2)}, u32[]{:S(2)}) collective-permute-start(f32[1024,256]{0,1:T(8,128)S(1)} %convolution_add_fusion), channel_id=1, source_target_pairs={{0,2},{1,3},{2,0},{3,1},{4,6},{5,7},{6,4},{7,5},{8,10},{9,11},{10,... | collective-permute-start | bytes 3145736 | tf_op jit(solution)/shard_map/ppermute | solution.py:68
  152.2 1.1 broadcast_select_fusion.8
  153.4 0.0 collective-permute-done.10
  153.4 1.7 collective-permute-start.13
  155.1 0.8 fusion.30
  155.9 0.8 convolution_add_fusion.3
  156.7 1.1 broadcast_select_fusion.5
  157.8 4.3 %collective-permute-done.11 = f32[1024,256]{0,1:T(8,128)S(1)} collective-permute-done((f32[1024,256]{0,1:T(8,128)S(1)}, f32[1024,256]{0,1:T(8,128)S(1)}, u32[]{:S(2)}, u32[]{:S(2)}) %collective-permute-start.11) | collective-permute-done | bytes 1048608 | tf_op jit(solution)/shard_map/ppermute | solution.py:68
  162.1 0.0 collective-permute-start.18
  162.1 0.2 add.29
  162.2 3.9 %collective-permute-done.13 = bf16[1024,256]{1,0:T(8,128)(2,1)S(1)} collective-permute-done((bf16[1024,256]{1,0:T(8,128)(2,1)S(1)}, bf16[1024,256]{1,0:T(8,128)(2,1)S(1)}, u32[]{:S(2)}, u32[]{:S(2)}) %collective-permute-start.13) | collective-permute-done | bytes 524320 | tf_op jit(solution)/shard_map/ppermute | solution.py:71
  166.1 1.1 broadcast_select_fusion.4
  167.3 0.0 collective-permute-start.19
  167.3 0.8 fusion.32
  168.1 0.8 convolution_add_fusion.1
  168.8 15.1 %collective-permute-done.14 = f32[1024,256]{0,1:T(8,128)S(1)} collective-permute-done((f32[1024,256]{0,1:T(8,128)S(1)}, f32[1024,256]{0,1:T(8,128)S(1)}, u32[]{:S(2)}, u32[]{:S(2)}) %collective-permute-start.14) | collective-permute-done | bytes 1048608 | tf_op jit(solution)/shard_map/ppermute | solution.py:68
  183.9 0.2 add.32
  184.1 0.6 collective-permute-start.16
  184.7 0.2 maximum_multiply_fusion
  184.9 1.8 copy.10
  186.7 4.6 %fusion.13 = f32[1024,1024]{1,0:T(8,128)S(1)} fusion(bf16[1024,256]{1,0:T(8,128)(2,1)} %collective-permute-done.19, bf16[1024,256]{1,0:T(8,128)(2,1)} %collective-permute-done.18, bf16[1024,256]{1,0:T(8,128)(2,1)} %get-tuple-element.26, bf16[1024,256]{1,0:T(8,128)(2,1)} %get-tuple-element.24, bf16[1024,512]{1,0:T(8,128)(2,1)} %collective-permute-done.20, ...), kind=kOutput, calls=%fused_computation.15 | convolution fusion | flops 2160066560 | bytes 8388608 | tf_op jit(solution)/shard_map/dot_general | solution.py:38
  191.4 6.0 %add_multiply_fusion = f32[1024,1024]{1,0:T(8,128)} fusion(f32[1024,1024]{1,0:T(8,128)S(1)} %fusion.13, f32[]{:T(128)} %bitcast, bf16[1024,512]{1,0:T(8,128)(2,1)} %collective-permute-done.17, bf16[1024,256]{1,0:T(8,128)(2,1)S(1)} %get-tuple-element.36, bf16[1024,256]{1,0:T(8,128)(2,1)S(1)} %get-tuple-element.34, ...), kind=kOutput, calls=%fused_computation | convolution fusion | flops 2164260864 | bytes 12582916 | tf_op jit(solution)/shard_map/dot_general | solution.py:38
  (22 shorter events, 0.0 us)
Async XLA Ops:
  1.7 1.3 copy-start.7
  1.7 28.5 %collective-permute-start.4 = (bf16[1024,256]{1,0:T(8,128)(2,1)S(1)}, bf16[1024,256]{1,0:T(8,128)(2,1)S(1)}, u32[]{:S(2)}, u32[]{:S(2)}) collective-permute-start(bf16[1024,256]{1,0:T(8,128)(2,1)S(1)} %slice.14), channel_id=1, source_target_pairs={{2,10},{3,11},{6,14},{7,15},{8,0},{9,1},{12,4},{13,5},{18,26},{19,... | collective-permute-start | bytes 1572872 | tf_op jit(solution)/shard_map/ppermute | solution.py:80
  3.0 28.7 %copy-start.1 = (bf16[1024,1024]{1,0:T(8,128)(2,1)S(1)}, bf16[1024,1024]{1,0:T(8,128)(2,1)}, u32[]{:S(2)}) copy-start(bf16[1024,1024]{1,0:T(8,128)(2,1)} %param.6) | copy-start | bytes 6291460
  31.7 13.2 %collective-permute-start.1 = (bf16[1024,256]{1,0:T(8,128)(2,1)S(1)}, bf16[1024,256]{1,0:T(8,128)(2,1)S(1)}, u32[]{:S(2)}, u32[]{:S(2)}) collective-permute-start(bf16[1024,256]{1,0:T(8,128)(2,1)S(1)} %get-tuple-element.30), channel_id=1, source_target_pairs={{0,2},{1,3},{2,0},{3,1},{4,6},{5,7},{6,4},{7,5},{8,10},{9,11},{10,... | collective-permute-start | bytes 1572872 | tf_op jit(solution)/shard_map/ppermute | solution.py:68
  31.8 84.1 %collective-permute-start = (bf16[1024,1024]{1,0:T(8,128)(2,1)S(1)}, bf16[1024,1024]{1,0:T(8,128)(2,1)}, u32[]{:S(2)}, u32[]{:S(2)}) collective-permute-start(bf16[1024,1024]{1,0:T(8,128)(2,1)S(1)} %copy-done.1), channel_id=1, source_target_pairs={{0,1},{1,0},{2,3},{3,2},{4,5},{5,4},{6,7},{7,6},{8,9},{9,8},{10,11... | collective-permute-start | bytes 6291464 | tf_op jit(solution)/shard_map/ppermute | solution.py:74
  44.9 0.8 copy-start.4
  44.9 12.2 %collective-permute-start.5 = (bf16[1024,256]{1,0:T(8,128)(2,1)S(1)}, bf16[1024,256]{1,0:T(8,128)(2,1)S(1)}, u32[]{:S(2)}, u32[]{:S(2)}) collective-permute-start(bf16[1024,256]{1,0:T(8,128)(2,1)S(1)} %get-tuple-element.10), channel_id=1, source_target_pairs={{0,2},{1,3},{2,0},{3,1},{4,6},{5,7},{6,4},{7,5},{8,10},{9,11},{10,... | collective-permute-start | bytes 1572872 | tf_op jit(solution)/shard_map/ppermute | solution.py:68
  45.7 12.0 %collective-permute-start.2 = (bf16[1024,256]{1,0:T(8,128)(2,1)S(1)}, bf16[1024,256]{1,0:T(8,128)(2,1)S(1)}, u32[]{:S(2)}, u32[]{:S(2)}) collective-permute-start(bf16[1024,256]{1,0:T(8,128)(2,1)S(1)} %collective-permute-done.1), channel_id=1, source_target_pairs={{0,8},{1,9},{4,12},{5,13},{10,2},{11,3},{14,6},{15,7},{16,24},{17,... | collective-permute-start | bytes 1572872 | tf_op jit(solution)/shard_map/ppermute | solution.py:77
  57.1 5.3 %copy-start.5 = (bf16[1024,256]{1,0:T(8,128)(2,1)}, bf16[1024,256]{1,0:T(8,128)(2,1)S(1)}, u32[]{:S(2)}) copy-start(bf16[1024,256]{1,0:T(8,128)(2,1)S(1)} %collective-permute-done.5) | copy-start | bytes 1572868
  57.1 11.4 %collective-permute-start.6 = (bf16[1024,256]{1,0:T(8,128)(2,1)S(1)}, bf16[1024,256]{1,0:T(8,128)(2,1)}, u32[]{:S(2)}, u32[]{:S(2)}) collective-permute-start(bf16[1024,256]{1,0:T(8,128)(2,1)S(1)} %get-tuple-element.11), channel_id=1, source_target_pairs={{0,2},{1,3},{2,0},{3,1},{4,6},{5,7},{6,4},{7,5},{8,10},{9,11},{10,... | collective-permute-start | bytes 1572872 | tf_op jit(solution)/shard_map/ppermute | solution.py:68
  57.6 10.8 %copy-start.6 = (bf16[1024,256]{1,0:T(8,128)(2,1)}, bf16[1024,256]{1,0:T(8,128)(2,1)S(1)}, u32[]{:S(2)}) copy-start(bf16[1024,256]{1,0:T(8,128)(2,1)S(1)} %collective-permute-done.2) | copy-start | bytes 1572868
  57.6 13.5 %collective-permute-start.3 = (bf16[1024,256]{1,0:T(8,128)(2,1)S(1)}, bf16[1024,256]{1,0:T(8,128)(2,1)S(1)}, u32[]{:S(2)}, u32[]{:S(2)}) collective-permute-start(bf16[1024,256]{1,0:T(8,128)(2,1)S(1)} %get-tuple-element.9), channel_id=1, source_target_pairs={{0,8},{1,9},{4,12},{5,13},{10,2},{11,3},{14,6},{15,7},{16,24},{17,... | collective-permute-start | bytes 1572872 | tf_op jit(solution)/shard_map/ppermute | solution.py:77
  68.4 13.4 %collective-permute-start.7 = (bf16[1024,256]{1,0:T(8,128)(2,1)}, bf16[1024,256]{1,0:T(8,128)(2,1)}, u32[]{:S(2)}, u32[]{:S(2)}) collective-permute-start(bf16[1024,256]{1,0:T(8,128)(2,1)} %collective-permute-done.6), channel_id=1, source_target_pairs={{2,10},{3,11},{6,14},{7,15},{8,0},{9,1},{12,4},{13,5},{18,26},{19,... | collective-permute-start | bytes 1572872 | tf_op jit(solution)/shard_map/ppermute | solution.py:80
  69.7 114.4 %collective-permute-start.20 = (bf16[1024,512]{1,0:T(8,128)(2,1)}, bf16[1024,512]{1,0:T(8,128)(2,1)}, u32[]{:S(2)}, u32[]{:S(2)}) collective-permute-start(bf16[1024,512]{1,0:T(8,128)(2,1)} %param.5), channel_id=1, source_target_pairs={{0,1},{1,0},{2,3},{3,2},{4,5},{5,4},{6,7},{7,6},{8,9},{9,8},{10,11... | collective-permute-start | bytes 3145736 | tf_op jit(solution)/shard_map/ppermute | solution.py:74
  71.2 5.5 %copy-start.8 = (bf16[1024,256]{1,0:T(8,128)(2,1)}, bf16[1024,256]{1,0:T(8,128)(2,1)S(1)}, u32[]{:S(2)}) copy-start(bf16[1024,256]{1,0:T(8,128)(2,1)S(1)} %collective-permute-done.3) | copy-start | bytes 1572868
  71.2 47.6 %collective-permute-start.12 = (bf16[1024,256]{1,0:T(8,128)(2,1)}, bf16[1024,256]{1,0:T(8,128)(2,1)S(1)}, u32[]{:S(2)}, u32[]{:S(2)}) collective-permute-start(bf16[1024,256]{1,0:T(8,128)(2,1)} %copy-done.7), channel_id=1, source_target_pairs={{0,8},{1,9},{4,12},{5,13},{10,2},{11,3},{14,6},{15,7},{16,24},{17,... | collective-permute-start | bytes 1572872 | tf_op jit(solution)/shard_map/ppermute | solution.py:77
  83.6 43.2 %collective-permute-start.8 = (bf16[1024,256]{1,0:T(8,128)(2,1)S(1)}, bf16[1024,256]{1,0:T(8,128)(2,1)S(1)}, u32[]{:S(2)}, u32[]{:S(2)}) collective-permute-start(bf16[1024,256]{1,0:T(8,128)(2,1)S(1)} %get-tuple-element.35), channel_id=1, source_target_pairs={{0,4},{1,5},{2,6},{3,7},{4,0},{5,1},{6,2},{7,3},{8,12},{9,13},{10,... | collective-permute-start | bytes 1572872 | tf_op jit(solution)/shard_map/ppermute | solution.py:71
  117.7 1.6 copy-start
  117.7 1.7 copy-start.9
  118.8 72.5 %collective-permute-start.17 = (bf16[1024,512]{1,0:T(8,128)(2,1)}, bf16[1024,512]{1,0:T(8,128)(2,1)}, u32[]{:S(2)}, u32[]{:S(2)}) collective-permute-start(bf16[1024,512]{1,0:T(8,128)(2,1)} %pad_maximum_fusion), channel_id=1, source_target_pairs={{0,1},{1,0},{2,3},{3,2},{4,5},{5,4},{6,7},{7,6},{8,9},{9,8},{10,11... | collective-permute-start | bytes 3145736 | tf_op jit(solution)/shard_map/ppermute | solution.py:74
  126.8 12.4 %collective-permute-start.9 = (bf16[1024,256]{1,0:T(8,128)(2,1)S(1)}, bf16[1024,256]{1,0:T(8,128)(2,1)S(1)}, u32[]{:S(2)}, u32[]{:S(2)}) collective-permute-start(bf16[1024,256]{1,0:T(8,128)(2,1)S(1)} %get-tuple-element.12), channel_id=1, source_target_pairs={{0,4},{1,5},{2,6},{3,7},{4,0},{5,1},{6,2},{7,3},{8,12},{9,13},{10,... | collective-permute-start | bytes 1572872 | tf_op jit(solution)/shard_map/ppermute | solution.py:71
  130.1 32.0 %collective-permute-start.11 = (f32[1024,256]{0,1:T(8,128)S(1)}, f32[1024,256]{0,1:T(8,128)S(1)}, u32[]{:S(2)}, u32[]{:S(2)}) collective-permute-start(f32[1024,256]{0,1:T(8,128)S(1)} %convolution_add_fusion.2), channel_id=1, source_target_pairs={{0,2},{1,3},{2,0},{3,1},{4,6},{5,7},{6,4},{7,5},{8,10},{9,11},{10,... | collective-permute-start | bytes 3145736 | tf_op jit(solution)/shard_map/ppermute | solution.py:68
  139.2 14.2 %collective-permute-start.10 = (bf16[1024,256]{1,0:T(8,128)(2,1)S(1)}, bf16[1024,256]{1,0:T(8,128)(2,1)S(1)}, u32[]{:S(2)}, u32[]{:S(2)}) collective-permute-start(bf16[1024,256]{1,0:T(8,128)(2,1)S(1)} %get-tuple-element.13), channel_id=1, source_target_pairs={{0,4},{1,5},{2,6},{3,7},{4,0},{5,1},{6,2},{7,3},{8,12},{9,13},{10,... | collective-permute-start | bytes 1572872 | tf_op jit(solution)/shard_map/ppermute | solution.py:71
  142.7 41.2 %collective-permute-start.14 = (f32[1024,256]{0,1:T(8,128)S(1)}, f32[1024,256]{0,1:T(8,128)S(1)}, u32[]{:S(2)}, u32[]{:S(2)}) collective-permute-start(f32[1024,256]{0,1:T(8,128)S(1)} %convolution_add_fusion), channel_id=1, source_target_pairs={{0,2},{1,3},{2,0},{3,1},{4,6},{5,7},{6,4},{7,5},{8,10},{9,11},{10,... | collective-permute-start | bytes 3145736 | tf_op jit(solution)/shard_map/ppermute | solution.py:68
  153.4 12.8 %collective-permute-start.13 = (bf16[1024,256]{1,0:T(8,128)(2,1)S(1)}, bf16[1024,256]{1,0:T(8,128)(2,1)S(1)}, u32[]{:S(2)}, u32[]{:S(2)}) collective-permute-start(bf16[1024,256]{1,0:T(8,128)(2,1)S(1)} %get-tuple-element.15), channel_id=1, source_target_pairs={{0,4},{1,5},{2,6},{3,7},{4,0},{5,1},{6,2},{7,3},{8,12},{9,13},{10,... | collective-permute-start | bytes 1572872 | tf_op jit(solution)/shard_map/ppermute | solution.py:71
  162.1 24.6 %collective-permute-start.18 = (bf16[1024,256]{1,0:T(8,128)(2,1)}, bf16[1024,256]{1,0:T(8,128)(2,1)}, u32[]{:S(2)}, u32[]{:S(2)}) collective-permute-start(bf16[1024,256]{1,0:T(8,128)(2,1)} %get-tuple-element.25), channel_id=1, source_target_pairs={{0,1},{1,0},{2,3},{3,2},{4,5},{5,4},{6,7},{7,6},{8,9},{9,8},{10,11... | collective-permute-start | bytes 1572872 | tf_op jit(solution)/shard_map/ppermute | solution.py:74
  167.3 19.4 %collective-permute-start.19 = (bf16[1024,256]{1,0:T(8,128)(2,1)}, bf16[1024,256]{1,0:T(8,128)(2,1)}, u32[]{:S(2)}, u32[]{:S(2)}) collective-permute-start(bf16[1024,256]{1,0:T(8,128)(2,1)} %get-tuple-element.27), channel_id=1, source_target_pairs={{0,1},{1,0},{2,3},{3,2},{4,5},{5,4},{6,7},{7,6},{8,9},{9,8},{10,11... | collective-permute-start | bytes 1572872 | tf_op jit(solution)/shard_map/ppermute | solution.py:74
  183.9 7.4 %collective-permute-start.15 = (bf16[1024,256]{1,0:T(8,128)(2,1)}, bf16[1024,256]{1,0:T(8,128)(2,1)}, u32[]{:S(2)}, u32[]{:S(2)}) collective-permute-start(bf16[1024,256]{1,0:T(8,128)(2,1)} %get-tuple-element.21), channel_id=1, source_target_pairs={{0,1},{1,0},{2,3},{3,2},{4,5},{5,4},{6,7},{7,6},{8,9},{9,8},{10,11... | collective-permute-start | bytes 1572872 | tf_op jit(solution)/shard_map/ppermute | solution.py:74
  184.1 7.2 %collective-permute-start.16 = (bf16[1024,256]{1,0:T(8,128)(2,1)}, bf16[1024,256]{1,0:T(8,128)(2,1)}, u32[]{:S(2)}, u32[]{:S(2)}) collective-permute-start(bf16[1024,256]{1,0:T(8,128)(2,1)} %get-tuple-element.23), channel_id=1, source_target_pairs={{0,1},{1,0},{2,3},{3,2},{4,5},{5,4},{6,7},{7,6},{8,9},{9,8},{10,11... | collective-permute-start | bytes 1572872 | tf_op jit(solution)/shard_map/ppermute | solution.py:74
  186.7 4.7 %copy-start.2 = (bf16[1024,256]{1,0:T(8,128)(2,1)S(1)}, bf16[1024,256]{1,0:T(8,128)(2,1)}, u32[]{:S(2)}) copy-start(bf16[1024,256]{1,0:T(8,128)(2,1)} %get-tuple-element.20) | copy-start | bytes 1572868
  186.7 4.7 %copy-start.3 = (bf16[1024,256]{1,0:T(8,128)(2,1)S(1)}, bf16[1024,256]{1,0:T(8,128)(2,1)}, u32[]{:S(2)}) copy-start(bf16[1024,256]{1,0:T(8,128)(2,1)} %get-tuple-element.22) | copy-start | bytes 1572868

commit v3 on v2

--- a/solution.py
+++ b/solution.py
@@ -92,33 +92,40 @@
         jq = away_jump(eq)
         t_other = swap(transition)
         v_other = swap(value_next)
+        vp2, vq2 = lax.optimization_barrier((vp, vq, x1))[:2]
+        x2 = cross(jnp.where(home, vq2, vp2))
+        jp = home_jump(x1)
+        vq3, jq3 = lax.optimization_barrier((vq, jq, x2))[:2]
+        x3 = cross(jnp.where(home, jq3, vq3))
+        jq2 = away_jump(x3)
+        bp = jnp.where(home, x1, after(jp, x3))
+        bp_next = step(bp)
+        jap = home_jump(after(ep, jp, x3))
+        t_other = after(t_other, x2)
         t_near, t_next = jnp.where(mine, transition, t_other), jnp.where(mine, t_other, transition)
 
         def adjoint_of(near, far):
             return tdot(t_near, near) + tdot(t_next, far)
 
+        part_p = cross(adjoint_of(bp, bp_next))
+        jq2_late, x3_late = lax.optimization_barrier((jq2, x3, bp_next))[:2]
+        bq = jnp.where(home, jq2_late, x3_late)
+        bq_next = step(bq)
+        jaq = home_jump(after(eq, jap, bp_next, jq2))
+        ep_late, jap_late = lax.optimization_barrier((ep, jap, bq_next))[:2]
+        ap = jnp.where(home, ep_late, jap_late)
+        ap_next = step(ap)
+        part_q = cross(after(adjoint_of(bq, bq_next), part_p))
+        eq_late, jaq_late = lax.optimization_barrier((eq, jaq, ap_next))[:2]
+        aq = jnp.where(home, eq_late, jaq_late)
+        aq_next = step(aq)
+
+        v_across = jnp.concatenate([jnp.where(home, x2, x1), jnp.where(home, x3, x2)], 1)
+        v_across_other = swap(after(v_across, bp_next))
+
         def own_and_swapped(near, far):
             return jnp.where(mine, near, far), swap(jnp.where(mine, far, near))
 
-        x2 = cross(after(jnp.where(home, vq, vp), x1))
-        jp = home_jump(x1)
-        x3 = cross(after(jnp.where(home, jq, vq), x2))
-        jq2 = away_jump(x3)
-        bp = jnp.where(home, x1, jp)
-        bp_next = step(bp)
-        jap = home_jump(after(ep, jp))
-        part_p = cross(adjoint_of(bp, bp_next))
-        bq = jnp.where(home, jq2, x3)
-        bq_next = step(after(bq, bp_next))
-        part_q = cross(adjoint_of(bq, bq_next))
-        ap = jnp.where(home, ep, jap)
-        ap_next = step(after(ap, bq_next))
-        jaq = home_jump(after(eq, jap))
-        aq = jnp.where(home, eq, jaq)
-        aq_next = step(after(aq, ap_next))
-
-        v_across = jnp.concatenate([jnp.where(home, x2, x1), jnp.where(home, x3, x2)], 1)
-        v_across_other = swap(v_across)
         bp_own, bp_swapped = own_and_swapped(bp, bp_next)
         bq_own, bq_swapped = own_and_swapped(bq, bq_next)
         grad = dott(
@@ -126,7 +133,8 @@
             jnp.concatenate([v_across, v_across_other], 1),
         )
         ap_own, ap_swapped = own_and_swapped(ap, ap_next)
-        aq_own, aq_swapped = own_and_swapped(aq, aq_next)
+        aq_near, aq_far = lax.optimization_barrier((aq, aq_next, grad))[:2]
+        aq_own, aq_swapped = own_and_swapped(aq_near, aq_far)
         grad = grad + dott(
             jnp.concatenate([ap_own, aq_own, ap_swapped, aq_swapped], 1),
             jnp.concatenate([value_next, v_other], 1),

time: 198 us -> 153 us (0.77)
  starting transfers between devices: 71.3 us -> 43.5 us
  waiting for transfers between devices: 92.5 us -> 76.7 us
  local copies, waits for them, and re-layouts: 4.1 us -> 1.83 us
    ppermute x4, starting transfers between devices: 37.8 us -> 7.62 us  [step(): return lax.ppermute(a, AXES, step_pairs)]
    ppermute x2, waiting for transfers between devices: 32.3 us -> 22.2 us  [away_jump(): return lax.ppermute(a, AXES, away_jump_pairs)]
    ppermute x3, starting transfers between devices: 11.7 us -> 17.5 us  [home_jump(): return lax.ppermute(a, AXES, home_jump_pairs)]
    ppermute x4, waiting for transfers between devices: 11.1 us -> 5.89 us  [step(): return lax.ppermute(a, AXES, step_pairs)]
    ppermute x5, starting transfers between devices: 18.5 us -> 14.7 us  [cross(): return lax.ppermute(a, AXES, cross_pairs)]
    ppermute x5, waiting for transfers between devices: 48.4 us -> 46 us  [cross(): return lax.ppermute(a, AXES, cross_pairs)]
    select_n x4, other arithmetic: 4.45 us -> 2.09 us  [own_and_swapped(): return (jnp.where(mine, near, far), swap(jnp.where(mine, far, near)))]
  transfers between devices with their start and end apart: 21 -> 21, of which waited for: 10 -> 8; matrix products, arithmetic and copies ran while one was open for 11% -> 13% of each run, Pallas kernels for 0% -> 0%
where the time goes in v3:
time: 153 us; the launch traced here: 151 us
  waiting for transfers between devices  76.7 us (50%)
  starting transfers between devices  43.5 us (28%)
  matrix products  18 us (12%)
  other arithmetic  9.84 us (6%)
  local copies, waits for them, and re-layouts  1.83 us (1%)
  between operations  1.6 us (1%)
    ppermute x5, waiting for transfers between devices, cross(): return lax.ppermute(a, AXES, cross_pairs)  46 us
    ppermute x2, waiting for transfers between devices, away_jump(): return lax.ppermute(a, AXES, away_jump_pairs)  22.2 us
    ppermute x3, starting transfers between devices, home_jump(): return lax.ppermute(a, AXES, home_jump_pairs)  17.5 us
    ppermute x5, starting transfers between devices, cross(): return lax.ppermute(a, AXES, cross_pairs)  14.7 us
    dot_general x2, matrix products, dott(): lax.dot_general(a, b, (((1,), (1,)), ((), ())), preferred_element_type=jn...  11.9 us
    ppermute x4, starting transfers between devices, step(): return lax.ppermute(a, AXES, step_pairs)  7.62 us
    dot_general x8, matrix products, tdot(): lax.dot_general(a, b, (((0,), (0,)), ((), ())), preferred_element_type=jn...  6.07 us
    ppermute x4, waiting for transfers between devices, step(): return lax.ppermute(a, AXES, step_pairs)  5.89 us
  transfers between devices with their start and end apart: 21, of which 8 were waited for; matrix products, arithmetic and copies ran while one was open for 13% of the time, Pallas kernels for 0%

profile of v3, /device:TPU:0, one launch (start us, length us, event | category | flops | bytes accessed | tf_op | source)
XLA Modules:
  0.0 151.5 jit_solution(3688813296401632290)
XLA Ops:
  0.6 1.7 %fusion.32 = (bf16[1024,256]{1,0:T(8,128)(2,1)S(1)}, bf16[1024,256]{1,0:T(8,128)(2,1)S(1)}, bf16[1024,256]{1,0:T(8,128)(2,1)S(1)}, bf16[1024,256]{1,0:T(8,128)(2,1)S(1)}, bf16[1024,256]{1,0:T(8,128)(2,1)S(1)}) fusion(bf16[1024,512]{1,0:T(8,128)(2,1)} %param.4, bf16[1024,512]{1,0:T(8,128)(2,1)} %param.5, pred[]{:T(512)S(6)} %eq.9), kind=kLoop, calls=%fused_computation.54 | loop fusion | flops 262144 | bytes 4718593 | tf_op jit(solution)/shard_map/slice | solution.py:88
  2.3 3.0 %collective-permute-start.1 = (bf16[1024,256]{1,0:T(8,128)(2,1)S(1)}, bf16[1024,256]{1,0:T(8,128)(2,1)S(1)}, u32[]{:S(2)}, u32[]{:S(2)}) collective-permute-start(bf16[1024,256]{1,0:T(8,128)(2,1)S(1)} %get-tuple-element.51), channel_id=1, source_target_pairs={{0,2},{1,3},{2,0},{3,1},{4,6},{5,7},{6,4},{7,5},{8,10},{9,11},{10,... | collective-permute-start | bytes 1572872 | tf_op jit(solution)/shard_map/ppermute | solution.py:68
  5.3 1.3 collective-permute-start.4
  6.6 10.6 %collective-permute-done.1 = bf16[1024,256]{1,0:T(8,128)(2,1)S(1)} collective-permute-done((bf16[1024,256]{1,0:T(8,128)(2,1)S(1)}, bf16[1024,256]{1,0:T(8,128)(2,1)S(1)}, u32[]{:S(2)}, u32[]{:S(2)}) %collective-permute-start.1) | collective-permute-done | bytes 524320 | tf_op jit(solution)/shard_map/ppermute | solution.py:68
  17.3 0.1 broadcast_select_fusion.17
  17.3 1.8 %collective-permute-start.2 = (bf16[1024,256]{1,0:T(8,128)(2,1)S(1)}, bf16[1024,256]{1,0:T(8,128)(2,1)S(1)}, u32[]{:S(2)}, u32[]{:S(2)}) collective-permute-start(bf16[1024,256]{1,0:T(8,128)(2,1)S(1)} %broadcast_select_fusion.17), channel_id=1, source_target_pairs={{0,2},{1,3},{2,0},{3,1},{4,6},{5,7},{6,4},{7,5},{8,10},{9,11},{10,... | collective-permute-start | bytes 1572872 | tf_op jit(solution)/shard_map/ppermute | solution.py:68
  19.1 0.0 collective-permute-start
  19.1 4.5 %collective-permute-start.3 = (bf16[1024,256]{1,0:T(8,128)(2,1)S(1)}, bf16[1024,256]{1,0:T(8,128)(2,1)S(1)}, u32[]{:S(2)}, u32[]{:S(2)}) collective-permute-start(bf16[1024,256]{1,0:T(8,128)(2,1)S(1)} %collective-permute-done.1), channel_id=1, source_target_pairs={{0,8},{1,9},{4,12},{5,13},{10,2},{11,3},{14,6},{15,7},{16,24},{17,... | collective-permute-start | bytes 1572872 | tf_op jit(solution)/shard_map/ppermute | solution.py:77
  23.7 9.1 %collective-permute-done.4 = bf16[1024,256]{1,0:T(8,128)(2,1)S(1)} collective-permute-done((bf16[1024,256]{1,0:T(8,128)(2,1)S(1)}, bf16[1024,256]{1,0:T(8,128)(2,1)S(1)}, u32[]{:S(2)}, u32[]{:S(2)}) %collective-permute-start.4) | collective-permute-done | bytes 524320 | tf_op jit(solution)/shard_map/ppermute | solution.py:80
  32.7 0.0 collective-permute-done.2
  32.7 0.1 broadcast_select_fusion.16
  32.8 0.1 collective-permute-start.5
  32.9 2.6 %collective-permute-done.3 = bf16[1024,256]{1,0:T(8,128)(2,1)S(1)} collective-permute-done((bf16[1024,256]{1,0:T(8,128)(2,1)S(1)}, bf16[1024,256]{1,0:T(8,128)(2,1)S(1)}, u32[]{:S(2)}, u32[]{:S(2)}) %collective-permute-start.3) | collective-permute-done | bytes 524320 | tf_op jit(solution)/shard_map/ppermute | solution.py:77
  35.5 10.1 %collective-permute-done.5 = bf16[1024,256]{1,0:T(8,128)(2,1)S(1)} collective-permute-done((bf16[1024,256]{1,0:T(8,128)(2,1)S(1)}, bf16[1024,256]{1,0:T(8,128)(2,1)S(1)}, u32[]{:S(2)}, u32[]{:S(2)}) %collective-permute-start.5) | collective-permute-done | bytes 524320 | tf_op jit(solution)/shard_map/ppermute | solution.py:68
  45.6 1.3 collective-permute-start.7
  46.9 0.9 broadcast_select_fusion.11
  47.9 2.5 %collective-permute-start.8 = (bf16[1024,256]{1,0:T(8,128)(2,1)S(1)}, bf16[1024,256]{1,0:T(8,128)(2,1)S(1)}, u32[]{:S(2)}, u32[]{:S(2)}) collective-permute-start(bf16[1024,256]{1,0:T(8,128)(2,1)S(1)} %get-tuple-element.56), channel_id=1, source_target_pairs={{0,4},{1,5},{2,6},{3,7},{4,0},{5,1},{6,2},{7,3},{8,12},{9,13},{10,... | collective-permute-start | bytes 1572872 | tf_op jit(solution)/shard_map/ppermute | solution.py:71
  50.4 0.0 collective-permute-start.20
  51.1 6.3 %collective-permute-start.6 = (bf16[1024,256]{1,0:T(8,128)(2,1)S(1)}, bf16[1024,256]{1,0:T(8,128)(2,1)S(1)}, u32[]{:S(2)}, u32[]{:S(2)}) collective-permute-start(bf16[1024,256]{1,0:T(8,128)(2,1)S(1)} %get-tuple-element.29), channel_id=1, source_target_pairs={{0,8},{1,9},{4,12},{5,13},{10,2},{11,3},{14,6},{15,7},{16,24},{17,... | collective-permute-start | bytes 1572872 | tf_op jit(solution)/shard_map/ppermute | solution.py:77
  57.4 1.1 pad_maximum_fusion
  58.5 0.0 collective-permute-done
  58.6 13.1 %collective-permute-done.7 = bf16[1024,256]{1,0:T(8,128)(2,1)} collective-permute-done((bf16[1024,256]{1,0:T(8,128)(2,1)S(1)}, bf16[1024,256]{1,0:T(8,128)(2,1)}, u32[]{:S(2)}, u32[]{:S(2)}) %collective-permute-start.7) | collective-permute-done | bytes 524320 | tf_op jit(solution)/shard_map/ppermute | solution.py:80
  71.7 0.0 collective-permute-done.8
  71.7 1.1 broadcast_select_fusion.14
  72.8 0.1 collective-permute-start.9
  72.8 2.5 %broadcast_select_fusion.1 = (bf16[1024,1024]{1,0:T(8,128)(2,1)S(1)}, bf16[1024,1024]{1,0:T(8,128)(2,1)S(1)}) fusion(bf16[1024,1024]{1,0:T(8,128)(2,1)} %param.6, bf16[1024,1024]{1,0:T(8,128)(2,1)} %collective-permute-done, pred[]{:T(512)S(6)} %eq.8), kind=kLoop, calls=%fused_computation.27 | loop fusion | flops 2097152 | bytes 8388609 | tf_op jit(solution)/shard_map/jit(_where)/select_n | solution.py:105
  75.3 0.8 fusion.34
  76.1 0.8 convolution_add_fusion.2
  76.9 1.5 %collective-permute-start.11 = (f32[1024,256]{0,1:T(8,128)S(1)}, f32[1024,256]{0,1:T(8,128)S(1)}, u32[]{:S(2)}, u32[]{:S(2)}) collective-permute-start(f32[1024,256]{0,1:T(8,128)S(1)} %convolution_add_fusion.2), channel_id=1, source_target_pairs={{0,2},{1,3},{2,0},{3,1},{4,6},{5,7},{6,4},{7,5},{8,10},{9,11},{10,... | collective-permute-start | bytes 3145736 | tf_op jit(solution)/shard_map/ppermute | solution.py:68
  78.4 0.0 collective-permute-done.6
  78.4 6.8 %collective-permute-start.12 = (bf16[1024,256]{1,0:T(8,128)(2,1)S(1)}, bf16[1024,256]{1,0:T(8,128)(2,1)S(1)}, u32[]{:S(2)}, u32[]{:S(2)}) collective-permute-start(bf16[1024,256]{1,0:T(8,128)(2,1)S(1)} %get-tuple-element.32), channel_id=1, source_target_pairs={{0,8},{1,9},{4,12},{5,13},{10,2},{11,3},{14,6},{15,7},{16,24},{17,... | collective-permute-start | bytes 1572872 | tf_op jit(solution)/shard_map/ppermute | solution.py:77
  85.2 0.1 broadcast_select_fusion.9
  85.3 0.1 collective-permute-start.15
  85.3 0.0 collective-permute-done.9
  85.3 0.1 broadcast_select_fusion.13
  85.4 2.5 %collective-permute-start.10 = (bf16[1024,256]{1,0:T(8,128)(2,1)S(1)}, bf16[1024,256]{1,0:T(8,128)(2,1)S(1)}, u32[]{:S(2)}, u32[]{:S(2)}) collective-permute-start(bf16[1024,256]{1,0:T(8,128)(2,1)S(1)} %broadcast_select_fusion.13), channel_id=1, source_target_pairs={{0,4},{1,5},{2,6},{3,7},{4,0},{5,1},{6,2},{7,3},{8,12},{9,13},{10,... | collective-permute-start | bytes 1572872 | tf_op jit(solution)/shard_map/ppermute | solution.py:71
  87.9 0.8 fusion.36
  88.6 0.1 broadcast_select_fusion.8
  88.7 0.8 convolution_add_fusion
  89.5 11.0 %collective-permute-done.11 = f32[1024,256]{0,1:T(8,128)S(1)} collective-permute-done((f32[1024,256]{0,1:T(8,128)S(1)}, f32[1024,256]{0,1:T(8,128)S(1)}, u32[]{:S(2)}, u32[]{:S(2)}) %collective-permute-start.11) | collective-permute-done | bytes 1048608 | tf_op jit(solution)/shard_map/ppermute | solution.py:68
  100.5 0.5 collective-permute-start.16
  101.0 5.9 %collective-permute-done.10 = bf16[1024,256]{1,0:T(8,128)(2,1)S(1)} collective-permute-done((bf16[1024,256]{1,0:T(8,128)(2,1)S(1)}, bf16[1024,256]{1,0:T(8,128)(2,1)S(1)}, u32[]{:S(2)}, u32[]{:S(2)}) %collective-permute-start.10) | collective-permute-done | bytes 524320 | tf_op jit(solution)/shard_map/ppermute | solution.py:71
  106.9 0.1 broadcast_select_fusion.12
  106.9 2.5 %collective-permute-start.13 = (bf16[1024,256]{1,0:T(8,128)(2,1)S(1)}, bf16[1024,256]{1,0:T(8,128)(2,1)S(1)}, u32[]{:S(2)}, u32[]{:S(2)}) collective-permute-start(bf16[1024,256]{1,0:T(8,128)(2,1)S(1)} %broadcast_select_fusion.12), channel_id=1, source_target_pairs={{0,4},{1,5},{2,6},{3,7},{4,0},{5,1},{6,2},{7,3},{8,12},{9,13},{10,... | collective-permute-start | bytes 1572872 | tf_op jit(solution)/shard_map/ppermute | solution.py:71
  109.5 0.8 fusion.33
  110.2 0.8 fusion.25
  111.0 0.0 copy-start
  111.0 0.9 broadcast_select_fusion.5
  111.9 8.3 %collective-permute-start.14 = (f32[1024,256]{0,1:T(8,128)S(1)}, f32[1024,256]{0,1:T(8,128)S(1)}, u32[]{:S(2)}, u32[]{:S(2)}) collective-permute-start(f32[1024,256]{0,1:T(8,128)S(1)} %convolution_add_fusion), channel_id=1, source_target_pairs={{0,2},{1,3},{2,0},{3,1},{4,6},{5,7},{6,4},{7,5},{8,10},{9,11},{10,... | collective-permute-start | bytes 3145736 | tf_op jit(solution)/shard_map/ppermute | solution.py:68
  120.2 0.0 collective-permute-done.17
  120.2 0.0 collective-permute-start.18
  120.2 0.0 collective-permute-done.16
  120.2 4.4 %fusion = f32[1024,1024]{1,0:T(8,128)} fusion(bf16[1024,256]{1,0:T(8,128)(2,1)S(1)} %collective-permute-done.16, bf16[1024,256]{1,0:T(8,128)(2,1)S(1)} %collective-permute-done.15, bf16[1024,256]{1,0:T(8,128)(2,1)S(1)} %get-tuple-element.48, bf16[1024,256]{1,0:T(8,128)(2,1)S(1)} %get-tuple-element.46, bf16[1024,512]{1,0:T(8,128)(2,1)S(1)} %collective-permute-done.17, ...), kind=kOutput, calls=%fused_computation.2 | convolution fusion | flops 2162163712 | bytes 8388608 | tf_op jit(solution)/shard_map/dot_general | solution.py:38
  124.6 0.0 collective-permute-done.13
  124.6 1.1 broadcast_select_fusion.4
  125.7 0.5 collective-permute-start.19
  126.2 0.8 fusion.35
  126.9 14.2 %collective-permute-done.14 = f32[1024,256]{0,1:T(8,128)S(1)} collective-permute-done((f32[1024,256]{0,1:T(8,128)S(1)}, f32[1024,256]{0,1:T(8,128)S(1)}, u32[]{:S(2)}, u32[]{:S(2)}) %collective-permute-start.14) | collective-permute-done | bytes 1048608 | tf_op jit(solution)/shard_map/ppermute | solution.py:68
  141.1 0.8 fusion.24
  141.9 0.2 maximum_multiply_fusion
  142.1 1.8 %copy.10 = f32[1024,512]{1,0:T(8,128)} copy(f32[1024,512]{0,1:T(8,128)S(1)} %maximum_multiply_fusion) | data formatting | bytes 4194304
  143.9 0.0 collective-permute-done.18
  143.9 0.0 collective-permute-done.19
  143.9 7.5 %add_multiply_fusion = f32[1024,1024]{1,0:T(8,128)} fusion(f32[1024,1024]{1,0:T(8,128)} %fusion, f32[]{:T(128)} %bitcast, bf16[1024,512]{1,0:T(8,128)(2,1)} %collective-permute-done.20, bf16[1024,512]{1,0:T(8,128)(2,1)} %param.5, bf16[1024,256]{1,0:T(8,128)(2,1)} %collective-permute-done.19, bf16[1024,256]{1,0:T(8,128)(2,1)} %collective-permute-done.18, ...), kind=kOutput, calls=%fused_computation | convolution fusion | flops 2162163712 | bytes 12582916 | tf_op jit(solution)/shard_map/dot_general | solution.py:38
  (7 shorter events, 0.0 us)
Async XLA Ops:
  2.3 14.9 %collective-permute-start.1 = (bf16[1024,256]{1,0:T(8,128)(2,1)S(1)}, bf16[1024,256]{1,0:T(8,128)(2,1)S(1)}, u32[]{:S(2)}, u32[]{:S(2)}) collective-permute-start(bf16[1024,256]{1,0:T(8,128)(2,1)S(1)} %get-tuple-element.51), channel_id=1, source_target_pairs={{0,2},{1,3},{2,0},{3,1},{4,6},{5,7},{6,4},{7,5},{8,10},{9,11},{10,... | collective-permute-start | bytes 1572872 | tf_op jit(solution)/shard_map/ppermute | solution.py:68
  5.3 27.4 %collective-permute-start.4 = (bf16[1024,256]{1,0:T(8,128)(2,1)S(1)}, bf16[1024,256]{1,0:T(8,128)(2,1)S(1)}, u32[]{:S(2)}, u32[]{:S(2)}) collective-permute-start(bf16[1024,256]{1,0:T(8,128)(2,1)S(1)} %get-tuple-element.32), channel_id=1, source_target_pairs={{2,10},{3,11},{6,14},{7,15},{8,0},{9,1},{12,4},{13,5},{18,26},{19,... | collective-permute-start | bytes 1572872 | tf_op jit(solution)/shard_map/ppermute | solution.py:80
  17.3 15.4 %collective-permute-start.2 = (bf16[1024,256]{1,0:T(8,128)(2,1)S(1)}, bf16[1024,256]{1,0:T(8,128)(2,1)S(1)}, u32[]{:S(2)}, u32[]{:S(2)}) collective-permute-start(bf16[1024,256]{1,0:T(8,128)(2,1)S(1)} %broadcast_select_fusion.17), channel_id=1, source_target_pairs={{0,2},{1,3},{2,0},{3,1},{4,6},{5,7},{6,4},{7,5},{8,10},{9,11},{10,... | collective-permute-start | bytes 1572872 | tf_op jit(solution)/shard_map/ppermute | solution.py:68
  19.1 39.4 %collective-permute-start = (bf16[1024,1024]{1,0:T(8,128)(2,1)}, bf16[1024,1024]{1,0:T(8,128)(2,1)}, u32[]{:S(2)}, u32[]{:S(2)}) collective-permute-start(bf16[1024,1024]{1,0:T(8,128)(2,1)} %param.6), channel_id=1, source_target_pairs={{0,1},{1,0},{2,3},{3,2},{4,5},{5,4},{6,7},{7,6},{8,9},{9,8},{10,11... | collective-permute-start | bytes 6291464 | tf_op jit(solution)/shard_map/ppermute | solution.py:74
  19.1 16.4 %collective-permute-start.3 = (bf16[1024,256]{1,0:T(8,128)(2,1)S(1)}, bf16[1024,256]{1,0:T(8,128)(2,1)S(1)}, u32[]{:S(2)}, u32[]{:S(2)}) collective-permute-start(bf16[1024,256]{1,0:T(8,128)(2,1)S(1)} %collective-permute-done.1), channel_id=1, source_target_pairs={{0,8},{1,9},{4,12},{5,13},{10,2},{11,3},{14,6},{15,7},{16,24},{17,... | collective-permute-start | bytes 1572872 | tf_op jit(solution)/shard_map/ppermute | solution.py:77
  32.8 12.8 %collective-permute-start.5 = (bf16[1024,256]{1,0:T(8,128)(2,1)S(1)}, bf16[1024,256]{1,0:T(8,128)(2,1)S(1)}, u32[]{:S(2)}, u32[]{:S(2)}) collective-permute-start(bf16[1024,256]{1,0:T(8,128)(2,1)S(1)} %broadcast_select_fusion.16), channel_id=1, source_target_pairs={{0,2},{1,3},{2,0},{3,1},{4,6},{5,7},{6,4},{7,5},{8,10},{9,11},{10,... | collective-permute-start | bytes 1572872 | tf_op jit(solution)/shard_map/ppermute | solution.py:68
  45.6 26.0 %collective-permute-start.7 = (bf16[1024,256]{1,0:T(8,128)(2,1)S(1)}, bf16[1024,256]{1,0:T(8,128)(2,1)}, u32[]{:S(2)}, u32[]{:S(2)}) collective-permute-start(bf16[1024,256]{1,0:T(8,128)(2,1)S(1)} %collective-permute-done.5), channel_id=1, source_target_pairs={{2,10},{3,11},{6,14},{7,15},{8,0},{9,1},{12,4},{13,5},{18,26},{19,... | collective-permute-start | bytes 1572872 | tf_op jit(solution)/shard_map/ppermute | solution.py:80
  47.9 23.8 %collective-permute-start.8 = (bf16[1024,256]{1,0:T(8,128)(2,1)S(1)}, bf16[1024,256]{1,0:T(8,128)(2,1)S(1)}, u32[]{:S(2)}, u32[]{:S(2)}) collective-permute-start(bf16[1024,256]{1,0:T(8,128)(2,1)S(1)} %get-tuple-element.56), channel_id=1, source_target_pairs={{0,4},{1,5},{2,6},{3,7},{4,0},{5,1},{6,2},{7,3},{8,12},{9,13},{10,... | collective-permute-start | bytes 1572872 | tf_op jit(solution)/shard_map/ppermute | solution.py:71
  50.4 93.5 %collective-permute-start.20 = (bf16[1024,512]{1,0:T(8,128)(2,1)}, bf16[1024,512]{1,0:T(8,128)(2,1)}, u32[]{:S(2)}, u32[]{:S(2)}) collective-permute-start(bf16[1024,512]{1,0:T(8,128)(2,1)} %param.5), channel_id=1, source_target_pairs={{0,1},{1,0},{2,3},{3,2},{4,5},{5,4},{6,7},{7,6},{8,9},{9,8},{10,11... | collective-permute-start | bytes 3145736 | tf_op jit(solution)/shard_map/ppermute | solution.py:74
  51.1 27.3 %collective-permute-start.6 = (bf16[1024,256]{1,0:T(8,128)(2,1)S(1)}, bf16[1024,256]{1,0:T(8,128)(2,1)S(1)}, u32[]{:S(2)}, u32[]{:S(2)}) collective-permute-start(bf16[1024,256]{1,0:T(8,128)(2,1)S(1)} %get-tuple-element.29), channel_id=1, source_target_pairs={{0,8},{1,9},{4,12},{5,13},{10,2},{11,3},{14,6},{15,7},{16,24},{17,... | collective-permute-start | bytes 1572872 | tf_op jit(solution)/shard_map/ppermute | solution.py:77
  72.8 12.6 %collective-permute-start.9 = (bf16[1024,256]{1,0:T(8,128)(2,1)S(1)}, bf16[1024,256]{1,0:T(8,128)(2,1)S(1)}, u32[]{:S(2)}, u32[]{:S(2)}) collective-permute-start(bf16[1024,256]{1,0:T(8,128)(2,1)S(1)} %broadcast_select_fusion.14), channel_id=1, source_target_pairs={{0,4},{1,5},{2,6},{3,7},{4,0},{5,1},{6,2},{7,3},{8,12},{9,13},{10,... | collective-permute-start | bytes 1572872 | tf_op jit(solution)/shard_map/ppermute | solution.py:71
  76.9 23.6 %collective-permute-start.11 = (f32[1024,256]{0,1:T(8,128)S(1)}, f32[1024,256]{0,1:T(8,128)S(1)}, u32[]{:S(2)}, u32[]{:S(2)}) collective-permute-start(f32[1024,256]{0,1:T(8,128)S(1)} %convolution_add_fusion.2), channel_id=1, source_target_pairs={{0,2},{1,3},{2,0},{3,1},{4,6},{5,7},{6,4},{7,5},{8,10},{9,11},{10,... | collective-permute-start | bytes 3145736 | tf_op jit(solution)/shard_map/ppermute | solution.py:68
  78.4 22.1 %collective-permute-start.12 = (bf16[1024,256]{1,0:T(8,128)(2,1)S(1)}, bf16[1024,256]{1,0:T(8,128)(2,1)S(1)}, u32[]{:S(2)}, u32[]{:S(2)}) collective-permute-start(bf16[1024,256]{1,0:T(8,128)(2,1)S(1)} %get-tuple-element.32), channel_id=1, source_target_pairs={{0,8},{1,9},{4,12},{5,13},{10,2},{11,3},{14,6},{15,7},{16,24},{17,... | collective-permute-start | bytes 1572872 | tf_op jit(solution)/shard_map/ppermute | solution.py:77
  85.3 26.6 %collective-permute-start.15 = (bf16[1024,256]{1,0:T(8,128)(2,1)S(1)}, bf16[1024,256]{1,0:T(8,128)(2,1)S(1)}, u32[]{:S(2)}, u32[]{:S(2)}) collective-permute-start(bf16[1024,256]{1,0:T(8,128)(2,1)S(1)} %get-tuple-element.47), channel_id=1, source_target_pairs={{0,1},{1,0},{2,3},{3,2},{4,5},{5,4},{6,7},{7,6},{8,9},{9,8},{10,11... | collective-permute-start | bytes 1572872 | tf_op jit(solution)/shard_map/ppermute | solution.py:74
  85.4 21.4 %collective-permute-start.10 = (bf16[1024,256]{1,0:T(8,128)(2,1)S(1)}, bf16[1024,256]{1,0:T(8,128)(2,1)S(1)}, u32[]{:S(2)}, u32[]{:S(2)}) collective-permute-start(bf16[1024,256]{1,0:T(8,128)(2,1)S(1)} %broadcast_select_fusion.13), channel_id=1, source_target_pairs={{0,4},{1,5},{2,6},{3,7},{4,0},{5,1},{6,2},{7,3},{8,12},{9,13},{10,... | collective-permute-start | bytes 1572872 | tf_op jit(solution)/shard_map/ppermute | solution.py:71
  100.5 19.7 %collective-permute-start.17 = (bf16[1024,512]{1,0:T(8,128)(2,1)S(1)}, bf16[1024,512]{1,0:T(8,128)(2,1)S(1)}, u32[]{:S(2)}, u32[]{:S(2)}) collective-permute-start(bf16[1024,512]{1,0:T(8,128)(2,1)S(1)} %pad_maximum_fusion), channel_id=1, source_target_pairs={{0,1},{1,0},{2,3},{3,2},{4,5},{5,4},{6,7},{7,6},{8,9},{9,8},{10,11... | collective-permute-start | bytes 3145736 | tf_op jit(solution)/shard_map/ppermute | solution.py:74
  100.5 19.7 %collective-permute-start.16 = (bf16[1024,256]{1,0:T(8,128)(2,1)S(1)}, bf16[1024,256]{1,0:T(8,128)(2,1)S(1)}, u32[]{:S(2)}, u32[]{:S(2)}) collective-permute-start(bf16[1024,256]{1,0:T(8,128)(2,1)S(1)} %get-tuple-element.49), channel_id=1, source_target_pairs={{0,1},{1,0},{2,3},{3,2},{4,5},{5,4},{6,7},{7,6},{8,9},{9,8},{10,11... | collective-permute-start | bytes 1572872 | tf_op jit(solution)/shard_map/ppermute | solution.py:74
  106.9 17.7 %collective-permute-start.13 = (bf16[1024,256]{1,0:T(8,128)(2,1)S(1)}, bf16[1024,256]{1,0:T(8,128)(2,1)S(1)}, u32[]{:S(2)}, u32[]{:S(2)}) collective-permute-start(bf16[1024,256]{1,0:T(8,128)(2,1)S(1)} %broadcast_select_fusion.12), channel_id=1, source_target_pairs={{0,4},{1,5},{2,6},{3,7},{4,0},{5,1},{6,2},{7,3},{8,12},{9,13},{10,... | collective-permute-start | bytes 1572872 | tf_op jit(solution)/shard_map/ppermute | solution.py:71
  111.0 9.2 %copy-start = (bf16[1024,256]{1,0:T(8,128)(2,1)S(1)}, bf16[1024,256]{1,0:T(8,128)(2,1)}, u32[]{:S(2)}) copy-start(bf16[1024,256]{1,0:T(8,128)(2,1)} %get-tuple-element.57) | copy-start | bytes 1572868
  111.9 29.2 %collective-permute-start.14 = (f32[1024,256]{0,1:T(8,128)S(1)}, f32[1024,256]{0,1:T(8,128)S(1)}, u32[]{:S(2)}, u32[]{:S(2)}) collective-permute-start(f32[1024,256]{0,1:T(8,128)S(1)} %convolution_add_fusion), channel_id=1, source_target_pairs={{0,2},{1,3},{2,0},{3,1},{4,6},{5,7},{6,4},{7,5},{8,10},{9,11},{10,... | collective-permute-start | bytes 3145736 | tf_op jit(solution)/shard_map/ppermute | solution.py:68
  120.2 23.7 %collective-permute-start.18 = (bf16[1024,256]{1,0:T(8,128)(2,1)}, bf16[1024,256]{1,0:T(8,128)(2,1)}, u32[]{:S(2)}, u32[]{:S(2)}) collective-permute-start(bf16[1024,256]{1,0:T(8,128)(2,1)} %get-tuple-element.43), channel_id=1, source_target_pairs={{0,1},{1,0},{2,3},{3,2},{4,5},{5,4},{6,7},{7,6},{8,9},{9,8},{10,11... | collective-permute-start | bytes 1572872 | tf_op jit(solution)/shard_map/ppermute | solution.py:74
  125.7 18.2 %collective-permute-start.19 = (bf16[1024,256]{1,0:T(8,128)(2,1)}, bf16[1024,256]{1,0:T(8,128)(2,1)}, u32[]{:S(2)}, u32[]{:S(2)}) collective-permute-start(bf16[1024,256]{1,0:T(8,128)(2,1)} %get-tuple-element.45), channel_id=1, source_target_pairs={{0,1},{1,0},{2,3},{3,2},{4,5},{5,4},{6,7},{7,6},{8,9},{9,8},{10,11... | collective-permute-start | bytes 1572872 | tf_op jit(solution)/shard_map/ppermute | solution.py:74
  142.1 1.8 %copy-start.1 = (bf16[1024,256]{1,0:T(8,128)(2,1)S(1)}, bf16[1024,256]{1,0:T(8,128)(2,1)}, u32[]{:S(2)}) copy-start(bf16[1024,256]{1,0:T(8,128)(2,1)} %get-tuple-element.44) | copy-start | bytes 1572868

commit v4 on v2

--- a/solution.py
+++ b/solution.py
@@ -85,54 +85,81 @@
         home = z // 2 == s
         mine = z % 2 == c
         half = expected_cot.shape[1] // 2
-        ep, eq = expected_cot[:, :half], expected_cot[:, half:]
-        vp, vq = value_next[:, :half], value_next[:, half:]
+        quarter = half // 2
 
-        x1 = cross(jnp.where(home, vp, ep))
-        jq = away_jump(eq)
-        t_other = swap(transition)
-        v_other = swap(value_next)
-        t_near, t_next = jnp.where(mine, transition, t_other), jnp.where(mine, t_other, transition)
+        def columns(array, start, stop):
+            return array[:, start * quarter : stop * quarter]
+
+        def together(arrays, *gates):
+            return lax.optimization_barrier(tuple(arrays) + gates)[: len(arrays)]
+
+        e_1, e_q = columns(expected_cot, 0, 1), columns(expected_cot, 2, 4)
+        first, e_1, e_q = together((jnp.where(home, columns(value_next, 0, 1), e_1), e_1, e_q))
+        c1 = cross(first)
+        ja1 = home_jump(e_1)
+        jq = away_jump(e_q)
+        v, e = together((columns(value_next, 1, 2), columns(expected_cot, 1, 2)), c1)
+        c2 = cross(jnp.where(home, v, e))
+        jp1 = home_jump(after(c1, ja1))
+        t_other = swap(after(transition, c1))
+        jq_late, vp = together((jq, columns(value_next, 0, 2)), c2)
+        c3 = cross(jnp.where(home, jq_late, vp))
+        x, j = together((c1, jp1), c2)
+        b1 = jnp.where(home, x, j)
+        b1_next = step(b1)
+        jp2 = home_jump(after(c2, jp1))
+        jq2 = away_jump(c3)
+        t, t_o = together((transition, t_other), b1_next)
+        t_near, t_next = jnp.where(mine, t, t_o), jnp.where(mine, t_o, t)
 
         def adjoint_of(near, far):
             return tdot(t_near, near) + tdot(t_next, far)
 
+        part1 = cross(after(adjoint_of(b1, b1_next), c3))
+        c4 = cross(after(columns(value_next, 2, 4), c3))
+        x, j = together((c2, jp2), b1_next)
+        b2 = jnp.where(home, x, j)
+        b2_next = step(b2)
+        ja2 = home_jump(after(columns(expected_cot, 1, 4), jp2, b1_next))
+        e, j = together((columns(expected_cot, 0, 1), ja1), b2_next)
+        a1 = jnp.where(home, e, j)
+        a1_next = step(a1)
+        part2 = cross(after(adjoint_of(b2, b2_next), part1, c4))
+        j, x = together((jq2, c3), a1_next, part1)
+        bq = jnp.where(home, j, x)
+        bq_next = step(bq)
+        v_other = swap(after(value_next, b2_next))
+        sum3 = adjoint_of(bq, bq_next)
+        part3 = cross(after(columns(sum3, 0, 1), part2))
+        part4 = cross(after(columns(sum3, 1, 2), part3))
+        e, j = together((columns(expected_cot, 1, 4), ja2), bq_next, part2, sum3)
+        a2 = jnp.where(home, e, j)
+        a2_next = step(a2)
+
         def own_and_swapped(near, far):
             return jnp.where(mine, near, far), swap(jnp.where(mine, far, near))
 
-        x2 = cross(after(jnp.where(home, vq, vp), x1))
-        jp = home_jump(x1)
-        x3 = cross(after(jnp.where(home, jq, vq), x2))
-        jq2 = away_jump(x3)
-        bp = jnp.where(home, x1, jp)
-        bp_next = step(bp)
-        jap = home_jump(after(ep, jp))
-        part_p = cross(adjoint_of(bp, bp_next))
-        bq = jnp.where(home, jq2, x3)
-        bq_next = step(after(bq, bp_next))
-        part_q = cross(adjoint_of(bq, bq_next))
-        ap = jnp.where(home, ep, jap)
-        ap_next = step(after(ap, bq_next))
-        jaq = home_jump(after(eq, jap))
-        aq = jnp.where(home, eq, jaq)
-        aq_next = step(after(aq, ap_next))
-
-        v_across = jnp.concatenate([jnp.where(home, x2, x1), jnp.where(home, x3, x2)], 1)
-        v_across_other = swap(v_across)
-        bp_own, bp_swapped = own_and_swapped(bp, bp_next)
+        v_across = jnp.concatenate([jnp.where(home, c3, jnp.concatenate([c1, c2], 1)), c4], 1)
+        v_across_other = swap(after(v_across, b2_next))
+        bp_own, bp_swapped = own_and_swapped(
+            jnp.concatenate([b1, b2], 1), jnp.concatenate([b1_next, b2_next], 1)
+        )
         bq_own, bq_swapped = own_and_swapped(bq, bq_next)
         grad = dott(
             jnp.concatenate([bp_own, bq_own, bp_swapped, bq_swapped], 1),
             jnp.concatenate([v_across, v_across_other], 1),
         )
-        ap_own, ap_swapped = own_and_swapped(ap, ap_next)
-        aq_own, aq_swapped = own_and_swapped(aq, aq_next)
-        grad = grad + dott(
-            jnp.concatenate([ap_own, aq_own, ap_swapped, aq_swapped], 1),
+        a1_own, a1_swapped = own_and_swapped(a1, a1_next)
+        a2_near, a2_far = together((a2, a2_next), grad, part3)
+        a2_own, a2_swapped = own_and_swapped(a2_near, a2_far)
+        grad = df * (grad + dott(
+            jnp.concatenate([a1_own, a2_own, a1_swapped, a2_swapped], 1),
             jnp.concatenate([value_next, v_other], 1),
-        )
-        adjoint = jnp.concatenate([adjoint_of(ap, ap_next) + part_p, adjoint_of(aq, aq_next) + part_q], 1)
-        return df * adjoint, df * grad
+        ))
+        own = adjoint_of(jnp.concatenate([a1, a2], 1), jnp.concatenate([a1_next, a2_next], 1))
+        own, part4, grad = together((own, part4, grad))
+        adjoint = df * (own + jnp.concatenate([part1, part2, part3, part4], 1))
+        return adjoint, grad
 
     return shards
 

time: 198 us -> 146 us (0.74)
  waiting for transfers between devices: 92.5 us -> 59.7 us
  starting transfers between devices: 71.3 us -> 55.4 us
    ppermute x5 -> x8, waiting for transfers between devices: 48.4 us -> 23.7 us  [cross(): return lax.ppermute(a, AXES, cross_pairs)]
    ppermute x2, waiting for transfers between devices: 32.3 us -> 11.8 us  [away_jump(): return lax.ppermute(a, AXES, away_jump_pairs)]
    ppermute x4 -> x5, starting transfers between devices: 37.8 us -> 19 us  [step(): return lax.ppermute(a, AXES, step_pairs)]
    ppermute x3 -> x4, waiting for transfers between devices: 0.68 us -> 7.91 us  [home_jump(): return lax.ppermute(a, AXES, home_jump_pairs)]
    ppermute x3 -> x4, starting transfers between devices: 11.7 us -> 18.2 us  [home_jump(): return lax.ppermute(a, AXES, home_jump_pairs)]
    ppermute x4 -> x5, waiting for transfers between devices: 11.1 us -> 16.2 us  [step(): return lax.ppermute(a, AXES, step_pairs)]
    ppermute x5 -> x8, starting transfers between devices: 18.5 us -> 14.3 us  [cross(): return lax.ppermute(a, AXES, cross_pairs)]
    select_n x4, other arithmetic: 4.45 us -> 0.48 us  [own_and_swapped(): return (jnp.where(mine, near, far), swap(jnp.where(mine, far, near)))]
  transfers between devices with their start and end apart: 21 -> 26, of which waited for: 10 -> 13; matrix products, arithmetic and copies ran while one was open for 11% -> 17% of each run, Pallas kernels for 0% -> 0%
where the time goes in v4:
time: 146 us; the launch traced here: 145 us
  waiting for transfers between devices  59.7 us (41%)
  starting transfers between devices  55.4 us (38%)
  matrix products  14.8 us (10%)
  other arithmetic  9.3 us (6%)
  local copies, waits for them, and re-layouts  4.22 us (3%)
  between operations  1.77 us (1%)
    ppermute x8, waiting for transfers between devices, cross(): return lax.ppermute(a, AXES, cross_pairs)  23.7 us
    ppermute x5, starting transfers between devices, step(): return lax.ppermute(a, AXES, step_pairs)  19 us
    ppermute x4, starting transfers between devices, home_jump(): return lax.ppermute(a, AXES, home_jump_pairs)  18.2 us
    ppermute x5, waiting for transfers between devices, step(): return lax.ppermute(a, AXES, step_pairs)  16.2 us
    ppermute x8, starting transfers between devices, cross(): return lax.ppermute(a, AXES, cross_pairs)  14.3 us
    ppermute x2, waiting for transfers between devices, away_jump(): return lax.ppermute(a, AXES, away_jump_pairs)  11.8 us
    dot_general x8, matrix products, tdot(): lax.dot_general(a, b, (((0,), (0,)), ((), ())), preferred_element_type=jn...  8 us
    ppermute x4, waiting for transfers between devices, home_jump(): return lax.ppermute(a, AXES, home_jump_pairs)  7.91 us
  transfers between devices with their start and end apart: 26, of which 13 were waited for; matrix products, arithmetic and copies ran while one was open for 17% of the time, Pallas kernels for 0%

profile of v4, /device:TPU:0, one launch (start us, length us, event | category | flops | bytes accessed | tf_op | source)
XLA Modules:
  0.0 145.2 jit_solution(17887411407399146465)
XLA Ops:
  0.7 1.2 slice.34
  1.8 1.3 fusion.42
  3.1 3.0 %collective-permute-start = (bf16[1024,128]{1,0:T(8,128)(2,1)S(1)}, bf16[1024,128]{1,0:T(8,128)(2,1)S(1)}, u32[]{:S(2)}, u32[]{:S(2)}) collective-permute-start(bf16[1024,128]{1,0:T(8,128)(2,1)S(1)} %get-tuple-element.37), channel_id=1, source_target_pairs={{0,2},{1,3},{2,0},{3,1},{4,6},{5,7},{6,4},{7,5},{8,10},{9,11},{10,... | collective-permute-start | bytes 786440 | tf_op jit(solution)/shard_map/ppermute | solution.py:68
  6.1 4.5 %collective-permute-start.2 = (bf16[1024,128]{1,0:T(8,128)(2,1)S(1)}, bf16[1024,128]{1,0:T(8,128)(2,1)S(1)}, u32[]{:S(2)}, u32[]{:S(2)}) collective-permute-start(bf16[1024,128]{1,0:T(8,128)(2,1)S(1)} %get-tuple-element.50), channel_id=1, source_target_pairs={{0,8},{1,9},{4,12},{5,13},{10,2},{11,3},{14,6},{15,7},{16,24},{17,... | collective-permute-start | bytes 786440 | tf_op jit(solution)/shard_map/ppermute | solution.py:77
  10.6 1.8 %collective-permute-done = bf16[1024,128]{1,0:T(8,128)(2,1)S(1)} collective-permute-done((bf16[1024,128]{1,0:T(8,128)(2,1)S(1)}, bf16[1024,128]{1,0:T(8,128)(2,1)S(1)}, u32[]{:S(2)}, u32[]{:S(2)}) %collective-permute-start) | collective-permute-done | bytes 262176 | tf_op jit(solution)/shard_map/ppermute | solution.py:68
  12.5 1.3 collective-permute-start.9
  13.7 2.2 %collective-permute-done.2 = bf16[1024,128]{1,0:T(8,128)(2,1)S(1)} collective-permute-done((bf16[1024,128]{1,0:T(8,128)(2,1)S(1)}, bf16[1024,128]{1,0:T(8,128)(2,1)S(1)}, u32[]{:S(2)}, u32[]{:S(2)}) %collective-permute-start.2) | collective-permute-done | bytes 262176 | tf_op jit(solution)/shard_map/ppermute | solution.py:77
  15.9 5.3 %collective-permute-start.3 = (bf16[1024,128]{1,0:T(8,128)(2,1)S(1)}, bf16[1024,128]{1,0:T(8,128)(2,1)S(1)}, u32[]{:S(2)}, u32[]{:S(2)}) collective-permute-start(bf16[1024,128]{1,0:T(8,128)(2,1)S(1)} %collective-permute-done), channel_id=1, source_target_pairs={{0,8},{1,9},{4,12},{5,13},{10,2},{11,3},{14,6},{15,7},{16,24},{17,... | collective-permute-start | bytes 786440 | tf_op jit(solution)/shard_map/ppermute | solution.py:77
  21.4 2.7 %collective-permute-start.4 = (bf16[1024,128]{1,0:T(8,128)(2,1)S(1)}, bf16[1024,128]{1,0:T(8,128)(2,1)S(1)}, u32[]{:S(2)}, u32[]{:S(2)}) collective-permute-start(bf16[1024,128]{1,0:T(8,128)(2,1)S(1)} %broadcast_select_fusion.16), channel_id=1, source_target_pairs={{0,2},{1,3},{2,0},{3,1},{4,6},{5,7},{6,4},{7,5},{8,10},{9,11},{10,... | collective-permute-start | bytes 786440 | tf_op jit(solution)/shard_map/ppermute | solution.py:68
  24.0 0.9 fusion.41
  24.9 0.7 collective-permute-done.3
  25.6 3.8 %collective-permute-done.4 = bf16[1024,128]{1,0:T(8,128)(2,1)S(1)} collective-permute-done((bf16[1024,128]{1,0:T(8,128)(2,1)S(1)}, bf16[1024,128]{1,0:T(8,128)(2,1)S(1)}, u32[]{:S(2)}, u32[]{:S(2)}) %collective-permute-start.4) | collective-permute-done | bytes 262176 | tf_op jit(solution)/shard_map/ppermute | solution.py:68
  29.5 12.6 %collective-permute-start.5 = (bf16[1024,128]{1,0:T(8,128)(2,1)S(1)}, bf16[1024,128]{1,0:T(8,128)(2,1)S(1)}, u32[]{:S(2)}, u32[]{:S(2)}) collective-permute-start(bf16[1024,128]{1,0:T(8,128)(2,1)S(1)} %broadcast_select_fusion.15), channel_id=1, source_target_pairs={{0,4},{1,5},{2,6},{3,7},{4,0},{5,1},{6,2},{7,3},{8,12},{9,13},{10,... | collective-permute-start | bytes 786440 | tf_op jit(solution)/shard_map/ppermute | solution.py:71
  42.1 2.9 %collective-permute-start.6 = (bf16[1024,128]{1,0:T(8,128)(2,1)S(1)}, bf16[1024,128]{1,0:T(8,128)(2,1)S(1)}, u32[]{:S(2)}, u32[]{:S(2)}) collective-permute-start(bf16[1024,128]{1,0:T(8,128)(2,1)S(1)} %collective-permute-done.4), channel_id=1, source_target_pairs={{0,8},{1,9},{4,12},{5,13},{10,2},{11,3},{14,6},{15,7},{16,24},{17,... | collective-permute-start | bytes 786440 | tf_op jit(solution)/shard_map/ppermute | solution.py:77
  45.0 0.9 broadcast_select_fusion.10
  45.9 3.0 %collective-permute-done.5 = bf16[1024,128]{1,0:T(8,128)(2,1)S(1)} collective-permute-done((bf16[1024,128]{1,0:T(8,128)(2,1)S(1)}, bf16[1024,128]{1,0:T(8,128)(2,1)S(1)}, u32[]{:S(2)}, u32[]{:S(2)}) %collective-permute-start.5) | collective-permute-done | bytes 262176 | tf_op jit(solution)/shard_map/ppermute | solution.py:71
  48.8 5.0 %collective-permute-done.6 = bf16[1024,128]{1,0:T(8,128)(2,1)S(1)} collective-permute-done((bf16[1024,128]{1,0:T(8,128)(2,1)S(1)}, bf16[1024,128]{1,0:T(8,128)(2,1)S(1)}, u32[]{:S(2)}, u32[]{:S(2)}) %collective-permute-start.6) | collective-permute-done | bytes 262176 | tf_op jit(solution)/shard_map/ppermute | solution.py:77
  53.8 1.9 %collective-permute-start.7 = (bf16[1024,128]{1,0:T(8,128)(2,1)S(1)}, bf16[1024,128]{1,0:T(8,128)(2,1)}, u32[]{:S(2)}, u32[]{:S(2)}) collective-permute-start(bf16[1024,128]{1,0:T(8,128)(2,1)S(1)} %broadcast_select_fusion.14), channel_id=1, source_target_pairs={{0,4},{1,5},{2,6},{3,7},{4,0},{5,1},{6,2},{7,3},{8,12},{9,13},{10,... | collective-permute-start | bytes 786440 | tf_op jit(solution)/shard_map/ppermute | solution.py:71
  55.7 0.1 slice.37
  55.8 5.4 %collective-permute-start.8 = (bf16[1024,384]{1,0:T(8,128)(2,1)S(1)}, bf16[1024,384]{1,0:T(8,128)(2,1)S(1)}, u32[]{:S(2)}, u32[]{:S(2)}) collective-permute-start(bf16[1024,384]{1,0:T(8,128)(2,1)S(1)} %slice.37), channel_id=1, source_target_pairs={{0,8},{1,9},{4,12},{5,13},{10,2},{11,3},{14,6},{15,7},{16,24},{17,... | collective-permute-start | bytes 2359304 | tf_op jit(solution)/shard_map/ppermute | solution.py:77
  61.2 1.0 constant_dynamic-update-slice_fusion.1
  62.2 0.2 collective-permute-done.7
  62.4 1.0 broadcast_select_fusion.13
  63.4 2.7 %collective-permute-start.12 = (bf16[1024,128]{1,0:T(8,128)(2,1)S(1)}, bf16[1024,128]{1,0:T(8,128)(2,1)S(1)}, u32[]{:S(2)}, u32[]{:S(2)}) collective-permute-start(bf16[1024,128]{1,0:T(8,128)(2,1)S(1)} %broadcast_select_fusion.13), channel_id=1, source_target_pairs={{0,4},{1,5},{2,6},{3,7},{4,0},{5,1},{6,2},{7,3},{8,12},{9,13},{10,... | collective-permute-start | bytes 786440 | tf_op jit(solution)/shard_map/ppermute | solution.py:71
  66.0 2.1 %collective-permute-start.15 = (bf16[1024,256]{1,0:T(8,128)(2,1)}, bf16[1024,256]{1,0:T(8,128)(2,1)S(1)}, u32[]{:S(2)}, u32[]{:S(2)}) collective-permute-start(bf16[1024,256]{1,0:T(8,128)(2,1)} %get-tuple-element.59), channel_id=1, source_target_pairs={{0,2},{1,3},{2,0},{3,1},{4,6},{5,7},{6,4},{7,5},{8,10},{9,11},{10,... | collective-permute-start | bytes 1572872 | tf_op jit(solution)/shard_map/ppermute | solution.py:68
  68.1 1.3 collective-permute-start.11
  69.4 1.0 constant_dynamic-update-slice_fusion
  70.5 2.5 %broadcast_select_fusion.1 = (bf16[1024,1024]{1,0:T(8,128)(2,1)S(1)}, bf16[1024,1024]{1,0:T(8,128)(2,1)S(1)}) fusion(bf16[1024,1024]{1,0:T(8,128)(2,1)} %param.6, bf16[1024,1024]{1,0:T(8,128)(2,1)} %collective-permute-done.1, pred[]{:T(512)S(6)} %eq.8), kind=kLoop, calls=%fused_computation.28 | loop fusion | flops 2097152 | bytes 8388609 | tf_op jit(solution)/shard_map/jit(_where)/select_n | solution.py:113
  73.0 0.7 fusion.43
  73.7 0.8 convolution_add_fusion.3
  74.5 5.5 %collective-permute-start.13 = (f32[1024,128]{1,0:T(8,128)S(1)}, f32[1024,128]{1,0:T(8,128)S(1)}, u32[]{:S(2)}, u32[]{:S(2)}) collective-permute-start(f32[1024,128]{1,0:T(8,128)S(1)} %convolution_add_fusion.3), channel_id=1, source_target_pairs={{0,2},{1,3},{2,0},{3,1},{4,6},{5,7},{6,4},{7,5},{8,10},{9,11},{10,... | collective-permute-start | bytes 1572872 | tf_op jit(solution)/shard_map/ppermute | solution.py:68
  80.0 0.2 broadcast_select_fusion.8
  80.3 1.2 maximum_select_fusion
  81.5 0.1 collective-permute-start.20
  81.6 0.1 pad_maximum_fusion
  81.6 0.6 collective-permute-start.22
  82.2 11.8 %collective-permute-done.11 = bf16[1024,256]{1,0:T(8,128)(2,1)S(1)} collective-permute-done((bf16[1024,256]{1,0:T(8,128)(2,1)}, bf16[1024,256]{1,0:T(8,128)(2,1)S(1)}, u32[]{:S(2)}, u32[]{:S(2)}) %collective-permute-start.11) | collective-permute-done | bytes 524320 | tf_op jit(solution)/shard_map/ppermute | solution.py:80
  94.1 0.1 broadcast_select_fusion.9
  94.1 0.1 collective-permute-start.14
  94.2 1.7 %fusion.44 = f32[1024,128]{1,0:T(8,128)S(1)} fusion(bf16[1024,1024]{1,0:T(8,128)(2,1)S(1)} %get-tuple-element.73, bf16[1024,128]{1,0:T(8,128)(2,1)} %collective-permute-done.7), kind=kOutput, calls=%fused_computation.69 | convolution fusion | flops 268435456 | bytes 2883584 | tf_op jit(solution)/shard_map/dot_general | solution.py:34
  95.9 0.8 convolution_add_fusion.2
  96.7 0.2 collective-permute-start.16
  96.9 9.1 %collective-permute-done.14 = bf16[1024,256]{1,0:T(8,128)(2,1)S(1)} collective-permute-done((bf16[1024,256]{1,0:T(8,128)(2,1)S(1)}, bf16[1024,256]{1,0:T(8,128)(2,1)S(1)}, u32[]{:S(2)}, u32[]{:S(2)}) %collective-permute-start.14) | collective-permute-done | bytes 524320 | tf_op jit(solution)/shard_map/ppermute | solution.py:71
  106.0 0.7 fusion.45
  106.8 0.8 convolution_add_fusion.1
  107.5 1.0 collective-permute-done.16
  108.5 0.1 broadcast_select_fusion.7
  108.6 0.1 collective-permute-start.21
  108.7 0.1 broadcast_select_fusion.4
  108.8 1.8 %collective-permute-start.17 = (bf16[1024,384]{1,0:T(8,128)(2,1)S(1)}, bf16[1024,384]{1,0:T(8,128)(2,1)S(1)}, u32[]{:S(2)}, u32[]{:S(2)}) collective-permute-start(bf16[1024,384]{1,0:T(8,128)(2,1)S(1)} %broadcast_select_fusion.4), channel_id=1, source_target_pairs={{0,4},{1,5},{2,6},{3,7},{4,0},{5,1},{6,2},{7,3},{8,12},{9,13},{10,... | collective-permute-start | bytes 2359304 | tf_op jit(solution)/shard_map/ppermute | solution.py:71
  110.7 0.4 collective-permute-start.18
  111.7 0.1 collective-permute-start.25
  111.8 2.4 %fusion = f32[1024,1024]{1,0:T(8,128)S(1)} fusion(bf16[1024,256]{1,0:T(8,128)(2,1)S(1)} %collective-permute-done.21, bf16[1024,256]{1,0:T(8,128)(2,1)S(1)} %collective-permute-done.20, bf16[1024,256]{1,0:T(8,128)(2,1)S(1)} %get-tuple-element.78, bf16[1024,256]{1,0:T(8,128)(2,1)S(1)} %get-tuple-element.76, bf16[1024,512]{1,0:T(8,128)(2,1)S(1)} %collective-permute-done.22, ...), kind=kOutput, calls=%fused_computation.1 | convolution fusion | flops 2162163712 | bytes 8388608 | tf_op jit(solution)/shard_map/dot_general | solution.py:38
  114.2 10.6 %collective-permute-done.18 = f32[1024,128]{1,0:T(8,128)S(1)} collective-permute-done((f32[1024,128]{1,0:T(8,128)S(1)}, f32[1024,128]{1,0:T(8,128)S(1)}, u32[]{:S(2)}, u32[]{:S(2)}) %collective-permute-start.18) | collective-permute-done | bytes 524320 | tf_op jit(solution)/shard_map/ppermute | solution.py:68
  124.8 4.0 %collective-permute-done.17 = bf16[1024,384]{1,0:T(8,128)(2,1)S(1)} collective-permute-done((bf16[1024,384]{1,0:T(8,128)(2,1)S(1)}, bf16[1024,384]{1,0:T(8,128)(2,1)S(1)}, u32[]{:S(2)}, u32[]{:S(2)}) %collective-permute-start.17) | collective-permute-done | bytes 786464 | tf_op jit(solution)/shard_map/ppermute | solution.py:71
  128.8 0.1 broadcast_select_fusion.3
  128.9 0.1 collective-permute-start.24
  129.1 0.6 collective-permute-start.23
  129.6 0.5 collective-permute-start.19
  130.1 1.3 fusion.32
  131.4 1.3 convolution_add_fusion
  132.7 4.4 %add_multiply_fusion = f32[1024,1024]{1,0:T(8,128)} fusion(f32[1024,1024]{1,0:T(8,128)S(1)} %fusion, f32[]{:T(128)} %bitcast, bf16[1024,512]{1,0:T(8,128)(2,1)S(1)} %collective-permute-done.25, bf16[1024,512]{1,0:T(8,128)(2,1)S(1)} %copy-done.1, bf16[1024,384]{1,0:T(8,128)(2,1)S(1)} %collective-permute-done.24, ...), kind=kOutput, calls=%fused_computation | convolution fusion | flops 2162163712 | bytes 12582916 | tf_op jit(solution)/shard_map/dot_general | solution.py:38
  137.1 6.4 %collective-permute-done.19 = f32[1024,128]{1,0:T(8,128)S(1)} collective-permute-done((f32[1024,128]{1,0:T(8,128)S(1)}, f32[1024,128]{1,0:T(8,128)S(1)}, u32[]{:S(2)}, u32[]{:S(2)}) %collective-permute-start.19) | collective-permute-done | bytes 524320 | tf_op jit(solution)/shard_map/ppermute | solution.py:68
  143.5 1.6 %fusion.24 = f32[1024,512]{1,0:T(8,128)} fusion(f32[1024,512]{1,0:T(8,128)S(1)} %convolution_add_fusion, f32[1024,128]{1,0:T(8,128)S(1)} %collective-permute-done.19, f32[1024,128]{1,0:T(8,128)S(1)} %collective-permute-done.18, f32[1024,128]{1,0:T(8,128)S(1)} %collective-permute-done.16, f32[1024,128]{1,0:T(8,128)S(1)} %collective-permute-done.13, f32[]{:T(128)} %bitcast), kind=kLoop, calls=%fused_computation.26 | loop fusion | flops 2621440 | bytes 6291460 | tf_op jit(solution)/shard_map/mul | solution.py:161
  (40 shorter events, 0.3 us)
Async XLA Ops:
  0.6 23.4 %copy-start.1 = (bf16[1024,512]{1,0:T(8,128)(2,1)S(1)}, bf16[1024,512]{1,0:T(8,128)(2,1)}, u32[]{:S(2)}) copy-start(bf16[1024,512]{1,0:T(8,128)(2,1)} %param.5) | copy-start | bytes 3145732
  3.1 18.2 %copy-start.4 = (bf16[1024,128]{1,0:T(8,128)(2,1)}, bf16[1024,128]{1,0:T(8,128)(2,1)S(1)}, u32[]{:S(2)}) copy-start(bf16[1024,128]{1,0:T(8,128)(2,1)S(1)} %get-tuple-element.50) | copy-start | bytes 786436
  3.1 9.3 %collective-permute-start = (bf16[1024,128]{1,0:T(8,128)(2,1)S(1)}, bf16[1024,128]{1,0:T(8,128)(2,1)S(1)}, u32[]{:S(2)}, u32[]{:S(2)}) collective-permute-start(bf16[1024,128]{1,0:T(8,128)(2,1)S(1)} %get-tuple-element.37), channel_id=1, source_target_pairs={{0,2},{1,3},{2,0},{3,1},{4,6},{5,7},{6,4},{7,5},{8,10},{9,11},{10,... | collective-permute-start | bytes 786440 | tf_op jit(solution)/shard_map/ppermute | solution.py:68
  6.1 9.8 %collective-permute-start.2 = (bf16[1024,128]{1,0:T(8,128)(2,1)S(1)}, bf16[1024,128]{1,0:T(8,128)(2,1)S(1)}, u32[]{:S(2)}, u32[]{:S(2)}) collective-permute-start(bf16[1024,128]{1,0:T(8,128)(2,1)S(1)} %get-tuple-element.50), channel_id=1, source_target_pairs={{0,8},{1,9},{4,12},{5,13},{10,2},{11,3},{14,6},{15,7},{16,24},{17,... | collective-permute-start | bytes 786440 | tf_op jit(solution)/shard_map/ppermute | solution.py:77
  12.4 33.4 %copy-start.5 = (bf16[1024,128]{1,0:T(8,128)(2,1)}, bf16[1024,128]{1,0:T(8,128)(2,1)S(1)}, u32[]{:S(2)}) copy-start(bf16[1024,128]{1,0:T(8,128)(2,1)S(1)} %collective-permute-done) | copy-start | bytes 786436
  12.4 58.0 %collective-permute-start.1 = (bf16[1024,1024]{1,0:T(8,128)(2,1)}, bf16[1024,1024]{1,0:T(8,128)(2,1)}, u32[]{:S(2)}, u32[]{:S(2)}) collective-permute-start(bf16[1024,1024]{1,0:T(8,128)(2,1)} %param.6), channel_id=1, source_target_pairs={{0,1},{1,0},{2,3},{3,2},{4,5},{5,4},{6,7},{7,6},{8,9},{9,8},{10,11... | collective-permute-start | bytes 6291464 | tf_op jit(solution)/shard_map/ppermute | solution.py:74
  12.5 32.6 %collective-permute-start.9 = (bf16[1024,256]{1,0:T(8,128)(2,1)S(1)}, bf16[1024,256]{1,0:T(8,128)(2,1)S(1)}, u32[]{:S(2)}, u32[]{:S(2)}) collective-permute-start(bf16[1024,256]{1,0:T(8,128)(2,1)S(1)} %slice.34), channel_id=1, source_target_pairs={{2,10},{3,11},{6,14},{7,15},{8,0},{9,1},{12,4},{13,5},{18,26},{19,... | collective-permute-start | bytes 1572872 | tf_op jit(solution)/shard_map/ppermute | solution.py:80
  15.9 5.4 %copy-start.9 = (bf16[1024,128]{1,0:T(8,128)(2,1)}, bf16[1024,128]{1,0:T(8,128)(2,1)S(1)}, u32[]{:S(2)}) copy-start(bf16[1024,128]{1,0:T(8,128)(2,1)S(1)} %collective-permute-done.2) | copy-start | bytes 786436
  15.9 9.7 %collective-permute-start.3 = (bf16[1024,128]{1,0:T(8,128)(2,1)S(1)}, bf16[1024,128]{1,0:T(8,128)(2,1)S(1)}, u32[]{:S(2)}, u32[]{:S(2)}) collective-permute-start(bf16[1024,128]{1,0:T(8,128)(2,1)S(1)} %collective-permute-done), channel_id=1, source_target_pairs={{0,8},{1,9},{4,12},{5,13},{10,2},{11,3},{14,6},{15,7},{16,24},{17,... | collective-permute-start | bytes 786440 | tf_op jit(solution)/shard_map/ppermute | solution.py:77
  21.4 8.1 %collective-permute-start.4 = (bf16[1024,128]{1,0:T(8,128)(2,1)S(1)}, bf16[1024,128]{1,0:T(8,128)(2,1)S(1)}, u32[]{:S(2)}, u32[]{:S(2)}) collective-permute-start(bf16[1024,128]{1,0:T(8,128)(2,1)S(1)} %broadcast_select_fusion.16), channel_id=1, source_target_pairs={{0,2},{1,3},{2,0},{3,1},{4,6},{5,7},{6,4},{7,5},{8,10},{9,11},{10,... | collective-permute-start | bytes 786440 | tf_op jit(solution)/shard_map/ppermute | solution.py:68
  24.9 30.8 %copy-start = (bf16[1024,512]{1,0:T(8,128)(2,1)S(1)}, bf16[1024,512]{1,0:T(8,128)(2,1)}, u32[]{:S(2)}) copy-start(bf16[1024,512]{1,0:T(8,128)(2,1)} %param.4) | copy-start | bytes 3145732
  29.5 24.4 %copy-start.7 = (bf16[1024,128]{1,0:T(8,128)(2,1)}, bf16[1024,128]{1,0:T(8,128)(2,1)S(1)}, u32[]{:S(2)}) copy-start(bf16[1024,128]{1,0:T(8,128)(2,1)S(1)} %collective-permute-done.4) | copy-start | bytes 786436
  29.5 19.3 %collective-permute-start.5 = (bf16[1024,128]{1,0:T(8,128)(2,1)S(1)}, bf16[1024,128]{1,0:T(8,128)(2,1)S(1)}, u32[]{:S(2)}, u32[]{:S(2)}) collective-permute-start(bf16[1024,128]{1,0:T(8,128)(2,1)S(1)} %broadcast_select_fusion.15), channel_id=1, source_target_pairs={{0,4},{1,5},{2,6},{3,7},{4,0},{5,1},{6,2},{7,3},{8,12},{9,13},{10,... | collective-permute-start | bytes 786440 | tf_op jit(solution)/shard_map/ppermute | solution.py:71
  42.1 11.7 %collective-permute-start.6 = (bf16[1024,128]{1,0:T(8,128)(2,1)S(1)}, bf16[1024,128]{1,0:T(8,128)(2,1)S(1)}, u32[]{:S(2)}, u32[]{:S(2)}) collective-permute-start(bf16[1024,128]{1,0:T(8,128)(2,1)S(1)} %collective-permute-done.4), channel_id=1, source_target_pairs={{0,8},{1,9},{4,12},{5,13},{10,2},{11,3},{14,6},{15,7},{16,24},{17,... | collective-permute-start | bytes 786440 | tf_op jit(solution)/shard_map/ppermute | solution.py:77
  45.9 20.2 %collective-permute-start.10 = (bf16[1024,256]{1,0:T(8,128)(2,1)}, bf16[1024,256]{1,0:T(8,128)(2,1)}, u32[]{:S(2)}, u32[]{:S(2)}) collective-permute-start(bf16[1024,256]{1,0:T(8,128)(2,1)} %broadcast_select_fusion.10), channel_id=1, source_target_pairs={{0,2},{1,3},{2,0},{3,1},{4,6},{5,7},{6,4},{7,5},{8,10},{9,11},{10,... | collective-permute-start | bytes 1572872 | tf_op jit(solution)/shard_map/ppermute | solution.py:68
  48.8 5.0 %copy-start.2 = (bf16[1024,128]{1,0:T(8,128)(2,1)}, bf16[1024,128]{1,0:T(8,128)(2,1)S(1)}, u32[]{:S(2)}) copy-start(bf16[1024,128]{1,0:T(8,128)(2,1)S(1)} %collective-permute-done.5) | copy-start | bytes 786436
  53.8 8.6 %collective-permute-start.7 = (bf16[1024,128]{1,0:T(8,128)(2,1)S(1)}, bf16[1024,128]{1,0:T(8,128)(2,1)}, u32[]{:S(2)}, u32[]{:S(2)}) collective-permute-start(bf16[1024,128]{1,0:T(8,128)(2,1)S(1)} %broadcast_select_fusion.14), channel_id=1, source_target_pairs={{0,4},{1,5},{2,6},{3,7},{4,0},{5,1},{6,2},{7,3},{8,12},{9,13},{10,... | collective-permute-start | bytes 786440 | tf_op jit(solution)/shard_map/ppermute | solution.py:71
  55.8 51.7 %collective-permute-start.8 = (bf16[1024,384]{1,0:T(8,128)(2,1)S(1)}, bf16[1024,384]{1,0:T(8,128)(2,1)S(1)}, u32[]{:S(2)}, u32[]{:S(2)}) collective-permute-start(bf16[1024,384]{1,0:T(8,128)(2,1)S(1)} %slice.37), channel_id=1, source_target_pairs={{0,8},{1,9},{4,12},{5,13},{10,2},{11,3},{14,6},{15,7},{16,24},{17,... | collective-permute-start | bytes 2359304 | tf_op jit(solution)/shard_map/ppermute | solution.py:77
  63.4 18.3 %collective-permute-start.12 = (bf16[1024,128]{1,0:T(8,128)(2,1)S(1)}, bf16[1024,128]{1,0:T(8,128)(2,1)S(1)}, u32[]{:S(2)}, u32[]{:S(2)}) collective-permute-start(bf16[1024,128]{1,0:T(8,128)(2,1)S(1)} %broadcast_select_fusion.13), channel_id=1, source_target_pairs={{0,4},{1,5},{2,6},{3,7},{4,0},{5,1},{6,2},{7,3},{8,12},{9,13},{10,... | collective-permute-start | bytes 786440 | tf_op jit(solution)/shard_map/ppermute | solution.py:71
  66.0 15.4 %collective-permute-start.15 = (bf16[1024,256]{1,0:T(8,128)(2,1)}, bf16[1024,256]{1,0:T(8,128)(2,1)S(1)}, u32[]{:S(2)}, u32[]{:S(2)}) collective-permute-start(bf16[1024,256]{1,0:T(8,128)(2,1)} %get-tuple-element.59), channel_id=1, source_target_pairs={{0,2},{1,3},{2,0},{3,1},{4,6},{5,7},{6,4},{7,5},{8,10},{9,11},{10,... | collective-permute-start | bytes 1572872 | tf_op jit(solution)/shard_map/ppermute | solution.py:68
  68.1 25.9 %collective-permute-start.11 = (bf16[1024,256]{1,0:T(8,128)(2,1)}, bf16[1024,256]{1,0:T(8,128)(2,1)S(1)}, u32[]{:S(2)}, u32[]{:S(2)}) collective-permute-start(bf16[1024,256]{1,0:T(8,128)(2,1)} %collective-permute-done.10), channel_id=1, source_target_pairs={{2,10},{3,11},{6,14},{7,15},{8,0},{9,1},{12,4},{13,5},{18,26},{19,... | collective-permute-start | bytes 1572872 | tf_op jit(solution)/shard_map/ppermute | solution.py:80
  70.4 2.6 %copy-start.3 = (bf16[1024,128]{1,0:T(8,128)(2,1)S(1)}, bf16[1024,128]{1,0:T(8,128)(2,1)}, u32[]{:S(2)}) copy-start(bf16[1024,128]{1,0:T(8,128)(2,1)} %copy-done.2) | copy-start | bytes 786436
  74.5 5.8 %copy-start.6 = (bf16[1024,128]{1,0:T(8,128)(2,1)S(1)}, bf16[1024,128]{1,0:T(8,128)(2,1)}, u32[]{:S(2)}) copy-start(bf16[1024,128]{1,0:T(8,128)(2,1)} %copy-done.5) | copy-start | bytes 786436
  74.5 5.8 %copy-start.8 = (bf16[1024,128]{1,0:T(8,128)(2,1)S(1)}, bf16[1024,128]{1,0:T(8,128)(2,1)}, u32[]{:S(2)}) copy-start(bf16[1024,128]{1,0:T(8,128)(2,1)} %copy-done.7) | copy-start | bytes 786436
  74.5 19.5 %collective-permute-start.13 = (f32[1024,128]{1,0:T(8,128)S(1)}, f32[1024,128]{1,0:T(8,128)S(1)}, u32[]{:S(2)}, u32[]{:S(2)}) collective-permute-start(f32[1024,128]{1,0:T(8,128)S(1)} %convolution_add_fusion.3), channel_id=1, source_target_pairs={{0,2},{1,3},{2,0},{3,1},{4,6},{5,7},{6,4},{7,5},{8,10},{9,11},{10,... | collective-permute-start | bytes 1572872 | tf_op jit(solution)/shard_map/ppermute | solution.py:68
  81.5 30.2 %collective-permute-start.20 = (bf16[1024,256]{1,0:T(8,128)(2,1)S(1)}, bf16[1024,256]{1,0:T(8,128)(2,1)S(1)}, u32[]{:S(2)}, u32[]{:S(2)}) collective-permute-start(bf16[1024,256]{1,0:T(8,128)(2,1)S(1)} %get-tuple-element.77), channel_id=1, source_target_pairs={{0,1},{1,0},{2,3},{3,2},{4,5},{5,4},{6,7},{7,6},{8,9},{9,8},{10,11... | collective-permute-start | bytes 1572872 | tf_op jit(solution)/shard_map/ppermute | solution.py:74
  81.6 30.1 %collective-permute-start.22 = (bf16[1024,512]{1,0:T(8,128)(2,1)S(1)}, bf16[1024,512]{1,0:T(8,128)(2,1)S(1)}, u32[]{:S(2)}, u32[]{:S(2)}) collective-permute-start(bf16[1024,512]{1,0:T(8,128)(2,1)S(1)} %pad_maximum_fusion), channel_id=1, source_target_pairs={{0,1},{1,0},{2,3},{3,2},{4,5},{5,4},{6,7},{7,6},{8,9},{9,8},{10,11... | collective-permute-start | bytes 3145736 | tf_op jit(solution)/shard_map/ppermute | solution.py:74
  94.1 11.9 %collective-permute-start.14 = (bf16[1024,256]{1,0:T(8,128)(2,1)S(1)}, bf16[1024,256]{1,0:T(8,128)(2,1)S(1)}, u32[]{:S(2)}, u32[]{:S(2)}) collective-permute-start(bf16[1024,256]{1,0:T(8,128)(2,1)S(1)} %broadcast_select_fusion.9), channel_id=1, source_target_pairs={{0,4},{1,5},{2,6},{3,7},{4,0},{5,1},{6,2},{7,3},{8,12},{9,13},{10,... | collective-permute-start | bytes 1572872 | tf_op jit(solution)/shard_map/ppermute | solution.py:71
  96.7 11.9 %collective-permute-start.16 = (f32[1024,128]{1,0:T(8,128)S(1)}, f32[1024,128]{1,0:T(8,128)S(1)}, u32[]{:S(2)}, u32[]{:S(2)}) collective-permute-start(f32[1024,128]{1,0:T(8,128)S(1)} %convolution_add_fusion.2), channel_id=1, source_target_pairs={{0,2},{1,3},{2,0},{3,1},{4,6},{5,7},{6,4},{7,5},{8,10},{9,11},{10,... | collective-permute-start | bytes 1572872 | tf_op jit(solution)/shard_map/ppermute | solution.py:68
  108.6 3.2 %collective-permute-start.21 = (bf16[1024,256]{1,0:T(8,128)(2,1)S(1)}, bf16[1024,256]{1,0:T(8,128)(2,1)S(1)}, u32[]{:S(2)}, u32[]{:S(2)}) collective-permute-start(bf16[1024,256]{1,0:T(8,128)(2,1)S(1)} %get-tuple-element.79), channel_id=1, source_target_pairs={{0,1},{1,0},{2,3},{3,2},{4,5},{5,4},{6,7},{7,6},{8,9},{9,8},{10,11... | collective-permute-start | bytes 1572872 | tf_op jit(solution)/shard_map/ppermute | solution.py:74
  108.8 20.0 %collective-permute-start.17 = (bf16[1024,384]{1,0:T(8,128)(2,1)S(1)}, bf16[1024,384]{1,0:T(8,128)(2,1)S(1)}, u32[]{:S(2)}, u32[]{:S(2)}) collective-permute-start(bf16[1024,384]{1,0:T(8,128)(2,1)S(1)} %broadcast_select_fusion.4), channel_id=1, source_target_pairs={{0,4},{1,5},{2,6},{3,7},{4,0},{5,1},{6,2},{7,3},{8,12},{9,13},{10,... | collective-permute-start | bytes 2359304 | tf_op jit(solution)/shard_map/ppermute | solution.py:71
  110.7 14.1 %collective-permute-start.18 = (f32[1024,128]{1,0:T(8,128)S(1)}, f32[1024,128]{1,0:T(8,128)S(1)}, u32[]{:S(2)}, u32[]{:S(2)}) collective-permute-start(f32[1024,128]{1,0:T(8,128)S(1)} %get-tuple-element.63), channel_id=1, source_target_pairs={{0,2},{1,3},{2,0},{3,1},{4,6},{5,7},{6,4},{7,5},{8,10},{9,11},{10,... | collective-permute-start | bytes 1572872 | tf_op jit(solution)/shard_map/ppermute | solution.py:68
  111.7 21.0 %collective-permute-start.25 = (bf16[1024,512]{1,0:T(8,128)(2,1)S(1)}, bf16[1024,512]{1,0:T(8,128)(2,1)S(1)}, u32[]{:S(2)}, u32[]{:S(2)}) collective-permute-start(bf16[1024,512]{1,0:T(8,128)(2,1)S(1)} %copy-done.1), channel_id=1, source_target_pairs={{0,1},{1,0},{2,3},{3,2},{4,5},{5,4},{6,7},{7,6},{8,9},{9,8},{10,11... | collective-permute-start | bytes 3145736 | tf_op jit(solution)/shard_map/ppermute | solution.py:74
  128.9 3.7 %collective-permute-start.24 = (bf16[1024,384]{1,0:T(8,128)(2,1)S(1)}, bf16[1024,384]{1,0:T(8,128)(2,1)S(1)}, u32[]{:S(2)}, u32[]{:S(2)}) collective-permute-start(bf16[1024,384]{1,0:T(8,128)(2,1)S(1)} %get-tuple-element.75), channel_id=1, source_target_pairs={{0,1},{1,0},{2,3},{3,2},{4,5},{5,4},{6,7},{7,6},{8,9},{9,8},{10,11... | collective-permute-start | bytes 2359304 | tf_op jit(solution)/shard_map/ppermute | solution.py:74
  129.1 3.6 %collective-permute-start.23 = (bf16[1024,128]{1,0:T(8,128)(2,1)S(1)}, bf16[1024,128]{1,0:T(8,128)(2,1)S(1)}, u32[]{:S(2)}, u32[]{:S(2)}) collective-permute-start(bf16[1024,128]{1,0:T(8,128)(2,1)S(1)} %get-tuple-element.89), channel_id=1, source_target_pairs={{0,1},{1,0},{2,3},{3,2},{4,5},{5,4},{6,7},{7,6},{8,9},{9,8},{10,11... | collective-permute-start | bytes 786440 | tf_op jit(solution)/shard_map/ppermute | solution.py:74
  129.6 13.9 %collective-permute-start.19 = (f32[1024,128]{1,0:T(8,128)S(1)}, f32[1024,128]{1,0:T(8,128)S(1)}, u32[]{:S(2)}, u32[]{:S(2)}) collective-permute-start(f32[1024,128]{1,0:T(8,128)S(1)} %get-tuple-element.64), channel_id=1, source_target_pairs={{0,2},{1,3},{2,0},{3,1},{4,6},{5,7},{6,4},{7,5},{8,10},{9,11},{10,... | collective-permute-start | bytes 1572872 | tf_op jit(solution)/shard_map/ppermute | solution.py:68

commit v5 on v2

--- a/solution.py
+++ b/solution.py
@@ -53,16 +53,13 @@
     def is_home(g, z, s, c):
         return z // 2 == s
 
-    def is_away(g, z, s, c):
-        return z // 2 != s
-
     def jumped(g, z, s, c):
         return (g, z ^ 2, s, c)
 
     cross_pairs = pairs(lambda g, z, s, c: (g, z, 1 - s, c))
     step_pairs = pairs(lambda g, z, s, c: (g, z ^ 1, s, c))
     core_pairs = pairs(lambda g, z, s, c: (g, z, s, 1 - c))
-    home_jump_pairs, away_jump_pairs = pairs(jumped, is_home), pairs(jumped, is_away)
+    jump_pairs, home_jump_pairs = pairs(jumped), pairs(jumped, is_home)
 
     def cross(a):
         return lax.ppermute(a, AXES, cross_pairs)
@@ -76,8 +73,8 @@
     def home_jump(a):
         return lax.ppermute(a, AXES, home_jump_pairs)
 
-    def away_jump(a):
-        return lax.ppermute(a, AXES, away_jump_pairs)
+    def jump(a):
+        return lax.ppermute(a, AXES, jump_pairs)
 
     def shards(expected_cot, value_next, transition, section):
         df = factor_of(section)
@@ -85,54 +82,92 @@
         home = z // 2 == s
         mine = z % 2 == c
         half = expected_cot.shape[1] // 2
-        ep, eq = expected_cot[:, :half], expected_cot[:, half:]
-        vp, vq = value_next[:, :half], value_next[:, half:]
+        quarter = half // 2
 
-        x1 = cross(jnp.where(home, vp, ep))
-        jq = away_jump(eq)
-        t_other = swap(transition)
-        v_other = swap(value_next)
-        t_near, t_next = jnp.where(mine, transition, t_other), jnp.where(mine, t_other, transition)
+        def columns(array, start, stop):
+            return array[:, start * quarter : stop * quarter]
+
+        def together(arrays, *gates):
+            return lax.optimization_barrier(tuple(arrays) + gates)[: len(arrays)]
+
+        e = [columns(expected_cot, i, i + 1) for i in range(4)]
+        v = [columns(value_next, i, i + 1) for i in range(4)]
+        first_cross, first_jump, e3 = together(
+            (jnp.where(home, v[0], e[0]), jnp.where(home, e[0], e[2]), e[3])
+        )
+        x1 = cross(first_cross)
+        j1 = jump(first_jump)
+        v1, e1 = together((v[1], e[1]), x1, j1)
+        x2 = cross(jnp.where(home, v1, e1))
+        near, far = together((x1, e3), j1)
+        j2 = jump(jnp.where(home, near, far))
+        t_other = swap(after(transition, j1))
+        near, far = together((j1, v[0]), x2)
+        x3 = cross(jnp.where(home, near, far))
+        t, t_o = together((transition, t_other), x2)
+        t_near, t_next = jnp.where(mine, t, t_o), jnp.where(mine, t_o, t)
 
         def adjoint_of(near, far):
             return tdot(t_near, near) + tdot(t_next, far)
 
+        near, far = together((x2, x3), j2)
+        j3 = jump(jnp.where(home, near, far))
+        near, far = together((j2, v[1]), x3)
+        x4 = cross(jnp.where(home, near, far))
+        near, far = together((x1, j2), x3, t_near)
+        b0 = jnp.where(home, near, far)
+        b0_next = step(b0)
+        x5 = cross(after(columns(value_next, 2, 4), x4, b0_next))
+        near, far = together((e[1], x4), j3, b0_next)
+        j4 = jump(jnp.where(home, near, far))
+        sum0 = adjoint_of(b0, b0_next)
+        part0 = cross(after(sum0, x4))
+        near, far = together((x2, j3), sum0, x4)
+        b1 = jnp.where(home, near, far)
+        b1_next = step(b1)
+        part1 = cross(after(adjoint_of(b1, b1_next), x5, part0))
+        near, far = together((j3, x3), b1_next)
+        b2 = jnp.where(home, near, far)
+        b2_next = step(b2)
+        part2 = cross(after(adjoint_of(b2, b2_next), part1))
+        near, far = together((j4, x4), b2_next, part0, x5)
+        b3 = jnp.where(home, near, far)
+        b3_next = step(b3)
+        part3 = cross(after(adjoint_of(b3, b3_next), part2))
+        j5 = home_jump(after(columns(expected_cot, 2, 4), j4))
+        v_other = swap(after(value_next, b1_next))
+        near, far = together((columns(expected_cot, 0, 2), jnp.concatenate([j1, j4], 1)), b3_next, part1)
+        a01 = jnp.where(home, near, far)
+        a01_next = step(a01)
+
         def own_and_swapped(near, far):
             return jnp.where(mine, near, far), swap(jnp.where(mine, far, near))
 
-        x2 = cross(after(jnp.where(home, vq, vp), x1))
-        jp = home_jump(x1)
-        x3 = cross(after(jnp.where(home, jq, vq), x2))
-        jq2 = away_jump(x3)
-        bp = jnp.where(home, x1, jp)
-        bp_next = step(bp)
-        jap = home_jump(after(ep, jp))
-        part_p = cross(adjoint_of(bp, bp_next))
-        bq = jnp.where(home, jq2, x3)
-        bq_next = step(after(bq, bp_next))
-        part_q = cross(adjoint_of(bq, bq_next))
-        ap = jnp.where(home, ep, jap)
-        ap_next = step(after(ap, bq_next))
-        jaq = home_jump(after(eq, jap))
-        aq = jnp.where(home, eq, jaq)
-        aq_next = step(after(aq, ap_next))
-
-        v_across = jnp.concatenate([jnp.where(home, x2, x1), jnp.where(home, x3, x2)], 1)
-        v_across_other = swap(v_across)
-        bp_own, bp_swapped = own_and_swapped(bp, bp_next)
-        bq_own, bq_swapped = own_and_swapped(bq, bq_next)
+        v_across = jnp.concatenate(
+            [jnp.where(home, jnp.concatenate([x3, x4], 1), jnp.concatenate([x1, x2], 1)), x5], 1
+        )
+        v_across_other = swap(after(v_across, b1_next))
+        b_own, b_swapped = own_and_swapped(
+            jnp.concatenate([b0, b1, b2, b3], 1),
+            jnp.concatenate([b0_next, b1_next, b2_next, b3_next], 1),
+        )
         grad = dott(
-            jnp.concatenate([bp_own, bq_own, bp_swapped, bq_swapped], 1),
-            jnp.concatenate([v_across, v_across_other], 1),
+            jnp.concatenate([b_own, b_swapped], 1), jnp.concatenate([v_across, v_across_other], 1)
         )
-        ap_own, ap_swapped = own_and_swapped(ap, ap_next)
-        aq_own, aq_swapped = own_and_swapped(aq, aq_next)
-        grad = grad + dott(
-            jnp.concatenate([ap_own, aq_own, ap_swapped, aq_swapped], 1),
+        a01_own, a01_swapped = own_and_swapped(a01, a01_next)
+        near, far = together((columns(expected_cot, 2, 4), j5), a01_next, part2)
+        a23 = jnp.where(home, near, far)
+        a23_next = step(a23)
+        near, far = together((a23, a23_next), grad)
+        a23_own, a23_swapped = own_and_swapped(near, far)
+        grad = df * (grad + dott(
+            jnp.concatenate([a01_own, a23_own, a01_swapped, a23_swapped], 1),
             jnp.concatenate([value_next, v_other], 1),
-        )
-        adjoint = jnp.concatenate([adjoint_of(ap, ap_next) + part_p, adjoint_of(aq, aq_next) + part_q], 1)
-        return df * adjoint, df * grad
+        ))
+        own = adjoint_of(jnp.concatenate([a01, a23], 1), jnp.concatenate([a01_next, a23_next], 1))
+        own, part3, grad = together((own, part3, grad))
+        adjoint = df * (own + jnp.concatenate([part0, part1, part2, part3], 1))
+        return adjoint, grad
 
     return shards
 

time: 198 us -> 144 us (0.73)
  starting transfers between devices: 71.3 us -> 34.8 us
  waiting for transfers between devices: 92.5 us -> 82.5 us
  local copies, waits for them, and re-layouts: 4.1 us -> 0.37 us
  other arithmetic: 11.1 us -> 9.05 us
    ppermute x4 -> x6, starting transfers between devices: 37.8 us -> 10.8 us  [step(): return lax.ppermute(a, AXES, step_pairs)]
    ppermute x5 -> x9, waiting for transfers between devices: 48.4 us -> 33.4 us  [cross(): return lax.ppermute(a, AXES, cross_pairs)]
    ppermute x4 -> x6, waiting for transfers between devices: 11.1 us -> 19.8 us  [step(): return lax.ppermute(a, AXES, step_pairs)]
    ppermute x3 -> x1, starting transfers between devices: 11.7 us -> 5.07 us  [home_jump(): return lax.ppermute(a, AXES, home_jump_pairs)]
    ppermute x5 -> x9, starting transfers between devices: 18.5 us -> 13.2 us  [cross(): return lax.ppermute(a, AXES, cross_pairs)]
    dot_general x2, matrix products: 10.6 us -> 6.74 us  [dott(): lax.dot_general(a, b, (((1,), (1,)), ((), ())), preferred_element_type=jn...]
    select_n x4 -> x3, other arithmetic: 4.45 us -> 0.76 us  [own_and_swapped(): return (jnp.where(mine, near, far), swap(jnp.where(mine, far, near)))]
    ppermute x2 -> x4, waiting for transfers between devices: 32.3 us -> 29.2 us  [jump(): return lax.ppermute(a, AXES, jump_pairs)]
  transfers between devices with their start and end apart: 21 -> 26, of which waited for: 10 -> 14; matrix products, arithmetic and copies ran while one was open for 11% -> 15% of each run, Pallas kernels for 0% -> 0%
where the time goes in v5:
time: 144 us
  waiting for transfers between devices  82.5 us (57%)
  starting transfers between devices  34.8 us (24%)
  matrix products  15.3 us (11%)
  other arithmetic  9.05 us (6%)
  between operations  1.73 us (1%)
    ppermute x9, waiting for transfers between devices, cross(): return lax.ppermute(a, AXES, cross_pairs)  33.4 us
    ppermute x4, waiting for transfers between devices, jump(): return lax.ppermute(a, AXES, jump_pairs)  29.2 us
    ppermute x6, waiting for transfers between devices, step(): return lax.ppermute(a, AXES, step_pairs)  19.8 us
    ppermute x9, starting transfers between devices, cross(): return lax.ppermute(a, AXES, cross_pairs)  13.2 us
    ppermute x6, starting transfers between devices, step(): return lax.ppermute(a, AXES, step_pairs)  10.8 us
    dot_general x10, matrix products, tdot(): lax.dot_general(a, b, (((0,), (0,)), ((), ())), preferred_element_type=jn...  8.58 us
    dot_general x2, matrix products, dott(): lax.dot_general(a, b, (((1,), (1,)), ((), ())), preferred_element_type=jn...  6.74 us
    ppermute x4, starting transfers between devices, jump(): return lax.ppermute(a, AXES, jump_pairs)  5.2 us
  transfers between devices with their start and end apart: 26, of which 14 were waited for; matrix products, arithmetic and copies ran while one was open for 15% of the time, Pallas kernels for 0%

profile of v5, /device:TPU:0, one launch (start us, length us, event | category | flops | bytes accessed | tf_op | source)
XLA Modules:
  0.0 143.7 jit_solution(7373930975404806377)
XLA Ops:
  0.7 1.6 %fusion.37 = (bf16[1024,128]{1,0:T(8,128)(2,1)S(1)}, bf16[1024,128]{1,0:T(8,128)(2,1)S(1)}, bf16[1024,128]{1,0:T(8,128)(2,1)S(1)}, bf16[1024,128]{1,0:T(8,128)(2...) fusion(bf16[1024,512]{1,0:T(8,128)(2,1)} %param.5, bf16[1024,512]{1,0:T(8,128)(2,1)} %param.4, ...), kind=kLoop, calls=%fused_computation.70 | loop fusion | flops 262144 | bytes 3145729 | tf_op jit(solution)/shard_map/slice | solution.py:88
  2.3 4.1 %collective-permute-start = (bf16[1024,128]{1,0:T(8,128)(2,1)S(1)}, bf16[1024,128]{1,0:T(8,128)(2,1)S(1)}, u32[]{:S(2)}, u32[]{:S(2)}) collective-permute-start(bf16[1024,128]{1,0:T(8,128)(2,1)S(1)} %get-tuple-element.45), channel_id=1, source_target_pairs={{0,8},{1,9},{2,10},{3,11},{4,12},{5,13},{6,14},{7,15},{8,0},{9,1},... | collective-permute-start | bytes 786440 | tf_op jit(solution)/shard_map/ppermute | solution.py:77
  6.4 11.9 %collective-permute-done = bf16[1024,128]{1,0:T(8,128)(2,1)S(1)} collective-permute-done((bf16[1024,128]{1,0:T(8,128)(2,1)S(1)}, bf16[1024,128]{1,0:T(8,128)(2,1)S(1)}, u32[]{:S(2)}, u32[]{:S(2)}) %collective-permute-start) | collective-permute-done | bytes 262176 | tf_op jit(solution)/shard_map/ppermute | solution.py:77
  18.3 1.6 %collective-permute-start.2 = (bf16[1024,128]{1,0:T(8,128)(2,1)S(1)}, bf16[1024,128]{1,0:T(8,128)(2,1)S(1)}, u32[]{:S(2)}, u32[]{:S(2)}) collective-permute-start(bf16[1024,128]{1,0:T(8,128)(2,1)S(1)} %get-tuple-element.47), channel_id=1, source_target_pairs={{0,2},{1,3},{2,0},{3,1},{4,6},{5,7},{6,4},{7,5},{8,10},{9,11},{10,... | collective-permute-start | bytes 786440 | tf_op jit(solution)/shard_map/ppermute | solution.py:65
  20.0 7.1 %collective-permute-done.2 = bf16[1024,128]{1,0:T(8,128)(2,1)S(1)} collective-permute-done((bf16[1024,128]{1,0:T(8,128)(2,1)S(1)}, bf16[1024,128]{1,0:T(8,128)(2,1)S(1)}, u32[]{:S(2)}, u32[]{:S(2)}) %collective-permute-start.2) | collective-permute-done | bytes 262176 | tf_op jit(solution)/shard_map/ppermute | solution.py:65
  27.1 1.6 %collective-permute-start.3 = (bf16[1024,128]{1,0:T(8,128)(2,1)S(1)}, bf16[1024,128]{1,0:T(8,128)(2,1)S(1)}, u32[]{:S(2)}, u32[]{:S(2)}) collective-permute-start(bf16[1024,128]{1,0:T(8,128)(2,1)S(1)} %broadcast_select_fusion.19), channel_id=1, source_target_pairs={{0,2},{1,3},{2,0},{3,1},{4,6},{5,7},{6,4},{7,5},{8,10},{9,11},{10,... | collective-permute-start | bytes 786440 | tf_op jit(solution)/shard_map/ppermute | solution.py:65
  28.7 0.7 broadcast_select_fusion.18
  29.4 5.6 %collective-permute-done.3 = bf16[1024,128]{1,0:T(8,128)(2,1)S(1)} collective-permute-done((bf16[1024,128]{1,0:T(8,128)(2,1)S(1)}, bf16[1024,128]{1,0:T(8,128)(2,1)S(1)}, u32[]{:S(2)}, u32[]{:S(2)}) %collective-permute-start.3) | collective-permute-done | bytes 262176 | tf_op jit(solution)/shard_map/ppermute | solution.py:65
  35.0 0.8 broadcast_select_fusion.17
  35.8 1.5 %collective-permute-start.5 = (bf16[1024,128]{1,0:T(8,128)(2,1)}, bf16[1024,128]{1,0:T(8,128)(2,1)S(1)}, u32[]{:S(2)}, u32[]{:S(2)}) collective-permute-start(bf16[1024,128]{1,0:T(8,128)(2,1)} %broadcast_select_fusion.17), channel_id=1, source_target_pairs={{0,2},{1,3},{2,0},{3,1},{4,6},{5,7},{6,4},{7,5},{8,10},{9,11},{10,... | collective-permute-start | bytes 786440 | tf_op jit(solution)/shard_map/ppermute | solution.py:65
  37.3 6.5 %collective-permute-done.4 = bf16[1024,128]{1,0:T(8,128)(2,1)} collective-permute-done((bf16[1024,128]{1,0:T(8,128)(2,1)}, bf16[1024,128]{1,0:T(8,128)(2,1)}, u32[]{:S(2)}, u32[]{:S(2)}) %collective-permute-start.4) | collective-permute-done | bytes 262176 | tf_op jit(solution)/shard_map/ppermute | solution.py:77
  43.9 0.1 collective-permute-start.7
  44.0 1.0 broadcast_select_fusion.16
  45.0 0.1 collective-permute-start.6
  45.0 1.9 %broadcast_select_fusion.1 = (bf16[1024,1024]{1,0:T(8,128)(2,1)S(1)}, bf16[1024,1024]{1,0:T(8,128)(2,1)S(1)}) fusion(bf16[1024,1024]{1,0:T(8,128)(2,1)S(1)} %copy-done.1, bf16[1024,1024]{1,0:T(8,128)(2,1)} %collective-permute-done.1, pred[]{:T(512)S(6)} %eq.8), kind=kLoop, calls=%fused_computation.24 | loop fusion | flops 2097152 | bytes 8388609 | tf_op jit(solution)/shard_map/jit(_where)/select_n | solution.py:108
  47.0 3.8 %collective-permute-start.8 = (bf16[1024,128]{1,0:T(8,128)(2,1)S(1)}, bf16[1024,128]{1,0:T(8,128)(2,1)S(1)}, u32[]{:S(2)}, u32[]{:S(2)}) collective-permute-start(bf16[1024,128]{1,0:T(8,128)(2,1)S(1)} %broadcast_select_fusion.14), channel_id=1, source_target_pairs={{0,4},{1,5},{2,6},{3,7},{4,0},{5,1},{6,2},{7,3},{8,12},{9,13},{10,... | collective-permute-start | bytes 786440 | tf_op jit(solution)/shard_map/ppermute | solution.py:68
  50.7 6.6 %collective-permute-done.7 = bf16[1024,128]{1,0:T(8,128)(2,1)S(1)} collective-permute-done((bf16[1024,128]{1,0:T(8,128)(2,1)S(1)}, bf16[1024,128]{1,0:T(8,128)(2,1)S(1)}, u32[]{:S(2)}, u32[]{:S(2)}) %collective-permute-start.7) | collective-permute-done | bytes 262176 | tf_op jit(solution)/shard_map/ppermute | solution.py:77
  57.3 3.1 %collective-permute-done.8 = bf16[1024,128]{1,0:T(8,128)(2,1)S(1)} collective-permute-done((bf16[1024,128]{1,0:T(8,128)(2,1)S(1)}, bf16[1024,128]{1,0:T(8,128)(2,1)S(1)}, u32[]{:S(2)}, u32[]{:S(2)}) %collective-permute-start.8) | collective-permute-done | bytes 262176 | tf_op jit(solution)/shard_map/ppermute | solution.py:68
  60.5 1.0 collective-permute-start.9
  61.5 0.7 fusion.38
  62.3 0.8 convolution_add_fusion.4
  63.1 2.5 %collective-permute-start.10 = (bf16[1024,128]{1,0:T(8,128)(2,1)S(1)}, bf16[1024,128]{1,0:T(8,128)(2,1)S(1)}, u32[]{:S(2)}, u32[]{:S(2)}) collective-permute-start(bf16[1024,128]{1,0:T(8,128)(2,1)S(1)} %broadcast_select_fusion.12), channel_id=1, source_target_pairs={{0,4},{1,5},{2,6},{3,7},{4,0},{5,1},{6,2},{7,3},{8,12},{9,13},{10,... | collective-permute-start | bytes 786440 | tf_op jit(solution)/shard_map/ppermute | solution.py:68
  65.7 0.1 fusion.36
  66.5 0.2 maximum_select_fusion
  66.7 0.3 collective-permute-start.12
  66.9 1.8 %collective-permute-start.13 = (bf16[1024,256]{1,0:T(8,128)(2,1)S(1)}, bf16[1024,256]{1,0:T(8,128)(2,1)S(1)}, u32[]{:S(2)}, u32[]{:S(2)}) collective-permute-start(bf16[1024,256]{1,0:T(8,128)(2,1)S(1)} %slice.35), channel_id=1, source_target_pairs={{0,2},{1,3},{2,0},{3,1},{4,6},{5,7},{6,4},{7,5},{8,10},{9,11},{10,... | collective-permute-start | bytes 1572872 | tf_op jit(solution)/shard_map/ppermute | solution.py:65
  68.8 4.2 %collective-permute-done.9 = bf16[1024,128]{1,0:T(8,128)(2,1)S(1)} collective-permute-done((bf16[1024,128]{1,0:T(8,128)(2,1)S(1)}, bf16[1024,128]{1,0:T(8,128)(2,1)S(1)}, u32[]{:S(2)}, u32[]{:S(2)}) %collective-permute-start.9) | collective-permute-done | bytes 262176 | tf_op jit(solution)/shard_map/ppermute | solution.py:77
  73.0 2.2 %collective-permute-done.10 = bf16[1024,128]{1,0:T(8,128)(2,1)S(1)} collective-permute-done((bf16[1024,128]{1,0:T(8,128)(2,1)S(1)}, bf16[1024,128]{1,0:T(8,128)(2,1)S(1)}, u32[]{:S(2)}, u32[]{:S(2)}) %collective-permute-start.10) | collective-permute-done | bytes 262176 | tf_op jit(solution)/shard_map/ppermute | solution.py:68
  75.2 0.1 collective-permute-start.11
  75.3 5.1 %collective-permute-start.16 = (bf16[1024,256]{1,0:T(8,128)(2,1)S(1)}, bf16[1024,256]{1,0:T(8,128)(2,1)S(1)}, u32[]{:S(2)}, u32[]{:S(2)}) collective-permute-start(bf16[1024,256]{1,0:T(8,128)(2,1)S(1)} %get-tuple-element.78), channel_id=1, source_target_pairs={{0,8},{1,9},{4,12},{5,13},{10,2},{11,3},{14,6},{15,7},{16,24},{17,... | collective-permute-start | bytes 1572872 | tf_op jit(solution)/shard_map/ppermute | solution.py:74
  80.4 0.7 fusion.39
  81.3 0.8 convolution_add_fusion.3
  82.0 0.7 fusion.40
  82.8 7.2 %collective-permute-done.13 = bf16[1024,256]{1,0:T(8,128)(2,1)S(1)} collective-permute-done((bf16[1024,256]{1,0:T(8,128)(2,1)S(1)}, bf16[1024,256]{1,0:T(8,128)(2,1)S(1)}, u32[]{:S(2)}, u32[]{:S(2)}) %collective-permute-start.13) | collective-permute-done | bytes 524320 | tf_op jit(solution)/shard_map/ppermute | solution.py:65
  90.0 1.4 %collective-permute-start.14 = (bf16[1024,128]{1,0:T(8,128)(2,1)S(1)}, bf16[1024,128]{1,0:T(8,128)(2,1)S(1)}, u32[]{:S(2)}, u32[]{:S(2)}) collective-permute-start(bf16[1024,128]{1,0:T(8,128)(2,1)S(1)} %broadcast_select_fusion.10), channel_id=1, source_target_pairs={{0,4},{1,5},{2,6},{3,7},{4,0},{5,1},{6,2},{7,3},{8,12},{9,13},{10,... | collective-permute-start | bytes 786440 | tf_op jit(solution)/shard_map/ppermute | solution.py:68
  91.4 0.8 convolution_add_fusion.2
  92.3 0.7 collective-permute-start.15
  93.0 0.1 pad_maximum_fusion.1
  93.1 0.1 collective-permute-start.22
  93.1 3.3 %collective-permute-done.14 = bf16[1024,128]{1,0:T(8,128)(2,1)S(1)} collective-permute-done((bf16[1024,128]{1,0:T(8,128)(2,1)S(1)}, bf16[1024,128]{1,0:T(8,128)(2,1)S(1)}, u32[]{:S(2)}, u32[]{:S(2)}) %collective-permute-start.14) | collective-permute-done | bytes 262176 | tf_op jit(solution)/shard_map/ppermute | solution.py:68
  96.5 0.6 broadcast_select_fusion.3
  97.1 0.1 collective-permute-start.21
  97.2 6.2 %collective-permute-done.15 = f32[1024,128]{1,0:T(8,128)S(1)} collective-permute-done((f32[1024,128]{1,0:T(8,128)S(1)}, f32[1024,128]{1,0:T(8,128)S(1)}, u32[]{:S(2)}, u32[]{:S(2)}) %collective-permute-start.15) | collective-permute-done | bytes 524320 | tf_op jit(solution)/shard_map/ppermute | solution.py:65
  103.4 0.1 broadcast_select_fusion.9
  103.5 1.2 collective-permute-start.17
  104.7 3.7 %collective-permute-start.18 = (f32[1024,128]{1,0:T(8,128)S(1)}, f32[1024,128]{1,0:T(8,128)S(1)}, u32[]{:S(2)}, u32[]{:S(2)}) collective-permute-start(f32[1024,128]{1,0:T(8,128)S(1)} %convolution_add_fusion.2), channel_id=1, source_target_pairs={{0,2},{1,3},{2,0},{3,1},{4,6},{5,7},{6,4},{7,5},{8,10},{9,11},{10,... | collective-permute-start | bytes 1572872 | tf_op jit(solution)/shard_map/ppermute | solution.py:65
  108.4 0.7 fusion.41
  109.2 0.8 convolution_add_fusion.1
  110.0 0.3 collective-permute-start.25
  110.2 3.5 %collective-permute-done.17 = bf16[1024,256]{1,0:T(8,128)(2,1)S(1)} collective-permute-done((bf16[1024,256]{1,0:T(8,128)(2,1)S(1)}, bf16[1024,256]{1,0:T(8,128)(2,1)S(1)}, u32[]{:S(2)}, u32[]{:S(2)}) %collective-permute-start.17) | collective-permute-done | bytes 524320 | tf_op jit(solution)/shard_map/ppermute | solution.py:68
  113.7 7.3 %collective-permute-done.18 = f32[1024,128]{1,0:T(8,128)S(1)} collective-permute-done((f32[1024,128]{1,0:T(8,128)S(1)}, f32[1024,128]{1,0:T(8,128)S(1)}, u32[]{:S(2)}, u32[]{:S(2)}) %collective-permute-start.18) | collective-permute-done | bytes 524320 | tf_op jit(solution)/shard_map/ppermute | solution.py:65
  121.0 0.1 broadcast_select_fusion.8
  121.1 1.7 %collective-permute-start.19 = (bf16[1024,256]{1,0:T(8,128)(2,1)S(1)}, bf16[1024,256]{1,0:T(8,128)(2,1)S(1)}, u32[]{:S(2)}, u32[]{:S(2)}) collective-permute-start(bf16[1024,256]{1,0:T(8,128)(2,1)S(1)} %broadcast_select_fusion.8), channel_id=1, source_target_pairs={{0,4},{1,5},{2,6},{3,7},{4,0},{5,1},{6,2},{7,3},{8,12},{9,13},{10,... | collective-permute-start | bytes 1572872 | tf_op jit(solution)/shard_map/ppermute | solution.py:68
  122.8 0.1 broadcast_select_fusion.7
  122.9 0.1 collective-permute-start.23
  123.0 1.8 %collective-permute-start.20 = (f32[1024,128]{1,0:T(8,128)S(1)}, f32[1024,128]{1,0:T(8,128)S(1)}, u32[]{:S(2)}, u32[]{:S(2)}) collective-permute-start(f32[1024,128]{1,0:T(8,128)S(1)} %convolution_add_fusion.1), channel_id=1, source_target_pairs={{0,2},{1,3},{2,0},{3,1},{4,6},{5,7},{6,4},{7,5},{8,10},{9,11},{10,... | collective-permute-start | bytes 1572872 | tf_op jit(solution)/shard_map/ppermute | solution.py:65
  124.8 2.4 %fusion = f32[1024,1024]{1,0:T(8,128)S(1)} fusion(bf16[1024,512]{1,0:T(8,128)(2,1)S(1)} %collective-permute-done.21, bf16[1024,512]{1,0:T(8,128)(2,1)S(1)} %get-tuple-element.90, bf16[1024,512]{1,0:T(8,128)(2,1)S(1)} %collective-permute-done.22, bf16[1024,256]{1,0:T(8,128)(2,1)S(1)} %collective-permute-done.13, bf16[1024,256]{1,0:T(8,128)(2,1)S(1)} %maximum_select_fusion), kind=kOutput, calls=%fused_computation.1 | convolution fusion | flops 2157969408 | bytes 8388608 | tf_op jit(solution)/shard_map/dot_general | solution.py:38
  127.2 7.7 %collective-permute-done.19 = bf16[1024,256]{1,0:T(8,128)(2,1)S(1)} collective-permute-done((bf16[1024,256]{1,0:T(8,128)(2,1)S(1)}, bf16[1024,256]{1,0:T(8,128)(2,1)S(1)}, u32[]{:S(2)}, u32[]{:S(2)}) %collective-permute-start.19) | collective-permute-done | bytes 524320 | tf_op jit(solution)/shard_map/ppermute | solution.py:68
  134.9 0.1 broadcast_select_fusion.6
  135.0 0.1 collective-permute-start.24
  135.1 1.3 fusion.28
  136.4 1.3 convolution_add_fusion
  137.7 4.4 %add_multiply_fusion = f32[1024,1024]{1,0:T(8,128)} fusion(f32[1024,1024]{1,0:T(8,128)S(1)} %fusion, f32[]{:T(128)} %bitcast, bf16[1024,512]{1,0:T(8,128)(2,1)S(1)} %collective-permute-done.25, bf16[1024,512]{1,0:T(8,128)(2,1)S(1)} %copy-done.2, bf16[1024,256]{1,0:T(8,128)(2,1)S(1)} %collective-permute-done.24, ...), kind=kOutput, calls=%fused_computation | convolution fusion | flops 2162163712 | bytes 12582916 | tf_op jit(solution)/shard_map/dot_general | solution.py:38
  142.1 1.6 %fusion.20 = f32[1024,512]{1,0:T(8,128)} fusion(f32[1024,512]{1,0:T(8,128)S(1)} %convolution_add_fusion, f32[1024,128]{1,0:T(8,128)S(1)} %collective-permute-done.20, f32[1024,128]{1,0:T(8,128)S(1)} %collective-permute-done.18, f32[1024,128]{1,0:T(8,128)S(1)} %collective-permute-done.15, f32[1024,128]{1,0:T(8,128)S(1)} %collective-permute-done.12, f32[]{:T(128)} %bitcast), kind=kLoop, calls=%fused_computation.22 | loop fusion | flops 2621440 | bytes 6291460 | tf_op jit(solution)/shard_map/mul | solution.py:169
  (37 shorter events, 0.6 us)
Async XLA Ops:
  0.6 17.7 %copy-start.1 = (bf16[1024,1024]{1,0:T(8,128)(2,1)S(1)}, bf16[1024,1024]{1,0:T(8,128)(2,1)}, u32[]{:S(2)}) copy-start(bf16[1024,1024]{1,0:T(8,128)(2,1)} %param.6) | copy-start | bytes 6291460
  2.3 16.0 %collective-permute-start = (bf16[1024,128]{1,0:T(8,128)(2,1)S(1)}, bf16[1024,128]{1,0:T(8,128)(2,1)S(1)}, u32[]{:S(2)}, u32[]{:S(2)}) collective-permute-start(bf16[1024,128]{1,0:T(8,128)(2,1)S(1)} %get-tuple-element.45), channel_id=1, source_target_pairs={{0,8},{1,9},{2,10},{3,11},{4,12},{5,13},{6,14},{7,15},{8,0},{9,1},... | collective-permute-start | bytes 786440 | tf_op jit(solution)/shard_map/ppermute | solution.py:77
  18.3 16.7 %copy-start.3 = (bf16[1024,128]{1,0:T(8,128)(2,1)}, bf16[1024,128]{1,0:T(8,128)(2,1)S(1)}, u32[]{:S(2)}) copy-start(bf16[1024,128]{1,0:T(8,128)(2,1)S(1)} %collective-permute-done) | copy-start | bytes 786436
  18.3 26.7 %collective-permute-start.1 = (bf16[1024,1024]{1,0:T(8,128)(2,1)S(1)}, bf16[1024,1024]{1,0:T(8,128)(2,1)}, u32[]{:S(2)}, u32[]{:S(2)}) collective-permute-start(bf16[1024,1024]{1,0:T(8,128)(2,1)S(1)} %copy-done.1), channel_id=1, source_target_pairs={{0,1},{1,0},{2,3},{3,2},{4,5},{5,4},{6,7},{7,6},{8,9},{9,8},{10,11... | collective-permute-start | bytes 6291464 | tf_op jit(solution)/shard_map/ppermute | solution.py:71
  18.3 8.7 %collective-permute-start.2 = (bf16[1024,128]{1,0:T(8,128)(2,1)S(1)}, bf16[1024,128]{1,0:T(8,128)(2,1)S(1)}, u32[]{:S(2)}, u32[]{:S(2)}) collective-permute-start(bf16[1024,128]{1,0:T(8,128)(2,1)S(1)} %get-tuple-element.47), channel_id=1, source_target_pairs={{0,2},{1,3},{2,0},{3,1},{4,6},{5,7},{6,4},{7,5},{8,10},{9,11},{10,... | collective-permute-start | bytes 786440 | tf_op jit(solution)/shard_map/ppermute | solution.py:65
  27.1 7.9 %collective-permute-start.3 = (bf16[1024,128]{1,0:T(8,128)(2,1)S(1)}, bf16[1024,128]{1,0:T(8,128)(2,1)S(1)}, u32[]{:S(2)}, u32[]{:S(2)}) collective-permute-start(bf16[1024,128]{1,0:T(8,128)(2,1)S(1)} %broadcast_select_fusion.19), channel_id=1, source_target_pairs={{0,2},{1,3},{2,0},{3,1},{4,6},{5,7},{6,4},{7,5},{8,10},{9,11},{10,... | collective-permute-start | bytes 786440 | tf_op jit(solution)/shard_map/ppermute | solution.py:65
  29.4 14.4 %collective-permute-start.4 = (bf16[1024,128]{1,0:T(8,128)(2,1)}, bf16[1024,128]{1,0:T(8,128)(2,1)}, u32[]{:S(2)}, u32[]{:S(2)}) collective-permute-start(bf16[1024,128]{1,0:T(8,128)(2,1)} %broadcast_select_fusion.18), channel_id=1, source_target_pairs={{0,8},{1,9},{2,10},{3,11},{4,12},{5,13},{6,14},{7,15},{8,0},{9,1},... | collective-permute-start | bytes 786440 | tf_op jit(solution)/shard_map/ppermute | solution.py:77
  35.8 8.1 %collective-permute-start.5 = (bf16[1024,128]{1,0:T(8,128)(2,1)}, bf16[1024,128]{1,0:T(8,128)(2,1)S(1)}, u32[]{:S(2)}, u32[]{:S(2)}) collective-permute-start(bf16[1024,128]{1,0:T(8,128)(2,1)} %broadcast_select_fusion.17), channel_id=1, source_target_pairs={{0,2},{1,3},{2,0},{3,1},{4,6},{5,7},{6,4},{7,5},{8,10},{9,11},{10,... | collective-permute-start | bytes 786440 | tf_op jit(solution)/shard_map/ppermute | solution.py:65
  43.9 13.5 %collective-permute-start.7 = (bf16[1024,128]{1,0:T(8,128)(2,1)S(1)}, bf16[1024,128]{1,0:T(8,128)(2,1)S(1)}, u32[]{:S(2)}, u32[]{:S(2)}) collective-permute-start(bf16[1024,128]{1,0:T(8,128)(2,1)S(1)} %broadcast_select_fusion.15), channel_id=1, source_target_pairs={{0,8},{1,9},{2,10},{3,11},{4,12},{5,13},{6,14},{7,15},{8,0},{9,1},... | collective-permute-start | bytes 786440 | tf_op jit(solution)/shard_map/ppermute | solution.py:77
  45.0 12.4 %collective-permute-start.6 = (bf16[1024,128]{1,0:T(8,128)(2,1)S(1)}, bf16[1024,128]{1,0:T(8,128)(2,1)S(1)}, u32[]{:S(2)}, u32[]{:S(2)}) collective-permute-start(bf16[1024,128]{1,0:T(8,128)(2,1)S(1)} %broadcast_select_fusion.16), channel_id=1, source_target_pairs={{0,2},{1,3},{2,0},{3,1},{4,6},{5,7},{6,4},{7,5},{8,10},{9,11},{10,... | collective-permute-start | bytes 786440 | tf_op jit(solution)/shard_map/ppermute | solution.py:65
  47.0 13.5 %collective-permute-start.8 = (bf16[1024,128]{1,0:T(8,128)(2,1)S(1)}, bf16[1024,128]{1,0:T(8,128)(2,1)S(1)}, u32[]{:S(2)}, u32[]{:S(2)}) collective-permute-start(bf16[1024,128]{1,0:T(8,128)(2,1)S(1)} %broadcast_select_fusion.14), channel_id=1, source_target_pairs={{0,4},{1,5},{2,6},{3,7},{4,0},{5,1},{6,2},{7,3},{8,12},{9,13},{10,... | collective-permute-start | bytes 786440 | tf_op jit(solution)/shard_map/ppermute | solution.py:68
  60.5 12.5 %collective-permute-start.9 = (bf16[1024,128]{1,0:T(8,128)(2,1)S(1)}, bf16[1024,128]{1,0:T(8,128)(2,1)S(1)}, u32[]{:S(2)}, u32[]{:S(2)}) collective-permute-start(bf16[1024,128]{1,0:T(8,128)(2,1)S(1)} %broadcast_select_fusion.13), channel_id=1, source_target_pairs={{0,8},{1,9},{2,10},{3,11},{4,12},{5,13},{6,14},{7,15},{8,0},{9,1},... | collective-permute-start | bytes 786440 | tf_op jit(solution)/shard_map/ppermute | solution.py:77
  62.3 3.4 %copy-start = (bf16[1024,512]{1,0:T(8,128)(2,1)S(1)}, bf16[1024,512]{1,0:T(8,128)(2,1)}, u32[]{:S(2)}) copy-start(bf16[1024,512]{1,0:T(8,128)(2,1)} %param.4) | copy-start | bytes 3145732
  63.1 2.7 %copy-start.2 = (bf16[1024,512]{1,0:T(8,128)(2,1)S(1)}, bf16[1024,512]{1,0:T(8,128)(2,1)}, u32[]{:S(2)}) copy-start(bf16[1024,512]{1,0:T(8,128)(2,1)} %param.5) | copy-start | bytes 3145732
  63.1 12.1 %collective-permute-start.10 = (bf16[1024,128]{1,0:T(8,128)(2,1)S(1)}, bf16[1024,128]{1,0:T(8,128)(2,1)S(1)}, u32[]{:S(2)}, u32[]{:S(2)}) collective-permute-start(bf16[1024,128]{1,0:T(8,128)(2,1)S(1)} %broadcast_select_fusion.12), channel_id=1, source_target_pairs={{0,4},{1,5},{2,6},{3,7},{4,0},{5,1},{6,2},{7,3},{8,12},{9,13},{10,... | collective-permute-start | bytes 786440 | tf_op jit(solution)/shard_map/ppermute | solution.py:68
  65.7 14.6 %copy-start.4 = (bf16[1024,128]{1,0:T(8,128)(2,1)S(1)}, bf16[1024,128]{1,0:T(8,128)(2,1)}, u32[]{:S(2)}) copy-start(bf16[1024,128]{1,0:T(8,128)(2,1)} %copy-done.3) | copy-start | bytes 786436
  66.7 16.1 %collective-permute-start.12 = (f32[1024,128]{1,0:T(8,128)S(1)}, f32[1024,128]{1,0:T(8,128)S(1)}, u32[]{:S(2)}, u32[]{:S(2)}) collective-permute-start(f32[1024,128]{1,0:T(8,128)S(1)} %convolution_add_fusion.4), channel_id=1, source_target_pairs={{0,2},{1,3},{2,0},{3,1},{4,6},{5,7},{6,4},{7,5},{8,10},{9,11},{10,... | collective-permute-start | bytes 1572872 | tf_op jit(solution)/shard_map/ppermute | solution.py:65
  66.9 23.0 %collective-permute-start.13 = (bf16[1024,256]{1,0:T(8,128)(2,1)S(1)}, bf16[1024,256]{1,0:T(8,128)(2,1)S(1)}, u32[]{:S(2)}, u32[]{:S(2)}) collective-permute-start(bf16[1024,256]{1,0:T(8,128)(2,1)S(1)} %slice.35), channel_id=1, source_target_pairs={{0,2},{1,3},{2,0},{3,1},{4,6},{5,7},{6,4},{7,5},{8,10},{9,11},{10,... | collective-permute-start | bytes 1572872 | tf_op jit(solution)/shard_map/ppermute | solution.py:65
  75.2 6.8 %collective-permute-start.11 = (bf16[1024,128]{1,0:T(8,128)(2,1)S(1)}, bf16[1024,128]{1,0:T(8,128)(2,1)S(1)}, u32[]{:S(2)}, u32[]{:S(2)}) collective-permute-start(bf16[1024,128]{1,0:T(8,128)(2,1)S(1)} %broadcast_select_fusion.11), channel_id=1, source_target_pairs={{0,4},{1,5},{2,6},{3,7},{4,0},{5,1},{6,2},{7,3},{8,12},{9,13},{10,... | collective-permute-start | bytes 786440 | tf_op jit(solution)/shard_map/ppermute | solution.py:68
  75.3 34.7 %collective-permute-start.16 = (bf16[1024,256]{1,0:T(8,128)(2,1)S(1)}, bf16[1024,256]{1,0:T(8,128)(2,1)S(1)}, u32[]{:S(2)}, u32[]{:S(2)}) collective-permute-start(bf16[1024,256]{1,0:T(8,128)(2,1)S(1)} %get-tuple-element.78), channel_id=1, source_target_pairs={{0,8},{1,9},{4,12},{5,13},{10,2},{11,3},{14,6},{15,7},{16,24},{17,... | collective-permute-start | bytes 1572872 | tf_op jit(solution)/shard_map/ppermute | solution.py:74
  90.0 6.4 %collective-permute-start.14 = (bf16[1024,128]{1,0:T(8,128)(2,1)S(1)}, bf16[1024,128]{1,0:T(8,128)(2,1)S(1)}, u32[]{:S(2)}, u32[]{:S(2)}) collective-permute-start(bf16[1024,128]{1,0:T(8,128)(2,1)S(1)} %broadcast_select_fusion.10), channel_id=1, source_target_pairs={{0,4},{1,5},{2,6},{3,7},{4,0},{5,1},{6,2},{7,3},{8,12},{9,13},{10,... | collective-permute-start | bytes 786440 | tf_op jit(solution)/shard_map/ppermute | solution.py:68
  92.3 11.1 %collective-permute-start.15 = (f32[1024,128]{1,0:T(8,128)S(1)}, f32[1024,128]{1,0:T(8,128)S(1)}, u32[]{:S(2)}, u32[]{:S(2)}) collective-permute-start(f32[1024,128]{1,0:T(8,128)S(1)} %convolution_add_fusion.3), channel_id=1, source_target_pairs={{0,2},{1,3},{2,0},{3,1},{4,6},{5,7},{6,4},{7,5},{8,10},{9,11},{10,... | collective-permute-start | bytes 1572872 | tf_op jit(solution)/shard_map/ppermute | solution.py:65
  93.1 29.9 %collective-permute-start.22 = (bf16[1024,512]{1,0:T(8,128)(2,1)S(1)}, bf16[1024,512]{1,0:T(8,128)(2,1)S(1)}, u32[]{:S(2)}, u32[]{:S(2)}) collective-permute-start(bf16[1024,512]{1,0:T(8,128)(2,1)S(1)} %pad_maximum_fusion.1), channel_id=1, source_target_pairs={{0,1},{1,0},{2,3},{3,2},{4,5},{5,4},{6,7},{7,6},{8,9},{9,8},{10,11... | collective-permute-start | bytes 3145736 | tf_op jit(solution)/shard_map/ppermute | solution.py:71
  97.1 27.7 %collective-permute-start.21 = (bf16[1024,512]{1,0:T(8,128)(2,1)S(1)}, bf16[1024,512]{1,0:T(8,128)(2,1)S(1)}, u32[]{:S(2)}, u32[]{:S(2)}) collective-permute-start(bf16[1024,512]{1,0:T(8,128)(2,1)S(1)} %get-tuple-element.91), channel_id=1, source_target_pairs={{0,1},{1,0},{2,3},{3,2},{4,5},{5,4},{6,7},{7,6},{8,9},{9,8},{10,11... | collective-permute-start | bytes 3145736 | tf_op jit(solution)/shard_map/ppermute | solution.py:71
  103.5 10.2 %collective-permute-start.17 = (bf16[1024,256]{1,0:T(8,128)(2,1)S(1)}, bf16[1024,256]{1,0:T(8,128)(2,1)S(1)}, u32[]{:S(2)}, u32[]{:S(2)}) collective-permute-start(bf16[1024,256]{1,0:T(8,128)(2,1)S(1)} %broadcast_select_fusion.9), channel_id=1, source_target_pairs={{0,4},{1,5},{2,6},{3,7},{4,0},{5,1},{6,2},{7,3},{8,12},{9,13},{10,... | collective-permute-start | bytes 1572872 | tf_op jit(solution)/shard_map/ppermute | solution.py:68
  104.7 16.3 %collective-permute-start.18 = (f32[1024,128]{1,0:T(8,128)S(1)}, f32[1024,128]{1,0:T(8,128)S(1)}, u32[]{:S(2)}, u32[]{:S(2)}) collective-permute-start(f32[1024,128]{1,0:T(8,128)S(1)} %convolution_add_fusion.2), channel_id=1, source_target_pairs={{0,2},{1,3},{2,0},{3,1},{4,6},{5,7},{6,4},{7,5},{8,10},{9,11},{10,... | collective-permute-start | bytes 1572872 | tf_op jit(solution)/shard_map/ppermute | solution.py:65
  110.0 27.7 %collective-permute-start.25 = (bf16[1024,512]{1,0:T(8,128)(2,1)S(1)}, bf16[1024,512]{1,0:T(8,128)(2,1)S(1)}, u32[]{:S(2)}, u32[]{:S(2)}) collective-permute-start(bf16[1024,512]{1,0:T(8,128)(2,1)S(1)} %copy-done.2), channel_id=1, source_target_pairs={{0,1},{1,0},{2,3},{3,2},{4,5},{5,4},{6,7},{7,6},{8,9},{9,8},{10,11... | collective-permute-start | bytes 3145736 | tf_op jit(solution)/shard_map/ppermute | solution.py:71
  121.1 13.8 %collective-permute-start.19 = (bf16[1024,256]{1,0:T(8,128)(2,1)S(1)}, bf16[1024,256]{1,0:T(8,128)(2,1)S(1)}, u32[]{:S(2)}, u32[]{:S(2)}) collective-permute-start(bf16[1024,256]{1,0:T(8,128)(2,1)S(1)} %broadcast_select_fusion.8), channel_id=1, source_target_pairs={{0,4},{1,5},{2,6},{3,7},{4,0},{5,1},{6,2},{7,3},{8,12},{9,13},{10,... | collective-permute-start | bytes 1572872 | tf_op jit(solution)/shard_map/ppermute | solution.py:68
  122.9 14.8 %collective-permute-start.23 = (bf16[1024,256]{1,0:T(8,128)(2,1)S(1)}, bf16[1024,256]{1,0:T(8,128)(2,1)S(1)}, u32[]{:S(2)}, u32[]{:S(2)}) collective-permute-start(bf16[1024,256]{1,0:T(8,128)(2,1)S(1)} %get-tuple-element.93), channel_id=1, source_target_pairs={{0,1},{1,0},{2,3},{3,2},{4,5},{5,4},{6,7},{7,6},{8,9},{9,8},{10,11... | collective-permute-start | bytes 1572872 | tf_op jit(solution)/shard_map/ppermute | solution.py:71
  123.0 19.1 %collective-permute-start.20 = (f32[1024,128]{1,0:T(8,128)S(1)}, f32[1024,128]{1,0:T(8,128)S(1)}, u32[]{:S(2)}, u32[]{:S(2)}) collective-permute-start(f32[1024,128]{1,0:T(8,128)S(1)} %convolution_add_fusion.1), channel_id=1, source_target_pairs={{0,2},{1,3},{2,0},{3,1},{4,6},{5,7},{6,4},{7,5},{8,10},{9,11},{10,... | collective-permute-start | bytes 1572872 | tf_op jit(solution)/shard_map/ppermute | solution.py:65
  135.0 2.7 %collective-permute-start.24 = (bf16[1024,256]{1,0:T(8,128)(2,1)S(1)}, bf16[1024,256]{1,0:T(8,128)(2,1)S(1)}, u32[]{:S(2)}, u32[]{:S(2)}) collective-permute-start(bf16[1024,256]{1,0:T(8,128)(2,1)S(1)} %get-tuple-element.95), channel_id=1, source_target_pairs={{0,1},{1,0},{2,3},{3,2},{4,5},{5,4},{6,7},{7,6},{8,9},{9,8},{10,11... | collective-permute-start | bytes 1572872 | tf_op jit(solution)/shard_map/ppermute | solution.py:71

commit v6 on v5

--- a/solution.py
+++ b/solution.py
@@ -93,18 +93,19 @@
         e = [columns(expected_cot, i, i + 1) for i in range(4)]
         v = [columns(value_next, i, i + 1) for i in range(4)]
         first_cross, first_jump, e3 = together(
-            (jnp.where(home, v[0], e[0]), jnp.where(home, e[0], e[2]), e[3])
+            (jnp.concatenate([jnp.where(home, v[0], e[0]), v[2]], 1), jnp.where(home, e[0], e[2]), e[3])
         )
         x1 = cross(first_cross)
+        x1, v_across2 = columns(x1, 0, 1), columns(x1, 1, 2)
         j1 = jump(first_jump)
         v1, e1 = together((v[1], e[1]), x1, j1)
         x2 = cross(jnp.where(home, v1, e1))
         near, far = together((x1, e3), j1)
         j2 = jump(jnp.where(home, near, far))
-        t_other = swap(after(transition, j1))
+        t_other = swap(transition)
         near, far = together((j1, v[0]), x2)
         x3 = cross(jnp.where(home, near, far))
-        t, t_o = together((transition, t_other), x2)
+        t, t_o = together((transition, t_other), x3)
         t_near, t_next = jnp.where(mine, t, t_o), jnp.where(mine, t_o, t)
 
         def adjoint_of(near, far):
@@ -113,11 +114,11 @@
         near, far = together((x2, x3), j2)
         j3 = jump(jnp.where(home, near, far))
         near, far = together((j2, v[1]), x3)
-        x4 = cross(jnp.where(home, near, far))
+        x4 = cross(jnp.concatenate([jnp.where(home, near, far), v[3]], 1))
+        x4, v_across3 = columns(x4, 0, 1), columns(x4, 1, 2)
         near, far = together((x1, j2), x3, t_near)
         b0 = jnp.where(home, near, far)
         b0_next = step(b0)
-        x5 = cross(after(columns(value_next, 2, 4), x4, b0_next))
         near, far = together((e[1], x4), j3, b0_next)
         j4 = jump(jnp.where(home, near, far))
         sum0 = adjoint_of(b0, b0_next)
@@ -125,12 +126,12 @@
         near, far = together((x2, j3), sum0, x4)
         b1 = jnp.where(home, near, far)
         b1_next = step(b1)
-        part1 = cross(after(adjoint_of(b1, b1_next), x5, part0))
+        part1 = cross(after(adjoint_of(b1, b1_next), part0))
         near, far = together((j3, x3), b1_next)
         b2 = jnp.where(home, near, far)
         b2_next = step(b2)
         part2 = cross(after(adjoint_of(b2, b2_next), part1))
-        near, far = together((j4, x4), b2_next, part0, x5)
+        near, far = together((j4, x4), b2_next, part0)
         b3 = jnp.where(home, near, far)
         b3_next = step(b3)
         part3 = cross(after(adjoint_of(b3, b3_next), part2))
@@ -144,7 +145,8 @@
             return jnp.where(mine, near, far), swap(jnp.where(mine, far, near))
 
         v_across = jnp.concatenate(
-            [jnp.where(home, jnp.concatenate([x3, x4], 1), jnp.concatenate([x1, x2], 1)), x5], 1
+            [jnp.where(home, jnp.concatenate([x3, x4], 1), jnp.concatenate([x1, x2], 1)), v_across2, v_across3],
+            1,
         )
         v_across_other = swap(after(v_across, b1_next))
         b_own, b_swapped = own_and_swapped(

time: 144 us -> 134 us (0.931)
  waiting for transfers between devices: 82.5 us -> 72.4 us
  starting transfers between devices: 34.8 us -> 32.4 us
  other arithmetic: 9.05 us -> 11 us
    ppermute x4, waiting for transfers between devices: 29.2 us -> 16.9 us  [jump(): return lax.ppermute(a, AXES, jump_pairs)]
    ppermute x6, waiting for transfers between devices: 19.8 us -> 24 us  [step(): return lax.ppermute(a, AXES, step_pairs)]
    ppermute x9 -> x8, starting transfers between devices: 13.2 us -> 10.9 us  [cross(): return lax.ppermute(a, AXES, cross_pairs)]
    ppermute x9 -> x8, waiting for transfers between devices: 33.4 us -> 31.5 us  [cross(): return lax.ppermute(a, AXES, cross_pairs)]
  transfers between devices with their start and end apart: 26 -> 25, of which waited for: 14 -> 13; matrix products, arithmetic and copies ran while one was open for 15% -> 17% of each run, Pallas kernels for 0% -> 0%
where the time goes in v6:
time: 134 us
  waiting for transfers between devices  72.4 us (54%)
  starting transfers between devices  32.4 us (24%)
  matrix products  15.3 us (11%)
  other arithmetic  11 us (8%)
  between operations  1.69 us (1%)
    ppermute x8, waiting for transfers between devices, cross(): return lax.ppermute(a, AXES, cross_pairs)  31.5 us
    ppermute x6, waiting for transfers between devices, step(): return lax.ppermute(a, AXES, step_pairs)  24 us
    ppermute x4, waiting for transfers between devices, jump(): return lax.ppermute(a, AXES, jump_pairs)  16.9 us
    ppermute x6, starting transfers between devices, step(): return lax.ppermute(a, AXES, step_pairs)  11.3 us
    ppermute x8, starting transfers between devices, cross(): return lax.ppermute(a, AXES, cross_pairs)  10.9 us
    dot_general x10, matrix products, tdot(): lax.dot_general(a, b, (((0,), (0,)), ((), ())), preferred_element_type=jn...  8.57 us
    dot_general x2, matrix products, dott(): lax.dot_general(a, b, (((1,), (1,)), ((), ())), preferred_element_type=jn...  6.75 us
    ppermute x1, starting transfers between devices, home_jump(): return lax.ppermute(a, AXES, home_jump_pairs)  5.34 us
  transfers between devices with their start and end apart: 25, of which 13 were waited for; matrix products, arithmetic and copies ran while one was open for 17% of the time, Pallas kernels for 0%

profile of v6, /device:TPU:0, one launch (start us, length us, event | category | flops | bytes accessed | tf_op | source)
XLA Modules:
  0.0 133.8 jit_solution(9347635850728235415)
XLA Ops:
  0.7 2.6 %fusion.39 = (bf16[1024,128]{1,0:T(8,128)(2,1)}, bf16[1024,128]{1,0:T(8,128)(2,1)S(1)}, bf16[1024,128]{1,0:T(8,128)(2,1)S(1)}, bf16[1024,128]{1,0:T(8,128)(2,1)S...) fusion(bf16[1024,512]{1,0:T(8,128)(2,1)} %param.5, ...), kind=kLoop, calls=%fused_computation.74 | loop fusion | flops 262144 | bytes 4194305 | tf_op jit(solution)/shard_map/slice | solution.py:88
  3.3 3.0 %collective-permute-start.2 = (bf16[1024,256]{1,0:T(8,128)(2,1)S(1)}, bf16[1024,256]{1,0:T(8,128)(2,1)S(1)}, u32[]{:S(2)}, u32[]{:S(2)}) collective-permute-start(bf16[1024,256]{1,0:T(8,128)(2,1)S(1)} %pad_maximum_fusion.2), channel_id=1, source_target_pairs={{0,2},{1,3},{2,0},{3,1},{4,6},{5,7},{6,4},{7,5},{8,10},{9,11},{10,... | collective-permute-start | bytes 1572872 | tf_op jit(solution)/shard_map/ppermute | solution.py:65
  6.3 2.6 %collective-permute-start.1 = (bf16[1024,128]{1,0:T(8,128)(2,1)S(1)}, bf16[1024,128]{1,0:T(8,128)(2,1)S(1)}, u32[]{:S(2)}, u32[]{:S(2)}) collective-permute-start(bf16[1024,128]{1,0:T(8,128)(2,1)S(1)} %get-tuple-element.43), channel_id=1, source_target_pairs={{0,8},{1,9},{2,10},{3,11},{4,12},{5,13},{6,14},{7,15},{8,0},{9,1},... | collective-permute-start | bytes 786440 | tf_op jit(solution)/shard_map/ppermute | solution.py:77
  8.9 9.3 %collective-permute-done.2 = bf16[1024,256]{1,0:T(8,128)(2,1)S(1)} collective-permute-done((bf16[1024,256]{1,0:T(8,128)(2,1)S(1)}, bf16[1024,256]{1,0:T(8,128)(2,1)S(1)}, u32[]{:S(2)}, u32[]{:S(2)}) %collective-permute-start.2) | collective-permute-done | bytes 524320 | tf_op jit(solution)/shard_map/ppermute | solution.py:65
  18.2 0.7 fusion.40
  18.9 2.6 %collective-permute-done.1 = bf16[1024,128]{1,0:T(8,128)(2,1)S(1)} collective-permute-done((bf16[1024,128]{1,0:T(8,128)(2,1)S(1)}, bf16[1024,128]{1,0:T(8,128)(2,1)S(1)}, u32[]{:S(2)}, u32[]{:S(2)}) %collective-permute-start.1) | collective-permute-done | bytes 262176 | tf_op jit(solution)/shard_map/ppermute | solution.py:77
  21.6 0.5 collective-permute-start.3
  22.1 0.7 broadcast_select_fusion.17
  22.8 1.3 collective-permute-start.5
  24.1 5.5 %collective-permute-done.3 = bf16[1024,128]{1,0:T(8,128)(2,1)S(1)} collective-permute-done((bf16[1024,128]{1,0:T(8,128)(2,1)S(1)}, bf16[1024,128]{1,0:T(8,128)(2,1)S(1)}, u32[]{:S(2)}, u32[]{:S(2)}) %collective-permute-start.3) | collective-permute-done | bytes 262176 | tf_op jit(solution)/shard_map/ppermute | solution.py:65
  29.6 0.7 broadcast_select_fusion.18
  30.3 0.7 collective-permute-start.4
  31.0 6.6 %collective-permute-done.5 = bf16[1024,128]{1,0:T(8,128)(2,1)} collective-permute-done((bf16[1024,128]{1,0:T(8,128)(2,1)}, bf16[1024,128]{1,0:T(8,128)(2,1)}, u32[]{:S(2)}, u32[]{:S(2)}) %collective-permute-start.5) | collective-permute-done | bytes 262176 | tf_op jit(solution)/shard_map/ppermute | solution.py:77
  37.6 0.1 collective-permute-start.7
  37.7 1.0 broadcast_select_fusion.16
  38.6 1.0 pad_maximum_fusion.3
  39.7 0.5 collective-permute-start.6
  40.1 1.9 %broadcast_select_fusion.1 = (bf16[1024,1024]{1,0:T(8,128)(2,1)S(1)}, bf16[1024,1024]{1,0:T(8,128)(2,1)S(1)}) fusion(bf16[1024,1024]{1,0:T(8,128)(2,1)S(1)} %copy-done.1, bf16[1024,1024]{1,0:T(8,128)(2,1)} %collective-permute-done, pred[]{:T(512)S(6)} %eq.8), kind=kLoop, calls=%fused_computation.26 | loop fusion | flops 2097152 | bytes 8388609 | tf_op jit(solution)/shard_map/jit(_where)/select_n | solution.py:109
  42.0 4.5 %collective-permute-start.8 = (bf16[1024,128]{1,0:T(8,128)(2,1)S(1)}, bf16[1024,128]{1,0:T(8,128)(2,1)S(1)}, u32[]{:S(2)}, u32[]{:S(2)}) collective-permute-start(bf16[1024,128]{1,0:T(8,128)(2,1)S(1)} %broadcast_select_fusion.14), channel_id=1, source_target_pairs={{0,4},{1,5},{2,6},{3,7},{4,0},{5,1},{6,2},{7,3},{8,12},{9,13},{10,... | collective-permute-start | bytes 786440 | tf_op jit(solution)/shard_map/ppermute | solution.py:68
  46.6 0.1 fusion.38
  47.4 5.1 %collective-permute-done.6 = bf16[1024,256]{1,0:T(8,128)(2,1)S(1)} collective-permute-done((bf16[1024,256]{1,0:T(8,128)(2,1)S(1)}, bf16[1024,256]{1,0:T(8,128)(2,1)S(1)}, u32[]{:S(2)}, u32[]{:S(2)}) %collective-permute-start.6) | collective-permute-done | bytes 524320 | tf_op jit(solution)/shard_map/ppermute | solution.py:65
  52.5 3.1 %collective-permute-done.8 = bf16[1024,128]{1,0:T(8,128)(2,1)S(1)} collective-permute-done((bf16[1024,128]{1,0:T(8,128)(2,1)S(1)}, bf16[1024,128]{1,0:T(8,128)(2,1)S(1)}, u32[]{:S(2)}, u32[]{:S(2)}) %collective-permute-start.8) | collective-permute-done | bytes 262176 | tf_op jit(solution)/shard_map/ppermute | solution.py:68
  55.7 0.6 collective-permute-start.9
  56.3 0.7 fusion.42
  57.0 0.8 convolution_add_fusion.4
  57.8 2.5 %collective-permute-start.10 = (bf16[1024,128]{1,0:T(8,128)(2,1)S(1)}, bf16[1024,128]{1,0:T(8,128)(2,1)S(1)}, u32[]{:S(2)}, u32[]{:S(2)}) collective-permute-start(bf16[1024,128]{1,0:T(8,128)(2,1)S(1)} %broadcast_select_fusion.12), channel_id=1, source_target_pairs={{0,4},{1,5},{2,6},{3,7},{4,0},{5,1},{6,2},{7,3},{8,12},{9,13},{10,... | collective-permute-start | bytes 786440 | tf_op jit(solution)/shard_map/ppermute | solution.py:68
  60.4 0.2 maximum_select_fusion
  60.6 0.1 pad_maximum_fusion.1
  60.7 0.8 collective-permute-start.12
  61.5 7.8 %collective-permute-done.9 = bf16[1024,128]{1,0:T(8,128)(2,1)S(1)} collective-permute-done((bf16[1024,128]{1,0:T(8,128)(2,1)S(1)}, bf16[1024,128]{1,0:T(8,128)(2,1)S(1)}, u32[]{:S(2)}, u32[]{:S(2)}) %collective-permute-start.9) | collective-permute-done | bytes 262176 | tf_op jit(solution)/shard_map/ppermute | solution.py:77
  69.2 1.7 %collective-permute-done.10 = bf16[1024,128]{1,0:T(8,128)(2,1)S(1)} collective-permute-done((bf16[1024,128]{1,0:T(8,128)(2,1)S(1)}, bf16[1024,128]{1,0:T(8,128)(2,1)S(1)}, u32[]{:S(2)}, u32[]{:S(2)}) %collective-permute-start.10) | collective-permute-done | bytes 262176 | tf_op jit(solution)/shard_map/ppermute | solution.py:68
  71.0 0.1 collective-permute-start.11
  71.0 5.3 %collective-permute-start.15 = (bf16[1024,256]{1,0:T(8,128)(2,1)S(1)}, bf16[1024,256]{1,0:T(8,128)(2,1)S(1)}, u32[]{:S(2)}, u32[]{:S(2)}) collective-permute-start(bf16[1024,256]{1,0:T(8,128)(2,1)S(1)} %get-tuple-element.74), channel_id=1, source_target_pairs={{0,8},{1,9},{4,12},{5,13},{10,2},{11,3},{14,6},{15,7},{16,24},{17,... | collective-permute-start | bytes 1572872 | tf_op jit(solution)/shard_map/ppermute | solution.py:74
  76.4 0.1 collective-permute-start.21
  76.5 0.7 fusion.43
  77.3 0.1 constant_dynamic-update-slice_fusion.2
  77.4 0.8 convolution_add_fusion.3
  78.1 0.3 collective-permute-done.11
  78.4 0.7 fusion.44
  79.2 1.9 %collective-permute-start.13 = (bf16[1024,128]{1,0:T(8,128)(2,1)S(1)}, bf16[1024,128]{1,0:T(8,128)(2,1)S(1)}, u32[]{:S(2)}, u32[]{:S(2)}) collective-permute-start(bf16[1024,128]{1,0:T(8,128)(2,1)S(1)} %broadcast_select_fusion.10), channel_id=1, source_target_pairs={{0,4},{1,5},{2,6},{3,7},{4,0},{5,1},{6,2},{7,3},{8,12},{9,13},{10,... | collective-permute-start | bytes 786440 | tf_op jit(solution)/shard_map/ppermute | solution.py:68
  81.1 0.8 convolution_add_fusion.2
  81.9 3.3 %collective-permute-start.14 = (f32[1024,128]{1,0:T(8,128)S(1)}, f32[1024,128]{1,0:T(8,128)S(1)}, u32[]{:S(2)}, u32[]{:S(2)}) collective-permute-start(f32[1024,128]{1,0:T(8,128)S(1)} %convolution_add_fusion.3), channel_id=1, source_target_pairs={{0,2},{1,3},{2,0},{3,1},{4,6},{5,7},{6,4},{7,5},{8,10},{9,11},{10,... | collective-permute-start | bytes 1572872 | tf_op jit(solution)/shard_map/ppermute | solution.py:65
  85.3 7.8 %collective-permute-done.13 = bf16[1024,128]{1,0:T(8,128)(2,1)S(1)} collective-permute-done((bf16[1024,128]{1,0:T(8,128)(2,1)S(1)}, bf16[1024,128]{1,0:T(8,128)(2,1)S(1)}, u32[]{:S(2)}, u32[]{:S(2)}) %collective-permute-start.13) | collective-permute-done | bytes 262176 | tf_op jit(solution)/shard_map/ppermute | solution.py:68
  93.1 0.1 constant_dynamic-update-slice_fusion
  93.2 0.6 broadcast_select_fusion.3
  93.8 0.1 collective-permute-start.20
  93.9 1.4 %collective-permute-done.14 = f32[1024,128]{1,0:T(8,128)S(1)} collective-permute-done((f32[1024,128]{1,0:T(8,128)S(1)}, f32[1024,128]{1,0:T(8,128)S(1)}, u32[]{:S(2)}, u32[]{:S(2)}) %collective-permute-start.14) | collective-permute-done | bytes 524320 | tf_op jit(solution)/shard_map/ppermute | solution.py:65
  95.3 1.8 %collective-permute-start.16 = (bf16[1024,256]{1,0:T(8,128)(2,1)S(1)}, bf16[1024,256]{1,0:T(8,128)(2,1)S(1)}, u32[]{:S(2)}, u32[]{:S(2)}) collective-permute-start(bf16[1024,256]{1,0:T(8,128)(2,1)S(1)} %broadcast_select_fusion.9), channel_id=1, source_target_pairs={{0,4},{1,5},{2,6},{3,7},{4,0},{5,1},{6,2},{7,3},{8,12},{9,13},{10,... | collective-permute-start | bytes 1572872 | tf_op jit(solution)/shard_map/ppermute | solution.py:68
  97.1 1.7 %collective-permute-start.17 = (f32[1024,128]{1,0:T(8,128)S(1)}, f32[1024,128]{1,0:T(8,128)S(1)}, u32[]{:S(2)}, u32[]{:S(2)}) collective-permute-start(f32[1024,128]{1,0:T(8,128)S(1)} %convolution_add_fusion.2), channel_id=1, source_target_pairs={{0,2},{1,3},{2,0},{3,1},{4,6},{5,7},{6,4},{7,5},{8,10},{9,11},{10,... | collective-permute-start | bytes 1572872 | tf_op jit(solution)/shard_map/ppermute | solution.py:65
  98.9 0.7 fusion.45
  99.6 0.8 convolution_add_fusion.1
  100.4 10.2 %collective-permute-done.17 = f32[1024,128]{1,0:T(8,128)S(1)} collective-permute-done((f32[1024,128]{1,0:T(8,128)S(1)}, f32[1024,128]{1,0:T(8,128)S(1)}, u32[]{:S(2)}, u32[]{:S(2)}) %collective-permute-start.17) | collective-permute-done | bytes 524320 | tf_op jit(solution)/shard_map/ppermute | solution.py:65
  110.6 0.3 collective-permute-start.19
  111.0 0.4 collective-permute-start.18
  111.4 0.1 broadcast_select_fusion.7
  111.5 0.1 collective-permute-start.22
  111.6 2.4 %fusion = f32[1024,1024]{1,0:T(8,128)S(1)} fusion(bf16[1024,512]{1,0:T(8,128)(2,1)S(1)} %collective-permute-done.20, bf16[1024,512]{1,0:T(8,128)(2,1)S(1)} %get-tuple-element.86, bf16[1024,512]{1,0:T(8,128)(2,1)S(1)} %collective-permute-done.21, bf16[1024,128]{1,0:T(8,128)(2,1)S(1)} %get-tuple-element.104, bf16[1024,128]{1,0:T(8,128)(2,1)S(1)} %copy-done.5, ...), kind=kOutput, calls=%fused_computation.1 | convolution fusion | flops 2160066560 | bytes 8388608 | tf_op jit(solution)/shard_map/dot_general | solution.py:38
  113.9 11.1 %collective-permute-done.18 = bf16[1024,256]{1,0:T(8,128)(2,1)S(1)} collective-permute-done((bf16[1024,256]{1,0:T(8,128)(2,1)S(1)}, bf16[1024,256]{1,0:T(8,128)(2,1)S(1)}, u32[]{:S(2)}, u32[]{:S(2)}) %collective-permute-start.18) | collective-permute-done | bytes 524320 | tf_op jit(solution)/shard_map/ppermute | solution.py:68
  125.0 0.1 broadcast_select_fusion.6
  125.1 0.1 collective-permute-start.23
  125.2 1.3 fusion.30
  126.5 1.3 convolution_add_fusion
  127.8 4.4 %add_multiply_fusion = f32[1024,1024]{1,0:T(8,128)} fusion(f32[1024,1024]{1,0:T(8,128)S(1)} %fusion, f32[]{:T(128)} %bitcast, bf16[1024,512]{1,0:T(8,128)(2,1)S(1)} %collective-permute-done.24, bf16[1024,512]{1,0:T(8,128)(2,1)S(1)} %copy-done.2, bf16[1024,256]{1,0:T(8,128)(2,1)S(1)} %collective-permute-done.23, ...), kind=kOutput, calls=%fused_computation | convolution fusion | flops 2162163712 | bytes 12582916 | tf_op jit(solution)/shard_map/dot_general | solution.py:38
  132.2 1.6 %fusion.22 = f32[1024,512]{1,0:T(8,128)} fusion(f32[1024,512]{1,0:T(8,128)S(1)} %convolution_add_fusion, f32[1024,128]{1,0:T(8,128)S(1)} %collective-permute-done.19, f32[1024,128]{1,0:T(8,128)S(1)} %collective-permute-done.17, f32[1024,128]{1,0:T(8,128)S(1)} %collective-permute-done.14, f32[1024,128]{1,0:T(8,128)S(1)} %collective-permute-done.12, f32[]{:T(128)} %bitcast), kind=kLoop, calls=%fused_computation.24 | loop fusion | flops 2621440 | bytes 6291460 | tf_op jit(solution)/shard_map/mul | solution.py:171
  (40 shorter events, 0.7 us)
Async XLA Ops:
  0.6 5.6 %copy-start.1 = (bf16[1024,1024]{1,0:T(8,128)(2,1)S(1)}, bf16[1024,1024]{1,0:T(8,128)(2,1)}, u32[]{:S(2)}) copy-start(bf16[1024,1024]{1,0:T(8,128)(2,1)} %param.6) | copy-start | bytes 6291460
  3.3 14.9 %collective-permute-start.2 = (bf16[1024,256]{1,0:T(8,128)(2,1)S(1)}, bf16[1024,256]{1,0:T(8,128)(2,1)S(1)}, u32[]{:S(2)}, u32[]{:S(2)}) collective-permute-start(bf16[1024,256]{1,0:T(8,128)(2,1)S(1)} %pad_maximum_fusion.2), channel_id=1, source_target_pairs={{0,2},{1,3},{2,0},{3,1},{4,6},{5,7},{6,4},{7,5},{8,10},{9,11},{10,... | collective-permute-start | bytes 1572872 | tf_op jit(solution)/shard_map/ppermute | solution.py:65
  6.3 33.8 %collective-permute-start = (bf16[1024,1024]{1,0:T(8,128)(2,1)S(1)}, bf16[1024,1024]{1,0:T(8,128)(2,1)}, u32[]{:S(2)}, u32[]{:S(2)}) collective-permute-start(bf16[1024,1024]{1,0:T(8,128)(2,1)S(1)} %copy-done.1), channel_id=1, source_target_pairs={{0,1},{1,0},{2,3},{3,2},{4,5},{5,4},{6,7},{7,6},{8,9},{9,8},{10,11... | collective-permute-start | bytes 6291464 | tf_op jit(solution)/shard_map/ppermute | solution.py:71
  6.3 15.2 %collective-permute-start.1 = (bf16[1024,128]{1,0:T(8,128)(2,1)S(1)}, bf16[1024,128]{1,0:T(8,128)(2,1)S(1)}, u32[]{:S(2)}, u32[]{:S(2)}) collective-permute-start(bf16[1024,128]{1,0:T(8,128)(2,1)S(1)} %get-tuple-element.43), channel_id=1, source_target_pairs={{0,8},{1,9},{2,10},{3,11},{4,12},{5,13},{6,14},{7,15},{8,0},{9,1},... | collective-permute-start | bytes 786440 | tf_op jit(solution)/shard_map/ppermute | solution.py:77
  21.5 8.8 %copy-start.3 = (bf16[1024,128]{1,0:T(8,128)(2,1)}, bf16[1024,128]{1,0:T(8,128)(2,1)S(1)}, u32[]{:S(2)}) copy-start(bf16[1024,128]{1,0:T(8,128)(2,1)S(1)} %collective-permute-done.1) | copy-start | bytes 786436
  21.6 8.0 %collective-permute-start.3 = (bf16[1024,128]{1,0:T(8,128)(2,1)S(1)}, bf16[1024,128]{1,0:T(8,128)(2,1)S(1)}, u32[]{:S(2)}, u32[]{:S(2)}) collective-permute-start(bf16[1024,128]{1,0:T(8,128)(2,1)S(1)} %broadcast_select_fusion.19), channel_id=1, source_target_pairs={{0,2},{1,3},{2,0},{3,1},{4,6},{5,7},{6,4},{7,5},{8,10},{9,11},{10,... | collective-permute-start | bytes 786440 | tf_op jit(solution)/shard_map/ppermute | solution.py:65
  22.8 14.7 %collective-permute-start.5 = (bf16[1024,128]{1,0:T(8,128)(2,1)}, bf16[1024,128]{1,0:T(8,128)(2,1)}, u32[]{:S(2)}, u32[]{:S(2)}) collective-permute-start(bf16[1024,128]{1,0:T(8,128)(2,1)} %broadcast_select_fusion.17), channel_id=1, source_target_pairs={{0,8},{1,9},{2,10},{3,11},{4,12},{5,13},{6,14},{7,15},{8,0},{9,1},... | collective-permute-start | bytes 786440 | tf_op jit(solution)/shard_map/ppermute | solution.py:77
  30.3 7.3 %collective-permute-start.4 = (bf16[1024,128]{1,0:T(8,128)(2,1)}, bf16[1024,128]{1,0:T(8,128)(2,1)S(1)}, u32[]{:S(2)}, u32[]{:S(2)}) collective-permute-start(bf16[1024,128]{1,0:T(8,128)(2,1)} %broadcast_select_fusion.18), channel_id=1, source_target_pairs={{0,2},{1,3},{2,0},{3,1},{4,6},{5,7},{6,4},{7,5},{8,10},{9,11},{10,... | collective-permute-start | bytes 786440 | tf_op jit(solution)/shard_map/ppermute | solution.py:65
  37.6 15.0 %collective-permute-start.7 = (bf16[1024,128]{1,0:T(8,128)(2,1)S(1)}, bf16[1024,128]{1,0:T(8,128)(2,1)S(1)}, u32[]{:S(2)}, u32[]{:S(2)}) collective-permute-start(bf16[1024,128]{1,0:T(8,128)(2,1)S(1)} %broadcast_select_fusion.15), channel_id=1, source_target_pairs={{0,8},{1,9},{2,10},{3,11},{4,12},{5,13},{6,14},{7,15},{8,0},{9,1},... | collective-permute-start | bytes 786440 | tf_op jit(solution)/shard_map/ppermute | solution.py:77
  39.7 6.9 %copy-start = (bf16[1024,512]{1,0:T(8,128)(2,1)S(1)}, bf16[1024,512]{1,0:T(8,128)(2,1)}, u32[]{:S(2)}) copy-start(bf16[1024,512]{1,0:T(8,128)(2,1)} %param.4) | copy-start | bytes 3145732
  39.7 12.8 %collective-permute-start.6 = (bf16[1024,256]{1,0:T(8,128)(2,1)S(1)}, bf16[1024,256]{1,0:T(8,128)(2,1)S(1)}, u32[]{:S(2)}, u32[]{:S(2)}) collective-permute-start(bf16[1024,256]{1,0:T(8,128)(2,1)S(1)} %pad_maximum_fusion.3), channel_id=1, source_target_pairs={{0,2},{1,3},{2,0},{3,1},{4,6},{5,7},{6,4},{7,5},{8,10},{9,11},{10,... | collective-permute-start | bytes 1572872 | tf_op jit(solution)/shard_map/ppermute | solution.py:65
  42.0 13.6 %collective-permute-start.8 = (bf16[1024,128]{1,0:T(8,128)(2,1)S(1)}, bf16[1024,128]{1,0:T(8,128)(2,1)S(1)}, u32[]{:S(2)}, u32[]{:S(2)}) collective-permute-start(bf16[1024,128]{1,0:T(8,128)(2,1)S(1)} %broadcast_select_fusion.14), channel_id=1, source_target_pairs={{0,4},{1,5},{2,6},{3,7},{4,0},{5,1},{6,2},{7,3},{8,12},{9,13},{10,... | collective-permute-start | bytes 786440 | tf_op jit(solution)/shard_map/ppermute | solution.py:68
  55.7 13.6 %collective-permute-start.9 = (bf16[1024,128]{1,0:T(8,128)(2,1)S(1)}, bf16[1024,128]{1,0:T(8,128)(2,1)S(1)}, u32[]{:S(2)}, u32[]{:S(2)}) collective-permute-start(bf16[1024,128]{1,0:T(8,128)(2,1)S(1)} %broadcast_select_fusion.13), channel_id=1, source_target_pairs={{0,8},{1,9},{2,10},{3,11},{4,12},{5,13},{6,14},{7,15},{8,0},{9,1},... | collective-permute-start | bytes 786440 | tf_op jit(solution)/shard_map/ppermute | solution.py:77
  57.8 2.8 %copy-start.5 = (bf16[1024,128]{1,0:T(8,128)(2,1)S(1)}, bf16[1024,128]{1,0:T(8,128)(2,1)}, u32[]{:S(2)}) copy-start(bf16[1024,128]{1,0:T(8,128)(2,1)} %get-tuple-element.102) | copy-start | bytes 786436
  57.8 13.1 %collective-permute-start.10 = (bf16[1024,128]{1,0:T(8,128)(2,1)S(1)}, bf16[1024,128]{1,0:T(8,128)(2,1)S(1)}, u32[]{:S(2)}, u32[]{:S(2)}) collective-permute-start(bf16[1024,128]{1,0:T(8,128)(2,1)S(1)} %broadcast_select_fusion.12), channel_id=1, source_target_pairs={{0,4},{1,5},{2,6},{3,7},{4,0},{5,1},{6,2},{7,3},{8,12},{9,13},{10,... | collective-permute-start | bytes 786440 | tf_op jit(solution)/shard_map/ppermute | solution.py:68
  60.5 15.9 %copy-start.4 = (bf16[1024,128]{1,0:T(8,128)(2,1)S(1)}, bf16[1024,128]{1,0:T(8,128)(2,1)}, u32[]{:S(2)}) copy-start(bf16[1024,128]{1,0:T(8,128)(2,1)} %copy-done.3) | copy-start | bytes 786436
  60.7 18.5 %collective-permute-start.12 = (f32[1024,128]{1,0:T(8,128)S(1)}, f32[1024,128]{1,0:T(8,128)S(1)}, u32[]{:S(2)}, u32[]{:S(2)}) collective-permute-start(f32[1024,128]{1,0:T(8,128)S(1)} %convolution_add_fusion.4), channel_id=1, source_target_pairs={{0,2},{1,3},{2,0},{3,1},{4,6},{5,7},{6,4},{7,5},{8,10},{9,11},{10,... | collective-permute-start | bytes 1572872 | tf_op jit(solution)/shard_map/ppermute | solution.py:65
  71.0 7.4 %collective-permute-start.11 = (bf16[1024,128]{1,0:T(8,128)(2,1)S(1)}, bf16[1024,128]{1,0:T(8,128)(2,1)S(1)}, u32[]{:S(2)}, u32[]{:S(2)}) collective-permute-start(bf16[1024,128]{1,0:T(8,128)(2,1)S(1)} %broadcast_select_fusion.11), channel_id=1, source_target_pairs={{0,4},{1,5},{2,6},{3,7},{4,0},{5,1},{6,2},{7,3},{8,12},{9,13},{10,... | collective-permute-start | bytes 786440 | tf_op jit(solution)/shard_map/ppermute | solution.py:68
  71.0 39.5 %collective-permute-start.15 = (bf16[1024,256]{1,0:T(8,128)(2,1)S(1)}, bf16[1024,256]{1,0:T(8,128)(2,1)S(1)}, u32[]{:S(2)}, u32[]{:S(2)}) collective-permute-start(bf16[1024,256]{1,0:T(8,128)(2,1)S(1)} %get-tuple-element.74), channel_id=1, source_target_pairs={{0,8},{1,9},{4,12},{5,13},{10,2},{11,3},{14,6},{15,7},{16,24},{17,... | collective-permute-start | bytes 1572872 | tf_op jit(solution)/shard_map/ppermute | solution.py:74
  76.4 35.1 %collective-permute-start.21 = (bf16[1024,512]{1,0:T(8,128)(2,1)S(1)}, bf16[1024,512]{1,0:T(8,128)(2,1)S(1)}, u32[]{:S(2)}, u32[]{:S(2)}) collective-permute-start(bf16[1024,512]{1,0:T(8,128)(2,1)S(1)} %pad_maximum_fusion.1), channel_id=1, source_target_pairs={{0,1},{1,0},{2,3},{3,2},{4,5},{5,4},{6,7},{7,6},{8,9},{9,8},{10,11... | collective-permute-start | bytes 3145736 | tf_op jit(solution)/shard_map/ppermute | solution.py:71
  79.2 13.9 %collective-permute-start.13 = (bf16[1024,128]{1,0:T(8,128)(2,1)S(1)}, bf16[1024,128]{1,0:T(8,128)(2,1)S(1)}, u32[]{:S(2)}, u32[]{:S(2)}) collective-permute-start(bf16[1024,128]{1,0:T(8,128)(2,1)S(1)} %broadcast_select_fusion.10), channel_id=1, source_target_pairs={{0,4},{1,5},{2,6},{3,7},{4,0},{5,1},{6,2},{7,3},{8,12},{9,13},{10,... | collective-permute-start | bytes 786440 | tf_op jit(solution)/shard_map/ppermute | solution.py:68
  81.9 13.4 %collective-permute-start.14 = (f32[1024,128]{1,0:T(8,128)S(1)}, f32[1024,128]{1,0:T(8,128)S(1)}, u32[]{:S(2)}, u32[]{:S(2)}) collective-permute-start(f32[1024,128]{1,0:T(8,128)S(1)} %convolution_add_fusion.3), channel_id=1, source_target_pairs={{0,2},{1,3},{2,0},{3,1},{4,6},{5,7},{6,4},{7,5},{8,10},{9,11},{10,... | collective-permute-start | bytes 1572872 | tf_op jit(solution)/shard_map/ppermute | solution.py:65
  93.8 17.8 %collective-permute-start.20 = (bf16[1024,512]{1,0:T(8,128)(2,1)S(1)}, bf16[1024,512]{1,0:T(8,128)(2,1)S(1)}, u32[]{:S(2)}, u32[]{:S(2)}) collective-permute-start(bf16[1024,512]{1,0:T(8,128)(2,1)S(1)} %get-tuple-element.87), channel_id=1, source_target_pairs={{0,1},{1,0},{2,3},{3,2},{4,5},{5,4},{6,7},{7,6},{8,9},{9,8},{10,11... | collective-permute-start | bytes 3145736 | tf_op jit(solution)/shard_map/ppermute | solution.py:71
  95.3 15.6 %collective-permute-start.16 = (bf16[1024,256]{1,0:T(8,128)(2,1)S(1)}, bf16[1024,256]{1,0:T(8,128)(2,1)S(1)}, u32[]{:S(2)}, u32[]{:S(2)}) collective-permute-start(bf16[1024,256]{1,0:T(8,128)(2,1)S(1)} %broadcast_select_fusion.9), channel_id=1, source_target_pairs={{0,4},{1,5},{2,6},{3,7},{4,0},{5,1},{6,2},{7,3},{8,12},{9,13},{10,... | collective-permute-start | bytes 1572872 | tf_op jit(solution)/shard_map/ppermute | solution.py:68
  97.1 13.4 %collective-permute-start.17 = (f32[1024,128]{1,0:T(8,128)S(1)}, f32[1024,128]{1,0:T(8,128)S(1)}, u32[]{:S(2)}, u32[]{:S(2)}) collective-permute-start(f32[1024,128]{1,0:T(8,128)S(1)} %convolution_add_fusion.2), channel_id=1, source_target_pairs={{0,2},{1,3},{2,0},{3,1},{4,6},{5,7},{6,4},{7,5},{8,10},{9,11},{10,... | collective-permute-start | bytes 1572872 | tf_op jit(solution)/shard_map/ppermute | solution.py:65
  99.6 10.9 %copy-start.2 = (bf16[1024,512]{1,0:T(8,128)(2,1)S(1)}, bf16[1024,512]{1,0:T(8,128)(2,1)}, u32[]{:S(2)}) copy-start(bf16[1024,512]{1,0:T(8,128)(2,1)} %param.5) | copy-start | bytes 3145732
  110.5 17.2 %collective-permute-start.24 = (bf16[1024,512]{1,0:T(8,128)(2,1)S(1)}, bf16[1024,512]{1,0:T(8,128)(2,1)S(1)}, u32[]{:S(2)}, u32[]{:S(2)}) collective-permute-start(bf16[1024,512]{1,0:T(8,128)(2,1)S(1)} %copy-done.2), channel_id=1, source_target_pairs={{0,1},{1,0},{2,3},{3,2},{4,5},{5,4},{6,7},{7,6},{8,9},{9,8},{10,11... | collective-permute-start | bytes 3145736 | tf_op jit(solution)/shard_map/ppermute | solution.py:71
  110.6 21.6 %collective-permute-start.19 = (f32[1024,128]{1,0:T(8,128)S(1)}, f32[1024,128]{1,0:T(8,128)S(1)}, u32[]{:S(2)}, u32[]{:S(2)}) collective-permute-start(f32[1024,128]{1,0:T(8,128)S(1)} %convolution_add_fusion.1), channel_id=1, source_target_pairs={{0,2},{1,3},{2,0},{3,1},{4,6},{5,7},{6,4},{7,5},{8,10},{9,11},{10,... | collective-permute-start | bytes 1572872 | tf_op jit(solution)/shard_map/ppermute | solution.py:65
  111.0 14.1 %collective-permute-start.18 = (bf16[1024,256]{1,0:T(8,128)(2,1)S(1)}, bf16[1024,256]{1,0:T(8,128)(2,1)S(1)}, u32[]{:S(2)}, u32[]{:S(2)}) collective-permute-start(bf16[1024,256]{1,0:T(8,128)(2,1)S(1)} %broadcast_select_fusion.8), channel_id=1, source_target_pairs={{0,4},{1,5},{2,6},{3,7},{4,0},{5,1},{6,2},{7,3},{8,12},{9,13},{10,... | collective-permute-start | bytes 1572872 | tf_op jit(solution)/shard_map/ppermute | solution.py:68
  111.5 16.3 %collective-permute-start.22 = (bf16[1024,256]{1,0:T(8,128)(2,1)S(1)}, bf16[1024,256]{1,0:T(8,128)(2,1)S(1)}, u32[]{:S(2)}, u32[]{:S(2)}) collective-permute-start(bf16[1024,256]{1,0:T(8,128)(2,1)S(1)} %get-tuple-element.89), channel_id=1, source_target_pairs={{0,1},{1,0},{2,3},{3,2},{4,5},{5,4},{6,7},{7,6},{8,9},{9,8},{10,11... | collective-permute-start | bytes 1572872 | tf_op jit(solution)/shard_map/ppermute | solution.py:71
  125.1 2.7 %collective-permute-start.23 = (bf16[1024,256]{1,0:T(8,128)(2,1)S(1)}, bf16[1024,256]{1,0:T(8,128)(2,1)S(1)}, u32[]{:S(2)}, u32[]{:S(2)}) collective-permute-start(bf16[1024,256]{1,0:T(8,128)(2,1)S(1)} %get-tuple-element.91), channel_id=1, source_target_pairs={{0,1},{1,0},{2,3},{3,2},{4,5},{5,4},{6,7},{7,6},{8,9},{9,8},{10,11... | collective-permute-start | bytes 1572872 | tf_op jit(solution)/shard_map/ppermute | solution.py:71

commit v7 on v6

--- a/solution.py
+++ b/solution.py
@@ -102,10 +102,12 @@
         x2 = cross(jnp.where(home, v1, e1))
         near, far = together((x1, e3), j1)
         j2 = jump(jnp.where(home, near, far))
+        a0 = jnp.where(home, e[0], j1)
+        a0_next = step(a0)
         t_other = swap(transition)
         near, far = together((j1, v[0]), x2)
         x3 = cross(jnp.where(home, near, far))
-        t, t_o = together((transition, t_other), x3)
+        t, t_o = together((transition, t_other), x2)
         t_near, t_next = jnp.where(mine, t, t_o), jnp.where(mine, t_o, t)
 
         def adjoint_of(near, far):
@@ -113,62 +115,73 @@
 
         near, far = together((x2, x3), j2)
         j3 = jump(jnp.where(home, near, far))
-        near, far = together((j2, v[1]), x3)
+        near, far = together((x1, j2), t_near, a0_next)
+        b0 = jnp.where(home, near, far)
+        b0_next = step(b0)
+        near, far = together((j2, v[1]), x3, b0)
         x4 = cross(jnp.concatenate([jnp.where(home, near, far), v[3]], 1))
         x4, v_across3 = columns(x4, 0, 1), columns(x4, 1, 2)
-        near, far = together((x1, j2), x3, t_near)
-        b0 = jnp.where(home, near, far)
-        b0_next = step(b0)
-        near, far = together((e[1], x4), j3, b0_next)
+        near, far = together((e[1], x4), j3)
         j4 = jump(jnp.where(home, near, far))
         sum0 = adjoint_of(b0, b0_next)
         part0 = cross(after(sum0, x4))
-        near, far = together((x2, j3), sum0, x4)
-        b1 = jnp.where(home, near, far)
-        b1_next = step(b1)
-        part1 = cross(after(adjoint_of(b1, b1_next), part0))
-        near, far = together((j3, x3), b1_next)
-        b2 = jnp.where(home, near, far)
-        b2_next = step(b2)
-        part2 = cross(after(adjoint_of(b2, b2_next), part1))
-        near, far = together((j4, x4), b2_next, part0)
-        b3 = jnp.where(home, near, far)
-        b3_next = step(b3)
-        part3 = cross(after(adjoint_of(b3, b3_next), part2))
-        j5 = home_jump(after(columns(expected_cot, 2, 4), j4))
-        v_other = swap(after(value_next, b1_next))
-        near, far = together((columns(expected_cot, 0, 2), jnp.concatenate([j1, j4], 1)), b3_next, part1)
-        a01 = jnp.where(home, near, far)
-        a01_next = step(a01)
+        near, both, far = together((x2, j3, x3), sum0)
+        b12 = jnp.where(home, jnp.concatenate([near, both], 1), jnp.concatenate([both, far], 1))
+        b12_next = step(b12)
+        sum12 = adjoint_of(b12, b12_next)
+        sum1, sum2 = columns(sum12, 0, 1), columns(sum12, 1, 2)
+        part1 = cross(after(sum1, part0))
+        part2 = cross(after(sum2, part1))
+        j5 = home_jump(after(e[2], j4))
+        near, both, far = together((e[1], j4, x4), sum12, part0)
+        a1b3 = jnp.where(home, jnp.concatenate([near, both], 1), jnp.concatenate([both, far], 1))
+        a1b3_next = step(a1b3)
+        j6 = home_jump(after(e[3], j5, part1))
+        v_other = swap(after(value_next, sum12))
+        sum3 = adjoint_of(columns(a1b3, 1, 2), columns(a1b3_next, 1, 2))
+        part3 = cross(after(sum3, part2))
 
         def own_and_swapped(near, far):
             return jnp.where(mine, near, far), swap(jnp.where(mine, far, near))
 
+        parts = together((x1, x2, x3, x4, v_across2, v_across3), sum12)
         v_across = jnp.concatenate(
-            [jnp.where(home, jnp.concatenate([x3, x4], 1), jnp.concatenate([x1, x2], 1)), v_across2, v_across3],
-            1,
-        )
-        v_across_other = swap(after(v_across, b1_next))
+            [jnp.where(home, parts[2], parts[0]), jnp.where(home, parts[3], parts[1]), parts[4], parts[5]], 1
+        )
+        v_across_other = swap(v_across)
+        a0, a0_next, b0, b0_next, b12, b12_next = together((a0, a0_next, b0, b0_next, b12, b12_next), a1b3_next, sum3, part2)
+        a1, a1_next = columns(a1b3, 0, 1), columns(a1b3_next, 0, 1)
         b_own, b_swapped = own_and_swapped(
-            jnp.concatenate([b0, b1, b2, b3], 1),
-            jnp.concatenate([b0_next, b1_next, b2_next, b3_next], 1),
+            jnp.concatenate([b0, b12, columns(a1b3, 1, 2)], 1),
+            jnp.concatenate([b0_next, b12_next, columns(a1b3_next, 1, 2)], 1),
+        )
+        a01_own, a01_swapped = own_and_swapped(
+            jnp.concatenate([a0, a1], 1), jnp.concatenate([a0_next, a1_next], 1)
         )
         grad = dott(
             jnp.concatenate([b_own, b_swapped], 1), jnp.concatenate([v_across, v_across_other], 1)
-        )
-        a01_own, a01_swapped = own_and_swapped(a01, a01_next)
-        near, far = together((columns(expected_cot, 2, 4), j5), a01_next, part2)
-        a23 = jnp.where(home, near, far)
-        a23_next = step(a23)
-        near, far = together((a23, a23_next), grad)
-        a23_own, a23_swapped = own_and_swapped(near, far)
+        ) + dott(
+            jnp.concatenate([a01_own, a01_swapped], 1),
+            jnp.concatenate([columns(value_next, 0, 2), columns(v_other, 0, 2)], 1),
+        )
+        near, far = together((e[2], j5), a1b3_next, sum3, part1)
+        a2 = jnp.where(home, near, far)
+        a2_next = step(a2)
+        own01 = adjoint_of(jnp.concatenate([a0, a1], 1), jnp.concatenate([a0_next, a1_next], 1))
+        near, far = together((e[3], j6), grad, own01, a2_next, part2)
+        a3 = jnp.where(home, near, far)
+        a3_next = step(a3)
+        a2_own, a2_swapped = own_and_swapped(a2, a2_next)
+        a3_own, a3_swapped = own_and_swapped(a3, a3_next)
         grad = df * (grad + dott(
-            jnp.concatenate([a01_own, a23_own, a01_swapped, a23_swapped], 1),
-            jnp.concatenate([value_next, v_other], 1),
+            jnp.concatenate([a2_own, a3_own, a2_swapped, a3_swapped], 1),
+            jnp.concatenate([columns(value_next, 2, 4), columns(v_other, 2, 4)], 1),
         ))
-        own = adjoint_of(jnp.concatenate([a01, a23], 1), jnp.concatenate([a01_next, a23_next], 1))
-        own, part3, grad = together((own, part3, grad))
-        adjoint = df * (own + jnp.concatenate([part0, part1, part2, part3], 1))
+        own23 = adjoint_of(jnp.concatenate([a2, a3], 1), jnp.concatenate([a2_next, a3_next], 1))
+        own23, part3, grad = together((own23, part3, grad))
+        adjoint = df * (
+            jnp.concatenate([own01, own23], 1) + jnp.concatenate([part0, part1, part2, part3], 1)
+        )
         return adjoint, grad
 
     return shards

time: 134 us -> 137 us (1.022)
  starting transfers between devices: 32.4 us -> 36 us
  waiting for transfers between devices: 72.4 us -> 75.6 us
  other arithmetic: 11 us -> 7.82 us
    ppermute x6, waiting for transfers between devices: 24 us -> 42.7 us  [step(): return lax.ppermute(a, AXES, step_pairs)]
    ppermute x8, waiting for transfers between devices: 31.5 us -> 14.4 us  [cross(): return lax.ppermute(a, AXES, cross_pairs)]
    ppermute x1 -> x2, starting transfers between devices: 5.34 us -> 10.4 us  [home_jump(): return lax.ppermute(a, AXES, home_jump_pairs)]
    ppermute x4, starting transfers between devices: 4.54 us -> 8.74 us  [jump(): return lax.ppermute(a, AXES, jump_pairs)]
    ppermute x8, starting transfers between devices: 10.9 us -> 7.25 us  [cross(): return lax.ppermute(a, AXES, cross_pairs)]
    ppermute x6, starting transfers between devices: 11.3 us -> 8.01 us  [step(): return lax.ppermute(a, AXES, step_pairs)]
    dot_general x2 -> x3, matrix products: 6.75 us -> 6.98 us  [dott(): lax.dot_general(a, b, (((1,), (1,)), ((), ())), preferred_element_type=jn...]
  transfers between devices with their start and end apart: 25 -> 27, of which waited for: 13 -> 12; matrix products, arithmetic and copies ran while one was open for 17% -> 16% of each run, Pallas kernels for 0% -> 0%
where the time goes in v7:
time: 137 us
  waiting for transfers between devices  75.6 us (55%)
  starting transfers between devices  36 us (26%)
  matrix products  14.5 us (11%)
  other arithmetic  7.82 us (6%)
  between operations  1.77 us (1%)
    ppermute x6, waiting for transfers between devices, step(): return lax.ppermute(a, AXES, step_pairs)  42.7 us
    ppermute x4, waiting for transfers between devices, jump(): return lax.ppermute(a, AXES, jump_pairs)  17.6 us
    ppermute x8, waiting for transfers between devices, cross(): return lax.ppermute(a, AXES, cross_pairs)  14.4 us
    ppermute x2, starting transfers between devices, home_jump(): return lax.ppermute(a, AXES, home_jump_pairs)  10.4 us
    ppermute x4, starting transfers between devices, jump(): return lax.ppermute(a, AXES, jump_pairs)  8.74 us
    ppermute x6, starting transfers between devices, step(): return lax.ppermute(a, AXES, step_pairs)  8.01 us
    dot_general x10, matrix products, tdot(): lax.dot_general(a, b, (((0,), (0,)), ((), ())), preferred_element_type=jn...  7.48 us
    ppermute x8, starting transfers between devices, cross(): return lax.ppermute(a, AXES, cross_pairs)  7.25 us
  transfers between devices with their start and end apart: 27, of which 12 were waited for; matrix products, arithmetic and copies ran while one was open for 16% of the time, Pallas kernels for 0%

profile of v7, /device:TPU:0, one launch (start us, length us, event | category | flops | bytes accessed | tf_op | source)
XLA Modules:
  0.0 136.5 jit_solution(8393313493496543257)
XLA Ops:
  0.6 0.5 collective-permute-start
  1.1 1.7 %fusion.46 = (bf16[1024,128]{1,0:T(8,128)(2,1)S(1)}, bf16[1024,128]{1,0:T(8,128)(2,1)S(1)}, bf16[1024,128]{1,0:T(8,128)(2,1)S(1)}, bf16[1024,128]{1,0:T(8,128)(2...) fusion(bf16[1024,512]{1,0:T(8,128)(2,1)} %param.5, ...), kind=kLoop, calls=%fused_computation.89 | loop fusion | flops 262144 | bytes 3670017 | tf_op jit(solution)/shard_map/slice | solution.py:88
  2.9 2.6 %collective-permute-start.1 = (bf16[1024,256]{1,0:T(8,128)(2,1)S(1)}, bf16[1024,256]{1,0:T(8,128)(2,1)S(1)}, u32[]{:S(2)}, u32[]{:S(2)}) collective-permute-start(bf16[1024,256]{1,0:T(8,128)(2,1)S(1)} %pad_maximum_fusion.3), channel_id=1, source_target_pairs={{0,2},{1,3},{2,0},{3,1},{4,6},{5,7},{6,4},{7,5},{8,10},{9,11},{10,... | collective-permute-start | bytes 1572872 | tf_op jit(solution)/shard_map/ppermute | solution.py:65
  5.5 2.6 %collective-permute-start.2 = (bf16[1024,128]{1,0:T(8,128)(2,1)S(1)}, bf16[1024,128]{1,0:T(8,128)(2,1)S(1)}, u32[]{:S(2)}, u32[]{:S(2)}) collective-permute-start(bf16[1024,128]{1,0:T(8,128)(2,1)S(1)} %get-tuple-element.54), channel_id=1, source_target_pairs={{0,8},{1,9},{2,10},{3,11},{4,12},{5,13},{6,14},{7,15},{8,0},{9,1},... | collective-permute-start | bytes 786440 | tf_op jit(solution)/shard_map/ppermute | solution.py:77
  8.1 12.3 %collective-permute-done.2 = bf16[1024,128]{1,0:T(8,128)(2,1)S(1)} collective-permute-done((bf16[1024,128]{1,0:T(8,128)(2,1)S(1)}, bf16[1024,128]{1,0:T(8,128)(2,1)S(1)}, u32[]{:S(2)}, u32[]{:S(2)}) %collective-permute-start.2) | collective-permute-done | bytes 262176 | tf_op jit(solution)/shard_map/ppermute | solution.py:77
  20.4 0.1 broadcast_select_fusion.20
  20.6 0.5 collective-permute-start.3
  21.2 1.4 %collective-permute-start.5 = (bf16[1024,128]{1,0:T(8,128)(2,1)S(1)}, bf16[1024,128]{1,0:T(8,128)(2,1)S(1)}, u32[]{:S(2)}, u32[]{:S(2)}) collective-permute-start(bf16[1024,128]{1,0:T(8,128)(2,1)S(1)} %broadcast_select_fusion.19), channel_id=1, source_target_pairs={{0,8},{1,9},{2,10},{3,11},{4,12},{5,13},{6,14},{7,15},{8,0},{9,1},... | collective-permute-start | bytes 786440 | tf_op jit(solution)/shard_map/ppermute | solution.py:77
  22.6 5.6 %collective-permute-done.3 = bf16[1024,128]{1,0:T(8,128)(2,1)S(1)} collective-permute-done((bf16[1024,128]{1,0:T(8,128)(2,1)S(1)}, bf16[1024,128]{1,0:T(8,128)(2,1)S(1)}, u32[]{:S(2)}, u32[]{:S(2)}) %collective-permute-start.3) | collective-permute-done | bytes 262176 | tf_op jit(solution)/shard_map/ppermute | solution.py:65
  28.3 0.9 collective-permute-start.7
  29.2 1.1 collective-permute-start.4
  30.2 5.3 %collective-permute-done.5 = bf16[1024,128]{1,0:T(8,128)(2,1)S(1)} collective-permute-done((bf16[1024,128]{1,0:T(8,128)(2,1)S(1)}, bf16[1024,128]{1,0:T(8,128)(2,1)S(1)}, u32[]{:S(2)}, u32[]{:S(2)}) %collective-permute-start.5) | collective-permute-done | bytes 262176 | tf_op jit(solution)/shard_map/ppermute | solution.py:77
  35.5 0.6 collective-permute-start.8
  36.1 2.5 %broadcast_select_fusion.1 = (bf16[1024,1024]{1,0:T(8,128)(2,1)S(1)}, bf16[1024,1024]{1,0:T(8,128)(2,1)S(1)}) fusion(bf16[1024,1024]{1,0:T(8,128)(2,1)} %param.6, bf16[1024,1024]{1,0:T(8,128)(2,1)} %collective-permute-done, pred[]{:T(512)S(6)} %eq.8), kind=kLoop, calls=%fused_computation.8 | loop fusion | flops 2097152 | bytes 8388609 | tf_op jit(solution)/shard_map/jit(_where)/select_n | solution.py:111
  38.6 3.0 %collective-permute-done.4 = bf16[1024,128]{1,0:T(8,128)(2,1)S(1)} collective-permute-done((bf16[1024,128]{1,0:T(8,128)(2,1)S(1)}, bf16[1024,128]{1,0:T(8,128)(2,1)S(1)}, u32[]{:S(2)}, u32[]{:S(2)}) %collective-permute-start.4) | collective-permute-done | bytes 262176 | tf_op jit(solution)/shard_map/ppermute | solution.py:68
  41.6 1.6 %collective-permute-start.6 = (bf16[1024,128]{1,0:T(8,128)(2,1)S(1)}, bf16[1024,128]{1,0:T(8,128)(2,1)S(1)}, u32[]{:S(2)}, u32[]{:S(2)}) collective-permute-start(bf16[1024,128]{1,0:T(8,128)(2,1)S(1)} %broadcast_select_fusion.18), channel_id=1, source_target_pairs={{0,4},{1,5},{2,6},{3,7},{4,0},{5,1},{6,2},{7,3},{8,12},{9,13},{10,... | collective-permute-start | bytes 786440 | tf_op jit(solution)/shard_map/ppermute | solution.py:68
  43.2 0.1 pad_maximum_fusion.4
  43.3 0.6 collective-permute-start.10
  43.9 9.2 %collective-permute-done.6 = bf16[1024,128]{1,0:T(8,128)(2,1)S(1)} collective-permute-done((bf16[1024,128]{1,0:T(8,128)(2,1)S(1)}, bf16[1024,128]{1,0:T(8,128)(2,1)S(1)}, u32[]{:S(2)}, u32[]{:S(2)}) %collective-permute-start.6) | collective-permute-done | bytes 262176 | tf_op jit(solution)/shard_map/ppermute | solution.py:68
  53.1 0.7 fusion.51
  53.9 0.8 convolution_add_fusion.4
  54.6 0.2 maximum_select_fusion
  54.8 0.1 collective-permute-start.9
  54.9 0.2 copy-done
  55.2 0.8 collective-permute-start.12
  56.0 4.1 %collective-permute-start.11 = (bf16[1024,128]{1,0:T(8,128)(2,1)S(1)}, bf16[1024,128]{1,0:T(8,128)(2,1)S(1)}, u32[]{:S(2)}, u32[]{:S(2)}) collective-permute-start(bf16[1024,128]{1,0:T(8,128)(2,1)S(1)} %broadcast_select_fusion.14), channel_id=1, source_target_pairs={{0,8},{1,9},{2,10},{3,11},{4,12},{5,13},{6,14},{7,15},{8,0},{9,1},... | collective-permute-start | bytes 786440 | tf_op jit(solution)/shard_map/ppermute | solution.py:77
  60.1 12.7 %collective-permute-done.9 = bf16[1024,256]{1,0:T(8,128)(2,1)S(1)} collective-permute-done((bf16[1024,256]{1,0:T(8,128)(2,1)S(1)}, bf16[1024,256]{1,0:T(8,128)(2,1)S(1)}, u32[]{:S(2)}, u32[]{:S(2)}) %collective-permute-start.9) | collective-permute-done | bytes 524320 | tf_op jit(solution)/shard_map/ppermute | solution.py:68
  72.8 0.7 fusion.52
  73.5 0.7 convolution_add_fusion.2
  74.3 4.4 %collective-permute-start.16 = (bf16[1024,128]{1,0:T(8,128)(2,1)S(1)}, bf16[1024,128]{1,0:T(8,128)(2,1)S(1)}, u32[]{:S(2)}, u32[]{:S(2)}) collective-permute-start(bf16[1024,128]{1,0:T(8,128)(2,1)S(1)} %get-tuple-element.84), channel_id=1, source_target_pairs={{0,8},{1,9},{4,12},{5,13},{10,2},{11,3},{14,6},{15,7},{16,24},{17,... | collective-permute-start | bytes 786440 | tf_op jit(solution)/shard_map/ppermute | solution.py:74
  78.7 0.1 constant_dynamic-update-slice_fusion.4
  78.8 0.1 constant_dynamic-update-slice_fusion.3
  79.0 0.1 pad_maximum_fusion.2
  79.1 0.1 collective-permute-start.19
  79.2 0.1 constant_dynamic-update-slice_fusion.2
  79.3 0.2 maximum_select_fusion.1
  79.5 2.5 %collective-permute-start.13 = (bf16[1024,256]{1,0:T(8,128)(2,1)S(1)}, bf16[1024,256]{1,0:T(8,128)(2,1)S(1)}, u32[]{:S(2)}, u32[]{:S(2)}) collective-permute-start(bf16[1024,256]{1,0:T(8,128)(2,1)S(1)} %maximum_select_fusion.1), channel_id=1, source_target_pairs={{0,4},{1,5},{2,6},{3,7},{4,0},{5,1},{6,2},{7,3},{8,12},{9,13},{10,... | collective-permute-start | bytes 1572872 | tf_op jit(solution)/shard_map/ppermute | solution.py:68
  82.0 0.1 constant_dynamic-update-slice_fusion.1
  82.1 0.3 collective-permute-start.21
  82.6 12.3 %collective-permute-done.13 = bf16[1024,256]{1,0:T(8,128)(2,1)S(1)} collective-permute-done((bf16[1024,256]{1,0:T(8,128)(2,1)S(1)}, bf16[1024,256]{1,0:T(8,128)(2,1)S(1)}, u32[]{:S(2)}, u32[]{:S(2)}) %collective-permute-start.13) | collective-permute-done | bytes 524320 | tf_op jit(solution)/shard_map/ppermute | solution.py:68
  94.9 0.8 fusion.40
  95.6 0.8 convolution_add_fusion.3
  96.4 0.2 collective-permute-done.14
  96.6 1.5 %collective-permute-start.15 = (f32[1024,128]{1,0:T(8,128)S(1)}, f32[1024,128]{1,0:T(8,128)S(1)}, u32[]{:S(2)}, u32[]{:S(2)}) collective-permute-start(f32[1024,128]{1,0:T(8,128)S(1)} %get-tuple-element.80), channel_id=1, source_target_pairs={{0,2},{1,3},{2,0},{3,1},{4,6},{5,7},{6,4},{7,5},{8,10},{9,11},{10,... | collective-permute-start | bytes 1572872 | tf_op jit(solution)/shard_map/ppermute | solution.py:65
  98.1 1.0 collective-permute-start.22
  99.1 6.0 %collective-permute-start.17 = (bf16[1024,128]{1,0:T(8,128)(2,1)S(1)}, bf16[1024,128]{1,0:T(8,128)(2,1)S(1)}, u32[]{:S(2)}, u32[]{:S(2)}) collective-permute-start(bf16[1024,128]{1,0:T(8,128)(2,1)S(1)} %get-tuple-element.98), channel_id=1, source_target_pairs={{0,8},{1,9},{4,12},{5,13},{10,2},{11,3},{14,6},{15,7},{16,24},{17,... | collective-permute-start | bytes 786440 | tf_op jit(solution)/shard_map/ppermute | solution.py:74
  105.2 5.0 %collective-permute-done.15 = f32[1024,128]{1,0:T(8,128)S(1)} collective-permute-done((f32[1024,128]{1,0:T(8,128)S(1)}, f32[1024,128]{1,0:T(8,128)S(1)}, u32[]{:S(2)}, u32[]{:S(2)}) %collective-permute-start.15) | collective-permute-done | bytes 524320 | tf_op jit(solution)/shard_map/ppermute | solution.py:65
  110.3 0.5 broadcast_select_fusion.3
  110.9 0.1 constant_dynamic-update-slice_fusion
  111.0 0.2 broadcast_select_fusion.5
  111.3 0.6 collective-permute-start.20
  111.8 0.7 fusion.32
  112.6 0.8 convolution_add_fusion.1
  113.3 0.9 collective-permute-done.20
  114.3 1.3 fusion.8
  115.6 2.4 %fusion.5 = f32[1024,1024]{1,0:T(8,128)S(1)} fusion(f32[1024,1024]{1,0:T(8,128)S(1)} %fusion.8, bf16[1024,1024]{1,0:T(8,128)(2,1)S(1)} %constant_dynamic-update-slice_fusion, bf16[1024,512]{1,0:T(8,128)(2,1)S(1)} %collective-permute-done.18, bf16[1024,512]{1,0:T(8,128)(2,1)S(1)} %get-tuple-element.110), kind=kOutput, calls=%fused_computation.9 | convolution fusion | flops 2152726528 | bytes 12582912 | tf_op jit(solution)/shard_map/dot_general | solution.py:38
  118.0 1.8 %collective-permute-start.23 = (bf16[1024,128]{1,0:T(8,128)(2,1)S(1)}, bf16[1024,128]{1,0:T(8,128)(2,1)S(1)}, u32[]{:S(2)}, u32[]{:S(2)}) collective-permute-start(bf16[1024,128]{1,0:T(8,128)(2,1)S(1)} %broadcast_select_fusion.10), channel_id=1, source_target_pairs={{0,4},{1,5},{2,6},{3,7},{4,0},{5,1},{6,2},{7,3},{8,12},{9,13},{10,... | collective-permute-start | bytes 786440 | tf_op jit(solution)/shard_map/ppermute | solution.py:68
  120.6 0.3 collective-permute-start.24
  120.9 5.5 %collective-permute-done.23 = bf16[1024,128]{1,0:T(8,128)(2,1)S(1)} collective-permute-done((bf16[1024,128]{1,0:T(8,128)(2,1)S(1)}, bf16[1024,128]{1,0:T(8,128)(2,1)S(1)}, u32[]{:S(2)}, u32[]{:S(2)}) %collective-permute-start.23) | collective-permute-done | bytes 262176 | tf_op jit(solution)/shard_map/ppermute | solution.py:68
  126.5 0.7 fusion.28
  127.3 0.8 convolution_add_fusion
  128.1 3.3 %add_multiply_fusion = f32[1024,1024]{1,0:T(8,128)} fusion(f32[1024,1024]{1,0:T(8,128)S(1)} %fusion.5, f32[]{:T(128)} %bitcast, bf16[1024,128]{1,0:T(8,128)(2,1)S(1)} %collective-permute-done.26, bf16[1024,128]{1,0:T(8,128)(2,1)S(1)} %collective-permute-done.25, bf16[1024,128]{1,0:T(8,128)(2,1)S(1)} %get-tuple-element.132, ...), kind=kOutput, calls=%fused_computation | convolution fusion | flops 1082130432 | bytes 10485764 | tf_op jit(solution)/shard_map/dot_general | solution.py:38
  131.4 3.5 %collective-permute-done.24 = f32[1024,128]{1,0:T(8,128)S(1)} collective-permute-done((f32[1024,128]{1,0:T(8,128)S(1)}, f32[1024,128]{1,0:T(8,128)S(1)}, u32[]{:S(2)}, u32[]{:S(2)}) %collective-permute-start.24) | collective-permute-done | bytes 524320 | tf_op jit(solution)/shard_map/ppermute | solution.py:65
  134.9 1.6 %fusion.4 = f32[1024,512]{1,0:T(8,128)} fusion(f32[1024,256]{1,0:T(8,128)S(1)} %convolution_add_fusion, f32[1024,256]{1,0:T(8,128)S(1)} %convolution_add_fusion.1, f32[1024,128]{1,0:T(8,128)S(1)} %collective-permute-done.24, f32[1024,128]{1,0:T(8,128)S(1)} %collective-permute-done.15, f32[1024,128]{1,0:T(8,128)S(1)} %collective-permute-done.14, ...), kind=kLoop, calls=%fused_computation.6 | loop fusion | flops 3145728 | bytes 6291460 | tf_op jit(solution)/shard_map/mul | solution.py:182
  (41 shorter events, 1.1 us)
Async XLA Ops:
  0.6 35.5 %collective-permute-start = (bf16[1024,1024]{1,0:T(8,128)(2,1)}, bf16[1024,1024]{1,0:T(8,128)(2,1)}, u32[]{:S(2)}, u32[]{:S(2)}) collective-permute-start(bf16[1024,1024]{1,0:T(8,128)(2,1)} %param.6), channel_id=1, source_target_pairs={{0,1},{1,0},{2,3},{3,2},{4,5},{5,4},{6,7},{7,6},{8,9},{9,8},{10,11... | collective-permute-start | bytes 6291464 | tf_op jit(solution)/shard_map/ppermute | solution.py:71
  1.1 19.3 %copy-start.1 = (bf16[1024,512]{1,0:T(8,128)(2,1)S(1)}, bf16[1024,512]{1,0:T(8,128)(2,1)}, u32[]{:S(2)}) copy-start(bf16[1024,512]{1,0:T(8,128)(2,1)} %param.4) | copy-start | bytes 3145732
  2.9 17.6 %collective-permute-start.1 = (bf16[1024,256]{1,0:T(8,128)(2,1)S(1)}, bf16[1024,256]{1,0:T(8,128)(2,1)S(1)}, u32[]{:S(2)}, u32[]{:S(2)}) collective-permute-start(bf16[1024,256]{1,0:T(8,128)(2,1)S(1)} %pad_maximum_fusion.3), channel_id=1, source_target_pairs={{0,2},{1,3},{2,0},{3,1},{4,6},{5,7},{6,4},{7,5},{8,10},{9,11},{10,... | collective-permute-start | bytes 1572872 | tf_op jit(solution)/shard_map/ppermute | solution.py:65
  5.5 14.9 %collective-permute-start.2 = (bf16[1024,128]{1,0:T(8,128)(2,1)S(1)}, bf16[1024,128]{1,0:T(8,128)(2,1)S(1)}, u32[]{:S(2)}, u32[]{:S(2)}) collective-permute-start(bf16[1024,128]{1,0:T(8,128)(2,1)S(1)} %get-tuple-element.54), channel_id=1, source_target_pairs={{0,8},{1,9},{2,10},{3,11},{4,12},{5,13},{6,14},{7,15},{8,0},{9,1},... | collective-permute-start | bytes 786440 | tf_op jit(solution)/shard_map/ppermute | solution.py:77
  20.6 7.6 %collective-permute-start.3 = (bf16[1024,128]{1,0:T(8,128)(2,1)S(1)}, bf16[1024,128]{1,0:T(8,128)(2,1)S(1)}, u32[]{:S(2)}, u32[]{:S(2)}) collective-permute-start(bf16[1024,128]{1,0:T(8,128)(2,1)S(1)} %broadcast_select_fusion.21), channel_id=1, source_target_pairs={{0,2},{1,3},{2,0},{3,1},{4,6},{5,7},{6,4},{7,5},{8,10},{9,11},{10,... | collective-permute-start | bytes 786440 | tf_op jit(solution)/shard_map/ppermute | solution.py:65
  21.2 14.3 %collective-permute-start.5 = (bf16[1024,128]{1,0:T(8,128)(2,1)S(1)}, bf16[1024,128]{1,0:T(8,128)(2,1)S(1)}, u32[]{:S(2)}, u32[]{:S(2)}) collective-permute-start(bf16[1024,128]{1,0:T(8,128)(2,1)S(1)} %broadcast_select_fusion.19), channel_id=1, source_target_pairs={{0,8},{1,9},{2,10},{3,11},{4,12},{5,13},{6,14},{7,15},{8,0},{9,1},... | collective-permute-start | bytes 786440 | tf_op jit(solution)/shard_map/ppermute | solution.py:77
  28.3 7.2 %collective-permute-start.7 = (bf16[1024,128]{1,0:T(8,128)(2,1)S(1)}, bf16[1024,128]{1,0:T(8,128)(2,1)S(1)}, u32[]{:S(2)}, u32[]{:S(2)}) collective-permute-start(bf16[1024,128]{1,0:T(8,128)(2,1)S(1)} %broadcast_select_fusion.17), channel_id=1, source_target_pairs={{0,2},{1,3},{2,0},{3,1},{4,6},{5,7},{6,4},{7,5},{8,10},{9,11},{10,... | collective-permute-start | bytes 786440 | tf_op jit(solution)/shard_map/ppermute | solution.py:65
  29.2 12.5 %collective-permute-start.4 = (bf16[1024,128]{1,0:T(8,128)(2,1)S(1)}, bf16[1024,128]{1,0:T(8,128)(2,1)S(1)}, u32[]{:S(2)}, u32[]{:S(2)}) collective-permute-start(bf16[1024,128]{1,0:T(8,128)(2,1)S(1)} %get-tuple-element.81), channel_id=1, source_target_pairs={{0,4},{1,5},{2,6},{3,7},{4,0},{5,1},{6,2},{7,3},{8,12},{9,13},{10,... | collective-permute-start | bytes 786440 | tf_op jit(solution)/shard_map/ppermute | solution.py:68
  35.5 19.1 %collective-permute-start.8 = (bf16[1024,128]{1,0:T(8,128)(2,1)S(1)}, bf16[1024,128]{1,0:T(8,128)(2,1)S(1)}, u32[]{:S(2)}, u32[]{:S(2)}) collective-permute-start(bf16[1024,128]{1,0:T(8,128)(2,1)S(1)} %broadcast_select_fusion.16), channel_id=1, source_target_pairs={{0,8},{1,9},{2,10},{3,11},{4,12},{5,13},{6,14},{7,15},{8,0},{9,1},... | collective-permute-start | bytes 786440 | tf_op jit(solution)/shard_map/ppermute | solution.py:77
  41.6 11.5 %collective-permute-start.6 = (bf16[1024,128]{1,0:T(8,128)(2,1)S(1)}, bf16[1024,128]{1,0:T(8,128)(2,1)S(1)}, u32[]{:S(2)}, u32[]{:S(2)}) collective-permute-start(bf16[1024,128]{1,0:T(8,128)(2,1)S(1)} %broadcast_select_fusion.18), channel_id=1, source_target_pairs={{0,4},{1,5},{2,6},{3,7},{4,0},{5,1},{6,2},{7,3},{8,12},{9,13},{10,... | collective-permute-start | bytes 786440 | tf_op jit(solution)/shard_map/ppermute | solution.py:68
  43.3 11.8 %collective-permute-start.10 = (bf16[1024,256]{1,0:T(8,128)(2,1)S(1)}, bf16[1024,256]{1,0:T(8,128)(2,1)S(1)}, u32[]{:S(2)}, u32[]{:S(2)}) collective-permute-start(bf16[1024,256]{1,0:T(8,128)(2,1)S(1)} %pad_maximum_fusion.4), channel_id=1, source_target_pairs={{0,2},{1,3},{2,0},{3,1},{4,6},{5,7},{6,4},{7,5},{8,10},{9,11},{10,... | collective-permute-start | bytes 1572872 | tf_op jit(solution)/shard_map/ppermute | solution.py:65
  53.8 1.2 copy-start
  54.8 18.0 %collective-permute-start.9 = (bf16[1024,256]{1,0:T(8,128)(2,1)S(1)}, bf16[1024,256]{1,0:T(8,128)(2,1)S(1)}, u32[]{:S(2)}, u32[]{:S(2)}) collective-permute-start(bf16[1024,256]{1,0:T(8,128)(2,1)S(1)} %maximum_select_fusion), channel_id=1, source_target_pairs={{0,4},{1,5},{2,6},{3,7},{4,0},{5,1},{6,2},{7,3},{8,12},{9,13},{10,... | collective-permute-start | bytes 1572872 | tf_op jit(solution)/shard_map/ppermute | solution.py:68
  55.2 24.1 %collective-permute-start.12 = (f32[1024,128]{1,0:T(8,128)S(1)}, f32[1024,128]{1,0:T(8,128)S(1)}, u32[]{:S(2)}, u32[]{:S(2)}) collective-permute-start(f32[1024,128]{1,0:T(8,128)S(1)} %convolution_add_fusion.4), channel_id=1, source_target_pairs={{0,2},{1,3},{2,0},{3,1},{4,6},{5,7},{6,4},{7,5},{8,10},{9,11},{10,... | collective-permute-start | bytes 1572872 | tf_op jit(solution)/shard_map/ppermute | solution.py:65
  56.0 18.3 %collective-permute-start.11 = (bf16[1024,128]{1,0:T(8,128)(2,1)S(1)}, bf16[1024,128]{1,0:T(8,128)(2,1)S(1)}, u32[]{:S(2)}, u32[]{:S(2)}) collective-permute-start(bf16[1024,128]{1,0:T(8,128)(2,1)S(1)} %broadcast_select_fusion.14), channel_id=1, source_target_pairs={{0,8},{1,9},{2,10},{3,11},{4,12},{5,13},{6,14},{7,15},{8,0},{9,1},... | collective-permute-start | bytes 786440 | tf_op jit(solution)/shard_map/ppermute | solution.py:77
  74.3 22.1 %collective-permute-start.16 = (bf16[1024,128]{1,0:T(8,128)(2,1)S(1)}, bf16[1024,128]{1,0:T(8,128)(2,1)S(1)}, u32[]{:S(2)}, u32[]{:S(2)}) collective-permute-start(bf16[1024,128]{1,0:T(8,128)(2,1)S(1)} %get-tuple-element.84), channel_id=1, source_target_pairs={{0,8},{1,9},{4,12},{5,13},{10,2},{11,3},{14,6},{15,7},{16,24},{17,... | collective-permute-start | bytes 786440 | tf_op jit(solution)/shard_map/ppermute | solution.py:74
  79.1 31.8 %collective-permute-start.19 = (bf16[1024,512]{1,0:T(8,128)(2,1)S(1)}, bf16[1024,512]{1,0:T(8,128)(2,1)S(1)}, u32[]{:S(2)}, u32[]{:S(2)}) collective-permute-start(bf16[1024,512]{1,0:T(8,128)(2,1)S(1)} %pad_maximum_fusion.2), channel_id=1, source_target_pairs={{0,1},{1,0},{2,3},{3,2},{4,5},{5,4},{6,7},{7,6},{8,9},{9,8},{10,11... | collective-permute-start | bytes 3145736 | tf_op jit(solution)/shard_map/ppermute | solution.py:71
  79.5 15.4 %collective-permute-start.13 = (bf16[1024,256]{1,0:T(8,128)(2,1)S(1)}, bf16[1024,256]{1,0:T(8,128)(2,1)S(1)}, u32[]{:S(2)}, u32[]{:S(2)}) collective-permute-start(bf16[1024,256]{1,0:T(8,128)(2,1)S(1)} %maximum_select_fusion.1), channel_id=1, source_target_pairs={{0,4},{1,5},{2,6},{3,7},{4,0},{5,1},{6,2},{7,3},{8,12},{9,13},{10,... | collective-permute-start | bytes 1572872 | tf_op jit(solution)/shard_map/ppermute | solution.py:68
  82.1 23.1 %collective-permute-start.21 = (bf16[1024,512]{1,0:T(8,128)(2,1)S(1)}, bf16[1024,512]{1,0:T(8,128)(2,1)S(1)}, u32[]{:S(2)}, u32[]{:S(2)}) collective-permute-start(bf16[1024,512]{1,0:T(8,128)(2,1)S(1)} %copy-done), channel_id=1, source_target_pairs={{0,1},{1,0},{2,3},{3,2},{4,5},{5,4},{6,7},{7,6},{8,9},{9,8},{10,11... | collective-permute-start | bytes 3145736 | tf_op jit(solution)/shard_map/ppermute | solution.py:71
  82.4 14.2 %collective-permute-start.14 = (f32[1024,128]{1,0:T(8,128)S(1)}, f32[1024,128]{1,0:T(8,128)S(1)}, u32[]{:S(2)}, u32[]{:S(2)}) collective-permute-start(f32[1024,128]{1,0:T(8,128)S(1)} %get-tuple-element.79), channel_id=1, source_target_pairs={{0,2},{1,3},{2,0},{3,1},{4,6},{5,7},{6,4},{7,5},{8,10},{9,11},{10,... | collective-permute-start | bytes 1572872 | tf_op jit(solution)/shard_map/ppermute | solution.py:65
  96.6 13.6 %collective-permute-start.15 = (f32[1024,128]{1,0:T(8,128)S(1)}, f32[1024,128]{1,0:T(8,128)S(1)}, u32[]{:S(2)}, u32[]{:S(2)}) collective-permute-start(f32[1024,128]{1,0:T(8,128)S(1)} %get-tuple-element.80), channel_id=1, source_target_pairs={{0,2},{1,3},{2,0},{3,1},{4,6},{5,7},{6,4},{7,5},{8,10},{9,11},{10,... | collective-permute-start | bytes 1572872 | tf_op jit(solution)/shard_map/ppermute | solution.py:65
  98.1 19.8 %collective-permute-start.22 = (bf16[1024,128]{1,0:T(8,128)(2,1)S(1)}, bf16[1024,128]{1,0:T(8,128)(2,1)S(1)}, u32[]{:S(2)}, u32[]{:S(2)}) collective-permute-start(bf16[1024,128]{1,0:T(8,128)(2,1)S(1)} %broadcast_select_fusion.13), channel_id=1, source_target_pairs={{0,4},{1,5},{2,6},{3,7},{4,0},{5,1},{6,2},{7,3},{8,12},{9,13},{10,... | collective-permute-start | bytes 786440 | tf_op jit(solution)/shard_map/ppermute | solution.py:68
  99.1 18.8 %collective-permute-start.17 = (bf16[1024,128]{1,0:T(8,128)(2,1)S(1)}, bf16[1024,128]{1,0:T(8,128)(2,1)S(1)}, u32[]{:S(2)}, u32[]{:S(2)}) collective-permute-start(bf16[1024,128]{1,0:T(8,128)(2,1)S(1)} %get-tuple-element.98), channel_id=1, source_target_pairs={{0,8},{1,9},{4,12},{5,13},{10,2},{11,3},{14,6},{15,7},{16,24},{17,... | collective-permute-start | bytes 786440 | tf_op jit(solution)/shard_map/ppermute | solution.py:74
  110.8 4.8 %collective-permute-start.18 = (bf16[1024,512]{1,0:T(8,128)(2,1)S(1)}, bf16[1024,512]{1,0:T(8,128)(2,1)S(1)}, u32[]{:S(2)}, u32[]{:S(2)}) collective-permute-start(bf16[1024,512]{1,0:T(8,128)(2,1)S(1)} %get-tuple-element.111), channel_id=1, source_target_pairs={{0,1},{1,0},{2,3},{3,2},{4,5},{5,4},{6,7},{7,6},{8,9},{9,8},{10,11... | collective-permute-start | bytes 3145736 | tf_op jit(solution)/shard_map/ppermute | solution.py:71
  111.3 3.0 %collective-permute-start.20 = (bf16[1024,256]{1,0:T(8,128)(2,1)S(1)}, bf16[1024,256]{1,0:T(8,128)(2,1)S(1)}, u32[]{:S(2)}, u32[]{:S(2)}) collective-permute-start(bf16[1024,256]{1,0:T(8,128)(2,1)S(1)} %get-tuple-element.117), channel_id=1, source_target_pairs={{0,1},{1,0},{2,3},{3,2},{4,5},{5,4},{6,7},{7,6},{8,9},{9,8},{10,11... | collective-permute-start | bytes 1572872 | tf_op jit(solution)/shard_map/ppermute | solution.py:71
  118.0 8.4 %collective-permute-start.23 = (bf16[1024,128]{1,0:T(8,128)(2,1)S(1)}, bf16[1024,128]{1,0:T(8,128)(2,1)S(1)}, u32[]{:S(2)}, u32[]{:S(2)}) collective-permute-start(bf16[1024,128]{1,0:T(8,128)(2,1)S(1)} %broadcast_select_fusion.10), channel_id=1, source_target_pairs={{0,4},{1,5},{2,6},{3,7},{4,0},{5,1},{6,2},{7,3},{8,12},{9,13},{10,... | collective-permute-start | bytes 786440 | tf_op jit(solution)/shard_map/ppermute | solution.py:68
  120.5 7.5 %collective-permute-start.25 = (bf16[1024,128]{1,0:T(8,128)(2,1)S(1)}, bf16[1024,128]{1,0:T(8,128)(2,1)S(1)}, u32[]{:S(2)}, u32[]{:S(2)}) collective-permute-start(bf16[1024,128]{1,0:T(8,128)(2,1)S(1)} %get-tuple-element.131), channel_id=1, source_target_pairs={{0,1},{1,0},{2,3},{3,2},{4,5},{5,4},{6,7},{7,6},{8,9},{9,8},{10,11... | collective-permute-start | bytes 786440 | tf_op jit(solution)/shard_map/ppermute | solution.py:71
  120.6 14.3 %collective-permute-start.24 = (f32[1024,128]{1,0:T(8,128)S(1)}, f32[1024,128]{1,0:T(8,128)S(1)}, u32[]{:S(2)}, u32[]{:S(2)}) collective-permute-start(f32[1024,128]{1,0:T(8,128)S(1)} %convolution_add_fusion.3), channel_id=1, source_target_pairs={{0,2},{1,3},{2,0},{3,1},{4,6},{5,7},{6,4},{7,5},{8,10},{9,11},{10,... | collective-permute-start | bytes 1572872 | tf_op jit(solution)/shard_map/ppermute | solution.py:65
  126.4 1.6 %collective-permute-start.26 = (bf16[1024,128]{1,0:T(8,128)(2,1)S(1)}, bf16[1024,128]{1,0:T(8,128)(2,1)S(1)}, u32[]{:S(2)}, u32[]{:S(2)}) collective-permute-start(bf16[1024,128]{1,0:T(8,128)(2,1)S(1)} %get-tuple-element.133), channel_id=1, source_target_pairs={{0,1},{1,0},{2,3},{3,2},{4,5},{5,4},{6,7},{7,6},{8,9},{9,8},{10,11... | collective-permute-start | bytes 786440 | tf_op jit(solution)/shard_map/ppermute | solution.py:71

commit v8 on v7

--- a/solution.py
+++ b/solution.py
@@ -92,68 +92,72 @@
 
         e = [columns(expected_cot, i, i + 1) for i in range(4)]
         v = [columns(value_next, i, i + 1) for i in range(4)]
-        first_cross, first_jump, e3 = together(
-            (jnp.concatenate([jnp.where(home, v[0], e[0]), v[2]], 1), jnp.where(home, e[0], e[2]), e[3])
-        )
-        x1 = cross(first_cross)
-        x1, v_across2 = columns(x1, 0, 1), columns(x1, 1, 2)
-        j1 = jump(first_jump)
-        v1, e1 = together((v[1], e[1]), x1, j1)
-        x2 = cross(jnp.where(home, v1, e1))
-        near, far = together((x1, e3), j1)
-        j2 = jump(jnp.where(home, near, far))
-        a0 = jnp.where(home, e[0], j1)
-        a0_next = step(a0)
+        x1 = cross(jnp.where(home, v[0], e[0]))
         t_other = swap(transition)
-        near, far = together((j1, v[0]), x2)
-        x3 = cross(jnp.where(home, near, far))
+        e2 = after(e[2], x1)
+        j1 = jump(jnp.where(home, x1, e2))
+        v1, e1 = together((v[1], e[1]), x1)
+        x2 = cross(jnp.concatenate([jnp.where(home, v1, e1), v[2]], 1))
+        x2, v_across2 = columns(x2, 0, 1), columns(x2, 1, 2)
         t, t_o = together((transition, t_other), x2)
         t_near, t_next = jnp.where(mine, t, t_o), jnp.where(mine, t_o, t)
 
         def adjoint_of(near, far):
             return tdot(t_near, near) + tdot(t_next, far)
 
-        near, far = together((x2, x3), j2)
-        j3 = jump(jnp.where(home, near, far))
-        near, far = together((x1, j2), t_near, a0_next)
+        near, far = together((x1, j1), x2)
         b0 = jnp.where(home, near, far)
         b0_next = step(b0)
-        near, far = together((j2, v[1]), x3, b0)
-        x4 = cross(jnp.concatenate([jnp.where(home, near, far), v[3]], 1))
-        x4, v_across3 = columns(x4, 0, 1), columns(x4, 1, 2)
-        near, far = together((e[1], x4), j3)
+        near, far = together((x2, e[3]), j1, b0)
+        j2 = jump(jnp.where(home, near, far))
+        near, far = together((j1, v[0]), x2)
+        x3 = cross(jnp.concatenate([jnp.where(home, near, far), v[3]], 1))
+        x3, v_across3 = columns(x3, 0, 1), columns(x3, 1, 2)
+        sum0 = adjoint_of(b0, b0_next)
+        part0 = cross(after(sum0, x3))
+        near, far = together((e[0], x3), j2, b0_next)
+        j3 = jump(jnp.where(home, near, far))
+        near, far = together((x2, j2), sum0)
+        b1 = jnp.where(home, near, far)
+        b1_next = step(b1)
+        near, far = together((j2, v[1]), x3, sum0)
+        x4 = cross(jnp.where(home, near, far))
+        near, far = together((e[1], x4), j3, part0)
         j4 = jump(jnp.where(home, near, far))
-        sum0 = adjoint_of(b0, b0_next)
-        part0 = cross(after(sum0, x4))
-        near, both, far = together((x2, j3, x3), sum0)
-        b12 = jnp.where(home, jnp.concatenate([near, both], 1), jnp.concatenate([both, far], 1))
-        b12_next = step(b12)
-        sum12 = adjoint_of(b12, b12_next)
-        sum1, sum2 = columns(sum12, 0, 1), columns(sum12, 1, 2)
-        part1 = cross(after(sum1, part0))
+        sum1 = adjoint_of(b1, b1_next)
+        part1 = cross(after(sum1, part0, x4))
+        near, both, far = together((e[0], j3, x3), sum1)
+        a0b2 = jnp.where(home, jnp.concatenate([near, both], 1), jnp.concatenate([both, far], 1))
+        a0b2_next = step(a0b2)
+        sum2 = adjoint_of(columns(a0b2, 1, 2), columns(a0b2_next, 1, 2))
         part2 = cross(after(sum2, part1))
-        j5 = home_jump(after(e[2], j4))
-        near, both, far = together((e[1], j4, x4), sum12, part0)
+        j5 = home_jump(after(columns(expected_cot, 2, 4), j4))
+        near, both, far = together((e[1], j4, x4), sum2, part0)
         a1b3 = jnp.where(home, jnp.concatenate([near, both], 1), jnp.concatenate([both, far], 1))
         a1b3_next = step(a1b3)
-        j6 = home_jump(after(e[3], j5, part1))
-        v_other = swap(after(value_next, sum12))
+        v_other = swap(after(value_next, sum1))
         sum3 = adjoint_of(columns(a1b3, 1, 2), columns(a1b3_next, 1, 2))
         part3 = cross(after(sum3, part2))
 
         def own_and_swapped(near, far):
             return jnp.where(mine, near, far), swap(jnp.where(mine, far, near))
 
-        parts = together((x1, x2, x3, x4, v_across2, v_across3), sum12)
+        parts = together((x1, x2, x3, x4, v_across2, v_across3), sum1)
         v_across = jnp.concatenate(
             [jnp.where(home, parts[2], parts[0]), jnp.where(home, parts[3], parts[1]), parts[4], parts[5]], 1
         )
         v_across_other = swap(v_across)
-        a0, a0_next, b0, b0_next, b12, b12_next = together((a0, a0_next, b0, b0_next, b12, b12_next), a1b3_next, sum3, part2)
+        near, far = together((columns(expected_cot, 2, 4), j5), a1b3_next, part2)
+        a23 = jnp.where(home, near, far)
+        a23_next = step(a23)
+        b0, b0_next, b1, b1_next, a0b2, a0b2_next = together(
+            (b0, b0_next, b1, b1_next, a0b2, a0b2_next), a1b3_next, sum3, part2
+        )
+        a0, a0_next = columns(a0b2, 0, 1), columns(a0b2_next, 0, 1)
         a1, a1_next = columns(a1b3, 0, 1), columns(a1b3_next, 0, 1)
         b_own, b_swapped = own_and_swapped(
-            jnp.concatenate([b0, b12, columns(a1b3, 1, 2)], 1),
-            jnp.concatenate([b0_next, b12_next, columns(a1b3_next, 1, 2)], 1),
+            jnp.concatenate([b0, b1, columns(a0b2, 1, 2), columns(a1b3, 1, 2)], 1),
+            jnp.concatenate([b0_next, b1_next, columns(a0b2_next, 1, 2), columns(a1b3_next, 1, 2)], 1),
         )
         a01_own, a01_swapped = own_and_swapped(
             jnp.concatenate([a0, a1], 1), jnp.concatenate([a0_next, a1_next], 1)
@@ -164,20 +168,14 @@
             jnp.concatenate([a01_own, a01_swapped], 1),
             jnp.concatenate([columns(value_next, 0, 2), columns(v_other, 0, 2)], 1),
         )
-        near, far = together((e[2], j5), a1b3_next, sum3, part1)
-        a2 = jnp.where(home, near, far)
-        a2_next = step(a2)
         own01 = adjoint_of(jnp.concatenate([a0, a1], 1), jnp.concatenate([a0_next, a1_next], 1))
-        near, far = together((e[3], j6), grad, own01, a2_next, part2)
-        a3 = jnp.where(home, near, far)
-        a3_next = step(a3)
-        a2_own, a2_swapped = own_and_swapped(a2, a2_next)
-        a3_own, a3_swapped = own_and_swapped(a3, a3_next)
+        near, far = together((a23, a23_next), grad, own01)
+        a23_own, a23_swapped = own_and_swapped(near, far)
         grad = df * (grad + dott(
-            jnp.concatenate([a2_own, a3_own, a2_swapped, a3_swapped], 1),
+            jnp.concatenate([a23_own, a23_swapped], 1),
             jnp.concatenate([columns(value_next, 2, 4), columns(v_other, 2, 4)], 1),
         ))
-        own23 = adjoint_of(jnp.concatenate([a2, a3], 1), jnp.concatenate([a2_next, a3_next], 1))
+        own23 = adjoint_of(near, far)
         own23, part3, grad = together((own23, part3, grad))
         adjoint = df * (
             jnp.concatenate([own01, own23], 1) + jnp.concatenate([part0, part1, part2, part3], 1)

time: 137 us -> 137 us (level); the launches traced: 137 us -> 134 us
  waiting for transfers between devices: 75.6 us -> 68.8 us
  starting transfers between devices: 36 us -> 30.6 us
  local copies, waits for them, and re-layouts: 0.87 us -> 4.61 us
  other arithmetic: 7.82 us -> 11.5 us
  matrix products: 14.5 us -> 16.9 us
    ppermute x6 -> x5, waiting for transfers between devices: 42.7 us -> 19.9 us  [step(): return lax.ppermute(a, AXES, step_pairs)]
    ppermute x8, waiting for transfers between devices: 14.4 us -> 29.2 us  [cross(): return lax.ppermute(a, AXES, cross_pairs)]
    ppermute x2 -> x1, starting transfers between devices: 10.4 us -> 3.96 us  [home_jump(): return lax.ppermute(a, AXES, home_jump_pairs)]
    slice x7 -> x8, local copies, waits for them, and re-layouts: 0.35 us -> 4.01 us  [columns(): return array[:, start * quarter:stop * quarter]]
    ppermute x6 -> x5, starting transfers between devices: 8.01 us -> 4.81 us  [step(): return lax.ppermute(a, AXES, step_pairs)]
    ppermute x8, starting transfers between devices: 7.25 us -> 10.2 us  [cross(): return lax.ppermute(a, AXES, cross_pairs)]
    ppermute x2 -> x1, waiting for transfers between devices: 0.01 us -> 2.73 us  [home_jump(): return lax.ppermute(a, AXES, home_jump_pairs)]
    dot_general x10 -> x12, matrix products: 7.48 us -> 9.98 us  [tdot(): lax.dot_general(a, b, (((0,), (0,)), ((), ())), preferred_element_type=jn...]
  transfers between devices with their start and end apart: 27 -> 24, of which waited for: 12 -> 15; matrix products, arithmetic and copies ran while one was open for 16% -> 18% of each run, Pallas kernels for 0% -> 0%
where the time goes in v8:
time: 137 us; the launch traced here: 134 us
  waiting for transfers between devices  68.8 us (50%)
  starting transfers between devices  30.6 us (22%)
  matrix products  16.9 us (12%)
  other arithmetic  11.5 us (8%)
  local copies, waits for them, and re-layouts  4.61 us (3%)
  between operations  1.78 us (1%)
    ppermute x8, waiting for transfers between devices, cross(): return lax.ppermute(a, AXES, cross_pairs)  29.2 us
    ppermute x5, waiting for transfers between devices, step(): return lax.ppermute(a, AXES, step_pairs)  19.9 us
    ppermute x4, waiting for transfers between devices, jump(): return lax.ppermute(a, AXES, jump_pairs)  16.5 us
    ppermute x4, starting transfers between devices, jump(): return lax.ppermute(a, AXES, jump_pairs)  10.4 us
    ppermute x8, starting transfers between devices, cross(): return lax.ppermute(a, AXES, cross_pairs)  10.2 us
    dot_general x12, matrix products, tdot(): lax.dot_general(a, b, (((0,), (0,)), ((), ())), preferred_element_type=jn...  9.98 us
    dot_general x3, matrix products, dott(): lax.dot_general(a, b, (((1,), (1,)), ((), ())), preferred_element_type=jn...  6.97 us
    ppermute x5, starting transfers between devices, step(): return lax.ppermute(a, AXES, step_pairs)  4.81 us
  transfers between devices with their start and end apart: 24, of which 15 were waited for; matrix products, arithmetic and copies ran while one was open for 18% of the time, Pallas kernels for 0%

profile of v8, /device:TPU:0, one launch (start us, length us, event | category | flops | bytes accessed | tf_op | source)
XLA Modules:
  0.0 134.2 jit_solution(15493479371698859379)
XLA Ops:
  0.6 1.7 %fusion.35 = (bf16[1024,128]{1,0:T(8,128)(2,1)S(1)}, bf16[1024,128]{1,0:T(8,128)(2,1)S(1)}, bf16[1024,128]{1,0:T(8,128)(2,1)S(1)}, bf16[1024,128]{1,0:T(8,128)(2...) fusion(bf16[1024,512]{1,0:T(8,128)(2,1)} %param.4, ...), kind=kLoop, calls=%fused_computation.76 | loop fusion | flops 131072 | bytes 4456449 | tf_op jit(solution)/shard_map/slice | solution.py:88
  2.4 3.0 %collective-permute-start.1 = (bf16[1024,128]{1,0:T(8,128)(2,1)S(1)}, bf16[1024,128]{1,0:T(8,128)(2,1)S(1)}, u32[]{:S(2)}, u32[]{:S(2)}) collective-permute-start(bf16[1024,128]{1,0:T(8,128)(2,1)S(1)} %get-tuple-element.119), channel_id=1, source_target_pairs={{0,2},{1,3},{2,0},{3,1},{4,6},{5,7},{6,4},{7,5},{8,10},{9,11},{10,... | collective-permute-start | bytes 786440 | tf_op jit(solution)/shard_map/ppermute | solution.py:65
  5.4 6.3 %collective-permute-done.1 = bf16[1024,128]{1,0:T(8,128)(2,1)S(1)} collective-permute-done((bf16[1024,128]{1,0:T(8,128)(2,1)S(1)}, bf16[1024,128]{1,0:T(8,128)(2,1)S(1)}, u32[]{:S(2)}, u32[]{:S(2)}) %collective-permute-start.1) | collective-permute-done | bytes 262176 | tf_op jit(solution)/shard_map/ppermute | solution.py:65
  11.8 1.8 %collective-permute-start.2 = (bf16[1024,256]{1,0:T(8,128)(2,1)S(1)}, bf16[1024,256]{1,0:T(8,128)(2,1)S(1)}, u32[]{:S(2)}, u32[]{:S(2)}) collective-permute-start(bf16[1024,256]{1,0:T(8,128)(2,1)S(1)} %pad_maximum_fusion.3), channel_id=1, source_target_pairs={{0,2},{1,3},{2,0},{3,1},{4,6},{5,7},{6,4},{7,5},{8,10},{9,11},{10,... | collective-permute-start | bytes 1572872 | tf_op jit(solution)/shard_map/ppermute | solution.py:65
  13.7 2.7 %collective-permute-start.3 = (bf16[1024,128]{1,0:T(8,128)(2,1)S(1)}, bf16[1024,128]{1,0:T(8,128)(2,1)S(1)}, u32[]{:S(2)}, u32[]{:S(2)}) collective-permute-start(bf16[1024,128]{1,0:T(8,128)(2,1)S(1)} %broadcast_select_fusion.18), channel_id=1, source_target_pairs={{0,8},{1,9},{2,10},{3,11},{4,12},{5,13},{6,14},{7,15},{8,0},{9,1},... | collective-permute-start | bytes 786440 | tf_op jit(solution)/shard_map/ppermute | solution.py:77
  16.3 8.7 %collective-permute-done.2 = bf16[1024,256]{1,0:T(8,128)(2,1)S(1)} collective-permute-done((bf16[1024,256]{1,0:T(8,128)(2,1)S(1)}, bf16[1024,256]{1,0:T(8,128)(2,1)S(1)}, u32[]{:S(2)}, u32[]{:S(2)}) %collective-permute-start.2) | collective-permute-done | bytes 524320 | tf_op jit(solution)/shard_map/ppermute | solution.py:65
  25.0 0.7 fusion.41
  25.7 3.2 %collective-permute-done.3 = bf16[1024,128]{1,0:T(8,128)(2,1)S(1)} collective-permute-done((bf16[1024,128]{1,0:T(8,128)(2,1)S(1)}, bf16[1024,128]{1,0:T(8,128)(2,1)S(1)}, u32[]{:S(2)}, u32[]{:S(2)}) %collective-permute-start.3) | collective-permute-done | bytes 262176 | tf_op jit(solution)/shard_map/ppermute | solution.py:77
  29.0 0.9 pad_maximum_fusion.4
  29.8 0.5 collective-permute-start.7
  30.4 0.8 collective-permute-start.4
  31.2 0.7 broadcast_select_fusion.16
  31.9 3.4 %collective-permute-start.5 = (bf16[1024,128]{1,0:T(8,128)(2,1)}, bf16[1024,128]{1,0:T(8,128)(2,1)}, u32[]{:S(2)}, u32[]{:S(2)}) collective-permute-start(bf16[1024,128]{1,0:T(8,128)(2,1)} %broadcast_select_fusion.16), channel_id=1, source_target_pairs={{0,8},{1,9},{2,10},{3,11},{4,12},{5,13},{6,14},{7,15},{8,0},{9,1},... | collective-permute-start | bytes 786440 | tf_op jit(solution)/shard_map/ppermute | solution.py:77
  35.3 1.1 fusion.33
  36.3 0.8 slice.102
  37.9 5.9 %collective-permute-done.7 = bf16[1024,256]{1,0:T(8,128)(2,1)} collective-permute-done((bf16[1024,256]{1,0:T(8,128)(2,1)}, bf16[1024,256]{1,0:T(8,128)(2,1)}, u32[]{:S(2)}, u32[]{:S(2)}) %collective-permute-start.7) | collective-permute-done | bytes 524320 | tf_op jit(solution)/shard_map/ppermute | solution.py:65
  43.7 1.1 fusion.40
  44.8 2.4 %collective-permute-done.5 = bf16[1024,128]{1,0:T(8,128)(2,1)} collective-permute-done((bf16[1024,128]{1,0:T(8,128)(2,1)}, bf16[1024,128]{1,0:T(8,128)(2,1)}, u32[]{:S(2)}, u32[]{:S(2)}) %collective-permute-start.5) | collective-permute-done | bytes 262176 | tf_op jit(solution)/shard_map/ppermute | solution.py:77
  47.2 2.5 %broadcast_select_fusion.1 = (bf16[1024,1024]{1,0:T(8,128)(2,1)S(1)}, bf16[1024,1024]{1,0:T(8,128)(2,1)S(1)}) fusion(bf16[1024,1024]{1,0:T(8,128)(2,1)} %param.6, bf16[1024,1024]{1,0:T(8,128)(2,1)} %collective-permute-done, pred[]{:T(512)S(6)} %eq.8), kind=kLoop, calls=%fused_computation.8 | loop fusion | flops 2097152 | bytes 8388609 | tf_op jit(solution)/shard_map/jit(_where)/select_n | solution.py:103
  49.7 1.7 %fusion.42 = f32[1024,128]{1,0:T(8,128)S(1)} fusion(bf16[1024,1024]{1,0:T(8,128)(2,1)S(1)} %get-tuple-element.107, bf16[1024,128]{1,0:T(8,128)(2,1)} %collective-permute-done.4), kind=kOutput, calls=%fused_computation.83 | convolution fusion | flops 268435456 | bytes 2883584 | tf_op jit(solution)/shard_map/dot_general | solution.py:34
  51.4 0.8 convolution_add_fusion.5
  52.4 3.9 %collective-permute-start.8 = (bf16[1024,128]{1,0:T(8,128)(2,1)S(1)}, bf16[1024,128]{1,0:T(8,128)(2,1)S(1)}, u32[]{:S(2)}, u32[]{:S(2)}) collective-permute-start(bf16[1024,128]{1,0:T(8,128)(2,1)S(1)} %broadcast_select_fusion.13), channel_id=1, source_target_pairs={{0,8},{1,9},{2,10},{3,11},{4,12},{5,13},{6,14},{7,15},{8,0},{9,1},... | collective-permute-start | bytes 786440 | tf_op jit(solution)/shard_map/ppermute | solution.py:77
  56.3 0.5 collective-permute-start.11
  56.8 1.0 broadcast_select_fusion.12
  57.8 0.6 collective-permute-start.10
  58.4 6.4 %collective-permute-done.6 = bf16[1024,128]{1,0:T(8,128)(2,1)S(1)} collective-permute-done((bf16[1024,128]{1,0:T(8,128)(2,1)S(1)}, bf16[1024,128]{1,0:T(8,128)(2,1)S(1)}, u32[]{:S(2)}, u32[]{:S(2)}) %collective-permute-start.6) | collective-permute-done | bytes 262176 | tf_op jit(solution)/shard_map/ppermute | solution.py:68
  64.8 0.7 fusion.43
  65.5 0.8 convolution_add_fusion.4
  66.3 0.8 collective-permute-done.8
  67.1 0.2 maximum_select_fusion
  67.3 0.3 collective-permute-start.9
  67.6 6.6 %collective-permute-done.10 = bf16[1024,128]{1,0:T(8,128)(2,1)S(1)} collective-permute-done((bf16[1024,128]{1,0:T(8,128)(2,1)S(1)}, bf16[1024,128]{1,0:T(8,128)(2,1)S(1)}, u32[]{:S(2)}, u32[]{:S(2)}) %collective-permute-start.10) | collective-permute-done | bytes 262176 | tf_op jit(solution)/shard_map/ppermute | solution.py:65
  74.6 0.5 collective-permute-start.21
  75.2 0.4 collective-permute-start.12
  75.6 1.4 %collective-permute-start.14 = (f32[1024,128]{1,0:T(8,128)S(1)}, f32[1024,128]{1,0:T(8,128)S(1)}, u32[]{:S(2)}, u32[]{:S(2)}) collective-permute-start(f32[1024,128]{1,0:T(8,128)S(1)} %convolution_add_fusion.4), channel_id=1, source_target_pairs={{0,2},{1,3},{2,0},{3,1},{4,6},{5,7},{6,4},{7,5},{8,10},{9,11},{10,... | collective-permute-start | bytes 1572872 | tf_op jit(solution)/shard_map/ppermute | solution.py:65
  77.1 1.4 %collective-permute-done.9 = bf16[1024,256]{1,0:T(8,128)(2,1)S(1)} collective-permute-done((bf16[1024,256]{1,0:T(8,128)(2,1)S(1)}, bf16[1024,256]{1,0:T(8,128)(2,1)S(1)}, u32[]{:S(2)}, u32[]{:S(2)}) %collective-permute-start.9) | collective-permute-done | bytes 524320 | tf_op jit(solution)/shard_map/ppermute | solution.py:68
  78.5 0.8 fusion.21
  79.2 0.8 convolution_add_fusion.3
  80.0 10.0 %collective-permute-done.12 = bf16[1024,128]{1,0:T(8,128)(2,1)S(1)} collective-permute-done((bf16[1024,128]{1,0:T(8,128)(2,1)S(1)}, bf16[1024,128]{1,0:T(8,128)(2,1)S(1)}, u32[]{:S(2)}, u32[]{:S(2)}) %collective-permute-start.12) | collective-permute-done | bytes 262176 | tf_op jit(solution)/shard_map/ppermute | solution.py:77
  90.0 0.2 maximum_select_fusion.1
  90.3 4.0 %collective-permute-start.16 = (bf16[1024,256]{1,0:T(8,128)(2,1)S(1)}, bf16[1024,256]{1,0:T(8,128)(2,1)S(1)}, u32[]{:S(2)}, u32[]{:S(2)}) collective-permute-start(bf16[1024,256]{1,0:T(8,128)(2,1)S(1)} %copy-done.5), channel_id=1, source_target_pairs={{0,8},{1,9},{4,12},{5,13},{10,2},{11,3},{14,6},{15,7},{16,24},{17,... | collective-permute-start | bytes 1572872 | tf_op jit(solution)/shard_map/ppermute | solution.py:74
  94.5 9.2 %collective-permute-done.13 = bf16[1024,256]{1,0:T(8,128)(2,1)S(1)} collective-permute-done((bf16[1024,256]{1,0:T(8,128)(2,1)S(1)}, bf16[1024,256]{1,0:T(8,128)(2,1)S(1)}, u32[]{:S(2)}, u32[]{:S(2)}) %collective-permute-start.13) | collective-permute-done | bytes 524320 | tf_op jit(solution)/shard_map/ppermute | solution.py:68
  103.7 0.8 fusion.30
  104.5 0.1 constant_dynamic-update-slice_fusion
  104.7 0.8 convolution_add_fusion.2
  105.5 1.8 %collective-permute-done.15 = f32[1024,128]{1,0:T(8,128)S(1)} collective-permute-done((f32[1024,128]{1,0:T(8,128)S(1)}, f32[1024,128]{1,0:T(8,128)S(1)}, u32[]{:S(2)}, u32[]{:S(2)}) %collective-permute-start.15) | collective-permute-done | bytes 524320 | tf_op jit(solution)/shard_map/ppermute | solution.py:65
  107.3 0.2 fusion.36
  107.5 1.7 %broadcast_select_fusion.3 = (bf16[1024,512]{1,0:T(8,128)(2,1)S(1)}, bf16[1024,512]{1,0:T(8,128)(2,1)S(1)}) fusion(pred[]{:T(512)S(6)} %eq.8, bf16[1024,128]{1,0:T(8,128)(2,1)S(1)} %get-tuple-element.133, bf16[1024,128]{1,0:T(8,128)(2,1)S(1)} %get-tuple-element.140, bf16[1024,128]{1,0:T(8,128)(2,1)S(1)} %collective-permute-done.6, ...), kind=kLoop, calls=%fused_computation.33 | loop fusion | flops 9437184 | bytes 4194305 | tf_op jit(solution)/shard_map/jit(_where)/select_n | solution.py:143
  109.3 0.2 broadcast_select_fusion.7
  109.5 0.6 collective-permute-start.20
  110.1 2.7 %collective-permute-done.16 = bf16[1024,256]{1,0:T(8,128)(2,1)S(1)} collective-permute-done((bf16[1024,256]{1,0:T(8,128)(2,1)S(1)}, bf16[1024,256]{1,0:T(8,128)(2,1)S(1)}, u32[]{:S(2)}, u32[]{:S(2)}) %collective-permute-start.16) | collective-permute-done | bytes 524320 | tf_op jit(solution)/shard_map/ppermute | solution.py:74
  112.9 3.6 %collective-permute-start.17 = (bf16[1024,256]{1,0:T(8,128)(2,1)S(1)}, bf16[1024,256]{1,0:T(8,128)(2,1)S(1)}, u32[]{:S(2)}, u32[]{:S(2)}) collective-permute-start(bf16[1024,256]{1,0:T(8,128)(2,1)S(1)} %broadcast_select_fusion.8), channel_id=1, source_target_pairs={{0,4},{1,5},{2,6},{3,7},{4,0},{5,1},{6,2},{7,3},{8,12},{9,13},{10,... | collective-permute-start | bytes 1572872 | tf_op jit(solution)/shard_map/ppermute | solution.py:68
  116.5 2.3 %collective-permute-start.22 = (f32[1024,128]{1,0:T(8,128)S(1)}, f32[1024,128]{1,0:T(8,128)S(1)}, u32[]{:S(2)}, u32[]{:S(2)}) collective-permute-start(f32[1024,128]{1,0:T(8,128)S(1)} %convolution_add_fusion.2), channel_id=1, source_target_pairs={{0,2},{1,3},{2,0},{3,1},{4,6},{5,7},{6,4},{7,5},{8,10},{9,11},{10,... | collective-permute-start | bytes 1572872 | tf_op jit(solution)/shard_map/ppermute | solution.py:65
  118.8 0.7 fusion.24
  119.5 0.8 convolution_add_fusion.1
  120.3 0.3 copy-done.7
  120.5 1.3 fusion.8
  121.8 2.4 %fusion.5 = f32[1024,1024]{1,0:T(8,128)S(1)} fusion(f32[1024,1024]{1,0:T(8,128)S(1)} %fusion.8, bf16[1024,1024]{1,0:T(8,128)(2,1)S(1)} %constant_dynamic-update-slice_fusion, bf16[1024,512]{1,0:T(8,128)(2,1)S(1)} %collective-permute-done.18, bf16[1024,512]{1,0:T(8,128)(2,1)S(1)} %get-tuple-element.108), kind=kOutput, calls=%fused_computation.9 | convolution fusion | flops 2152726528 | bytes 12582912 | tf_op jit(solution)/shard_map/dot_general | solution.py:38
  124.2 3.0 %collective-permute-done.17 = bf16[1024,256]{1,0:T(8,128)(2,1)S(1)} collective-permute-done((bf16[1024,256]{1,0:T(8,128)(2,1)S(1)}, bf16[1024,256]{1,0:T(8,128)(2,1)S(1)}, u32[]{:S(2)}, u32[]{:S(2)}) %collective-permute-start.17) | collective-permute-done | bytes 524320 | tf_op jit(solution)/shard_map/ppermute | solution.py:68
  127.3 0.7 fusion.44
  128.1 0.7 convolution_add_fusion
  128.8 0.4 collective-permute-done.23
  129.2 3.3 %add_multiply_fusion = f32[1024,1024]{1,0:T(8,128)} fusion(f32[1024,1024]{1,0:T(8,128)S(1)} %fusion.5, f32[]{:T(128)} %bitcast, bf16[1024,256]{1,0:T(8,128)(2,1)S(1)} %collective-permute-done.23, bf16[1024,256]{1,0:T(8,128)(2,1)S(1)} %get-tuple-element.114, bf16[1024,256]{1,0:T(8,128)(2,1)S(1)} %get-tuple-element.112, bf16[1024,256]{1,0:T(8,128)(2,1)S(1)} %copy-done.6), kind=kOutput, calls=%fused_computation | convolution fusion | flops 1080033280 | bytes 10485764 | tf_op jit(solution)/shard_map/dot_general | solution.py:38
  132.6 1.6 %fusion.4 = f32[1024,512]{1,0:T(8,128)} fusion(f32[1024,256]{1,0:T(8,128)S(1)} %convolution_add_fusion, f32[1024,256]{1,0:T(8,128)S(1)} %convolution_add_fusion.1, f32[1024,128]{1,0:T(8,128)S(1)} %collective-permute-done.22, f32[1024,128]{1,0:T(8,128)S(1)} %collective-permute-done.15, f32[1024,128]{1,0:T(8,128)S(1)} %collective-permute-done.14, ...), kind=kLoop, calls=%fused_computation.6 | loop fusion | flops 3145728 | bytes 6291460 | tf_op jit(solution)/shard_map/mul | solution.py:180
  (49 shorter events, 1.5 us)
Async XLA Ops:
  2.4 9.3 %collective-permute-start.1 = (bf16[1024,128]{1,0:T(8,128)(2,1)S(1)}, bf16[1024,128]{1,0:T(8,128)(2,1)S(1)}, u32[]{:S(2)}, u32[]{:S(2)}) collective-permute-start(bf16[1024,128]{1,0:T(8,128)(2,1)S(1)} %get-tuple-element.119), channel_id=1, source_target_pairs={{0,2},{1,3},{2,0},{3,1},{4,6},{5,7},{6,4},{7,5},{8,10},{9,11},{10,... | collective-permute-start | bytes 786440 | tf_op jit(solution)/shard_map/ppermute | solution.py:65
  11.7 18.6 %copy-start.2 = (bf16[1024,128]{1,0:T(8,128)(2,1)}, bf16[1024,128]{1,0:T(8,128)(2,1)S(1)}, u32[]{:S(2)}) copy-start(bf16[1024,128]{1,0:T(8,128)(2,1)S(1)} %collective-permute-done.1) | copy-start | bytes 786436
  11.8 13.2 %collective-permute-start.2 = (bf16[1024,256]{1,0:T(8,128)(2,1)S(1)}, bf16[1024,256]{1,0:T(8,128)(2,1)S(1)}, u32[]{:S(2)}, u32[]{:S(2)}) collective-permute-start(bf16[1024,256]{1,0:T(8,128)(2,1)S(1)} %pad_maximum_fusion.3), channel_id=1, source_target_pairs={{0,2},{1,3},{2,0},{3,1},{4,6},{5,7},{6,4},{7,5},{8,10},{9,11},{10,... | collective-permute-start | bytes 1572872 | tf_op jit(solution)/shard_map/ppermute | solution.py:65
  13.6 33.6 %collective-permute-start = (bf16[1024,1024]{1,0:T(8,128)(2,1)}, bf16[1024,1024]{1,0:T(8,128)(2,1)}, u32[]{:S(2)}, u32[]{:S(2)}) collective-permute-start(bf16[1024,1024]{1,0:T(8,128)(2,1)} %param.6), channel_id=1, source_target_pairs={{0,1},{1,0},{2,3},{3,2},{4,5},{5,4},{6,7},{7,6},{8,9},{9,8},{10,11... | collective-permute-start | bytes 6291464 | tf_op jit(solution)/shard_map/ppermute | solution.py:71
  13.6 21.6 %copy-start = (bf16[1024,512]{1,0:T(8,128)(2,1)S(1)}, bf16[1024,512]{1,0:T(8,128)(2,1)}, u32[]{:S(2)}) copy-start(bf16[1024,512]{1,0:T(8,128)(2,1)} %param.5) | copy-start | bytes 3145732
  13.7 15.3 %collective-permute-start.3 = (bf16[1024,128]{1,0:T(8,128)(2,1)S(1)}, bf16[1024,128]{1,0:T(8,128)(2,1)S(1)}, u32[]{:S(2)}, u32[]{:S(2)}) collective-permute-start(bf16[1024,128]{1,0:T(8,128)(2,1)S(1)} %broadcast_select_fusion.18), channel_id=1, source_target_pairs={{0,8},{1,9},{2,10},{3,11},{4,12},{5,13},{6,14},{7,15},{8,0},{9,1},... | collective-permute-start | bytes 786440 | tf_op jit(solution)/shard_map/ppermute | solution.py:77
  29.8 6.5 %copy-start.1 = (bf16[1024,512]{1,0:T(8,128)(2,1)S(1)}, bf16[1024,512]{1,0:T(8,128)(2,1)}, u32[]{:S(2)}) copy-start(bf16[1024,512]{1,0:T(8,128)(2,1)} %param.4) | copy-start | bytes 3145732
  29.8 13.9 %collective-permute-start.7 = (bf16[1024,256]{1,0:T(8,128)(2,1)}, bf16[1024,256]{1,0:T(8,128)(2,1)}, u32[]{:S(2)}, u32[]{:S(2)}) collective-permute-start(bf16[1024,256]{1,0:T(8,128)(2,1)} %pad_maximum_fusion.4), channel_id=1, source_target_pairs={{0,2},{1,3},{2,0},{3,1},{4,6},{5,7},{6,4},{7,5},{8,10},{9,11},{10,... | collective-permute-start | bytes 1572872 | tf_op jit(solution)/shard_map/ppermute | solution.py:65
  30.4 14.4 %collective-permute-start.4 = (bf16[1024,128]{1,0:T(8,128)(2,1)S(1)}, bf16[1024,128]{1,0:T(8,128)(2,1)}, u32[]{:S(2)}, u32[]{:S(2)}) collective-permute-start(bf16[1024,128]{1,0:T(8,128)(2,1)S(1)} %broadcast_select_fusion.17), channel_id=1, source_target_pairs={{0,4},{1,5},{2,6},{3,7},{4,0},{5,1},{6,2},{7,3},{8,12},{9,13},{10,... | collective-permute-start | bytes 786440 | tf_op jit(solution)/shard_map/ppermute | solution.py:68
  31.9 15.3 %collective-permute-start.5 = (bf16[1024,128]{1,0:T(8,128)(2,1)}, bf16[1024,128]{1,0:T(8,128)(2,1)}, u32[]{:S(2)}, u32[]{:S(2)}) collective-permute-start(bf16[1024,128]{1,0:T(8,128)(2,1)} %broadcast_select_fusion.16), channel_id=1, source_target_pairs={{0,8},{1,9},{2,10},{3,11},{4,12},{5,13},{6,14},{7,15},{8,0},{9,1},... | collective-permute-start | bytes 786440 | tf_op jit(solution)/shard_map/ppermute | solution.py:77
  52.2 12.5 %collective-permute-start.6 = (bf16[1024,128]{1,0:T(8,128)(2,1)S(1)}, bf16[1024,128]{1,0:T(8,128)(2,1)S(1)}, u32[]{:S(2)}, u32[]{:S(2)}) collective-permute-start(bf16[1024,128]{1,0:T(8,128)(2,1)S(1)} %broadcast_select_fusion.15), channel_id=1, source_target_pairs={{0,4},{1,5},{2,6},{3,7},{4,0},{5,1},{6,2},{7,3},{8,12},{9,13},{10,... | collective-permute-start | bytes 786440 | tf_op jit(solution)/shard_map/ppermute | solution.py:68
  52.4 14.8 %collective-permute-start.8 = (bf16[1024,128]{1,0:T(8,128)(2,1)S(1)}, bf16[1024,128]{1,0:T(8,128)(2,1)S(1)}, u32[]{:S(2)}, u32[]{:S(2)}) collective-permute-start(bf16[1024,128]{1,0:T(8,128)(2,1)S(1)} %broadcast_select_fusion.13), channel_id=1, source_target_pairs={{0,8},{1,9},{2,10},{3,11},{4,12},{5,13},{6,14},{7,15},{8,0},{9,1},... | collective-permute-start | bytes 786440 | tf_op jit(solution)/shard_map/ppermute | solution.py:77
  56.3 18.9 %collective-permute-start.11 = (f32[1024,128]{1,0:T(8,128)S(1)}, f32[1024,128]{1,0:T(8,128)S(1)}, u32[]{:S(2)}, u32[]{:S(2)}) collective-permute-start(f32[1024,128]{1,0:T(8,128)S(1)} %convolution_add_fusion.5), channel_id=1, source_target_pairs={{0,2},{1,3},{2,0},{3,1},{4,6},{5,7},{6,4},{7,5},{8,10},{9,11},{10,... | collective-permute-start | bytes 1572872 | tf_op jit(solution)/shard_map/ppermute | solution.py:65
  57.8 16.3 %collective-permute-start.10 = (bf16[1024,128]{1,0:T(8,128)(2,1)S(1)}, bf16[1024,128]{1,0:T(8,128)(2,1)S(1)}, u32[]{:S(2)}, u32[]{:S(2)}) collective-permute-start(bf16[1024,128]{1,0:T(8,128)(2,1)S(1)} %broadcast_select_fusion.12), channel_id=1, source_target_pairs={{0,2},{1,3},{2,0},{3,1},{4,6},{5,7},{6,4},{7,5},{8,10},{9,11},{10,... | collective-permute-start | bytes 786440 | tf_op jit(solution)/shard_map/ppermute | solution.py:65
  65.5 8.6 %copy-start.3 = (bf16[1024,128]{1,0:T(8,128)(2,1)S(1)}, bf16[1024,128]{1,0:T(8,128)(2,1)}, u32[]{:S(2)}) copy-start(bf16[1024,128]{1,0:T(8,128)(2,1)} %copy-done.2) | copy-start | bytes 786436
  66.3 8.1 %copy-start.4 = (bf16[1024,128]{1,0:T(8,128)(2,1)S(1)}, bf16[1024,128]{1,0:T(8,128)(2,1)}, u32[]{:S(2)}) copy-start(bf16[1024,128]{1,0:T(8,128)(2,1)} %get-tuple-element.93) | copy-start | bytes 786436
  67.3 11.2 %collective-permute-start.9 = (bf16[1024,256]{1,0:T(8,128)(2,1)S(1)}, bf16[1024,256]{1,0:T(8,128)(2,1)S(1)}, u32[]{:S(2)}, u32[]{:S(2)}) collective-permute-start(bf16[1024,256]{1,0:T(8,128)(2,1)S(1)} %maximum_select_fusion), channel_id=1, source_target_pairs={{0,4},{1,5},{2,6},{3,7},{4,0},{5,1},{6,2},{7,3},{8,12},{9,13},{10,... | collective-permute-start | bytes 1572872 | tf_op jit(solution)/shard_map/ppermute | solution.py:68
  74.5 30.0 %collective-permute-start.19 = (bf16[1024,512]{1,0:T(8,128)(2,1)S(1)}, bf16[1024,512]{1,0:T(8,128)(2,1)S(1)}, u32[]{:S(2)}, u32[]{:S(2)}) collective-permute-start(bf16[1024,512]{1,0:T(8,128)(2,1)S(1)} %pad_maximum_fusion.2), channel_id=1, source_target_pairs={{0,1},{1,0},{2,3},{3,2},{4,5},{5,4},{6,7},{7,6},{8,9},{9,8},{10,11... | collective-permute-start | bytes 3145736 | tf_op jit(solution)/shard_map/ppermute | solution.py:71
  74.6 19.9 %collective-permute-start.21 = (bf16[1024,512]{1,0:T(8,128)(2,1)S(1)}, bf16[1024,512]{1,0:T(8,128)(2,1)S(1)}, u32[]{:S(2)}, u32[]{:S(2)}) collective-permute-start(bf16[1024,512]{1,0:T(8,128)(2,1)S(1)} %copy-done), channel_id=1, source_target_pairs={{0,1},{1,0},{2,3},{3,2},{4,5},{5,4},{6,7},{7,6},{8,9},{9,8},{10,11... | collective-permute-start | bytes 3145736 | tf_op jit(solution)/shard_map/ppermute | solution.py:71
  75.2 14.8 %collective-permute-start.12 = (bf16[1024,128]{1,0:T(8,128)(2,1)S(1)}, bf16[1024,128]{1,0:T(8,128)(2,1)S(1)}, u32[]{:S(2)}, u32[]{:S(2)}) collective-permute-start(bf16[1024,128]{1,0:T(8,128)(2,1)S(1)} %broadcast_select_fusion.11), channel_id=1, source_target_pairs={{0,8},{1,9},{2,10},{3,11},{4,12},{5,13},{6,14},{7,15},{8,0},{9,1},... | collective-permute-start | bytes 786440 | tf_op jit(solution)/shard_map/ppermute | solution.py:77
  75.6 18.7 %collective-permute-start.14 = (f32[1024,128]{1,0:T(8,128)S(1)}, f32[1024,128]{1,0:T(8,128)S(1)}, u32[]{:S(2)}, u32[]{:S(2)}) collective-permute-start(f32[1024,128]{1,0:T(8,128)S(1)} %convolution_add_fusion.4), channel_id=1, source_target_pairs={{0,2},{1,3},{2,0},{3,1},{4,6},{5,7},{6,4},{7,5},{8,10},{9,11},{10,... | collective-permute-start | bytes 1572872 | tf_op jit(solution)/shard_map/ppermute | solution.py:65
  79.2 11.1 %copy-start.5 = (bf16[1024,256]{1,0:T(8,128)(2,1)S(1)}, bf16[1024,256]{1,0:T(8,128)(2,1)}, u32[]{:S(2)}) copy-start(bf16[1024,256]{1,0:T(8,128)(2,1)} %slice.102) | copy-start | bytes 1572868
  90.2 13.6 %collective-permute-start.13 = (bf16[1024,256]{1,0:T(8,128)(2,1)S(1)}, bf16[1024,256]{1,0:T(8,128)(2,1)S(1)}, u32[]{:S(2)}, u32[]{:S(2)}) collective-permute-start(bf16[1024,256]{1,0:T(8,128)(2,1)S(1)} %maximum_select_fusion.1), channel_id=1, source_target_pairs={{0,4},{1,5},{2,6},{3,7},{4,0},{5,1},{6,2},{7,3},{8,12},{9,13},{10,... | collective-permute-start | bytes 1572872 | tf_op jit(solution)/shard_map/ppermute | solution.py:68
  90.3 22.5 %collective-permute-start.16 = (bf16[1024,256]{1,0:T(8,128)(2,1)S(1)}, bf16[1024,256]{1,0:T(8,128)(2,1)S(1)}, u32[]{:S(2)}, u32[]{:S(2)}) collective-permute-start(bf16[1024,256]{1,0:T(8,128)(2,1)S(1)} %copy-done.5), channel_id=1, source_target_pairs={{0,8},{1,9},{4,12},{5,13},{10,2},{11,3},{14,6},{15,7},{16,24},{17,... | collective-permute-start | bytes 1572872 | tf_op jit(solution)/shard_map/ppermute | solution.py:74
  94.4 12.9 %collective-permute-start.15 = (f32[1024,128]{1,0:T(8,128)S(1)}, f32[1024,128]{1,0:T(8,128)S(1)}, u32[]{:S(2)}, u32[]{:S(2)}) collective-permute-start(f32[1024,128]{1,0:T(8,128)S(1)} %convolution_add_fusion.3), channel_id=1, source_target_pairs={{0,2},{1,3},{2,0},{3,1},{4,6},{5,7},{6,4},{7,5},{8,10},{9,11},{10,... | collective-permute-start | bytes 1572872 | tf_op jit(solution)/shard_map/ppermute | solution.py:65
  109.2 12.6 %collective-permute-start.18 = (bf16[1024,512]{1,0:T(8,128)(2,1)S(1)}, bf16[1024,512]{1,0:T(8,128)(2,1)S(1)}, u32[]{:S(2)}, u32[]{:S(2)}) collective-permute-start(bf16[1024,512]{1,0:T(8,128)(2,1)S(1)} %get-tuple-element.109), channel_id=1, source_target_pairs={{0,1},{1,0},{2,3},{3,2},{4,5},{5,4},{6,7},{7,6},{8,9},{9,8},{10,11... | collective-permute-start | bytes 3145736 | tf_op jit(solution)/shard_map/ppermute | solution.py:71
  109.5 10.7 %collective-permute-start.20 = (bf16[1024,256]{1,0:T(8,128)(2,1)S(1)}, bf16[1024,256]{1,0:T(8,128)(2,1)S(1)}, u32[]{:S(2)}, u32[]{:S(2)}) collective-permute-start(bf16[1024,256]{1,0:T(8,128)(2,1)S(1)} %get-tuple-element.117), channel_id=1, source_target_pairs={{0,1},{1,0},{2,3},{3,2},{4,5},{5,4},{6,7},{7,6},{8,9},{9,8},{10,11... | collective-permute-start | bytes 1572872 | tf_op jit(solution)/shard_map/ppermute | solution.py:71
  112.9 14.3 %collective-permute-start.17 = (bf16[1024,256]{1,0:T(8,128)(2,1)S(1)}, bf16[1024,256]{1,0:T(8,128)(2,1)S(1)}, u32[]{:S(2)}, u32[]{:S(2)}) collective-permute-start(bf16[1024,256]{1,0:T(8,128)(2,1)S(1)} %broadcast_select_fusion.8), channel_id=1, source_target_pairs={{0,4},{1,5},{2,6},{3,7},{4,0},{5,1},{6,2},{7,3},{8,12},{9,13},{10,... | collective-permute-start | bytes 1572872 | tf_op jit(solution)/shard_map/ppermute | solution.py:68
  116.5 16.1 %collective-permute-start.22 = (f32[1024,128]{1,0:T(8,128)S(1)}, f32[1024,128]{1,0:T(8,128)S(1)}, u32[]{:S(2)}, u32[]{:S(2)}) collective-permute-start(f32[1024,128]{1,0:T(8,128)S(1)} %convolution_add_fusion.2), channel_id=1, source_target_pairs={{0,2},{1,3},{2,0},{3,1},{4,6},{5,7},{6,4},{7,5},{8,10},{9,11},{10,... | collective-permute-start | bytes 1572872 | tf_op jit(solution)/shard_map/ppermute | solution.py:65
  119.5 1.0 copy-start.7
  127.2 2.0 %collective-permute-start.23 = (bf16[1024,256]{1,0:T(8,128)(2,1)S(1)}, bf16[1024,256]{1,0:T(8,128)(2,1)S(1)}, u32[]{:S(2)}, u32[]{:S(2)}) collective-permute-start(bf16[1024,256]{1,0:T(8,128)(2,1)S(1)} %get-tuple-element.115), channel_id=1, source_target_pairs={{0,1},{1,0},{2,3},{3,2},{4,5},{5,4},{6,7},{7,6},{8,9},{9,8},{10,11... | collective-permute-start | bytes 1572872 | tf_op jit(solution)/shard_map/ppermute | solution.py:71
  128.1 1.2 copy-start.6

commit v9 on v8

--- a/solution.py
+++ b/solution.py
@@ -99,7 +99,7 @@
         v1, e1 = together((v[1], e[1]), x1)
         x2 = cross(jnp.concatenate([jnp.where(home, v1, e1), v[2]], 1))
         x2, v_across2 = columns(x2, 0, 1), columns(x2, 1, 2)
-        t, t_o = together((transition, t_other), x2)
+        t, t_o = together((transition, t_other), x1)
         t_near, t_next = jnp.where(mine, t, t_o), jnp.where(mine, t_o, t)
 
         def adjoint_of(near, far):
@@ -108,30 +108,31 @@
         near, far = together((x1, j1), x2)
         b0 = jnp.where(home, near, far)
         b0_next = step(b0)
-        near, far = together((x2, e[3]), j1, b0)
+        near, far = together((x2, e[3]))
         j2 = jump(jnp.where(home, near, far))
-        near, far = together((j1, v[0]), x2)
-        x3 = cross(jnp.concatenate([jnp.where(home, near, far), v[3]], 1))
-        x3, v_across3 = columns(x3, 0, 1), columns(x3, 1, 2)
+        near, far = together((j1, v[0]), x2, t_near)
+        x3 = cross(jnp.where(home, near, far))
         sum0 = adjoint_of(b0, b0_next)
-        part0 = cross(after(sum0, x3))
-        near, far = together((e[0], x3), j2, b0_next)
-        j3 = jump(jnp.where(home, near, far))
-        near, far = together((x2, j2), sum0)
+        near, far = together((e[0], x3))
+        third = jnp.where(home, near, far)
+        j3 = jump(third)
+        near, far = together((x2, j2), sum0, third)
         b1 = jnp.where(home, near, far)
         b1_next = step(b1)
-        near, far = together((j2, v[1]), x3, sum0)
+        near, far = together((j2, v[1]), third, sum0)
         x4 = cross(jnp.where(home, near, far))
-        near, far = together((e[1], x4), j3, part0)
+        part0 = cross(after(sum0, x4))
+        near, far = together((e[1], x4))
         j4 = jump(jnp.where(home, near, far))
         sum1 = adjoint_of(b1, b1_next)
-        part1 = cross(after(sum1, part0, x4))
-        near, both, far = together((e[0], j3, x3), sum1)
+        part1 = cross(after(sum1, part0))
+        v_across3 = cross(after(v[3], part0))
+        near, both, far = together((e[0], j3, x3), sum1, x4)
         a0b2 = jnp.where(home, jnp.concatenate([near, both], 1), jnp.concatenate([both, far], 1))
         a0b2_next = step(a0b2)
         sum2 = adjoint_of(columns(a0b2, 1, 2), columns(a0b2_next, 1, 2))
         part2 = cross(after(sum2, part1))
-        j5 = home_jump(after(columns(expected_cot, 2, 4), j4))
+        j5 = home_jump(after(columns(expected_cot, 2, 4), j3))
         near, both, far = together((e[1], j4, x4), sum2, part0)
         a1b3 = jnp.where(home, jnp.concatenate([near, both], 1), jnp.concatenate([both, far], 1))
         a1b3_next = step(a1b3)

time: 137 us -> 136 us (level); the launches traced: 134 us -> 136 us
  waiting for transfers between devices: 68.8 us -> 79.7 us
  starting transfers between devices: 30.6 us -> 25.7 us
  local copies, waits for them, and re-layouts: 4.61 us -> 2.23 us
    ppermute x8 -> x9, waiting for transfers between devices: 29.2 us -> 43 us  [cross(): return lax.ppermute(a, AXES, cross_pairs)]
    ppermute x4, waiting for transfers between devices: 16.5 us -> 3.06 us  [jump(): return lax.ppermute(a, AXES, jump_pairs)]
    ppermute x5, waiting for transfers between devices: 19.9 us -> 33.2 us  [step(): return lax.ppermute(a, AXES, step_pairs)]
    ppermute x5, starting transfers between devices: 4.81 us -> 1.06 us  [step(): return lax.ppermute(a, AXES, step_pairs)]
    ppermute x4, starting transfers between devices: 10.4 us -> 13.3 us  [jump(): return lax.ppermute(a, AXES, jump_pairs)]
    ppermute x8 -> x9, starting transfers between devices: 10.2 us -> 7.43 us  [cross(): return lax.ppermute(a, AXES, cross_pairs)]
    ppermute x1, waiting for transfers between devices: 2.73 us -> 0.01 us  [home_jump(): return lax.ppermute(a, AXES, home_jump_pairs)]
    slice x8 -> x7, local copies, waits for them, and re-layouts: 4.01 us -> 1.49 us  [columns(): return array[:, start * quarter:stop * quarter]]
  transfers between devices with their start and end apart: 24 -> 25, of which waited for: 15 -> 14; matrix products, arithmetic and copies ran while one was open for 18% -> 20% of each run, Pallas kernels for 0% -> 0%
where the time goes in v9:
time: 136 us
  waiting for transfers between devices  79.7 us (59%)
  starting transfers between devices  25.7 us (19%)
  matrix products  16 us (12%)
  other arithmetic  10.6 us (8%)
  local copies, waits for them, and re-layouts  2.23 us (2%)
  between operations  1.72 us (1%)
    ppermute x9, waiting for transfers between devices, cross(): return lax.ppermute(a, AXES, cross_pairs)  43 us
    ppermute x5, waiting for transfers between devices, step(): return lax.ppermute(a, AXES, step_pairs)  33.2 us
    ppermute x4, starting transfers between devices, jump(): return lax.ppermute(a, AXES, jump_pairs)  13.3 us
    dot_general x12, matrix products, tdot(): lax.dot_general(a, b, (((0,), (0,)), ((), ())), preferred_element_type=jn...  9.03 us
    ppermute x9, starting transfers between devices, cross(): return lax.ppermute(a, AXES, cross_pairs)  7.43 us
    dot_general x3, matrix products, dott(): lax.dot_general(a, b, (((1,), (1,)), ((), ())), preferred_element_type=jn...  6.95 us
    ppermute x4, waiting for transfers between devices, jump(): return lax.ppermute(a, AXES, jump_pairs)  3.06 us
  transfers between devices with their start and end apart: 25, of which 14 were waited for; matrix products, arithmetic and copies ran while one was open for 20% of the time, Pallas kernels for 0%

profile of v9, /device:TPU:0, one launch (start us, length us, event | category | flops | bytes accessed | tf_op | source)
XLA Modules:
  0.0 136.0 jit_solution(6938587607978922502)
XLA Ops:
  0.6 0.5 collective-permute-start
  1.1 2.5 %fusion.35 = (bf16[1024,128]{1,0:T(8,128)(2,1)}, bf16[1024,128]{1,0:T(8,128)(2,1)S(1)}, bf16[1024,128]{1,0:T(8,128)(2,1)}, bf16[1024,128]{1,0:T(8,128)(2,1)S(1)}...) fusion(bf16[1024,512]{1,0:T(8,128)(2,1)} %param.5, ...), kind=kLoop, calls=%fused_computation.75 | loop fusion | flops 131072 | bytes 4456449 | tf_op jit(solution)/shard_map/slice | solution.py:88
  3.7 2.5 %collective-permute-start.1 = (bf16[1024,128]{1,0:T(8,128)(2,1)S(1)}, bf16[1024,128]{1,0:T(8,128)(2,1)S(1)}, u32[]{:S(2)}, u32[]{:S(2)}) collective-permute-start(bf16[1024,128]{1,0:T(8,128)(2,1)S(1)} %get-tuple-element.119), channel_id=1, source_target_pairs={{0,2},{1,3},{2,0},{3,1},{4,6},{5,7},{6,4},{7,5},{8,10},{9,11},{10,... | collective-permute-start | bytes 786440 | tf_op jit(solution)/shard_map/ppermute | solution.py:65
  6.2 6.9 %collective-permute-done.1 = bf16[1024,128]{1,0:T(8,128)(2,1)S(1)} collective-permute-done((bf16[1024,128]{1,0:T(8,128)(2,1)S(1)}, bf16[1024,128]{1,0:T(8,128)(2,1)S(1)}, u32[]{:S(2)}, u32[]{:S(2)}) %collective-permute-start.1) | collective-permute-done | bytes 262176 | tf_op jit(solution)/shard_map/ppermute | solution.py:65
  13.2 0.9 pad_maximum_fusion.3
  14.0 1.7 %collective-permute-start.3 = (bf16[1024,256]{1,0:T(8,128)(2,1)}, bf16[1024,256]{1,0:T(8,128)(2,1)}, u32[]{:S(2)}, u32[]{:S(2)}) collective-permute-start(bf16[1024,256]{1,0:T(8,128)(2,1)} %pad_maximum_fusion.3), channel_id=1, source_target_pairs={{0,2},{1,3},{2,0},{3,1},{4,6},{5,7},{6,4},{7,5},{8,10},{9,11},{10,... | collective-permute-start | bytes 1572872 | tf_op jit(solution)/shard_map/ppermute | solution.py:65
  15.8 0.7 broadcast_select_fusion.19
  16.5 2.6 %collective-permute-start.2 = (bf16[1024,128]{1,0:T(8,128)(2,1)}, bf16[1024,128]{1,0:T(8,128)(2,1)}, u32[]{:S(2)}, u32[]{:S(2)}) collective-permute-start(bf16[1024,128]{1,0:T(8,128)(2,1)} %broadcast_select_fusion.19), channel_id=1, source_target_pairs={{0,8},{1,9},{2,10},{3,11},{4,12},{5,13},{6,14},{7,15},{8,0},{9,1},... | collective-permute-start | bytes 786440 | tf_op jit(solution)/shard_map/ppermute | solution.py:77
  19.1 9.0 %collective-permute-done.3 = bf16[1024,256]{1,0:T(8,128)(2,1)} collective-permute-done((bf16[1024,256]{1,0:T(8,128)(2,1)}, bf16[1024,256]{1,0:T(8,128)(2,1)}, u32[]{:S(2)}, u32[]{:S(2)}) %collective-permute-start.3) | collective-permute-done | bytes 524320 | tf_op jit(solution)/shard_map/ppermute | solution.py:65
  28.1 1.1 fusion.40
  29.1 1.8 %collective-permute-done.2 = bf16[1024,128]{1,0:T(8,128)(2,1)} collective-permute-done((bf16[1024,128]{1,0:T(8,128)(2,1)}, bf16[1024,128]{1,0:T(8,128)(2,1)}, u32[]{:S(2)}, u32[]{:S(2)}) %collective-permute-start.2) | collective-permute-done | bytes 262176 | tf_op jit(solution)/shard_map/ppermute | solution.py:77
  31.0 0.7 collective-permute-start.4
  31.8 5.3 %collective-permute-start.5 = (bf16[1024,128]{1,0:T(8,128)(2,1)S(1)}, bf16[1024,128]{1,0:T(8,128)(2,1)S(1)}, u32[]{:S(2)}, u32[]{:S(2)}) collective-permute-start(bf16[1024,128]{1,0:T(8,128)(2,1)S(1)} %broadcast_select_fusion.16), channel_id=1, source_target_pairs={{0,8},{1,9},{2,10},{3,11},{4,12},{5,13},{6,14},{7,15},{8,0},{9,1},... | collective-permute-start | bytes 786440 | tf_op jit(solution)/shard_map/ppermute | solution.py:77
  37.1 1.9 %broadcast_select_fusion.1 = (bf16[1024,1024]{1,0:T(8,128)(2,1)S(1)}, bf16[1024,1024]{1,0:T(8,128)(2,1)S(1)}) fusion(bf16[1024,1024]{1,0:T(8,128)(2,1)S(1)} %copy-done.2, bf16[1024,1024]{1,0:T(8,128)(2,1)} %collective-permute-done, pred[]{:T(512)S(6)} %eq.8), kind=kLoop, calls=%fused_computation.8 | loop fusion | flops 2097152 | bytes 8388609 | tf_op jit(solution)/shard_map/jit(_where)/select_n | solution.py:103
  39.0 1.0 broadcast_select_fusion.15
  40.0 2.2 %collective-permute-done.4 = bf16[1024,128]{1,0:T(8,128)(2,1)S(1)} collective-permute-done((bf16[1024,128]{1,0:T(8,128)(2,1)S(1)}, bf16[1024,128]{1,0:T(8,128)(2,1)S(1)}, u32[]{:S(2)}, u32[]{:S(2)}) %collective-permute-start.4) | collective-permute-done | bytes 262176 | tf_op jit(solution)/shard_map/ppermute | solution.py:68
  42.3 0.7 fusion.41
  43.0 0.8 convolution_add_fusion.5
  43.8 3.9 %collective-permute-done.6 = bf16[1024,128]{1,0:T(8,128)(2,1)S(1)} collective-permute-done((bf16[1024,128]{1,0:T(8,128)(2,1)S(1)}, bf16[1024,128]{1,0:T(8,128)(2,1)S(1)}, u32[]{:S(2)}, u32[]{:S(2)}) %collective-permute-start.6) | collective-permute-done | bytes 262176 | tf_op jit(solution)/shard_map/ppermute | solution.py:65
  47.7 1.2 collective-permute-done.5
  49.1 2.9 %collective-permute-start.8 = (bf16[1024,128]{1,0:T(8,128)(2,1)S(1)}, bf16[1024,128]{1,0:T(8,128)(2,1)S(1)}, u32[]{:S(2)}, u32[]{:S(2)}) collective-permute-start(bf16[1024,128]{1,0:T(8,128)(2,1)S(1)} %broadcast_select_fusion.14), channel_id=1, source_target_pairs={{0,8},{1,9},{2,10},{3,11},{4,12},{5,13},{6,14},{7,15},{8,0},{9,1},... | collective-permute-start | bytes 786440 | tf_op jit(solution)/shard_map/ppermute | solution.py:77
  52.1 9.7 %collective-permute-done.7 = bf16[1024,128]{1,0:T(8,128)(2,1)S(1)} collective-permute-done((bf16[1024,128]{1,0:T(8,128)(2,1)S(1)}, bf16[1024,128]{1,0:T(8,128)(2,1)S(1)}, u32[]{:S(2)}, u32[]{:S(2)}) %collective-permute-start.7) | collective-permute-done | bytes 262176 | tf_op jit(solution)/shard_map/ppermute | solution.py:68
  61.8 0.7 fusion.42
  62.5 0.8 convolution_add_fusion.4
  63.3 0.2 maximum_select_fusion
  63.5 0.1 collective-permute-start.10
  63.6 0.1 copy-done.1
  64.5 0.1 copy-done
  64.8 2.5 %collective-permute-start.11 = (bf16[1024,128]{1,0:T(8,128)(2,1)S(1)}, bf16[1024,128]{1,0:T(8,128)(2,1)S(1)}, u32[]{:S(2)}, u32[]{:S(2)}) collective-permute-start(bf16[1024,128]{1,0:T(8,128)(2,1)S(1)} %broadcast_select_fusion.11), channel_id=1, source_target_pairs={{0,8},{1,9},{2,10},{3,11},{4,12},{5,13},{6,14},{7,15},{8,0},{9,1},... | collective-permute-start | bytes 786440 | tf_op jit(solution)/shard_map/ppermute | solution.py:77
  67.3 2.6 %collective-permute-start.16 = (bf16[1024,256]{1,0:T(8,128)(2,1)S(1)}, bf16[1024,256]{1,0:T(8,128)(2,1)S(1)}, u32[]{:S(2)}, u32[]{:S(2)}) collective-permute-start(bf16[1024,256]{1,0:T(8,128)(2,1)S(1)} %slice.94), channel_id=1, source_target_pairs={{0,8},{1,9},{4,12},{5,13},{10,2},{11,3},{14,6},{15,7},{16,24},{17,... | collective-permute-start | bytes 1572872 | tf_op jit(solution)/shard_map/ppermute | solution.py:74
  69.9 12.1 %collective-permute-done.10 = bf16[1024,256]{1,0:T(8,128)(2,1)S(1)} collective-permute-done((bf16[1024,256]{1,0:T(8,128)(2,1)S(1)}, bf16[1024,256]{1,0:T(8,128)(2,1)S(1)}, u32[]{:S(2)}, u32[]{:S(2)}) %collective-permute-start.10) | collective-permute-done | bytes 524320 | tf_op jit(solution)/shard_map/ppermute | solution.py:68
  82.0 0.8 fusion.21
  82.8 0.8 convolution_add_fusion.3
  83.6 0.1 copy-done.3
  83.7 0.2 maximum_select_fusion.1
  84.0 2.1 %collective-permute-start.14 = (f32[1024,128]{1,0:T(8,128)S(1)}, f32[1024,128]{1,0:T(8,128)S(1)}, u32[]{:S(2)}, u32[]{:S(2)}) collective-permute-start(f32[1024,128]{1,0:T(8,128)S(1)} %convolution_add_fusion.4), channel_id=1, source_target_pairs={{0,2},{1,3},{2,0},{3,1},{4,6},{5,7},{6,4},{7,5},{8,10},{9,11},{10,... | collective-permute-start | bytes 1572872 | tf_op jit(solution)/shard_map/ppermute | solution.py:65
  86.1 6.9 %collective-permute-done.19 = bf16[1024,128]{1,0:T(8,128)(2,1)S(1)} collective-permute-done((bf16[1024,128]{1,0:T(8,128)(2,1)S(1)}, bf16[1024,128]{1,0:T(8,128)(2,1)S(1)}, u32[]{:S(2)}, u32[]{:S(2)}) %collective-permute-start.19) | collective-permute-done | bytes 262176 | tf_op jit(solution)/shard_map/ppermute | solution.py:65
  92.9 0.1 constant_dynamic-update-slice_fusion.4
  93.0 0.1 constant_dynamic-update-slice_fusion.3
  93.2 0.1 pad_maximum_fusion.2
  93.4 0.1 constant_dynamic-update-slice_fusion.2
  93.5 0.1 constant_dynamic-update-slice_fusion.1
  93.6 7.8 %collective-permute-done.14 = f32[1024,128]{1,0:T(8,128)S(1)} collective-permute-done((f32[1024,128]{1,0:T(8,128)S(1)}, f32[1024,128]{1,0:T(8,128)S(1)}, u32[]{:S(2)}, u32[]{:S(2)}) %collective-permute-start.14) | collective-permute-done | bytes 524320 | tf_op jit(solution)/shard_map/ppermute | solution.py:65
  101.5 0.8 collective-permute-done.13
  102.3 0.8 fusion.30
  103.2 0.8 convolution_add_fusion.2
  104.0 8.4 %collective-permute-done.15 = f32[1024,128]{1,0:T(8,128)S(1)} collective-permute-done((f32[1024,128]{1,0:T(8,128)S(1)}, f32[1024,128]{1,0:T(8,128)S(1)}, u32[]{:S(2)}, u32[]{:S(2)}) %collective-permute-start.15) | collective-permute-done | bytes 524320 | tf_op jit(solution)/shard_map/ppermute | solution.py:65
  112.4 0.2 fusion.36
  112.6 0.8 broadcast_select_fusion.3
  113.4 0.7 fusion.24
  114.2 0.2 broadcast_select_fusion.7
  114.4 0.6 collective-permute-start.21
  115.2 0.8 collective-permute-start.23
  116.0 0.7 convolution_add_fusion.1
  116.7 0.1 constant_dynamic-update-slice_fusion
  116.9 1.3 fusion.8
  118.2 2.4 %fusion.5 = f32[1024,1024]{1,0:T(8,128)S(1)} fusion(f32[1024,1024]{1,0:T(8,128)S(1)} %fusion.8, bf16[1024,1024]{1,0:T(8,128)(2,1)S(1)} %constant_dynamic-update-slice_fusion, bf16[1024,512]{1,0:T(8,128)(2,1)S(1)} %collective-permute-done.18, bf16[1024,512]{1,0:T(8,128)(2,1)S(1)} %get-tuple-element.110), kind=kOutput, calls=%fused_computation.9 | convolution fusion | flops 2152726528 | bytes 12582912 | tf_op jit(solution)/shard_map/dot_general | solution.py:38
  120.6 8.4 %collective-permute-done.17 = bf16[1024,256]{1,0:T(8,128)(2,1)S(1)} collective-permute-done((bf16[1024,256]{1,0:T(8,128)(2,1)S(1)}, bf16[1024,256]{1,0:T(8,128)(2,1)S(1)}, u32[]{:S(2)}, u32[]{:S(2)}) %collective-permute-start.17) | collective-permute-done | bytes 524320 | tf_op jit(solution)/shard_map/ppermute | solution.py:68
  129.0 0.1 broadcast_select_fusion.5
  129.1 0.7 fusion.43
  129.9 0.7 convolution_add_fusion
  130.6 0.4 collective-permute-done.24
  131.0 3.3 %add_multiply_fusion = f32[1024,1024]{1,0:T(8,128)} fusion(f32[1024,1024]{1,0:T(8,128)S(1)} %fusion.5, f32[]{:T(128)} %bitcast, bf16[1024,256]{1,0:T(8,128)(2,1)S(1)} %collective-permute-done.24, bf16[1024,256]{1,0:T(8,128)(2,1)S(1)} %get-tuple-element.116, bf16[1024,256]{1,0:T(8,128)(2,1)S(1)} %get-tuple-element.114, bf16[1024,256]{1,0:T(8,128)(2,1)S(1)} %get-tuple-element.112), kind=kOutput, calls=%fused_computation | convolution fusion | flops 1080033280 | bytes 10485764 | tf_op jit(solution)/shard_map/dot_general | solution.py:38
  134.3 1.6 %fusion.4 = f32[1024,512]{1,0:T(8,128)} fusion(f32[1024,256]{1,0:T(8,128)S(1)} %convolution_add_fusion, f32[1024,256]{1,0:T(8,128)S(1)} %convolution_add_fusion.1, f32[1024,128]{1,0:T(8,128)S(1)} %collective-permute-done.23, f32[1024,128]{1,0:T(8,128)S(1)} %collective-permute-done.15, f32[1024,128]{1,0:T(8,128)S(1)} %collective-permute-done.14, ...), kind=kLoop, calls=%fused_computation.6 | loop fusion | flops 3145728 | bytes 6291460 | tf_op jit(solution)/shard_map/mul | solution.py:181
  (41 shorter events, 1.3 us)
Async XLA Ops:
  0.6 36.5 %collective-permute-start = (bf16[1024,1024]{1,0:T(8,128)(2,1)}, bf16[1024,1024]{1,0:T(8,128)(2,1)}, u32[]{:S(2)}, u32[]{:S(2)}) collective-permute-start(bf16[1024,1024]{1,0:T(8,128)(2,1)} %param.6), channel_id=1, source_target_pairs={{0,1},{1,0},{2,3},{3,2},{4,5},{5,4},{6,7},{7,6},{8,9},{9,8},{10,11... | collective-permute-start | bytes 6291464 | tf_op jit(solution)/shard_map/ppermute | solution.py:71
  3.7 9.5 %collective-permute-start.1 = (bf16[1024,128]{1,0:T(8,128)(2,1)S(1)}, bf16[1024,128]{1,0:T(8,128)(2,1)S(1)}, u32[]{:S(2)}, u32[]{:S(2)}) collective-permute-start(bf16[1024,128]{1,0:T(8,128)(2,1)S(1)} %get-tuple-element.119), channel_id=1, source_target_pairs={{0,2},{1,3},{2,0},{3,1},{4,6},{5,7},{6,4},{7,5},{8,10},{9,11},{10,... | collective-permute-start | bytes 786440 | tf_op jit(solution)/shard_map/ppermute | solution.py:65
  13.2 23.9 %copy-start.2 = (bf16[1024,1024]{1,0:T(8,128)(2,1)S(1)}, bf16[1024,1024]{1,0:T(8,128)(2,1)}, u32[]{:S(2)}) copy-start(bf16[1024,1024]{1,0:T(8,128)(2,1)} %param.6) | copy-start | bytes 6291460
  14.0 14.0 %collective-permute-start.3 = (bf16[1024,256]{1,0:T(8,128)(2,1)}, bf16[1024,256]{1,0:T(8,128)(2,1)}, u32[]{:S(2)}, u32[]{:S(2)}) collective-permute-start(bf16[1024,256]{1,0:T(8,128)(2,1)} %pad_maximum_fusion.3), channel_id=1, source_target_pairs={{0,2},{1,3},{2,0},{3,1},{4,6},{5,7},{6,4},{7,5},{8,10},{9,11},{10,... | collective-permute-start | bytes 1572872 | tf_op jit(solution)/shard_map/ppermute | solution.py:65
  16.5 14.4 %collective-permute-start.2 = (bf16[1024,128]{1,0:T(8,128)(2,1)}, bf16[1024,128]{1,0:T(8,128)(2,1)}, u32[]{:S(2)}, u32[]{:S(2)}) collective-permute-start(bf16[1024,128]{1,0:T(8,128)(2,1)} %broadcast_select_fusion.19), channel_id=1, source_target_pairs={{0,8},{1,9},{2,10},{3,11},{4,12},{5,13},{6,14},{7,15},{8,0},{9,1},... | collective-permute-start | bytes 786440 | tf_op jit(solution)/shard_map/ppermute | solution.py:77
  31.0 11.3 %collective-permute-start.4 = (bf16[1024,128]{1,0:T(8,128)(2,1)S(1)}, bf16[1024,128]{1,0:T(8,128)(2,1)S(1)}, u32[]{:S(2)}, u32[]{:S(2)}) collective-permute-start(bf16[1024,128]{1,0:T(8,128)(2,1)S(1)} %broadcast_select_fusion.17), channel_id=1, source_target_pairs={{0,4},{1,5},{2,6},{3,7},{4,0},{5,1},{6,2},{7,3},{8,12},{9,13},{10,... | collective-permute-start | bytes 786440 | tf_op jit(solution)/shard_map/ppermute | solution.py:68
  31.8 17.2 %collective-permute-start.5 = (bf16[1024,128]{1,0:T(8,128)(2,1)S(1)}, bf16[1024,128]{1,0:T(8,128)(2,1)S(1)}, u32[]{:S(2)}, u32[]{:S(2)}) collective-permute-start(bf16[1024,128]{1,0:T(8,128)(2,1)S(1)} %broadcast_select_fusion.16), channel_id=1, source_target_pairs={{0,8},{1,9},{2,10},{3,11},{4,12},{5,13},{6,14},{7,15},{8,0},{9,1},... | collective-permute-start | bytes 786440 | tf_op jit(solution)/shard_map/ppermute | solution.py:77
  40.0 7.7 %collective-permute-start.6 = (bf16[1024,128]{1,0:T(8,128)(2,1)S(1)}, bf16[1024,128]{1,0:T(8,128)(2,1)S(1)}, u32[]{:S(2)}, u32[]{:S(2)}) collective-permute-start(bf16[1024,128]{1,0:T(8,128)(2,1)S(1)} %broadcast_select_fusion.15), channel_id=1, source_target_pairs={{0,2},{1,3},{2,0},{3,1},{4,6},{5,7},{6,4},{7,5},{8,10},{9,11},{10,... | collective-permute-start | bytes 786440 | tf_op jit(solution)/shard_map/ppermute | solution.py:65
  49.0 12.8 %collective-permute-start.7 = (bf16[1024,128]{1,0:T(8,128)(2,1)S(1)}, bf16[1024,128]{1,0:T(8,128)(2,1)S(1)}, u32[]{:S(2)}, u32[]{:S(2)}) collective-permute-start(bf16[1024,128]{1,0:T(8,128)(2,1)S(1)} %broadcast_select_fusion.13), channel_id=1, source_target_pairs={{0,4},{1,5},{2,6},{3,7},{4,0},{5,1},{6,2},{7,3},{8,12},{9,13},{10,... | collective-permute-start | bytes 786440 | tf_op jit(solution)/shard_map/ppermute | solution.py:68
  49.1 14.2 %collective-permute-start.8 = (bf16[1024,128]{1,0:T(8,128)(2,1)S(1)}, bf16[1024,128]{1,0:T(8,128)(2,1)S(1)}, u32[]{:S(2)}, u32[]{:S(2)}) collective-permute-start(bf16[1024,128]{1,0:T(8,128)(2,1)S(1)} %broadcast_select_fusion.14), channel_id=1, source_target_pairs={{0,8},{1,9},{2,10},{3,11},{4,12},{5,13},{6,14},{7,15},{8,0},{9,1},... | collective-permute-start | bytes 786440 | tf_op jit(solution)/shard_map/ppermute | solution.py:77
  52.0 11.3 %collective-permute-start.9 = (bf16[1024,128]{1,0:T(8,128)(2,1)S(1)}, bf16[1024,128]{1,0:T(8,128)(2,1)S(1)}, u32[]{:S(2)}, u32[]{:S(2)}) collective-permute-start(bf16[1024,128]{1,0:T(8,128)(2,1)S(1)} %broadcast_select_fusion.12), channel_id=1, source_target_pairs={{0,2},{1,3},{2,0},{3,1},{4,6},{5,7},{6,4},{7,5},{8,10},{9,11},{10,... | collective-permute-start | bytes 786440 | tf_op jit(solution)/shard_map/ppermute | solution.py:65
  62.5 1.2 copy-start.1
  63.3 1.3 copy-start
  63.5 18.5 %collective-permute-start.10 = (bf16[1024,256]{1,0:T(8,128)(2,1)S(1)}, bf16[1024,256]{1,0:T(8,128)(2,1)S(1)}, u32[]{:S(2)}, u32[]{:S(2)}) collective-permute-start(bf16[1024,256]{1,0:T(8,128)(2,1)S(1)} %maximum_select_fusion), channel_id=1, source_target_pairs={{0,4},{1,5},{2,6},{3,7},{4,0},{5,1},{6,2},{7,3},{8,12},{9,13},{10,... | collective-permute-start | bytes 1572872 | tf_op jit(solution)/shard_map/ppermute | solution.py:68
  64.7 18.9 %collective-permute-start.12 = (f32[1024,128]{1,0:T(8,128)S(1)}, f32[1024,128]{1,0:T(8,128)S(1)}, u32[]{:S(2)}, u32[]{:S(2)}) collective-permute-start(f32[1024,128]{1,0:T(8,128)S(1)} %convolution_add_fusion.5), channel_id=1, source_target_pairs={{0,2},{1,3},{2,0},{3,1},{4,6},{5,7},{6,4},{7,5},{8,10},{9,11},{10,... | collective-permute-start | bytes 1572872 | tf_op jit(solution)/shard_map/ppermute | solution.py:65
  64.8 18.8 %collective-permute-start.11 = (bf16[1024,128]{1,0:T(8,128)(2,1)S(1)}, bf16[1024,128]{1,0:T(8,128)(2,1)S(1)}, u32[]{:S(2)}, u32[]{:S(2)}) collective-permute-start(bf16[1024,128]{1,0:T(8,128)(2,1)S(1)} %broadcast_select_fusion.11), channel_id=1, source_target_pairs={{0,8},{1,9},{2,10},{3,11},{4,12},{5,13},{6,14},{7,15},{8,0},{9,1},... | collective-permute-start | bytes 786440 | tf_op jit(solution)/shard_map/ppermute | solution.py:77
  67.3 35.8 %collective-permute-start.22 = (bf16[1024,512]{1,0:T(8,128)(2,1)S(1)}, bf16[1024,512]{1,0:T(8,128)(2,1)S(1)}, u32[]{:S(2)}, u32[]{:S(2)}) collective-permute-start(bf16[1024,512]{1,0:T(8,128)(2,1)S(1)} %copy-done), channel_id=1, source_target_pairs={{0,1},{1,0},{2,3},{3,2},{4,5},{5,4},{6,7},{7,6},{8,9},{9,8},{10,11... | collective-permute-start | bytes 3145736 | tf_op jit(solution)/shard_map/ppermute | solution.py:71
  67.3 47.7 %collective-permute-start.16 = (bf16[1024,256]{1,0:T(8,128)(2,1)S(1)}, bf16[1024,256]{1,0:T(8,128)(2,1)S(1)}, u32[]{:S(2)}, u32[]{:S(2)}) collective-permute-start(bf16[1024,256]{1,0:T(8,128)(2,1)S(1)} %slice.94), channel_id=1, source_target_pairs={{0,8},{1,9},{4,12},{5,13},{10,2},{11,3},{14,6},{15,7},{16,24},{17,... | collective-permute-start | bytes 1572872 | tf_op jit(solution)/shard_map/ppermute | solution.py:74
  82.7 1.0 copy-start.3
  83.7 9.2 %collective-permute-start.19 = (bf16[1024,128]{1,0:T(8,128)(2,1)S(1)}, bf16[1024,128]{1,0:T(8,128)(2,1)S(1)}, u32[]{:S(2)}, u32[]{:S(2)}) collective-permute-start(bf16[1024,128]{1,0:T(8,128)(2,1)S(1)} %copy-done.3), channel_id=1, source_target_pairs={{0,2},{1,3},{2,0},{3,1},{4,6},{5,7},{6,4},{7,5},{8,10},{9,11},{10,... | collective-permute-start | bytes 786440 | tf_op jit(solution)/shard_map/ppermute | solution.py:65
  83.9 18.4 %collective-permute-start.13 = (bf16[1024,256]{1,0:T(8,128)(2,1)S(1)}, bf16[1024,256]{1,0:T(8,128)(2,1)S(1)}, u32[]{:S(2)}, u32[]{:S(2)}) collective-permute-start(bf16[1024,256]{1,0:T(8,128)(2,1)S(1)} %maximum_select_fusion.1), channel_id=1, source_target_pairs={{0,4},{1,5},{2,6},{3,7},{4,0},{5,1},{6,2},{7,3},{8,12},{9,13},{10,... | collective-permute-start | bytes 1572872 | tf_op jit(solution)/shard_map/ppermute | solution.py:68
  84.0 17.5 %collective-permute-start.14 = (f32[1024,128]{1,0:T(8,128)S(1)}, f32[1024,128]{1,0:T(8,128)S(1)}, u32[]{:S(2)}, u32[]{:S(2)}) collective-permute-start(f32[1024,128]{1,0:T(8,128)S(1)} %convolution_add_fusion.4), channel_id=1, source_target_pairs={{0,2},{1,3},{2,0},{3,1},{4,6},{5,7},{6,4},{7,5},{8,10},{9,11},{10,... | collective-permute-start | bytes 1572872 | tf_op jit(solution)/shard_map/ppermute | solution.py:65
  93.3 23.4 %collective-permute-start.20 = (bf16[1024,512]{1,0:T(8,128)(2,1)S(1)}, bf16[1024,512]{1,0:T(8,128)(2,1)S(1)}, u32[]{:S(2)}, u32[]{:S(2)}) collective-permute-start(bf16[1024,512]{1,0:T(8,128)(2,1)S(1)} %pad_maximum_fusion.2), channel_id=1, source_target_pairs={{0,1},{1,0},{2,3},{3,2},{4,5},{5,4},{6,7},{7,6},{8,9},{9,8},{10,11... | collective-permute-start | bytes 3145736 | tf_op jit(solution)/shard_map/ppermute | solution.py:71
  101.4 11.0 %collective-permute-start.15 = (f32[1024,128]{1,0:T(8,128)S(1)}, f32[1024,128]{1,0:T(8,128)S(1)}, u32[]{:S(2)}, u32[]{:S(2)}) collective-permute-start(f32[1024,128]{1,0:T(8,128)S(1)} %convolution_add_fusion.3), channel_id=1, source_target_pairs={{0,2},{1,3},{2,0},{3,1},{4,6},{5,7},{6,4},{7,5},{8,10},{9,11},{10,... | collective-permute-start | bytes 1572872 | tf_op jit(solution)/shard_map/ppermute | solution.py:65
  113.4 4.8 %collective-permute-start.18 = (bf16[1024,512]{1,0:T(8,128)(2,1)S(1)}, bf16[1024,512]{1,0:T(8,128)(2,1)S(1)}, u32[]{:S(2)}, u32[]{:S(2)}) collective-permute-start(bf16[1024,512]{1,0:T(8,128)(2,1)S(1)} %get-tuple-element.111), channel_id=1, source_target_pairs={{0,1},{1,0},{2,3},{3,2},{4,5},{5,4},{6,7},{7,6},{8,9},{9,8},{10,11... | collective-permute-start | bytes 3145736 | tf_op jit(solution)/shard_map/ppermute | solution.py:71
  114.4 2.4 %collective-permute-start.21 = (bf16[1024,256]{1,0:T(8,128)(2,1)S(1)}, bf16[1024,256]{1,0:T(8,128)(2,1)S(1)}, u32[]{:S(2)}, u32[]{:S(2)}) collective-permute-start(bf16[1024,256]{1,0:T(8,128)(2,1)S(1)} %get-tuple-element.128), channel_id=1, source_target_pairs={{0,1},{1,0},{2,3},{3,2},{4,5},{5,4},{6,7},{7,6},{8,9},{9,8},{10,11... | collective-permute-start | bytes 1572872 | tf_op jit(solution)/shard_map/ppermute | solution.py:71
  115.1 13.9 %collective-permute-start.17 = (bf16[1024,256]{1,0:T(8,128)(2,1)S(1)}, bf16[1024,256]{1,0:T(8,128)(2,1)S(1)}, u32[]{:S(2)}, u32[]{:S(2)}) collective-permute-start(bf16[1024,256]{1,0:T(8,128)(2,1)S(1)} %broadcast_select_fusion.8), channel_id=1, source_target_pairs={{0,4},{1,5},{2,6},{3,7},{4,0},{5,1},{6,2},{7,3},{8,12},{9,13},{10,... | collective-permute-start | bytes 1572872 | tf_op jit(solution)/shard_map/ppermute | solution.py:68
  115.2 19.2 %collective-permute-start.23 = (f32[1024,128]{1,0:T(8,128)S(1)}, f32[1024,128]{1,0:T(8,128)S(1)}, u32[]{:S(2)}, u32[]{:S(2)}) collective-permute-start(f32[1024,128]{1,0:T(8,128)S(1)} %convolution_add_fusion.2), channel_id=1, source_target_pairs={{0,2},{1,3},{2,0},{3,1},{4,6},{5,7},{6,4},{7,5},{8,10},{9,11},{10,... | collective-permute-start | bytes 1572872 | tf_op jit(solution)/shard_map/ppermute | solution.py:65
  129.1 2.0 %collective-permute-start.24 = (bf16[1024,256]{1,0:T(8,128)(2,1)S(1)}, bf16[1024,256]{1,0:T(8,128)(2,1)S(1)}, u32[]{:S(2)}, u32[]{:S(2)}) collective-permute-start(bf16[1024,256]{1,0:T(8,128)(2,1)S(1)} %get-tuple-element.117), channel_id=1, source_target_pairs={{0,1},{1,0},{2,3},{3,2},{4,5},{5,4},{6,7},{7,6},{8,9},{9,8},{10,11... | collective-permute-start | bytes 1572872 | tf_op jit(solution)/shard_map/ppermute | solution.py:71

commit v10 on v9

--- a/solution.py
+++ b/solution.py
@@ -113,6 +113,7 @@
         near, far = together((j1, v[0]), x2, t_near)
         x3 = cross(jnp.where(home, near, far))
         sum0 = adjoint_of(b0, b0_next)
+        part0 = cross(after(sum0, x3))
         near, far = together((e[0], x3))
         third = jnp.where(home, near, far)
         j3 = jump(third)
@@ -121,19 +122,18 @@
         b1_next = step(b1)
         near, far = together((j2, v[1]), third, sum0)
         x4 = cross(jnp.where(home, near, far))
-        part0 = cross(after(sum0, x4))
         near, far = together((e[1], x4))
         j4 = jump(jnp.where(home, near, far))
         sum1 = adjoint_of(b1, b1_next)
         part1 = cross(after(sum1, part0))
-        v_across3 = cross(after(v[3], part0))
-        near, both, far = together((e[0], j3, x3), sum1, x4)
+        v_across3 = cross(after(v[3], part1))
+        near, both, far = together((e[0], j3, x3), sum1, x4, part0)
         a0b2 = jnp.where(home, jnp.concatenate([near, both], 1), jnp.concatenate([both, far], 1))
         a0b2_next = step(a0b2)
         sum2 = adjoint_of(columns(a0b2, 1, 2), columns(a0b2_next, 1, 2))
         part2 = cross(after(sum2, part1))
         j5 = home_jump(after(columns(expected_cot, 2, 4), j3))
-        near, both, far = together((e[1], j4, x4), sum2, part0)
+        near, both, far = together((e[1], j4, x4), sum2)
         a1b3 = jnp.where(home, jnp.concatenate([near, both], 1), jnp.concatenate([both, far], 1))
         a1b3_next = step(a1b3)
         v_other = swap(after(value_next, sum1))
@@ -148,11 +148,11 @@
             [jnp.where(home, parts[2], parts[0]), jnp.where(home, parts[3], parts[1]), parts[4], parts[5]], 1
         )
         v_across_other = swap(v_across)
-        near, far = together((columns(expected_cot, 2, 4), j5), a1b3_next, part2)
+        near, far = together((columns(expected_cot, 2, 4), j5), a1b3_next, part1)
         a23 = jnp.where(home, near, far)
         a23_next = step(a23)
         b0, b0_next, b1, b1_next, a0b2, a0b2_next = together(
-            (b0, b0_next, b1, b1_next, a0b2, a0b2_next), a1b3_next, sum3, part2
+            (b0, b0_next, b1, b1_next, a0b2, a0b2_next), a1b3_next, sum3, part2, a23
         )
         a0, a0_next = columns(a0b2, 0, 1), columns(a0b2_next, 0, 1)
         a1, a1_next = columns(a1b3, 0, 1), columns(a1b3_next, 0, 1)

time: 136 us -> 133 us (0.978)
  waiting for transfers between devices: 79.7 us -> 68 us
  starting transfers between devices: 25.7 us -> 34.9 us
    ppermute x5, waiting for transfers between devices: 33.2 us -> 20.5 us  [step(): return lax.ppermute(a, AXES, step_pairs)]
    ppermute x9, starting transfers between devices: 7.43 us -> 12.9 us  [cross(): return lax.ppermute(a, AXES, cross_pairs)]
    ppermute x5, starting transfers between devices: 1.06 us -> 4.7 us  [step(): return lax.ppermute(a, AXES, step_pairs)]
  transfers between devices with their start and end apart: 25 -> 25, of which waited for: 14 -> 13; matrix products, arithmetic and copies ran while one was open for 20% -> 20% of each run, Pallas kernels for 0% -> 0%
where the time goes in v10:
time: 133 us
  waiting for transfers between devices  68 us (51%)
  starting transfers between devices  34.9 us (26%)
  matrix products  16 us (12%)
  other arithmetic  10.6 us (8%)
  local copies, waits for them, and re-layouts  1.83 us (1%)
  between operations  1.73 us (1%)
    ppermute x9, waiting for transfers between devices, cross(): return lax.ppermute(a, AXES, cross_pairs)  44 us
    ppermute x5, waiting for transfers between devices, step(): return lax.ppermute(a, AXES, step_pairs)  20.5 us
    ppermute x9, starting transfers between devices, cross(): return lax.ppermute(a, AXES, cross_pairs)  12.9 us
    ppermute x4, starting transfers between devices, jump(): return lax.ppermute(a, AXES, jump_pairs)  12.6 us
    dot_general x12, matrix products, tdot(): lax.dot_general(a, b, (((0,), (0,)), ((), ())), preferred_element_type=jn...  9.01 us
    dot_general x3, matrix products, dott(): lax.dot_general(a, b, (((1,), (1,)), ((), ())), preferred_element_type=jn...  6.95 us
    ppermute x5, starting transfers between devices, step(): return lax.ppermute(a, AXES, step_pairs)  4.7 us
    ppermute x1, starting transfers between devices, home_jump(): return lax.ppermute(a, AXES, home_jump_pairs)  3.38 us
  transfers between devices with their start and end apart: 25, of which 13 were waited for; matrix products, arithmetic and copies ran while one was open for 20% of the time, Pallas kernels for 0%

profile of v10, /device:TPU:0, one launch (start us, length us, event | category | flops | bytes accessed | tf_op | source)
XLA Modules:
  0.0 133.1 jit_solution(1885257922839093214)
XLA Ops:
  0.6 0.5 collective-permute-start
  1.1 2.5 %fusion.35 = (bf16[1024,128]{1,0:T(8,128)(2,1)}, bf16[1024,128]{1,0:T(8,128)(2,1)S(1)}, bf16[1024,128]{1,0:T(8,128)(2,1)}, bf16[1024,128]{1,0:T(8,128)(2,1)S(1)}...) fusion(bf16[1024,512]{1,0:T(8,128)(2,1)} %param.5, ...), kind=kLoop, calls=%fused_computation.75 | loop fusion | flops 131072 | bytes 4456449 | tf_op jit(solution)/shard_map/slice | solution.py:88
  3.7 2.5 %collective-permute-start.1 = (bf16[1024,128]{1,0:T(8,128)(2,1)S(1)}, bf16[1024,128]{1,0:T(8,128)(2,1)S(1)}, u32[]{:S(2)}, u32[]{:S(2)}) collective-permute-start(bf16[1024,128]{1,0:T(8,128)(2,1)S(1)} %get-tuple-element.119), channel_id=1, source_target_pairs={{0,2},{1,3},{2,0},{3,1},{4,6},{5,7},{6,4},{7,5},{8,10},{9,11},{10,... | collective-permute-start | bytes 786440 | tf_op jit(solution)/shard_map/ppermute | solution.py:65
  6.2 6.9 %collective-permute-done.1 = bf16[1024,128]{1,0:T(8,128)(2,1)S(1)} collective-permute-done((bf16[1024,128]{1,0:T(8,128)(2,1)S(1)}, bf16[1024,128]{1,0:T(8,128)(2,1)S(1)}, u32[]{:S(2)}, u32[]{:S(2)}) %collective-permute-start.1) | collective-permute-done | bytes 262176 | tf_op jit(solution)/shard_map/ppermute | solution.py:65
  13.2 0.9 pad_maximum_fusion.3
  14.0 1.7 %collective-permute-start.3 = (bf16[1024,256]{1,0:T(8,128)(2,1)}, bf16[1024,256]{1,0:T(8,128)(2,1)}, u32[]{:S(2)}, u32[]{:S(2)}) collective-permute-start(bf16[1024,256]{1,0:T(8,128)(2,1)} %pad_maximum_fusion.3), channel_id=1, source_target_pairs={{0,2},{1,3},{2,0},{3,1},{4,6},{5,7},{6,4},{7,5},{8,10},{9,11},{10,... | collective-permute-start | bytes 1572872 | tf_op jit(solution)/shard_map/ppermute | solution.py:65
  15.8 0.7 broadcast_select_fusion.19
  16.5 2.6 %collective-permute-start.2 = (bf16[1024,128]{1,0:T(8,128)(2,1)}, bf16[1024,128]{1,0:T(8,128)(2,1)}, u32[]{:S(2)}, u32[]{:S(2)}) collective-permute-start(bf16[1024,128]{1,0:T(8,128)(2,1)} %broadcast_select_fusion.19), channel_id=1, source_target_pairs={{0,8},{1,9},{2,10},{3,11},{4,12},{5,13},{6,14},{7,15},{8,0},{9,1},... | collective-permute-start | bytes 786440 | tf_op jit(solution)/shard_map/ppermute | solution.py:77
  19.1 9.0 %collective-permute-done.3 = bf16[1024,256]{1,0:T(8,128)(2,1)} collective-permute-done((bf16[1024,256]{1,0:T(8,128)(2,1)}, bf16[1024,256]{1,0:T(8,128)(2,1)}, u32[]{:S(2)}, u32[]{:S(2)}) %collective-permute-start.3) | collective-permute-done | bytes 524320 | tf_op jit(solution)/shard_map/ppermute | solution.py:65
  28.1 1.1 fusion.40
  29.1 1.8 %collective-permute-done.2 = bf16[1024,128]{1,0:T(8,128)(2,1)} collective-permute-done((bf16[1024,128]{1,0:T(8,128)(2,1)}, bf16[1024,128]{1,0:T(8,128)(2,1)}, u32[]{:S(2)}, u32[]{:S(2)}) %collective-permute-start.2) | collective-permute-done | bytes 262176 | tf_op jit(solution)/shard_map/ppermute | solution.py:77
  31.0 0.7 collective-permute-start.4
  31.8 5.3 %collective-permute-start.5 = (bf16[1024,128]{1,0:T(8,128)(2,1)S(1)}, bf16[1024,128]{1,0:T(8,128)(2,1)S(1)}, u32[]{:S(2)}, u32[]{:S(2)}) collective-permute-start(bf16[1024,128]{1,0:T(8,128)(2,1)S(1)} %broadcast_select_fusion.16), channel_id=1, source_target_pairs={{0,8},{1,9},{2,10},{3,11},{4,12},{5,13},{6,14},{7,15},{8,0},{9,1},... | collective-permute-start | bytes 786440 | tf_op jit(solution)/shard_map/ppermute | solution.py:77
  37.1 1.9 %broadcast_select_fusion.1 = (bf16[1024,1024]{1,0:T(8,128)(2,1)S(1)}, bf16[1024,1024]{1,0:T(8,128)(2,1)S(1)}) fusion(bf16[1024,1024]{1,0:T(8,128)(2,1)S(1)} %copy-done.2, bf16[1024,1024]{1,0:T(8,128)(2,1)} %collective-permute-done, pred[]{:T(512)S(6)} %eq.8), kind=kLoop, calls=%fused_computation.8 | loop fusion | flops 2097152 | bytes 8388609 | tf_op jit(solution)/shard_map/jit(_where)/select_n | solution.py:103
  39.0 1.0 broadcast_select_fusion.15
  40.0 2.2 %collective-permute-done.4 = bf16[1024,128]{1,0:T(8,128)(2,1)S(1)} collective-permute-done((bf16[1024,128]{1,0:T(8,128)(2,1)S(1)}, bf16[1024,128]{1,0:T(8,128)(2,1)S(1)}, u32[]{:S(2)}, u32[]{:S(2)}) %collective-permute-start.4) | collective-permute-done | bytes 262176 | tf_op jit(solution)/shard_map/ppermute | solution.py:68
  42.3 0.7 fusion.41
  43.0 0.8 convolution_add_fusion.5
  43.8 3.9 %collective-permute-done.6 = bf16[1024,128]{1,0:T(8,128)(2,1)S(1)} collective-permute-done((bf16[1024,128]{1,0:T(8,128)(2,1)S(1)}, bf16[1024,128]{1,0:T(8,128)(2,1)S(1)}, u32[]{:S(2)}, u32[]{:S(2)}) %collective-permute-start.6) | collective-permute-done | bytes 262176 | tf_op jit(solution)/shard_map/ppermute | solution.py:65
  47.7 1.2 collective-permute-done.5
  49.1 2.9 %collective-permute-start.8 = (bf16[1024,128]{1,0:T(8,128)(2,1)S(1)}, bf16[1024,128]{1,0:T(8,128)(2,1)S(1)}, u32[]{:S(2)}, u32[]{:S(2)}) collective-permute-start(bf16[1024,128]{1,0:T(8,128)(2,1)S(1)} %broadcast_select_fusion.14), channel_id=1, source_target_pairs={{0,8},{1,9},{2,10},{3,11},{4,12},{5,13},{6,14},{7,15},{8,0},{9,1},... | collective-permute-start | bytes 786440 | tf_op jit(solution)/shard_map/ppermute | solution.py:77
  52.0 2.1 %collective-permute-start.9 = (bf16[1024,128]{1,0:T(8,128)(2,1)S(1)}, bf16[1024,128]{1,0:T(8,128)(2,1)S(1)}, u32[]{:S(2)}, u32[]{:S(2)}) collective-permute-start(bf16[1024,128]{1,0:T(8,128)(2,1)S(1)} %broadcast_select_fusion.12), channel_id=1, source_target_pairs={{0,2},{1,3},{2,0},{3,1},{4,6},{5,7},{6,4},{7,5},{8,10},{9,11},{10,... | collective-permute-start | bytes 786440 | tf_op jit(solution)/shard_map/ppermute | solution.py:65
  54.1 7.6 %collective-permute-done.7 = bf16[1024,128]{1,0:T(8,128)(2,1)S(1)} collective-permute-done((bf16[1024,128]{1,0:T(8,128)(2,1)S(1)}, bf16[1024,128]{1,0:T(8,128)(2,1)S(1)}, u32[]{:S(2)}, u32[]{:S(2)}) %collective-permute-start.7) | collective-permute-done | bytes 262176 | tf_op jit(solution)/shard_map/ppermute | solution.py:68
  61.8 0.7 fusion.42
  62.5 0.8 convolution_add_fusion.4
  63.3 6.8 %collective-permute-done.9 = bf16[1024,128]{1,0:T(8,128)(2,1)S(1)} collective-permute-done((bf16[1024,128]{1,0:T(8,128)(2,1)S(1)}, bf16[1024,128]{1,0:T(8,128)(2,1)S(1)}, u32[]{:S(2)}, u32[]{:S(2)}) %collective-permute-start.9) | collective-permute-done | bytes 262176 | tf_op jit(solution)/shard_map/ppermute | solution.py:65
  70.1 0.2 maximum_select_fusion
  70.2 0.4 collective-permute-start.11
  71.6 1.7 %collective-permute-start.12 = (bf16[1024,128]{1,0:T(8,128)(2,1)S(1)}, bf16[1024,128]{1,0:T(8,128)(2,1)S(1)}, u32[]{:S(2)}, u32[]{:S(2)}) collective-permute-start(bf16[1024,128]{1,0:T(8,128)(2,1)S(1)} %broadcast_select_fusion.11), channel_id=1, source_target_pairs={{0,8},{1,9},{2,10},{3,11},{4,12},{5,13},{6,14},{7,15},{8,0},{9,1},... | collective-permute-start | bytes 786440 | tf_op jit(solution)/shard_map/ppermute | solution.py:77
  73.3 3.4 %collective-permute-start.16 = (bf16[1024,256]{1,0:T(8,128)(2,1)S(1)}, bf16[1024,256]{1,0:T(8,128)(2,1)S(1)}, u32[]{:S(2)}, u32[]{:S(2)}) collective-permute-start(bf16[1024,256]{1,0:T(8,128)(2,1)S(1)} %slice.90), channel_id=1, source_target_pairs={{0,8},{1,9},{4,12},{5,13},{10,2},{11,3},{14,6},{15,7},{16,24},{17,... | collective-permute-start | bytes 1572872 | tf_op jit(solution)/shard_map/ppermute | solution.py:74
  76.8 10.7 %collective-permute-done.11 = bf16[1024,256]{1,0:T(8,128)(2,1)S(1)} collective-permute-done((bf16[1024,256]{1,0:T(8,128)(2,1)S(1)}, bf16[1024,256]{1,0:T(8,128)(2,1)S(1)}, u32[]{:S(2)}, u32[]{:S(2)}) %collective-permute-start.11) | collective-permute-done | bytes 524320 | tf_op jit(solution)/shard_map/ppermute | solution.py:68
  87.4 0.8 fusion.21
  88.2 0.8 convolution_add_fusion.3
  89.0 1.5 %collective-permute-done.14 = f32[1024,128]{1,0:T(8,128)S(1)} collective-permute-done((f32[1024,128]{1,0:T(8,128)S(1)}, f32[1024,128]{1,0:T(8,128)S(1)}, u32[]{:S(2)}, u32[]{:S(2)}) %collective-permute-start.14) | collective-permute-done | bytes 524320 | tf_op jit(solution)/shard_map/ppermute | solution.py:65
  90.5 0.3 collective-permute-start.15
  90.8 0.2 maximum_select_fusion.1
  91.0 1.7 %collective-permute-start.13 = (bf16[1024,256]{1,0:T(8,128)(2,1)S(1)}, bf16[1024,256]{1,0:T(8,128)(2,1)S(1)}, u32[]{:S(2)}, u32[]{:S(2)}) collective-permute-start(bf16[1024,256]{1,0:T(8,128)(2,1)S(1)} %maximum_select_fusion.1), channel_id=1, source_target_pairs={{0,4},{1,5},{2,6},{3,7},{4,0},{5,1},{6,2},{7,3},{8,12},{9,13},{10,... | collective-permute-start | bytes 1572872 | tf_op jit(solution)/shard_map/ppermute | solution.py:68
  92.7 1.7 %collective-permute-start.19 = (bf16[1024,128]{1,0:T(8,128)(2,1)S(1)}, bf16[1024,128]{1,0:T(8,128)(2,1)S(1)}, u32[]{:S(2)}, u32[]{:S(2)}) collective-permute-start(bf16[1024,128]{1,0:T(8,128)(2,1)S(1)} %copy-done.3), channel_id=1, source_target_pairs={{0,2},{1,3},{2,0},{3,1},{4,6},{5,7},{6,4},{7,5},{8,10},{9,11},{10,... | collective-permute-start | bytes 786440 | tf_op jit(solution)/shard_map/ppermute | solution.py:65
  94.6 14.4 %collective-permute-done.19 = bf16[1024,128]{1,0:T(8,128)(2,1)S(1)} collective-permute-done((bf16[1024,128]{1,0:T(8,128)(2,1)S(1)}, bf16[1024,128]{1,0:T(8,128)(2,1)S(1)}, u32[]{:S(2)}, u32[]{:S(2)}) %collective-permute-start.19) | collective-permute-done | bytes 262176 | tf_op jit(solution)/shard_map/ppermute | solution.py:65
  109.1 0.1 constant_dynamic-update-slice_fusion.4
  109.1 0.1 constant_dynamic-update-slice_fusion.3
  109.3 0.1 pad_maximum_fusion.2
  109.5 0.1 constant_dynamic-update-slice_fusion.2
  109.6 0.1 constant_dynamic-update-slice_fusion.1
  109.8 1.7 %collective-permute-start.17 = (bf16[1024,256]{1,0:T(8,128)(2,1)S(1)}, bf16[1024,256]{1,0:T(8,128)(2,1)S(1)}, u32[]{:S(2)}, u32[]{:S(2)}) collective-permute-start(bf16[1024,256]{1,0:T(8,128)(2,1)S(1)} %broadcast_select_fusion.8), channel_id=1, source_target_pairs={{0,4},{1,5},{2,6},{3,7},{4,0},{5,1},{6,2},{7,3},{8,12},{9,13},{10,... | collective-permute-start | bytes 1572872 | tf_op jit(solution)/shard_map/ppermute | solution.py:68
  111.5 0.8 fusion.30
  112.2 0.8 convolution_add_fusion.2
  113.0 0.2 fusion.36
  113.3 0.8 broadcast_select_fusion.3
  114.0 0.3 collective-permute-start.18
  114.3 0.2 broadcast_select_fusion.7
  114.6 0.4 collective-permute-start.21
  114.9 4.4 %collective-permute-start.23 = (f32[1024,128]{1,0:T(8,128)S(1)}, f32[1024,128]{1,0:T(8,128)S(1)}, u32[]{:S(2)}, u32[]{:S(2)}) collective-permute-start(f32[1024,128]{1,0:T(8,128)S(1)} %convolution_add_fusion.2), channel_id=1, source_target_pairs={{0,2},{1,3},{2,0},{3,1},{4,6},{5,7},{6,4},{7,5},{8,10},{9,11},{10,... | collective-permute-start | bytes 1572872 | tf_op jit(solution)/shard_map/ppermute | solution.py:65
  119.3 0.7 fusion.24
  120.0 0.8 convolution_add_fusion.1
  120.8 1.3 fusion.8
  122.1 0.1 constant_dynamic-update-slice_fusion
  122.2 2.4 %fusion.5 = f32[1024,1024]{1,0:T(8,128)S(1)} fusion(f32[1024,1024]{1,0:T(8,128)S(1)} %fusion.8, bf16[1024,1024]{1,0:T(8,128)(2,1)S(1)} %constant_dynamic-update-slice_fusion, bf16[1024,512]{1,0:T(8,128)(2,1)S(1)} %collective-permute-done.18, bf16[1024,512]{1,0:T(8,128)(2,1)S(1)} %get-tuple-element.110), kind=kOutput, calls=%fused_computation.9 | convolution fusion | flops 2152726528 | bytes 12582912 | tf_op jit(solution)/shard_map/dot_general | solution.py:38
  124.8 0.7 fusion.43
  125.5 0.7 convolution_add_fusion
  126.3 0.4 collective-permute-done.24
  126.7 3.3 %add_multiply_fusion = f32[1024,1024]{1,0:T(8,128)} fusion(f32[1024,1024]{1,0:T(8,128)S(1)} %fusion.5, f32[]{:T(128)} %bitcast, bf16[1024,256]{1,0:T(8,128)(2,1)S(1)} %collective-permute-done.24, bf16[1024,256]{1,0:T(8,128)(2,1)S(1)} %get-tuple-element.116, bf16[1024,256]{1,0:T(8,128)(2,1)S(1)} %get-tuple-element.114, bf16[1024,256]{1,0:T(8,128)(2,1)S(1)} %get-tuple-element.112), kind=kOutput, calls=%fused_computation | convolution fusion | flops 1080033280 | bytes 10485764 | tf_op jit(solution)/shard_map/dot_general | solution.py:38
  130.0 1.4 %collective-permute-done.23 = f32[1024,128]{1,0:T(8,128)S(1)} collective-permute-done((f32[1024,128]{1,0:T(8,128)S(1)}, f32[1024,128]{1,0:T(8,128)S(1)}, u32[]{:S(2)}, u32[]{:S(2)}) %collective-permute-start.23) | collective-permute-done | bytes 524320 | tf_op jit(solution)/shard_map/ppermute | solution.py:65
  131.4 1.6 %fusion.4 = f32[1024,512]{1,0:T(8,128)} fusion(f32[1024,256]{1,0:T(8,128)S(1)} %convolution_add_fusion, f32[1024,256]{1,0:T(8,128)S(1)} %convolution_add_fusion.1, f32[1024,128]{1,0:T(8,128)S(1)} %collective-permute-done.23, f32[1024,128]{1,0:T(8,128)S(1)} %collective-permute-done.15, f32[1024,128]{1,0:T(8,128)S(1)} %collective-permute-done.14, ...), kind=kLoop, calls=%fused_computation.6 | loop fusion | flops 3145728 | bytes 6291460 | tf_op jit(solution)/shard_map/mul | solution.py:181
  (41 shorter events, 1.1 us)
Async XLA Ops:
  0.6 36.5 %collective-permute-start = (bf16[1024,1024]{1,0:T(8,128)(2,1)}, bf16[1024,1024]{1,0:T(8,128)(2,1)}, u32[]{:S(2)}, u32[]{:S(2)}) collective-permute-start(bf16[1024,1024]{1,0:T(8,128)(2,1)} %param.6), channel_id=1, source_target_pairs={{0,1},{1,0},{2,3},{3,2},{4,5},{5,4},{6,7},{7,6},{8,9},{9,8},{10,11... | collective-permute-start | bytes 6291464 | tf_op jit(solution)/shard_map/ppermute | solution.py:71
  3.7 9.5 %collective-permute-start.1 = (bf16[1024,128]{1,0:T(8,128)(2,1)S(1)}, bf16[1024,128]{1,0:T(8,128)(2,1)S(1)}, u32[]{:S(2)}, u32[]{:S(2)}) collective-permute-start(bf16[1024,128]{1,0:T(8,128)(2,1)S(1)} %get-tuple-element.119), channel_id=1, source_target_pairs={{0,2},{1,3},{2,0},{3,1},{4,6},{5,7},{6,4},{7,5},{8,10},{9,11},{10,... | collective-permute-start | bytes 786440 | tf_op jit(solution)/shard_map/ppermute | solution.py:65
  13.2 23.9 %copy-start.2 = (bf16[1024,1024]{1,0:T(8,128)(2,1)S(1)}, bf16[1024,1024]{1,0:T(8,128)(2,1)}, u32[]{:S(2)}) copy-start(bf16[1024,1024]{1,0:T(8,128)(2,1)} %param.6) | copy-start | bytes 6291460
  14.0 14.0 %collective-permute-start.3 = (bf16[1024,256]{1,0:T(8,128)(2,1)}, bf16[1024,256]{1,0:T(8,128)(2,1)}, u32[]{:S(2)}, u32[]{:S(2)}) collective-permute-start(bf16[1024,256]{1,0:T(8,128)(2,1)} %pad_maximum_fusion.3), channel_id=1, source_target_pairs={{0,2},{1,3},{2,0},{3,1},{4,6},{5,7},{6,4},{7,5},{8,10},{9,11},{10,... | collective-permute-start | bytes 1572872 | tf_op jit(solution)/shard_map/ppermute | solution.py:65
  16.5 14.4 %collective-permute-start.2 = (bf16[1024,128]{1,0:T(8,128)(2,1)}, bf16[1024,128]{1,0:T(8,128)(2,1)}, u32[]{:S(2)}, u32[]{:S(2)}) collective-permute-start(bf16[1024,128]{1,0:T(8,128)(2,1)} %broadcast_select_fusion.19), channel_id=1, source_target_pairs={{0,8},{1,9},{2,10},{3,11},{4,12},{5,13},{6,14},{7,15},{8,0},{9,1},... | collective-permute-start | bytes 786440 | tf_op jit(solution)/shard_map/ppermute | solution.py:77
  31.0 11.3 %collective-permute-start.4 = (bf16[1024,128]{1,0:T(8,128)(2,1)S(1)}, bf16[1024,128]{1,0:T(8,128)(2,1)S(1)}, u32[]{:S(2)}, u32[]{:S(2)}) collective-permute-start(bf16[1024,128]{1,0:T(8,128)(2,1)S(1)} %broadcast_select_fusion.17), channel_id=1, source_target_pairs={{0,4},{1,5},{2,6},{3,7},{4,0},{5,1},{6,2},{7,3},{8,12},{9,13},{10,... | collective-permute-start | bytes 786440 | tf_op jit(solution)/shard_map/ppermute | solution.py:68
  31.8 17.2 %collective-permute-start.5 = (bf16[1024,128]{1,0:T(8,128)(2,1)S(1)}, bf16[1024,128]{1,0:T(8,128)(2,1)S(1)}, u32[]{:S(2)}, u32[]{:S(2)}) collective-permute-start(bf16[1024,128]{1,0:T(8,128)(2,1)S(1)} %broadcast_select_fusion.16), channel_id=1, source_target_pairs={{0,8},{1,9},{2,10},{3,11},{4,12},{5,13},{6,14},{7,15},{8,0},{9,1},... | collective-permute-start | bytes 786440 | tf_op jit(solution)/shard_map/ppermute | solution.py:77
  40.0 7.7 %collective-permute-start.6 = (bf16[1024,128]{1,0:T(8,128)(2,1)S(1)}, bf16[1024,128]{1,0:T(8,128)(2,1)S(1)}, u32[]{:S(2)}, u32[]{:S(2)}) collective-permute-start(bf16[1024,128]{1,0:T(8,128)(2,1)S(1)} %broadcast_select_fusion.15), channel_id=1, source_target_pairs={{0,2},{1,3},{2,0},{3,1},{4,6},{5,7},{6,4},{7,5},{8,10},{9,11},{10,... | collective-permute-start | bytes 786440 | tf_op jit(solution)/shard_map/ppermute | solution.py:65
  49.0 12.8 %collective-permute-start.7 = (bf16[1024,128]{1,0:T(8,128)(2,1)S(1)}, bf16[1024,128]{1,0:T(8,128)(2,1)S(1)}, u32[]{:S(2)}, u32[]{:S(2)}) collective-permute-start(bf16[1024,128]{1,0:T(8,128)(2,1)S(1)} %broadcast_select_fusion.13), channel_id=1, source_target_pairs={{0,4},{1,5},{2,6},{3,7},{4,0},{5,1},{6,2},{7,3},{8,12},{9,13},{10,... | collective-permute-start | bytes 786440 | tf_op jit(solution)/shard_map/ppermute | solution.py:68
  49.1 21.0 %collective-permute-start.8 = (bf16[1024,128]{1,0:T(8,128)(2,1)S(1)}, bf16[1024,128]{1,0:T(8,128)(2,1)S(1)}, u32[]{:S(2)}, u32[]{:S(2)}) collective-permute-start(bf16[1024,128]{1,0:T(8,128)(2,1)S(1)} %broadcast_select_fusion.14), channel_id=1, source_target_pairs={{0,8},{1,9},{2,10},{3,11},{4,12},{5,13},{6,14},{7,15},{8,0},{9,1},... | collective-permute-start | bytes 786440 | tf_op jit(solution)/shard_map/ppermute | solution.py:77
  52.0 18.1 %collective-permute-start.10 = (f32[1024,128]{1,0:T(8,128)S(1)}, f32[1024,128]{1,0:T(8,128)S(1)}, u32[]{:S(2)}, u32[]{:S(2)}) collective-permute-start(f32[1024,128]{1,0:T(8,128)S(1)} %convolution_add_fusion.5), channel_id=1, source_target_pairs={{0,2},{1,3},{2,0},{3,1},{4,6},{5,7},{6,4},{7,5},{8,10},{9,11},{10,... | collective-permute-start | bytes 1572872 | tf_op jit(solution)/shard_map/ppermute | solution.py:65
  52.0 18.0 %collective-permute-start.9 = (bf16[1024,128]{1,0:T(8,128)(2,1)S(1)}, bf16[1024,128]{1,0:T(8,128)(2,1)S(1)}, u32[]{:S(2)}, u32[]{:S(2)}) collective-permute-start(bf16[1024,128]{1,0:T(8,128)(2,1)S(1)} %broadcast_select_fusion.12), channel_id=1, source_target_pairs={{0,2},{1,3},{2,0},{3,1},{4,6},{5,7},{6,4},{7,5},{8,10},{9,11},{10,... | collective-permute-start | bytes 786440 | tf_op jit(solution)/shard_map/ppermute | solution.py:65
  62.5 8.2 %copy-start.1 = (bf16[1024,512]{1,0:T(8,128)(2,1)S(1)}, bf16[1024,512]{1,0:T(8,128)(2,1)}, u32[]{:S(2)}) copy-start(bf16[1024,512]{1,0:T(8,128)(2,1)} %param.4) | copy-start | bytes 3145732
  63.3 8.1 %copy-start = (bf16[1024,512]{1,0:T(8,128)(2,1)S(1)}, bf16[1024,512]{1,0:T(8,128)(2,1)}, u32[]{:S(2)}) copy-start(bf16[1024,512]{1,0:T(8,128)(2,1)} %param.5) | copy-start | bytes 3145732
  70.2 17.2 %collective-permute-start.11 = (bf16[1024,256]{1,0:T(8,128)(2,1)S(1)}, bf16[1024,256]{1,0:T(8,128)(2,1)S(1)}, u32[]{:S(2)}, u32[]{:S(2)}) collective-permute-start(bf16[1024,256]{1,0:T(8,128)(2,1)S(1)} %maximum_select_fusion), channel_id=1, source_target_pairs={{0,4},{1,5},{2,6},{3,7},{4,0},{5,1},{6,2},{7,3},{8,12},{9,13},{10,... | collective-permute-start | bytes 1572872 | tf_op jit(solution)/shard_map/ppermute | solution.py:68
  71.5 23.0 %collective-permute-start.22 = (bf16[1024,512]{1,0:T(8,128)(2,1)S(1)}, bf16[1024,512]{1,0:T(8,128)(2,1)S(1)}, u32[]{:S(2)}, u32[]{:S(2)}) collective-permute-start(bf16[1024,512]{1,0:T(8,128)(2,1)S(1)} %copy-done), channel_id=1, source_target_pairs={{0,1},{1,0},{2,3},{3,2},{4,5},{5,4},{6,7},{7,6},{8,9},{9,8},{10,11... | collective-permute-start | bytes 3145736 | tf_op jit(solution)/shard_map/ppermute | solution.py:71
  71.6 19.2 %collective-permute-start.12 = (bf16[1024,128]{1,0:T(8,128)(2,1)S(1)}, bf16[1024,128]{1,0:T(8,128)(2,1)S(1)}, u32[]{:S(2)}, u32[]{:S(2)}) collective-permute-start(bf16[1024,128]{1,0:T(8,128)(2,1)S(1)} %broadcast_select_fusion.11), channel_id=1, source_target_pairs={{0,8},{1,9},{2,10},{3,11},{4,12},{5,13},{6,14},{7,15},{8,0},{9,1},... | collective-permute-start | bytes 786440 | tf_op jit(solution)/shard_map/ppermute | solution.py:77
  73.3 36.3 %collective-permute-start.16 = (bf16[1024,256]{1,0:T(8,128)(2,1)S(1)}, bf16[1024,256]{1,0:T(8,128)(2,1)S(1)}, u32[]{:S(2)}, u32[]{:S(2)}) collective-permute-start(bf16[1024,256]{1,0:T(8,128)(2,1)S(1)} %slice.90), channel_id=1, source_target_pairs={{0,8},{1,9},{4,12},{5,13},{10,2},{11,3},{14,6},{15,7},{16,24},{17,... | collective-permute-start | bytes 1572872 | tf_op jit(solution)/shard_map/ppermute | solution.py:74
  76.7 13.8 %collective-permute-start.14 = (f32[1024,128]{1,0:T(8,128)S(1)}, f32[1024,128]{1,0:T(8,128)S(1)}, u32[]{:S(2)}, u32[]{:S(2)}) collective-permute-start(f32[1024,128]{1,0:T(8,128)S(1)} %convolution_add_fusion.4), channel_id=1, source_target_pairs={{0,2},{1,3},{2,0},{3,1},{4,6},{5,7},{6,4},{7,5},{8,10},{9,11},{10,... | collective-permute-start | bytes 1572872 | tf_op jit(solution)/shard_map/ppermute | solution.py:65
  88.2 4.5 %copy-start.3 = (bf16[1024,128]{1,0:T(8,128)(2,1)S(1)}, bf16[1024,128]{1,0:T(8,128)(2,1)}, u32[]{:S(2)}) copy-start(bf16[1024,128]{1,0:T(8,128)(2,1)} %get-tuple-element.90) | copy-start | bytes 786436
  90.5 22.5 %collective-permute-start.15 = (f32[1024,128]{1,0:T(8,128)S(1)}, f32[1024,128]{1,0:T(8,128)S(1)}, u32[]{:S(2)}, u32[]{:S(2)}) collective-permute-start(f32[1024,128]{1,0:T(8,128)S(1)} %convolution_add_fusion.3), channel_id=1, source_target_pairs={{0,2},{1,3},{2,0},{3,1},{4,6},{5,7},{6,4},{7,5},{8,10},{9,11},{10,... | collective-permute-start | bytes 1572872 | tf_op jit(solution)/shard_map/ppermute | solution.py:65
  91.0 18.7 %collective-permute-start.13 = (bf16[1024,256]{1,0:T(8,128)(2,1)S(1)}, bf16[1024,256]{1,0:T(8,128)(2,1)S(1)}, u32[]{:S(2)}, u32[]{:S(2)}) collective-permute-start(bf16[1024,256]{1,0:T(8,128)(2,1)S(1)} %maximum_select_fusion.1), channel_id=1, source_target_pairs={{0,4},{1,5},{2,6},{3,7},{4,0},{5,1},{6,2},{7,3},{8,12},{9,13},{10,... | collective-permute-start | bytes 1572872 | tf_op jit(solution)/shard_map/ppermute | solution.py:68
  92.7 16.3 %collective-permute-start.19 = (bf16[1024,128]{1,0:T(8,128)(2,1)S(1)}, bf16[1024,128]{1,0:T(8,128)(2,1)S(1)}, u32[]{:S(2)}, u32[]{:S(2)}) collective-permute-start(bf16[1024,128]{1,0:T(8,128)(2,1)S(1)} %copy-done.3), channel_id=1, source_target_pairs={{0,2},{1,3},{2,0},{3,1},{4,6},{5,7},{6,4},{7,5},{8,10},{9,11},{10,... | collective-permute-start | bytes 786440 | tf_op jit(solution)/shard_map/ppermute | solution.py:65
  109.4 12.7 %collective-permute-start.20 = (bf16[1024,512]{1,0:T(8,128)(2,1)S(1)}, bf16[1024,512]{1,0:T(8,128)(2,1)S(1)}, u32[]{:S(2)}, u32[]{:S(2)}) collective-permute-start(bf16[1024,512]{1,0:T(8,128)(2,1)S(1)} %pad_maximum_fusion.2), channel_id=1, source_target_pairs={{0,1},{1,0},{2,3},{3,2},{4,5},{5,4},{6,7},{7,6},{8,9},{9,8},{10,11... | collective-permute-start | bytes 3145736 | tf_op jit(solution)/shard_map/ppermute | solution.py:71
  109.8 14.9 %collective-permute-start.17 = (bf16[1024,256]{1,0:T(8,128)(2,1)S(1)}, bf16[1024,256]{1,0:T(8,128)(2,1)S(1)}, u32[]{:S(2)}, u32[]{:S(2)}) collective-permute-start(bf16[1024,256]{1,0:T(8,128)(2,1)S(1)} %broadcast_select_fusion.8), channel_id=1, source_target_pairs={{0,4},{1,5},{2,6},{3,7},{4,0},{5,1},{6,2},{7,3},{8,12},{9,13},{10,... | collective-permute-start | bytes 1572872 | tf_op jit(solution)/shard_map/ppermute | solution.py:68
  114.0 8.2 %collective-permute-start.18 = (bf16[1024,512]{1,0:T(8,128)(2,1)S(1)}, bf16[1024,512]{1,0:T(8,128)(2,1)S(1)}, u32[]{:S(2)}, u32[]{:S(2)}) collective-permute-start(bf16[1024,512]{1,0:T(8,128)(2,1)S(1)} %get-tuple-element.111), channel_id=1, source_target_pairs={{0,1},{1,0},{2,3},{3,2},{4,5},{5,4},{6,7},{7,6},{8,9},{9,8},{10,11... | collective-permute-start | bytes 3145736 | tf_op jit(solution)/shard_map/ppermute | solution.py:71
  114.6 6.2 %collective-permute-start.21 = (bf16[1024,256]{1,0:T(8,128)(2,1)S(1)}, bf16[1024,256]{1,0:T(8,128)(2,1)S(1)}, u32[]{:S(2)}, u32[]{:S(2)}) collective-permute-start(bf16[1024,256]{1,0:T(8,128)(2,1)S(1)} %get-tuple-element.128), channel_id=1, source_target_pairs={{0,1},{1,0},{2,3},{3,2},{4,5},{5,4},{6,7},{7,6},{8,9},{9,8},{10,11... | collective-permute-start | bytes 1572872 | tf_op jit(solution)/shard_map/ppermute | solution.py:71
  114.9 16.5 %collective-permute-start.23 = (f32[1024,128]{1,0:T(8,128)S(1)}, f32[1024,128]{1,0:T(8,128)S(1)}, u32[]{:S(2)}, u32[]{:S(2)}) collective-permute-start(f32[1024,128]{1,0:T(8,128)S(1)} %convolution_add_fusion.2), channel_id=1, source_target_pairs={{0,2},{1,3},{2,0},{3,1},{4,6},{5,7},{6,4},{7,5},{8,10},{9,11},{10,... | collective-permute-start | bytes 1572872 | tf_op jit(solution)/shard_map/ppermute | solution.py:65
  124.7 2.0 %collective-permute-start.24 = (bf16[1024,256]{1,0:T(8,128)(2,1)S(1)}, bf16[1024,256]{1,0:T(8,128)(2,1)S(1)}, u32[]{:S(2)}, u32[]{:S(2)}) collective-permute-start(bf16[1024,256]{1,0:T(8,128)(2,1)S(1)} %get-tuple-element.117), channel_id=1, source_target_pairs={{0,1},{1,0},{2,3},{3,2},{4,5},{5,4},{6,7},{7,6},{8,9},{9,8},{10,11... | collective-permute-start | bytes 1572872 | tf_op jit(solution)/shard_map/ppermute | solution.py:71

commit v11 on v10

--- a/solution.py
+++ b/solution.py
@@ -96,44 +96,42 @@
         t_other = swap(transition)
         e2 = after(e[2], x1)
         j1 = jump(jnp.where(home, x1, e2))
-        v1, e1 = together((v[1], e[1]), x1)
-        x2 = cross(jnp.concatenate([jnp.where(home, v1, e1), v[2]], 1))
-        x2, v_across2 = columns(x2, 0, 1), columns(x2, 1, 2)
-        t, t_o = together((transition, t_other), x1)
-        t_near, t_next = jnp.where(mine, t, t_o), jnp.where(mine, t_o, t)
+        t_near, t_next = jnp.where(mine, transition, t_other), jnp.where(mine, t_other, transition)
 
         def adjoint_of(near, far):
             return tdot(t_near, near) + tdot(t_next, far)
 
-        near, far = together((x1, j1), x2)
+        v1, e1 = together((v[1], e[1]), x1, t_near)
+        x2 = cross(jnp.concatenate([jnp.where(home, v1, e1), v[2], v[3]], 1))
+        x2, v_across2, v_across3 = columns(x2, 0, 1), columns(x2, 1, 2), columns(x2, 2, 3)
+        second = jnp.where(home, x2, e[3])
+        j2 = jump(second)
+        near, far = together((j1, v[0]), second)
+        third_cross = jnp.where(home, near, far)
+        x3 = cross(third_cross)
+        near, far = together((x1, j1), third_cross)
         b0 = jnp.where(home, near, far)
         b0_next = step(b0)
-        near, far = together((x2, e[3]))
-        j2 = jump(jnp.where(home, near, far))
-        near, far = together((j1, v[0]), x2, t_near)
-        x3 = cross(jnp.where(home, near, far))
+        third = jnp.where(home, e[0], x3)
+        j3 = jump(third)
         sum0 = adjoint_of(b0, b0_next)
-        part0 = cross(after(sum0, x3))
-        near, far = together((e[0], x3))
-        third = jnp.where(home, near, far)
-        j3 = jump(third)
+        near, far = together((j2, v[1]), third)
+        x4 = cross(jnp.where(home, near, far))
         near, far = together((x2, j2), sum0, third)
         b1 = jnp.where(home, near, far)
         b1_next = step(b1)
-        near, far = together((j2, v[1]), third, sum0)
-        x4 = cross(jnp.where(home, near, far))
-        near, far = together((e[1], x4))
-        j4 = jump(jnp.where(home, near, far))
+        part0 = cross(after(sum0, x4))
+        fourth = jnp.where(home, e[1], x4)
+        j4 = jump(fourth)
         sum1 = adjoint_of(b1, b1_next)
         part1 = cross(after(sum1, part0))
-        v_across3 = cross(after(v[3], part1))
-        near, both, far = together((e[0], j3, x3), sum1, x4, part0)
+        near, both, far = together((e[0], j3, x3), sum1, fourth)
         a0b2 = jnp.where(home, jnp.concatenate([near, both], 1), jnp.concatenate([both, far], 1))
         a0b2_next = step(a0b2)
         sum2 = adjoint_of(columns(a0b2, 1, 2), columns(a0b2_next, 1, 2))
         part2 = cross(after(sum2, part1))
         j5 = home_jump(after(columns(expected_cot, 2, 4), j3))
-        near, both, far = together((e[1], j4, x4), sum2)
+        near, both, far = together((e[1], j4, x4), sum2, part0)
         a1b3 = jnp.where(home, jnp.concatenate([near, both], 1), jnp.concatenate([both, far], 1))
         a1b3_next = step(a1b3)
         v_other = swap(after(value_next, sum1))

time: 133 us -> 122 us (0.917); the launches traced: 133 us -> 120 us
  waiting for transfers between devices: 68 us -> 58.5 us
  other arithmetic: 10.6 us -> 7.43 us
    ppermute x9 -> x8, waiting for transfers between devices: 44 us -> 25.4 us  [cross(): return lax.ppermute(a, AXES, cross_pairs)]
    ppermute x5, starting transfers between devices: 4.7 us -> 9.98 us  [step(): return lax.ppermute(a, AXES, step_pairs)]
    ppermute x1, waiting for transfers between devices: 0.01 us -> 4.96 us  [home_jump(): return lax.ppermute(a, AXES, home_jump_pairs)]
    ppermute x9 -> x8, starting transfers between devices: 12.9 us -> 8.89 us  [cross(): return lax.ppermute(a, AXES, cross_pairs)]
    ppermute x4, waiting for transfers between devices: 3.06 us -> 5.85 us  [jump(): return lax.ppermute(a, AXES, jump_pairs)]
    ppermute x4, starting transfers between devices: 12.6 us -> 10.9 us  [jump(): return lax.ppermute(a, AXES, jump_pairs)]
    unnamed x10 -> x8, local copies, waits for them, and re-layouts: 0.19 us -> 1.68 us
    ppermute x5, waiting for transfers between devices: 20.5 us -> 21.9 us  [step(): return lax.ppermute(a, AXES, step_pairs)]
  transfers between devices with their start and end apart: 25 -> 24, of which waited for: 13 -> 13; matrix products, arithmetic and copies ran while one was open for 20% -> 19% of each run, Pallas kernels for 0% -> 0%
where the time goes in v11:
time: 122 us; the launch traced here: 120 us
  waiting for transfers between devices  58.5 us (48%)
  starting transfers between devices  33.8 us (28%)
  matrix products  16 us (13%)
  other arithmetic  7.43 us (6%)
  local copies, waits for them, and re-layouts  2.26 us (2%)
  between operations  1.73 us (1%)
    ppermute x8, waiting for transfers between devices, cross(): return lax.ppermute(a, AXES, cross_pairs)  25.4 us
    ppermute x5, waiting for transfers between devices, step(): return lax.ppermute(a, AXES, step_pairs)  21.9 us
    ppermute x4, starting transfers between devices, jump(): return lax.ppermute(a, AXES, jump_pairs)  10.9 us
    ppermute x5, starting transfers between devices, step(): return lax.ppermute(a, AXES, step_pairs)  9.98 us
    dot_general x12, matrix products, tdot(): lax.dot_general(a, b, (((0,), (0,)), ((), ())), preferred_element_type=jn...  9.03 us
    ppermute x8, starting transfers between devices, cross(): return lax.ppermute(a, AXES, cross_pairs)  8.89 us
    dot_general x3, matrix products, dott(): lax.dot_general(a, b, (((1,), (1,)), ((), ())), preferred_element_type=jn...  6.94 us
    ppermute x4, waiting for transfers between devices, jump(): return lax.ppermute(a, AXES, jump_pairs)  5.85 us
  transfers between devices with their start and end apart: 24, of which 13 were waited for; matrix products, arithmetic and copies ran while one was open for 19% of the time, Pallas kernels for 0%

profile of v11, /device:TPU:0, one launch (start us, length us, event | category | flops | bytes accessed | tf_op | source)
XLA Modules:
  0.0 119.7 jit_solution(1378587150960288484)
XLA Ops:
  0.6 0.5 collective-permute-start
  1.2 1.4 %fusion.35 = (bf16[1024,128]{1,0:T(8,128)(2,1)S(1)}, bf16[1024,128]{1,0:T(8,128)(2,1)S(1)}, bf16[1024,128]{1,0:T(8,128)(2,1)S(1)}, bf16[1024,128]{1,0:T(8,128)(2...) fusion(bf16[1024,512]{1,0:T(8,128)(2,1)} %param.4, bf16[1024,512]{1,0:T(8,128)(2,1)} %param.5, ...), kind=kLoop, calls=%fused_computation.75 | loop fusion | flops 131072 | bytes 2883585 | tf_op jit(solution)/shard_map/slice | solution.py:88
  2.6 2.7 %collective-permute-start.1 = (bf16[1024,128]{1,0:T(8,128)(2,1)S(1)}, bf16[1024,128]{1,0:T(8,128)(2,1)S(1)}, u32[]{:S(2)}, u32[]{:S(2)}) collective-permute-start(bf16[1024,128]{1,0:T(8,128)(2,1)S(1)} %get-tuple-element.103), channel_id=1, source_target_pairs={{0,2},{1,3},{2,0},{3,1},{4,6},{5,7},{6,4},{7,5},{8,10},{9,11},{10,... | collective-permute-start | bytes 786440 | tf_op jit(solution)/shard_map/ppermute | solution.py:65
  5.3 1.5 %copy-done.2 = bf16[1024,1024]{1,0:T(8,128)(2,1)S(1)} copy-done((bf16[1024,1024]{1,0:T(8,128)(2,1)S(1)}, bf16[1024,1024]{1,0:T(8,128)(2,1)}, u32[]{:S(2)}) %copy-start.2) | copy-done | bytes 2097176
  6.8 2.1 %broadcast_select_fusion.1 = (bf16[1024,1024]{1,0:T(8,128)(2,1)S(1)}, bf16[1024,1024]{1,0:T(8,128)(2,1)S(1)}) fusion(bf16[1024,1024]{1,0:T(8,128)(2,1)S(1)} %copy-done.2, bf16[1024,1024]{1,0:T(8,128)(2,1)} %collective-permute-done, pred[]{:T(512)S(6)} %eq.8), kind=kLoop, calls=%fused_computation.8 | loop fusion | flops 2097152 | bytes 8388609 | tf_op jit(solution)/shard_map/jit(_where)/select_n | solution.py:99
  9.0 3.1 %collective-permute-done.1 = bf16[1024,128]{1,0:T(8,128)(2,1)S(1)} collective-permute-done((bf16[1024,128]{1,0:T(8,128)(2,1)S(1)}, bf16[1024,128]{1,0:T(8,128)(2,1)S(1)}, u32[]{:S(2)}, u32[]{:S(2)}) %collective-permute-start.1) | collective-permute-done | bytes 262176 | tf_op jit(solution)/shard_map/ppermute | solution.py:65
  12.1 0.1 pad_maximum_fusion.3
  12.2 1.8 %collective-permute-start.3 = (bf16[1024,384]{1,0:T(8,128)(2,1)S(1)}, bf16[1024,384]{1,0:T(8,128)(2,1)S(1)}, u32[]{:S(2)}, u32[]{:S(2)}) collective-permute-start(bf16[1024,384]{1,0:T(8,128)(2,1)S(1)} %pad_maximum_fusion.3), channel_id=1, source_target_pairs={{0,2},{1,3},{2,0},{3,1},{4,6},{5,7},{6,4},{7,5},{8,10},{9,11},{10,... | collective-permute-start | bytes 2359304 | tf_op jit(solution)/shard_map/ppermute | solution.py:65
  14.1 2.7 %collective-permute-start.2 = (bf16[1024,128]{1,0:T(8,128)(2,1)S(1)}, bf16[1024,128]{1,0:T(8,128)(2,1)S(1)}, u32[]{:S(2)}, u32[]{:S(2)}) collective-permute-start(bf16[1024,128]{1,0:T(8,128)(2,1)S(1)} %broadcast_select_fusion.18), channel_id=1, source_target_pairs={{0,8},{1,9},{2,10},{3,11},{4,12},{5,13},{6,14},{7,15},{8,0},{9,1},... | collective-permute-start | bytes 786440 | tf_op jit(solution)/shard_map/ppermute | solution.py:77
  16.8 14.8 %collective-permute-done.3 = bf16[1024,384]{1,0:T(8,128)(2,1)S(1)} collective-permute-done((bf16[1024,384]{1,0:T(8,128)(2,1)S(1)}, bf16[1024,384]{1,0:T(8,128)(2,1)S(1)}, u32[]{:S(2)}, u32[]{:S(2)}) %collective-permute-start.3) | collective-permute-done | bytes 786464 | tf_op jit(solution)/shard_map/ppermute | solution.py:65
  31.7 1.7 %collective-permute-start.4 = (bf16[1024,128]{1,0:T(8,128)(2,1)S(1)}, bf16[1024,128]{1,0:T(8,128)(2,1)S(1)}, u32[]{:S(2)}, u32[]{:S(2)}) collective-permute-start(bf16[1024,128]{1,0:T(8,128)(2,1)S(1)} %broadcast_select_fusion.15), channel_id=1, source_target_pairs={{0,4},{1,5},{2,6},{3,7},{4,0},{5,1},{6,2},{7,3},{8,12},{9,13},{10,... | collective-permute-start | bytes 786440 | tf_op jit(solution)/shard_map/ppermute | solution.py:68
  33.5 1.5 %collective-permute-start.6 = (bf16[1024,128]{1,0:T(8,128)(2,1)S(1)}, bf16[1024,128]{1,0:T(8,128)(2,1)S(1)}, u32[]{:S(2)}, u32[]{:S(2)}) collective-permute-start(bf16[1024,128]{1,0:T(8,128)(2,1)S(1)} %broadcast_select_fusion.16), channel_id=1, source_target_pairs={{0,2},{1,3},{2,0},{3,1},{4,6},{5,7},{6,4},{7,5},{8,10},{9,11},{10,... | collective-permute-start | bytes 786440 | tf_op jit(solution)/shard_map/ppermute | solution.py:65
  35.0 2.6 %collective-permute-start.5 = (bf16[1024,128]{1,0:T(8,128)(2,1)S(1)}, bf16[1024,128]{1,0:T(8,128)(2,1)S(1)}, u32[]{:S(2)}, u32[]{:S(2)}) collective-permute-start(bf16[1024,128]{1,0:T(8,128)(2,1)S(1)} %get-tuple-element.109), channel_id=1, source_target_pairs={{0,8},{1,9},{2,10},{3,11},{4,12},{5,13},{6,14},{7,15},{8,0},{9,1},... | collective-permute-start | bytes 786440 | tf_op jit(solution)/shard_map/ppermute | solution.py:77
  37.6 5.6 %collective-permute-done.4 = bf16[1024,128]{1,0:T(8,128)(2,1)S(1)} collective-permute-done((bf16[1024,128]{1,0:T(8,128)(2,1)S(1)}, bf16[1024,128]{1,0:T(8,128)(2,1)S(1)}, u32[]{:S(2)}, u32[]{:S(2)}) %collective-permute-start.4) | collective-permute-done | bytes 262176 | tf_op jit(solution)/shard_map/ppermute | solution.py:68
  43.2 0.7 fusion.41
  43.9 0.8 convolution_add_fusion.5
  44.7 3.3 %collective-permute-done.5 = bf16[1024,128]{1,0:T(8,128)(2,1)S(1)} collective-permute-done((bf16[1024,128]{1,0:T(8,128)(2,1)S(1)}, bf16[1024,128]{1,0:T(8,128)(2,1)S(1)}, u32[]{:S(2)}, u32[]{:S(2)}) %collective-permute-start.5) | collective-permute-done | bytes 262176 | tf_op jit(solution)/shard_map/ppermute | solution.py:77
  48.0 0.5 collective-permute-start.9
  48.6 0.3 collective-permute-start.7
  48.8 2.8 %collective-permute-start.8 = (bf16[1024,128]{1,0:T(8,128)(2,1)S(1)}, bf16[1024,128]{1,0:T(8,128)(2,1)S(1)}, u32[]{:S(2)}, u32[]{:S(2)}) collective-permute-start(bf16[1024,128]{1,0:T(8,128)(2,1)S(1)} %broadcast_select_fusion.14), channel_id=1, source_target_pairs={{0,8},{1,9},{2,10},{3,11},{4,12},{5,13},{6,14},{7,15},{8,0},{9,1},... | collective-permute-start | bytes 786440 | tf_op jit(solution)/shard_map/ppermute | solution.py:77
  51.7 5.6 %collective-permute-done.9 = bf16[1024,128]{1,0:T(8,128)(2,1)S(1)} collective-permute-done((bf16[1024,128]{1,0:T(8,128)(2,1)S(1)}, bf16[1024,128]{1,0:T(8,128)(2,1)S(1)}, u32[]{:S(2)}, u32[]{:S(2)}) %collective-permute-start.9) | collective-permute-done | bytes 262176 | tf_op jit(solution)/shard_map/ppermute | solution.py:65
  57.3 1.6 %collective-permute-done.7 = bf16[1024,128]{1,0:T(8,128)(2,1)S(1)} collective-permute-done((bf16[1024,128]{1,0:T(8,128)(2,1)S(1)}, bf16[1024,128]{1,0:T(8,128)(2,1)S(1)}, u32[]{:S(2)}, u32[]{:S(2)}) %collective-permute-start.7) | collective-permute-done | bytes 262176 | tf_op jit(solution)/shard_map/ppermute | solution.py:68
  58.8 0.7 fusion.42
  59.6 0.8 convolution_add_fusion.4
  60.4 0.9 collective-permute-done.8
  61.3 0.2 maximum_select_fusion
  61.5 0.3 collective-permute-start.10
  62.6 2.8 %collective-permute-start.11 = (bf16[1024,128]{1,0:T(8,128)(2,1)S(1)}, bf16[1024,128]{1,0:T(8,128)(2,1)S(1)}, u32[]{:S(2)}, u32[]{:S(2)}) collective-permute-start(bf16[1024,128]{1,0:T(8,128)(2,1)S(1)} %broadcast_select_fusion.11), channel_id=1, source_target_pairs={{0,8},{1,9},{2,10},{3,11},{4,12},{5,13},{6,14},{7,15},{8,0},{9,1},... | collective-permute-start | bytes 786440 | tf_op jit(solution)/shard_map/ppermute | solution.py:77
  65.3 2.3 %collective-permute-start.16 = (bf16[1024,256]{1,0:T(8,128)(2,1)S(1)}, bf16[1024,256]{1,0:T(8,128)(2,1)S(1)}, u32[]{:S(2)}, u32[]{:S(2)}) collective-permute-start(bf16[1024,256]{1,0:T(8,128)(2,1)S(1)} %slice.90), channel_id=1, source_target_pairs={{0,8},{1,9},{4,12},{5,13},{10,2},{11,3},{14,6},{15,7},{16,24},{17,... | collective-permute-start | bytes 1572872 | tf_op jit(solution)/shard_map/ppermute | solution.py:74
  67.7 0.1 constant_dynamic-update-slice_fusion.4
  67.8 0.1 constant_dynamic-update-slice_fusion.3
  67.9 0.8 collective-permute-start.14
  68.7 7.9 %collective-permute-done.10 = bf16[1024,256]{1,0:T(8,128)(2,1)S(1)} collective-permute-done((bf16[1024,256]{1,0:T(8,128)(2,1)S(1)}, bf16[1024,256]{1,0:T(8,128)(2,1)S(1)}, u32[]{:S(2)}, u32[]{:S(2)}) %collective-permute-start.10) | collective-permute-done | bytes 524320 | tf_op jit(solution)/shard_map/ppermute | solution.py:68
  76.7 0.8 fusion.21
  77.4 0.8 convolution_add_fusion.3
  78.2 1.7 %collective-permute-done.11 = bf16[1024,128]{1,0:T(8,128)(2,1)S(1)} collective-permute-done((bf16[1024,128]{1,0:T(8,128)(2,1)S(1)}, bf16[1024,128]{1,0:T(8,128)(2,1)S(1)}, u32[]{:S(2)}, u32[]{:S(2)}) %collective-permute-start.11) | collective-permute-done | bytes 262176 | tf_op jit(solution)/shard_map/ppermute | solution.py:77
  79.9 0.2 maximum_select_fusion.1
  80.0 5.1 %collective-permute-start.13 = (bf16[1024,256]{1,0:T(8,128)(2,1)S(1)}, bf16[1024,256]{1,0:T(8,128)(2,1)S(1)}, u32[]{:S(2)}, u32[]{:S(2)}) collective-permute-start(bf16[1024,256]{1,0:T(8,128)(2,1)S(1)} %maximum_select_fusion.1), channel_id=1, source_target_pairs={{0,4},{1,5},{2,6},{3,7},{4,0},{5,1},{6,2},{7,3},{8,12},{9,13},{10,... | collective-permute-start | bytes 1572872 | tf_op jit(solution)/shard_map/ppermute | solution.py:68
  85.1 0.1 pad_maximum_fusion.2
  85.3 0.5 collective-permute-start.21
  85.8 0.1 constant_dynamic-update-slice_fusion.2
  85.9 0.1 constant_dynamic-update-slice_fusion.1
  86.2 5.0 %collective-permute-done.16 = bf16[1024,256]{1,0:T(8,128)(2,1)S(1)} collective-permute-done((bf16[1024,256]{1,0:T(8,128)(2,1)S(1)}, bf16[1024,256]{1,0:T(8,128)(2,1)S(1)}, u32[]{:S(2)}, u32[]{:S(2)}) %collective-permute-start.16) | collective-permute-done | bytes 524320 | tf_op jit(solution)/shard_map/ppermute | solution.py:74
  91.1 6.8 %collective-permute-done.13 = bf16[1024,256]{1,0:T(8,128)(2,1)S(1)} collective-permute-done((bf16[1024,256]{1,0:T(8,128)(2,1)S(1)}, bf16[1024,256]{1,0:T(8,128)(2,1)S(1)}, u32[]{:S(2)}, u32[]{:S(2)}) %collective-permute-start.13) | collective-permute-done | bytes 524320 | tf_op jit(solution)/shard_map/ppermute | solution.py:68
  97.9 0.8 fusion.30
  98.6 0.8 convolution_add_fusion.2
  99.5 2.6 %collective-permute-start.17 = (bf16[1024,256]{1,0:T(8,128)(2,1)S(1)}, bf16[1024,256]{1,0:T(8,128)(2,1)S(1)}, u32[]{:S(2)}, u32[]{:S(2)}) collective-permute-start(bf16[1024,256]{1,0:T(8,128)(2,1)S(1)} %broadcast_select_fusion.8), channel_id=1, source_target_pairs={{0,4},{1,5},{2,6},{3,7},{4,0},{5,1},{6,2},{7,3},{8,12},{9,13},{10,... | collective-permute-start | bytes 1572872 | tf_op jit(solution)/shard_map/ppermute | solution.py:68
  102.2 0.2 fusion.37
  102.4 0.8 broadcast_select_fusion.3
  103.2 0.1 constant_dynamic-update-slice_fusion
  103.4 0.2 broadcast_select_fusion.7
  103.7 0.6 collective-permute-start.20
  104.2 1.5 %collective-permute-start.22 = (f32[1024,128]{1,0:T(8,128)S(1)}, f32[1024,128]{1,0:T(8,128)S(1)}, u32[]{:S(2)}, u32[]{:S(2)}) collective-permute-start(f32[1024,128]{1,0:T(8,128)S(1)} %convolution_add_fusion.2), channel_id=1, source_target_pairs={{0,2},{1,3},{2,0},{3,1},{4,6},{5,7},{6,4},{7,5},{8,10},{9,11},{10,... | collective-permute-start | bytes 1572872 | tf_op jit(solution)/shard_map/ppermute | solution.py:65
  105.7 0.7 fusion.24
  106.4 0.7 convolution_add_fusion.1
  107.2 1.3 %fusion.8 = f32[1024,1024]{1,0:T(8,128)S(1)} fusion(bf16[1024,256]{1,0:T(8,128)(2,1)S(1)} %collective-permute-done.20, bf16[1024,256]{1,0:T(8,128)(2,1)S(1)} %get-tuple-element.100, bf16[1024,256]{1,0:T(8,128)(2,1)S(1)} %get-tuple-element.95, bf16[1024,256]{1,0:T(8,128)(2,1)S(1)} %get-tuple-element.98), kind=kOutput, calls=%fused_computation.19 | convolution fusion | flops 1077936128 | bytes 6291456 | tf_op jit(solution)/shard_map/dot_general | solution.py:38
  108.5 2.4 %fusion.5 = f32[1024,1024]{1,0:T(8,128)S(1)} fusion(f32[1024,1024]{1,0:T(8,128)S(1)} %fusion.8, bf16[1024,1024]{1,0:T(8,128)(2,1)S(1)} %constant_dynamic-update-slice_fusion, bf16[1024,512]{1,0:T(8,128)(2,1)S(1)} %collective-permute-done.18, bf16[1024,512]{1,0:T(8,128)(2,1)S(1)} %get-tuple-element.92), kind=kOutput, calls=%fused_computation.9 | convolution fusion | flops 2152726528 | bytes 12582912 | tf_op jit(solution)/shard_map/dot_general | solution.py:38
  110.9 0.1 broadcast_select_fusion.5
  111.0 0.7 fusion.43
  111.8 0.7 convolution_add_fusion
  112.5 0.4 collective-permute-done.23
  112.9 3.3 %add_multiply_fusion = f32[1024,1024]{1,0:T(8,128)} fusion(f32[1024,1024]{1,0:T(8,128)S(1)} %fusion.5, f32[]{:T(128)} %bitcast, bf16[1024,256]{1,0:T(8,128)(2,1)S(1)} %collective-permute-done.23, bf16[1024,256]{1,0:T(8,128)(2,1)S(1)} %get-tuple-element.96, bf16[1024,256]{1,0:T(8,128)(2,1)S(1)} %get-tuple-element.94, bf16[1024,256]{1,0:T(8,128)(2,1)S(1)} %get-tuple-element.99), kind=kOutput, calls=%fused_computation | convolution fusion | flops 1080033280 | bytes 10485764 | tf_op jit(solution)/shard_map/dot_general | solution.py:38
  116.2 1.9 %collective-permute-done.22 = f32[1024,128]{1,0:T(8,128)S(1)} collective-permute-done((f32[1024,128]{1,0:T(8,128)S(1)}, f32[1024,128]{1,0:T(8,128)S(1)}, u32[]{:S(2)}, u32[]{:S(2)}) %collective-permute-start.22) | collective-permute-done | bytes 524320 | tf_op jit(solution)/shard_map/ppermute | solution.py:65
  118.1 1.6 %fusion.4 = f32[1024,512]{1,0:T(8,128)} fusion(f32[1024,256]{1,0:T(8,128)S(1)} %convolution_add_fusion, f32[1024,256]{1,0:T(8,128)S(1)} %convolution_add_fusion.1, f32[1024,128]{1,0:T(8,128)S(1)} %collective-permute-done.22, f32[1024,128]{1,0:T(8,128)S(1)} %collective-permute-done.15, f32[1024,128]{1,0:T(8,128)S(1)} %collective-permute-done.14, ...), kind=kLoop, calls=%fused_computation.6 | loop fusion | flops 3145728 | bytes 6291460 | tf_op jit(solution)/shard_map/mul | solution.py:179
  (36 shorter events, 1.0 us)
Async XLA Ops:
  0.6 4.6 %copy-start.1 = (bf16[1024,512]{1,0:T(8,128)(2,1)S(1)}, bf16[1024,512]{1,0:T(8,128)(2,1)}, u32[]{:S(2)}) copy-start(bf16[1024,512]{1,0:T(8,128)(2,1)} %param.5) | copy-start | bytes 3145732
  0.6 4.7 %collective-permute-start = (bf16[1024,1024]{1,0:T(8,128)(2,1)}, bf16[1024,1024]{1,0:T(8,128)(2,1)}, u32[]{:S(2)}, u32[]{:S(2)}) collective-permute-start(bf16[1024,1024]{1,0:T(8,128)(2,1)} %param.6), channel_id=1, source_target_pairs={{0,1},{1,0},{2,3},{3,2},{4,5},{5,4},{6,7},{7,6},{8,9},{9,8},{10,11... | collective-permute-start | bytes 6291464 | tf_op jit(solution)/shard_map/ppermute | solution.py:71
  2.6 9.5 %collective-permute-start.1 = (bf16[1024,128]{1,0:T(8,128)(2,1)S(1)}, bf16[1024,128]{1,0:T(8,128)(2,1)S(1)}, u32[]{:S(2)}, u32[]{:S(2)}) collective-permute-start(bf16[1024,128]{1,0:T(8,128)(2,1)S(1)} %get-tuple-element.103), channel_id=1, source_target_pairs={{0,2},{1,3},{2,0},{3,1},{4,6},{5,7},{6,4},{7,5},{8,10},{9,11},{10,... | collective-permute-start | bytes 786440 | tf_op jit(solution)/shard_map/ppermute | solution.py:65
  5.2 1.6 %copy-start.2 = (bf16[1024,1024]{1,0:T(8,128)(2,1)S(1)}, bf16[1024,1024]{1,0:T(8,128)(2,1)}, u32[]{:S(2)}) copy-start(bf16[1024,1024]{1,0:T(8,128)(2,1)} %param.6) | copy-start | bytes 6291460
  9.0 22.6 %copy-start = (bf16[1024,512]{1,0:T(8,128)(2,1)S(1)}, bf16[1024,512]{1,0:T(8,128)(2,1)}, u32[]{:S(2)}) copy-start(bf16[1024,512]{1,0:T(8,128)(2,1)} %param.4) | copy-start | bytes 3145732
  12.2 19.3 %collective-permute-start.3 = (bf16[1024,384]{1,0:T(8,128)(2,1)S(1)}, bf16[1024,384]{1,0:T(8,128)(2,1)S(1)}, u32[]{:S(2)}, u32[]{:S(2)}) collective-permute-start(bf16[1024,384]{1,0:T(8,128)(2,1)S(1)} %pad_maximum_fusion.3), channel_id=1, source_target_pairs={{0,2},{1,3},{2,0},{3,1},{4,6},{5,7},{6,4},{7,5},{8,10},{9,11},{10,... | collective-permute-start | bytes 2359304 | tf_op jit(solution)/shard_map/ppermute | solution.py:65
  14.1 17.6 %collective-permute-start.2 = (bf16[1024,128]{1,0:T(8,128)(2,1)S(1)}, bf16[1024,128]{1,0:T(8,128)(2,1)S(1)}, u32[]{:S(2)}, u32[]{:S(2)}) collective-permute-start(bf16[1024,128]{1,0:T(8,128)(2,1)S(1)} %broadcast_select_fusion.18), channel_id=1, source_target_pairs={{0,8},{1,9},{2,10},{3,11},{4,12},{5,13},{6,14},{7,15},{8,0},{9,1},... | collective-permute-start | bytes 786440 | tf_op jit(solution)/shard_map/ppermute | solution.py:77
  31.7 11.4 %collective-permute-start.4 = (bf16[1024,128]{1,0:T(8,128)(2,1)S(1)}, bf16[1024,128]{1,0:T(8,128)(2,1)S(1)}, u32[]{:S(2)}, u32[]{:S(2)}) collective-permute-start(bf16[1024,128]{1,0:T(8,128)(2,1)S(1)} %broadcast_select_fusion.15), channel_id=1, source_target_pairs={{0,4},{1,5},{2,6},{3,7},{4,0},{5,1},{6,2},{7,3},{8,12},{9,13},{10,... | collective-permute-start | bytes 786440 | tf_op jit(solution)/shard_map/ppermute | solution.py:68
  33.5 11.2 %collective-permute-start.6 = (bf16[1024,128]{1,0:T(8,128)(2,1)S(1)}, bf16[1024,128]{1,0:T(8,128)(2,1)S(1)}, u32[]{:S(2)}, u32[]{:S(2)}) collective-permute-start(bf16[1024,128]{1,0:T(8,128)(2,1)S(1)} %broadcast_select_fusion.16), channel_id=1, source_target_pairs={{0,2},{1,3},{2,0},{3,1},{4,6},{5,7},{6,4},{7,5},{8,10},{9,11},{10,... | collective-permute-start | bytes 786440 | tf_op jit(solution)/shard_map/ppermute | solution.py:65
  35.0 13.0 %collective-permute-start.5 = (bf16[1024,128]{1,0:T(8,128)(2,1)S(1)}, bf16[1024,128]{1,0:T(8,128)(2,1)S(1)}, u32[]{:S(2)}, u32[]{:S(2)}) collective-permute-start(bf16[1024,128]{1,0:T(8,128)(2,1)S(1)} %get-tuple-element.109), channel_id=1, source_target_pairs={{0,8},{1,9},{2,10},{3,11},{4,12},{5,13},{6,14},{7,15},{8,0},{9,1},... | collective-permute-start | bytes 786440 | tf_op jit(solution)/shard_map/ppermute | solution.py:77
  48.0 9.2 %collective-permute-start.9 = (bf16[1024,128]{1,0:T(8,128)(2,1)S(1)}, bf16[1024,128]{1,0:T(8,128)(2,1)S(1)}, u32[]{:S(2)}, u32[]{:S(2)}) collective-permute-start(bf16[1024,128]{1,0:T(8,128)(2,1)S(1)} %broadcast_select_fusion.12), channel_id=1, source_target_pairs={{0,2},{1,3},{2,0},{3,1},{4,6},{5,7},{6,4},{7,5},{8,10},{9,11},{10,... | collective-permute-start | bytes 786440 | tf_op jit(solution)/shard_map/ppermute | solution.py:65
  48.6 10.2 %collective-permute-start.7 = (bf16[1024,128]{1,0:T(8,128)(2,1)S(1)}, bf16[1024,128]{1,0:T(8,128)(2,1)S(1)}, u32[]{:S(2)}, u32[]{:S(2)}) collective-permute-start(bf16[1024,128]{1,0:T(8,128)(2,1)S(1)} %broadcast_select_fusion.13), channel_id=1, source_target_pairs={{0,4},{1,5},{2,6},{3,7},{4,0},{5,1},{6,2},{7,3},{8,12},{9,13},{10,... | collective-permute-start | bytes 786440 | tf_op jit(solution)/shard_map/ppermute | solution.py:68
  48.8 12.5 %collective-permute-start.8 = (bf16[1024,128]{1,0:T(8,128)(2,1)S(1)}, bf16[1024,128]{1,0:T(8,128)(2,1)S(1)}, u32[]{:S(2)}, u32[]{:S(2)}) collective-permute-start(bf16[1024,128]{1,0:T(8,128)(2,1)S(1)} %broadcast_select_fusion.14), channel_id=1, source_target_pairs={{0,8},{1,9},{2,10},{3,11},{4,12},{5,13},{6,14},{7,15},{8,0},{9,1},... | collective-permute-start | bytes 786440 | tf_op jit(solution)/shard_map/ppermute | solution.py:77
  57.3 10.6 %collective-permute-start.12 = (f32[1024,128]{1,0:T(8,128)S(1)}, f32[1024,128]{1,0:T(8,128)S(1)}, u32[]{:S(2)}, u32[]{:S(2)}) collective-permute-start(f32[1024,128]{1,0:T(8,128)S(1)} %convolution_add_fusion.5), channel_id=1, source_target_pairs={{0,2},{1,3},{2,0},{3,1},{4,6},{5,7},{6,4},{7,5},{8,10},{9,11},{10,... | collective-permute-start | bytes 1572872 | tf_op jit(solution)/shard_map/ppermute | solution.py:65
  61.5 15.2 %collective-permute-start.10 = (bf16[1024,256]{1,0:T(8,128)(2,1)S(1)}, bf16[1024,256]{1,0:T(8,128)(2,1)S(1)}, u32[]{:S(2)}, u32[]{:S(2)}) collective-permute-start(bf16[1024,256]{1,0:T(8,128)(2,1)S(1)} %maximum_select_fusion), channel_id=1, source_target_pairs={{0,4},{1,5},{2,6},{3,7},{4,0},{5,1},{6,2},{7,3},{8,12},{9,13},{10,... | collective-permute-start | bytes 1572872 | tf_op jit(solution)/shard_map/ppermute | solution.py:68
  62.6 17.3 %collective-permute-start.11 = (bf16[1024,128]{1,0:T(8,128)(2,1)S(1)}, bf16[1024,128]{1,0:T(8,128)(2,1)S(1)}, u32[]{:S(2)}, u32[]{:S(2)}) collective-permute-start(bf16[1024,128]{1,0:T(8,128)(2,1)S(1)} %broadcast_select_fusion.11), channel_id=1, source_target_pairs={{0,8},{1,9},{2,10},{3,11},{4,12},{5,13},{6,14},{7,15},{8,0},{9,1},... | collective-permute-start | bytes 786440 | tf_op jit(solution)/shard_map/ppermute | solution.py:77
  65.3 25.8 %collective-permute-start.16 = (bf16[1024,256]{1,0:T(8,128)(2,1)S(1)}, bf16[1024,256]{1,0:T(8,128)(2,1)S(1)}, u32[]{:S(2)}, u32[]{:S(2)}) collective-permute-start(bf16[1024,256]{1,0:T(8,128)(2,1)S(1)} %slice.90), channel_id=1, source_target_pairs={{0,8},{1,9},{4,12},{5,13},{10,2},{11,3},{14,6},{15,7},{16,24},{17,... | collective-permute-start | bytes 1572872 | tf_op jit(solution)/shard_map/ppermute | solution.py:74
  67.9 18.2 %collective-permute-start.14 = (f32[1024,128]{1,0:T(8,128)S(1)}, f32[1024,128]{1,0:T(8,128)S(1)}, u32[]{:S(2)}, u32[]{:S(2)}) collective-permute-start(f32[1024,128]{1,0:T(8,128)S(1)} %convolution_add_fusion.4), channel_id=1, source_target_pairs={{0,2},{1,3},{2,0},{3,1},{4,6},{5,7},{6,4},{7,5},{8,10},{9,11},{10,... | collective-permute-start | bytes 1572872 | tf_op jit(solution)/shard_map/ppermute | solution.py:65
  80.0 17.8 %collective-permute-start.13 = (bf16[1024,256]{1,0:T(8,128)(2,1)S(1)}, bf16[1024,256]{1,0:T(8,128)(2,1)S(1)}, u32[]{:S(2)}, u32[]{:S(2)}) collective-permute-start(bf16[1024,256]{1,0:T(8,128)(2,1)S(1)} %maximum_select_fusion.1), channel_id=1, source_target_pairs={{0,4},{1,5},{2,6},{3,7},{4,0},{5,1},{6,2},{7,3},{8,12},{9,13},{10,... | collective-permute-start | bytes 1572872 | tf_op jit(solution)/shard_map/ppermute | solution.py:68
  85.3 18.0 %collective-permute-start.19 = (bf16[1024,512]{1,0:T(8,128)(2,1)S(1)}, bf16[1024,512]{1,0:T(8,128)(2,1)S(1)}, u32[]{:S(2)}, u32[]{:S(2)}) collective-permute-start(bf16[1024,512]{1,0:T(8,128)(2,1)S(1)} %pad_maximum_fusion.2), channel_id=1, source_target_pairs={{0,1},{1,0},{2,3},{3,2},{4,5},{5,4},{6,7},{7,6},{8,9},{9,8},{10,11... | collective-permute-start | bytes 3145736 | tf_op jit(solution)/shard_map/ppermute | solution.py:71
  85.3 16.8 %collective-permute-start.21 = (bf16[1024,512]{1,0:T(8,128)(2,1)S(1)}, bf16[1024,512]{1,0:T(8,128)(2,1)S(1)}, u32[]{:S(2)}, u32[]{:S(2)}) collective-permute-start(bf16[1024,512]{1,0:T(8,128)(2,1)S(1)} %copy-done.1), channel_id=1, source_target_pairs={{0,1},{1,0},{2,3},{3,2},{4,5},{5,4},{6,7},{7,6},{8,9},{9,8},{10,11... | collective-permute-start | bytes 3145736 | tf_op jit(solution)/shard_map/ppermute | solution.py:71
  86.1 16.1 %collective-permute-start.15 = (f32[1024,128]{1,0:T(8,128)S(1)}, f32[1024,128]{1,0:T(8,128)S(1)}, u32[]{:S(2)}, u32[]{:S(2)}) collective-permute-start(f32[1024,128]{1,0:T(8,128)S(1)} %convolution_add_fusion.3), channel_id=1, source_target_pairs={{0,2},{1,3},{2,0},{3,1},{4,6},{5,7},{6,4},{7,5},{8,10},{9,11},{10,... | collective-permute-start | bytes 1572872 | tf_op jit(solution)/shard_map/ppermute | solution.py:65
  99.5 11.4 %collective-permute-start.17 = (bf16[1024,256]{1,0:T(8,128)(2,1)S(1)}, bf16[1024,256]{1,0:T(8,128)(2,1)S(1)}, u32[]{:S(2)}, u32[]{:S(2)}) collective-permute-start(bf16[1024,256]{1,0:T(8,128)(2,1)S(1)} %broadcast_select_fusion.8), channel_id=1, source_target_pairs={{0,4},{1,5},{2,6},{3,7},{4,0},{5,1},{6,2},{7,3},{8,12},{9,13},{10,... | collective-permute-start | bytes 1572872 | tf_op jit(solution)/shard_map/ppermute | solution.py:68
  103.2 5.3 %collective-permute-start.18 = (bf16[1024,512]{1,0:T(8,128)(2,1)S(1)}, bf16[1024,512]{1,0:T(8,128)(2,1)S(1)}, u32[]{:S(2)}, u32[]{:S(2)}) collective-permute-start(bf16[1024,512]{1,0:T(8,128)(2,1)S(1)} %get-tuple-element.93), channel_id=1, source_target_pairs={{0,1},{1,0},{2,3},{3,2},{4,5},{5,4},{6,7},{7,6},{8,9},{9,8},{10,11... | collective-permute-start | bytes 3145736 | tf_op jit(solution)/shard_map/ppermute | solution.py:71
  103.7 3.5 %collective-permute-start.20 = (bf16[1024,256]{1,0:T(8,128)(2,1)S(1)}, bf16[1024,256]{1,0:T(8,128)(2,1)S(1)}, u32[]{:S(2)}, u32[]{:S(2)}) collective-permute-start(bf16[1024,256]{1,0:T(8,128)(2,1)S(1)} %get-tuple-element.101), channel_id=1, source_target_pairs={{0,1},{1,0},{2,3},{3,2},{4,5},{5,4},{6,7},{7,6},{8,9},{9,8},{10,11... | collective-permute-start | bytes 1572872 | tf_op jit(solution)/shard_map/ppermute | solution.py:71
  104.2 13.9 %collective-permute-start.22 = (f32[1024,128]{1,0:T(8,128)S(1)}, f32[1024,128]{1,0:T(8,128)S(1)}, u32[]{:S(2)}, u32[]{:S(2)}) collective-permute-start(f32[1024,128]{1,0:T(8,128)S(1)} %convolution_add_fusion.2), channel_id=1, source_target_pairs={{0,2},{1,3},{2,0},{3,1},{4,6},{5,7},{6,4},{7,5},{8,10},{9,11},{10,... | collective-permute-start | bytes 1572872 | tf_op jit(solution)/shard_map/ppermute | solution.py:65
  111.0 2.0 %collective-permute-start.23 = (bf16[1024,256]{1,0:T(8,128)(2,1)S(1)}, bf16[1024,256]{1,0:T(8,128)(2,1)S(1)}, u32[]{:S(2)}, u32[]{:S(2)}) collective-permute-start(bf16[1024,256]{1,0:T(8,128)(2,1)S(1)} %get-tuple-element.97), channel_id=1, source_target_pairs={{0,1},{1,0},{2,3},{3,2},{4,5},{5,4},{6,7},{7,6},{8,9},{9,8},{10,11... | collective-permute-start | bytes 1572872 | tf_op jit(solution)/shard_map/ppermute | solution.py:71

commit v12 on v11

--- a/solution.py
+++ b/solution.py
@@ -93,26 +93,32 @@
         e = [columns(expected_cot, i, i + 1) for i in range(4)]
         v = [columns(value_next, i, i + 1) for i in range(4)]
         x1 = cross(jnp.where(home, v[0], e[0]))
+        j0 = home_jump(e[0])
         t_other = swap(transition)
-        e2 = after(e[2], x1)
-        j1 = jump(jnp.where(home, x1, e2))
         t_near, t_next = jnp.where(mine, transition, t_other), jnp.where(mine, t_other, transition)
 
         def adjoint_of(near, far):
             return tdot(t_near, near) + tdot(t_next, far)
 
-        v1, e1 = together((v[1], e[1]), x1, t_near)
-        x2 = cross(jnp.concatenate([jnp.where(home, v1, e1), v[2], v[3]], 1))
-        x2, v_across2, v_across3 = columns(x2, 0, 1), columns(x2, 1, 2), columns(x2, 2, 3)
-        second = jnp.where(home, x2, e[3])
+        v1, e1 = together((v[1], e[1]), x1, t_near, j0)
+        x2 = cross(jnp.concatenate([jnp.where(home, v1, e1), v[2]], 1))
+        x2, v_across2 = columns(x2, 0, 1), columns(x2, 1, 2)
+        near, far = together((x1, e[2]), j0)
+        j1 = jump(jnp.where(home, near, far))
+        near, far = together((e[0], j0), x1)
+        a0 = jnp.where(home, near, far)
+        a0_next = step(a0)
+        near, far = together((x2, e[3]), j1)
+        second = jnp.where(home, near, far)
         j2 = jump(second)
-        near, far = together((j1, v[0]), second)
+        near, far = together((j1, v[0]), second, a0_next)
         third_cross = jnp.where(home, near, far)
-        x3 = cross(third_cross)
+        x3 = cross(jnp.concatenate([third_cross, v[3]], 1))
+        x3, v_across3 = columns(x3, 0, 1), columns(x3, 1, 2)
         near, far = together((x1, j1), third_cross)
         b0 = jnp.where(home, near, far)
         b0_next = step(b0)
-        third = jnp.where(home, e[0], x3)
+        third = jnp.where(home, e[1], x3)
         j3 = jump(third)
         sum0 = adjoint_of(b0, b0_next)
         near, far = together((j2, v[1]), third)
@@ -121,63 +127,58 @@
         b1 = jnp.where(home, near, far)
         b1_next = step(b1)
         part0 = cross(after(sum0, x4))
-        fourth = jnp.where(home, e[1], x4)
+        fourth = jnp.where(home, e[2], x4)
         j4 = jump(fourth)
-        sum1 = adjoint_of(b1, b1_next)
-        part1 = cross(after(sum1, part0))
-        near, both, far = together((e[0], j3, x3), sum1, fourth)
-        a0b2 = jnp.where(home, jnp.concatenate([near, both], 1), jnp.concatenate([both, far], 1))
-        a0b2_next = step(a0b2)
-        sum2 = adjoint_of(columns(a0b2, 1, 2), columns(a0b2_next, 1, 2))
-        part2 = cross(after(sum2, part1))
-        j5 = home_jump(after(columns(expected_cot, 2, 4), j3))
-        near, both, far = together((e[1], j4, x4), sum2, part0)
-        a1b3 = jnp.where(home, jnp.concatenate([near, both], 1), jnp.concatenate([both, far], 1))
-        a1b3_next = step(a1b3)
-        v_other = swap(after(value_next, sum1))
-        sum3 = adjoint_of(columns(a1b3, 1, 2), columns(a1b3_next, 1, 2))
-        part3 = cross(after(sum3, part2))
-
-        def own_and_swapped(near, far):
-            return jnp.where(mine, near, far), swap(jnp.where(mine, far, near))
-
-        parts = together((x1, x2, x3, x4, v_across2, v_across3), sum1)
+        sum1 = adjoint_of(b1, after(b1_next, part0))
+        part1 = cross(sum1)
+        near, both, far = together((e[1], j3, x3), b1_next, fourth)
+        a1b2 = jnp.where(home, jnp.concatenate([near, both], 1), jnp.concatenate([both, far], 1))
+        a1b2_next = step(a1b2)
+        sum2 = adjoint_of(columns(a1b2, 1, 2), columns(after(a1b2_next, part1), 1, 2))
+        part2 = cross(sum2)
+        j5 = home_jump(after(e[3], j3))
+        near, both, far = together((e[2], j4, x4), a1b2_next, part0)
+        a2b3 = jnp.where(home, jnp.concatenate([near, both], 1), jnp.concatenate([both, far], 1))
+        a2b3_next = step(a2b3)
+        v_other = swap(after(value_next, b1_next))
+        sum3 = adjoint_of(columns(a2b3, 1, 2), columns(after(a2b3_next, part2), 1, 2))
+        part3 = cross(sum3)
+
+        def product(near, far, values, values_other):
+            own, swapped = jnp.where(mine, near, far), swap(jnp.where(mine, far, near))
+            return dott(jnp.concatenate([own, swapped], 1), jnp.concatenate(values + values_other, 1))
+
+        parts = together((x1, x2, x3, x4, v_across2, v_across3), b1_next)
         v_across = jnp.concatenate(
             [jnp.where(home, parts[2], parts[0]), jnp.where(home, parts[3], parts[1]), parts[4], parts[5]], 1
         )
         v_across_other = swap(v_across)
-        near, far = together((columns(expected_cot, 2, 4), j5), a1b3_next, part1)
-        a23 = jnp.where(home, near, far)
-        a23_next = step(a23)
-        b0, b0_next, b1, b1_next, a0b2, a0b2_next = together(
-            (b0, b0_next, b1, b1_next, a0b2, a0b2_next), a1b3_next, sum3, part2, a23
-        )
-        a0, a0_next = columns(a0b2, 0, 1), columns(a0b2_next, 0, 1)
-        a1, a1_next = columns(a1b3, 0, 1), columns(a1b3_next, 0, 1)
-        b_own, b_swapped = own_and_swapped(
-            jnp.concatenate([b0, b1, columns(a0b2, 1, 2), columns(a1b3, 1, 2)], 1),
-            jnp.concatenate([b0_next, b1_next, columns(a0b2_next, 1, 2), columns(a1b3_next, 1, 2)], 1),
-        )
-        a01_own, a01_swapped = own_and_swapped(
-            jnp.concatenate([a0, a1], 1), jnp.concatenate([a0_next, a1_next], 1)
-        )
-        grad = dott(
-            jnp.concatenate([b_own, b_swapped], 1), jnp.concatenate([v_across, v_across_other], 1)
-        ) + dott(
-            jnp.concatenate([a01_own, a01_swapped], 1),
-            jnp.concatenate([columns(value_next, 0, 2), columns(v_other, 0, 2)], 1),
-        )
-        own01 = adjoint_of(jnp.concatenate([a0, a1], 1), jnp.concatenate([a0_next, a1_next], 1))
-        near, far = together((a23, a23_next), grad, own01)
-        a23_own, a23_swapped = own_and_swapped(near, far)
-        grad = df * (grad + dott(
-            jnp.concatenate([a23_own, a23_swapped], 1),
-            jnp.concatenate([columns(value_next, 2, 4), columns(v_other, 2, 4)], 1),
-        ))
-        own23 = adjoint_of(near, far)
-        own23, part3, grad = together((own23, part3, grad))
+        w, w_other, u, u_other = (
+            [columns(array, i, i + 1) for i in range(4)] for array in (value_next, v_other, v_across, v_across_other)
+        )
+        early = together((b0, b1, a1b2, a0, b0_next, b1_next, a1b2_next, a0_next), a2b3, sum2)
+        grad = product(
+            jnp.concatenate(early[:4], 1),
+            jnp.concatenate(early[4:], 1),
+            [u[0], u[1], w[1], u[2], w[0]],
+            [u_other[0], u_other[1], w_other[1], u_other[2], w_other[0]],
+        )
+        near, far = together((e[3], j5), a2b3_next, part1, grad)
+        a3 = jnp.where(home, near, far)
+        a3_next = step(a3)
+        near, far = together((a2b3, a2b3_next), a3, sum3)
+        grad = grad + product(near, far, [w[2], u[3]], [w_other[2], u_other[3]])
+        a1, a1_next = columns(a1b2, 0, 1), columns(a1b2_next, 0, 1)
+        own012 = adjoint_of(
+            jnp.concatenate([a0, a1, columns(near, 0, 1)], 1),
+            jnp.concatenate([a0_next, a1_next, columns(far, 0, 1)], 1),
+        )
+        near, far = together((a3, a3_next), grad, own012)
+        grad = df * (grad + product(near, far, [w[3]], [w_other[3]]))
+        own3 = adjoint_of(near, far)
+        own3, part3, grad = together((own3, part3, grad))
         adjoint = df * (
-            jnp.concatenate([own01, own23], 1) + jnp.concatenate([part0, part1, part2, part3], 1)
+            jnp.concatenate([own012, own3], 1) + jnp.concatenate([part0, part1, part2, part3], 1)
         )
         return adjoint, grad
 

time: 122 us -> 134 us (1.098); the launches traced: 120 us -> 134 us
  waiting for transfers between devices: 58.5 us -> 70.2 us
  starting transfers between devices: 33.8 us -> 35.5 us
  matrix products: 16 us -> 17.4 us
    ppermute x8, waiting for transfers between devices: 25.4 us -> 48.1 us  [cross(): return lax.ppermute(a, AXES, cross_pairs)]
    ppermute x5 -> x6, waiting for transfers between devices: 21.9 us -> 8.93 us  [step(): return lax.ppermute(a, AXES, step_pairs)]
    ppermute x1 -> x2, starting transfers between devices: 2.32 us -> 10.6 us  [home_jump(): return lax.ppermute(a, AXES, home_jump_pairs)]
    ppermute x5 -> x6, starting transfers between devices: 9.98 us -> 4.65 us  [step(): return lax.ppermute(a, AXES, step_pairs)]
    ppermute x4, starting transfers between devices: 10.9 us -> 6.45 us  [jump(): return lax.ppermute(a, AXES, jump_pairs)]
    ppermute x8, starting transfers between devices: 8.89 us -> 12.9 us  [cross(): return lax.ppermute(a, AXES, cross_pairs)]
    ppermute x4, waiting for transfers between devices: 5.85 us -> 8.97 us  [jump(): return lax.ppermute(a, AXES, jump_pairs)]
    ppermute x1 -> x2, waiting for transfers between devices: 4.96 us -> 3.39 us  [home_jump(): return lax.ppermute(a, AXES, home_jump_pairs)]
  transfers between devices with their start and end apart: 24 -> 26, of which waited for: 13 -> 13; matrix products, arithmetic and copies ran while one was open for 19% -> 18% of each run, Pallas kernels for 0% -> 0%
where the time goes in v12:
time: 134 us
  waiting for transfers between devices  70.2 us (52%)
  starting transfers between devices  35.5 us (26%)
  matrix products  17.4 us (13%)
  other arithmetic  7.41 us (6%)
  between operations  1.93 us (1%)
  local copies, waits for them, and re-layouts  1.75 us (1%)
    ppermute x8, waiting for transfers between devices, cross(): return lax.ppermute(a, AXES, cross_pairs)  48.1 us
    ppermute x8, starting transfers between devices, cross(): return lax.ppermute(a, AXES, cross_pairs)  12.9 us
    ppermute x2, starting transfers between devices, home_jump(): return lax.ppermute(a, AXES, home_jump_pairs)  10.6 us
    dot_general x12, matrix products, tdot(): lax.dot_general(a, b, (((0,), (0,)), ((), ())), preferred_element_type=jn...  10.4 us
    ppermute x4, waiting for transfers between devices, jump(): return lax.ppermute(a, AXES, jump_pairs)  8.97 us
    ppermute x6, waiting for transfers between devices, step(): return lax.ppermute(a, AXES, step_pairs)  8.93 us
    dot_general x3, matrix products, dott(): lax.dot_general(a, b, (((1,), (1,)), ((), ())), preferred_element_type=jn...  7 us
    ppermute x4, starting transfers between devices, jump(): return lax.ppermute(a, AXES, jump_pairs)  6.45 us
  transfers between devices with their start and end apart: 26, of which 13 were waited for; matrix products, arithmetic and copies ran while one was open for 18% of the time, Pallas kernels for 0%

profile of v12, /device:TPU:0, one launch (start us, length us, event | category | flops | bytes accessed | tf_op | source)
XLA Modules:
  0.0 134.1 jit_solution(11822882407151056820)
XLA Ops:
  0.6 0.5 collective-permute-start
  1.1 1.7 %fusion.45 = (bf16[1024,128]{1,0:T(8,128)(2,1)S(1)}, bf16[1024,128]{1,0:T(8,128)(2,1)S(1)}, bf16[1024,128]{1,0:T(8,128)(2,1)S(1)}, bf16[1024,128]{1,0:T(8,128)(2...) fusion(bf16[1024,512]{1,0:T(8,128)(2,1)} %param.4, ...), kind=kLoop, calls=%fused_computation.98 | loop fusion | flops 131072 | bytes 4456449 | tf_op jit(solution)/shard_map/slice | solution.py:88
  2.9 2.6 %collective-permute-start.2 = (bf16[1024,128]{1,0:T(8,128)(2,1)S(1)}, bf16[1024,128]{1,0:T(8,128)(2,1)S(1)}, u32[]{:S(2)}, u32[]{:S(2)}) collective-permute-start(bf16[1024,128]{1,0:T(8,128)(2,1)S(1)} %get-tuple-element.120), channel_id=1, source_target_pairs={{0,2},{1,3},{2,0},{3,1},{4,6},{5,7},{6,4},{7,5},{8,10},{9,11},{10,... | collective-permute-start | bytes 786440 | tf_op jit(solution)/shard_map/ppermute | solution.py:65
  5.5 4.5 %collective-permute-start.1 = (bf16[1024,128]{1,0:T(8,128)(2,1)S(1)}, bf16[1024,128]{1,0:T(8,128)(2,1)S(1)}, u32[]{:S(2)}, u32[]{:S(2)}) collective-permute-start(bf16[1024,128]{1,0:T(8,128)(2,1)S(1)} %get-tuple-element.53), channel_id=1, source_target_pairs={{0,8},{1,9},{4,12},{5,13},{10,2},{11,3},{14,6},{15,7},{16,24},{17,... | collective-permute-start | bytes 786440 | tf_op jit(solution)/shard_map/ppermute | solution.py:74
  10.0 2.5 %broadcast_select_fusion.1 = (bf16[1024,1024]{1,0:T(8,128)(2,1)S(1)}, bf16[1024,1024]{1,0:T(8,128)(2,1)S(1)}) fusion(bf16[1024,1024]{1,0:T(8,128)(2,1)} %param.6, bf16[1024,1024]{1,0:T(8,128)(2,1)} %collective-permute-done, pred[]{:T(512)S(6)} %eq.8), kind=kLoop, calls=%fused_computation.9 | loop fusion | flops 2097152 | bytes 8388609 | tf_op jit(solution)/shard_map/jit(_where)/select_n | solution.py:98
  12.5 3.4 %collective-permute-done.1 = bf16[1024,128]{1,0:T(8,128)(2,1)S(1)} collective-permute-done((bf16[1024,128]{1,0:T(8,128)(2,1)S(1)}, bf16[1024,128]{1,0:T(8,128)(2,1)S(1)}, u32[]{:S(2)}, u32[]{:S(2)}) %collective-permute-start.1) | collective-permute-done | bytes 262176 | tf_op jit(solution)/shard_map/ppermute | solution.py:74
  16.0 6.7 %collective-permute-start.4 = (bf16[1024,256]{1,0:T(8,128)(2,1)S(1)}, bf16[1024,256]{1,0:T(8,128)(2,1)S(1)}, u32[]{:S(2)}, u32[]{:S(2)}) collective-permute-start(bf16[1024,256]{1,0:T(8,128)(2,1)S(1)} %pad_maximum_fusion.1), channel_id=1, source_target_pairs={{0,2},{1,3},{2,0},{3,1},{4,6},{5,7},{6,4},{7,5},{8,10},{9,11},{10,... | collective-permute-start | bytes 1572872 | tf_op jit(solution)/shard_map/ppermute | solution.py:65
  22.9 3.8 %collective-permute-start.5 = (bf16[1024,128]{1,0:T(8,128)(2,1)S(1)}, bf16[1024,128]{1,0:T(8,128)(2,1)S(1)}, u32[]{:S(2)}, u32[]{:S(2)}) collective-permute-start(bf16[1024,128]{1,0:T(8,128)(2,1)S(1)} %broadcast_select_fusion.20), channel_id=1, source_target_pairs={{0,4},{1,5},{2,6},{3,7},{4,0},{5,1},{6,2},{7,3},{8,12},{9,13},{10,... | collective-permute-start | bytes 786440 | tf_op jit(solution)/shard_map/ppermute | solution.py:68
  26.7 7.8 %collective-permute-done.4 = bf16[1024,256]{1,0:T(8,128)(2,1)S(1)} collective-permute-done((bf16[1024,256]{1,0:T(8,128)(2,1)S(1)}, bf16[1024,256]{1,0:T(8,128)(2,1)S(1)}, u32[]{:S(2)}, u32[]{:S(2)}) %collective-permute-start.4) | collective-permute-done | bytes 524320 | tf_op jit(solution)/shard_map/ppermute | solution.py:65
  34.6 2.5 %collective-permute-done.3 = bf16[1024,128]{1,0:T(8,128)(2,1)S(1)} collective-permute-done((bf16[1024,128]{1,0:T(8,128)(2,1)S(1)}, bf16[1024,128]{1,0:T(8,128)(2,1)S(1)}, u32[]{:S(2)}, u32[]{:S(2)}) %collective-permute-start.3) | collective-permute-done | bytes 262176 | tf_op jit(solution)/shard_map/ppermute | solution.py:77
  37.1 0.1 collective-permute-done.5
  37.3 0.1 collective-permute-start.9
  37.4 3.3 %collective-permute-start.8 = (bf16[1024,128]{1,0:T(8,128)(2,1)S(1)}, bf16[1024,128]{1,0:T(8,128)(2,1)S(1)}, u32[]{:S(2)}, u32[]{:S(2)}) collective-permute-start(bf16[1024,128]{1,0:T(8,128)(2,1)S(1)} %broadcast_select_fusion.17), channel_id=1, source_target_pairs={{0,8},{1,9},{2,10},{3,11},{4,12},{5,13},{6,14},{7,15},{8,0},{9,1},... | collective-permute-start | bytes 786440 | tf_op jit(solution)/shard_map/ppermute | solution.py:77
  40.8 1.8 %collective-permute-start.6 = (bf16[1024,256]{1,0:T(8,128)(2,1)S(1)}, bf16[1024,256]{1,0:T(8,128)(2,1)S(1)}, u32[]{:S(2)}, u32[]{:S(2)}) collective-permute-start(bf16[1024,256]{1,0:T(8,128)(2,1)S(1)} %pad_maximum_fusion.2), channel_id=1, source_target_pairs={{0,2},{1,3},{2,0},{3,1},{4,6},{5,7},{6,4},{7,5},{8,10},{9,11},{10,... | collective-permute-start | bytes 1572872 | tf_op jit(solution)/shard_map/ppermute | solution.py:65
  42.6 7.2 %collective-permute-done.9 = bf16[1024,128]{1,0:T(8,128)(2,1)S(1)} collective-permute-done((bf16[1024,128]{1,0:T(8,128)(2,1)S(1)}, bf16[1024,128]{1,0:T(8,128)(2,1)S(1)}, u32[]{:S(2)}, u32[]{:S(2)}) %collective-permute-start.9) | collective-permute-done | bytes 262176 | tf_op jit(solution)/shard_map/ppermute | solution.py:68
  49.8 0.7 fusion.48
  50.5 0.8 convolution_add_fusion.6
  51.3 2.0 %collective-permute-done.6 = bf16[1024,256]{1,0:T(8,128)(2,1)S(1)} collective-permute-done((bf16[1024,256]{1,0:T(8,128)(2,1)S(1)}, bf16[1024,256]{1,0:T(8,128)(2,1)S(1)}, u32[]{:S(2)}, u32[]{:S(2)}) %collective-permute-start.6) | collective-permute-done | bytes 524320 | tf_op jit(solution)/shard_map/ppermute | solution.py:65
  53.4 0.3 collective-permute-start.7
  53.8 1.5 %collective-permute-start.11 = (bf16[1024,128]{1,0:T(8,128)(2,1)S(1)}, bf16[1024,128]{1,0:T(8,128)(2,1)S(1)}, u32[]{:S(2)}, u32[]{:S(2)}) collective-permute-start(bf16[1024,128]{1,0:T(8,128)(2,1)S(1)} %broadcast_select_fusion.12), channel_id=1, source_target_pairs={{0,2},{1,3},{2,0},{3,1},{4,6},{5,7},{6,4},{7,5},{8,10},{9,11},{10,... | collective-permute-start | bytes 786440 | tf_op jit(solution)/shard_map/ppermute | solution.py:65
  55.3 0.6 collective-permute-start.10
  56.6 3.7 %collective-permute-done.11 = bf16[1024,128]{1,0:T(8,128)(2,1)S(1)} collective-permute-done((bf16[1024,128]{1,0:T(8,128)(2,1)S(1)}, bf16[1024,128]{1,0:T(8,128)(2,1)S(1)}, u32[]{:S(2)}, u32[]{:S(2)}) %collective-permute-start.11) | collective-permute-done | bytes 262176 | tf_op jit(solution)/shard_map/ppermute | solution.py:65
  60.3 2.7 %collective-permute-start.12 = (bf16[1024,128]{1,0:T(8,128)(2,1)S(1)}, bf16[1024,128]{1,0:T(8,128)(2,1)S(1)}, u32[]{:S(2)}, u32[]{:S(2)}) collective-permute-start(bf16[1024,128]{1,0:T(8,128)(2,1)S(1)} %broadcast_select_fusion.11), channel_id=1, source_target_pairs={{0,8},{1,9},{2,10},{3,11},{4,12},{5,13},{6,14},{7,15},{8,0},{9,1},... | collective-permute-start | bytes 786440 | tf_op jit(solution)/shard_map/ppermute | solution.py:77
  63.0 6.4 %collective-permute-done.7 = bf16[1024,128]{1,0:T(8,128)(2,1)S(1)} collective-permute-done((bf16[1024,128]{1,0:T(8,128)(2,1)S(1)}, bf16[1024,128]{1,0:T(8,128)(2,1)S(1)}, u32[]{:S(2)}, u32[]{:S(2)}) %collective-permute-start.7) | collective-permute-done | bytes 262176 | tf_op jit(solution)/shard_map/ppermute | solution.py:77
  69.5 0.2 maximum_select_fusion
  69.7 6.1 %collective-permute-start.16 = (bf16[1024,128]{1,0:T(8,128)(2,1)S(1)}, bf16[1024,128]{1,0:T(8,128)(2,1)S(1)}, u32[]{:S(2)}, u32[]{:S(2)}) collective-permute-start(bf16[1024,128]{1,0:T(8,128)(2,1)S(1)} %get-tuple-element.94), channel_id=1, source_target_pairs={{0,8},{1,9},{4,12},{5,13},{10,2},{11,3},{14,6},{15,7},{16,24},{17,... | collective-permute-start | bytes 786440 | tf_op jit(solution)/shard_map/ppermute | solution.py:74
  75.8 0.1 collective-permute-start.14
  76.0 0.1 constant_dynamic-update-slice_fusion.12
  76.1 0.1 constant_dynamic-update-slice_fusion.11
  76.2 0.1 constant_dynamic-update-slice_fusion.10
  76.3 11.8 %collective-permute-done.14 = f32[1024,128]{1,0:T(8,128)S(1)} collective-permute-done((f32[1024,128]{1,0:T(8,128)S(1)}, f32[1024,128]{1,0:T(8,128)S(1)}, u32[]{:S(2)}, u32[]{:S(2)}) %collective-permute-start.14) | collective-permute-done | bytes 524320 | tf_op jit(solution)/shard_map/ppermute | solution.py:65
  88.1 0.7 fusion.49
  88.8 0.8 convolution_add_fusion.5
  89.6 0.1 collective-permute-start.17
  89.7 0.1 pad_maximum_fusion
  89.9 0.1 constant_dynamic-update-slice_fusion.8
  90.0 0.1 collective-permute-start.19
  90.1 0.2 maximum_select_fusion.1
  90.2 0.1 collective-permute-start.15
  90.3 12.0 %collective-permute-done.17 = f32[1024,128]{1,0:T(8,128)S(1)} collective-permute-done((f32[1024,128]{1,0:T(8,128)S(1)}, f32[1024,128]{1,0:T(8,128)S(1)}, u32[]{:S(2)}, u32[]{:S(2)}) %collective-permute-start.17) | collective-permute-done | bytes 524320 | tf_op jit(solution)/shard_map/ppermute | solution.py:65
  102.3 0.8 fusion.36
  103.1 0.8 convolution_add_fusion.4
  104.3 0.1 constant_dynamic-update-slice_fusion
  104.5 0.2 broadcast_select_fusion.3
  104.8 0.1 slice_dynamic-update-slice_fusion.3
  104.9 0.1 fusion.44
  105.0 0.2 fusion.43
  105.2 10.8 %collective-permute-done.21 = f32[1024,128]{1,0:T(8,128)S(1)} collective-permute-done((f32[1024,128]{1,0:T(8,128)S(1)}, f32[1024,128]{1,0:T(8,128)S(1)}, u32[]{:S(2)}, u32[]{:S(2)}) %collective-permute-start.21) | collective-permute-done | bytes 524320 | tf_op jit(solution)/shard_map/ppermute | solution.py:65
  116.0 0.8 fusion.34
  116.8 0.8 convolution_add_fusion.3
  117.6 0.1 collective-permute-start.24
  117.6 2.9 %fusion = f32[1024,1024]{1,0:T(8,128)S(1)} fusion(bf16[1024,1280]{1,0:T(8,128)(2,1)S(1)} %get-tuple-element.114, bf16[1024,640]{1,0:T(8,128)(2,1)S(1)} %collective-permute-done.18, bf16[1024,640]{1,0:T(8,128)(2,1)S(1)} %get-tuple-element.110), kind=kOutput, calls=%fused_computation.1 | convolution fusion | flops 2689597440 | bytes 9437184 | tf_op jit(solution)/shard_map/dot_general | solution.py:38
  120.6 0.1 collective-permute-start.22
  120.7 0.1 broadcast_select_fusion.5
  120.9 0.6 slice-done
  121.5 1.3 fusion.20
  122.8 1.3 convolution_add_fusion.1
  124.1 1.3 convolution_add_fusion
  125.5 1.6 %collective-permute-done.22 = bf16[1024,128]{1,0:T(8,128)(2,1)S(1)} collective-permute-done((bf16[1024,128]{1,0:T(8,128)(2,1)S(1)}, bf16[1024,128]{1,0:T(8,128)(2,1)S(1)}, u32[]{:S(2)}, u32[]{:S(2)}) %collective-permute-start.22) | collective-permute-done | bytes 262176 | tf_op jit(solution)/shard_map/ppermute | solution.py:68
  127.0 1.0 fusion.50
  128.1 0.8 convolution_add_fusion.2
  128.9 0.8 collective-permute-done.25
  129.6 2.8 %add_multiply_fusion = f32[1024,1024]{1,0:T(8,128)} fusion(f32[1024,1024]{1,0:T(8,128)S(1)} %convolution_add_fusion, f32[]{:T(128)} %bitcast, bf16[1024,128]{1,0:T(8,128)(2,1)S(1)} %collective-permute-done.25, bf16[1024,128]{1,0:T(8,128)(2,1)S(1)} %get-tuple-element.128, bf16[1024,128]{1,0:T(8,128)(2,1)S(1)} %get-tuple-element.112, ...), kind=kOutput, calls=%fused_computation | convolution fusion | flops 541065216 | bytes 9437188 | tf_op jit(solution)/shard_map/dot_general | solution.py:38
  132.4 1.7 %fusion.4 = f32[1024,512]{1,0:T(8,128)} fusion(f32[1024,128]{1,0:T(8,128)S(1)} %convolution_add_fusion.2, f32[1024,384]{1,0:T(8,128)S(1)} %convolution_add_fusion.1, f32[1024,128]{1,0:T(8,128)S(1)} %collective-permute-done.24, f32[1024,128]{1,0:T(8,128)S(1)} %collective-permute-done.21, f32[1024,128]{1,0:T(8,128)S(1)} %collective-permute-done.17, ...), kind=kLoop, calls=%fused_computation.7 | loop fusion | flops 3145728 | bytes 6291460 | tf_op jit(solution)/shard_map/mul | solution.py:180
  (53 shorter events, 1.6 us)
Async XLA Ops:
  0.6 9.4 %collective-permute-start = (bf16[1024,1024]{1,0:T(8,128)(2,1)}, bf16[1024,1024]{1,0:T(8,128)(2,1)}, u32[]{:S(2)}, u32[]{:S(2)}) collective-permute-start(bf16[1024,1024]{1,0:T(8,128)(2,1)} %param.6), channel_id=1, source_target_pairs={{0,1},{1,0},{2,3},{3,2},{4,5},{5,4},{6,7},{7,6},{8,9},{9,8},{10,11... | collective-permute-start | bytes 6291464 | tf_op jit(solution)/shard_map/ppermute | solution.py:71
  2.9 9.6 %collective-permute-start.2 = (bf16[1024,128]{1,0:T(8,128)(2,1)S(1)}, bf16[1024,128]{1,0:T(8,128)(2,1)S(1)}, u32[]{:S(2)}, u32[]{:S(2)}) collective-permute-start(bf16[1024,128]{1,0:T(8,128)(2,1)S(1)} %get-tuple-element.120), channel_id=1, source_target_pairs={{0,2},{1,3},{2,0},{3,1},{4,6},{5,7},{6,4},{7,5},{8,10},{9,11},{10,... | collective-permute-start | bytes 786440 | tf_op jit(solution)/shard_map/ppermute | solution.py:65
  5.5 10.4 %collective-permute-start.1 = (bf16[1024,128]{1,0:T(8,128)(2,1)S(1)}, bf16[1024,128]{1,0:T(8,128)(2,1)S(1)}, u32[]{:S(2)}, u32[]{:S(2)}) collective-permute-start(bf16[1024,128]{1,0:T(8,128)(2,1)S(1)} %get-tuple-element.53), channel_id=1, source_target_pairs={{0,8},{1,9},{4,12},{5,13},{10,2},{11,3},{14,6},{15,7},{16,24},{17,... | collective-permute-start | bytes 786440 | tf_op jit(solution)/shard_map/ppermute | solution.py:74
  16.0 18.5 %collective-permute-start.4 = (bf16[1024,256]{1,0:T(8,128)(2,1)S(1)}, bf16[1024,256]{1,0:T(8,128)(2,1)S(1)}, u32[]{:S(2)}, u32[]{:S(2)}) collective-permute-start(bf16[1024,256]{1,0:T(8,128)(2,1)S(1)} %pad_maximum_fusion.1), channel_id=1, source_target_pairs={{0,2},{1,3},{2,0},{3,1},{4,6},{5,7},{6,4},{7,5},{8,10},{9,11},{10,... | collective-permute-start | bytes 1572872 | tf_op jit(solution)/shard_map/ppermute | solution.py:65
  22.8 14.3 %collective-permute-start.3 = (bf16[1024,128]{1,0:T(8,128)(2,1)S(1)}, bf16[1024,128]{1,0:T(8,128)(2,1)S(1)}, u32[]{:S(2)}, u32[]{:S(2)}) collective-permute-start(bf16[1024,128]{1,0:T(8,128)(2,1)S(1)} %broadcast_select_fusion.19), channel_id=1, source_target_pairs={{0,8},{1,9},{2,10},{3,11},{4,12},{5,13},{6,14},{7,15},{8,0},{9,1},... | collective-permute-start | bytes 786440 | tf_op jit(solution)/shard_map/ppermute | solution.py:77
  22.9 14.4 %collective-permute-start.5 = (bf16[1024,128]{1,0:T(8,128)(2,1)S(1)}, bf16[1024,128]{1,0:T(8,128)(2,1)S(1)}, u32[]{:S(2)}, u32[]{:S(2)}) collective-permute-start(bf16[1024,128]{1,0:T(8,128)(2,1)S(1)} %broadcast_select_fusion.20), channel_id=1, source_target_pairs={{0,4},{1,5},{2,6},{3,7},{4,0},{5,1},{6,2},{7,3},{8,12},{9,13},{10,... | collective-permute-start | bytes 786440 | tf_op jit(solution)/shard_map/ppermute | solution.py:68
  37.3 12.5 %collective-permute-start.9 = (bf16[1024,128]{1,0:T(8,128)(2,1)S(1)}, bf16[1024,128]{1,0:T(8,128)(2,1)S(1)}, u32[]{:S(2)}, u32[]{:S(2)}) collective-permute-start(bf16[1024,128]{1,0:T(8,128)(2,1)S(1)} %broadcast_select_fusion.14), channel_id=1, source_target_pairs={{0,4},{1,5},{2,6},{3,7},{4,0},{5,1},{6,2},{7,3},{8,12},{9,13},{10,... | collective-permute-start | bytes 786440 | tf_op jit(solution)/shard_map/ppermute | solution.py:68
  37.4 16.4 %collective-permute-start.8 = (bf16[1024,128]{1,0:T(8,128)(2,1)S(1)}, bf16[1024,128]{1,0:T(8,128)(2,1)S(1)}, u32[]{:S(2)}, u32[]{:S(2)}) collective-permute-start(bf16[1024,128]{1,0:T(8,128)(2,1)S(1)} %broadcast_select_fusion.17), channel_id=1, source_target_pairs={{0,8},{1,9},{2,10},{3,11},{4,12},{5,13},{6,14},{7,15},{8,0},{9,1},... | collective-permute-start | bytes 786440 | tf_op jit(solution)/shard_map/ppermute | solution.py:77
  40.8 12.5 %collective-permute-start.6 = (bf16[1024,256]{1,0:T(8,128)(2,1)S(1)}, bf16[1024,256]{1,0:T(8,128)(2,1)S(1)}, u32[]{:S(2)}, u32[]{:S(2)}) collective-permute-start(bf16[1024,256]{1,0:T(8,128)(2,1)S(1)} %pad_maximum_fusion.2), channel_id=1, source_target_pairs={{0,2},{1,3},{2,0},{3,1},{4,6},{5,7},{6,4},{7,5},{8,10},{9,11},{10,... | collective-permute-start | bytes 1572872 | tf_op jit(solution)/shard_map/ppermute | solution.py:65
  50.5 2.8 %copy-start.1 = (bf16[1024,512]{1,0:T(8,128)(2,1)S(1)}, bf16[1024,512]{1,0:T(8,128)(2,1)}, u32[]{:S(2)}) copy-start(bf16[1024,512]{1,0:T(8,128)(2,1)} %param.4) | copy-start | bytes 3145732
  53.4 22.5 %copy-start = (bf16[1024,512]{1,0:T(8,128)(2,1)S(1)}, bf16[1024,512]{1,0:T(8,128)(2,1)}, u32[]{:S(2)}) copy-start(bf16[1024,512]{1,0:T(8,128)(2,1)} %param.5) | copy-start | bytes 3145732
  53.4 16.0 %collective-permute-start.7 = (bf16[1024,128]{1,0:T(8,128)(2,1)S(1)}, bf16[1024,128]{1,0:T(8,128)(2,1)S(1)}, u32[]{:S(2)}, u32[]{:S(2)}) collective-permute-start(bf16[1024,128]{1,0:T(8,128)(2,1)S(1)} %get-tuple-element.131), channel_id=1, source_target_pairs={{0,8},{1,9},{2,10},{3,11},{4,12},{5,13},{6,14},{7,15},{8,0},{9,1},... | collective-permute-start | bytes 786440 | tf_op jit(solution)/shard_map/ppermute | solution.py:77
  53.8 6.4 %collective-permute-start.11 = (bf16[1024,128]{1,0:T(8,128)(2,1)S(1)}, bf16[1024,128]{1,0:T(8,128)(2,1)S(1)}, u32[]{:S(2)}, u32[]{:S(2)}) collective-permute-start(bf16[1024,128]{1,0:T(8,128)(2,1)S(1)} %broadcast_select_fusion.12), channel_id=1, source_target_pairs={{0,2},{1,3},{2,0},{3,1},{4,6},{5,7},{6,4},{7,5},{8,10},{9,11},{10,... | collective-permute-start | bytes 786440 | tf_op jit(solution)/shard_map/ppermute | solution.py:65
  55.3 14.1 %collective-permute-start.10 = (bf16[1024,128]{1,0:T(8,128)(2,1)S(1)}, bf16[1024,128]{1,0:T(8,128)(2,1)S(1)}, u32[]{:S(2)}, u32[]{:S(2)}) collective-permute-start(bf16[1024,128]{1,0:T(8,128)(2,1)S(1)} %broadcast_select_fusion.13), channel_id=1, source_target_pairs={{0,4},{1,5},{2,6},{3,7},{4,0},{5,1},{6,2},{7,3},{8,12},{9,13},{10,... | collective-permute-start | bytes 786440 | tf_op jit(solution)/shard_map/ppermute | solution.py:68
  60.3 29.7 %collective-permute-start.12 = (bf16[1024,128]{1,0:T(8,128)(2,1)S(1)}, bf16[1024,128]{1,0:T(8,128)(2,1)S(1)}, u32[]{:S(2)}, u32[]{:S(2)}) collective-permute-start(bf16[1024,128]{1,0:T(8,128)(2,1)S(1)} %broadcast_select_fusion.11), channel_id=1, source_target_pairs={{0,8},{1,9},{2,10},{3,11},{4,12},{5,13},{6,14},{7,15},{8,0},{9,1},... | collective-permute-start | bytes 786440 | tf_op jit(solution)/shard_map/ppermute | solution.py:77
  69.6 20.4 %collective-permute-start.13 = (bf16[1024,256]{1,0:T(8,128)(2,1)S(1)}, bf16[1024,256]{1,0:T(8,128)(2,1)S(1)}, u32[]{:S(2)}, u32[]{:S(2)}) collective-permute-start(bf16[1024,256]{1,0:T(8,128)(2,1)S(1)} %maximum_select_fusion), channel_id=1, source_target_pairs={{0,4},{1,5},{2,6},{3,7},{4,0},{5,1},{6,2},{7,3},{8,12},{9,13},{10,... | collective-permute-start | bytes 1572872 | tf_op jit(solution)/shard_map/ppermute | solution.py:68
  69.7 50.8 %collective-permute-start.16 = (bf16[1024,128]{1,0:T(8,128)(2,1)S(1)}, bf16[1024,128]{1,0:T(8,128)(2,1)S(1)}, u32[]{:S(2)}, u32[]{:S(2)}) collective-permute-start(bf16[1024,128]{1,0:T(8,128)(2,1)S(1)} %get-tuple-element.94), channel_id=1, source_target_pairs={{0,8},{1,9},{4,12},{5,13},{10,2},{11,3},{14,6},{15,7},{16,24},{17,... | collective-permute-start | bytes 786440 | tf_op jit(solution)/shard_map/ppermute | solution.py:74
  75.8 12.2 %collective-permute-start.14 = (f32[1024,128]{1,0:T(8,128)S(1)}, f32[1024,128]{1,0:T(8,128)S(1)}, u32[]{:S(2)}, u32[]{:S(2)}) collective-permute-start(f32[1024,128]{1,0:T(8,128)S(1)} %convolution_add_fusion.6), channel_id=1, source_target_pairs={{0,2},{1,3},{2,0},{3,1},{4,6},{5,7},{6,4},{7,5},{8,10},{9,11},{10,... | collective-permute-start | bytes 1572872 | tf_op jit(solution)/shard_map/ppermute | solution.py:65
  75.9 28.9 %collective-permute-start.20 = (bf16[1024,512]{1,0:T(8,128)(2,1)S(1)}, bf16[1024,512]{1,0:T(8,128)(2,1)S(1)}, u32[]{:S(2)}, u32[]{:S(2)}) collective-permute-start(bf16[1024,512]{1,0:T(8,128)(2,1)S(1)} %copy-done), channel_id=1, source_target_pairs={{0,1},{1,0},{2,3},{3,2},{4,5},{5,4},{6,7},{7,6},{8,9},{9,8},{10,11... | collective-permute-start | bytes 3145736 | tf_op jit(solution)/shard_map/ppermute | solution.py:71
  89.6 12.7 %collective-permute-start.17 = (f32[1024,128]{1,0:T(8,128)S(1)}, f32[1024,128]{1,0:T(8,128)S(1)}, u32[]{:S(2)}, u32[]{:S(2)}) collective-permute-start(f32[1024,128]{1,0:T(8,128)S(1)} %convolution_add_fusion.5), channel_id=1, source_target_pairs={{0,2},{1,3},{2,0},{3,1},{4,6},{5,7},{6,4},{7,5},{8,10},{9,11},{10,... | collective-permute-start | bytes 1572872 | tf_op jit(solution)/shard_map/ppermute | solution.py:65
  90.0 14.7 %collective-permute-start.19 = (bf16[1024,512]{1,0:T(8,128)(2,1)S(1)}, bf16[1024,512]{1,0:T(8,128)(2,1)S(1)}, u32[]{:S(2)}, u32[]{:S(2)}) collective-permute-start(bf16[1024,512]{1,0:T(8,128)(2,1)S(1)} %pad_maximum_fusion), channel_id=1, source_target_pairs={{0,1},{1,0},{2,3},{3,2},{4,5},{5,4},{6,7},{7,6},{8,9},{9,8},{10,11... | collective-permute-start | bytes 3145736 | tf_op jit(solution)/shard_map/ppermute | solution.py:71
  90.0 14.2 %copy-start.2 = (bf16[1024,256]{1,0:T(8,128)(2,1)}, bf16[1024,256]{1,0:T(8,128)(2,1)S(1)}, u32[]{:S(2)}) copy-start(bf16[1024,256]{1,0:T(8,128)(2,1)S(1)} %collective-permute-done.13) | copy-start | bytes 1572868
  90.2 15.0 %collective-permute-start.15 = (bf16[1024,256]{1,0:T(8,128)(2,1)S(1)}, bf16[1024,256]{1,0:T(8,128)(2,1)S(1)}, u32[]{:S(2)}, u32[]{:S(2)}) collective-permute-start(bf16[1024,256]{1,0:T(8,128)(2,1)S(1)} %maximum_select_fusion.1), channel_id=1, source_target_pairs={{0,4},{1,5},{2,6},{3,7},{4,0},{5,1},{6,2},{7,3},{8,12},{9,13},{10,... | collective-permute-start | bytes 1572872 | tf_op jit(solution)/shard_map/ppermute | solution.py:68
  103.9 12.1 %collective-permute-start.21 = (f32[1024,128]{1,0:T(8,128)S(1)}, f32[1024,128]{1,0:T(8,128)S(1)}, u32[]{:S(2)}, u32[]{:S(2)}) collective-permute-start(f32[1024,128]{1,0:T(8,128)S(1)} %convolution_add_fusion.4), channel_id=1, source_target_pairs={{0,2},{1,3},{2,0},{3,1},{4,6},{5,7},{6,4},{7,5},{8,10},{9,11},{10,... | collective-permute-start | bytes 1572872 | tf_op jit(solution)/shard_map/ppermute | solution.py:65
  104.7 12.9 %collective-permute-start.18 = (bf16[1024,640]{1,0:T(8,128)(2,1)S(1)}, bf16[1024,640]{1,0:T(8,128)(2,1)S(1)}, u32[]{:S(2)}, u32[]{:S(2)}) collective-permute-start(bf16[1024,640]{1,0:T(8,128)(2,1)S(1)} %get-tuple-element.111), channel_id=1, source_target_pairs={{0,1},{1,0},{2,3},{3,2},{4,5},{5,4},{6,7},{7,6},{8,9},{9,8},{10,11... | collective-permute-start | bytes 3932168 | tf_op jit(solution)/shard_map/ppermute | solution.py:71
  117.6 14.9 %collective-permute-start.24 = (f32[1024,128]{1,0:T(8,128)S(1)}, f32[1024,128]{1,0:T(8,128)S(1)}, u32[]{:S(2)}, u32[]{:S(2)}) collective-permute-start(f32[1024,128]{1,0:T(8,128)S(1)} %convolution_add_fusion.3), channel_id=1, source_target_pairs={{0,2},{1,3},{2,0},{3,1},{4,6},{5,7},{6,4},{7,5},{8,10},{9,11},{10,... | collective-permute-start | bytes 1572872 | tf_op jit(solution)/shard_map/ppermute | solution.py:65
  120.5 1.0 slice-start
  120.6 6.4 %collective-permute-start.22 = (bf16[1024,128]{1,0:T(8,128)(2,1)S(1)}, bf16[1024,128]{1,0:T(8,128)(2,1)S(1)}, u32[]{:S(2)}, u32[]{:S(2)}) collective-permute-start(bf16[1024,128]{1,0:T(8,128)(2,1)S(1)} %broadcast_select_fusion.8), channel_id=1, source_target_pairs={{0,4},{1,5},{2,6},{3,7},{4,0},{5,1},{6,2},{7,3},{8,12},{9,13},{10,... | collective-permute-start | bytes 786440 | tf_op jit(solution)/shard_map/ppermute | solution.py:68
  120.8 3.3 %collective-permute-start.23 = (bf16[1024,256]{1,0:T(8,128)(2,1)S(1)}, bf16[1024,256]{1,0:T(8,128)(2,1)S(1)}, u32[]{:S(2)}, u32[]{:S(2)}) collective-permute-start(bf16[1024,256]{1,0:T(8,128)(2,1)S(1)} %get-tuple-element.118), channel_id=1, source_target_pairs={{0,1},{1,0},{2,3},{3,2},{4,5},{5,4},{6,7},{7,6},{8,9},{9,8},{10,11... | collective-permute-start | bytes 1572872 | tf_op jit(solution)/shard_map/ppermute | solution.py:71
  128.0 1.6 %collective-permute-start.25 = (bf16[1024,128]{1,0:T(8,128)(2,1)S(1)}, bf16[1024,128]{1,0:T(8,128)(2,1)S(1)}, u32[]{:S(2)}, u32[]{:S(2)}) collective-permute-start(bf16[1024,128]{1,0:T(8,128)(2,1)S(1)} %get-tuple-element.129), channel_id=1, source_target_pairs={{0,1},{1,0},{2,3},{3,2},{4,5},{5,4},{6,7},{7,6},{8,9},{9,8},{10,11... | collective-permute-start | bytes 786440 | tf_op jit(solution)/shard_map/ppermute | solution.py:71

commit v13 on v11

--- a/solution.py
+++ b/solution.py
@@ -102,13 +102,14 @@
             return tdot(t_near, near) + tdot(t_next, far)
 
         v1, e1 = together((v[1], e[1]), x1, t_near)
-        x2 = cross(jnp.concatenate([jnp.where(home, v1, e1), v[2], v[3]], 1))
-        x2, v_across2, v_across3 = columns(x2, 0, 1), columns(x2, 1, 2), columns(x2, 2, 3)
+        x2 = cross(jnp.concatenate([jnp.where(home, v1, e1), v[2]], 1))
+        x2, v_across2 = columns(x2, 0, 1), columns(x2, 1, 2)
         second = jnp.where(home, x2, e[3])
         j2 = jump(second)
         near, far = together((j1, v[0]), second)
         third_cross = jnp.where(home, near, far)
-        x3 = cross(third_cross)
+        x3 = cross(jnp.concatenate([third_cross, v[3]], 1))
+        x3, v_across3 = columns(x3, 0, 1), columns(x3, 1, 2)
         near, far = together((x1, j1), third_cross)
         b0 = jnp.where(home, near, far)
         b0_next = step(b0)
@@ -128,52 +129,46 @@
         near, both, far = together((e[0], j3, x3), sum1, fourth)
         a0b2 = jnp.where(home, jnp.concatenate([near, both], 1), jnp.concatenate([both, far], 1))
         a0b2_next = step(a0b2)
-        sum2 = adjoint_of(columns(a0b2, 1, 2), columns(a0b2_next, 1, 2))
-        part2 = cross(after(sum2, part1))
+        sum2 = adjoint_of(columns(a0b2, 1, 2), columns(after(a0b2_next, part1), 1, 2))
+        part2 = cross(sum2)
         j5 = home_jump(after(columns(expected_cot, 2, 4), j3))
-        near, both, far = together((e[1], j4, x4), sum2, part0)
+        near, both, far = together((e[1], j4, x4), a0b2_next, part0)
         a1b3 = jnp.where(home, jnp.concatenate([near, both], 1), jnp.concatenate([both, far], 1))
         a1b3_next = step(a1b3)
         v_other = swap(after(value_next, sum1))
-        sum3 = adjoint_of(columns(a1b3, 1, 2), columns(a1b3_next, 1, 2))
-        part3 = cross(after(sum3, part2))
+        sum3 = adjoint_of(columns(a1b3, 1, 2), columns(after(a1b3_next, part2), 1, 2))
+        part3 = cross(sum3)
 
-        def own_and_swapped(near, far):
-            return jnp.where(mine, near, far), swap(jnp.where(mine, far, near))
+        def product(near, far, values, values_other):
+            own, swapped = jnp.where(mine, near, far), swap(jnp.where(mine, far, near))
+            return dott(jnp.concatenate([own, swapped], 1), jnp.concatenate(values + values_other, 1))
 
         parts = together((x1, x2, x3, x4, v_across2, v_across3), sum1)
         v_across = jnp.concatenate(
             [jnp.where(home, parts[2], parts[0]), jnp.where(home, parts[3], parts[1]), parts[4], parts[5]], 1
         )
         v_across_other = swap(v_across)
-        near, far = together((columns(expected_cot, 2, 4), j5), a1b3_next, part1)
+        w, w_other, u, u_other = (
+            [columns(array, i, i + 1) for i in range(4)] for array in (value_next, v_other, v_across, v_across_other)
+        )
+        early = together((b0, b1, a0b2, b0_next, b1_next, a0b2_next), a1b3, sum2)
+        grad = product(
+            jnp.concatenate(early[:3], 1),
+            jnp.concatenate(early[3:], 1),
+            [u[0], u[1], w[0], u[2]],
+            [u_other[0], u_other[1], w_other[0], u_other[2]],
+        )
+        near, far = together((columns(expected_cot, 2, 4), j5), a1b3_next, part1, grad)
         a23 = jnp.where(home, near, far)
         a23_next = step(a23)
-        b0, b0_next, b1, b1_next, a0b2, a0b2_next = together(
-            (b0, b0_next, b1, b1_next, a0b2, a0b2_next), a1b3_next, sum3, part2, a23
+        near, far = together((a1b3, a1b3_next), a23, sum3)
+        grad = grad + product(near, far, [w[1], u[3]], [w_other[1], u_other[3]])
+        own01 = adjoint_of(
+            jnp.concatenate([columns(a0b2, 0, 1), columns(near, 0, 1)], 1),
+            jnp.concatenate([columns(a0b2_next, 0, 1), columns(far, 0, 1)], 1),
         )
-        a0, a0_next = columns(a0b2, 0, 1), columns(a0b2_next, 0, 1)
-        a1, a1_next = columns(a1b3, 0, 1), columns(a1b3_next, 0, 1)
-        b_own, b_swapped = own_and_swapped(
-            jnp.concatenate([b0, b1, columns(a0b2, 1, 2), columns(a1b3, 1, 2)], 1),
-            jnp.concatenate([b0_next, b1_next, columns(a0b2_next, 1, 2), columns(a1b3_next, 1, 2)], 1),
-        )
-        a01_own, a01_swapped = own_and_swapped(
-            jnp.concatenate([a0, a1], 1), jnp.concatenate([a0_next, a1_next], 1)
-        )
-        grad = dott(
-            jnp.concatenate([b_own, b_swapped], 1), jnp.concatenate([v_across, v_across_other], 1)
-        ) + dott(
-            jnp.concatenate([a01_own, a01_swapped], 1),
-            jnp.concatenate([columns(value_next, 0, 2), columns(v_other, 0, 2)], 1),
-        )
-        own01 = adjoint_of(jnp.concatenate([a0, a1], 1), jnp.concatenate([a0_next, a1_next], 1))
         near, far = together((a23, a23_next), grad, own01)
-        a23_own, a23_swapped = own_and_swapped(near, far)
-        grad = df * (grad + dott(
-            jnp.concatenate([a23_own, a23_swapped], 1),
-            jnp.concatenate([columns(value_next, 2, 4), columns(v_other, 2, 4)], 1),
-        ))
+        grad = df * (grad + product(near, far, [w[2], w[3]], [w_other[2], w_other[3]]))
         own23 = adjoint_of(near, far)
         own23, part3, grad = together((own23, part3, grad))
         adjoint = df * (

time: 122 us -> 133 us (1.090); the launches traced: 120 us -> 133 us
  waiting for transfers between devices: 58.5 us -> 71.3 us
    ppermute x5, waiting for transfers between devices: 21.9 us -> 35.4 us  [step(): return lax.ppermute(a, AXES, step_pairs)]
    ppermute x8, starting transfers between devices: 8.89 us -> 20.6 us  [cross(): return lax.ppermute(a, AXES, cross_pairs)]
    ppermute x5, starting transfers between devices: 9.98 us -> 1.37 us  [step(): return lax.ppermute(a, AXES, step_pairs)]
    ppermute x4, waiting for transfers between devices: 5.85 us -> 13.2 us  [jump(): return lax.ppermute(a, AXES, jump_pairs)]
    ppermute x1, waiting for transfers between devices: 4.96 us -> 0.01 us  [home_jump(): return lax.ppermute(a, AXES, home_jump_pairs)]
    ppermute x8, waiting for transfers between devices: 25.4 us -> 22.3 us  [cross(): return lax.ppermute(a, AXES, cross_pairs)]
    ppermute x4, starting transfers between devices: 10.9 us -> 7.79 us  [jump(): return lax.ppermute(a, AXES, jump_pairs)]
    slice x2 -> x3, other arithmetic: 1.47 us -> 2.71 us  [columns(): return array[:, start * quarter:stop * quarter]]
  transfers between devices with their start and end apart: 24 -> 24, of which waited for: 13 -> 14; matrix products, arithmetic and copies ran while one was open for 19% -> 17% of each run, Pallas kernels for 0% -> 0%
where the time goes in v13:
time: 133 us
  waiting for transfers between devices  71.3 us (54%)
  starting transfers between devices  34.3 us (26%)
  matrix products  16.2 us (12%)
  other arithmetic  7.65 us (6%)
  between operations  1.83 us (1%)
  local copies, waits for them, and re-layouts  1.47 us (1%)
    ppermute x5, waiting for transfers between devices, step(): return lax.ppermute(a, AXES, step_pairs)  35.4 us
    ppermute x8, waiting for transfers between devices, cross(): return lax.ppermute(a, AXES, cross_pairs)  22.3 us
    ppermute x8, starting transfers between devices, cross(): return lax.ppermute(a, AXES, cross_pairs)  20.6 us
    ppermute x4, waiting for transfers between devices, jump(): return lax.ppermute(a, AXES, jump_pairs)  13.2 us
    dot_general x12, matrix products, tdot(): lax.dot_general(a, b, (((0,), (0,)), ((), ())), preferred_element_type=jn...  9.11 us
    ppermute x4, starting transfers between devices, jump(): return lax.ppermute(a, AXES, jump_pairs)  7.79 us
    dot_general x3, matrix products, dott(): lax.dot_general(a, b, (((1,), (1,)), ((), ())), preferred_element_type=jn...  7.06 us
    ppermute x1, starting transfers between devices, home_jump(): return lax.ppermute(a, AXES, home_jump_pairs)  3.19 us
  transfers between devices with their start and end apart: 24, of which 14 were waited for; matrix products, arithmetic and copies ran while one was open for 17% of the time, Pallas kernels for 0%

profile of v13, /device:TPU:0, one launch (start us, length us, event | category | flops | bytes accessed | tf_op | source)
XLA Modules:
  0.0 132.7 jit_solution(2871998729114204640)
XLA Ops:
  0.6 0.5 collective-permute-start
  1.2 2.6 %fusion.41 = (bf16[1024,128]{1,0:T(8,128)(2,1)S(1)}, bf16[1024,128]{1,0:T(8,128)(2,1)}, bf16[1024,128]{1,0:T(8,128)(2,1)S(1)}, bf16[1024,128]{1,0:T(8,128)(2,1)}...) fusion(bf16[1024,512]{1,0:T(8,128)(2,1)} %param.4, ...), kind=kLoop, calls=%fused_computation.89 | loop fusion | flops 131072 | bytes 3932161 | tf_op jit(solution)/shard_map/slice | solution.py:88
  3.8 2.6 %collective-permute-start.1 = (bf16[1024,128]{1,0:T(8,128)(2,1)}, bf16[1024,128]{1,0:T(8,128)(2,1)S(1)}, u32[]{:S(2)}, u32[]{:S(2)}) collective-permute-start(bf16[1024,128]{1,0:T(8,128)(2,1)} %get-tuple-element.107), channel_id=1, source_target_pairs={{0,2},{1,3},{2,0},{3,1},{4,6},{5,7},{6,4},{7,5},{8,10},{9,11},{10,... | collective-permute-start | bytes 786440 | tf_op jit(solution)/shard_map/ppermute | solution.py:65
  6.3 1.9 %broadcast_select_fusion.1 = (bf16[1024,1024]{1,0:T(8,128)(2,1)S(1)}, bf16[1024,1024]{1,0:T(8,128)(2,1)S(1)}) fusion(bf16[1024,1024]{1,0:T(8,128)(2,1)S(1)} %copy-done.3, bf16[1024,1024]{1,0:T(8,128)(2,1)} %collective-permute-done, pred[]{:T(512)S(6)} %eq.8), kind=kLoop, calls=%fused_computation.9 | loop fusion | flops 2097152 | bytes 8388609 | tf_op jit(solution)/shard_map/jit(_where)/select_n | solution.py:99
  8.3 5.1 %collective-permute-done.1 = bf16[1024,128]{1,0:T(8,128)(2,1)S(1)} collective-permute-done((bf16[1024,128]{1,0:T(8,128)(2,1)}, bf16[1024,128]{1,0:T(8,128)(2,1)S(1)}, u32[]{:S(2)}, u32[]{:S(2)}) %collective-permute-start.1) | collective-permute-done | bytes 262176 | tf_op jit(solution)/shard_map/ppermute | solution.py:65
  13.4 1.8 %collective-permute-start.3 = (bf16[1024,256]{1,0:T(8,128)(2,1)S(1)}, bf16[1024,256]{1,0:T(8,128)(2,1)S(1)}, u32[]{:S(2)}, u32[]{:S(2)}) collective-permute-start(bf16[1024,256]{1,0:T(8,128)(2,1)S(1)} %pad_maximum_fusion.1), channel_id=1, source_target_pairs={{0,2},{1,3},{2,0},{3,1},{4,6},{5,7},{6,4},{7,5},{8,10},{9,11},{10,... | collective-permute-start | bytes 1572872 | tf_op jit(solution)/shard_map/ppermute | solution.py:65
  15.3 2.7 %collective-permute-start.2 = (bf16[1024,128]{1,0:T(8,128)(2,1)S(1)}, bf16[1024,128]{1,0:T(8,128)(2,1)S(1)}, u32[]{:S(2)}, u32[]{:S(2)}) collective-permute-start(bf16[1024,128]{1,0:T(8,128)(2,1)S(1)} %broadcast_select_fusion.18), channel_id=1, source_target_pairs={{0,8},{1,9},{2,10},{3,11},{4,12},{5,13},{6,14},{7,15},{8,0},{9,1},... | collective-permute-start | bytes 786440 | tf_op jit(solution)/shard_map/ppermute | solution.py:77
  17.9 9.3 %collective-permute-done.3 = bf16[1024,256]{1,0:T(8,128)(2,1)S(1)} collective-permute-done((bf16[1024,256]{1,0:T(8,128)(2,1)S(1)}, bf16[1024,256]{1,0:T(8,128)(2,1)S(1)}, u32[]{:S(2)}, u32[]{:S(2)}) %collective-permute-start.3) | collective-permute-done | bytes 524320 | tf_op jit(solution)/shard_map/ppermute | solution.py:65
  27.3 2.1 %collective-permute-done.2 = bf16[1024,128]{1,0:T(8,128)(2,1)S(1)} collective-permute-done((bf16[1024,128]{1,0:T(8,128)(2,1)S(1)}, bf16[1024,128]{1,0:T(8,128)(2,1)S(1)}, u32[]{:S(2)}, u32[]{:S(2)}) %collective-permute-start.2) | collective-permute-done | bytes 262176 | tf_op jit(solution)/shard_map/ppermute | solution.py:77
  29.4 0.7 collective-permute-start.7
  30.2 3.4 %collective-permute-start.6 = (bf16[1024,128]{1,0:T(8,128)(2,1)S(1)}, bf16[1024,128]{1,0:T(8,128)(2,1)S(1)}, u32[]{:S(2)}, u32[]{:S(2)}) collective-permute-start(bf16[1024,128]{1,0:T(8,128)(2,1)S(1)} %get-tuple-element.118), channel_id=1, source_target_pairs={{0,8},{1,9},{2,10},{3,11},{4,12},{5,13},{6,14},{7,15},{8,0},{9,1},... | collective-permute-start | bytes 786440 | tf_op jit(solution)/shard_map/ppermute | solution.py:77
  33.6 0.6 collective-permute-start.4
  34.2 7.8 %collective-permute-done.7 = bf16[1024,128]{1,0:T(8,128)(2,1)S(1)} collective-permute-done((bf16[1024,128]{1,0:T(8,128)(2,1)S(1)}, bf16[1024,128]{1,0:T(8,128)(2,1)S(1)}, u32[]{:S(2)}, u32[]{:S(2)}) %collective-permute-start.7) | collective-permute-done | bytes 262176 | tf_op jit(solution)/shard_map/ppermute | solution.py:68
  42.0 0.7 fusion.44
  42.8 0.8 convolution_add_fusion.6
  43.6 3.4 %collective-permute-done.4 = bf16[1024,256]{1,0:T(8,128)(2,1)S(1)} collective-permute-done((bf16[1024,256]{1,0:T(8,128)(2,1)S(1)}, bf16[1024,256]{1,0:T(8,128)(2,1)S(1)}, u32[]{:S(2)}, u32[]{:S(2)}) %collective-permute-start.4) | collective-permute-done | bytes 524320 | tf_op jit(solution)/shard_map/ppermute | solution.py:65
  47.1 0.6 collective-permute-start.9
  47.7 0.4 collective-permute-start.8
  48.9 1.1 collective-permute-start.5
  50.0 3.9 %collective-permute-done.9 = bf16[1024,128]{1,0:T(8,128)(2,1)S(1)} collective-permute-done((bf16[1024,128]{1,0:T(8,128)(2,1)S(1)}, bf16[1024,128]{1,0:T(8,128)(2,1)S(1)}, u32[]{:S(2)}, u32[]{:S(2)}) %collective-permute-start.9) | collective-permute-done | bytes 262176 | tf_op jit(solution)/shard_map/ppermute | solution.py:65
  53.9 0.5 collective-permute-start.12
  54.5 0.7 collective-permute-start.10
  55.1 2.7 %collective-permute-done.8 = bf16[1024,128]{1,0:T(8,128)(2,1)S(1)} collective-permute-done((bf16[1024,128]{1,0:T(8,128)(2,1)S(1)}, bf16[1024,128]{1,0:T(8,128)(2,1)S(1)}, u32[]{:S(2)}, u32[]{:S(2)}) %collective-permute-start.8) | collective-permute-done | bytes 262176 | tf_op jit(solution)/shard_map/ppermute | solution.py:68
  57.8 0.7 fusion.45
  58.5 0.8 convolution_add_fusion.5
  59.3 10.3 %collective-permute-done.5 = bf16[1024,128]{1,0:T(8,128)(2,1)S(1)} collective-permute-done((bf16[1024,128]{1,0:T(8,128)(2,1)S(1)}, bf16[1024,128]{1,0:T(8,128)(2,1)S(1)}, u32[]{:S(2)}, u32[]{:S(2)}) %collective-permute-start.5) | collective-permute-done | bytes 262176 | tf_op jit(solution)/shard_map/ppermute | solution.py:77
  69.6 0.2 maximum_select_fusion
  69.8 0.1 collective-permute-start.11
  69.9 0.1 constant_dynamic-update-slice_fusion.9
  70.0 0.1 constant_dynamic-update-slice_fusion.8
  70.1 1.6 %collective-permute-start.15 = (f32[1024,128]{1,0:T(8,128)S(1)}, f32[1024,128]{1,0:T(8,128)S(1)}, u32[]{:S(2)}, u32[]{:S(2)}) collective-permute-start(f32[1024,128]{1,0:T(8,128)S(1)} %convolution_add_fusion.5), channel_id=1, source_target_pairs={{0,2},{1,3},{2,0},{3,1},{4,6},{5,7},{6,4},{7,5},{8,10},{9,11},{10,... | collective-permute-start | bytes 1572872 | tf_op jit(solution)/shard_map/ppermute | solution.py:65
  71.7 0.1 pad_maximum_fusion
  71.9 0.5 collective-permute-start.18
  72.4 0.1 constant_dynamic-update-slice_fusion.7
  72.5 0.1 constant_dynamic-update-slice_fusion.6
  72.6 0.8 collective-permute-done.10
  73.4 3.2 %collective-permute-start.14 = (bf16[1024,256]{1,0:T(8,128)(2,1)S(1)}, bf16[1024,256]{1,0:T(8,128)(2,1)S(1)}, u32[]{:S(2)}, u32[]{:S(2)}) collective-permute-start(bf16[1024,256]{1,0:T(8,128)(2,1)S(1)} %slice.104), channel_id=1, source_target_pairs={{0,8},{1,9},{4,12},{5,13},{10,2},{11,3},{14,6},{15,7},{16,24},{17,... | collective-permute-start | bytes 1572872 | tf_op jit(solution)/shard_map/ppermute | solution.py:74
  76.6 7.2 %collective-permute-done.11 = bf16[1024,256]{1,0:T(8,128)(2,1)S(1)} collective-permute-done((bf16[1024,256]{1,0:T(8,128)(2,1)S(1)}, bf16[1024,256]{1,0:T(8,128)(2,1)S(1)}, u32[]{:S(2)}, u32[]{:S(2)}) %collective-permute-start.11) | collective-permute-done | bytes 524320 | tf_op jit(solution)/shard_map/ppermute | solution.py:68
  83.7 0.2 maximum_select_fusion.1
  84.0 0.8 fusion.32
  84.7 0.8 convolution_add_fusion.4
  85.5 3.1 %collective-permute-start.19 = (f32[1024,128]{1,0:T(8,128)S(1)}, f32[1024,128]{1,0:T(8,128)S(1)}, u32[]{:S(2)}, u32[]{:S(2)}) collective-permute-start(f32[1024,128]{1,0:T(8,128)S(1)} %convolution_add_fusion.4), channel_id=1, source_target_pairs={{0,2},{1,3},{2,0},{3,1},{4,6},{5,7},{6,4},{7,5},{8,10},{9,11},{10,... | collective-permute-start | bytes 1572872 | tf_op jit(solution)/shard_map/ppermute | solution.py:65
  88.9 0.1 constant_dynamic-update-slice_fusion
  88.9 0.1 broadcast_select_fusion.3
  89.3 0.1 fusion.39
  89.4 0.1 fusion.40
  89.5 9.6 %collective-permute-done.13 = bf16[1024,256]{1,0:T(8,128)(2,1)S(1)} collective-permute-done((bf16[1024,256]{1,0:T(8,128)(2,1)S(1)}, bf16[1024,256]{1,0:T(8,128)(2,1)S(1)}, u32[]{:S(2)}, u32[]{:S(2)}) %collective-permute-start.13) | collective-permute-done | bytes 524320 | tf_op jit(solution)/shard_map/ppermute | solution.py:68
  99.1 0.7 collective-permute-done.19
  99.8 0.8 fusion.30
  100.6 0.8 convolution_add_fusion.3
  101.3 9.9 %collective-permute-start.22 = (f32[1024,128]{1,0:T(8,128)S(1)}, f32[1024,128]{1,0:T(8,128)S(1)}, u32[]{:S(2)}, u32[]{:S(2)}) collective-permute-start(f32[1024,128]{1,0:T(8,128)S(1)} %convolution_add_fusion.3), channel_id=1, source_target_pairs={{0,2},{1,3},{2,0},{3,1},{4,6},{5,7},{6,4},{7,5},{8,10},{9,11},{10,... | collective-permute-start | bytes 1572872 | tf_op jit(solution)/shard_map/ppermute | solution.py:65
  111.2 2.4 %fusion = f32[1024,1024]{1,0:T(8,128)S(1)} fusion(bf16[1024,1024]{1,0:T(8,128)(2,1)S(1)} %get-tuple-element.103, bf16[1024,512]{1,0:T(8,128)(2,1)S(1)} %collective-permute-done.16, bf16[1024,512]{1,0:T(8,128)(2,1)S(1)} %get-tuple-element.96), kind=kOutput, calls=%fused_computation.2 | convolution fusion | flops 2151677952 | bytes 8388608 | tf_op jit(solution)/shard_map/dot_general | solution.py:38
  113.8 0.1 broadcast_select_fusion.7
  114.0 0.6 slice-done
  114.6 0.7 fusion.24
  115.3 0.8 convolution_add_fusion.2
  116.1 1.4 %convolution_add_fusion = f32[1024,1024]{1,0:T(8,128)S(1)} fusion(f32[1024,1024]{1,0:T(8,128)S(1)} %fusion, bf16[1024,256]{1,0:T(8,128)(2,1)S(1)} %collective-permute-done.21, bf16[1024,256]{1,0:T(8,128)(2,1)S(1)} %get-tuple-element.104, bf16[1024,128]{1,0:T(8,128)(2,1)S(1)} %get-tuple-element.102, bf16[1024,128]{1,0:T(8,128)(2,1)S(1)} %get-tuple-element.100, ...), kind=kOutput, calls=%fused_computation.1 | convolution fusion | flops 1081081856 | bytes 10485760 | tf_op jit(solution)/shard_map/dot_general | solution.py:38
  117.5 8.2 %collective-permute-done.20 = bf16[1024,256]{1,0:T(8,128)(2,1)S(1)} collective-permute-done((bf16[1024,256]{1,0:T(8,128)(2,1)S(1)}, bf16[1024,256]{1,0:T(8,128)(2,1)S(1)}, u32[]{:S(2)}, u32[]{:S(2)}) %collective-permute-start.20) | collective-permute-done | bytes 524320 | tf_op jit(solution)/shard_map/ppermute | solution.py:68
  125.6 0.1 broadcast_select_fusion.5
  125.8 0.8 fusion.46
  126.6 0.8 convolution_add_fusion.1
  127.3 0.4 collective-permute-done.23
  127.7 3.3 %add_multiply_fusion = f32[1024,1024]{1,0:T(8,128)} fusion(f32[1024,1024]{1,0:T(8,128)S(1)} %convolution_add_fusion, f32[]{:T(128)} %bitcast, bf16[1024,256]{1,0:T(8,128)(2,1)S(1)} %collective-permute-done.23, bf16[1024,256]{1,0:T(8,128)(2,1)S(1)} %get-tuple-element.98, bf16[1024,256]{1,0:T(8,128)(2,1)S(1)} %slice-done.1, bf16[1024,256]{1,0:T(8,128)(2,1)S(1)} %slice.119), kind=kOutput, calls=%fused_computation | convolution fusion | flops 1080033280 | bytes 10485764 | tf_op jit(solution)/shard_map/dot_general | solution.py:38
  131.0 1.7 %fusion.4 = f32[1024,512]{1,0:T(8,128)} fusion(f32[1024,256]{1,0:T(8,128)S(1)} %convolution_add_fusion.1, f32[1024,256]{1,0:T(8,128)S(1)} %convolution_add_fusion.2, f32[1024,128]{1,0:T(8,128)S(1)} %collective-permute-done.22, f32[1024,128]{1,0:T(8,128)S(1)} %collective-permute-done.19, f32[1024,128]{1,0:T(8,128)S(1)} %collective-permute-done.15, ...), kind=kLoop, calls=%fused_computation.7 | loop fusion | flops 3145728 | bytes 6291460 | tf_op jit(solution)/shard_map/mul | solution.py:174
  (57 shorter events, 1.4 us)
Async XLA Ops:
  0.6 5.7 %copy-start.3 = (bf16[1024,1024]{1,0:T(8,128)(2,1)S(1)}, bf16[1024,1024]{1,0:T(8,128)(2,1)}, u32[]{:S(2)}) copy-start(bf16[1024,1024]{1,0:T(8,128)(2,1)} %param.6) | copy-start | bytes 6291460
  0.6 5.7 %collective-permute-start = (bf16[1024,1024]{1,0:T(8,128)(2,1)}, bf16[1024,1024]{1,0:T(8,128)(2,1)}, u32[]{:S(2)}, u32[]{:S(2)}) collective-permute-start(bf16[1024,1024]{1,0:T(8,128)(2,1)} %param.6), channel_id=1, source_target_pairs={{0,1},{1,0},{2,3},{3,2},{4,5},{5,4},{6,7},{7,6},{8,9},{9,8},{10,11... | collective-permute-start | bytes 6291464 | tf_op jit(solution)/shard_map/ppermute | solution.py:71
  3.8 9.6 %collective-permute-start.1 = (bf16[1024,128]{1,0:T(8,128)(2,1)}, bf16[1024,128]{1,0:T(8,128)(2,1)S(1)}, u32[]{:S(2)}, u32[]{:S(2)}) collective-permute-start(bf16[1024,128]{1,0:T(8,128)(2,1)} %get-tuple-element.107), channel_id=1, source_target_pairs={{0,2},{1,3},{2,0},{3,1},{4,6},{5,7},{6,4},{7,5},{8,10},{9,11},{10,... | collective-permute-start | bytes 786440 | tf_op jit(solution)/shard_map/ppermute | solution.py:65
  6.3 7.1 %copy-start.7 = (bf16[1024,128]{1,0:T(8,128)(2,1)S(1)}, bf16[1024,128]{1,0:T(8,128)(2,1)}, u32[]{:S(2)}) copy-start(bf16[1024,128]{1,0:T(8,128)(2,1)} %get-tuple-element.109) | copy-start | bytes 786436
  6.3 8.9 %copy-start.6 = (bf16[1024,128]{1,0:T(8,128)(2,1)S(1)}, bf16[1024,128]{1,0:T(8,128)(2,1)}, u32[]{:S(2)}) copy-start(bf16[1024,128]{1,0:T(8,128)(2,1)} %get-tuple-element.46) | copy-start | bytes 786436
  8.3 18.9 %copy-start = (bf16[1024,512]{1,0:T(8,128)(2,1)S(1)}, bf16[1024,512]{1,0:T(8,128)(2,1)}, u32[]{:S(2)}) copy-start(bf16[1024,512]{1,0:T(8,128)(2,1)} %param.4) | copy-start | bytes 3145732
  13.3 16.0 %copy-start.5 = (bf16[1024,128]{1,0:T(8,128)(2,1)S(1)}, bf16[1024,128]{1,0:T(8,128)(2,1)}, u32[]{:S(2)}) copy-start(bf16[1024,128]{1,0:T(8,128)(2,1)} %get-tuple-element.50) | copy-start | bytes 786436
  13.4 13.8 %collective-permute-start.3 = (bf16[1024,256]{1,0:T(8,128)(2,1)S(1)}, bf16[1024,256]{1,0:T(8,128)(2,1)S(1)}, u32[]{:S(2)}, u32[]{:S(2)}) collective-permute-start(bf16[1024,256]{1,0:T(8,128)(2,1)S(1)} %pad_maximum_fusion.1), channel_id=1, source_target_pairs={{0,2},{1,3},{2,0},{3,1},{4,6},{5,7},{6,4},{7,5},{8,10},{9,11},{10,... | collective-permute-start | bytes 1572872 | tf_op jit(solution)/shard_map/ppermute | solution.py:65
  15.3 14.1 %collective-permute-start.2 = (bf16[1024,128]{1,0:T(8,128)(2,1)S(1)}, bf16[1024,128]{1,0:T(8,128)(2,1)S(1)}, u32[]{:S(2)}, u32[]{:S(2)}) collective-permute-start(bf16[1024,128]{1,0:T(8,128)(2,1)S(1)} %broadcast_select_fusion.18), channel_id=1, source_target_pairs={{0,8},{1,9},{2,10},{3,11},{4,12},{5,13},{6,14},{7,15},{8,0},{9,1},... | collective-permute-start | bytes 786440 | tf_op jit(solution)/shard_map/ppermute | solution.py:77
  29.4 12.6 %collective-permute-start.7 = (bf16[1024,128]{1,0:T(8,128)(2,1)S(1)}, bf16[1024,128]{1,0:T(8,128)(2,1)S(1)}, u32[]{:S(2)}, u32[]{:S(2)}) collective-permute-start(bf16[1024,128]{1,0:T(8,128)(2,1)S(1)} %broadcast_select_fusion.14), channel_id=1, source_target_pairs={{0,4},{1,5},{2,6},{3,7},{4,0},{5,1},{6,2},{7,3},{8,12},{9,13},{10,... | collective-permute-start | bytes 786440 | tf_op jit(solution)/shard_map/ppermute | solution.py:68
  30.2 16.9 %collective-permute-start.6 = (bf16[1024,128]{1,0:T(8,128)(2,1)S(1)}, bf16[1024,128]{1,0:T(8,128)(2,1)S(1)}, u32[]{:S(2)}, u32[]{:S(2)}) collective-permute-start(bf16[1024,128]{1,0:T(8,128)(2,1)S(1)} %get-tuple-element.118), channel_id=1, source_target_pairs={{0,8},{1,9},{2,10},{3,11},{4,12},{5,13},{6,14},{7,15},{8,0},{9,1},... | collective-permute-start | bytes 786440 | tf_op jit(solution)/shard_map/ppermute | solution.py:77
  33.6 13.4 %collective-permute-start.4 = (bf16[1024,256]{1,0:T(8,128)(2,1)S(1)}, bf16[1024,256]{1,0:T(8,128)(2,1)S(1)}, u32[]{:S(2)}, u32[]{:S(2)}) collective-permute-start(bf16[1024,256]{1,0:T(8,128)(2,1)S(1)} %pad_maximum_fusion.2), channel_id=1, source_target_pairs={{0,2},{1,3},{2,0},{3,1},{4,6},{5,7},{6,4},{7,5},{8,10},{9,11},{10,... | collective-permute-start | bytes 1572872 | tf_op jit(solution)/shard_map/ppermute | solution.py:65
  43.5 4.6 %copy-start.1 = (bf16[1024,512]{1,0:T(8,128)(2,1)S(1)}, bf16[1024,512]{1,0:T(8,128)(2,1)}, u32[]{:S(2)}) copy-start(bf16[1024,512]{1,0:T(8,128)(2,1)} %param.5) | copy-start | bytes 3145732
  47.1 6.8 %collective-permute-start.9 = (bf16[1024,128]{1,0:T(8,128)(2,1)S(1)}, bf16[1024,128]{1,0:T(8,128)(2,1)S(1)}, u32[]{:S(2)}, u32[]{:S(2)}) collective-permute-start(bf16[1024,128]{1,0:T(8,128)(2,1)S(1)} %broadcast_select_fusion.12), channel_id=1, source_target_pairs={{0,2},{1,3},{2,0},{3,1},{4,6},{5,7},{6,4},{7,5},{8,10},{9,11},{10,... | collective-permute-start | bytes 786440 | tf_op jit(solution)/shard_map/ppermute | solution.py:65
  47.7 10.1 %collective-permute-start.8 = (bf16[1024,128]{1,0:T(8,128)(2,1)S(1)}, bf16[1024,128]{1,0:T(8,128)(2,1)S(1)}, u32[]{:S(2)}, u32[]{:S(2)}) collective-permute-start(bf16[1024,128]{1,0:T(8,128)(2,1)S(1)} %broadcast_select_fusion.13), channel_id=1, source_target_pairs={{0,4},{1,5},{2,6},{3,7},{4,0},{5,1},{6,2},{7,3},{8,12},{9,13},{10,... | collective-permute-start | bytes 786440 | tf_op jit(solution)/shard_map/ppermute | solution.py:68
  48.9 20.7 %collective-permute-start.5 = (bf16[1024,128]{1,0:T(8,128)(2,1)S(1)}, bf16[1024,128]{1,0:T(8,128)(2,1)S(1)}, u32[]{:S(2)}, u32[]{:S(2)}) collective-permute-start(bf16[1024,128]{1,0:T(8,128)(2,1)S(1)} %get-tuple-element.115), channel_id=1, source_target_pairs={{0,8},{1,9},{2,10},{3,11},{4,12},{5,13},{6,14},{7,15},{8,0},{9,1},... | collective-permute-start | bytes 786440 | tf_op jit(solution)/shard_map/ppermute | solution.py:77
  53.9 16.2 %collective-permute-start.12 = (f32[1024,128]{1,0:T(8,128)S(1)}, f32[1024,128]{1,0:T(8,128)S(1)}, u32[]{:S(2)}, u32[]{:S(2)}) collective-permute-start(f32[1024,128]{1,0:T(8,128)S(1)} %convolution_add_fusion.6), channel_id=1, source_target_pairs={{0,2},{1,3},{2,0},{3,1},{4,6},{5,7},{6,4},{7,5},{8,10},{9,11},{10,... | collective-permute-start | bytes 1572872 | tf_op jit(solution)/shard_map/ppermute | solution.py:65
  54.5 18.9 %collective-permute-start.10 = (bf16[1024,128]{1,0:T(8,128)(2,1)S(1)}, bf16[1024,128]{1,0:T(8,128)(2,1)S(1)}, u32[]{:S(2)}, u32[]{:S(2)}) collective-permute-start(bf16[1024,128]{1,0:T(8,128)(2,1)S(1)} %broadcast_select_fusion.11), channel_id=1, source_target_pairs={{0,8},{1,9},{2,10},{3,11},{4,12},{5,13},{6,14},{7,15},{8,0},{9,1},... | collective-permute-start | bytes 786440 | tf_op jit(solution)/shard_map/ppermute | solution.py:77
  69.8 13.9 %collective-permute-start.11 = (bf16[1024,256]{1,0:T(8,128)(2,1)S(1)}, bf16[1024,256]{1,0:T(8,128)(2,1)S(1)}, u32[]{:S(2)}, u32[]{:S(2)}) collective-permute-start(bf16[1024,256]{1,0:T(8,128)(2,1)S(1)} %maximum_select_fusion), channel_id=1, source_target_pairs={{0,4},{1,5},{2,6},{3,7},{4,0},{5,1},{6,2},{7,3},{8,12},{9,13},{10,... | collective-permute-start | bytes 1572872 | tf_op jit(solution)/shard_map/ppermute | solution.py:68
  70.1 13.9 %collective-permute-start.15 = (f32[1024,128]{1,0:T(8,128)S(1)}, f32[1024,128]{1,0:T(8,128)S(1)}, u32[]{:S(2)}, u32[]{:S(2)}) collective-permute-start(f32[1024,128]{1,0:T(8,128)S(1)} %convolution_add_fusion.5), channel_id=1, source_target_pairs={{0,2},{1,3},{2,0},{3,1},{4,6},{5,7},{6,4},{7,5},{8,10},{9,11},{10,... | collective-permute-start | bytes 1572872 | tf_op jit(solution)/shard_map/ppermute | solution.py:65
  71.8 17.3 %collective-permute-start.17 = (bf16[1024,512]{1,0:T(8,128)(2,1)S(1)}, bf16[1024,512]{1,0:T(8,128)(2,1)S(1)}, u32[]{:S(2)}, u32[]{:S(2)}) collective-permute-start(bf16[1024,512]{1,0:T(8,128)(2,1)S(1)} %pad_maximum_fusion), channel_id=1, source_target_pairs={{0,1},{1,0},{2,3},{3,2},{4,5},{5,4},{6,7},{7,6},{8,9},{9,8},{10,11... | collective-permute-start | bytes 3145736 | tf_op jit(solution)/shard_map/ppermute | solution.py:71
  71.9 17.4 %collective-permute-start.18 = (bf16[1024,512]{1,0:T(8,128)(2,1)S(1)}, bf16[1024,512]{1,0:T(8,128)(2,1)S(1)}, u32[]{:S(2)}, u32[]{:S(2)}) collective-permute-start(bf16[1024,512]{1,0:T(8,128)(2,1)S(1)} %copy-done.1), channel_id=1, source_target_pairs={{0,1},{1,0},{2,3},{3,2},{4,5},{5,4},{6,7},{7,6},{8,9},{9,8},{10,11... | collective-permute-start | bytes 3145736 | tf_op jit(solution)/shard_map/ppermute | solution.py:71
  73.4 40.3 %collective-permute-start.14 = (bf16[1024,256]{1,0:T(8,128)(2,1)S(1)}, bf16[1024,256]{1,0:T(8,128)(2,1)S(1)}, u32[]{:S(2)}, u32[]{:S(2)}) collective-permute-start(bf16[1024,256]{1,0:T(8,128)(2,1)S(1)} %slice.104), channel_id=1, source_target_pairs={{0,8},{1,9},{4,12},{5,13},{10,2},{11,3},{14,6},{15,7},{16,24},{17,... | collective-permute-start | bytes 1572872 | tf_op jit(solution)/shard_map/ppermute | solution.py:74
  83.7 5.1 %copy-start.2 = (bf16[1024,256]{1,0:T(8,128)(2,1)}, bf16[1024,256]{1,0:T(8,128)(2,1)S(1)}, u32[]{:S(2)}) copy-start(bf16[1024,256]{1,0:T(8,128)(2,1)S(1)} %collective-permute-done.11) | copy-start | bytes 1572868
  83.9 15.2 %collective-permute-start.13 = (bf16[1024,256]{1,0:T(8,128)(2,1)S(1)}, bf16[1024,256]{1,0:T(8,128)(2,1)S(1)}, u32[]{:S(2)}, u32[]{:S(2)}) collective-permute-start(bf16[1024,256]{1,0:T(8,128)(2,1)S(1)} %maximum_select_fusion.1), channel_id=1, source_target_pairs={{0,4},{1,5},{2,6},{3,7},{4,0},{5,1},{6,2},{7,3},{8,12},{9,13},{10,... | collective-permute-start | bytes 1572872 | tf_op jit(solution)/shard_map/ppermute | solution.py:68
  85.5 14.3 %collective-permute-start.19 = (f32[1024,128]{1,0:T(8,128)S(1)}, f32[1024,128]{1,0:T(8,128)S(1)}, u32[]{:S(2)}, u32[]{:S(2)}) collective-permute-start(f32[1024,128]{1,0:T(8,128)S(1)} %convolution_add_fusion.4), channel_id=1, source_target_pairs={{0,2},{1,3},{2,0},{3,1},{4,6},{5,7},{6,4},{7,5},{8,10},{9,11},{10,... | collective-permute-start | bytes 1572872 | tf_op jit(solution)/shard_map/ppermute | solution.py:65
  89.1 22.1 %collective-permute-start.16 = (bf16[1024,512]{1,0:T(8,128)(2,1)S(1)}, bf16[1024,512]{1,0:T(8,128)(2,1)S(1)}, u32[]{:S(2)}, u32[]{:S(2)}) collective-permute-start(bf16[1024,512]{1,0:T(8,128)(2,1)S(1)} %get-tuple-element.97), channel_id=1, source_target_pairs={{0,1},{1,0},{2,3},{3,2},{4,5},{5,4},{6,7},{7,6},{8,9},{9,8},{10,11... | collective-permute-start | bytes 3145736 | tf_op jit(solution)/shard_map/ppermute | solution.py:71
  89.3 11.3 %copy-start.4 = (bf16[1024,512]{1,0:T(8,128)(2,1)}, bf16[1024,512]{1,0:T(8,128)(2,1)S(1)}, u32[]{:S(2)}) copy-start(bf16[1024,512]{1,0:T(8,128)(2,1)S(1)} %collective-permute-done.18) | copy-start | bytes 3145732
  101.3 29.7 %collective-permute-start.22 = (f32[1024,128]{1,0:T(8,128)S(1)}, f32[1024,128]{1,0:T(8,128)S(1)}, u32[]{:S(2)}, u32[]{:S(2)}) collective-permute-start(f32[1024,128]{1,0:T(8,128)S(1)} %convolution_add_fusion.3), channel_id=1, source_target_pairs={{0,2},{1,3},{2,0},{3,1},{4,6},{5,7},{6,4},{7,5},{8,10},{9,11},{10,... | collective-permute-start | bytes 1572872 | tf_op jit(solution)/shard_map/ppermute | solution.py:65
  113.6 1.0 slice-start
  113.8 11.8 %collective-permute-start.20 = (bf16[1024,256]{1,0:T(8,128)(2,1)S(1)}, bf16[1024,256]{1,0:T(8,128)(2,1)S(1)}, u32[]{:S(2)}, u32[]{:S(2)}) collective-permute-start(bf16[1024,256]{1,0:T(8,128)(2,1)S(1)} %broadcast_select_fusion.8), channel_id=1, source_target_pairs={{0,4},{1,5},{2,6},{3,7},{4,0},{5,1},{6,2},{7,3},{8,12},{9,13},{10,... | collective-permute-start | bytes 1572872 | tf_op jit(solution)/shard_map/ppermute | solution.py:68
  113.9 2.2 %collective-permute-start.21 = (bf16[1024,256]{1,0:T(8,128)(2,1)S(1)}, bf16[1024,256]{1,0:T(8,128)(2,1)S(1)}, u32[]{:S(2)}, u32[]{:S(2)}) collective-permute-start(bf16[1024,256]{1,0:T(8,128)(2,1)S(1)} %get-tuple-element.105), channel_id=1, source_target_pairs={{0,1},{1,0},{2,3},{3,2},{4,5},{5,4},{6,7},{7,6},{8,9},{9,8},{10,11... | collective-permute-start | bytes 1572872 | tf_op jit(solution)/shard_map/ppermute | solution.py:71
  125.7 2.0 %collective-permute-start.23 = (bf16[1024,256]{1,0:T(8,128)(2,1)S(1)}, bf16[1024,256]{1,0:T(8,128)(2,1)S(1)}, u32[]{:S(2)}, u32[]{:S(2)}) collective-permute-start(bf16[1024,256]{1,0:T(8,128)(2,1)S(1)} %get-tuple-element.99), channel_id=1, source_target_pairs={{0,1},{1,0},{2,3},{3,2},{4,5},{5,4},{6,7},{7,6},{8,9},{9,8},{10,11... | collective-permute-start | bytes 1572872 | tf_op jit(solution)/shard_map/ppermute | solution.py:71
  126.6 1.1 slice-start.1

commit v14 on v13

--- a/solution.py
+++ b/solution.py
@@ -122,11 +122,12 @@
         b1 = jnp.where(home, near, far)
         b1_next = step(b1)
         part0 = cross(after(sum0, x4))
-        fourth = jnp.where(home, e[1], x4)
+        near, far = together((e[1], x4), j3)
+        fourth = jnp.where(home, near, far)
         j4 = jump(fourth)
         sum1 = adjoint_of(b1, b1_next)
         part1 = cross(after(sum1, part0))
-        near, both, far = together((e[0], j3, x3), sum1, fourth)
+        near, both, far = together((e[0], j3, x3), sum1, x4)
         a0b2 = jnp.where(home, jnp.concatenate([near, both], 1), jnp.concatenate([both, far], 1))
         a0b2_next = step(a0b2)
         sum2 = adjoint_of(columns(a0b2, 1, 2), columns(after(a0b2_next, part1), 1, 2))

time: 133 us -> 126 us (0.947)
  starting transfers between devices: 34.3 us -> 26.7 us
    ppermute x8, starting transfers between devices: 20.6 us -> 8.92 us  [cross(): return lax.ppermute(a, AXES, cross_pairs)]
    ppermute x1, starting transfers between devices: 3.19 us -> 5.54 us  [home_jump(): return lax.ppermute(a, AXES, home_jump_pairs)]
    ppermute x4, waiting for transfers between devices: 13.2 us -> 15.2 us  [jump(): return lax.ppermute(a, AXES, jump_pairs)]
    ppermute x5, waiting for transfers between devices: 35.4 us -> 33.8 us  [step(): return lax.ppermute(a, AXES, step_pairs)]
    ppermute x4, starting transfers between devices: 7.79 us -> 9.23 us  [jump(): return lax.ppermute(a, AXES, jump_pairs)]
  transfers between devices with their start and end apart: 24 -> 24, of which waited for: 14 -> 14; matrix products, arithmetic and copies ran while one was open for 17% -> 18% of each run, Pallas kernels for 0% -> 0%
where the time goes in v14:
time: 126 us
  waiting for transfers between devices  72.4 us (57%)
  starting transfers between devices  26.7 us (21%)
  matrix products  16.2 us (13%)
  other arithmetic  7.64 us (6%)
  between operations  1.83 us (1%)
    ppermute x5, waiting for transfers between devices, step(): return lax.ppermute(a, AXES, step_pairs)  33.8 us
    ppermute x8, waiting for transfers between devices, cross(): return lax.ppermute(a, AXES, cross_pairs)  22.9 us
    ppermute x4, waiting for transfers between devices, jump(): return lax.ppermute(a, AXES, jump_pairs)  15.2 us
    ppermute x4, starting transfers between devices, jump(): return lax.ppermute(a, AXES, jump_pairs)  9.23 us
    dot_general x12, matrix products, tdot(): lax.dot_general(a, b, (((0,), (0,)), ((), ())), preferred_element_type=jn...  9.11 us
    ppermute x8, starting transfers between devices, cross(): return lax.ppermute(a, AXES, cross_pairs)  8.92 us
    dot_general x3, matrix products, dott(): lax.dot_general(a, b, (((1,), (1,)), ((), ())), preferred_element_type=jn...  7.05 us
    ppermute x1, starting transfers between devices, home_jump(): return lax.ppermute(a, AXES, home_jump_pairs)  5.54 us
  transfers between devices with their start and end apart: 24, of which 14 were waited for; matrix products, arithmetic and copies ran while one was open for 18% of the time, Pallas kernels for 0%

profile of v14, /device:TPU:0, one launch (start us, length us, event | category | flops | bytes accessed | tf_op | source)
XLA Modules:
  0.0 125.9 jit_solution(12412946486762644994)
XLA Ops:
  0.6 0.5 collective-permute-start
  1.2 2.6 %fusion.41 = (bf16[1024,128]{1,0:T(8,128)(2,1)S(1)}, bf16[1024,128]{1,0:T(8,128)(2,1)}, bf16[1024,128]{1,0:T(8,128)(2,1)S(1)}, bf16[1024,128]{1,0:T(8,128)(2,1)}...) fusion(bf16[1024,512]{1,0:T(8,128)(2,1)} %param.4, ...), kind=kLoop, calls=%fused_computation.89 | loop fusion | flops 131072 | bytes 3932161 | tf_op jit(solution)/shard_map/slice | solution.py:88
  3.8 2.6 %collective-permute-start.1 = (bf16[1024,128]{1,0:T(8,128)(2,1)}, bf16[1024,128]{1,0:T(8,128)(2,1)S(1)}, u32[]{:S(2)}, u32[]{:S(2)}) collective-permute-start(bf16[1024,128]{1,0:T(8,128)(2,1)} %get-tuple-element.111), channel_id=1, source_target_pairs={{0,2},{1,3},{2,0},{3,1},{4,6},{5,7},{6,4},{7,5},{8,10},{9,11},{10,... | collective-permute-start | bytes 786440 | tf_op jit(solution)/shard_map/ppermute | solution.py:65
  6.3 1.9 %broadcast_select_fusion.1 = (bf16[1024,1024]{1,0:T(8,128)(2,1)S(1)}, bf16[1024,1024]{1,0:T(8,128)(2,1)S(1)}) fusion(bf16[1024,1024]{1,0:T(8,128)(2,1)S(1)} %copy-done.3, bf16[1024,1024]{1,0:T(8,128)(2,1)} %collective-permute-done, pred[]{:T(512)S(6)} %eq.8), kind=kLoop, calls=%fused_computation.9 | loop fusion | flops 2097152 | bytes 8388609 | tf_op jit(solution)/shard_map/jit(_where)/select_n | solution.py:99
  8.3 5.1 %collective-permute-done.1 = bf16[1024,128]{1,0:T(8,128)(2,1)S(1)} collective-permute-done((bf16[1024,128]{1,0:T(8,128)(2,1)}, bf16[1024,128]{1,0:T(8,128)(2,1)S(1)}, u32[]{:S(2)}, u32[]{:S(2)}) %collective-permute-start.1) | collective-permute-done | bytes 262176 | tf_op jit(solution)/shard_map/ppermute | solution.py:65
  13.4 1.8 %collective-permute-start.3 = (bf16[1024,256]{1,0:T(8,128)(2,1)S(1)}, bf16[1024,256]{1,0:T(8,128)(2,1)S(1)}, u32[]{:S(2)}, u32[]{:S(2)}) collective-permute-start(bf16[1024,256]{1,0:T(8,128)(2,1)S(1)} %pad_maximum_fusion.1), channel_id=1, source_target_pairs={{0,2},{1,3},{2,0},{3,1},{4,6},{5,7},{6,4},{7,5},{8,10},{9,11},{10,... | collective-permute-start | bytes 1572872 | tf_op jit(solution)/shard_map/ppermute | solution.py:65
  15.3 2.7 %collective-permute-start.2 = (bf16[1024,128]{1,0:T(8,128)(2,1)S(1)}, bf16[1024,128]{1,0:T(8,128)(2,1)S(1)}, u32[]{:S(2)}, u32[]{:S(2)}) collective-permute-start(bf16[1024,128]{1,0:T(8,128)(2,1)S(1)} %broadcast_select_fusion.18), channel_id=1, source_target_pairs={{0,8},{1,9},{2,10},{3,11},{4,12},{5,13},{6,14},{7,15},{8,0},{9,1},... | collective-permute-start | bytes 786440 | tf_op jit(solution)/shard_map/ppermute | solution.py:77
  17.9 9.3 %collective-permute-done.3 = bf16[1024,256]{1,0:T(8,128)(2,1)S(1)} collective-permute-done((bf16[1024,256]{1,0:T(8,128)(2,1)S(1)}, bf16[1024,256]{1,0:T(8,128)(2,1)S(1)}, u32[]{:S(2)}, u32[]{:S(2)}) %collective-permute-start.3) | collective-permute-done | bytes 524320 | tf_op jit(solution)/shard_map/ppermute | solution.py:65
  27.3 2.1 %collective-permute-done.2 = bf16[1024,128]{1,0:T(8,128)(2,1)S(1)} collective-permute-done((bf16[1024,128]{1,0:T(8,128)(2,1)S(1)}, bf16[1024,128]{1,0:T(8,128)(2,1)S(1)}, u32[]{:S(2)}, u32[]{:S(2)}) %collective-permute-start.2) | collective-permute-done | bytes 262176 | tf_op jit(solution)/shard_map/ppermute | solution.py:77
  29.4 0.7 collective-permute-start.7
  30.2 3.4 %collective-permute-start.6 = (bf16[1024,128]{1,0:T(8,128)(2,1)S(1)}, bf16[1024,128]{1,0:T(8,128)(2,1)S(1)}, u32[]{:S(2)}, u32[]{:S(2)}) collective-permute-start(bf16[1024,128]{1,0:T(8,128)(2,1)S(1)} %get-tuple-element.122), channel_id=1, source_target_pairs={{0,8},{1,9},{2,10},{3,11},{4,12},{5,13},{6,14},{7,15},{8,0},{9,1},... | collective-permute-start | bytes 786440 | tf_op jit(solution)/shard_map/ppermute | solution.py:77
  33.6 0.6 collective-permute-start.4
  34.2 7.8 %collective-permute-done.7 = bf16[1024,128]{1,0:T(8,128)(2,1)S(1)} collective-permute-done((bf16[1024,128]{1,0:T(8,128)(2,1)S(1)}, bf16[1024,128]{1,0:T(8,128)(2,1)S(1)}, u32[]{:S(2)}, u32[]{:S(2)}) %collective-permute-start.7) | collective-permute-done | bytes 262176 | tf_op jit(solution)/shard_map/ppermute | solution.py:68
  42.0 0.7 fusion.44
  42.8 0.8 convolution_add_fusion.6
  43.6 3.4 %collective-permute-done.4 = bf16[1024,256]{1,0:T(8,128)(2,1)S(1)} collective-permute-done((bf16[1024,256]{1,0:T(8,128)(2,1)S(1)}, bf16[1024,256]{1,0:T(8,128)(2,1)S(1)}, u32[]{:S(2)}, u32[]{:S(2)}) %collective-permute-start.4) | collective-permute-done | bytes 524320 | tf_op jit(solution)/shard_map/ppermute | solution.py:65
  47.1 0.6 collective-permute-start.9
  47.7 0.4 collective-permute-start.8
  48.9 1.1 collective-permute-start.5
  50.0 3.9 %collective-permute-done.9 = bf16[1024,128]{1,0:T(8,128)(2,1)S(1)} collective-permute-done((bf16[1024,128]{1,0:T(8,128)(2,1)S(1)}, bf16[1024,128]{1,0:T(8,128)(2,1)S(1)}, u32[]{:S(2)}, u32[]{:S(2)}) %collective-permute-start.9) | collective-permute-done | bytes 262176 | tf_op jit(solution)/shard_map/ppermute | solution.py:65
  53.9 0.5 collective-permute-start.12
  54.4 3.4 %collective-permute-done.8 = bf16[1024,128]{1,0:T(8,128)(2,1)S(1)} collective-permute-done((bf16[1024,128]{1,0:T(8,128)(2,1)S(1)}, bf16[1024,128]{1,0:T(8,128)(2,1)S(1)}, u32[]{:S(2)}, u32[]{:S(2)}) %collective-permute-start.8) | collective-permute-done | bytes 262176 | tf_op jit(solution)/shard_map/ppermute | solution.py:68
  57.8 0.7 fusion.45
  58.5 0.8 convolution_add_fusion.5
  59.3 2.7 %collective-permute-done.5 = bf16[1024,128]{1,0:T(8,128)(2,1)S(1)} collective-permute-done((bf16[1024,128]{1,0:T(8,128)(2,1)S(1)}, bf16[1024,128]{1,0:T(8,128)(2,1)S(1)}, u32[]{:S(2)}, u32[]{:S(2)}) %collective-permute-start.5) | collective-permute-done | bytes 262176 | tf_op jit(solution)/shard_map/ppermute | solution.py:77
  62.0 0.2 maximum_select_fusion
  62.2 0.1 collective-permute-start.11
  62.3 0.1 constant_dynamic-update-slice_fusion.9
  62.4 0.1 constant_dynamic-update-slice_fusion.8
  62.6 2.1 %collective-permute-start.10 = (bf16[1024,128]{1,0:T(8,128)(2,1)S(1)}, bf16[1024,128]{1,0:T(8,128)(2,1)S(1)}, u32[]{:S(2)}, u32[]{:S(2)}) collective-permute-start(bf16[1024,128]{1,0:T(8,128)(2,1)S(1)} %broadcast_select_fusion.11), channel_id=1, source_target_pairs={{0,8},{1,9},{2,10},{3,11},{4,12},{5,13},{6,14},{7,15},{8,0},{9,1},... | collective-permute-start | bytes 786440 | tf_op jit(solution)/shard_map/ppermute | solution.py:77
  64.7 1.3 %collective-permute-done.12 = f32[1024,128]{1,0:T(8,128)S(1)} collective-permute-done((f32[1024,128]{1,0:T(8,128)S(1)}, f32[1024,128]{1,0:T(8,128)S(1)}, u32[]{:S(2)}, u32[]{:S(2)}) %collective-permute-start.12) | collective-permute-done | bytes 524320 | tf_op jit(solution)/shard_map/ppermute | solution.py:65
  66.0 0.5 collective-permute-start.15
  66.5 0.1 pad_maximum_fusion
  66.7 0.5 collective-permute-start.18
  67.2 0.1 constant_dynamic-update-slice_fusion.7
  67.3 0.1 constant_dynamic-update-slice_fusion.6
  67.4 10.4 %collective-permute-done.10 = bf16[1024,128]{1,0:T(8,128)(2,1)S(1)} collective-permute-done((bf16[1024,128]{1,0:T(8,128)(2,1)S(1)}, bf16[1024,128]{1,0:T(8,128)(2,1)S(1)}, u32[]{:S(2)}, u32[]{:S(2)}) %collective-permute-start.10) | collective-permute-done | bytes 262176 | tf_op jit(solution)/shard_map/ppermute | solution.py:77
  77.8 5.5 %collective-permute-start.14 = (bf16[1024,256]{1,0:T(8,128)(2,1)S(1)}, bf16[1024,256]{1,0:T(8,128)(2,1)S(1)}, u32[]{:S(2)}, u32[]{:S(2)}) collective-permute-start(bf16[1024,256]{1,0:T(8,128)(2,1)S(1)} %slice.104), channel_id=1, source_target_pairs={{0,8},{1,9},{4,12},{5,13},{10,2},{11,3},{14,6},{15,7},{16,24},{17,... | collective-permute-start | bytes 1572872 | tf_op jit(solution)/shard_map/ppermute | solution.py:74
  83.4 0.2 maximum_select_fusion.1
  83.6 0.8 fusion.32
  84.4 0.8 convolution_add_fusion.4
  85.5 0.1 constant_dynamic-update-slice_fusion
  85.6 0.1 broadcast_select_fusion.3
  85.9 0.1 fusion.39
  86.0 0.1 fusion.40
  86.1 17.1 %collective-permute-done.13 = bf16[1024,256]{1,0:T(8,128)(2,1)S(1)} collective-permute-done((bf16[1024,256]{1,0:T(8,128)(2,1)S(1)}, bf16[1024,256]{1,0:T(8,128)(2,1)S(1)}, u32[]{:S(2)}, u32[]{:S(2)}) %collective-permute-start.13) | collective-permute-done | bytes 524320 | tf_op jit(solution)/shard_map/ppermute | solution.py:68
  103.2 0.8 fusion.30
  104.0 0.8 convolution_add_fusion.3
  104.8 2.2 %collective-permute-start.22 = (f32[1024,128]{1,0:T(8,128)S(1)}, f32[1024,128]{1,0:T(8,128)S(1)}, u32[]{:S(2)}, u32[]{:S(2)}) collective-permute-start(f32[1024,128]{1,0:T(8,128)S(1)} %convolution_add_fusion.3), channel_id=1, source_target_pairs={{0,2},{1,3},{2,0},{3,1},{4,6},{5,7},{6,4},{7,5},{8,10},{9,11},{10,... | collective-permute-start | bytes 1572872 | tf_op jit(solution)/shard_map/ppermute | solution.py:65
  107.0 2.4 %fusion = f32[1024,1024]{1,0:T(8,128)S(1)} fusion(bf16[1024,1024]{1,0:T(8,128)(2,1)S(1)} %get-tuple-element.107, bf16[1024,512]{1,0:T(8,128)(2,1)S(1)} %collective-permute-done.16, bf16[1024,512]{1,0:T(8,128)(2,1)S(1)} %get-tuple-element.100), kind=kOutput, calls=%fused_computation.2 | convolution fusion | flops 2151677952 | bytes 8388608 | tf_op jit(solution)/shard_map/dot_general | solution.py:38
  109.5 0.1 broadcast_select_fusion.7
  109.6 0.4 collective-permute-start.20
  110.0 0.3 slice-done
  110.3 0.7 fusion.24
  111.1 0.8 convolution_add_fusion.2
  111.8 0.1 collective-permute-done.21
  111.9 1.4 %convolution_add_fusion = f32[1024,1024]{1,0:T(8,128)S(1)} fusion(f32[1024,1024]{1,0:T(8,128)S(1)} %fusion, bf16[1024,256]{1,0:T(8,128)(2,1)S(1)} %collective-permute-done.21, bf16[1024,256]{1,0:T(8,128)(2,1)S(1)} %get-tuple-element.108, bf16[1024,128]{1,0:T(8,128)(2,1)S(1)} %get-tuple-element.106, bf16[1024,128]{1,0:T(8,128)(2,1)S(1)} %get-tuple-element.104, ...), kind=kOutput, calls=%fused_computation.1 | convolution fusion | flops 1081081856 | bytes 10485760 | tf_op jit(solution)/shard_map/dot_general | solution.py:38
  113.3 5.5 %collective-permute-done.20 = bf16[1024,256]{1,0:T(8,128)(2,1)S(1)} collective-permute-done((bf16[1024,256]{1,0:T(8,128)(2,1)S(1)}, bf16[1024,256]{1,0:T(8,128)(2,1)S(1)}, u32[]{:S(2)}, u32[]{:S(2)}) %collective-permute-start.20) | collective-permute-done | bytes 524320 | tf_op jit(solution)/shard_map/ppermute | solution.py:68
  118.8 0.1 broadcast_select_fusion.5
  119.0 0.8 fusion.46
  119.8 0.8 convolution_add_fusion.1
  120.5 0.3 collective-permute-done.23
  120.9 3.3 %add_multiply_fusion = f32[1024,1024]{1,0:T(8,128)} fusion(f32[1024,1024]{1,0:T(8,128)S(1)} %convolution_add_fusion, f32[]{:T(128)} %bitcast, bf16[1024,256]{1,0:T(8,128)(2,1)S(1)} %collective-permute-done.23, bf16[1024,256]{1,0:T(8,128)(2,1)S(1)} %get-tuple-element.102, bf16[1024,256]{1,0:T(8,128)(2,1)S(1)} %slice-done.1, bf16[1024,256]{1,0:T(8,128)(2,1)S(1)} %slice.119), kind=kOutput, calls=%fused_computation | convolution fusion | flops 1080033280 | bytes 10485764 | tf_op jit(solution)/shard_map/dot_general | solution.py:38
  124.2 1.7 %fusion.4 = f32[1024,512]{1,0:T(8,128)} fusion(f32[1024,256]{1,0:T(8,128)S(1)} %convolution_add_fusion.1, f32[1024,256]{1,0:T(8,128)S(1)} %convolution_add_fusion.2, f32[1024,128]{1,0:T(8,128)S(1)} %collective-permute-done.22, f32[1024,128]{1,0:T(8,128)S(1)} %collective-permute-done.19, f32[1024,128]{1,0:T(8,128)S(1)} %collective-permute-done.15, ...), kind=kLoop, calls=%fused_computation.7 | loop fusion | flops 3145728 | bytes 6291460 | tf_op jit(solution)/shard_map/mul | solution.py:175
  (57 shorter events, 1.3 us)
Async XLA Ops:
  0.6 5.7 %copy-start.3 = (bf16[1024,1024]{1,0:T(8,128)(2,1)S(1)}, bf16[1024,1024]{1,0:T(8,128)(2,1)}, u32[]{:S(2)}) copy-start(bf16[1024,1024]{1,0:T(8,128)(2,1)} %param.6) | copy-start | bytes 6291460
  0.6 5.7 %collective-permute-start = (bf16[1024,1024]{1,0:T(8,128)(2,1)}, bf16[1024,1024]{1,0:T(8,128)(2,1)}, u32[]{:S(2)}, u32[]{:S(2)}) collective-permute-start(bf16[1024,1024]{1,0:T(8,128)(2,1)} %param.6), channel_id=1, source_target_pairs={{0,1},{1,0},{2,3},{3,2},{4,5},{5,4},{6,7},{7,6},{8,9},{9,8},{10,11... | collective-permute-start | bytes 6291464 | tf_op jit(solution)/shard_map/ppermute | solution.py:71
  3.8 9.6 %collective-permute-start.1 = (bf16[1024,128]{1,0:T(8,128)(2,1)}, bf16[1024,128]{1,0:T(8,128)(2,1)S(1)}, u32[]{:S(2)}, u32[]{:S(2)}) collective-permute-start(bf16[1024,128]{1,0:T(8,128)(2,1)} %get-tuple-element.111), channel_id=1, source_target_pairs={{0,2},{1,3},{2,0},{3,1},{4,6},{5,7},{6,4},{7,5},{8,10},{9,11},{10,... | collective-permute-start | bytes 786440 | tf_op jit(solution)/shard_map/ppermute | solution.py:65
  6.3 7.1 %copy-start.7 = (bf16[1024,128]{1,0:T(8,128)(2,1)S(1)}, bf16[1024,128]{1,0:T(8,128)(2,1)}, u32[]{:S(2)}) copy-start(bf16[1024,128]{1,0:T(8,128)(2,1)} %get-tuple-element.113) | copy-start | bytes 786436
  6.3 8.9 %copy-start.6 = (bf16[1024,128]{1,0:T(8,128)(2,1)S(1)}, bf16[1024,128]{1,0:T(8,128)(2,1)}, u32[]{:S(2)}) copy-start(bf16[1024,128]{1,0:T(8,128)(2,1)} %get-tuple-element.48) | copy-start | bytes 786436
  8.3 18.9 %copy-start = (bf16[1024,512]{1,0:T(8,128)(2,1)S(1)}, bf16[1024,512]{1,0:T(8,128)(2,1)}, u32[]{:S(2)}) copy-start(bf16[1024,512]{1,0:T(8,128)(2,1)} %param.4) | copy-start | bytes 3145732
  13.3 16.0 %copy-start.5 = (bf16[1024,128]{1,0:T(8,128)(2,1)S(1)}, bf16[1024,128]{1,0:T(8,128)(2,1)}, u32[]{:S(2)}) copy-start(bf16[1024,128]{1,0:T(8,128)(2,1)} %get-tuple-element.52) | copy-start | bytes 786436
  13.4 13.8 %collective-permute-start.3 = (bf16[1024,256]{1,0:T(8,128)(2,1)S(1)}, bf16[1024,256]{1,0:T(8,128)(2,1)S(1)}, u32[]{:S(2)}, u32[]{:S(2)}) collective-permute-start(bf16[1024,256]{1,0:T(8,128)(2,1)S(1)} %pad_maximum_fusion.1), channel_id=1, source_target_pairs={{0,2},{1,3},{2,0},{3,1},{4,6},{5,7},{6,4},{7,5},{8,10},{9,11},{10,... | collective-permute-start | bytes 1572872 | tf_op jit(solution)/shard_map/ppermute | solution.py:65
  15.3 14.1 %collective-permute-start.2 = (bf16[1024,128]{1,0:T(8,128)(2,1)S(1)}, bf16[1024,128]{1,0:T(8,128)(2,1)S(1)}, u32[]{:S(2)}, u32[]{:S(2)}) collective-permute-start(bf16[1024,128]{1,0:T(8,128)(2,1)S(1)} %broadcast_select_fusion.18), channel_id=1, source_target_pairs={{0,8},{1,9},{2,10},{3,11},{4,12},{5,13},{6,14},{7,15},{8,0},{9,1},... | collective-permute-start | bytes 786440 | tf_op jit(solution)/shard_map/ppermute | solution.py:77
  29.4 12.6 %collective-permute-start.7 = (bf16[1024,128]{1,0:T(8,128)(2,1)S(1)}, bf16[1024,128]{1,0:T(8,128)(2,1)S(1)}, u32[]{:S(2)}, u32[]{:S(2)}) collective-permute-start(bf16[1024,128]{1,0:T(8,128)(2,1)S(1)} %broadcast_select_fusion.14), channel_id=1, source_target_pairs={{0,4},{1,5},{2,6},{3,7},{4,0},{5,1},{6,2},{7,3},{8,12},{9,13},{10,... | collective-permute-start | bytes 786440 | tf_op jit(solution)/shard_map/ppermute | solution.py:68
  30.2 16.9 %collective-permute-start.6 = (bf16[1024,128]{1,0:T(8,128)(2,1)S(1)}, bf16[1024,128]{1,0:T(8,128)(2,1)S(1)}, u32[]{:S(2)}, u32[]{:S(2)}) collective-permute-start(bf16[1024,128]{1,0:T(8,128)(2,1)S(1)} %get-tuple-element.122), channel_id=1, source_target_pairs={{0,8},{1,9},{2,10},{3,11},{4,12},{5,13},{6,14},{7,15},{8,0},{9,1},... | collective-permute-start | bytes 786440 | tf_op jit(solution)/shard_map/ppermute | solution.py:77
  33.6 13.4 %collective-permute-start.4 = (bf16[1024,256]{1,0:T(8,128)(2,1)S(1)}, bf16[1024,256]{1,0:T(8,128)(2,1)S(1)}, u32[]{:S(2)}, u32[]{:S(2)}) collective-permute-start(bf16[1024,256]{1,0:T(8,128)(2,1)S(1)} %pad_maximum_fusion.2), channel_id=1, source_target_pairs={{0,2},{1,3},{2,0},{3,1},{4,6},{5,7},{6,4},{7,5},{8,10},{9,11},{10,... | collective-permute-start | bytes 1572872 | tf_op jit(solution)/shard_map/ppermute | solution.py:65
  43.5 4.6 %copy-start.1 = (bf16[1024,512]{1,0:T(8,128)(2,1)S(1)}, bf16[1024,512]{1,0:T(8,128)(2,1)}, u32[]{:S(2)}) copy-start(bf16[1024,512]{1,0:T(8,128)(2,1)} %param.5) | copy-start | bytes 3145732
  47.1 6.8 %collective-permute-start.9 = (bf16[1024,128]{1,0:T(8,128)(2,1)S(1)}, bf16[1024,128]{1,0:T(8,128)(2,1)S(1)}, u32[]{:S(2)}, u32[]{:S(2)}) collective-permute-start(bf16[1024,128]{1,0:T(8,128)(2,1)S(1)} %broadcast_select_fusion.12), channel_id=1, source_target_pairs={{0,2},{1,3},{2,0},{3,1},{4,6},{5,7},{6,4},{7,5},{8,10},{9,11},{10,... | collective-permute-start | bytes 786440 | tf_op jit(solution)/shard_map/ppermute | solution.py:65
  47.7 10.1 %collective-permute-start.8 = (bf16[1024,128]{1,0:T(8,128)(2,1)S(1)}, bf16[1024,128]{1,0:T(8,128)(2,1)S(1)}, u32[]{:S(2)}, u32[]{:S(2)}) collective-permute-start(bf16[1024,128]{1,0:T(8,128)(2,1)S(1)} %broadcast_select_fusion.13), channel_id=1, source_target_pairs={{0,4},{1,5},{2,6},{3,7},{4,0},{5,1},{6,2},{7,3},{8,12},{9,13},{10,... | collective-permute-start | bytes 786440 | tf_op jit(solution)/shard_map/ppermute | solution.py:68
  48.9 13.1 %collective-permute-start.5 = (bf16[1024,128]{1,0:T(8,128)(2,1)S(1)}, bf16[1024,128]{1,0:T(8,128)(2,1)S(1)}, u32[]{:S(2)}, u32[]{:S(2)}) collective-permute-start(bf16[1024,128]{1,0:T(8,128)(2,1)S(1)} %get-tuple-element.119), channel_id=1, source_target_pairs={{0,8},{1,9},{2,10},{3,11},{4,12},{5,13},{6,14},{7,15},{8,0},{9,1},... | collective-permute-start | bytes 786440 | tf_op jit(solution)/shard_map/ppermute | solution.py:77
  53.9 12.1 %collective-permute-start.12 = (f32[1024,128]{1,0:T(8,128)S(1)}, f32[1024,128]{1,0:T(8,128)S(1)}, u32[]{:S(2)}, u32[]{:S(2)}) collective-permute-start(f32[1024,128]{1,0:T(8,128)S(1)} %convolution_add_fusion.6), channel_id=1, source_target_pairs={{0,2},{1,3},{2,0},{3,1},{4,6},{5,7},{6,4},{7,5},{8,10},{9,11},{10,... | collective-permute-start | bytes 1572872 | tf_op jit(solution)/shard_map/ppermute | solution.py:65
  62.2 21.1 %collective-permute-start.11 = (bf16[1024,256]{1,0:T(8,128)(2,1)S(1)}, bf16[1024,256]{1,0:T(8,128)(2,1)S(1)}, u32[]{:S(2)}, u32[]{:S(2)}) collective-permute-start(bf16[1024,256]{1,0:T(8,128)(2,1)S(1)} %maximum_select_fusion), channel_id=1, source_target_pairs={{0,4},{1,5},{2,6},{3,7},{4,0},{5,1},{6,2},{7,3},{8,12},{9,13},{10,... | collective-permute-start | bytes 1572872 | tf_op jit(solution)/shard_map/ppermute | solution.py:68
  62.6 15.2 %collective-permute-start.10 = (bf16[1024,128]{1,0:T(8,128)(2,1)S(1)}, bf16[1024,128]{1,0:T(8,128)(2,1)S(1)}, u32[]{:S(2)}, u32[]{:S(2)}) collective-permute-start(bf16[1024,128]{1,0:T(8,128)(2,1)S(1)} %broadcast_select_fusion.11), channel_id=1, source_target_pairs={{0,8},{1,9},{2,10},{3,11},{4,12},{5,13},{6,14},{7,15},{8,0},{9,1},... | collective-permute-start | bytes 786440 | tf_op jit(solution)/shard_map/ppermute | solution.py:77
  66.0 17.7 %collective-permute-start.15 = (f32[1024,128]{1,0:T(8,128)S(1)}, f32[1024,128]{1,0:T(8,128)S(1)}, u32[]{:S(2)}, u32[]{:S(2)}) collective-permute-start(f32[1024,128]{1,0:T(8,128)S(1)} %convolution_add_fusion.5), channel_id=1, source_target_pairs={{0,2},{1,3},{2,0},{3,1},{4,6},{5,7},{6,4},{7,5},{8,10},{9,11},{10,... | collective-permute-start | bytes 1572872 | tf_op jit(solution)/shard_map/ppermute | solution.py:65
  66.6 19.1 %collective-permute-start.17 = (bf16[1024,512]{1,0:T(8,128)(2,1)S(1)}, bf16[1024,512]{1,0:T(8,128)(2,1)S(1)}, u32[]{:S(2)}, u32[]{:S(2)}) collective-permute-start(bf16[1024,512]{1,0:T(8,128)(2,1)S(1)} %pad_maximum_fusion), channel_id=1, source_target_pairs={{0,1},{1,0},{2,3},{3,2},{4,5},{5,4},{6,7},{7,6},{8,9},{9,8},{10,11... | collective-permute-start | bytes 3145736 | tf_op jit(solution)/shard_map/ppermute | solution.py:71
  66.7 19.2 %collective-permute-start.18 = (bf16[1024,512]{1,0:T(8,128)(2,1)S(1)}, bf16[1024,512]{1,0:T(8,128)(2,1)S(1)}, u32[]{:S(2)}, u32[]{:S(2)}) collective-permute-start(bf16[1024,512]{1,0:T(8,128)(2,1)S(1)} %copy-done.1), channel_id=1, source_target_pairs={{0,1},{1,0},{2,3},{3,2},{4,5},{5,4},{6,7},{7,6},{8,9},{9,8},{10,11... | collective-permute-start | bytes 3145736 | tf_op jit(solution)/shard_map/ppermute | solution.py:71
  77.8 31.6 %collective-permute-start.14 = (bf16[1024,256]{1,0:T(8,128)(2,1)S(1)}, bf16[1024,256]{1,0:T(8,128)(2,1)S(1)}, u32[]{:S(2)}, u32[]{:S(2)}) collective-permute-start(bf16[1024,256]{1,0:T(8,128)(2,1)S(1)} %slice.104), channel_id=1, source_target_pairs={{0,8},{1,9},{4,12},{5,13},{10,2},{11,3},{14,6},{15,7},{16,24},{17,... | collective-permute-start | bytes 1572872 | tf_op jit(solution)/shard_map/ppermute | solution.py:74
  83.3 2.2 %copy-start.2 = (bf16[1024,256]{1,0:T(8,128)(2,1)}, bf16[1024,256]{1,0:T(8,128)(2,1)S(1)}, u32[]{:S(2)}) copy-start(bf16[1024,256]{1,0:T(8,128)(2,1)S(1)} %collective-permute-done.11) | copy-start | bytes 1572868
  83.5 19.7 %collective-permute-start.13 = (bf16[1024,256]{1,0:T(8,128)(2,1)S(1)}, bf16[1024,256]{1,0:T(8,128)(2,1)S(1)}, u32[]{:S(2)}, u32[]{:S(2)}) collective-permute-start(bf16[1024,256]{1,0:T(8,128)(2,1)S(1)} %maximum_select_fusion.1), channel_id=1, source_target_pairs={{0,4},{1,5},{2,6},{3,7},{4,0},{5,1},{6,2},{7,3},{8,12},{9,13},{10,... | collective-permute-start | bytes 1572872 | tf_op jit(solution)/shard_map/ppermute | solution.py:68
  85.2 18.0 %collective-permute-start.19 = (f32[1024,128]{1,0:T(8,128)S(1)}, f32[1024,128]{1,0:T(8,128)S(1)}, u32[]{:S(2)}, u32[]{:S(2)}) collective-permute-start(f32[1024,128]{1,0:T(8,128)S(1)} %convolution_add_fusion.4), channel_id=1, source_target_pairs={{0,2},{1,3},{2,0},{3,1},{4,6},{5,7},{6,4},{7,5},{8,10},{9,11},{10,... | collective-permute-start | bytes 1572872 | tf_op jit(solution)/shard_map/ppermute | solution.py:65
  85.8 21.2 %collective-permute-start.16 = (bf16[1024,512]{1,0:T(8,128)(2,1)S(1)}, bf16[1024,512]{1,0:T(8,128)(2,1)S(1)}, u32[]{:S(2)}, u32[]{:S(2)}) collective-permute-start(bf16[1024,512]{1,0:T(8,128)(2,1)S(1)} %get-tuple-element.101), channel_id=1, source_target_pairs={{0,1},{1,0},{2,3},{3,2},{4,5},{5,4},{6,7},{7,6},{8,9},{9,8},{10,11... | collective-permute-start | bytes 3145736 | tf_op jit(solution)/shard_map/ppermute | solution.py:71
  85.9 18.1 %copy-start.4 = (bf16[1024,512]{1,0:T(8,128)(2,1)}, bf16[1024,512]{1,0:T(8,128)(2,1)S(1)}, u32[]{:S(2)}) copy-start(bf16[1024,512]{1,0:T(8,128)(2,1)S(1)} %collective-permute-done.18) | copy-start | bytes 3145732
  104.8 19.4 %collective-permute-start.22 = (f32[1024,128]{1,0:T(8,128)S(1)}, f32[1024,128]{1,0:T(8,128)S(1)}, u32[]{:S(2)}, u32[]{:S(2)}) collective-permute-start(f32[1024,128]{1,0:T(8,128)S(1)} %convolution_add_fusion.3), channel_id=1, source_target_pairs={{0,2},{1,3},{2,0},{3,1},{4,6},{5,7},{6,4},{7,5},{8,10},{9,11},{10,... | collective-permute-start | bytes 1572872 | tf_op jit(solution)/shard_map/ppermute | solution.py:65
  109.4 1.0 slice-start
  109.6 9.2 %collective-permute-start.20 = (bf16[1024,256]{1,0:T(8,128)(2,1)S(1)}, bf16[1024,256]{1,0:T(8,128)(2,1)S(1)}, u32[]{:S(2)}, u32[]{:S(2)}) collective-permute-start(bf16[1024,256]{1,0:T(8,128)(2,1)S(1)} %broadcast_select_fusion.8), channel_id=1, source_target_pairs={{0,4},{1,5},{2,6},{3,7},{4,0},{5,1},{6,2},{7,3},{8,12},{9,13},{10,... | collective-permute-start | bytes 1572872 | tf_op jit(solution)/shard_map/ppermute | solution.py:68
  110.0 1.9 %collective-permute-start.21 = (bf16[1024,256]{1,0:T(8,128)(2,1)S(1)}, bf16[1024,256]{1,0:T(8,128)(2,1)S(1)}, u32[]{:S(2)}, u32[]{:S(2)}) collective-permute-start(bf16[1024,256]{1,0:T(8,128)(2,1)S(1)} %get-tuple-element.109), channel_id=1, source_target_pairs={{0,1},{1,0},{2,3},{3,2},{4,5},{5,4},{6,7},{7,6},{8,9},{9,8},{10,11... | collective-permute-start | bytes 1572872 | tf_op jit(solution)/shard_map/ppermute | solution.py:71
  118.9 2.0 %collective-permute-start.23 = (bf16[1024,256]{1,0:T(8,128)(2,1)S(1)}, bf16[1024,256]{1,0:T(8,128)(2,1)S(1)}, u32[]{:S(2)}, u32[]{:S(2)}) collective-permute-start(bf16[1024,256]{1,0:T(8,128)(2,1)S(1)} %get-tuple-element.103), channel_id=1, source_target_pairs={{0,1},{1,0},{2,3},{3,2},{4,5},{5,4},{6,7},{7,6},{8,9},{9,8},{10,11... | collective-permute-start | bytes 1572872 | tf_op jit(solution)/shard_map/ppermute | solution.py:71
  119.7 1.1 slice-start.1

commit v15 on v11

--- a/solution.py
+++ b/solution.py
@@ -102,13 +102,14 @@
             return tdot(t_near, near) + tdot(t_next, far)
 
         v1, e1 = together((v[1], e[1]), x1, t_near)
-        x2 = cross(jnp.concatenate([jnp.where(home, v1, e1), v[2], v[3]], 1))
-        x2, v_across2, v_across3 = columns(x2, 0, 1), columns(x2, 1, 2), columns(x2, 2, 3)
+        x2 = cross(jnp.concatenate([jnp.where(home, v1, e1), v[2]], 1))
+        x2, v_across2 = columns(x2, 0, 1), columns(x2, 1, 2)
         second = jnp.where(home, x2, e[3])
         j2 = jump(second)
         near, far = together((j1, v[0]), second)
         third_cross = jnp.where(home, near, far)
-        x3 = cross(third_cross)
+        x3 = cross(jnp.concatenate([third_cross, v[3]], 1))
+        x3, v_across3 = columns(x3, 0, 1), columns(x3, 1, 2)
         near, far = together((x1, j1), third_cross)
         b0 = jnp.where(home, near, far)
         b0_next = step(b0)

time: 122 us -> 122 us (level); the launches traced: 120 us -> 122 us
  waiting for transfers between devices: 58.5 us -> 62.7 us
  starting transfers between devices: 33.8 us -> 32.2 us
  local copies, waits for them, and re-layouts: 2.26 us -> 0.77 us
    ppermute x5, waiting for transfers between devices: 21.9 us -> 31.1 us  [step(): return lax.ppermute(a, AXES, step_pairs)]
    ppermute x5, starting transfers between devices: 9.98 us -> 3.84 us  [step(): return lax.ppermute(a, AXES, step_pairs)]
    ppermute x8, starting transfers between devices: 8.89 us -> 14.4 us  [cross(): return lax.ppermute(a, AXES, cross_pairs)]
    ppermute x4, waiting for transfers between devices: 5.85 us -> 3.06 us  [jump(): return lax.ppermute(a, AXES, jump_pairs)]
    ppermute x4, starting transfers between devices: 10.9 us -> 9.25 us  [jump(): return lax.ppermute(a, AXES, jump_pairs)]
    unnamed x8 -> x14, local copies, waits for them, and re-layouts: 1.68 us -> 0.2 us
    ppermute x8, waiting for transfers between devices: 25.4 us -> 24.1 us  [cross(): return lax.ppermute(a, AXES, cross_pairs)]
    slice x2 -> x3, other arithmetic: 1.47 us -> 2.71 us  [columns(): return array[:, start * quarter:stop * quarter]]
where the time goes in v15:
time: 122 us
  waiting for transfers between devices  62.7 us (51%)
  starting transfers between devices  32.2 us (26%)
  matrix products  16 us (13%)
  other arithmetic  8.43 us (7%)
  between operations  1.76 us (1%)
    ppermute x5, waiting for transfers between devices, step(): return lax.ppermute(a, AXES, step_pairs)  31.1 us
    ppermute x8, waiting for transfers between devices, cross(): return lax.ppermute(a, AXES, cross_pairs)  24.1 us
    ppermute x8, starting transfers between devices, cross(): return lax.ppermute(a, AXES, cross_pairs)  14.4 us
    ppermute x4, starting transfers between devices, jump(): return lax.ppermute(a, AXES, jump_pairs)  9.25 us
    dot_general x12, matrix products, tdot(): lax.dot_general(a, b, (((0,), (0,)), ((), ())), preferred_element_type=jn...  9.05 us
    dot_general x3, matrix products, dott(): lax.dot_general(a, b, (((1,), (1,)), ((), ())), preferred_element_type=jn...  6.94 us
    ppermute x1, waiting for transfers between devices, home_jump(): return lax.ppermute(a, AXES, home_jump_pairs)  3.99 us
    ppermute x5, starting transfers between devices, step(): return lax.ppermute(a, AXES, step_pairs)  3.84 us
  transfers between devices with their start and end apart: 24, of which 13 were waited for; matrix products, arithmetic and copies ran while one was open for 19% of the time, Pallas kernels for 0%

profile of v15, /device:TPU:0, one launch (start us, length us, event | category | flops | bytes accessed | tf_op | source)
XLA Modules:
  0.0 121.8 jit_solution(9516446386949348511)
XLA Ops:
  0.6 0.5 collective-permute-start
  1.2 2.6 %fusion.35 = (bf16[1024,128]{1,0:T(8,128)(2,1)S(1)}, bf16[1024,128]{1,0:T(8,128)(2,1)}, bf16[1024,128]{1,0:T(8,128)(2,1)S(1)}, bf16[1024,128]{1,0:T(8,128)(2,1)}...) fusion(bf16[1024,512]{1,0:T(8,128)(2,1)} %param.4, ...), kind=kLoop, calls=%fused_computation.76 | loop fusion | flops 131072 | bytes 3932161 | tf_op jit(solution)/shard_map/slice | solution.py:88
  3.8 2.6 %collective-permute-start.1 = (bf16[1024,128]{1,0:T(8,128)(2,1)}, bf16[1024,128]{1,0:T(8,128)(2,1)S(1)}, u32[]{:S(2)}, u32[]{:S(2)}) collective-permute-start(bf16[1024,128]{1,0:T(8,128)(2,1)} %get-tuple-element.103), channel_id=1, source_target_pairs={{0,2},{1,3},{2,0},{3,1},{4,6},{5,7},{6,4},{7,5},{8,10},{9,11},{10,... | collective-permute-start | bytes 786440 | tf_op jit(solution)/shard_map/ppermute | solution.py:65
  6.3 1.9 %broadcast_select_fusion.1 = (bf16[1024,1024]{1,0:T(8,128)(2,1)S(1)}, bf16[1024,1024]{1,0:T(8,128)(2,1)S(1)}) fusion(bf16[1024,1024]{1,0:T(8,128)(2,1)S(1)} %copy-done.2, bf16[1024,1024]{1,0:T(8,128)(2,1)} %collective-permute-done, pred[]{:T(512)S(6)} %eq.8), kind=kLoop, calls=%fused_computation.8 | loop fusion | flops 2097152 | bytes 8388609 | tf_op jit(solution)/shard_map/jit(_where)/select_n | solution.py:99
  8.3 5.1 %collective-permute-done.1 = bf16[1024,128]{1,0:T(8,128)(2,1)S(1)} collective-permute-done((bf16[1024,128]{1,0:T(8,128)(2,1)}, bf16[1024,128]{1,0:T(8,128)(2,1)S(1)}, u32[]{:S(2)}, u32[]{:S(2)}) %collective-permute-start.1) | collective-permute-done | bytes 262176 | tf_op jit(solution)/shard_map/ppermute | solution.py:65
  13.4 1.8 %collective-permute-start.3 = (bf16[1024,256]{1,0:T(8,128)(2,1)S(1)}, bf16[1024,256]{1,0:T(8,128)(2,1)S(1)}, u32[]{:S(2)}, u32[]{:S(2)}) collective-permute-start(bf16[1024,256]{1,0:T(8,128)(2,1)S(1)} %pad_maximum_fusion.3), channel_id=1, source_target_pairs={{0,2},{1,3},{2,0},{3,1},{4,6},{5,7},{6,4},{7,5},{8,10},{9,11},{10,... | collective-permute-start | bytes 1572872 | tf_op jit(solution)/shard_map/ppermute | solution.py:65
  15.3 2.7 %collective-permute-start.2 = (bf16[1024,128]{1,0:T(8,128)(2,1)S(1)}, bf16[1024,128]{1,0:T(8,128)(2,1)S(1)}, u32[]{:S(2)}, u32[]{:S(2)}) collective-permute-start(bf16[1024,128]{1,0:T(8,128)(2,1)S(1)} %broadcast_select_fusion.18), channel_id=1, source_target_pairs={{0,8},{1,9},{2,10},{3,11},{4,12},{5,13},{6,14},{7,15},{8,0},{9,1},... | collective-permute-start | bytes 786440 | tf_op jit(solution)/shard_map/ppermute | solution.py:77
  17.9 9.3 %collective-permute-done.3 = bf16[1024,256]{1,0:T(8,128)(2,1)S(1)} collective-permute-done((bf16[1024,256]{1,0:T(8,128)(2,1)S(1)}, bf16[1024,256]{1,0:T(8,128)(2,1)S(1)}, u32[]{:S(2)}, u32[]{:S(2)}) %collective-permute-start.3) | collective-permute-done | bytes 524320 | tf_op jit(solution)/shard_map/ppermute | solution.py:65
  27.3 2.1 %collective-permute-done.2 = bf16[1024,128]{1,0:T(8,128)(2,1)S(1)} collective-permute-done((bf16[1024,128]{1,0:T(8,128)(2,1)S(1)}, bf16[1024,128]{1,0:T(8,128)(2,1)S(1)}, u32[]{:S(2)}, u32[]{:S(2)}) %collective-permute-start.2) | collective-permute-done | bytes 262176 | tf_op jit(solution)/shard_map/ppermute | solution.py:77
  29.4 0.7 collective-permute-start.4
  30.2 3.4 %collective-permute-start.5 = (bf16[1024,128]{1,0:T(8,128)(2,1)S(1)}, bf16[1024,128]{1,0:T(8,128)(2,1)S(1)}, u32[]{:S(2)}, u32[]{:S(2)}) collective-permute-start(bf16[1024,128]{1,0:T(8,128)(2,1)S(1)} %get-tuple-element.122), channel_id=1, source_target_pairs={{0,8},{1,9},{2,10},{3,11},{4,12},{5,13},{6,14},{7,15},{8,0},{9,1},... | collective-permute-start | bytes 786440 | tf_op jit(solution)/shard_map/ppermute | solution.py:77
  33.6 0.6 collective-permute-start.6
  34.2 7.8 %collective-permute-done.4 = bf16[1024,128]{1,0:T(8,128)(2,1)S(1)} collective-permute-done((bf16[1024,128]{1,0:T(8,128)(2,1)S(1)}, bf16[1024,128]{1,0:T(8,128)(2,1)S(1)}, u32[]{:S(2)}, u32[]{:S(2)}) %collective-permute-start.4) | collective-permute-done | bytes 262176 | tf_op jit(solution)/shard_map/ppermute | solution.py:68
  42.0 0.7 fusion.42
  42.8 0.8 convolution_add_fusion.5
  43.5 3.4 %collective-permute-done.6 = bf16[1024,256]{1,0:T(8,128)(2,1)S(1)} collective-permute-done((bf16[1024,256]{1,0:T(8,128)(2,1)S(1)}, bf16[1024,256]{1,0:T(8,128)(2,1)S(1)}, u32[]{:S(2)}, u32[]{:S(2)}) %collective-permute-start.6) | collective-permute-done | bytes 524320 | tf_op jit(solution)/shard_map/ppermute | solution.py:65
  47.1 0.6 collective-permute-start.9
  47.7 0.4 collective-permute-start.7
  48.1 1.0 collective-permute-start.8
  49.1 4.7 %collective-permute-done.9 = bf16[1024,128]{1,0:T(8,128)(2,1)S(1)} collective-permute-done((bf16[1024,128]{1,0:T(8,128)(2,1)S(1)}, bf16[1024,128]{1,0:T(8,128)(2,1)S(1)}, u32[]{:S(2)}, u32[]{:S(2)}) %collective-permute-start.9) | collective-permute-done | bytes 262176 | tf_op jit(solution)/shard_map/ppermute | solution.py:65
  53.9 0.5 collective-permute-start.12
  54.4 4.2 %collective-permute-done.7 = bf16[1024,128]{1,0:T(8,128)(2,1)S(1)} collective-permute-done((bf16[1024,128]{1,0:T(8,128)(2,1)S(1)}, bf16[1024,128]{1,0:T(8,128)(2,1)S(1)}, u32[]{:S(2)}, u32[]{:S(2)}) %collective-permute-start.7) | collective-permute-done | bytes 262176 | tf_op jit(solution)/shard_map/ppermute | solution.py:68
  58.6 0.7 fusion.43
  59.4 0.8 convolution_add_fusion.4
  60.2 1.0 collective-permute-done.8
  61.2 0.2 maximum_select_fusion
  61.4 0.1 collective-permute-start.10
  62.3 2.2 %collective-permute-start.11 = (bf16[1024,128]{1,0:T(8,128)(2,1)S(1)}, bf16[1024,128]{1,0:T(8,128)(2,1)S(1)}, u32[]{:S(2)}, u32[]{:S(2)}) collective-permute-start(bf16[1024,128]{1,0:T(8,128)(2,1)S(1)} %broadcast_select_fusion.11), channel_id=1, source_target_pairs={{0,8},{1,9},{2,10},{3,11},{4,12},{5,13},{6,14},{7,15},{8,0},{9,1},... | collective-permute-start | bytes 786440 | tf_op jit(solution)/shard_map/ppermute | solution.py:77
  64.4 2.9 %collective-permute-start.16 = (bf16[1024,256]{1,0:T(8,128)(2,1)S(1)}, bf16[1024,256]{1,0:T(8,128)(2,1)S(1)}, u32[]{:S(2)}, u32[]{:S(2)}) collective-permute-start(bf16[1024,256]{1,0:T(8,128)(2,1)S(1)} %slice.98), channel_id=1, source_target_pairs={{0,8},{1,9},{4,12},{5,13},{10,2},{11,3},{14,6},{15,7},{16,24},{17,... | collective-permute-start | bytes 1572872 | tf_op jit(solution)/shard_map/ppermute | solution.py:74
  67.4 0.1 constant_dynamic-update-slice_fusion.4
  67.4 0.1 constant_dynamic-update-slice_fusion.3
  67.6 0.1 collective-permute-start.14
  67.7 10.9 %collective-permute-done.10 = bf16[1024,256]{1,0:T(8,128)(2,1)S(1)} collective-permute-done((bf16[1024,256]{1,0:T(8,128)(2,1)S(1)}, bf16[1024,256]{1,0:T(8,128)(2,1)S(1)}, u32[]{:S(2)}, u32[]{:S(2)}) %collective-permute-start.10) | collective-permute-done | bytes 524320 | tf_op jit(solution)/shard_map/ppermute | solution.py:68
  78.6 0.8 fusion.21
  79.3 0.8 convolution_add_fusion.3
  80.1 0.2 maximum_select_fusion.1
  80.3 0.1 collective-permute-start.13
  80.4 0.1 pad_maximum_fusion.2
  80.6 0.5 collective-permute-start.21
  81.1 0.1 constant_dynamic-update-slice_fusion.2
  81.2 0.1 constant_dynamic-update-slice_fusion.1
  81.3 5.4 %collective-permute-start.15 = (f32[1024,128]{1,0:T(8,128)S(1)}, f32[1024,128]{1,0:T(8,128)S(1)}, u32[]{:S(2)}, u32[]{:S(2)}) collective-permute-start(f32[1024,128]{1,0:T(8,128)S(1)} %convolution_add_fusion.3), channel_id=1, source_target_pairs={{0,2},{1,3},{2,0},{3,1},{4,6},{5,7},{6,4},{7,5},{8,10},{9,11},{10,... | collective-permute-start | bytes 1572872 | tf_op jit(solution)/shard_map/ppermute | solution.py:65
  86.7 4.0 %collective-permute-done.16 = bf16[1024,256]{1,0:T(8,128)(2,1)S(1)} collective-permute-done((bf16[1024,256]{1,0:T(8,128)(2,1)S(1)}, bf16[1024,256]{1,0:T(8,128)(2,1)S(1)}, u32[]{:S(2)}, u32[]{:S(2)}) %collective-permute-start.16) | collective-permute-done | bytes 524320 | tf_op jit(solution)/shard_map/ppermute | solution.py:74
  90.7 8.2 %collective-permute-done.13 = bf16[1024,256]{1,0:T(8,128)(2,1)S(1)} collective-permute-done((bf16[1024,256]{1,0:T(8,128)(2,1)S(1)}, bf16[1024,256]{1,0:T(8,128)(2,1)S(1)}, u32[]{:S(2)}, u32[]{:S(2)}) %collective-permute-start.13) | collective-permute-done | bytes 524320 | tf_op jit(solution)/shard_map/ppermute | solution.py:68
  98.9 0.8 fusion.30
  99.6 0.8 convolution_add_fusion.2
  100.5 2.5 %collective-permute-start.17 = (bf16[1024,256]{1,0:T(8,128)(2,1)S(1)}, bf16[1024,256]{1,0:T(8,128)(2,1)S(1)}, u32[]{:S(2)}, u32[]{:S(2)}) collective-permute-start(bf16[1024,256]{1,0:T(8,128)(2,1)S(1)} %broadcast_select_fusion.8), channel_id=1, source_target_pairs={{0,4},{1,5},{2,6},{3,7},{4,0},{5,1},{6,2},{7,3},{8,12},{9,13},{10,... | collective-permute-start | bytes 1572872 | tf_op jit(solution)/shard_map/ppermute | solution.py:68
  103.2 0.2 fusion.36
  103.4 0.8 broadcast_select_fusion.3
  104.2 0.1 constant_dynamic-update-slice_fusion
  104.4 0.2 broadcast_select_fusion.7
  104.6 0.6 collective-permute-start.20
  105.2 2.8 %collective-permute-start.22 = (f32[1024,128]{1,0:T(8,128)S(1)}, f32[1024,128]{1,0:T(8,128)S(1)}, u32[]{:S(2)}, u32[]{:S(2)}) collective-permute-start(f32[1024,128]{1,0:T(8,128)S(1)} %convolution_add_fusion.2), channel_id=1, source_target_pairs={{0,2},{1,3},{2,0},{3,1},{4,6},{5,7},{6,4},{7,5},{8,10},{9,11},{10,... | collective-permute-start | bytes 1572872 | tf_op jit(solution)/shard_map/ppermute | solution.py:65
  108.0 0.7 fusion.24
  108.8 0.8 convolution_add_fusion.1
  109.5 1.3 %fusion.8 = f32[1024,1024]{1,0:T(8,128)S(1)} fusion(bf16[1024,256]{1,0:T(8,128)(2,1)S(1)} %collective-permute-done.20, bf16[1024,256]{1,0:T(8,128)(2,1)S(1)} %get-tuple-element.100, bf16[1024,256]{1,0:T(8,128)(2,1)S(1)} %get-tuple-element.97, bf16[1024,256]{1,0:T(8,128)(2,1)S(1)} %get-tuple-element.95), kind=kOutput, calls=%fused_computation.19 | convolution fusion | flops 1077936128 | bytes 6291456 | tf_op jit(solution)/shard_map/dot_general | solution.py:38
  110.8 2.4 %fusion.5 = f32[1024,1024]{1,0:T(8,128)S(1)} fusion(f32[1024,1024]{1,0:T(8,128)S(1)} %fusion.8, bf16[1024,1024]{1,0:T(8,128)(2,1)S(1)} %constant_dynamic-update-slice_fusion, bf16[1024,512]{1,0:T(8,128)(2,1)S(1)} %collective-permute-done.18, bf16[1024,512]{1,0:T(8,128)(2,1)S(1)} %get-tuple-element.92), kind=kOutput, calls=%fused_computation.9 | convolution fusion | flops 2152726528 | bytes 12582912 | tf_op jit(solution)/shard_map/dot_general | solution.py:38
  113.2 0.1 broadcast_select_fusion.5
  113.4 0.7 fusion.44
  114.1 0.7 convolution_add_fusion
  114.9 0.4 collective-permute-done.23
  115.3 3.3 %add_multiply_fusion = f32[1024,1024]{1,0:T(8,128)} fusion(f32[1024,1024]{1,0:T(8,128)S(1)} %fusion.5, f32[]{:T(128)} %bitcast, bf16[1024,256]{1,0:T(8,128)(2,1)S(1)} %collective-permute-done.23, bf16[1024,256]{1,0:T(8,128)(2,1)S(1)} %get-tuple-element.98, bf16[1024,256]{1,0:T(8,128)(2,1)S(1)} %get-tuple-element.96, bf16[1024,256]{1,0:T(8,128)(2,1)S(1)} %get-tuple-element.94), kind=kOutput, calls=%fused_computation | convolution fusion | flops 1080033280 | bytes 10485764 | tf_op jit(solution)/shard_map/dot_general | solution.py:38
  118.6 1.6 %collective-permute-done.22 = f32[1024,128]{1,0:T(8,128)S(1)} collective-permute-done((f32[1024,128]{1,0:T(8,128)S(1)}, f32[1024,128]{1,0:T(8,128)S(1)}, u32[]{:S(2)}, u32[]{:S(2)}) %collective-permute-start.22) | collective-permute-done | bytes 524320 | tf_op jit(solution)/shard_map/ppermute | solution.py:65
  120.2 1.6 %fusion.4 = f32[1024,512]{1,0:T(8,128)} fusion(f32[1024,256]{1,0:T(8,128)S(1)} %convolution_add_fusion, f32[1024,256]{1,0:T(8,128)S(1)} %convolution_add_fusion.1, f32[1024,128]{1,0:T(8,128)S(1)} %collective-permute-done.22, f32[1024,128]{1,0:T(8,128)S(1)} %collective-permute-done.15, f32[1024,128]{1,0:T(8,128)S(1)} %collective-permute-done.14, ...), kind=kLoop, calls=%fused_computation.6 | loop fusion | flops 3145728 | bytes 6291460 | tf_op jit(solution)/shard_map/mul | solution.py:180
  (43 shorter events, 1.0 us)
Async XLA Ops:
  0.6 5.7 %copy-start.2 = (bf16[1024,1024]{1,0:T(8,128)(2,1)S(1)}, bf16[1024,1024]{1,0:T(8,128)(2,1)}, u32[]{:S(2)}) copy-start(bf16[1024,1024]{1,0:T(8,128)(2,1)} %param.6) | copy-start | bytes 6291460
  0.6 5.7 %collective-permute-start = (bf16[1024,1024]{1,0:T(8,128)(2,1)}, bf16[1024,1024]{1,0:T(8,128)(2,1)}, u32[]{:S(2)}, u32[]{:S(2)}) collective-permute-start(bf16[1024,1024]{1,0:T(8,128)(2,1)} %param.6), channel_id=1, source_target_pairs={{0,1},{1,0},{2,3},{3,2},{4,5},{5,4},{6,7},{7,6},{8,9},{9,8},{10,11... | collective-permute-start | bytes 6291464 | tf_op jit(solution)/shard_map/ppermute | solution.py:71
  3.8 9.6 %collective-permute-start.1 = (bf16[1024,128]{1,0:T(8,128)(2,1)}, bf16[1024,128]{1,0:T(8,128)(2,1)S(1)}, u32[]{:S(2)}, u32[]{:S(2)}) collective-permute-start(bf16[1024,128]{1,0:T(8,128)(2,1)} %get-tuple-element.103), channel_id=1, source_target_pairs={{0,2},{1,3},{2,0},{3,1},{4,6},{5,7},{6,4},{7,5},{8,10},{9,11},{10,... | collective-permute-start | bytes 786440 | tf_op jit(solution)/shard_map/ppermute | solution.py:65
  6.3 7.1 %copy-start.5 = (bf16[1024,128]{1,0:T(8,128)(2,1)S(1)}, bf16[1024,128]{1,0:T(8,128)(2,1)}, u32[]{:S(2)}) copy-start(bf16[1024,128]{1,0:T(8,128)(2,1)} %get-tuple-element.105) | copy-start | bytes 786436
  6.3 8.9 %copy-start.4 = (bf16[1024,128]{1,0:T(8,128)(2,1)S(1)}, bf16[1024,128]{1,0:T(8,128)(2,1)}, u32[]{:S(2)}) copy-start(bf16[1024,128]{1,0:T(8,128)(2,1)} %get-tuple-element.44) | copy-start | bytes 786436
  8.3 18.9 %copy-start = (bf16[1024,512]{1,0:T(8,128)(2,1)S(1)}, bf16[1024,512]{1,0:T(8,128)(2,1)}, u32[]{:S(2)}) copy-start(bf16[1024,512]{1,0:T(8,128)(2,1)} %param.4) | copy-start | bytes 3145732
  13.3 16.0 %copy-start.3 = (bf16[1024,128]{1,0:T(8,128)(2,1)S(1)}, bf16[1024,128]{1,0:T(8,128)(2,1)}, u32[]{:S(2)}) copy-start(bf16[1024,128]{1,0:T(8,128)(2,1)} %get-tuple-element.48) | copy-start | bytes 786436
  13.4 13.8 %collective-permute-start.3 = (bf16[1024,256]{1,0:T(8,128)(2,1)S(1)}, bf16[1024,256]{1,0:T(8,128)(2,1)S(1)}, u32[]{:S(2)}, u32[]{:S(2)}) collective-permute-start(bf16[1024,256]{1,0:T(8,128)(2,1)S(1)} %pad_maximum_fusion.3), channel_id=1, source_target_pairs={{0,2},{1,3},{2,0},{3,1},{4,6},{5,7},{6,4},{7,5},{8,10},{9,11},{10,... | collective-permute-start | bytes 1572872 | tf_op jit(solution)/shard_map/ppermute | solution.py:65
  15.3 14.1 %collective-permute-start.2 = (bf16[1024,128]{1,0:T(8,128)(2,1)S(1)}, bf16[1024,128]{1,0:T(8,128)(2,1)S(1)}, u32[]{:S(2)}, u32[]{:S(2)}) collective-permute-start(bf16[1024,128]{1,0:T(8,128)(2,1)S(1)} %broadcast_select_fusion.18), channel_id=1, source_target_pairs={{0,8},{1,9},{2,10},{3,11},{4,12},{5,13},{6,14},{7,15},{8,0},{9,1},... | collective-permute-start | bytes 786440 | tf_op jit(solution)/shard_map/ppermute | solution.py:77
  29.4 12.6 %collective-permute-start.4 = (bf16[1024,128]{1,0:T(8,128)(2,1)S(1)}, bf16[1024,128]{1,0:T(8,128)(2,1)S(1)}, u32[]{:S(2)}, u32[]{:S(2)}) collective-permute-start(bf16[1024,128]{1,0:T(8,128)(2,1)S(1)} %broadcast_select_fusion.15), channel_id=1, source_target_pairs={{0,4},{1,5},{2,6},{3,7},{4,0},{5,1},{6,2},{7,3},{8,12},{9,13},{10,... | collective-permute-start | bytes 786440 | tf_op jit(solution)/shard_map/ppermute | solution.py:68
  30.2 16.9 %collective-permute-start.5 = (bf16[1024,128]{1,0:T(8,128)(2,1)S(1)}, bf16[1024,128]{1,0:T(8,128)(2,1)S(1)}, u32[]{:S(2)}, u32[]{:S(2)}) collective-permute-start(bf16[1024,128]{1,0:T(8,128)(2,1)S(1)} %get-tuple-element.122), channel_id=1, source_target_pairs={{0,8},{1,9},{2,10},{3,11},{4,12},{5,13},{6,14},{7,15},{8,0},{9,1},... | collective-permute-start | bytes 786440 | tf_op jit(solution)/shard_map/ppermute | solution.py:77
  33.6 13.4 %collective-permute-start.6 = (bf16[1024,256]{1,0:T(8,128)(2,1)S(1)}, bf16[1024,256]{1,0:T(8,128)(2,1)S(1)}, u32[]{:S(2)}, u32[]{:S(2)}) collective-permute-start(bf16[1024,256]{1,0:T(8,128)(2,1)S(1)} %pad_maximum_fusion.4), channel_id=1, source_target_pairs={{0,2},{1,3},{2,0},{3,1},{4,6},{5,7},{6,4},{7,5},{8,10},{9,11},{10,... | collective-permute-start | bytes 1572872 | tf_op jit(solution)/shard_map/ppermute | solution.py:65
  47.1 6.8 %collective-permute-start.9 = (bf16[1024,128]{1,0:T(8,128)(2,1)S(1)}, bf16[1024,128]{1,0:T(8,128)(2,1)S(1)}, u32[]{:S(2)}, u32[]{:S(2)}) collective-permute-start(bf16[1024,128]{1,0:T(8,128)(2,1)S(1)} %broadcast_select_fusion.12), channel_id=1, source_target_pairs={{0,2},{1,3},{2,0},{3,1},{4,6},{5,7},{6,4},{7,5},{8,10},{9,11},{10,... | collective-permute-start | bytes 786440 | tf_op jit(solution)/shard_map/ppermute | solution.py:65
  47.7 10.9 %collective-permute-start.7 = (bf16[1024,128]{1,0:T(8,128)(2,1)S(1)}, bf16[1024,128]{1,0:T(8,128)(2,1)S(1)}, u32[]{:S(2)}, u32[]{:S(2)}) collective-permute-start(bf16[1024,128]{1,0:T(8,128)(2,1)S(1)} %broadcast_select_fusion.13), channel_id=1, source_target_pairs={{0,4},{1,5},{2,6},{3,7},{4,0},{5,1},{6,2},{7,3},{8,12},{9,13},{10,... | collective-permute-start | bytes 786440 | tf_op jit(solution)/shard_map/ppermute | solution.py:68
  48.1 13.1 %collective-permute-start.8 = (bf16[1024,128]{1,0:T(8,128)(2,1)S(1)}, bf16[1024,128]{1,0:T(8,128)(2,1)S(1)}, u32[]{:S(2)}, u32[]{:S(2)}) collective-permute-start(bf16[1024,128]{1,0:T(8,128)(2,1)S(1)} %get-tuple-element.119), channel_id=1, source_target_pairs={{0,8},{1,9},{2,10},{3,11},{4,12},{5,13},{6,14},{7,15},{8,0},{9,1},... | collective-permute-start | bytes 786440 | tf_op jit(solution)/shard_map/ppermute | solution.py:77
  53.9 13.7 %collective-permute-start.12 = (f32[1024,128]{1,0:T(8,128)S(1)}, f32[1024,128]{1,0:T(8,128)S(1)}, u32[]{:S(2)}, u32[]{:S(2)}) collective-permute-start(f32[1024,128]{1,0:T(8,128)S(1)} %convolution_add_fusion.5), channel_id=1, source_target_pairs={{0,2},{1,3},{2,0},{3,1},{4,6},{5,7},{6,4},{7,5},{8,10},{9,11},{10,... | collective-permute-start | bytes 1572872 | tf_op jit(solution)/shard_map/ppermute | solution.py:65
  60.1 1.3 %copy-start.1 = (bf16[1024,512]{1,0:T(8,128)(2,1)S(1)}, bf16[1024,512]{1,0:T(8,128)(2,1)}, u32[]{:S(2)}) copy-start(bf16[1024,512]{1,0:T(8,128)(2,1)} %param.5) | copy-start | bytes 3145732
  61.4 17.2 %collective-permute-start.10 = (bf16[1024,256]{1,0:T(8,128)(2,1)S(1)}, bf16[1024,256]{1,0:T(8,128)(2,1)S(1)}, u32[]{:S(2)}, u32[]{:S(2)}) collective-permute-start(bf16[1024,256]{1,0:T(8,128)(2,1)S(1)} %maximum_select_fusion), channel_id=1, source_target_pairs={{0,4},{1,5},{2,6},{3,7},{4,0},{5,1},{6,2},{7,3},{8,12},{9,13},{10,... | collective-permute-start | bytes 1572872 | tf_op jit(solution)/shard_map/ppermute | solution.py:68
  62.3 17.9 %collective-permute-start.11 = (bf16[1024,128]{1,0:T(8,128)(2,1)S(1)}, bf16[1024,128]{1,0:T(8,128)(2,1)S(1)}, u32[]{:S(2)}, u32[]{:S(2)}) collective-permute-start(bf16[1024,128]{1,0:T(8,128)(2,1)S(1)} %broadcast_select_fusion.11), channel_id=1, source_target_pairs={{0,8},{1,9},{2,10},{3,11},{4,12},{5,13},{6,14},{7,15},{8,0},{9,1},... | collective-permute-start | bytes 786440 | tf_op jit(solution)/shard_map/ppermute | solution.py:77
  64.4 26.3 %collective-permute-start.16 = (bf16[1024,256]{1,0:T(8,128)(2,1)S(1)}, bf16[1024,256]{1,0:T(8,128)(2,1)S(1)}, u32[]{:S(2)}, u32[]{:S(2)}) collective-permute-start(bf16[1024,256]{1,0:T(8,128)(2,1)S(1)} %slice.98), channel_id=1, source_target_pairs={{0,8},{1,9},{4,12},{5,13},{10,2},{11,3},{14,6},{15,7},{16,24},{17,... | collective-permute-start | bytes 1572872 | tf_op jit(solution)/shard_map/ppermute | solution.py:74
  67.6 13.7 %collective-permute-start.14 = (f32[1024,128]{1,0:T(8,128)S(1)}, f32[1024,128]{1,0:T(8,128)S(1)}, u32[]{:S(2)}, u32[]{:S(2)}) collective-permute-start(f32[1024,128]{1,0:T(8,128)S(1)} %convolution_add_fusion.4), channel_id=1, source_target_pairs={{0,2},{1,3},{2,0},{3,1},{4,6},{5,7},{6,4},{7,5},{8,10},{9,11},{10,... | collective-permute-start | bytes 1572872 | tf_op jit(solution)/shard_map/ppermute | solution.py:65
  80.3 18.6 %collective-permute-start.13 = (bf16[1024,256]{1,0:T(8,128)(2,1)S(1)}, bf16[1024,256]{1,0:T(8,128)(2,1)S(1)}, u32[]{:S(2)}, u32[]{:S(2)}) collective-permute-start(bf16[1024,256]{1,0:T(8,128)(2,1)S(1)} %maximum_select_fusion.1), channel_id=1, source_target_pairs={{0,4},{1,5},{2,6},{3,7},{4,0},{5,1},{6,2},{7,3},{8,12},{9,13},{10,... | collective-permute-start | bytes 1572872 | tf_op jit(solution)/shard_map/ppermute | solution.py:68
  80.5 23.7 %collective-permute-start.19 = (bf16[1024,512]{1,0:T(8,128)(2,1)S(1)}, bf16[1024,512]{1,0:T(8,128)(2,1)S(1)}, u32[]{:S(2)}, u32[]{:S(2)}) collective-permute-start(bf16[1024,512]{1,0:T(8,128)(2,1)S(1)} %pad_maximum_fusion.2), channel_id=1, source_target_pairs={{0,1},{1,0},{2,3},{3,2},{4,5},{5,4},{6,7},{7,6},{8,9},{9,8},{10,11... | collective-permute-start | bytes 3145736 | tf_op jit(solution)/shard_map/ppermute | solution.py:71
  80.6 22.5 %collective-permute-start.21 = (bf16[1024,512]{1,0:T(8,128)(2,1)S(1)}, bf16[1024,512]{1,0:T(8,128)(2,1)S(1)}, u32[]{:S(2)}, u32[]{:S(2)}) collective-permute-start(bf16[1024,512]{1,0:T(8,128)(2,1)S(1)} %copy-done.1), channel_id=1, source_target_pairs={{0,1},{1,0},{2,3},{3,2},{4,5},{5,4},{6,7},{7,6},{8,9},{9,8},{10,11... | collective-permute-start | bytes 3145736 | tf_op jit(solution)/shard_map/ppermute | solution.py:71
  81.3 21.8 %collective-permute-start.15 = (f32[1024,128]{1,0:T(8,128)S(1)}, f32[1024,128]{1,0:T(8,128)S(1)}, u32[]{:S(2)}, u32[]{:S(2)}) collective-permute-start(f32[1024,128]{1,0:T(8,128)S(1)} %convolution_add_fusion.3), channel_id=1, source_target_pairs={{0,2},{1,3},{2,0},{3,1},{4,6},{5,7},{6,4},{7,5},{8,10},{9,11},{10,... | collective-permute-start | bytes 1572872 | tf_op jit(solution)/shard_map/ppermute | solution.py:65
  100.5 12.7 %collective-permute-start.17 = (bf16[1024,256]{1,0:T(8,128)(2,1)S(1)}, bf16[1024,256]{1,0:T(8,128)(2,1)S(1)}, u32[]{:S(2)}, u32[]{:S(2)}) collective-permute-start(bf16[1024,256]{1,0:T(8,128)(2,1)S(1)} %broadcast_select_fusion.8), channel_id=1, source_target_pairs={{0,4},{1,5},{2,6},{3,7},{4,0},{5,1},{6,2},{7,3},{8,12},{9,13},{10,... | collective-permute-start | bytes 1572872 | tf_op jit(solution)/shard_map/ppermute | solution.py:68
  104.1 6.7 %collective-permute-start.18 = (bf16[1024,512]{1,0:T(8,128)(2,1)S(1)}, bf16[1024,512]{1,0:T(8,128)(2,1)S(1)}, u32[]{:S(2)}, u32[]{:S(2)}) collective-permute-start(bf16[1024,512]{1,0:T(8,128)(2,1)S(1)} %get-tuple-element.93), channel_id=1, source_target_pairs={{0,1},{1,0},{2,3},{3,2},{4,5},{5,4},{6,7},{7,6},{8,9},{9,8},{10,11... | collective-permute-start | bytes 3145736 | tf_op jit(solution)/shard_map/ppermute | solution.py:71
  104.6 4.9 %collective-permute-start.20 = (bf16[1024,256]{1,0:T(8,128)(2,1)S(1)}, bf16[1024,256]{1,0:T(8,128)(2,1)S(1)}, u32[]{:S(2)}, u32[]{:S(2)}) collective-permute-start(bf16[1024,256]{1,0:T(8,128)(2,1)S(1)} %get-tuple-element.101), channel_id=1, source_target_pairs={{0,1},{1,0},{2,3},{3,2},{4,5},{5,4},{6,7},{7,6},{8,9},{9,8},{10,11... | collective-permute-start | bytes 1572872 | tf_op jit(solution)/shard_map/ppermute | solution.py:71
  105.2 15.0 %collective-permute-start.22 = (f32[1024,128]{1,0:T(8,128)S(1)}, f32[1024,128]{1,0:T(8,128)S(1)}, u32[]{:S(2)}, u32[]{:S(2)}) collective-permute-start(f32[1024,128]{1,0:T(8,128)S(1)} %convolution_add_fusion.2), channel_id=1, source_target_pairs={{0,2},{1,3},{2,0},{3,1},{4,6},{5,7},{6,4},{7,5},{8,10},{9,11},{10,... | collective-permute-start | bytes 1572872 | tf_op jit(solution)/shard_map/ppermute | solution.py:65
  113.3 2.0 %collective-permute-start.23 = (bf16[1024,256]{1,0:T(8,128)(2,1)S(1)}, bf16[1024,256]{1,0:T(8,128)(2,1)S(1)}, u32[]{:S(2)}, u32[]{:S(2)}) collective-permute-start(bf16[1024,256]{1,0:T(8,128)(2,1)S(1)} %get-tuple-element.99), channel_id=1, source_target_pairs={{0,1},{1,0},{2,3},{3,2},{4,5},{5,4},{6,7},{7,6},{8,9},{9,8},{10,11... | collective-permute-start | bytes 1572872 | tf_op jit(solution)/shard_map/ppermute | solution.py:71

commit v16 on v15

--- a/solution.py
+++ b/solution.py
@@ -122,22 +122,29 @@
         b1 = jnp.where(home, near, far)
         b1_next = step(b1)
         part0 = cross(after(sum0, x4))
-        fourth = jnp.where(home, e[1], x4)
+        near, far = together((e[1], x4), j3)
+        fourth = jnp.where(home, near, far)
         j4 = jump(fourth)
         sum1 = adjoint_of(b1, b1_next)
         part1 = cross(after(sum1, part0))
-        near, both, far = together((e[0], j3, x3), sum1, fourth)
-        a0b2 = jnp.where(home, jnp.concatenate([near, both], 1), jnp.concatenate([both, far], 1))
-        a0b2_next = step(a0b2)
-        sum2 = adjoint_of(columns(a0b2, 1, 2), columns(a0b2_next, 1, 2))
+        near, far = together((j3, x3), sum1, x4)
+        b2 = jnp.where(home, near, far)
+        b2_next = step(b2)
+        sum2 = adjoint_of(b2, b2_next)
         part2 = cross(after(sum2, part1))
         j5 = home_jump(after(columns(expected_cot, 2, 4), j3))
-        near, both, far = together((e[1], j4, x4), sum2, part0)
-        a1b3 = jnp.where(home, jnp.concatenate([near, both], 1), jnp.concatenate([both, far], 1))
-        a1b3_next = step(a1b3)
+        near, far = together((e[0], j3), b2_next, part0)
+        a0 = jnp.where(home, near, far)
+        a0_next = step(a0)
+        near, far = together((j4, x4), sum2, part0, a0_next)
+        b3 = jnp.where(home, near, far)
+        b3_next = step(b3)
         v_other = swap(after(value_next, sum1))
-        sum3 = adjoint_of(columns(a1b3, 1, 2), columns(a1b3_next, 1, 2))
+        sum3 = adjoint_of(b3, b3_next)
         part3 = cross(after(sum3, part2))
+        near, far = together((e[1], j4), sum3)
+        a1 = jnp.where(home, near, far)
+        a1_next = step(a1)
 
         def own_and_swapped(near, far):
             return jnp.where(mine, near, far), swap(jnp.where(mine, far, near))
@@ -147,18 +154,13 @@
             [jnp.where(home, parts[2], parts[0]), jnp.where(home, parts[3], parts[1]), parts[4], parts[5]], 1
         )
         v_across_other = swap(v_across)
-        near, far = together((columns(expected_cot, 2, 4), j5), a1b3_next, part1)
+        near, far = together((columns(expected_cot, 2, 4), j5), a1_next, sum3, part2)
         a23 = jnp.where(home, near, far)
         a23_next = step(a23)
-        b0, b0_next, b1, b1_next, a0b2, a0b2_next = together(
-            (b0, b0_next, b1, b1_next, a0b2, a0b2_next), a1b3_next, sum3, part2, a23
-        )
-        a0, a0_next = columns(a0b2, 0, 1), columns(a0b2_next, 0, 1)
-        a1, a1_next = columns(a1b3, 0, 1), columns(a1b3_next, 0, 1)
-        b_own, b_swapped = own_and_swapped(
-            jnp.concatenate([b0, b1, columns(a0b2, 1, 2), columns(a1b3, 1, 2)], 1),
-            jnp.concatenate([b0_next, b1_next, columns(a0b2_next, 1, 2), columns(a1b3_next, 1, 2)], 1),
-        )
+        near = together((b0, b1, b2, b3), sum3, part2)
+        far = together((b0_next, b1_next, b2_next, b3_next), sum3, part2)
+        b_own, b_swapped = own_and_swapped(jnp.concatenate(near, 1), jnp.concatenate(far, 1))
+        a0, a0_next, a1, a1_next = together((a0, a0_next, a1, a1_next), a23)
         a01_own, a01_swapped = own_and_swapped(
             jnp.concatenate([a0, a1], 1), jnp.concatenate([a0_next, a1_next], 1)
         )
@@ -176,7 +178,6 @@
             jnp.concatenate([columns(value_next, 2, 4), columns(v_other, 2, 4)], 1),
         ))
         own23 = adjoint_of(near, far)
-        own23, part3, grad = together((own23, part3, grad))
         adjoint = df * (
             jnp.concatenate([own01, own23], 1) + jnp.concatenate([part0, part1, part2, part3], 1)
         )

time: 122 us -> 134 us (1.098)
  waiting for transfers between devices: 62.7 us -> 70.8 us
  starting transfers between devices: 32.2 us -> 36.6 us
    ppermute x8, waiting for transfers between devices: 24.1 us -> 31.8 us  [cross(): return lax.ppermute(a, AXES, cross_pairs)]
    ppermute x5 -> x7, waiting for transfers between devices: 31.1 us -> 35.7 us  [step(): return lax.ppermute(a, AXES, step_pairs)]
    ppermute x1, waiting for transfers between devices: 3.99 us -> 0.01 us  [home_jump(): return lax.ppermute(a, AXES, home_jump_pairs)]
    ppermute x5 -> x7, starting transfers between devices: 3.84 us -> 6 us  [step(): return lax.ppermute(a, AXES, step_pairs)]
    ppermute x8, starting transfers between devices: 14.4 us -> 16.5 us  [cross(): return lax.ppermute(a, AXES, cross_pairs)]
  transfers between devices with their start and end apart: 24 -> 26, of which waited for: 13 -> 14; matrix products, arithmetic and copies ran while one was open for 19% -> 16% of each run, Pallas kernels for 0% -> 0%
where the time goes in v16:
time: 134 us
  waiting for transfers between devices  70.8 us (53%)
  starting transfers between devices  36.6 us (27%)
  matrix products  15.9 us (12%)
  other arithmetic  7.47 us (6%)
  between operations  1.8 us (1%)
    ppermute x7, waiting for transfers between devices, step(): return lax.ppermute(a, AXES, step_pairs)  35.7 us
    ppermute x8, waiting for transfers between devices, cross(): return lax.ppermute(a, AXES, cross_pairs)  31.8 us
    ppermute x8, starting transfers between devices, cross(): return lax.ppermute(a, AXES, cross_pairs)  16.5 us
    ppermute x4, starting transfers between devices, jump(): return lax.ppermute(a, AXES, jump_pairs)  9.26 us
    dot_general x12, matrix products, tdot(): lax.dot_general(a, b, (((0,), (0,)), ((), ())), preferred_element_type=jn...  8.93 us
    dot_general x3, matrix products, dott(): lax.dot_general(a, b, (((1,), (1,)), ((), ())), preferred_element_type=jn...  6.97 us
    ppermute x7, starting transfers between devices, step(): return lax.ppermute(a, AXES, step_pairs)  6 us
    ppermute x4, waiting for transfers between devices, jump(): return lax.ppermute(a, AXES, jump_pairs)  3.27 us
  transfers between devices with their start and end apart: 26, of which 14 were waited for; matrix products, arithmetic and copies ran while one was open for 16% of the time, Pallas kernels for 0%

profile of v16, /device:TPU:0, one launch (start us, length us, event | category | flops | bytes accessed | tf_op | source)
XLA Modules:
  0.0 133.7 jit_solution(10506274622717299412)
XLA Ops:
  0.6 0.5 collective-permute-start
  1.2 2.6 %fusion.26 = (bf16[1024,128]{1,0:T(8,128)(2,1)S(1)}, bf16[1024,128]{1,0:T(8,128)(2,1)}, bf16[1024,128]{1,0:T(8,128)(2,1)S(1)}, bf16[1024,128]{1,0:T(8,128)(2,1)}...) fusion(bf16[1024,512]{1,0:T(8,128)(2,1)} %param.4, ...), kind=kLoop, calls=%fused_computation.77 | loop fusion | flops 131072 | bytes 3932161 | tf_op jit(solution)/shard_map/slice | solution.py:88
  3.8 2.6 %collective-permute-start.1 = (bf16[1024,128]{1,0:T(8,128)(2,1)}, bf16[1024,128]{1,0:T(8,128)(2,1)S(1)}, u32[]{:S(2)}, u32[]{:S(2)}) collective-permute-start(bf16[1024,128]{1,0:T(8,128)(2,1)} %get-tuple-element.117), channel_id=1, source_target_pairs={{0,2},{1,3},{2,0},{3,1},{4,6},{5,7},{6,4},{7,5},{8,10},{9,11},{10,... | collective-permute-start | bytes 786440 | tf_op jit(solution)/shard_map/ppermute | solution.py:65
  6.3 1.9 %broadcast_select_fusion.1 = (bf16[1024,1024]{1,0:T(8,128)(2,1)S(1)}, bf16[1024,1024]{1,0:T(8,128)(2,1)S(1)}) fusion(bf16[1024,1024]{1,0:T(8,128)(2,1)S(1)} %copy-done.2, bf16[1024,1024]{1,0:T(8,128)(2,1)} %collective-permute-done, pred[]{:T(512)S(6)} %eq.8), kind=kLoop, calls=%fused_computation.8 | loop fusion | flops 2097152 | bytes 8388609 | tf_op jit(solution)/shard_map/jit(_where)/select_n | solution.py:99
  8.3 5.1 %collective-permute-done.1 = bf16[1024,128]{1,0:T(8,128)(2,1)S(1)} collective-permute-done((bf16[1024,128]{1,0:T(8,128)(2,1)}, bf16[1024,128]{1,0:T(8,128)(2,1)S(1)}, u32[]{:S(2)}, u32[]{:S(2)}) %collective-permute-start.1) | collective-permute-done | bytes 262176 | tf_op jit(solution)/shard_map/ppermute | solution.py:65
  13.5 1.8 %collective-permute-start.3 = (bf16[1024,256]{1,0:T(8,128)(2,1)S(1)}, bf16[1024,256]{1,0:T(8,128)(2,1)S(1)}, u32[]{:S(2)}, u32[]{:S(2)}) collective-permute-start(bf16[1024,256]{1,0:T(8,128)(2,1)S(1)} %pad_maximum_fusion.1), channel_id=1, source_target_pairs={{0,2},{1,3},{2,0},{3,1},{4,6},{5,7},{6,4},{7,5},{8,10},{9,11},{10,... | collective-permute-start | bytes 1572872 | tf_op jit(solution)/shard_map/ppermute | solution.py:65
  15.3 2.7 %collective-permute-start.2 = (bf16[1024,128]{1,0:T(8,128)(2,1)S(1)}, bf16[1024,128]{1,0:T(8,128)(2,1)S(1)}, u32[]{:S(2)}, u32[]{:S(2)}) collective-permute-start(bf16[1024,128]{1,0:T(8,128)(2,1)S(1)} %broadcast_select_fusion.22), channel_id=1, source_target_pairs={{0,8},{1,9},{2,10},{3,11},{4,12},{5,13},{6,14},{7,15},{8,0},{9,1},... | collective-permute-start | bytes 786440 | tf_op jit(solution)/shard_map/ppermute | solution.py:77
  18.0 9.3 %collective-permute-done.3 = bf16[1024,256]{1,0:T(8,128)(2,1)S(1)} collective-permute-done((bf16[1024,256]{1,0:T(8,128)(2,1)S(1)}, bf16[1024,256]{1,0:T(8,128)(2,1)S(1)}, u32[]{:S(2)}, u32[]{:S(2)}) %collective-permute-start.3) | collective-permute-done | bytes 524320 | tf_op jit(solution)/shard_map/ppermute | solution.py:65
  27.3 2.1 %collective-permute-done.2 = bf16[1024,128]{1,0:T(8,128)(2,1)S(1)} collective-permute-done((bf16[1024,128]{1,0:T(8,128)(2,1)S(1)}, bf16[1024,128]{1,0:T(8,128)(2,1)S(1)}, u32[]{:S(2)}, u32[]{:S(2)}) %collective-permute-start.2) | collective-permute-done | bytes 262176 | tf_op jit(solution)/shard_map/ppermute | solution.py:77
  29.4 0.7 collective-permute-start.7
  30.9 3.4 %collective-permute-start.6 = (bf16[1024,128]{1,0:T(8,128)(2,1)S(1)}, bf16[1024,128]{1,0:T(8,128)(2,1)S(1)}, u32[]{:S(2)}, u32[]{:S(2)}) collective-permute-start(bf16[1024,128]{1,0:T(8,128)(2,1)S(1)} %get-tuple-element.128), channel_id=1, source_target_pairs={{0,8},{1,9},{2,10},{3,11},{4,12},{5,13},{6,14},{7,15},{8,0},{9,1},... | collective-permute-start | bytes 786440 | tf_op jit(solution)/shard_map/ppermute | solution.py:77
  34.4 0.6 collective-permute-start.4
  35.0 6.2 %collective-permute-done.7 = bf16[1024,128]{1,0:T(8,128)(2,1)S(1)} collective-permute-done((bf16[1024,128]{1,0:T(8,128)(2,1)S(1)}, bf16[1024,128]{1,0:T(8,128)(2,1)S(1)}, u32[]{:S(2)}, u32[]{:S(2)}) %collective-permute-start.7) | collective-permute-done | bytes 262176 | tf_op jit(solution)/shard_map/ppermute | solution.py:68
  41.3 0.7 fusion.29
  42.0 0.8 convolution_add_fusion.5
  42.8 5.0 %collective-permute-done.4 = bf16[1024,256]{1,0:T(8,128)(2,1)S(1)} collective-permute-done((bf16[1024,256]{1,0:T(8,128)(2,1)S(1)}, bf16[1024,256]{1,0:T(8,128)(2,1)S(1)}, u32[]{:S(2)}, u32[]{:S(2)}) %collective-permute-start.4) | collective-permute-done | bytes 524320 | tf_op jit(solution)/shard_map/ppermute | solution.py:65
  47.9 0.6 collective-permute-start.9
  48.5 0.4 collective-permute-start.8
  48.9 1.1 collective-permute-start.5
  50.0 4.7 %collective-permute-done.9 = bf16[1024,128]{1,0:T(8,128)(2,1)S(1)} collective-permute-done((bf16[1024,128]{1,0:T(8,128)(2,1)S(1)}, bf16[1024,128]{1,0:T(8,128)(2,1)S(1)}, u32[]{:S(2)}, u32[]{:S(2)}) %collective-permute-start.9) | collective-permute-done | bytes 262176 | tf_op jit(solution)/shard_map/ppermute | solution.py:65
  54.7 0.5 collective-permute-start.11
  55.2 4.2 %collective-permute-done.8 = bf16[1024,128]{1,0:T(8,128)(2,1)S(1)} collective-permute-done((bf16[1024,128]{1,0:T(8,128)(2,1)S(1)}, bf16[1024,128]{1,0:T(8,128)(2,1)S(1)}, u32[]{:S(2)}, u32[]{:S(2)}) %collective-permute-start.8) | collective-permute-done | bytes 262176 | tf_op jit(solution)/shard_map/ppermute | solution.py:68
  59.4 0.7 fusion.30
  60.1 0.8 convolution_add_fusion.4
  60.9 1.2 collective-permute-done.5
  62.2 2.1 %collective-permute-start.13 = (bf16[1024,128]{1,0:T(8,128)(2,1)S(1)}, bf16[1024,128]{1,0:T(8,128)(2,1)S(1)}, u32[]{:S(2)}, u32[]{:S(2)}) collective-permute-start(bf16[1024,128]{1,0:T(8,128)(2,1)S(1)} %broadcast_select_fusion.13), channel_id=1, source_target_pairs={{0,8},{1,9},{2,10},{3,11},{4,12},{5,13},{6,14},{7,15},{8,0},{9,1},... | collective-permute-start | bytes 786440 | tf_op jit(solution)/shard_map/ppermute | solution.py:77
  64.3 3.0 %collective-permute-start.16 = (bf16[1024,256]{1,0:T(8,128)(2,1)S(1)}, bf16[1024,256]{1,0:T(8,128)(2,1)S(1)}, u32[]{:S(2)}, u32[]{:S(2)}) collective-permute-start(bf16[1024,256]{1,0:T(8,128)(2,1)S(1)} %slice.62), channel_id=1, source_target_pairs={{0,8},{1,9},{4,12},{5,13},{10,2},{11,3},{14,6},{15,7},{16,24},{17,... | collective-permute-start | bytes 1572872 | tf_op jit(solution)/shard_map/ppermute | solution.py:74
  67.3 0.1 constant_dynamic-update-slice_fusion.16
  67.4 0.1 constant_dynamic-update-slice_fusion.15
  67.6 5.3 %collective-permute-done.10 = bf16[1024,128]{1,0:T(8,128)(2,1)S(1)} collective-permute-done((bf16[1024,128]{1,0:T(8,128)(2,1)S(1)}, bf16[1024,128]{1,0:T(8,128)(2,1)S(1)}, u32[]{:S(2)}, u32[]{:S(2)}) %collective-permute-start.10) | collective-permute-done | bytes 262176 | tf_op jit(solution)/shard_map/ppermute | solution.py:68
  72.8 0.7 fusion.31
  73.7 0.8 convolution_add_fusion.3
  74.5 1.6 %collective-permute-start.17 = (f32[1024,128]{1,0:T(8,128)S(1)}, f32[1024,128]{1,0:T(8,128)S(1)}, u32[]{:S(2)}, u32[]{:S(2)}) collective-permute-start(f32[1024,128]{1,0:T(8,128)S(1)} %convolution_add_fusion.4), channel_id=1, source_target_pairs={{0,2},{1,3},{2,0},{3,1},{4,6},{5,7},{6,4},{7,5},{8,10},{9,11},{10,... | collective-permute-start | bytes 1572872 | tf_op jit(solution)/shard_map/ppermute | solution.py:65
  76.0 12.5 %collective-permute-done.12 = bf16[1024,128]{1,0:T(8,128)(2,1)S(1)} collective-permute-done((bf16[1024,128]{1,0:T(8,128)(2,1)S(1)}, bf16[1024,128]{1,0:T(8,128)(2,1)S(1)}, u32[]{:S(2)}, u32[]{:S(2)}) %collective-permute-start.12) | collective-permute-done | bytes 262176 | tf_op jit(solution)/shard_map/ppermute | solution.py:68
  88.6 2.5 %collective-permute-start.14 = (bf16[1024,128]{1,0:T(8,128)(2,1)S(1)}, bf16[1024,128]{1,0:T(8,128)(2,1)S(1)}, u32[]{:S(2)}, u32[]{:S(2)}) collective-permute-start(bf16[1024,128]{1,0:T(8,128)(2,1)S(1)} %broadcast_select_fusion.12), channel_id=1, source_target_pairs={{0,4},{1,5},{2,6},{3,7},{4,0},{5,1},{6,2},{7,3},{8,12},{9,13},{10,... | collective-permute-start | bytes 786440 | tf_op jit(solution)/shard_map/ppermute | solution.py:68
  91.1 0.1 pad_maximum_fusion
  91.3 0.5 collective-permute-start.23
  91.8 0.1 constant_dynamic-update-slice_fusion.14
  91.9 0.1 constant_dynamic-update-slice_fusion.13
  92.1 3.4 %collective-permute-done.14 = bf16[1024,128]{1,0:T(8,128)(2,1)S(1)} collective-permute-done((bf16[1024,128]{1,0:T(8,128)(2,1)S(1)}, bf16[1024,128]{1,0:T(8,128)(2,1)S(1)}, u32[]{:S(2)}, u32[]{:S(2)}) %collective-permute-start.14) | collective-permute-done | bytes 262176 | tf_op jit(solution)/shard_map/ppermute | solution.py:68
  95.5 0.7 fusion.32
  96.2 0.8 convolution_add_fusion.2
  97.0 2.1 %collective-permute-start.15 = (bf16[1024,128]{1,0:T(8,128)(2,1)S(1)}, bf16[1024,128]{1,0:T(8,128)(2,1)S(1)}, u32[]{:S(2)}, u32[]{:S(2)}) collective-permute-start(bf16[1024,128]{1,0:T(8,128)(2,1)S(1)} %broadcast_select_fusion.11), channel_id=1, source_target_pairs={{0,4},{1,5},{2,6},{3,7},{4,0},{5,1},{6,2},{7,3},{8,12},{9,13},{10,... | collective-permute-start | bytes 786440 | tf_op jit(solution)/shard_map/ppermute | solution.py:68
  99.2 0.1 constant_dynamic-update-slice_fusion.12
  99.4 4.1 %collective-permute-done.15 = bf16[1024,128]{1,0:T(8,128)(2,1)S(1)} collective-permute-done((bf16[1024,128]{1,0:T(8,128)(2,1)S(1)}, bf16[1024,128]{1,0:T(8,128)(2,1)S(1)}, u32[]{:S(2)}, u32[]{:S(2)}) %collective-permute-start.15) | collective-permute-done | bytes 262176 | tf_op jit(solution)/shard_map/ppermute | solution.py:68
  103.5 2.5 %collective-permute-done.18 = f32[1024,128]{1,0:T(8,128)S(1)} collective-permute-done((f32[1024,128]{1,0:T(8,128)S(1)}, f32[1024,128]{1,0:T(8,128)S(1)}, u32[]{:S(2)}, u32[]{:S(2)}) %collective-permute-start.18) | collective-permute-done | bytes 524320 | tf_op jit(solution)/shard_map/ppermute | solution.py:65
  106.0 0.1 broadcast_select_fusion.8
  106.1 0.1 collective-permute-start.19
  106.6 0.1 constant_dynamic-update-slice_fusion.4
  106.7 0.1 broadcast_select_fusion.3
  107.0 0.1 constant_dynamic-update-slice_fusion.1
  107.2 0.1 broadcast_select_fusion.7
  107.2 0.6 collective-permute-start.22
  107.8 8.8 %collective-permute-start.24 = (f32[1024,128]{1,0:T(8,128)S(1)}, f32[1024,128]{1,0:T(8,128)S(1)}, u32[]{:S(2)}, u32[]{:S(2)}) collective-permute-start(f32[1024,128]{1,0:T(8,128)S(1)} %convolution_add_fusion.2), channel_id=1, source_target_pairs={{0,2},{1,3},{2,0},{3,1},{4,6},{5,7},{6,4},{7,5},{8,10},{9,11},{10,... | collective-permute-start | bytes 1572872 | tf_op jit(solution)/shard_map/ppermute | solution.py:65
  116.6 0.7 fusion.33
  117.4 0.7 convolution_add_fusion.1
  118.1 1.3 fusion.8
  119.4 2.4 %fusion.5 = f32[1024,1024]{1,0:T(8,128)S(1)} fusion(f32[1024,1024]{1,0:T(8,128)S(1)} %fusion.8, bf16[1024,1024]{1,0:T(8,128)(2,1)S(1)} %constant_dynamic-update-slice_fusion.12, bf16[1024,512]{1,0:T(8,128)(2,1)S(1)} %collective-permute-done.20, bf16[1024,512]{1,0:T(8,128)(2,1)S(1)} %get-tuple-element.106), kind=kOutput, calls=%fused_computation.9 | convolution fusion | flops 2152726528 | bytes 12582912 | tf_op jit(solution)/shard_map/dot_general | solution.py:38
  121.8 0.1 broadcast_select_fusion.5
  122.0 0.7 fusion.34
  122.7 0.7 convolution_add_fusion
  123.5 5.3 %collective-permute-done.24 = f32[1024,128]{1,0:T(8,128)S(1)} collective-permute-done((f32[1024,128]{1,0:T(8,128)S(1)}, f32[1024,128]{1,0:T(8,128)S(1)}, u32[]{:S(2)}, u32[]{:S(2)}) %collective-permute-start.24) | collective-permute-done | bytes 524320 | tf_op jit(solution)/shard_map/ppermute | solution.py:65
  128.8 1.6 %fusion.4 = f32[1024,512]{1,0:T(8,128)} fusion(f32[1024,256]{1,0:T(8,128)S(1)} %convolution_add_fusion, f32[1024,256]{1,0:T(8,128)S(1)} %convolution_add_fusion.1, f32[1024,128]{1,0:T(8,128)S(1)} %collective-permute-done.24, f32[1024,128]{1,0:T(8,128)S(1)} %collective-permute-done.18, f32[1024,128]{1,0:T(8,128)S(1)} %collective-permute-done.17, ...), kind=kLoop, calls=%fused_computation.6 | loop fusion | flops 3145728 | bytes 6291460 | tf_op jit(solution)/shard_map/mul | solution.py:181
  130.4 3.3 %add_multiply_fusion = f32[1024,1024]{1,0:T(8,128)} fusion(f32[1024,1024]{1,0:T(8,128)S(1)} %fusion.5, f32[]{:T(128)} %bitcast, bf16[1024,256]{1,0:T(8,128)(2,1)S(1)} %collective-permute-done.25, bf16[1024,256]{1,0:T(8,128)(2,1)S(1)} %get-tuple-element.112, bf16[1024,256]{1,0:T(8,128)(2,1)S(1)} %get-tuple-element.110, bf16[1024,256]{1,0:T(8,128)(2,1)S(1)} %get-tuple-element.108), kind=kOutput, calls=%fused_computation | convolution fusion | flops 1080033280 | bytes 10485764 | tf_op jit(solution)/shard_map/dot_general | solution.py:38
  (56 shorter events, 1.7 us)
Async XLA Ops:
  0.6 5.7 %copy-start.2 = (bf16[1024,1024]{1,0:T(8,128)(2,1)S(1)}, bf16[1024,1024]{1,0:T(8,128)(2,1)}, u32[]{:S(2)}) copy-start(bf16[1024,1024]{1,0:T(8,128)(2,1)} %param.6) | copy-start | bytes 6291460
  0.6 5.7 %collective-permute-start = (bf16[1024,1024]{1,0:T(8,128)(2,1)}, bf16[1024,1024]{1,0:T(8,128)(2,1)}, u32[]{:S(2)}, u32[]{:S(2)}) collective-permute-start(bf16[1024,1024]{1,0:T(8,128)(2,1)} %param.6), channel_id=1, source_target_pairs={{0,1},{1,0},{2,3},{3,2},{4,5},{5,4},{6,7},{7,6},{8,9},{9,8},{10,11... | collective-permute-start | bytes 6291464 | tf_op jit(solution)/shard_map/ppermute | solution.py:71
  3.8 9.6 %collective-permute-start.1 = (bf16[1024,128]{1,0:T(8,128)(2,1)}, bf16[1024,128]{1,0:T(8,128)(2,1)S(1)}, u32[]{:S(2)}, u32[]{:S(2)}) collective-permute-start(bf16[1024,128]{1,0:T(8,128)(2,1)} %get-tuple-element.117), channel_id=1, source_target_pairs={{0,2},{1,3},{2,0},{3,1},{4,6},{5,7},{6,4},{7,5},{8,10},{9,11},{10,... | collective-permute-start | bytes 786440 | tf_op jit(solution)/shard_map/ppermute | solution.py:65
  6.3 7.1 %copy-start.5 = (bf16[1024,128]{1,0:T(8,128)(2,1)S(1)}, bf16[1024,128]{1,0:T(8,128)(2,1)}, u32[]{:S(2)}) copy-start(bf16[1024,128]{1,0:T(8,128)(2,1)} %get-tuple-element.119) | copy-start | bytes 786436
  6.3 8.9 %copy-start.4 = (bf16[1024,128]{1,0:T(8,128)(2,1)S(1)}, bf16[1024,128]{1,0:T(8,128)(2,1)}, u32[]{:S(2)}) copy-start(bf16[1024,128]{1,0:T(8,128)(2,1)} %get-tuple-element.51) | copy-start | bytes 786436
  8.3 18.9 %copy-start.1 = (bf16[1024,512]{1,0:T(8,128)(2,1)S(1)}, bf16[1024,512]{1,0:T(8,128)(2,1)}, u32[]{:S(2)}) copy-start(bf16[1024,512]{1,0:T(8,128)(2,1)} %param.4) | copy-start | bytes 3145732
  13.4 16.0 %copy-start.3 = (bf16[1024,128]{1,0:T(8,128)(2,1)S(1)}, bf16[1024,128]{1,0:T(8,128)(2,1)}, u32[]{:S(2)}) copy-start(bf16[1024,128]{1,0:T(8,128)(2,1)} %get-tuple-element.55) | copy-start | bytes 786436
  13.5 13.8 %collective-permute-start.3 = (bf16[1024,256]{1,0:T(8,128)(2,1)S(1)}, bf16[1024,256]{1,0:T(8,128)(2,1)S(1)}, u32[]{:S(2)}, u32[]{:S(2)}) collective-permute-start(bf16[1024,256]{1,0:T(8,128)(2,1)S(1)} %pad_maximum_fusion.1), channel_id=1, source_target_pairs={{0,2},{1,3},{2,0},{3,1},{4,6},{5,7},{6,4},{7,5},{8,10},{9,11},{10,... | collective-permute-start | bytes 1572872 | tf_op jit(solution)/shard_map/ppermute | solution.py:65
  15.3 14.1 %collective-permute-start.2 = (bf16[1024,128]{1,0:T(8,128)(2,1)S(1)}, bf16[1024,128]{1,0:T(8,128)(2,1)S(1)}, u32[]{:S(2)}, u32[]{:S(2)}) collective-permute-start(bf16[1024,128]{1,0:T(8,128)(2,1)S(1)} %broadcast_select_fusion.22), channel_id=1, source_target_pairs={{0,8},{1,9},{2,10},{3,11},{4,12},{5,13},{6,14},{7,15},{8,0},{9,1},... | collective-permute-start | bytes 786440 | tf_op jit(solution)/shard_map/ppermute | solution.py:77
  29.4 11.8 %collective-permute-start.7 = (bf16[1024,128]{1,0:T(8,128)(2,1)S(1)}, bf16[1024,128]{1,0:T(8,128)(2,1)S(1)}, u32[]{:S(2)}, u32[]{:S(2)}) collective-permute-start(bf16[1024,128]{1,0:T(8,128)(2,1)S(1)} %broadcast_select_fusion.18), channel_id=1, source_target_pairs={{0,4},{1,5},{2,6},{3,7},{4,0},{5,1},{6,2},{7,3},{8,12},{9,13},{10,... | collective-permute-start | bytes 786440 | tf_op jit(solution)/shard_map/ppermute | solution.py:68
  30.9 16.9 %collective-permute-start.6 = (bf16[1024,128]{1,0:T(8,128)(2,1)S(1)}, bf16[1024,128]{1,0:T(8,128)(2,1)S(1)}, u32[]{:S(2)}, u32[]{:S(2)}) collective-permute-start(bf16[1024,128]{1,0:T(8,128)(2,1)S(1)} %get-tuple-element.128), channel_id=1, source_target_pairs={{0,8},{1,9},{2,10},{3,11},{4,12},{5,13},{6,14},{7,15},{8,0},{9,1},... | collective-permute-start | bytes 786440 | tf_op jit(solution)/shard_map/ppermute | solution.py:77
  34.4 13.4 %collective-permute-start.4 = (bf16[1024,256]{1,0:T(8,128)(2,1)S(1)}, bf16[1024,256]{1,0:T(8,128)(2,1)S(1)}, u32[]{:S(2)}, u32[]{:S(2)}) collective-permute-start(bf16[1024,256]{1,0:T(8,128)(2,1)S(1)} %pad_maximum_fusion.2), channel_id=1, source_target_pairs={{0,2},{1,3},{2,0},{3,1},{4,6},{5,7},{6,4},{7,5},{8,10},{9,11},{10,... | collective-permute-start | bytes 1572872 | tf_op jit(solution)/shard_map/ppermute | solution.py:65
  42.8 6.1 %copy-start = (bf16[1024,512]{1,0:T(8,128)(2,1)S(1)}, bf16[1024,512]{1,0:T(8,128)(2,1)}, u32[]{:S(2)}) copy-start(bf16[1024,512]{1,0:T(8,128)(2,1)} %param.5) | copy-start | bytes 3145732
  47.9 6.8 %collective-permute-start.9 = (bf16[1024,128]{1,0:T(8,128)(2,1)S(1)}, bf16[1024,128]{1,0:T(8,128)(2,1)S(1)}, u32[]{:S(2)}, u32[]{:S(2)}) collective-permute-start(bf16[1024,128]{1,0:T(8,128)(2,1)S(1)} %broadcast_select_fusion.16), channel_id=1, source_target_pairs={{0,2},{1,3},{2,0},{3,1},{4,6},{5,7},{6,4},{7,5},{8,10},{9,11},{10,... | collective-permute-start | bytes 786440 | tf_op jit(solution)/shard_map/ppermute | solution.py:65
  48.5 10.9 %collective-permute-start.8 = (bf16[1024,128]{1,0:T(8,128)(2,1)S(1)}, bf16[1024,128]{1,0:T(8,128)(2,1)S(1)}, u32[]{:S(2)}, u32[]{:S(2)}) collective-permute-start(bf16[1024,128]{1,0:T(8,128)(2,1)S(1)} %broadcast_select_fusion.17), channel_id=1, source_target_pairs={{0,4},{1,5},{2,6},{3,7},{4,0},{5,1},{6,2},{7,3},{8,12},{9,13},{10,... | collective-permute-start | bytes 786440 | tf_op jit(solution)/shard_map/ppermute | solution.py:68
  48.9 13.1 %collective-permute-start.5 = (bf16[1024,128]{1,0:T(8,128)(2,1)S(1)}, bf16[1024,128]{1,0:T(8,128)(2,1)S(1)}, u32[]{:S(2)}, u32[]{:S(2)}) collective-permute-start(bf16[1024,128]{1,0:T(8,128)(2,1)S(1)} %get-tuple-element.125), channel_id=1, source_target_pairs={{0,8},{1,9},{2,10},{3,11},{4,12},{5,13},{6,14},{7,15},{8,0},{9,1},... | collective-permute-start | bytes 786440 | tf_op jit(solution)/shard_map/ppermute | solution.py:77
  54.7 18.9 %collective-permute-start.11 = (f32[1024,128]{1,0:T(8,128)S(1)}, f32[1024,128]{1,0:T(8,128)S(1)}, u32[]{:S(2)}, u32[]{:S(2)}) collective-permute-start(f32[1024,128]{1,0:T(8,128)S(1)} %convolution_add_fusion.5), channel_id=1, source_target_pairs={{0,2},{1,3},{2,0},{3,1},{4,6},{5,7},{6,4},{7,5},{8,10},{9,11},{10,... | collective-permute-start | bytes 1572872 | tf_op jit(solution)/shard_map/ppermute | solution.py:65
  62.1 10.7 %collective-permute-start.10 = (bf16[1024,128]{1,0:T(8,128)(2,1)S(1)}, bf16[1024,128]{1,0:T(8,128)(2,1)S(1)}, u32[]{:S(2)}, u32[]{:S(2)}) collective-permute-start(bf16[1024,128]{1,0:T(8,128)(2,1)S(1)} %broadcast_select_fusion.15), channel_id=1, source_target_pairs={{0,4},{1,5},{2,6},{3,7},{4,0},{5,1},{6,2},{7,3},{8,12},{9,13},{10,... | collective-permute-start | bytes 786440 | tf_op jit(solution)/shard_map/ppermute | solution.py:68
  62.2 13.8 %collective-permute-start.13 = (bf16[1024,128]{1,0:T(8,128)(2,1)S(1)}, bf16[1024,128]{1,0:T(8,128)(2,1)S(1)}, u32[]{:S(2)}, u32[]{:S(2)}) collective-permute-start(bf16[1024,128]{1,0:T(8,128)(2,1)S(1)} %broadcast_select_fusion.13), channel_id=1, source_target_pairs={{0,8},{1,9},{2,10},{3,11},{4,12},{5,13},{6,14},{7,15},{8,0},{9,1},... | collective-permute-start | bytes 786440 | tf_op jit(solution)/shard_map/ppermute | solution.py:77
  64.3 35.1 %collective-permute-start.16 = (bf16[1024,256]{1,0:T(8,128)(2,1)S(1)}, bf16[1024,256]{1,0:T(8,128)(2,1)S(1)}, u32[]{:S(2)}, u32[]{:S(2)}) collective-permute-start(bf16[1024,256]{1,0:T(8,128)(2,1)S(1)} %slice.62), channel_id=1, source_target_pairs={{0,8},{1,9},{4,12},{5,13},{10,2},{11,3},{14,6},{15,7},{16,24},{17,... | collective-permute-start | bytes 1572872 | tf_op jit(solution)/shard_map/ppermute | solution.py:74
  73.6 14.9 %collective-permute-start.12 = (bf16[1024,128]{1,0:T(8,128)(2,1)S(1)}, bf16[1024,128]{1,0:T(8,128)(2,1)S(1)}, u32[]{:S(2)}, u32[]{:S(2)}) collective-permute-start(bf16[1024,128]{1,0:T(8,128)(2,1)S(1)} %broadcast_select_fusion.14), channel_id=1, source_target_pairs={{0,4},{1,5},{2,6},{3,7},{4,0},{5,1},{6,2},{7,3},{8,12},{9,13},{10,... | collective-permute-start | bytes 786440 | tf_op jit(solution)/shard_map/ppermute | solution.py:68
  74.5 17.6 %collective-permute-start.17 = (f32[1024,128]{1,0:T(8,128)S(1)}, f32[1024,128]{1,0:T(8,128)S(1)}, u32[]{:S(2)}, u32[]{:S(2)}) collective-permute-start(f32[1024,128]{1,0:T(8,128)S(1)} %convolution_add_fusion.4), channel_id=1, source_target_pairs={{0,2},{1,3},{2,0},{3,1},{4,6},{5,7},{6,4},{7,5},{8,10},{9,11},{10,... | collective-permute-start | bytes 1572872 | tf_op jit(solution)/shard_map/ppermute | solution.py:65
  88.6 6.9 %collective-permute-start.14 = (bf16[1024,128]{1,0:T(8,128)(2,1)S(1)}, bf16[1024,128]{1,0:T(8,128)(2,1)S(1)}, u32[]{:S(2)}, u32[]{:S(2)}) collective-permute-start(bf16[1024,128]{1,0:T(8,128)(2,1)S(1)} %broadcast_select_fusion.12), channel_id=1, source_target_pairs={{0,4},{1,5},{2,6},{3,7},{4,0},{5,1},{6,2},{7,3},{8,12},{9,13},{10,... | collective-permute-start | bytes 786440 | tf_op jit(solution)/shard_map/ppermute | solution.py:68
  91.3 7.9 %collective-permute-start.21 = (bf16[1024,512]{1,0:T(8,128)(2,1)S(1)}, bf16[1024,512]{1,0:T(8,128)(2,1)S(1)}, u32[]{:S(2)}, u32[]{:S(2)}) collective-permute-start(bf16[1024,512]{1,0:T(8,128)(2,1)S(1)} %pad_maximum_fusion), channel_id=1, source_target_pairs={{0,1},{1,0},{2,3},{3,2},{4,5},{5,4},{6,7},{7,6},{8,9},{9,8},{10,11... | collective-permute-start | bytes 3145736 | tf_op jit(solution)/shard_map/ppermute | solution.py:71
  91.3 8.0 %collective-permute-start.23 = (bf16[1024,512]{1,0:T(8,128)(2,1)S(1)}, bf16[1024,512]{1,0:T(8,128)(2,1)S(1)}, u32[]{:S(2)}, u32[]{:S(2)}) collective-permute-start(bf16[1024,512]{1,0:T(8,128)(2,1)S(1)} %copy-done), channel_id=1, source_target_pairs={{0,1},{1,0},{2,3},{3,2},{4,5},{5,4},{6,7},{7,6},{8,9},{9,8},{10,11... | collective-permute-start | bytes 3145736 | tf_op jit(solution)/shard_map/ppermute | solution.py:71
  92.0 14.0 %collective-permute-start.18 = (f32[1024,128]{1,0:T(8,128)S(1)}, f32[1024,128]{1,0:T(8,128)S(1)}, u32[]{:S(2)}, u32[]{:S(2)}) collective-permute-start(f32[1024,128]{1,0:T(8,128)S(1)} %convolution_add_fusion.3), channel_id=1, source_target_pairs={{0,2},{1,3},{2,0},{3,1},{4,6},{5,7},{6,4},{7,5},{8,10},{9,11},{10,... | collective-permute-start | bytes 1572872 | tf_op jit(solution)/shard_map/ppermute | solution.py:65
  97.0 6.5 %collective-permute-start.15 = (bf16[1024,128]{1,0:T(8,128)(2,1)S(1)}, bf16[1024,128]{1,0:T(8,128)(2,1)S(1)}, u32[]{:S(2)}, u32[]{:S(2)}) collective-permute-start(bf16[1024,128]{1,0:T(8,128)(2,1)S(1)} %broadcast_select_fusion.11), channel_id=1, source_target_pairs={{0,4},{1,5},{2,6},{3,7},{4,0},{5,1},{6,2},{7,3},{8,12},{9,13},{10,... | collective-permute-start | bytes 786440 | tf_op jit(solution)/shard_map/ppermute | solution.py:68
  106.1 15.7 %collective-permute-start.19 = (bf16[1024,256]{1,0:T(8,128)(2,1)S(1)}, bf16[1024,256]{1,0:T(8,128)(2,1)S(1)}, u32[]{:S(2)}, u32[]{:S(2)}) collective-permute-start(bf16[1024,256]{1,0:T(8,128)(2,1)S(1)} %broadcast_select_fusion.8), channel_id=1, source_target_pairs={{0,4},{1,5},{2,6},{3,7},{4,0},{5,1},{6,2},{7,3},{8,12},{9,13},{10,... | collective-permute-start | bytes 1572872 | tf_op jit(solution)/shard_map/ppermute | solution.py:68
  106.9 12.5 %collective-permute-start.20 = (bf16[1024,512]{1,0:T(8,128)(2,1)S(1)}, bf16[1024,512]{1,0:T(8,128)(2,1)S(1)}, u32[]{:S(2)}, u32[]{:S(2)}) collective-permute-start(bf16[1024,512]{1,0:T(8,128)(2,1)S(1)} %get-tuple-element.107), channel_id=1, source_target_pairs={{0,1},{1,0},{2,3},{3,2},{4,5},{5,4},{6,7},{7,6},{8,9},{9,8},{10,11... | collective-permute-start | bytes 3145736 | tf_op jit(solution)/shard_map/ppermute | solution.py:71
  107.2 10.9 %collective-permute-start.22 = (bf16[1024,256]{1,0:T(8,128)(2,1)S(1)}, bf16[1024,256]{1,0:T(8,128)(2,1)S(1)}, u32[]{:S(2)}, u32[]{:S(2)}) collective-permute-start(bf16[1024,256]{1,0:T(8,128)(2,1)S(1)} %get-tuple-element.115), channel_id=1, source_target_pairs={{0,1},{1,0},{2,3},{3,2},{4,5},{5,4},{6,7},{7,6},{8,9},{9,8},{10,11... | collective-permute-start | bytes 1572872 | tf_op jit(solution)/shard_map/ppermute | solution.py:71
  107.8 21.0 %collective-permute-start.24 = (f32[1024,128]{1,0:T(8,128)S(1)}, f32[1024,128]{1,0:T(8,128)S(1)}, u32[]{:S(2)}, u32[]{:S(2)}) collective-permute-start(f32[1024,128]{1,0:T(8,128)S(1)} %convolution_add_fusion.2), channel_id=1, source_target_pairs={{0,2},{1,3},{2,0},{3,1},{4,6},{5,7},{6,4},{7,5},{8,10},{9,11},{10,... | collective-permute-start | bytes 1572872 | tf_op jit(solution)/shard_map/ppermute | solution.py:65
  121.9 8.5 %collective-permute-start.25 = (bf16[1024,256]{1,0:T(8,128)(2,1)S(1)}, bf16[1024,256]{1,0:T(8,128)(2,1)S(1)}, u32[]{:S(2)}, u32[]{:S(2)}) collective-permute-start(bf16[1024,256]{1,0:T(8,128)(2,1)S(1)} %get-tuple-element.113), channel_id=1, source_target_pairs={{0,1},{1,0},{2,3},{3,2},{4,5},{5,4},{6,7},{7,6},{8,9},{9,8},{10,11... | collective-permute-start | bytes 1572872 | tf_op jit(solution)/shard_map/ppermute | solution.py:71

commit v17 on v15

--- a/solution.py
+++ b/solution.py
@@ -90,13 +90,15 @@
         def together(arrays, *gates):
             return lax.optimization_barrier(tuple(arrays) + gates)[: len(arrays)]
 
+        first = jnp.where(home, columns(value_next, 0, 1), columns(expected_cot, 0, 1))
+        x1 = cross(first)
+        expected_cot, value_next, transition = together((expected_cot, value_next, transition), first)
         e = [columns(expected_cot, i, i + 1) for i in range(4)]
         v = [columns(value_next, i, i + 1) for i in range(4)]
-        x1 = cross(jnp.where(home, v[0], e[0]))
         t_other = swap(transition)
-        e2 = after(e[2], x1)
-        j1 = jump(jnp.where(home, x1, e2))
         t_near, t_next = jnp.where(mine, transition, t_other), jnp.where(mine, t_other, transition)
+        first_jump = jnp.where(home, x1, after(e[2], x1, t_near))
+        j1 = jump(first_jump)
 
         def adjoint_of(near, far):
             return tdot(t_near, near) + tdot(t_next, far)
@@ -104,7 +106,7 @@
         v1, e1 = together((v[1], e[1]), x1, t_near)
         x2 = cross(jnp.concatenate([jnp.where(home, v1, e1), v[2]], 1))
         x2, v_across2 = columns(x2, 0, 1), columns(x2, 1, 2)
-        second = jnp.where(home, x2, e[3])
+        second = jnp.where(home, x2, columns(after(expected_cot, first_jump), 3, 4))
         j2 = jump(second)
         near, far = together((j1, v[0]), second)
         third_cross = jnp.where(home, near, far)

time: 122 us -> 122 us (level)
  waiting for transfers between devices: 62.7 us -> 61.4 us
  local copies, waits for them, and re-layouts: 0.77 us -> 2.01 us
    slice x3, other arithmetic: 2.71 us -> 0.15 us  [columns(): return array[:, start * quarter:stop * quarter]]
    select_n x2, other arithmetic: 0.07 us -> 1.95 us  [the longest x1 1.92 us: shards(): jnp.where(home, columns(value_next, 0, 1), columns(expected_cot, 0, 1))]
    ppermute x8, waiting for transfers between devices: 24.1 us -> 22.8 us  [cross(): return lax.ppermute(a, AXES, cross_pairs)]
    slice x6 -> x8, local copies, waits for them, and re-layouts: 0.43 us -> 1.68 us  [columns(): return array[:, start * quarter:stop * quarter]]
  transfers between devices with their start and end apart: 24 -> 24, of which waited for: 13 -> 14; matrix products, arithmetic and copies ran while one was open for 19% -> 18% of each run, Pallas kernels for 0% -> 0%
where the time goes in v17:
time: 122 us
  waiting for transfers between devices  61.4 us (50%)
  starting transfers between devices  33.2 us (27%)
  matrix products  16 us (13%)
  other arithmetic  7.66 us (6%)
  local copies, waits for them, and re-layouts  2.01 us (2%)
  between operations  1.79 us (1%)
    ppermute x5, waiting for transfers between devices, step(): return lax.ppermute(a, AXES, step_pairs)  31.1 us
    ppermute x8, waiting for transfers between devices, cross(): return lax.ppermute(a, AXES, cross_pairs)  22.8 us
    ppermute x8, starting transfers between devices, cross(): return lax.ppermute(a, AXES, cross_pairs)  15.5 us
    ppermute x4, starting transfers between devices, jump(): return lax.ppermute(a, AXES, jump_pairs)  9.2 us
    dot_general x12, matrix products, tdot(): lax.dot_general(a, b, (((0,), (0,)), ((), ())), preferred_element_type=jn...  9.03 us
    dot_general x3, matrix products, dott(): lax.dot_general(a, b, (((1,), (1,)), ((), ())), preferred_element_type=jn...  6.94 us
    ppermute x5, starting transfers between devices, step(): return lax.ppermute(a, AXES, step_pairs)  3.84 us
    ppermute x1, waiting for transfers between devices, home_jump(): return lax.ppermute(a, AXES, home_jump_pairs)  3.57 us
  transfers between devices with their start and end apart: 24, of which 14 were waited for; matrix products, arithmetic and copies ran while one was open for 18% of the time, Pallas kernels for 0%

profile of v17, /device:TPU:0, one launch (start us, length us, event | category | flops | bytes accessed | tf_op | source)
XLA Modules:
  0.0 122.0 jit_solution(363145186098690157)
XLA Ops:
  0.7 1.9 %slice_select_fusion.1 = bf16[1024,128]{1,0:T(8,128)(2,1)} fusion(bf16[1024,512]{1,0:T(8,128)(2,1)} %param.4, bf16[1024,512]{1,0:T(8,128)(2,1)} %param.5, pred[]{:T(512)S(6)} %eq.9), kind=kLoop, calls=%fused_computation.49 | loop fusion | flops 131072 | bytes 786433 | tf_op jit(solution)/shard_map/jit(_where)/select_n | solution.py:93
  2.6 0.5 collective-permute-start
  3.0 2.5 %collective-permute-start.1 = (bf16[1024,128]{1,0:T(8,128)(2,1)}, bf16[1024,128]{1,0:T(8,128)(2,1)S(1)}, u32[]{:S(2)}, u32[]{:S(2)}) collective-permute-start(bf16[1024,128]{1,0:T(8,128)(2,1)} %slice_select_fusion.1), channel_id=1, source_target_pairs={{0,2},{1,3},{2,0},{3,1},{4,6},{5,7},{6,4},{7,5},{8,10},{9,11},{10,... | collective-permute-start | bytes 786440 | tf_op jit(solution)/shard_map/ppermute | solution.py:65
  5.5 1.1 fusion.36
  6.6 0.2 fusion.37
  6.8 0.4 collective-permute-done
  7.2 1.9 %broadcast_select_fusion.1 = (bf16[1024,1024]{1,0:T(8,128)(2,1)S(1)}, bf16[1024,1024]{1,0:T(8,128)(2,1)S(1)}) fusion(bf16[1024,1024]{1,0:T(8,128)(2,1)S(1)} %copy-done.2, bf16[1024,1024]{1,0:T(8,128)(2,1)} %collective-permute-done, pred[]{:T(512)S(6)} %eq.8), kind=kLoop, calls=%fused_computation.8 | loop fusion | flops 2097152 | bytes 8388609 | tf_op jit(solution)/shard_map/jit(_where)/select_n | solution.py:99
  9.1 3.7 %collective-permute-done.1 = bf16[1024,128]{1,0:T(8,128)(2,1)S(1)} collective-permute-done((bf16[1024,128]{1,0:T(8,128)(2,1)}, bf16[1024,128]{1,0:T(8,128)(2,1)S(1)}, u32[]{:S(2)}, u32[]{:S(2)}) %collective-permute-start.1) | collective-permute-done | bytes 262176 | tf_op jit(solution)/shard_map/ppermute | solution.py:65
  12.8 1.8 %collective-permute-start.3 = (bf16[1024,256]{1,0:T(8,128)(2,1)S(1)}, bf16[1024,256]{1,0:T(8,128)(2,1)S(1)}, u32[]{:S(2)}, u32[]{:S(2)}) collective-permute-start(bf16[1024,256]{1,0:T(8,128)(2,1)S(1)} %pad_maximum_fusion.3), channel_id=1, source_target_pairs={{0,2},{1,3},{2,0},{3,1},{4,6},{5,7},{6,4},{7,5},{8,10},{9,11},{10,... | collective-permute-start | bytes 1572872 | tf_op jit(solution)/shard_map/ppermute | solution.py:65
  14.7 2.7 %collective-permute-start.2 = (bf16[1024,128]{1,0:T(8,128)(2,1)S(1)}, bf16[1024,128]{1,0:T(8,128)(2,1)S(1)}, u32[]{:S(2)}, u32[]{:S(2)}) collective-permute-start(bf16[1024,128]{1,0:T(8,128)(2,1)S(1)} %broadcast_select_fusion.18), channel_id=1, source_target_pairs={{0,8},{1,9},{2,10},{3,11},{4,12},{5,13},{6,14},{7,15},{8,0},{9,1},... | collective-permute-start | bytes 786440 | tf_op jit(solution)/shard_map/ppermute | solution.py:77
  17.3 9.3 %collective-permute-done.3 = bf16[1024,256]{1,0:T(8,128)(2,1)S(1)} collective-permute-done((bf16[1024,256]{1,0:T(8,128)(2,1)S(1)}, bf16[1024,256]{1,0:T(8,128)(2,1)S(1)}, u32[]{:S(2)}, u32[]{:S(2)}) %collective-permute-start.3) | collective-permute-done | bytes 524320 | tf_op jit(solution)/shard_map/ppermute | solution.py:65
  26.7 2.2 %collective-permute-done.2 = bf16[1024,128]{1,0:T(8,128)(2,1)S(1)} collective-permute-done((bf16[1024,128]{1,0:T(8,128)(2,1)S(1)}, bf16[1024,128]{1,0:T(8,128)(2,1)S(1)}, u32[]{:S(2)}, u32[]{:S(2)}) %collective-permute-start.2) | collective-permute-done | bytes 262176 | tf_op jit(solution)/shard_map/ppermute | solution.py:77
  29.0 0.7 collective-permute-start.4
  29.7 3.4 %collective-permute-start.5 = (bf16[1024,128]{1,0:T(8,128)(2,1)S(1)}, bf16[1024,128]{1,0:T(8,128)(2,1)S(1)}, u32[]{:S(2)}, u32[]{:S(2)}) collective-permute-start(bf16[1024,128]{1,0:T(8,128)(2,1)S(1)} %get-tuple-element.130), channel_id=1, source_target_pairs={{0,8},{1,9},{2,10},{3,11},{4,12},{5,13},{6,14},{7,15},{8,0},{9,1},... | collective-permute-start | bytes 786440 | tf_op jit(solution)/shard_map/ppermute | solution.py:77
  33.1 0.6 collective-permute-start.6
  33.8 7.8 %collective-permute-done.4 = bf16[1024,128]{1,0:T(8,128)(2,1)S(1)} collective-permute-done((bf16[1024,128]{1,0:T(8,128)(2,1)S(1)}, bf16[1024,128]{1,0:T(8,128)(2,1)S(1)}, u32[]{:S(2)}, u32[]{:S(2)}) %collective-permute-start.4) | collective-permute-done | bytes 262176 | tf_op jit(solution)/shard_map/ppermute | solution.py:68
  41.6 0.7 fusion.44
  42.3 0.8 convolution_add_fusion.5
  43.1 3.4 %collective-permute-done.6 = bf16[1024,256]{1,0:T(8,128)(2,1)S(1)} collective-permute-done((bf16[1024,256]{1,0:T(8,128)(2,1)S(1)}, bf16[1024,256]{1,0:T(8,128)(2,1)S(1)}, u32[]{:S(2)}, u32[]{:S(2)}) %collective-permute-start.6) | collective-permute-done | bytes 524320 | tf_op jit(solution)/shard_map/ppermute | solution.py:65
  46.6 0.6 collective-permute-start.9
  47.2 0.4 collective-permute-start.7
  47.7 1.0 collective-permute-start.8
  48.7 4.7 %collective-permute-done.9 = bf16[1024,128]{1,0:T(8,128)(2,1)S(1)} collective-permute-done((bf16[1024,128]{1,0:T(8,128)(2,1)S(1)}, bf16[1024,128]{1,0:T(8,128)(2,1)S(1)}, u32[]{:S(2)}, u32[]{:S(2)}) %collective-permute-start.9) | collective-permute-done | bytes 262176 | tf_op jit(solution)/shard_map/ppermute | solution.py:65
  53.4 0.5 collective-permute-start.12
  54.0 4.2 %collective-permute-done.7 = bf16[1024,128]{1,0:T(8,128)(2,1)S(1)} collective-permute-done((bf16[1024,128]{1,0:T(8,128)(2,1)S(1)}, bf16[1024,128]{1,0:T(8,128)(2,1)S(1)}, u32[]{:S(2)}, u32[]{:S(2)}) %collective-permute-start.7) | collective-permute-done | bytes 262176 | tf_op jit(solution)/shard_map/ppermute | solution.py:68
  58.2 0.7 fusion.45
  58.9 0.8 convolution_add_fusion.4
  59.7 1.0 collective-permute-done.8
  60.7 0.2 maximum_select_fusion
  61.8 2.1 %collective-permute-start.11 = (bf16[1024,128]{1,0:T(8,128)(2,1)S(1)}, bf16[1024,128]{1,0:T(8,128)(2,1)S(1)}, u32[]{:S(2)}, u32[]{:S(2)}) collective-permute-start(bf16[1024,128]{1,0:T(8,128)(2,1)S(1)} %get-tuple-element.111), channel_id=1, source_target_pairs={{0,8},{1,9},{2,10},{3,11},{4,12},{5,13},{6,14},{7,15},{8,0},{9,1},... | collective-permute-start | bytes 786440 | tf_op jit(solution)/shard_map/ppermute | solution.py:77
  63.9 3.0 %collective-permute-start.16 = (bf16[1024,256]{1,0:T(8,128)(2,1)S(1)}, bf16[1024,256]{1,0:T(8,128)(2,1)S(1)}, u32[]{:S(2)}, u32[]{:S(2)}) collective-permute-start(bf16[1024,256]{1,0:T(8,128)(2,1)S(1)} %slice.106), channel_id=1, source_target_pairs={{0,8},{1,9},{4,12},{5,13},{10,2},{11,3},{14,6},{15,7},{16,24},{17,... | collective-permute-start | bytes 1572872 | tf_op jit(solution)/shard_map/ppermute | solution.py:74
  66.9 0.1 constant_dynamic-update-slice_fusion.4
  67.0 0.1 constant_dynamic-update-slice_fusion.3
  67.2 10.9 %collective-permute-done.10 = bf16[1024,256]{1,0:T(8,128)(2,1)S(1)} collective-permute-done((bf16[1024,256]{1,0:T(8,128)(2,1)S(1)}, bf16[1024,256]{1,0:T(8,128)(2,1)S(1)}, u32[]{:S(2)}, u32[]{:S(2)}) %collective-permute-start.10) | collective-permute-done | bytes 524320 | tf_op jit(solution)/shard_map/ppermute | solution.py:68
  78.1 0.8 fusion.21
  78.9 0.8 convolution_add_fusion.3
  79.7 0.2 maximum_select_fusion.1
  79.9 0.1 pad_maximum_fusion.2
  80.1 0.5 collective-permute-start.21
  80.6 0.1 constant_dynamic-update-slice_fusion.2
  80.7 0.1 constant_dynamic-update-slice_fusion.1
  80.8 5.8 %collective-permute-start.15 = (f32[1024,128]{1,0:T(8,128)S(1)}, f32[1024,128]{1,0:T(8,128)S(1)}, u32[]{:S(2)}, u32[]{:S(2)}) collective-permute-start(f32[1024,128]{1,0:T(8,128)S(1)} %convolution_add_fusion.3), channel_id=1, source_target_pairs={{0,2},{1,3},{2,0},{3,1},{4,6},{5,7},{6,4},{7,5},{8,10},{9,11},{10,... | collective-permute-start | bytes 1572872 | tf_op jit(solution)/shard_map/ppermute | solution.py:65
  86.7 3.6 %collective-permute-done.16 = bf16[1024,256]{1,0:T(8,128)(2,1)S(1)} collective-permute-done((bf16[1024,256]{1,0:T(8,128)(2,1)S(1)}, bf16[1024,256]{1,0:T(8,128)(2,1)S(1)}, u32[]{:S(2)}, u32[]{:S(2)}) %collective-permute-start.16) | collective-permute-done | bytes 524320 | tf_op jit(solution)/shard_map/ppermute | solution.py:74
  90.3 8.2 %collective-permute-done.13 = bf16[1024,256]{1,0:T(8,128)(2,1)S(1)} collective-permute-done((bf16[1024,256]{1,0:T(8,128)(2,1)S(1)}, bf16[1024,256]{1,0:T(8,128)(2,1)S(1)}, u32[]{:S(2)}, u32[]{:S(2)}) %collective-permute-start.13) | collective-permute-done | bytes 524320 | tf_op jit(solution)/shard_map/ppermute | solution.py:68
  98.4 0.8 fusion.30
  99.2 0.8 convolution_add_fusion.2
  100.0 2.5 %collective-permute-start.17 = (bf16[1024,256]{1,0:T(8,128)(2,1)S(1)}, bf16[1024,256]{1,0:T(8,128)(2,1)S(1)}, u32[]{:S(2)}, u32[]{:S(2)}) collective-permute-start(bf16[1024,256]{1,0:T(8,128)(2,1)S(1)} %broadcast_select_fusion.8), channel_id=1, source_target_pairs={{0,4},{1,5},{2,6},{3,7},{4,0},{5,1},{6,2},{7,3},{8,12},{9,13},{10,... | collective-permute-start | bytes 1572872 | tf_op jit(solution)/shard_map/ppermute | solution.py:68
  102.7 0.2 fusion.38
  102.9 0.8 broadcast_select_fusion.3
  103.7 0.1 constant_dynamic-update-slice_fusion
  103.9 0.2 broadcast_select_fusion.7
  104.2 0.6 collective-permute-start.20
  104.7 3.5 %collective-permute-start.22 = (f32[1024,128]{1,0:T(8,128)S(1)}, f32[1024,128]{1,0:T(8,128)S(1)}, u32[]{:S(2)}, u32[]{:S(2)}) collective-permute-start(f32[1024,128]{1,0:T(8,128)S(1)} %convolution_add_fusion.2), channel_id=1, source_target_pairs={{0,2},{1,3},{2,0},{3,1},{4,6},{5,7},{6,4},{7,5},{8,10},{9,11},{10,... | collective-permute-start | bytes 1572872 | tf_op jit(solution)/shard_map/ppermute | solution.py:65
  108.2 0.7 fusion.24
  109.0 0.7 convolution_add_fusion.1
  109.7 1.3 %fusion.8 = f32[1024,1024]{1,0:T(8,128)S(1)} fusion(bf16[1024,256]{1,0:T(8,128)(2,1)S(1)} %collective-permute-done.20, bf16[1024,256]{1,0:T(8,128)(2,1)S(1)} %get-tuple-element.108, bf16[1024,256]{1,0:T(8,128)(2,1)S(1)} %get-tuple-element.105, bf16[1024,256]{1,0:T(8,128)(2,1)S(1)} %get-tuple-element.103), kind=kOutput, calls=%fused_computation.19 | convolution fusion | flops 1077936128 | bytes 6291456 | tf_op jit(solution)/shard_map/dot_general | solution.py:38
  111.0 2.4 %fusion.5 = f32[1024,1024]{1,0:T(8,128)S(1)} fusion(f32[1024,1024]{1,0:T(8,128)S(1)} %fusion.8, bf16[1024,1024]{1,0:T(8,128)(2,1)S(1)} %constant_dynamic-update-slice_fusion, bf16[1024,512]{1,0:T(8,128)(2,1)S(1)} %collective-permute-done.18, bf16[1024,512]{1,0:T(8,128)(2,1)S(1)} %get-tuple-element.100), kind=kOutput, calls=%fused_computation.9 | convolution fusion | flops 2152726528 | bytes 12582912 | tf_op jit(solution)/shard_map/dot_general | solution.py:38
  113.4 0.1 broadcast_select_fusion.5
  113.6 0.7 fusion.46
  114.3 0.7 convolution_add_fusion
  115.1 0.4 collective-permute-done.23
  115.5 3.3 %add_multiply_fusion = f32[1024,1024]{1,0:T(8,128)} fusion(f32[1024,1024]{1,0:T(8,128)S(1)} %fusion.5, f32[]{:T(128)} %bitcast, bf16[1024,256]{1,0:T(8,128)(2,1)S(1)} %collective-permute-done.23, bf16[1024,256]{1,0:T(8,128)(2,1)S(1)} %get-tuple-element.106, bf16[1024,256]{1,0:T(8,128)(2,1)S(1)} %get-tuple-element.104, bf16[1024,256]{1,0:T(8,128)(2,1)S(1)} %get-tuple-element.102), kind=kOutput, calls=%fused_computation | convolution fusion | flops 1080033280 | bytes 10485764 | tf_op jit(solution)/shard_map/dot_general | solution.py:38
  118.8 1.6 %collective-permute-done.22 = f32[1024,128]{1,0:T(8,128)S(1)} collective-permute-done((f32[1024,128]{1,0:T(8,128)S(1)}, f32[1024,128]{1,0:T(8,128)S(1)}, u32[]{:S(2)}, u32[]{:S(2)}) %collective-permute-start.22) | collective-permute-done | bytes 524320 | tf_op jit(solution)/shard_map/ppermute | solution.py:65
  120.4 1.6 %fusion.4 = f32[1024,512]{1,0:T(8,128)} fusion(f32[1024,256]{1,0:T(8,128)S(1)} %convolution_add_fusion, f32[1024,256]{1,0:T(8,128)S(1)} %convolution_add_fusion.1, f32[1024,128]{1,0:T(8,128)S(1)} %collective-permute-done.22, f32[1024,128]{1,0:T(8,128)S(1)} %collective-permute-done.15, f32[1024,128]{1,0:T(8,128)S(1)} %collective-permute-done.14, ...), kind=kLoop, calls=%fused_computation.6 | loop fusion | flops 3145728 | bytes 6291460 | tf_op jit(solution)/shard_map/mul | solution.py:182
  (39 shorter events, 1.2 us)
Async XLA Ops:
  0.6 6.0 %copy-start.1 = (bf16[1024,512]{1,0:T(8,128)(2,1)S(1)}, bf16[1024,512]{1,0:T(8,128)(2,1)}, u32[]{:S(2)}) copy-start(bf16[1024,512]{1,0:T(8,128)(2,1)} %param.5) | copy-start | bytes 3145732
  0.6 6.5 %copy-start.2 = (bf16[1024,1024]{1,0:T(8,128)(2,1)S(1)}, bf16[1024,1024]{1,0:T(8,128)(2,1)}, u32[]{:S(2)}) copy-start(bf16[1024,1024]{1,0:T(8,128)(2,1)} %param.6) | copy-start | bytes 6291460
  2.6 4.6 %collective-permute-start = (bf16[1024,1024]{1,0:T(8,128)(2,1)}, bf16[1024,1024]{1,0:T(8,128)(2,1)}, u32[]{:S(2)}, u32[]{:S(2)}) collective-permute-start(bf16[1024,1024]{1,0:T(8,128)(2,1)} %param.6), channel_id=1, source_target_pairs={{0,1},{1,0},{2,3},{3,2},{4,5},{5,4},{6,7},{7,6},{8,9},{9,8},{10,11... | collective-permute-start | bytes 6291464 | tf_op jit(solution)/shard_map/ppermute | solution.py:71
  3.0 9.7 %collective-permute-start.1 = (bf16[1024,128]{1,0:T(8,128)(2,1)}, bf16[1024,128]{1,0:T(8,128)(2,1)S(1)}, u32[]{:S(2)}, u32[]{:S(2)}) collective-permute-start(bf16[1024,128]{1,0:T(8,128)(2,1)} %slice_select_fusion.1), channel_id=1, source_target_pairs={{0,2},{1,3},{2,0},{3,1},{4,6},{5,7},{6,4},{7,5},{8,10},{9,11},{10,... | collective-permute-start | bytes 786440 | tf_op jit(solution)/shard_map/ppermute | solution.py:65
  9.0 17.6 %copy-start = (bf16[1024,512]{1,0:T(8,128)(2,1)S(1)}, bf16[1024,512]{1,0:T(8,128)(2,1)}, u32[]{:S(2)}) copy-start(bf16[1024,512]{1,0:T(8,128)(2,1)} %param.4) | copy-start | bytes 3145732
  12.8 13.8 %collective-permute-start.3 = (bf16[1024,256]{1,0:T(8,128)(2,1)S(1)}, bf16[1024,256]{1,0:T(8,128)(2,1)S(1)}, u32[]{:S(2)}, u32[]{:S(2)}) collective-permute-start(bf16[1024,256]{1,0:T(8,128)(2,1)S(1)} %pad_maximum_fusion.3), channel_id=1, source_target_pairs={{0,2},{1,3},{2,0},{3,1},{4,6},{5,7},{6,4},{7,5},{8,10},{9,11},{10,... | collective-permute-start | bytes 1572872 | tf_op jit(solution)/shard_map/ppermute | solution.py:65
  14.7 14.2 %collective-permute-start.2 = (bf16[1024,128]{1,0:T(8,128)(2,1)S(1)}, bf16[1024,128]{1,0:T(8,128)(2,1)S(1)}, u32[]{:S(2)}, u32[]{:S(2)}) collective-permute-start(bf16[1024,128]{1,0:T(8,128)(2,1)S(1)} %broadcast_select_fusion.18), channel_id=1, source_target_pairs={{0,8},{1,9},{2,10},{3,11},{4,12},{5,13},{6,14},{7,15},{8,0},{9,1},... | collective-permute-start | bytes 786440 | tf_op jit(solution)/shard_map/ppermute | solution.py:77
  29.0 12.6 %collective-permute-start.4 = (bf16[1024,128]{1,0:T(8,128)(2,1)S(1)}, bf16[1024,128]{1,0:T(8,128)(2,1)S(1)}, u32[]{:S(2)}, u32[]{:S(2)}) collective-permute-start(bf16[1024,128]{1,0:T(8,128)(2,1)S(1)} %broadcast_select_fusion.15), channel_id=1, source_target_pairs={{0,4},{1,5},{2,6},{3,7},{4,0},{5,1},{6,2},{7,3},{8,12},{9,13},{10,... | collective-permute-start | bytes 786440 | tf_op jit(solution)/shard_map/ppermute | solution.py:68
  29.7 16.9 %collective-permute-start.5 = (bf16[1024,128]{1,0:T(8,128)(2,1)S(1)}, bf16[1024,128]{1,0:T(8,128)(2,1)S(1)}, u32[]{:S(2)}, u32[]{:S(2)}) collective-permute-start(bf16[1024,128]{1,0:T(8,128)(2,1)S(1)} %get-tuple-element.130), channel_id=1, source_target_pairs={{0,8},{1,9},{2,10},{3,11},{4,12},{5,13},{6,14},{7,15},{8,0},{9,1},... | collective-permute-start | bytes 786440 | tf_op jit(solution)/shard_map/ppermute | solution.py:77
  33.1 13.4 %collective-permute-start.6 = (bf16[1024,256]{1,0:T(8,128)(2,1)S(1)}, bf16[1024,256]{1,0:T(8,128)(2,1)S(1)}, u32[]{:S(2)}, u32[]{:S(2)}) collective-permute-start(bf16[1024,256]{1,0:T(8,128)(2,1)S(1)} %pad_maximum_fusion.4), channel_id=1, source_target_pairs={{0,2},{1,3},{2,0},{3,1},{4,6},{5,7},{6,4},{7,5},{8,10},{9,11},{10,... | collective-permute-start | bytes 1572872 | tf_op jit(solution)/shard_map/ppermute | solution.py:65
  46.6 6.8 %collective-permute-start.9 = (bf16[1024,128]{1,0:T(8,128)(2,1)S(1)}, bf16[1024,128]{1,0:T(8,128)(2,1)S(1)}, u32[]{:S(2)}, u32[]{:S(2)}) collective-permute-start(bf16[1024,128]{1,0:T(8,128)(2,1)S(1)} %broadcast_select_fusion.12), channel_id=1, source_target_pairs={{0,2},{1,3},{2,0},{3,1},{4,6},{5,7},{6,4},{7,5},{8,10},{9,11},{10,... | collective-permute-start | bytes 786440 | tf_op jit(solution)/shard_map/ppermute | solution.py:65
  47.2 10.9 %collective-permute-start.7 = (bf16[1024,128]{1,0:T(8,128)(2,1)S(1)}, bf16[1024,128]{1,0:T(8,128)(2,1)S(1)}, u32[]{:S(2)}, u32[]{:S(2)}) collective-permute-start(bf16[1024,128]{1,0:T(8,128)(2,1)S(1)} %broadcast_select_fusion.13), channel_id=1, source_target_pairs={{0,4},{1,5},{2,6},{3,7},{4,0},{5,1},{6,2},{7,3},{8,12},{9,13},{10,... | collective-permute-start | bytes 786440 | tf_op jit(solution)/shard_map/ppermute | solution.py:68
  47.7 13.1 %collective-permute-start.8 = (bf16[1024,128]{1,0:T(8,128)(2,1)S(1)}, bf16[1024,128]{1,0:T(8,128)(2,1)S(1)}, u32[]{:S(2)}, u32[]{:S(2)}) collective-permute-start(bf16[1024,128]{1,0:T(8,128)(2,1)S(1)} %get-tuple-element.127), channel_id=1, source_target_pairs={{0,8},{1,9},{2,10},{3,11},{4,12},{5,13},{6,14},{7,15},{8,0},{9,1},... | collective-permute-start | bytes 786440 | tf_op jit(solution)/shard_map/ppermute | solution.py:77
  53.4 13.7 %collective-permute-start.12 = (f32[1024,128]{1,0:T(8,128)S(1)}, f32[1024,128]{1,0:T(8,128)S(1)}, u32[]{:S(2)}, u32[]{:S(2)}) collective-permute-start(f32[1024,128]{1,0:T(8,128)S(1)} %convolution_add_fusion.5), channel_id=1, source_target_pairs={{0,2},{1,3},{2,0},{3,1},{4,6},{5,7},{6,4},{7,5},{8,10},{9,11},{10,... | collective-permute-start | bytes 1572872 | tf_op jit(solution)/shard_map/ppermute | solution.py:65
  60.9 17.2 %collective-permute-start.10 = (bf16[1024,256]{1,0:T(8,128)(2,1)S(1)}, bf16[1024,256]{1,0:T(8,128)(2,1)S(1)}, u32[]{:S(2)}, u32[]{:S(2)}) collective-permute-start(bf16[1024,256]{1,0:T(8,128)(2,1)S(1)} %maximum_select_fusion), channel_id=1, source_target_pairs={{0,4},{1,5},{2,6},{3,7},{4,0},{5,1},{6,2},{7,3},{8,12},{9,13},{10,... | collective-permute-start | bytes 1572872 | tf_op jit(solution)/shard_map/ppermute | solution.py:68
  61.8 17.9 %collective-permute-start.11 = (bf16[1024,128]{1,0:T(8,128)(2,1)S(1)}, bf16[1024,128]{1,0:T(8,128)(2,1)S(1)}, u32[]{:S(2)}, u32[]{:S(2)}) collective-permute-start(bf16[1024,128]{1,0:T(8,128)(2,1)S(1)} %get-tuple-element.111), channel_id=1, source_target_pairs={{0,8},{1,9},{2,10},{3,11},{4,12},{5,13},{6,14},{7,15},{8,0},{9,1},... | collective-permute-start | bytes 786440 | tf_op jit(solution)/shard_map/ppermute | solution.py:77
  63.9 26.3 %collective-permute-start.16 = (bf16[1024,256]{1,0:T(8,128)(2,1)S(1)}, bf16[1024,256]{1,0:T(8,128)(2,1)S(1)}, u32[]{:S(2)}, u32[]{:S(2)}) collective-permute-start(bf16[1024,256]{1,0:T(8,128)(2,1)S(1)} %slice.106), channel_id=1, source_target_pairs={{0,8},{1,9},{4,12},{5,13},{10,2},{11,3},{14,6},{15,7},{16,24},{17,... | collective-permute-start | bytes 1572872 | tf_op jit(solution)/shard_map/ppermute | solution.py:74
  67.1 13.7 %collective-permute-start.14 = (f32[1024,128]{1,0:T(8,128)S(1)}, f32[1024,128]{1,0:T(8,128)S(1)}, u32[]{:S(2)}, u32[]{:S(2)}) collective-permute-start(f32[1024,128]{1,0:T(8,128)S(1)} %convolution_add_fusion.4), channel_id=1, source_target_pairs={{0,2},{1,3},{2,0},{3,1},{4,6},{5,7},{6,4},{7,5},{8,10},{9,11},{10,... | collective-permute-start | bytes 1572872 | tf_op jit(solution)/shard_map/ppermute | solution.py:65
  79.8 18.6 %collective-permute-start.13 = (bf16[1024,256]{1,0:T(8,128)(2,1)S(1)}, bf16[1024,256]{1,0:T(8,128)(2,1)S(1)}, u32[]{:S(2)}, u32[]{:S(2)}) collective-permute-start(bf16[1024,256]{1,0:T(8,128)(2,1)S(1)} %maximum_select_fusion.1), channel_id=1, source_target_pairs={{0,4},{1,5},{2,6},{3,7},{4,0},{5,1},{6,2},{7,3},{8,12},{9,13},{10,... | collective-permute-start | bytes 1572872 | tf_op jit(solution)/shard_map/ppermute | solution.py:68
  80.0 23.7 %collective-permute-start.19 = (bf16[1024,512]{1,0:T(8,128)(2,1)S(1)}, bf16[1024,512]{1,0:T(8,128)(2,1)S(1)}, u32[]{:S(2)}, u32[]{:S(2)}) collective-permute-start(bf16[1024,512]{1,0:T(8,128)(2,1)S(1)} %pad_maximum_fusion.2), channel_id=1, source_target_pairs={{0,1},{1,0},{2,3},{3,2},{4,5},{5,4},{6,7},{7,6},{8,9},{9,8},{10,11... | collective-permute-start | bytes 3145736 | tf_op jit(solution)/shard_map/ppermute | solution.py:71
  80.1 22.5 %collective-permute-start.21 = (bf16[1024,512]{1,0:T(8,128)(2,1)S(1)}, bf16[1024,512]{1,0:T(8,128)(2,1)S(1)}, u32[]{:S(2)}, u32[]{:S(2)}) collective-permute-start(bf16[1024,512]{1,0:T(8,128)(2,1)S(1)} %copy-done.1), channel_id=1, source_target_pairs={{0,1},{1,0},{2,3},{3,2},{4,5},{5,4},{6,7},{7,6},{8,9},{9,8},{10,11... | collective-permute-start | bytes 3145736 | tf_op jit(solution)/shard_map/ppermute | solution.py:71
  80.8 21.8 %collective-permute-start.15 = (f32[1024,128]{1,0:T(8,128)S(1)}, f32[1024,128]{1,0:T(8,128)S(1)}, u32[]{:S(2)}, u32[]{:S(2)}) collective-permute-start(f32[1024,128]{1,0:T(8,128)S(1)} %convolution_add_fusion.3), channel_id=1, source_target_pairs={{0,2},{1,3},{2,0},{3,1},{4,6},{5,7},{6,4},{7,5},{8,10},{9,11},{10,... | collective-permute-start | bytes 1572872 | tf_op jit(solution)/shard_map/ppermute | solution.py:65
  100.0 13.4 %collective-permute-start.17 = (bf16[1024,256]{1,0:T(8,128)(2,1)S(1)}, bf16[1024,256]{1,0:T(8,128)(2,1)S(1)}, u32[]{:S(2)}, u32[]{:S(2)}) collective-permute-start(bf16[1024,256]{1,0:T(8,128)(2,1)S(1)} %broadcast_select_fusion.8), channel_id=1, source_target_pairs={{0,4},{1,5},{2,6},{3,7},{4,0},{5,1},{6,2},{7,3},{8,12},{9,13},{10,... | collective-permute-start | bytes 1572872 | tf_op jit(solution)/shard_map/ppermute | solution.py:68
  103.7 7.4 %collective-permute-start.18 = (bf16[1024,512]{1,0:T(8,128)(2,1)S(1)}, bf16[1024,512]{1,0:T(8,128)(2,1)S(1)}, u32[]{:S(2)}, u32[]{:S(2)}) collective-permute-start(bf16[1024,512]{1,0:T(8,128)(2,1)S(1)} %get-tuple-element.101), channel_id=1, source_target_pairs={{0,1},{1,0},{2,3},{3,2},{4,5},{5,4},{6,7},{7,6},{8,9},{9,8},{10,11... | collective-permute-start | bytes 3145736 | tf_op jit(solution)/shard_map/ppermute | solution.py:71
  104.2 5.6 %collective-permute-start.20 = (bf16[1024,256]{1,0:T(8,128)(2,1)S(1)}, bf16[1024,256]{1,0:T(8,128)(2,1)S(1)}, u32[]{:S(2)}, u32[]{:S(2)}) collective-permute-start(bf16[1024,256]{1,0:T(8,128)(2,1)S(1)} %get-tuple-element.109), channel_id=1, source_target_pairs={{0,1},{1,0},{2,3},{3,2},{4,5},{5,4},{6,7},{7,6},{8,9},{9,8},{10,11... | collective-permute-start | bytes 1572872 | tf_op jit(solution)/shard_map/ppermute | solution.py:71
  104.7 15.7 %collective-permute-start.22 = (f32[1024,128]{1,0:T(8,128)S(1)}, f32[1024,128]{1,0:T(8,128)S(1)}, u32[]{:S(2)}, u32[]{:S(2)}) collective-permute-start(f32[1024,128]{1,0:T(8,128)S(1)} %convolution_add_fusion.2), channel_id=1, source_target_pairs={{0,2},{1,3},{2,0},{3,1},{4,6},{5,7},{6,4},{7,5},{8,10},{9,11},{10,... | collective-permute-start | bytes 1572872 | tf_op jit(solution)/shard_map/ppermute | solution.py:65
  113.5 2.0 %collective-permute-start.23 = (bf16[1024,256]{1,0:T(8,128)(2,1)S(1)}, bf16[1024,256]{1,0:T(8,128)(2,1)S(1)}, u32[]{:S(2)}, u32[]{:S(2)}) collective-permute-start(bf16[1024,256]{1,0:T(8,128)(2,1)S(1)} %get-tuple-element.107), channel_id=1, source_target_pairs={{0,1},{1,0},{2,3},{3,2},{4,5},{5,4},{6,7},{7,6},{8,9},{9,8},{10,11... | collective-permute-start | bytes 1572872 | tf_op jit(solution)/shard_map/ppermute | solution.py:71

commit v18 on v15

--- a/solution.py
+++ b/solution.py
@@ -93,6 +93,8 @@
         e = [columns(expected_cot, i, i + 1) for i in range(4)]
         v = [columns(value_next, i, i + 1) for i in range(4)]
         x1 = cross(jnp.where(home, v[0], e[0]))
+        rows = e[3].shape[0] // 2
+        j0 = home_jump(e[3][:rows])
         t_other = swap(transition)
         e2 = after(e[2], x1)
         j1 = jump(jnp.where(home, x1, e2))
@@ -101,16 +103,19 @@
         def adjoint_of(near, far):
             return tdot(t_near, near) + tdot(t_next, far)
 
-        v1, e1 = together((v[1], e[1]), x1, t_near)
+        v1, e1 = together((v[1], e[1]), x1, t_near, j0)
         x2 = cross(jnp.concatenate([jnp.where(home, v1, e1), v[2]], 1))
         x2, v_across2 = columns(x2, 0, 1), columns(x2, 1, 2)
+        near, far = together((e[3][:rows], j0), x1)
+        a3_top = jnp.where(home, near, far)
+        a3_top_next = step(a3_top)
         second = jnp.where(home, x2, e[3])
         j2 = jump(second)
         near, far = together((j1, v[0]), second)
         third_cross = jnp.where(home, near, far)
         x3 = cross(jnp.concatenate([third_cross, v[3]], 1))
         x3, v_across3 = columns(x3, 0, 1), columns(x3, 1, 2)
-        near, far = together((x1, j1), third_cross)
+        near, far = together((x1, j1), third_cross, a3_top_next)
         b0 = jnp.where(home, near, far)
         b0_next = step(b0)
         third = jnp.where(home, e[0], x3)
@@ -131,7 +136,8 @@
         a0b2_next = step(a0b2)
         sum2 = adjoint_of(columns(a0b2, 1, 2), columns(a0b2_next, 1, 2))
         part2 = cross(after(sum2, part1))
-        j5 = home_jump(after(columns(expected_cot, 2, 4), j3))
+        rest = jnp.concatenate([e[2], e[3][rows:]], 0)
+        j5 = home_jump(after(rest, j3))
         near, both, far = together((e[1], j4, x4), sum2, part0)
         a1b3 = jnp.where(home, jnp.concatenate([near, both], 1), jnp.concatenate([both, far], 1))
         a1b3_next = step(a1b3)
@@ -147,11 +153,11 @@
             [jnp.where(home, parts[2], parts[0]), jnp.where(home, parts[3], parts[1]), parts[4], parts[5]], 1
         )
         v_across_other = swap(v_across)
-        near, far = together((columns(expected_cot, 2, 4), j5), a1b3_next, part1)
-        a23 = jnp.where(home, near, far)
-        a23_next = step(a23)
+        near, far = together((rest, j5), a1b3_next, part1)
+        a_rest = jnp.where(home, near, far)
+        a_rest_next = step(a_rest)
         b0, b0_next, b1, b1_next, a0b2, a0b2_next = together(
-            (b0, b0_next, b1, b1_next, a0b2, a0b2_next), a1b3_next, sum3, part2, a23
+            (b0, b0_next, b1, b1_next, a0b2, a0b2_next), a1b3_next, sum3, part2, a_rest
         )
         a0, a0_next = columns(a0b2, 0, 1), columns(a0b2_next, 0, 1)
         a1, a1_next = columns(a1b3, 0, 1), columns(a1b3_next, 0, 1)
@@ -169,7 +175,12 @@
             jnp.concatenate([columns(value_next, 0, 2), columns(v_other, 0, 2)], 1),
         )
         own01 = adjoint_of(jnp.concatenate([a0, a1], 1), jnp.concatenate([a0_next, a1_next], 1))
-        near, far = together((a23, a23_next), grad, own01)
+        near, far, near_top, far_top = together((a_rest, a_rest_next, a3_top, a3_top_next), grad, own01)
+
+        def two_quarters(rest, top):
+            return jnp.concatenate([rest[: 2 * rows], jnp.concatenate([top, rest[2 * rows :]], 0)], 1)
+
+        near, far = two_quarters(near, near_top), two_quarters(far, far_top)
         a23_own, a23_swapped = own_and_swapped(near, far)
         grad = df * (grad + dott(
             jnp.concatenate([a23_own, a23_swapped], 1),

time: 122 us -> 120 us (0.984)
  waiting for transfers between devices: 62.7 us -> 52.8 us
  starting transfers between devices: 32.2 us -> 38.9 us
    ppermute x8, waiting for transfers between devices: 24.1 us -> 16.3 us  [cross(): return lax.ppermute(a, AXES, cross_pairs)]
    ppermute x1 -> x2, starting transfers between devices: 2.91 us -> 7.68 us  [home_jump(): return lax.ppermute(a, AXES, home_jump_pairs)]
    ppermute x1 -> x2, waiting for transfers between devices: 3.99 us -> 0.56 us  [home_jump(): return lax.ppermute(a, AXES, home_jump_pairs)]
    ppermute x5 -> x6, starting transfers between devices: 3.84 us -> 7.21 us  [step(): return lax.ppermute(a, AXES, step_pairs)]
    ppermute x4, starting transfers between devices: 9.25 us -> 6.45 us  [jump(): return lax.ppermute(a, AXES, jump_pairs)]
    ppermute x8, starting transfers between devices: 14.4 us -> 15.8 us  [cross(): return lax.ppermute(a, AXES, cross_pairs)]
    ppermute x5 -> x6, waiting for transfers between devices: 31.1 us -> 31.7 us  [step(): return lax.ppermute(a, AXES, step_pairs)]
  transfers between devices with their start and end apart: 24 -> 26, of which waited for: 13 -> 12; matrix products, arithmetic and copies ran while one was open for 19% -> 20% of each run, Pallas kernels for 0% -> 0%
where the time goes in v18:
time: 120 us; the launch traced here: 119 us
  waiting for transfers between devices  52.8 us (44%)
  starting transfers between devices  38.9 us (32%)
  matrix products  16 us (13%)
  other arithmetic  8.9 us (7%)
  between operations  1.84 us (2%)
    ppermute x6, waiting for transfers between devices, step(): return lax.ppermute(a, AXES, step_pairs)  31.7 us
    ppermute x8, waiting for transfers between devices, cross(): return lax.ppermute(a, AXES, cross_pairs)  16.3 us
    ppermute x8, starting transfers between devices, cross(): return lax.ppermute(a, AXES, cross_pairs)  15.8 us
    dot_general x12, matrix products, tdot(): lax.dot_general(a, b, (((0,), (0,)), ((), ())), preferred_element_type=jn...  9.04 us
    ppermute x2, starting transfers between devices, home_jump(): return lax.ppermute(a, AXES, home_jump_pairs)  7.68 us
    ppermute x6, starting transfers between devices, step(): return lax.ppermute(a, AXES, step_pairs)  7.21 us
    dot_general x3, matrix products, dott(): lax.dot_general(a, b, (((1,), (1,)), ((), ())), preferred_element_type=jn...  6.99 us
    ppermute x4, starting transfers between devices, jump(): return lax.ppermute(a, AXES, jump_pairs)  6.45 us
  transfers between devices with their start and end apart: 26, of which 12 were waited for; matrix products, arithmetic and copies ran while one was open for 20% of the time, Pallas kernels for 0%

profile of v18, /device:TPU:0, one launch (start us, length us, event | category | flops | bytes accessed | tf_op | source)
XLA Modules:
  0.0 119.3 jit_solution(1596382411581865898)
XLA Ops:
  0.6 0.5 collective-permute-start
  1.2 2.3 %fusion.36 = (bf16[1024,128]{1,0:T(8,128)(2,1)S(1)}, bf16[1024,128]{1,0:T(8,128)(2,1)}, bf16[1024,128]{1,0:T(8,128)(2,1)S(1)}, bf16[1024,128]{1,0:T(8,128)(2,1)S...) fusion(bf16[1024,512]{1,0:T(8,128)(2,1)} %param.4, ...), kind=kLoop, calls=%fused_computation.81 | loop fusion | flops 131072 | bytes 3932161 | tf_op jit(solution)/shard_map/slice | solution.py:88
  3.5 2.6 %collective-permute-start.1 = (bf16[1024,128]{1,0:T(8,128)(2,1)}, bf16[1024,128]{1,0:T(8,128)(2,1)S(1)}, u32[]{:S(2)}, u32[]{:S(2)}) collective-permute-start(bf16[1024,128]{1,0:T(8,128)(2,1)} %get-tuple-element.111), channel_id=1, source_target_pairs={{0,2},{1,3},{2,0},{3,1},{4,6},{5,7},{6,4},{7,5},{8,10},{9,11},{10,... | collective-permute-start | bytes 786440 | tf_op jit(solution)/shard_map/ppermute | solution.py:65
  6.1 4.5 %collective-permute-start.3 = (bf16[512,128]{1,0:T(8,128)(2,1)S(1)}, bf16[512,128]{1,0:T(8,128)(2,1)S(1)}, u32[]{:S(2)}, u32[]{:S(2)}) collective-permute-start(bf16[512,128]{1,0:T(8,128)(2,1)S(1)} %get-tuple-element.53), channel_id=1, source_target_pairs={{0,8},{1,9},{4,12},{5,13},{10,2},{11,3},{14,6},{15,7},{16,24},{17,... | collective-permute-start | bytes 393224 | tf_op jit(solution)/shard_map/ppermute | solution.py:74
  10.6 2.5 %broadcast_select_fusion.1 = (bf16[1024,1024]{1,0:T(8,128)(2,1)S(1)}, bf16[1024,1024]{1,0:T(8,128)(2,1)S(1)}) fusion(bf16[1024,1024]{1,0:T(8,128)(2,1)} %param.6, bf16[1024,1024]{1,0:T(8,128)(2,1)} %collective-permute-done, pred[]{:T(512)S(6)} %eq.8), kind=kLoop, calls=%fused_computation.8 | loop fusion | flops 2097152 | bytes 8388609 | tf_op jit(solution)/shard_map/jit(_where)/select_n | solution.py:101
  13.1 0.6 collective-permute-done.3
  13.8 3.9 %collective-permute-start.4 = (bf16[1024,256]{1,0:T(8,128)(2,1)S(1)}, bf16[1024,256]{1,0:T(8,128)(2,1)S(1)}, u32[]{:S(2)}, u32[]{:S(2)}) collective-permute-start(bf16[1024,256]{1,0:T(8,128)(2,1)S(1)} %pad_maximum_fusion.3), channel_id=1, source_target_pairs={{0,2},{1,3},{2,0},{3,1},{4,6},{5,7},{6,4},{7,5},{8,10},{9,11},{10,... | collective-permute-start | bytes 1572872 | tf_op jit(solution)/shard_map/ppermute | solution.py:65
  17.9 3.8 %collective-permute-start.5 = (bf16[512,128]{1,0:T(8,128)(2,1)S(1)}, bf16[512,128]{1,0:T(8,128)(2,1)S(1)}, u32[]{:S(2)}, u32[]{:S(2)}) collective-permute-start(bf16[512,128]{1,0:T(8,128)(2,1)S(1)} %broadcast_select_fusion.20), channel_id=1, source_target_pairs={{0,4},{1,5},{2,6},{3,7},{4,0},{5,1},{6,2},{7,3},{8,12},{9,13},{10,... | collective-permute-start | bytes 393224 | tf_op jit(solution)/shard_map/ppermute | solution.py:68
  21.7 7.8 %collective-permute-done.4 = bf16[1024,256]{1,0:T(8,128)(2,1)S(1)} collective-permute-done((bf16[1024,256]{1,0:T(8,128)(2,1)S(1)}, bf16[1024,256]{1,0:T(8,128)(2,1)S(1)}, u32[]{:S(2)}, u32[]{:S(2)}) %collective-permute-start.4) | collective-permute-done | bytes 524320 | tf_op jit(solution)/shard_map/ppermute | solution.py:65
  29.5 2.4 %collective-permute-done.2 = bf16[1024,128]{1,0:T(8,128)(2,1)S(1)} collective-permute-done((bf16[1024,128]{1,0:T(8,128)(2,1)S(1)}, bf16[1024,128]{1,0:T(8,128)(2,1)S(1)}, u32[]{:S(2)}, u32[]{:S(2)}) %collective-permute-start.2) | collective-permute-done | bytes 262176 | tf_op jit(solution)/shard_map/ppermute | solution.py:77
  32.0 0.2 collective-permute-start.6
  32.2 3.4 %collective-permute-start.7 = (bf16[1024,128]{1,0:T(8,128)(2,1)S(1)}, bf16[1024,128]{1,0:T(8,128)(2,1)S(1)}, u32[]{:S(2)}, u32[]{:S(2)}) collective-permute-start(bf16[1024,128]{1,0:T(8,128)(2,1)S(1)} %get-tuple-element.132), channel_id=1, source_target_pairs={{0,8},{1,9},{2,10},{3,11},{4,12},{5,13},{6,14},{7,15},{8,0},{9,1},... | collective-permute-start | bytes 786440 | tf_op jit(solution)/shard_map/ppermute | solution.py:77
  35.6 0.4 collective-permute-start.8
  36.0 8.3 %collective-permute-done.6 = bf16[1024,128]{1,0:T(8,128)(2,1)S(1)} collective-permute-done((bf16[1024,128]{1,0:T(8,128)(2,1)S(1)}, bf16[1024,128]{1,0:T(8,128)(2,1)S(1)}, u32[]{:S(2)}, u32[]{:S(2)}) %collective-permute-start.6) | collective-permute-done | bytes 262176 | tf_op jit(solution)/shard_map/ppermute | solution.py:68
  44.3 0.7 fusion.44
  45.1 0.8 convolution_add_fusion.5
  45.8 2.3 %collective-permute-done.8 = bf16[1024,256]{1,0:T(8,128)(2,1)S(1)} collective-permute-done((bf16[1024,256]{1,0:T(8,128)(2,1)S(1)}, bf16[1024,256]{1,0:T(8,128)(2,1)S(1)}, u32[]{:S(2)}, u32[]{:S(2)}) %collective-permute-start.8) | collective-permute-done | bytes 524320 | tf_op jit(solution)/shard_map/ppermute | solution.py:65
  48.3 0.7 collective-permute-start.11
  49.0 0.4 collective-permute-start.9
  49.5 1.1 collective-permute-start.10
  50.6 4.9 %collective-permute-done.11 = bf16[1024,128]{1,0:T(8,128)(2,1)S(1)} collective-permute-done((bf16[1024,128]{1,0:T(8,128)(2,1)S(1)}, bf16[1024,128]{1,0:T(8,128)(2,1)S(1)}, u32[]{:S(2)}, u32[]{:S(2)}) %collective-permute-start.11) | collective-permute-done | bytes 262176 | tf_op jit(solution)/shard_map/ppermute | solution.py:65
  55.5 0.3 collective-permute-start.14
  55.8 3.4 %collective-permute-done.9 = bf16[1024,128]{1,0:T(8,128)(2,1)S(1)} collective-permute-done((bf16[1024,128]{1,0:T(8,128)(2,1)S(1)}, bf16[1024,128]{1,0:T(8,128)(2,1)S(1)}, u32[]{:S(2)}, u32[]{:S(2)}) %collective-permute-start.9) | collective-permute-done | bytes 262176 | tf_op jit(solution)/shard_map/ppermute | solution.py:68
  59.2 0.7 fusion.45
  59.9 0.8 convolution_add_fusion.4
  60.7 1.4 %collective-permute-done.10 = bf16[1024,128]{1,0:T(8,128)(2,1)S(1)} collective-permute-done((bf16[1024,128]{1,0:T(8,128)(2,1)S(1)}, bf16[1024,128]{1,0:T(8,128)(2,1)S(1)}, u32[]{:S(2)}, u32[]{:S(2)}) %collective-permute-start.10) | collective-permute-done | bytes 262176 | tf_op jit(solution)/shard_map/ppermute | solution.py:77
  62.1 0.2 maximum_select_fusion
  62.3 0.1 collective-permute-start.12
  63.1 1.9 %collective-permute-start.13 = (bf16[1024,128]{1,0:T(8,128)(2,1)S(1)}, bf16[1024,128]{1,0:T(8,128)(2,1)S(1)}, u32[]{:S(2)}, u32[]{:S(2)}) collective-permute-start(bf16[1024,128]{1,0:T(8,128)(2,1)S(1)} %broadcast_select_fusion.11), channel_id=1, source_target_pairs={{0,8},{1,9},{2,10},{3,11},{4,12},{5,13},{6,14},{7,15},{8,0},{9,1},... | collective-permute-start | bytes 786440 | tf_op jit(solution)/shard_map/ppermute | solution.py:77
  65.0 3.2 %collective-permute-start.18 = (bf16[1536,128]{1,0:T(8,128)(2,1)S(1)}, bf16[1536,128]{1,0:T(8,128)(2,1)S(1)}, u32[]{:S(2)}, u32[]{:S(2)}) collective-permute-start(bf16[1536,128]{1,0:T(8,128)(2,1)S(1)} %pad_maximum_fusion.7), channel_id=1, source_target_pairs={{0,8},{1,9},{4,12},{5,13},{10,2},{11,3},{14,6},{15,7},{16,24},{17,... | collective-permute-start | bytes 1179656 | tf_op jit(solution)/shard_map/ppermute | solution.py:74
  68.2 0.1 constant_dynamic-update-slice_fusion.4
  68.3 0.1 constant_dynamic-update-slice_fusion.3
  68.5 0.1 collective-permute-start.16
  68.5 10.4 %collective-permute-done.12 = bf16[1024,256]{1,0:T(8,128)(2,1)S(1)} collective-permute-done((bf16[1024,256]{1,0:T(8,128)(2,1)S(1)}, bf16[1024,256]{1,0:T(8,128)(2,1)S(1)}, u32[]{:S(2)}, u32[]{:S(2)}) %collective-permute-start.12) | collective-permute-done | bytes 524320 | tf_op jit(solution)/shard_map/ppermute | solution.py:68
  78.9 0.8 fusion.21
  79.7 0.8 convolution_add_fusion.3
  80.5 0.2 maximum_select_fusion.1
  80.6 0.1 collective-permute-start.15
  80.7 0.1 pad_maximum_fusion.2
  80.9 0.5 collective-permute-start.23
  81.4 0.1 constant_dynamic-update-slice_fusion.2
  81.5 0.1 constant_dynamic-update-slice_fusion.1
  81.7 4.4 %collective-permute-start.17 = (f32[1024,128]{1,0:T(8,128)S(1)}, f32[1024,128]{1,0:T(8,128)S(1)}, u32[]{:S(2)}, u32[]{:S(2)}) collective-permute-start(f32[1024,128]{1,0:T(8,128)S(1)} %convolution_add_fusion.3), channel_id=1, source_target_pairs={{0,2},{1,3},{2,0},{3,1},{4,6},{5,7},{6,4},{7,5},{8,10},{9,11},{10,... | collective-permute-start | bytes 1572872 | tf_op jit(solution)/shard_map/ppermute | solution.py:65
  86.0 9.6 %collective-permute-done.15 = bf16[1024,256]{1,0:T(8,128)(2,1)S(1)} collective-permute-done((bf16[1024,256]{1,0:T(8,128)(2,1)S(1)}, bf16[1024,256]{1,0:T(8,128)(2,1)S(1)}, u32[]{:S(2)}, u32[]{:S(2)}) %collective-permute-start.15) | collective-permute-done | bytes 524320 | tf_op jit(solution)/shard_map/ppermute | solution.py:68
  95.6 0.8 fusion.30
  96.4 0.8 convolution_add_fusion.2
  97.2 2.6 %collective-permute-start.19 = (bf16[1536,128]{1,0:T(8,128)(2,1)S(1)}, bf16[1536,128]{1,0:T(8,128)(2,1)S(1)}, u32[]{:S(2)}, u32[]{:S(2)}) collective-permute-start(bf16[1536,128]{1,0:T(8,128)(2,1)S(1)} %broadcast_select_fusion.8), channel_id=1, source_target_pairs={{0,4},{1,5},{2,6},{3,7},{4,0},{5,1},{6,2},{7,3},{8,12},{9,13},{10,... | collective-permute-start | bytes 1179656 | tf_op jit(solution)/shard_map/ppermute | solution.py:68
  99.9 0.2 fusion.38
  100.1 0.8 broadcast_select_fusion.3
  101.0 0.1 constant_dynamic-update-slice_fusion
  101.1 0.2 broadcast_select_fusion.7
  101.4 0.6 collective-permute-start.22
  102.0 3.6 %collective-permute-start.24 = (f32[1024,128]{1,0:T(8,128)S(1)}, f32[1024,128]{1,0:T(8,128)S(1)}, u32[]{:S(2)}, u32[]{:S(2)}) collective-permute-start(f32[1024,128]{1,0:T(8,128)S(1)} %convolution_add_fusion.2), channel_id=1, source_target_pairs={{0,2},{1,3},{2,0},{3,1},{4,6},{5,7},{6,4},{7,5},{8,10},{9,11},{10,... | collective-permute-start | bytes 1572872 | tf_op jit(solution)/shard_map/ppermute | solution.py:65
  105.5 0.7 fusion.24
  106.3 0.7 convolution_add_fusion.1
  107.0 1.3 %fusion.8 = f32[1024,1024]{1,0:T(8,128)S(1)} fusion(bf16[1024,256]{1,0:T(8,128)(2,1)S(1)} %collective-permute-done.22, bf16[1024,256]{1,0:T(8,128)(2,1)S(1)} %get-tuple-element.108, bf16[1024,256]{1,0:T(8,128)(2,1)S(1)} %get-tuple-element.105, bf16[1024,256]{1,0:T(8,128)(2,1)S(1)} %get-tuple-element.103), kind=kOutput, calls=%fused_computation.19 | convolution fusion | flops 1077936128 | bytes 6291456 | tf_op jit(solution)/shard_map/dot_general | solution.py:38
  108.3 2.4 %fusion.5 = f32[1024,1024]{1,0:T(8,128)S(1)} fusion(f32[1024,1024]{1,0:T(8,128)S(1)} %fusion.8, bf16[1024,1024]{1,0:T(8,128)(2,1)S(1)} %constant_dynamic-update-slice_fusion, bf16[1024,512]{1,0:T(8,128)(2,1)S(1)} %collective-permute-done.20, bf16[1024,512]{1,0:T(8,128)(2,1)S(1)} %get-tuple-element.100), kind=kOutput, calls=%fused_computation.9 | convolution fusion | flops 2152726528 | bytes 12582912 | tf_op jit(solution)/shard_map/dot_general | solution.py:38
  110.8 0.2 broadcast_select_fusion.5
  111.1 0.7 fusion.33
  111.9 0.8 convolution_add_fusion
  112.6 0.4 collective-permute-done.25
  113.0 3.3 %add_multiply_fusion = f32[1024,1024]{1,0:T(8,128)} fusion(f32[1024,1024]{1,0:T(8,128)S(1)} %fusion.5, f32[]{:T(128)} %bitcast, bf16[1024,256]{1,0:T(8,128)(2,1)S(1)} %collective-permute-done.25, bf16[1024,256]{1,0:T(8,128)(2,1)S(1)} %get-tuple-element.106, bf16[1024,256]{1,0:T(8,128)(2,1)S(1)} %get-tuple-element.104, bf16[1024,256]{1,0:T(8,128)(2,1)S(1)} %get-tuple-element.102), kind=kOutput, calls=%fused_computation | convolution fusion | flops 1080033280 | bytes 10485764 | tf_op jit(solution)/shard_map/dot_general | solution.py:38
  116.4 1.3 %collective-permute-done.24 = f32[1024,128]{1,0:T(8,128)S(1)} collective-permute-done((f32[1024,128]{1,0:T(8,128)S(1)}, f32[1024,128]{1,0:T(8,128)S(1)}, u32[]{:S(2)}, u32[]{:S(2)}) %collective-permute-start.24) | collective-permute-done | bytes 524320 | tf_op jit(solution)/shard_map/ppermute | solution.py:65
  117.7 1.6 %fusion.4 = f32[1024,512]{1,0:T(8,128)} fusion(f32[1024,256]{1,0:T(8,128)S(1)} %convolution_add_fusion, f32[1024,256]{1,0:T(8,128)S(1)} %convolution_add_fusion.1, f32[1024,128]{1,0:T(8,128)S(1)} %collective-permute-done.24, f32[1024,128]{1,0:T(8,128)S(1)} %collective-permute-done.17, f32[1024,128]{1,0:T(8,128)S(1)} %collective-permute-done.16, ...), kind=kLoop, calls=%fused_computation.6 | loop fusion | flops 3145728 | bytes 6291460 | tf_op jit(solution)/shard_map/mul | solution.py:191
  (45 shorter events, 1.2 us)
Async XLA Ops:
  0.6 5.4 %copy-start.1 = (bf16[1024,512]{1,0:T(8,128)(2,1)S(1)}, bf16[1024,512]{1,0:T(8,128)(2,1)}, u32[]{:S(2)}) copy-start(bf16[1024,512]{1,0:T(8,128)(2,1)} %param.4) | copy-start | bytes 3145732
  0.6 10.0 %collective-permute-start = (bf16[1024,1024]{1,0:T(8,128)(2,1)}, bf16[1024,1024]{1,0:T(8,128)(2,1)}, u32[]{:S(2)}, u32[]{:S(2)}) collective-permute-start(bf16[1024,1024]{1,0:T(8,128)(2,1)} %param.6), channel_id=1, source_target_pairs={{0,1},{1,0},{2,3},{3,2},{4,5},{5,4},{6,7},{7,6},{8,9},{9,8},{10,11... | collective-permute-start | bytes 6291464 | tf_op jit(solution)/shard_map/ppermute | solution.py:71
  3.5 10.2 %collective-permute-start.1 = (bf16[1024,128]{1,0:T(8,128)(2,1)}, bf16[1024,128]{1,0:T(8,128)(2,1)S(1)}, u32[]{:S(2)}, u32[]{:S(2)}) collective-permute-start(bf16[1024,128]{1,0:T(8,128)(2,1)} %get-tuple-element.111), channel_id=1, source_target_pairs={{0,2},{1,3},{2,0},{3,1},{4,6},{5,7},{6,4},{7,5},{8,10},{9,11},{10,... | collective-permute-start | bytes 786440 | tf_op jit(solution)/shard_map/ppermute | solution.py:65
  6.1 7.6 %collective-permute-start.3 = (bf16[512,128]{1,0:T(8,128)(2,1)S(1)}, bf16[512,128]{1,0:T(8,128)(2,1)S(1)}, u32[]{:S(2)}, u32[]{:S(2)}) collective-permute-start(bf16[512,128]{1,0:T(8,128)(2,1)S(1)} %get-tuple-element.53), channel_id=1, source_target_pairs={{0,8},{1,9},{4,12},{5,13},{10,2},{11,3},{14,6},{15,7},{16,24},{17,... | collective-permute-start | bytes 393224 | tf_op jit(solution)/shard_map/ppermute | solution.py:74
  13.8 15.6 %collective-permute-start.4 = (bf16[1024,256]{1,0:T(8,128)(2,1)S(1)}, bf16[1024,256]{1,0:T(8,128)(2,1)S(1)}, u32[]{:S(2)}, u32[]{:S(2)}) collective-permute-start(bf16[1024,256]{1,0:T(8,128)(2,1)S(1)} %pad_maximum_fusion.3), channel_id=1, source_target_pairs={{0,2},{1,3},{2,0},{3,1},{4,6},{5,7},{6,4},{7,5},{8,10},{9,11},{10,... | collective-permute-start | bytes 1572872 | tf_op jit(solution)/shard_map/ppermute | solution.py:65
  17.8 14.2 %collective-permute-start.2 = (bf16[1024,128]{1,0:T(8,128)(2,1)S(1)}, bf16[1024,128]{1,0:T(8,128)(2,1)S(1)}, u32[]{:S(2)}, u32[]{:S(2)}) collective-permute-start(bf16[1024,128]{1,0:T(8,128)(2,1)S(1)} %broadcast_select_fusion.18), channel_id=1, source_target_pairs={{0,8},{1,9},{2,10},{3,11},{4,12},{5,13},{6,14},{7,15},{8,0},{9,1},... | collective-permute-start | bytes 786440 | tf_op jit(solution)/shard_map/ppermute | solution.py:77
  17.9 14.1 %collective-permute-start.5 = (bf16[512,128]{1,0:T(8,128)(2,1)S(1)}, bf16[512,128]{1,0:T(8,128)(2,1)S(1)}, u32[]{:S(2)}, u32[]{:S(2)}) collective-permute-start(bf16[512,128]{1,0:T(8,128)(2,1)S(1)} %broadcast_select_fusion.20), channel_id=1, source_target_pairs={{0,4},{1,5},{2,6},{3,7},{4,0},{5,1},{6,2},{7,3},{8,12},{9,13},{10,... | collective-permute-start | bytes 393224 | tf_op jit(solution)/shard_map/ppermute | solution.py:68
  32.0 12.4 %collective-permute-start.6 = (bf16[1024,128]{1,0:T(8,128)(2,1)S(1)}, bf16[1024,128]{1,0:T(8,128)(2,1)S(1)}, u32[]{:S(2)}, u32[]{:S(2)}) collective-permute-start(bf16[1024,128]{1,0:T(8,128)(2,1)S(1)} %broadcast_select_fusion.15), channel_id=1, source_target_pairs={{0,4},{1,5},{2,6},{3,7},{4,0},{5,1},{6,2},{7,3},{8,12},{9,13},{10,... | collective-permute-start | bytes 786440 | tf_op jit(solution)/shard_map/ppermute | solution.py:68
  32.2 16.0 %collective-permute-start.7 = (bf16[1024,128]{1,0:T(8,128)(2,1)S(1)}, bf16[1024,128]{1,0:T(8,128)(2,1)S(1)}, u32[]{:S(2)}, u32[]{:S(2)}) collective-permute-start(bf16[1024,128]{1,0:T(8,128)(2,1)S(1)} %get-tuple-element.132), channel_id=1, source_target_pairs={{0,8},{1,9},{2,10},{3,11},{4,12},{5,13},{6,14},{7,15},{8,0},{9,1},... | collective-permute-start | bytes 786440 | tf_op jit(solution)/shard_map/ppermute | solution.py:77
  35.6 12.5 %collective-permute-start.8 = (bf16[1024,256]{1,0:T(8,128)(2,1)S(1)}, bf16[1024,256]{1,0:T(8,128)(2,1)S(1)}, u32[]{:S(2)}, u32[]{:S(2)}) collective-permute-start(bf16[1024,256]{1,0:T(8,128)(2,1)S(1)} %pad_maximum_fusion.4), channel_id=1, source_target_pairs={{0,2},{1,3},{2,0},{3,1},{4,6},{5,7},{6,4},{7,5},{8,10},{9,11},{10,... | collective-permute-start | bytes 1572872 | tf_op jit(solution)/shard_map/ppermute | solution.py:65
  45.8 3.6 %copy-start = (bf16[1024,512]{1,0:T(8,128)(2,1)S(1)}, bf16[1024,512]{1,0:T(8,128)(2,1)}, u32[]{:S(2)}) copy-start(bf16[1024,512]{1,0:T(8,128)(2,1)} %param.5) | copy-start | bytes 3145732
  48.3 7.2 %collective-permute-start.11 = (bf16[1024,128]{1,0:T(8,128)(2,1)S(1)}, bf16[1024,128]{1,0:T(8,128)(2,1)S(1)}, u32[]{:S(2)}, u32[]{:S(2)}) collective-permute-start(bf16[1024,128]{1,0:T(8,128)(2,1)S(1)} %broadcast_select_fusion.12), channel_id=1, source_target_pairs={{0,2},{1,3},{2,0},{3,1},{4,6},{5,7},{6,4},{7,5},{8,10},{9,11},{10,... | collective-permute-start | bytes 786440 | tf_op jit(solution)/shard_map/ppermute | solution.py:65
  49.0 10.2 %collective-permute-start.9 = (bf16[1024,128]{1,0:T(8,128)(2,1)S(1)}, bf16[1024,128]{1,0:T(8,128)(2,1)S(1)}, u32[]{:S(2)}, u32[]{:S(2)}) collective-permute-start(bf16[1024,128]{1,0:T(8,128)(2,1)S(1)} %broadcast_select_fusion.13), channel_id=1, source_target_pairs={{0,4},{1,5},{2,6},{3,7},{4,0},{5,1},{6,2},{7,3},{8,12},{9,13},{10,... | collective-permute-start | bytes 786440 | tf_op jit(solution)/shard_map/ppermute | solution.py:68
  49.5 12.7 %collective-permute-start.10 = (bf16[1024,128]{1,0:T(8,128)(2,1)S(1)}, bf16[1024,128]{1,0:T(8,128)(2,1)S(1)}, u32[]{:S(2)}, u32[]{:S(2)}) collective-permute-start(bf16[1024,128]{1,0:T(8,128)(2,1)S(1)} %get-tuple-element.129), channel_id=1, source_target_pairs={{0,8},{1,9},{2,10},{3,11},{4,12},{5,13},{6,14},{7,15},{8,0},{9,1},... | collective-permute-start | bytes 786440 | tf_op jit(solution)/shard_map/ppermute | solution.py:77
  55.5 13.0 %collective-permute-start.14 = (f32[1024,128]{1,0:T(8,128)S(1)}, f32[1024,128]{1,0:T(8,128)S(1)}, u32[]{:S(2)}, u32[]{:S(2)}) collective-permute-start(f32[1024,128]{1,0:T(8,128)S(1)} %convolution_add_fusion.5), channel_id=1, source_target_pairs={{0,2},{1,3},{2,0},{3,1},{4,6},{5,7},{6,4},{7,5},{8,10},{9,11},{10,... | collective-permute-start | bytes 1572872 | tf_op jit(solution)/shard_map/ppermute | solution.py:65
  62.3 16.6 %collective-permute-start.12 = (bf16[1024,256]{1,0:T(8,128)(2,1)S(1)}, bf16[1024,256]{1,0:T(8,128)(2,1)S(1)}, u32[]{:S(2)}, u32[]{:S(2)}) collective-permute-start(bf16[1024,256]{1,0:T(8,128)(2,1)S(1)} %maximum_select_fusion), channel_id=1, source_target_pairs={{0,4},{1,5},{2,6},{3,7},{4,0},{5,1},{6,2},{7,3},{8,12},{9,13},{10,... | collective-permute-start | bytes 1572872 | tf_op jit(solution)/shard_map/ppermute | solution.py:68
  63.1 17.3 %collective-permute-start.13 = (bf16[1024,128]{1,0:T(8,128)(2,1)S(1)}, bf16[1024,128]{1,0:T(8,128)(2,1)S(1)}, u32[]{:S(2)}, u32[]{:S(2)}) collective-permute-start(bf16[1024,128]{1,0:T(8,128)(2,1)S(1)} %broadcast_select_fusion.11), channel_id=1, source_target_pairs={{0,8},{1,9},{2,10},{3,11},{4,12},{5,13},{6,14},{7,15},{8,0},{9,1},... | collective-permute-start | bytes 786440 | tf_op jit(solution)/shard_map/ppermute | solution.py:77
  65.0 31.3 %collective-permute-start.18 = (bf16[1536,128]{1,0:T(8,128)(2,1)S(1)}, bf16[1536,128]{1,0:T(8,128)(2,1)S(1)}, u32[]{:S(2)}, u32[]{:S(2)}) collective-permute-start(bf16[1536,128]{1,0:T(8,128)(2,1)S(1)} %pad_maximum_fusion.7), channel_id=1, source_target_pairs={{0,8},{1,9},{4,12},{5,13},{10,2},{11,3},{14,6},{15,7},{16,24},{17,... | collective-permute-start | bytes 1179656 | tf_op jit(solution)/shard_map/ppermute | solution.py:74
  68.5 13.2 %collective-permute-start.16 = (f32[1024,128]{1,0:T(8,128)S(1)}, f32[1024,128]{1,0:T(8,128)S(1)}, u32[]{:S(2)}, u32[]{:S(2)}) collective-permute-start(f32[1024,128]{1,0:T(8,128)S(1)} %convolution_add_fusion.4), channel_id=1, source_target_pairs={{0,2},{1,3},{2,0},{3,1},{4,6},{5,7},{6,4},{7,5},{8,10},{9,11},{10,... | collective-permute-start | bytes 1572872 | tf_op jit(solution)/shard_map/ppermute | solution.py:65
  80.6 15.0 %collective-permute-start.15 = (bf16[1024,256]{1,0:T(8,128)(2,1)S(1)}, bf16[1024,256]{1,0:T(8,128)(2,1)S(1)}, u32[]{:S(2)}, u32[]{:S(2)}) collective-permute-start(bf16[1024,256]{1,0:T(8,128)(2,1)S(1)} %maximum_select_fusion.1), channel_id=1, source_target_pairs={{0,4},{1,5},{2,6},{3,7},{4,0},{5,1},{6,2},{7,3},{8,12},{9,13},{10,... | collective-permute-start | bytes 1572872 | tf_op jit(solution)/shard_map/ppermute | solution.py:68
  80.8 20.1 %collective-permute-start.21 = (bf16[1024,512]{1,0:T(8,128)(2,1)S(1)}, bf16[1024,512]{1,0:T(8,128)(2,1)S(1)}, u32[]{:S(2)}, u32[]{:S(2)}) collective-permute-start(bf16[1024,512]{1,0:T(8,128)(2,1)S(1)} %pad_maximum_fusion.2), channel_id=1, source_target_pairs={{0,1},{1,0},{2,3},{3,2},{4,5},{5,4},{6,7},{7,6},{8,9},{9,8},{10,11... | collective-permute-start | bytes 3145736 | tf_op jit(solution)/shard_map/ppermute | solution.py:71
  80.9 18.9 %collective-permute-start.23 = (bf16[1024,512]{1,0:T(8,128)(2,1)S(1)}, bf16[1024,512]{1,0:T(8,128)(2,1)S(1)}, u32[]{:S(2)}, u32[]{:S(2)}) collective-permute-start(bf16[1024,512]{1,0:T(8,128)(2,1)S(1)} %copy-done), channel_id=1, source_target_pairs={{0,1},{1,0},{2,3},{3,2},{4,5},{5,4},{6,7},{7,6},{8,9},{9,8},{10,11... | collective-permute-start | bytes 3145736 | tf_op jit(solution)/shard_map/ppermute | solution.py:71
  81.7 18.3 %collective-permute-start.17 = (f32[1024,128]{1,0:T(8,128)S(1)}, f32[1024,128]{1,0:T(8,128)S(1)}, u32[]{:S(2)}, u32[]{:S(2)}) collective-permute-start(f32[1024,128]{1,0:T(8,128)S(1)} %convolution_add_fusion.3), channel_id=1, source_target_pairs={{0,2},{1,3},{2,0},{3,1},{4,6},{5,7},{6,4},{7,5},{8,10},{9,11},{10,... | collective-permute-start | bytes 1572872 | tf_op jit(solution)/shard_map/ppermute | solution.py:65
  97.2 13.5 %collective-permute-start.19 = (bf16[1536,128]{1,0:T(8,128)(2,1)S(1)}, bf16[1536,128]{1,0:T(8,128)(2,1)S(1)}, u32[]{:S(2)}, u32[]{:S(2)}) collective-permute-start(bf16[1536,128]{1,0:T(8,128)(2,1)S(1)} %broadcast_select_fusion.8), channel_id=1, source_target_pairs={{0,4},{1,5},{2,6},{3,7},{4,0},{5,1},{6,2},{7,3},{8,12},{9,13},{10,... | collective-permute-start | bytes 1179656 | tf_op jit(solution)/shard_map/ppermute | solution.py:68
  100.9 7.4 %collective-permute-start.20 = (bf16[1024,512]{1,0:T(8,128)(2,1)S(1)}, bf16[1024,512]{1,0:T(8,128)(2,1)S(1)}, u32[]{:S(2)}, u32[]{:S(2)}) collective-permute-start(bf16[1024,512]{1,0:T(8,128)(2,1)S(1)} %get-tuple-element.101), channel_id=1, source_target_pairs={{0,1},{1,0},{2,3},{3,2},{4,5},{5,4},{6,7},{7,6},{8,9},{9,8},{10,11... | collective-permute-start | bytes 3145736 | tf_op jit(solution)/shard_map/ppermute | solution.py:71
  101.4 5.6 %collective-permute-start.22 = (bf16[1024,256]{1,0:T(8,128)(2,1)S(1)}, bf16[1024,256]{1,0:T(8,128)(2,1)S(1)}, u32[]{:S(2)}, u32[]{:S(2)}) collective-permute-start(bf16[1024,256]{1,0:T(8,128)(2,1)S(1)} %get-tuple-element.109), channel_id=1, source_target_pairs={{0,1},{1,0},{2,3},{3,2},{4,5},{5,4},{6,7},{7,6},{8,9},{9,8},{10,11... | collective-permute-start | bytes 1572872 | tf_op jit(solution)/shard_map/ppermute | solution.py:71
  102.0 15.7 %collective-permute-start.24 = (f32[1024,128]{1,0:T(8,128)S(1)}, f32[1024,128]{1,0:T(8,128)S(1)}, u32[]{:S(2)}, u32[]{:S(2)}) collective-permute-start(f32[1024,128]{1,0:T(8,128)S(1)} %convolution_add_fusion.2), channel_id=1, source_target_pairs={{0,2},{1,3},{2,0},{3,1},{4,6},{5,7},{6,4},{7,5},{8,10},{9,11},{10,... | collective-permute-start | bytes 1572872 | tf_op jit(solution)/shard_map/ppermute | solution.py:65
  111.0 2.0 %collective-permute-start.25 = (bf16[1024,256]{1,0:T(8,128)(2,1)S(1)}, bf16[1024,256]{1,0:T(8,128)(2,1)S(1)}, u32[]{:S(2)}, u32[]{:S(2)}) collective-permute-start(bf16[1024,256]{1,0:T(8,128)(2,1)S(1)} %get-tuple-element.107), channel_id=1, source_target_pairs={{0,1},{1,0},{2,3},{3,2},{4,5},{5,4},{6,7},{7,6},{8,9},{9,8},{10,11... | collective-permute-start | bytes 1572872 | tf_op jit(solution)/shard_map/ppermute | solution.py:71

commit v19 on v18

--- a/solution.py
+++ b/solution.py
@@ -92,9 +92,13 @@
 
         e = [columns(expected_cot, i, i + 1) for i in range(4)]
         v = [columns(value_next, i, i + 1) for i in range(4)]
+        rows = e[3].shape[0] // 2
+        early_rows = after(e[3][:rows])
+        j0 = home_jump(early_rows)
+        value_next, expected_cot = together((value_next, expected_cot), early_rows)
+        e = [columns(expected_cot, i, i + 1) for i in range(4)]
+        v = [columns(value_next, i, i + 1) for i in range(4)]
         x1 = cross(jnp.where(home, v[0], e[0]))
-        rows = e[3].shape[0] // 2
-        j0 = home_jump(e[3][:rows])
         t_other = swap(transition)
         e2 = after(e[2], x1)
         j1 = jump(jnp.where(home, x1, e2))

time: 120 us -> 122 us (1.017)
  waiting for transfers between devices: 52.8 us -> 57.9 us
  starting transfers between devices: 38.9 us -> 35.3 us
  local copies, waits for them, and re-layouts: 0.81 us -> 2.5 us
    ppermute x8, waiting for transfers between devices: 16.3 us -> 23.1 us  [cross(): return lax.ppermute(a, AXES, cross_pairs)]
    ppermute x8, starting transfers between devices: 15.8 us -> 11.7 us  [cross(): return lax.ppermute(a, AXES, cross_pairs)]
    ppermute x6, starting transfers between devices: 7.21 us -> 5.34 us  [step(): return lax.ppermute(a, AXES, step_pairs)]
    slice x1 -> x2, local copies, waits for them, and re-layouts: 0.03 us -> 1.71 us  [the longest x1 1.67 us: shards(): early_rows = after(e[3][:rows])]
    ppermute x4, starting transfers between devices: 6.45 us -> 7.74 us  [jump(): return lax.ppermute(a, AXES, jump_pairs)]
  transfers between devices with their start and end apart: 26 -> 26, of which waited for: 12 -> 12; matrix products, arithmetic and copies ran while one was open for 20% -> 21% of each run, Pallas kernels for 0% -> 0%
where the time goes in v19:
time: 122 us
  waiting for transfers between devices  57.9 us (47%)
  starting transfers between devices  35.3 us (29%)
  matrix products  16 us (13%)
  other arithmetic  8.58 us (7%)
  local copies, waits for them, and re-layouts  2.5 us (2%)
  between operations  1.87 us (2%)
    ppermute x6, waiting for transfers between devices, step(): return lax.ppermute(a, AXES, step_pairs)  31.6 us
    ppermute x8, waiting for transfers between devices, cross(): return lax.ppermute(a, AXES, cross_pairs)  23.1 us
    ppermute x8, starting transfers between devices, cross(): return lax.ppermute(a, AXES, cross_pairs)  11.7 us
    dot_general x12, matrix products, tdot(): lax.dot_general(a, b, (((0,), (0,)), ((), ())), preferred_element_type=jn...  9.04 us
    ppermute x2, starting transfers between devices, home_jump(): return lax.ppermute(a, AXES, home_jump_pairs)  8.71 us
    ppermute x4, starting transfers between devices, jump(): return lax.ppermute(a, AXES, jump_pairs)  7.74 us
    dot_general x3, matrix products, dott(): lax.dot_general(a, b, (((1,), (1,)), ((), ())), preferred_element_type=jn...  6.99 us
    ppermute x6, starting transfers between devices, step(): return lax.ppermute(a, AXES, step_pairs)  5.34 us
  transfers between devices with their start and end apart: 26, of which 12 were waited for; matrix products, arithmetic and copies ran while one was open for 21% of the time, Pallas kernels for 0%

profile of v19, /device:TPU:0, one launch (start us, length us, event | category | flops | bytes accessed | tf_op | source)
XLA Modules:
  0.0 122.1 jit_solution(11686191367473293760)
XLA Ops:
  0.6 0.5 collective-permute-start
  1.2 1.7 %slice.105 = bf16[512,128]{1,0:T(8,128)(2,1)} slice(bf16[1024,512]{1,0:T(8,128)(2,1)} %param.4), slice={[0:512], [384:512]} | slice | bytes 262144 | tf_op jit(solution)/shard_map/slice | solution.py:96
  2.8 5.5 %collective-permute-start.3 = (bf16[512,128]{1,0:T(8,128)(2,1)}, bf16[512,128]{1,0:T(8,128)(2,1)S(1)}, u32[]{:S(2)}, u32[]{:S(2)}) collective-permute-start(bf16[512,128]{1,0:T(8,128)(2,1)} %slice.105), channel_id=1, source_target_pairs={{0,8},{1,9},{4,12},{5,13},{10,2},{11,3},{14,6},{15,7},{16,24},{17,... | collective-permute-start | bytes 393224 | tf_op jit(solution)/shard_map/ppermute | solution.py:74
  8.4 2.5 %fusion.37 = (bf16[1024,128]{1,0:T(8,128)(2,1)S(1)}, bf16[1024,128]{1,0:T(8,128)(2,1)}, bf16[1024,128]{1,0:T(8,128)(2,1)S(1)}, bf16[1024,128]{1,0:T(8,128)(2,1)}...) fusion(bf16[1024,512]{1,0:T(8,128)(2,1)} %param.4, ...), kind=kLoop, calls=%fused_computation.82 | loop fusion | flops 131072 | bytes 3932161 | tf_op jit(solution)/shard_map/slice | solution.py:88
  11.0 2.0 %broadcast_select_fusion.1 = (bf16[1024,1024]{1,0:T(8,128)(2,1)S(1)}, bf16[1024,1024]{1,0:T(8,128)(2,1)S(1)}) fusion(bf16[1024,1024]{1,0:T(8,128)(2,1)S(1)} %copy-done.2, bf16[1024,1024]{1,0:T(8,128)(2,1)} %collective-permute-done, pred[]{:T(512)S(6)} %eq.8), kind=kLoop, calls=%fused_computation.8 | loop fusion | flops 2097152 | bytes 8388609 | tf_op jit(solution)/shard_map/jit(_where)/select_n | solution.py:105
  12.9 6.5 %collective-permute-done.1 = bf16[1024,128]{1,0:T(8,128)(2,1)S(1)} collective-permute-done((bf16[1024,128]{1,0:T(8,128)(2,1)}, bf16[1024,128]{1,0:T(8,128)(2,1)S(1)}, u32[]{:S(2)}, u32[]{:S(2)}) %collective-permute-start.1) | collective-permute-done | bytes 262176 | tf_op jit(solution)/shard_map/ppermute | solution.py:65
  19.5 0.3 collective-permute-start.4
  20.0 1.6 %collective-permute-start.2 = (bf16[1024,128]{1,0:T(8,128)(2,1)S(1)}, bf16[1024,128]{1,0:T(8,128)(2,1)S(1)}, u32[]{:S(2)}, u32[]{:S(2)}) collective-permute-start(bf16[1024,128]{1,0:T(8,128)(2,1)S(1)} %broadcast_select_fusion.18), channel_id=1, source_target_pairs={{0,8},{1,9},{2,10},{3,11},{4,12},{5,13},{6,14},{7,15},{8,0},{9,1},... | collective-permute-start | bytes 786440 | tf_op jit(solution)/shard_map/ppermute | solution.py:77
  21.6 1.6 %collective-permute-start.5 = (bf16[512,128]{1,0:T(8,128)(2,1)S(1)}, bf16[512,128]{1,0:T(8,128)(2,1)S(1)}, u32[]{:S(2)}, u32[]{:S(2)}) collective-permute-start(bf16[512,128]{1,0:T(8,128)(2,1)S(1)} %broadcast_select_fusion.20), channel_id=1, source_target_pairs={{0,4},{1,5},{2,6},{3,7},{4,0},{5,1},{6,2},{7,3},{8,12},{9,13},{10,... | collective-permute-start | bytes 393224 | tf_op jit(solution)/shard_map/ppermute | solution.py:68
  23.2 9.4 %collective-permute-done.4 = bf16[1024,256]{1,0:T(8,128)(2,1)S(1)} collective-permute-done((bf16[1024,256]{1,0:T(8,128)(2,1)S(1)}, bf16[1024,256]{1,0:T(8,128)(2,1)S(1)}, u32[]{:S(2)}, u32[]{:S(2)}) %collective-permute-start.4) | collective-permute-done | bytes 524320 | tf_op jit(solution)/shard_map/ppermute | solution.py:65
  32.7 1.3 %collective-permute-done.2 = bf16[1024,128]{1,0:T(8,128)(2,1)S(1)} collective-permute-done((bf16[1024,128]{1,0:T(8,128)(2,1)S(1)}, bf16[1024,128]{1,0:T(8,128)(2,1)S(1)}, u32[]{:S(2)}, u32[]{:S(2)}) %collective-permute-start.2) | collective-permute-done | bytes 262176 | tf_op jit(solution)/shard_map/ppermute | solution.py:77
  34.1 0.3 collective-permute-start.6
  34.4 2.4 %collective-permute-start.7 = (bf16[1024,128]{1,0:T(8,128)(2,1)S(1)}, bf16[1024,128]{1,0:T(8,128)(2,1)S(1)}, u32[]{:S(2)}, u32[]{:S(2)}) collective-permute-start(bf16[1024,128]{1,0:T(8,128)(2,1)S(1)} %get-tuple-element.136), channel_id=1, source_target_pairs={{0,8},{1,9},{2,10},{3,11},{4,12},{5,13},{6,14},{7,15},{8,0},{9,1},... | collective-permute-start | bytes 786440 | tf_op jit(solution)/shard_map/ppermute | solution.py:77
  36.9 0.7 collective-permute-start.8
  37.6 9.1 %collective-permute-done.6 = bf16[1024,128]{1,0:T(8,128)(2,1)S(1)} collective-permute-done((bf16[1024,128]{1,0:T(8,128)(2,1)S(1)}, bf16[1024,128]{1,0:T(8,128)(2,1)S(1)}, u32[]{:S(2)}, u32[]{:S(2)}) %collective-permute-start.6) | collective-permute-done | bytes 262176 | tf_op jit(solution)/shard_map/ppermute | solution.py:68
  46.7 0.7 fusion.44
  47.4 0.8 convolution_add_fusion.5
  48.2 2.1 %collective-permute-done.8 = bf16[1024,256]{1,0:T(8,128)(2,1)S(1)} collective-permute-done((bf16[1024,256]{1,0:T(8,128)(2,1)S(1)}, bf16[1024,256]{1,0:T(8,128)(2,1)S(1)}, u32[]{:S(2)}, u32[]{:S(2)}) %collective-permute-start.8) | collective-permute-done | bytes 524320 | tf_op jit(solution)/shard_map/ppermute | solution.py:65
  50.4 0.7 collective-permute-start.11
  51.1 0.4 collective-permute-start.9
  51.6 1.8 %collective-permute-start.10 = (bf16[1024,128]{1,0:T(8,128)(2,1)S(1)}, bf16[1024,128]{1,0:T(8,128)(2,1)S(1)}, u32[]{:S(2)}, u32[]{:S(2)}) collective-permute-start(bf16[1024,128]{1,0:T(8,128)(2,1)S(1)} %get-tuple-element.133), channel_id=1, source_target_pairs={{0,8},{1,9},{2,10},{3,11},{4,12},{5,13},{6,14},{7,15},{8,0},{9,1},... | collective-permute-start | bytes 786440 | tf_op jit(solution)/shard_map/ppermute | solution.py:77
  53.4 3.8 %collective-permute-done.11 = bf16[1024,128]{1,0:T(8,128)(2,1)S(1)} collective-permute-done((bf16[1024,128]{1,0:T(8,128)(2,1)S(1)}, bf16[1024,128]{1,0:T(8,128)(2,1)S(1)}, u32[]{:S(2)}, u32[]{:S(2)}) %collective-permute-start.11) | collective-permute-done | bytes 262176 | tf_op jit(solution)/shard_map/ppermute | solution.py:65
  57.2 0.6 collective-permute-start.14
  57.8 3.7 %collective-permute-done.9 = bf16[1024,128]{1,0:T(8,128)(2,1)S(1)} collective-permute-done((bf16[1024,128]{1,0:T(8,128)(2,1)S(1)}, bf16[1024,128]{1,0:T(8,128)(2,1)S(1)}, u32[]{:S(2)}, u32[]{:S(2)}) %collective-permute-start.9) | collective-permute-done | bytes 262176 | tf_op jit(solution)/shard_map/ppermute | solution.py:68
  61.5 0.7 fusion.45
  62.3 0.8 convolution_add_fusion.4
  63.1 1.5 %collective-permute-done.10 = bf16[1024,128]{1,0:T(8,128)(2,1)S(1)} collective-permute-done((bf16[1024,128]{1,0:T(8,128)(2,1)S(1)}, bf16[1024,128]{1,0:T(8,128)(2,1)S(1)}, u32[]{:S(2)}, u32[]{:S(2)}) %collective-permute-start.10) | collective-permute-done | bytes 262176 | tf_op jit(solution)/shard_map/ppermute | solution.py:77
  64.6 0.2 maximum_select_fusion
  64.8 0.1 collective-permute-start.12
  65.6 1.9 %collective-permute-start.13 = (bf16[1024,128]{1,0:T(8,128)(2,1)S(1)}, bf16[1024,128]{1,0:T(8,128)(2,1)S(1)}, u32[]{:S(2)}, u32[]{:S(2)}) collective-permute-start(bf16[1024,128]{1,0:T(8,128)(2,1)S(1)} %broadcast_select_fusion.11), channel_id=1, source_target_pairs={{0,8},{1,9},{2,10},{3,11},{4,12},{5,13},{6,14},{7,15},{8,0},{9,1},... | collective-permute-start | bytes 786440 | tf_op jit(solution)/shard_map/ppermute | solution.py:77
  67.5 3.2 %collective-permute-start.18 = (bf16[1536,128]{1,0:T(8,128)(2,1)S(1)}, bf16[1536,128]{1,0:T(8,128)(2,1)S(1)}, u32[]{:S(2)}, u32[]{:S(2)}) collective-permute-start(bf16[1536,128]{1,0:T(8,128)(2,1)S(1)} %pad_maximum_fusion.7), channel_id=1, source_target_pairs={{0,8},{1,9},{4,12},{5,13},{10,2},{11,3},{14,6},{15,7},{16,24},{17,... | collective-permute-start | bytes 1179656 | tf_op jit(solution)/shard_map/ppermute | solution.py:74
  70.7 0.1 constant_dynamic-update-slice_fusion.4
  70.8 0.1 constant_dynamic-update-slice_fusion.3
  71.0 10.4 %collective-permute-done.12 = bf16[1024,256]{1,0:T(8,128)(2,1)S(1)} collective-permute-done((bf16[1024,256]{1,0:T(8,128)(2,1)S(1)}, bf16[1024,256]{1,0:T(8,128)(2,1)S(1)}, u32[]{:S(2)}, u32[]{:S(2)}) %collective-permute-start.12) | collective-permute-done | bytes 524320 | tf_op jit(solution)/shard_map/ppermute | solution.py:68
  81.4 0.8 fusion.21
  82.2 0.8 convolution_add_fusion.3
  82.9 0.2 maximum_select_fusion.1
  83.1 0.3 collective-permute-start.15
  83.4 0.1 pad_maximum_fusion.2
  83.6 0.5 collective-permute-start.23
  84.1 0.1 constant_dynamic-update-slice_fusion.2
  84.2 0.1 constant_dynamic-update-slice_fusion.1
  84.4 5.8 %collective-permute-start.17 = (f32[1024,128]{1,0:T(8,128)S(1)}, f32[1024,128]{1,0:T(8,128)S(1)}, u32[]{:S(2)}, u32[]{:S(2)}) collective-permute-start(f32[1024,128]{1,0:T(8,128)S(1)} %convolution_add_fusion.3), channel_id=1, source_target_pairs={{0,2},{1,3},{2,0},{3,1},{4,6},{5,7},{6,4},{7,5},{8,10},{9,11},{10,... | collective-permute-start | bytes 1572872 | tf_op jit(solution)/shard_map/ppermute | solution.py:65
  90.2 8.3 %collective-permute-done.15 = bf16[1024,256]{1,0:T(8,128)(2,1)S(1)} collective-permute-done((bf16[1024,256]{1,0:T(8,128)(2,1)S(1)}, bf16[1024,256]{1,0:T(8,128)(2,1)S(1)}, u32[]{:S(2)}, u32[]{:S(2)}) %collective-permute-start.15) | collective-permute-done | bytes 524320 | tf_op jit(solution)/shard_map/ppermute | solution.py:68
  98.5 0.8 fusion.30
  99.3 0.8 convolution_add_fusion.2
  100.1 2.5 %collective-permute-start.19 = (bf16[1536,128]{1,0:T(8,128)(2,1)S(1)}, bf16[1536,128]{1,0:T(8,128)(2,1)S(1)}, u32[]{:S(2)}, u32[]{:S(2)}) collective-permute-start(bf16[1536,128]{1,0:T(8,128)(2,1)S(1)} %broadcast_select_fusion.8), channel_id=1, source_target_pairs={{0,4},{1,5},{2,6},{3,7},{4,0},{5,1},{6,2},{7,3},{8,12},{9,13},{10,... | collective-permute-start | bytes 1179656 | tf_op jit(solution)/shard_map/ppermute | solution.py:68
  102.8 0.2 fusion.38
  102.9 0.8 broadcast_select_fusion.3
  103.8 0.1 constant_dynamic-update-slice_fusion
  104.0 0.2 broadcast_select_fusion.7
  104.2 0.6 collective-permute-start.22
  104.8 3.6 %collective-permute-start.24 = (f32[1024,128]{1,0:T(8,128)S(1)}, f32[1024,128]{1,0:T(8,128)S(1)}, u32[]{:S(2)}, u32[]{:S(2)}) collective-permute-start(f32[1024,128]{1,0:T(8,128)S(1)} %convolution_add_fusion.2), channel_id=1, source_target_pairs={{0,2},{1,3},{2,0},{3,1},{4,6},{5,7},{6,4},{7,5},{8,10},{9,11},{10,... | collective-permute-start | bytes 1572872 | tf_op jit(solution)/shard_map/ppermute | solution.py:65
  108.3 0.7 fusion.24
  109.1 0.7 convolution_add_fusion.1
  109.8 1.3 %fusion.8 = f32[1024,1024]{1,0:T(8,128)S(1)} fusion(bf16[1024,256]{1,0:T(8,128)(2,1)S(1)} %collective-permute-done.22, bf16[1024,256]{1,0:T(8,128)(2,1)S(1)} %get-tuple-element.112, bf16[1024,256]{1,0:T(8,128)(2,1)S(1)} %get-tuple-element.109, bf16[1024,256]{1,0:T(8,128)(2,1)S(1)} %get-tuple-element.107), kind=kOutput, calls=%fused_computation.19 | convolution fusion | flops 1077936128 | bytes 6291456 | tf_op jit(solution)/shard_map/dot_general | solution.py:38
  111.1 2.4 %fusion.5 = f32[1024,1024]{1,0:T(8,128)S(1)} fusion(f32[1024,1024]{1,0:T(8,128)S(1)} %fusion.8, bf16[1024,1024]{1,0:T(8,128)(2,1)S(1)} %constant_dynamic-update-slice_fusion, bf16[1024,512]{1,0:T(8,128)(2,1)S(1)} %collective-permute-done.20, bf16[1024,512]{1,0:T(8,128)(2,1)S(1)} %get-tuple-element.104), kind=kOutput, calls=%fused_computation.9 | convolution fusion | flops 2152726528 | bytes 12582912 | tf_op jit(solution)/shard_map/dot_general | solution.py:38
  113.6 0.2 broadcast_select_fusion.5
  113.9 0.7 fusion.33
  114.7 0.8 convolution_add_fusion
  115.5 0.4 collective-permute-done.25
  115.8 3.3 %add_multiply_fusion = f32[1024,1024]{1,0:T(8,128)} fusion(f32[1024,1024]{1,0:T(8,128)S(1)} %fusion.5, f32[]{:T(128)} %bitcast, bf16[1024,256]{1,0:T(8,128)(2,1)S(1)} %collective-permute-done.25, bf16[1024,256]{1,0:T(8,128)(2,1)S(1)} %get-tuple-element.110, bf16[1024,256]{1,0:T(8,128)(2,1)S(1)} %get-tuple-element.108, bf16[1024,256]{1,0:T(8,128)(2,1)S(1)} %get-tuple-element.106), kind=kOutput, calls=%fused_computation | convolution fusion | flops 1080033280 | bytes 10485764 | tf_op jit(solution)/shard_map/dot_general | solution.py:38
  119.2 1.3 %collective-permute-done.24 = f32[1024,128]{1,0:T(8,128)S(1)} collective-permute-done((f32[1024,128]{1,0:T(8,128)S(1)}, f32[1024,128]{1,0:T(8,128)S(1)}, u32[]{:S(2)}, u32[]{:S(2)}) %collective-permute-start.24) | collective-permute-done | bytes 524320 | tf_op jit(solution)/shard_map/ppermute | solution.py:65
  120.5 1.6 %fusion.4 = f32[1024,512]{1,0:T(8,128)} fusion(f32[1024,256]{1,0:T(8,128)S(1)} %convolution_add_fusion, f32[1024,256]{1,0:T(8,128)S(1)} %convolution_add_fusion.1, f32[1024,128]{1,0:T(8,128)S(1)} %collective-permute-done.24, f32[1024,128]{1,0:T(8,128)S(1)} %collective-permute-done.17, f32[1024,128]{1,0:T(8,128)S(1)} %collective-permute-done.16, ...), kind=kLoop, calls=%fused_computation.6 | loop fusion | flops 3145728 | bytes 6291460 | tf_op jit(solution)/shard_map/mul | solution.py:195
  (54 shorter events, 1.2 us)
Async XLA Ops:
  0.6 10.3 %copy-start.2 = (bf16[1024,1024]{1,0:T(8,128)(2,1)S(1)}, bf16[1024,1024]{1,0:T(8,128)(2,1)}, u32[]{:S(2)}) copy-start(bf16[1024,1024]{1,0:T(8,128)(2,1)} %param.6) | copy-start | bytes 6291460
  0.6 10.3 %collective-permute-start = (bf16[1024,1024]{1,0:T(8,128)(2,1)}, bf16[1024,1024]{1,0:T(8,128)(2,1)}, u32[]{:S(2)}, u32[]{:S(2)}) collective-permute-start(bf16[1024,1024]{1,0:T(8,128)(2,1)} %param.6), channel_id=1, source_target_pairs={{0,1},{1,0},{2,3},{3,2},{4,5},{5,4},{6,7},{7,6},{8,9},{9,8},{10,11... | collective-permute-start | bytes 6291464 | tf_op jit(solution)/shard_map/ppermute | solution.py:71
  2.8 10.1 %collective-permute-start.3 = (bf16[512,128]{1,0:T(8,128)(2,1)}, bf16[512,128]{1,0:T(8,128)(2,1)S(1)}, u32[]{:S(2)}, u32[]{:S(2)}) collective-permute-start(bf16[512,128]{1,0:T(8,128)(2,1)} %slice.105), channel_id=1, source_target_pairs={{0,8},{1,9},{4,12},{5,13},{10,2},{11,3},{14,6},{15,7},{16,24},{17,... | collective-permute-start | bytes 393224 | tf_op jit(solution)/shard_map/ppermute | solution.py:74
  10.9 8.5 %collective-permute-start.1 = (bf16[1024,128]{1,0:T(8,128)(2,1)}, bf16[1024,128]{1,0:T(8,128)(2,1)S(1)}, u32[]{:S(2)}, u32[]{:S(2)}) collective-permute-start(bf16[1024,128]{1,0:T(8,128)(2,1)} %get-tuple-element.117), channel_id=1, source_target_pairs={{0,2},{1,3},{2,0},{3,1},{4,6},{5,7},{6,4},{7,5},{8,10},{9,11},{10,... | collective-permute-start | bytes 786440 | tf_op jit(solution)/shard_map/ppermute | solution.py:65
  10.9 8.5 %copy-start.5 = (bf16[1024,128]{1,0:T(8,128)(2,1)S(1)}, bf16[1024,128]{1,0:T(8,128)(2,1)}, u32[]{:S(2)}) copy-start(bf16[1024,128]{1,0:T(8,128)(2,1)} %get-tuple-element.119) | copy-start | bytes 786436
  10.9 8.9 %copy-start.1 = (bf16[1024,512]{1,0:T(8,128)(2,1)S(1)}, bf16[1024,512]{1,0:T(8,128)(2,1)}, u32[]{:S(2)}) copy-start(bf16[1024,512]{1,0:T(8,128)(2,1)} %param.4) | copy-start | bytes 3145732
  19.4 14.6 %copy-start.4 = (bf16[1024,128]{1,0:T(8,128)(2,1)S(1)}, bf16[1024,128]{1,0:T(8,128)(2,1)}, u32[]{:S(2)}) copy-start(bf16[1024,128]{1,0:T(8,128)(2,1)} %get-tuple-element.56) | copy-start | bytes 786436
  19.5 13.1 %collective-permute-start.4 = (bf16[1024,256]{1,0:T(8,128)(2,1)S(1)}, bf16[1024,256]{1,0:T(8,128)(2,1)S(1)}, u32[]{:S(2)}, u32[]{:S(2)}) collective-permute-start(bf16[1024,256]{1,0:T(8,128)(2,1)S(1)} %pad_maximum_fusion.3), channel_id=1, source_target_pairs={{0,2},{1,3},{2,0},{3,1},{4,6},{5,7},{6,4},{7,5},{8,10},{9,11},{10,... | collective-permute-start | bytes 1572872 | tf_op jit(solution)/shard_map/ppermute | solution.py:65
  19.9 16.9 %copy-start.3 = (bf16[1024,128]{1,0:T(8,128)(2,1)S(1)}, bf16[1024,128]{1,0:T(8,128)(2,1)}, u32[]{:S(2)}) copy-start(bf16[1024,128]{1,0:T(8,128)(2,1)} %get-tuple-element.121) | copy-start | bytes 786436
  20.0 14.1 %collective-permute-start.2 = (bf16[1024,128]{1,0:T(8,128)(2,1)S(1)}, bf16[1024,128]{1,0:T(8,128)(2,1)S(1)}, u32[]{:S(2)}, u32[]{:S(2)}) collective-permute-start(bf16[1024,128]{1,0:T(8,128)(2,1)S(1)} %broadcast_select_fusion.18), channel_id=1, source_target_pairs={{0,8},{1,9},{2,10},{3,11},{4,12},{5,13},{6,14},{7,15},{8,0},{9,1},... | collective-permute-start | bytes 786440 | tf_op jit(solution)/shard_map/ppermute | solution.py:77
  21.6 12.5 %collective-permute-start.5 = (bf16[512,128]{1,0:T(8,128)(2,1)S(1)}, bf16[512,128]{1,0:T(8,128)(2,1)S(1)}, u32[]{:S(2)}, u32[]{:S(2)}) collective-permute-start(bf16[512,128]{1,0:T(8,128)(2,1)S(1)} %broadcast_select_fusion.20), channel_id=1, source_target_pairs={{0,4},{1,5},{2,6},{3,7},{4,0},{5,1},{6,2},{7,3},{8,12},{9,13},{10,... | collective-permute-start | bytes 393224 | tf_op jit(solution)/shard_map/ppermute | solution.py:68
  34.1 12.6 %collective-permute-start.6 = (bf16[1024,128]{1,0:T(8,128)(2,1)S(1)}, bf16[1024,128]{1,0:T(8,128)(2,1)S(1)}, u32[]{:S(2)}, u32[]{:S(2)}) collective-permute-start(bf16[1024,128]{1,0:T(8,128)(2,1)S(1)} %broadcast_select_fusion.15), channel_id=1, source_target_pairs={{0,4},{1,5},{2,6},{3,7},{4,0},{5,1},{6,2},{7,3},{8,12},{9,13},{10,... | collective-permute-start | bytes 786440 | tf_op jit(solution)/shard_map/ppermute | solution.py:68
  34.4 15.9 %collective-permute-start.7 = (bf16[1024,128]{1,0:T(8,128)(2,1)S(1)}, bf16[1024,128]{1,0:T(8,128)(2,1)S(1)}, u32[]{:S(2)}, u32[]{:S(2)}) collective-permute-start(bf16[1024,128]{1,0:T(8,128)(2,1)S(1)} %get-tuple-element.136), channel_id=1, source_target_pairs={{0,8},{1,9},{2,10},{3,11},{4,12},{5,13},{6,14},{7,15},{8,0},{9,1},... | collective-permute-start | bytes 786440 | tf_op jit(solution)/shard_map/ppermute | solution.py:77
  36.9 13.4 %collective-permute-start.8 = (bf16[1024,256]{1,0:T(8,128)(2,1)S(1)}, bf16[1024,256]{1,0:T(8,128)(2,1)S(1)}, u32[]{:S(2)}, u32[]{:S(2)}) collective-permute-start(bf16[1024,256]{1,0:T(8,128)(2,1)S(1)} %pad_maximum_fusion.4), channel_id=1, source_target_pairs={{0,2},{1,3},{2,0},{3,1},{4,6},{5,7},{6,4},{7,5},{8,10},{9,11},{10,... | collective-permute-start | bytes 1572872 | tf_op jit(solution)/shard_map/ppermute | solution.py:65
  48.2 3.3 %copy-start = (bf16[1024,512]{1,0:T(8,128)(2,1)S(1)}, bf16[1024,512]{1,0:T(8,128)(2,1)}, u32[]{:S(2)}) copy-start(bf16[1024,512]{1,0:T(8,128)(2,1)} %param.5) | copy-start | bytes 3145732
  50.4 6.8 %collective-permute-start.11 = (bf16[1024,128]{1,0:T(8,128)(2,1)S(1)}, bf16[1024,128]{1,0:T(8,128)(2,1)S(1)}, u32[]{:S(2)}, u32[]{:S(2)}) collective-permute-start(bf16[1024,128]{1,0:T(8,128)(2,1)S(1)} %broadcast_select_fusion.12), channel_id=1, source_target_pairs={{0,2},{1,3},{2,0},{3,1},{4,6},{5,7},{6,4},{7,5},{8,10},{9,11},{10,... | collective-permute-start | bytes 786440 | tf_op jit(solution)/shard_map/ppermute | solution.py:65
  51.1 10.4 %collective-permute-start.9 = (bf16[1024,128]{1,0:T(8,128)(2,1)S(1)}, bf16[1024,128]{1,0:T(8,128)(2,1)S(1)}, u32[]{:S(2)}, u32[]{:S(2)}) collective-permute-start(bf16[1024,128]{1,0:T(8,128)(2,1)S(1)} %broadcast_select_fusion.13), channel_id=1, source_target_pairs={{0,4},{1,5},{2,6},{3,7},{4,0},{5,1},{6,2},{7,3},{8,12},{9,13},{10,... | collective-permute-start | bytes 786440 | tf_op jit(solution)/shard_map/ppermute | solution.py:68
  51.6 13.0 %collective-permute-start.10 = (bf16[1024,128]{1,0:T(8,128)(2,1)S(1)}, bf16[1024,128]{1,0:T(8,128)(2,1)S(1)}, u32[]{:S(2)}, u32[]{:S(2)}) collective-permute-start(bf16[1024,128]{1,0:T(8,128)(2,1)S(1)} %get-tuple-element.133), channel_id=1, source_target_pairs={{0,8},{1,9},{2,10},{3,11},{4,12},{5,13},{6,14},{7,15},{8,0},{9,1},... | collective-permute-start | bytes 786440 | tf_op jit(solution)/shard_map/ppermute | solution.py:77
  57.2 13.7 %collective-permute-start.14 = (f32[1024,128]{1,0:T(8,128)S(1)}, f32[1024,128]{1,0:T(8,128)S(1)}, u32[]{:S(2)}, u32[]{:S(2)}) collective-permute-start(f32[1024,128]{1,0:T(8,128)S(1)} %convolution_add_fusion.5), channel_id=1, source_target_pairs={{0,2},{1,3},{2,0},{3,1},{4,6},{5,7},{6,4},{7,5},{8,10},{9,11},{10,... | collective-permute-start | bytes 1572872 | tf_op jit(solution)/shard_map/ppermute | solution.py:65
  64.8 16.6 %collective-permute-start.12 = (bf16[1024,256]{1,0:T(8,128)(2,1)S(1)}, bf16[1024,256]{1,0:T(8,128)(2,1)S(1)}, u32[]{:S(2)}, u32[]{:S(2)}) collective-permute-start(bf16[1024,256]{1,0:T(8,128)(2,1)S(1)} %maximum_select_fusion), channel_id=1, source_target_pairs={{0,4},{1,5},{2,6},{3,7},{4,0},{5,1},{6,2},{7,3},{8,12},{9,13},{10,... | collective-permute-start | bytes 1572872 | tf_op jit(solution)/shard_map/ppermute | solution.py:68
  65.6 17.4 %collective-permute-start.13 = (bf16[1024,128]{1,0:T(8,128)(2,1)S(1)}, bf16[1024,128]{1,0:T(8,128)(2,1)S(1)}, u32[]{:S(2)}, u32[]{:S(2)}) collective-permute-start(bf16[1024,128]{1,0:T(8,128)(2,1)S(1)} %broadcast_select_fusion.11), channel_id=1, source_target_pairs={{0,8},{1,9},{2,10},{3,11},{4,12},{5,13},{6,14},{7,15},{8,0},{9,1},... | collective-permute-start | bytes 786440 | tf_op jit(solution)/shard_map/ppermute | solution.py:77
  67.5 31.7 %collective-permute-start.18 = (bf16[1536,128]{1,0:T(8,128)(2,1)S(1)}, bf16[1536,128]{1,0:T(8,128)(2,1)S(1)}, u32[]{:S(2)}, u32[]{:S(2)}) collective-permute-start(bf16[1536,128]{1,0:T(8,128)(2,1)S(1)} %pad_maximum_fusion.7), channel_id=1, source_target_pairs={{0,8},{1,9},{4,12},{5,13},{10,2},{11,3},{14,6},{15,7},{16,24},{17,... | collective-permute-start | bytes 1179656 | tf_op jit(solution)/shard_map/ppermute | solution.py:74
  70.9 13.4 %collective-permute-start.16 = (f32[1024,128]{1,0:T(8,128)S(1)}, f32[1024,128]{1,0:T(8,128)S(1)}, u32[]{:S(2)}, u32[]{:S(2)}) collective-permute-start(f32[1024,128]{1,0:T(8,128)S(1)} %convolution_add_fusion.4), channel_id=1, source_target_pairs={{0,2},{1,3},{2,0},{3,1},{4,6},{5,7},{6,4},{7,5},{8,10},{9,11},{10,... | collective-permute-start | bytes 1572872 | tf_op jit(solution)/shard_map/ppermute | solution.py:65
  83.1 15.3 %collective-permute-start.15 = (bf16[1024,256]{1,0:T(8,128)(2,1)S(1)}, bf16[1024,256]{1,0:T(8,128)(2,1)S(1)}, u32[]{:S(2)}, u32[]{:S(2)}) collective-permute-start(bf16[1024,256]{1,0:T(8,128)(2,1)S(1)} %maximum_select_fusion.1), channel_id=1, source_target_pairs={{0,4},{1,5},{2,6},{3,7},{4,0},{5,1},{6,2},{7,3},{8,12},{9,13},{10,... | collective-permute-start | bytes 1572872 | tf_op jit(solution)/shard_map/ppermute | solution.py:68
  83.5 20.2 %collective-permute-start.21 = (bf16[1024,512]{1,0:T(8,128)(2,1)S(1)}, bf16[1024,512]{1,0:T(8,128)(2,1)S(1)}, u32[]{:S(2)}, u32[]{:S(2)}) collective-permute-start(bf16[1024,512]{1,0:T(8,128)(2,1)S(1)} %pad_maximum_fusion.2), channel_id=1, source_target_pairs={{0,1},{1,0},{2,3},{3,2},{4,5},{5,4},{6,7},{7,6},{8,9},{9,8},{10,11... | collective-permute-start | bytes 3145736 | tf_op jit(solution)/shard_map/ppermute | solution.py:71
  83.6 19.0 %collective-permute-start.23 = (bf16[1024,512]{1,0:T(8,128)(2,1)S(1)}, bf16[1024,512]{1,0:T(8,128)(2,1)S(1)}, u32[]{:S(2)}, u32[]{:S(2)}) collective-permute-start(bf16[1024,512]{1,0:T(8,128)(2,1)S(1)} %copy-done), channel_id=1, source_target_pairs={{0,1},{1,0},{2,3},{3,2},{4,5},{5,4},{6,7},{7,6},{8,9},{9,8},{10,11... | collective-permute-start | bytes 3145736 | tf_op jit(solution)/shard_map/ppermute | solution.py:71
  84.4 18.4 %collective-permute-start.17 = (f32[1024,128]{1,0:T(8,128)S(1)}, f32[1024,128]{1,0:T(8,128)S(1)}, u32[]{:S(2)}, u32[]{:S(2)}) collective-permute-start(f32[1024,128]{1,0:T(8,128)S(1)} %convolution_add_fusion.3), channel_id=1, source_target_pairs={{0,2},{1,3},{2,0},{3,1},{4,6},{5,7},{6,4},{7,5},{8,10},{9,11},{10,... | collective-permute-start | bytes 1572872 | tf_op jit(solution)/shard_map/ppermute | solution.py:65
  100.1 13.5 %collective-permute-start.19 = (bf16[1536,128]{1,0:T(8,128)(2,1)S(1)}, bf16[1536,128]{1,0:T(8,128)(2,1)S(1)}, u32[]{:S(2)}, u32[]{:S(2)}) collective-permute-start(bf16[1536,128]{1,0:T(8,128)(2,1)S(1)} %broadcast_select_fusion.8), channel_id=1, source_target_pairs={{0,4},{1,5},{2,6},{3,7},{4,0},{5,1},{6,2},{7,3},{8,12},{9,13},{10,... | collective-permute-start | bytes 1179656 | tf_op jit(solution)/shard_map/ppermute | solution.py:68
  103.7 7.4 %collective-permute-start.20 = (bf16[1024,512]{1,0:T(8,128)(2,1)S(1)}, bf16[1024,512]{1,0:T(8,128)(2,1)S(1)}, u32[]{:S(2)}, u32[]{:S(2)}) collective-permute-start(bf16[1024,512]{1,0:T(8,128)(2,1)S(1)} %get-tuple-element.105), channel_id=1, source_target_pairs={{0,1},{1,0},{2,3},{3,2},{4,5},{5,4},{6,7},{7,6},{8,9},{9,8},{10,11... | collective-permute-start | bytes 3145736 | tf_op jit(solution)/shard_map/ppermute | solution.py:71
  104.2 5.6 %collective-permute-start.22 = (bf16[1024,256]{1,0:T(8,128)(2,1)S(1)}, bf16[1024,256]{1,0:T(8,128)(2,1)S(1)}, u32[]{:S(2)}, u32[]{:S(2)}) collective-permute-start(bf16[1024,256]{1,0:T(8,128)(2,1)S(1)} %get-tuple-element.113), channel_id=1, source_target_pairs={{0,1},{1,0},{2,3},{3,2},{4,5},{5,4},{6,7},{7,6},{8,9},{9,8},{10,11... | collective-permute-start | bytes 1572872 | tf_op jit(solution)/shard_map/ppermute | solution.py:71
  104.8 15.7 %collective-permute-start.24 = (f32[1024,128]{1,0:T(8,128)S(1)}, f32[1024,128]{1,0:T(8,128)S(1)}, u32[]{:S(2)}, u32[]{:S(2)}) collective-permute-start(f32[1024,128]{1,0:T(8,128)S(1)} %convolution_add_fusion.2), channel_id=1, source_target_pairs={{0,2},{1,3},{2,0},{3,1},{4,6},{5,7},{6,4},{7,5},{8,10},{9,11},{10,... | collective-permute-start | bytes 1572872 | tf_op jit(solution)/shard_map/ppermute | solution.py:65
  113.9 2.0 %collective-permute-start.25 = (bf16[1024,256]{1,0:T(8,128)(2,1)S(1)}, bf16[1024,256]{1,0:T(8,128)(2,1)S(1)}, u32[]{:S(2)}, u32[]{:S(2)}) collective-permute-start(bf16[1024,256]{1,0:T(8,128)(2,1)S(1)} %get-tuple-element.111), channel_id=1, source_target_pairs={{0,1},{1,0},{2,3},{3,2},{4,5},{5,4},{6,7},{7,6},{8,9},{9,8},{10,11... | collective-permute-start | bytes 1572872 | tf_op jit(solution)/shard_map/ppermute | solution.py:71

commit v20 on v18

--- a/solution.py
+++ b/solution.py
@@ -93,7 +93,8 @@
         e = [columns(expected_cot, i, i + 1) for i in range(4)]
         v = [columns(value_next, i, i + 1) for i in range(4)]
         x1 = cross(jnp.where(home, v[0], e[0]))
-        rows = e[3].shape[0] // 2
+        height = e[3].shape[0]
+        rows = height // 4
         j0 = home_jump(e[3][:rows])
         t_other = swap(transition)
         e2 = after(e[2], x1)
@@ -178,7 +179,7 @@
         near, far, near_top, far_top = together((a_rest, a_rest_next, a3_top, a3_top_next), grad, own01)
 
         def two_quarters(rest, top):
-            return jnp.concatenate([rest[: 2 * rows], jnp.concatenate([top, rest[2 * rows :]], 0)], 1)
+            return jnp.concatenate([rest[:height], jnp.concatenate([top, rest[height:]], 0)], 1)
 
         near, far = two_quarters(near, near_top), two_quarters(far, far_top)
         a23_own, a23_swapped = own_and_swapped(near, far)

time: 120 us -> 121 us (level)
  waiting for transfers between devices: 52.8 us -> 54.3 us
    ppermute x4, starting transfers between devices: 6.45 us -> 9.24 us  [jump(): return lax.ppermute(a, AXES, jump_pairs)]
    ppermute x6, starting transfers between devices: 7.21 us -> 5.43 us  [step(): return lax.ppermute(a, AXES, step_pairs)]
    ppermute x6, waiting for transfers between devices: 31.7 us -> 33.4 us  [step(): return lax.ppermute(a, AXES, step_pairs)]
  transfers between devices with their start and end apart: 26 -> 26, of which waited for: 12 -> 11; matrix products, arithmetic and copies ran while one was open for 20% -> 19% of each run, Pallas kernels for 0% -> 0%
where the time goes in v20:
time: 121 us; the launch traced here: 120 us
  waiting for transfers between devices  54.3 us (45%)
  starting transfers between devices  39.2 us (32%)
  matrix products  16 us (13%)
  other arithmetic  8.21 us (7%)
  between operations  1.85 us (2%)
    ppermute x6, waiting for transfers between devices, step(): return lax.ppermute(a, AXES, step_pairs)  33.4 us
    ppermute x8, waiting for transfers between devices, cross(): return lax.ppermute(a, AXES, cross_pairs)  17.4 us
    ppermute x8, starting transfers between devices, cross(): return lax.ppermute(a, AXES, cross_pairs)  15.3 us
    ppermute x4, starting transfers between devices, jump(): return lax.ppermute(a, AXES, jump_pairs)  9.24 us
    dot_general x12, matrix products, tdot(): lax.dot_general(a, b, (((0,), (0,)), ((), ())), preferred_element_type=jn...  9.05 us
    ppermute x2, starting transfers between devices, home_jump(): return lax.ppermute(a, AXES, home_jump_pairs)  7.51 us
    dot_general x3, matrix products, dott(): lax.dot_general(a, b, (((1,), (1,)), ((), ())), preferred_element_type=jn...  6.96 us
    ppermute x6, starting transfers between devices, step(): return lax.ppermute(a, AXES, step_pairs)  5.43 us
  transfers between devices with their start and end apart: 26, of which 11 were waited for; matrix products, arithmetic and copies ran while one was open for 19% of the time, Pallas kernels for 0%

profile of v20, /device:TPU:0, one launch (start us, length us, event | category | flops | bytes accessed | tf_op | source)
XLA Modules:
  0.0 120.4 jit_solution(7733265840054780012)
XLA Ops:
  0.6 0.5 collective-permute-start
  1.2 1.6 %fusion.36 = (bf16[1024,128]{1,0:T(8,128)(2,1)S(1)}, bf16[1024,128]{1,0:T(8,128)(2,1)S(1)}, bf16[1024,128]{1,0:T(8,128)(2,1)S(1)}, bf16[1024,128]{1,0:T(8,128)(2...) fusion(bf16[1024,512]{1,0:T(8,128)(2,1)} %param.4, ...), kind=kLoop, calls=%fused_computation.81 | loop fusion | flops 131072 | bytes 3932161 | tf_op jit(solution)/shard_map/slice | solution.py:88
  2.8 2.7 %collective-permute-start.1 = (bf16[1024,128]{1,0:T(8,128)(2,1)S(1)}, bf16[1024,128]{1,0:T(8,128)(2,1)S(1)}, u32[]{:S(2)}, u32[]{:S(2)}) collective-permute-start(bf16[1024,128]{1,0:T(8,128)(2,1)S(1)} %get-tuple-element.111), channel_id=1, source_target_pairs={{0,2},{1,3},{2,0},{3,1},{4,6},{5,7},{6,4},{7,5},{8,10},{9,11},{10,... | collective-permute-start | bytes 786440 | tf_op jit(solution)/shard_map/ppermute | solution.py:65
  5.5 4.5 %collective-permute-start.3 = (bf16[256,128]{1,0:T(8,128)(2,1)S(1)}, bf16[256,128]{1,0:T(8,128)(2,1)S(1)}, u32[]{:S(2)}, u32[]{:S(2)}) collective-permute-start(bf16[256,128]{1,0:T(8,128)(2,1)S(1)} %slice.106), channel_id=1, source_target_pairs={{0,8},{1,9},{4,12},{5,13},{10,2},{11,3},{14,6},{15,7},{16,24},{17,... | collective-permute-start | bytes 196616 | tf_op jit(solution)/shard_map/ppermute | solution.py:74
  10.0 2.5 %broadcast_select_fusion.1 = (bf16[1024,1024]{1,0:T(8,128)(2,1)S(1)}, bf16[1024,1024]{1,0:T(8,128)(2,1)S(1)}) fusion(bf16[1024,1024]{1,0:T(8,128)(2,1)} %param.6, bf16[1024,1024]{1,0:T(8,128)(2,1)} %collective-permute-done, pred[]{:T(512)S(6)} %eq.8), kind=kLoop, calls=%fused_computation.8 | loop fusion | flops 2097152 | bytes 8388609 | tf_op jit(solution)/shard_map/jit(_where)/select_n | solution.py:102
  12.6 1.7 %collective-permute-start.4 = (bf16[1024,256]{1,0:T(8,128)(2,1)S(1)}, bf16[1024,256]{1,0:T(8,128)(2,1)S(1)}, u32[]{:S(2)}, u32[]{:S(2)}) collective-permute-start(bf16[1024,256]{1,0:T(8,128)(2,1)S(1)} %pad_maximum_fusion.3), channel_id=1, source_target_pairs={{0,2},{1,3},{2,0},{3,1},{4,6},{5,7},{6,4},{7,5},{8,10},{9,11},{10,... | collective-permute-start | bytes 1572872 | tf_op jit(solution)/shard_map/ppermute | solution.py:65
  14.3 2.6 %collective-permute-start.2 = (bf16[1024,128]{1,0:T(8,128)(2,1)S(1)}, bf16[1024,128]{1,0:T(8,128)(2,1)S(1)}, u32[]{:S(2)}, u32[]{:S(2)}) collective-permute-start(bf16[1024,128]{1,0:T(8,128)(2,1)S(1)} %broadcast_select_fusion.18), channel_id=1, source_target_pairs={{0,8},{1,9},{2,10},{3,11},{4,12},{5,13},{6,14},{7,15},{8,0},{9,1},... | collective-permute-start | bytes 786440 | tf_op jit(solution)/shard_map/ppermute | solution.py:77
  16.9 1.6 %collective-permute-start.5 = (bf16[256,128]{1,0:T(8,128)(2,1)S(1)}, bf16[256,128]{1,0:T(8,128)(2,1)S(1)}, u32[]{:S(2)}, u32[]{:S(2)}) collective-permute-start(bf16[256,128]{1,0:T(8,128)(2,1)S(1)} %broadcast_select_fusion.20), channel_id=1, source_target_pairs={{0,4},{1,5},{2,6},{3,7},{4,0},{5,1},{6,2},{7,3},{8,12},{9,13},{10,... | collective-permute-start | bytes 196616 | tf_op jit(solution)/shard_map/ppermute | solution.py:68
  18.6 7.8 %collective-permute-done.4 = bf16[1024,256]{1,0:T(8,128)(2,1)S(1)} collective-permute-done((bf16[1024,256]{1,0:T(8,128)(2,1)S(1)}, bf16[1024,256]{1,0:T(8,128)(2,1)S(1)}, u32[]{:S(2)}, u32[]{:S(2)}) %collective-permute-start.4) | collective-permute-done | bytes 524320 | tf_op jit(solution)/shard_map/ppermute | solution.py:65
  26.4 2.0 %collective-permute-done.2 = bf16[1024,128]{1,0:T(8,128)(2,1)S(1)} collective-permute-done((bf16[1024,128]{1,0:T(8,128)(2,1)S(1)}, bf16[1024,128]{1,0:T(8,128)(2,1)S(1)}, u32[]{:S(2)}, u32[]{:S(2)}) %collective-permute-start.2) | collective-permute-done | bytes 262176 | tf_op jit(solution)/shard_map/ppermute | solution.py:77
  28.5 0.7 collective-permute-start.6
  29.3 3.4 %collective-permute-start.7 = (bf16[1024,128]{1,0:T(8,128)(2,1)S(1)}, bf16[1024,128]{1,0:T(8,128)(2,1)S(1)}, u32[]{:S(2)}, u32[]{:S(2)}) collective-permute-start(bf16[1024,128]{1,0:T(8,128)(2,1)S(1)} %get-tuple-element.130), channel_id=1, source_target_pairs={{0,8},{1,9},{2,10},{3,11},{4,12},{5,13},{6,14},{7,15},{8,0},{9,1},... | collective-permute-start | bytes 786440 | tf_op jit(solution)/shard_map/ppermute | solution.py:77
  32.8 0.6 collective-permute-start.8
  33.4 7.6 %collective-permute-done.6 = bf16[1024,128]{1,0:T(8,128)(2,1)S(1)} collective-permute-done((bf16[1024,128]{1,0:T(8,128)(2,1)S(1)}, bf16[1024,128]{1,0:T(8,128)(2,1)S(1)}, u32[]{:S(2)}, u32[]{:S(2)}) %collective-permute-start.6) | collective-permute-done | bytes 262176 | tf_op jit(solution)/shard_map/ppermute | solution.py:68
  41.0 0.7 fusion.43
  41.8 0.8 convolution_add_fusion.5
  42.5 3.6 %collective-permute-done.8 = bf16[1024,256]{1,0:T(8,128)(2,1)S(1)} collective-permute-done((bf16[1024,256]{1,0:T(8,128)(2,1)S(1)}, bf16[1024,256]{1,0:T(8,128)(2,1)S(1)}, u32[]{:S(2)}, u32[]{:S(2)}) %collective-permute-start.8) | collective-permute-done | bytes 524320 | tf_op jit(solution)/shard_map/ppermute | solution.py:65
  46.2 0.6 collective-permute-start.11
  46.9 0.4 collective-permute-start.9
  47.3 1.1 collective-permute-start.10
  48.4 4.7 %collective-permute-done.11 = bf16[1024,128]{1,0:T(8,128)(2,1)S(1)} collective-permute-done((bf16[1024,128]{1,0:T(8,128)(2,1)S(1)}, bf16[1024,128]{1,0:T(8,128)(2,1)S(1)}, u32[]{:S(2)}, u32[]{:S(2)}) %collective-permute-start.11) | collective-permute-done | bytes 262176 | tf_op jit(solution)/shard_map/ppermute | solution.py:65
  53.0 0.5 collective-permute-start.14
  53.6 4.2 %collective-permute-done.9 = bf16[1024,128]{1,0:T(8,128)(2,1)S(1)} collective-permute-done((bf16[1024,128]{1,0:T(8,128)(2,1)S(1)}, bf16[1024,128]{1,0:T(8,128)(2,1)S(1)}, u32[]{:S(2)}, u32[]{:S(2)}) %collective-permute-start.9) | collective-permute-done | bytes 262176 | tf_op jit(solution)/shard_map/ppermute | solution.py:68
  57.8 0.7 fusion.44
  58.5 0.8 convolution_add_fusion.4
  59.3 1.1 collective-permute-done.10
  60.4 0.2 maximum_select_fusion
  60.6 0.1 collective-permute-start.12
  61.4 2.1 %collective-permute-start.13 = (bf16[1024,128]{1,0:T(8,128)(2,1)S(1)}, bf16[1024,128]{1,0:T(8,128)(2,1)S(1)}, u32[]{:S(2)}, u32[]{:S(2)}) collective-permute-start(bf16[1024,128]{1,0:T(8,128)(2,1)S(1)} %broadcast_select_fusion.11), channel_id=1, source_target_pairs={{0,8},{1,9},{2,10},{3,11},{4,12},{5,13},{6,14},{7,15},{8,0},{9,1},... | collective-permute-start | bytes 786440 | tf_op jit(solution)/shard_map/ppermute | solution.py:77
  63.5 3.0 %collective-permute-start.18 = (bf16[1792,128]{1,0:T(8,128)(2,1)S(1)}, bf16[1792,128]{1,0:T(8,128)(2,1)S(1)}, u32[]{:S(2)}, u32[]{:S(2)}) collective-permute-start(bf16[1792,128]{1,0:T(8,128)(2,1)S(1)} %pad_maximum_fusion.7), channel_id=1, source_target_pairs={{0,8},{1,9},{4,12},{5,13},{10,2},{11,3},{14,6},{15,7},{16,24},{17,... | collective-permute-start | bytes 1376264 | tf_op jit(solution)/shard_map/ppermute | solution.py:74
  66.5 0.1 constant_dynamic-update-slice_fusion.4
  66.6 0.1 constant_dynamic-update-slice_fusion.3
  66.8 0.1 collective-permute-start.16
  66.8 10.8 %collective-permute-done.12 = bf16[1024,256]{1,0:T(8,128)(2,1)S(1)} collective-permute-done((bf16[1024,256]{1,0:T(8,128)(2,1)S(1)}, bf16[1024,256]{1,0:T(8,128)(2,1)S(1)}, u32[]{:S(2)}, u32[]{:S(2)}) %collective-permute-start.12) | collective-permute-done | bytes 524320 | tf_op jit(solution)/shard_map/ppermute | solution.py:68
  77.6 0.8 fusion.21
  78.3 0.8 convolution_add_fusion.3
  79.1 0.2 maximum_select_fusion.1
  79.4 0.1 pad_maximum_fusion.2
  79.6 0.5 collective-permute-start.23
  80.1 0.1 constant_dynamic-update-slice_fusion.2
  80.2 0.1 constant_dynamic-update-slice_fusion.1
  80.3 5.3 %collective-permute-start.17 = (f32[1024,128]{1,0:T(8,128)S(1)}, f32[1024,128]{1,0:T(8,128)S(1)}, u32[]{:S(2)}, u32[]{:S(2)}) collective-permute-start(f32[1024,128]{1,0:T(8,128)S(1)} %convolution_add_fusion.3), channel_id=1, source_target_pairs={{0,2},{1,3},{2,0},{3,1},{4,6},{5,7},{6,4},{7,5},{8,10},{9,11},{10,... | collective-permute-start | bytes 1572872 | tf_op jit(solution)/shard_map/ppermute | solution.py:65
  85.7 10.9 %collective-permute-done.15 = bf16[1024,256]{1,0:T(8,128)(2,1)S(1)} collective-permute-done((bf16[1024,256]{1,0:T(8,128)(2,1)S(1)}, bf16[1024,256]{1,0:T(8,128)(2,1)S(1)}, u32[]{:S(2)}, u32[]{:S(2)}) %collective-permute-start.15) | collective-permute-done | bytes 524320 | tf_op jit(solution)/shard_map/ppermute | solution.py:68
  96.5 0.8 fusion.30
  97.3 0.8 convolution_add_fusion.2
  98.1 2.5 %collective-permute-start.19 = (bf16[1792,128]{1,0:T(8,128)(2,1)S(1)}, bf16[1792,128]{1,0:T(8,128)(2,1)S(1)}, u32[]{:S(2)}, u32[]{:S(2)}) collective-permute-start(bf16[1792,128]{1,0:T(8,128)(2,1)S(1)} %broadcast_select_fusion.8), channel_id=1, source_target_pairs={{0,4},{1,5},{2,6},{3,7},{4,0},{5,1},{6,2},{7,3},{8,12},{9,13},{10,... | collective-permute-start | bytes 1376264 | tf_op jit(solution)/shard_map/ppermute | solution.py:68
  100.8 0.2 fusion.37
  101.0 0.8 broadcast_select_fusion.3
  101.8 0.1 constant_dynamic-update-slice_fusion
  102.0 0.2 broadcast_select_fusion.7
  102.2 0.6 collective-permute-start.22
  102.8 3.8 %collective-permute-start.24 = (f32[1024,128]{1,0:T(8,128)S(1)}, f32[1024,128]{1,0:T(8,128)S(1)}, u32[]{:S(2)}, u32[]{:S(2)}) collective-permute-start(f32[1024,128]{1,0:T(8,128)S(1)} %convolution_add_fusion.2), channel_id=1, source_target_pairs={{0,2},{1,3},{2,0},{3,1},{4,6},{5,7},{6,4},{7,5},{8,10},{9,11},{10,... | collective-permute-start | bytes 1572872 | tf_op jit(solution)/shard_map/ppermute | solution.py:65
  106.6 0.7 fusion.24
  107.4 0.7 convolution_add_fusion.1
  108.1 1.3 %fusion.8 = f32[1024,1024]{1,0:T(8,128)S(1)} fusion(bf16[1024,256]{1,0:T(8,128)(2,1)S(1)} %collective-permute-done.22, bf16[1024,256]{1,0:T(8,128)(2,1)S(1)} %get-tuple-element.108, bf16[1024,256]{1,0:T(8,128)(2,1)S(1)} %get-tuple-element.105, bf16[1024,256]{1,0:T(8,128)(2,1)S(1)} %get-tuple-element.103), kind=kOutput, calls=%fused_computation.19 | convolution fusion | flops 1077936128 | bytes 6291456 | tf_op jit(solution)/shard_map/dot_general | solution.py:38
  109.4 2.4 %fusion.5 = f32[1024,1024]{1,0:T(8,128)S(1)} fusion(f32[1024,1024]{1,0:T(8,128)S(1)} %fusion.8, bf16[1024,1024]{1,0:T(8,128)(2,1)S(1)} %constant_dynamic-update-slice_fusion, bf16[1024,512]{1,0:T(8,128)(2,1)S(1)} %collective-permute-done.20, bf16[1024,512]{1,0:T(8,128)(2,1)S(1)} %get-tuple-element.100), kind=kOutput, calls=%fused_computation.9 | convolution fusion | flops 2152726528 | bytes 12582912 | tf_op jit(solution)/shard_map/dot_general | solution.py:38
  111.9 0.3 broadcast_select_fusion.5
  112.2 0.1 collective-permute-start.25
  112.3 0.7 fusion.33
  113.0 0.8 convolution_add_fusion
  113.8 0.4 collective-permute-done.25
  114.2 3.3 %add_multiply_fusion = f32[1024,1024]{1,0:T(8,128)} fusion(f32[1024,1024]{1,0:T(8,128)S(1)} %fusion.5, f32[]{:T(128)} %bitcast, bf16[1024,256]{1,0:T(8,128)(2,1)S(1)} %collective-permute-done.25, bf16[1024,256]{1,0:T(8,128)(2,1)S(1)} %get-tuple-element.106, bf16[1024,256]{1,0:T(8,128)(2,1)S(1)} %get-tuple-element.104, bf16[1024,256]{1,0:T(8,128)(2,1)S(1)} %get-tuple-element.102), kind=kOutput, calls=%fused_computation | convolution fusion | flops 1080033280 | bytes 10485764 | tf_op jit(solution)/shard_map/dot_general | solution.py:38
  117.5 1.3 %collective-permute-done.24 = f32[1024,128]{1,0:T(8,128)S(1)} collective-permute-done((f32[1024,128]{1,0:T(8,128)S(1)}, f32[1024,128]{1,0:T(8,128)S(1)}, u32[]{:S(2)}, u32[]{:S(2)}) %collective-permute-start.24) | collective-permute-done | bytes 524320 | tf_op jit(solution)/shard_map/ppermute | solution.py:65
  118.8 1.6 %fusion.4 = f32[1024,512]{1,0:T(8,128)} fusion(f32[1024,256]{1,0:T(8,128)S(1)} %convolution_add_fusion, f32[1024,256]{1,0:T(8,128)S(1)} %convolution_add_fusion.1, f32[1024,128]{1,0:T(8,128)S(1)} %collective-permute-done.24, f32[1024,128]{1,0:T(8,128)S(1)} %collective-permute-done.17, f32[1024,128]{1,0:T(8,128)S(1)} %collective-permute-done.16, ...), kind=kLoop, calls=%fused_computation.6 | loop fusion | flops 3145728 | bytes 6291460 | tf_op jit(solution)/shard_map/mul | solution.py:192
  (46 shorter events, 1.1 us)
Async XLA Ops:
  0.6 4.8 %copy-start.1 = (bf16[1024,512]{1,0:T(8,128)(2,1)S(1)}, bf16[1024,512]{1,0:T(8,128)(2,1)}, u32[]{:S(2)}) copy-start(bf16[1024,512]{1,0:T(8,128)(2,1)} %param.4) | copy-start | bytes 3145732
  0.6 9.3 %collective-permute-start = (bf16[1024,1024]{1,0:T(8,128)(2,1)}, bf16[1024,1024]{1,0:T(8,128)(2,1)}, u32[]{:S(2)}, u32[]{:S(2)}) collective-permute-start(bf16[1024,1024]{1,0:T(8,128)(2,1)} %param.6), channel_id=1, source_target_pairs={{0,1},{1,0},{2,3},{3,2},{4,5},{5,4},{6,7},{7,6},{8,9},{9,8},{10,11... | collective-permute-start | bytes 6291464 | tf_op jit(solution)/shard_map/ppermute | solution.py:71
  2.8 9.7 %collective-permute-start.1 = (bf16[1024,128]{1,0:T(8,128)(2,1)S(1)}, bf16[1024,128]{1,0:T(8,128)(2,1)S(1)}, u32[]{:S(2)}, u32[]{:S(2)}) collective-permute-start(bf16[1024,128]{1,0:T(8,128)(2,1)S(1)} %get-tuple-element.111), channel_id=1, source_target_pairs={{0,2},{1,3},{2,0},{3,1},{4,6},{5,7},{6,4},{7,5},{8,10},{9,11},{10,... | collective-permute-start | bytes 786440 | tf_op jit(solution)/shard_map/ppermute | solution.py:65
  5.5 7.0 %collective-permute-start.3 = (bf16[256,128]{1,0:T(8,128)(2,1)S(1)}, bf16[256,128]{1,0:T(8,128)(2,1)S(1)}, u32[]{:S(2)}, u32[]{:S(2)}) collective-permute-start(bf16[256,128]{1,0:T(8,128)(2,1)S(1)} %slice.106), channel_id=1, source_target_pairs={{0,8},{1,9},{4,12},{5,13},{10,2},{11,3},{14,6},{15,7},{16,24},{17,... | collective-permute-start | bytes 196616 | tf_op jit(solution)/shard_map/ppermute | solution.py:74
  12.6 13.8 %collective-permute-start.4 = (bf16[1024,256]{1,0:T(8,128)(2,1)S(1)}, bf16[1024,256]{1,0:T(8,128)(2,1)S(1)}, u32[]{:S(2)}, u32[]{:S(2)}) collective-permute-start(bf16[1024,256]{1,0:T(8,128)(2,1)S(1)} %pad_maximum_fusion.3), channel_id=1, source_target_pairs={{0,2},{1,3},{2,0},{3,1},{4,6},{5,7},{6,4},{7,5},{8,10},{9,11},{10,... | collective-permute-start | bytes 1572872 | tf_op jit(solution)/shard_map/ppermute | solution.py:65
  14.3 14.1 %collective-permute-start.2 = (bf16[1024,128]{1,0:T(8,128)(2,1)S(1)}, bf16[1024,128]{1,0:T(8,128)(2,1)S(1)}, u32[]{:S(2)}, u32[]{:S(2)}) collective-permute-start(bf16[1024,128]{1,0:T(8,128)(2,1)S(1)} %broadcast_select_fusion.18), channel_id=1, source_target_pairs={{0,8},{1,9},{2,10},{3,11},{4,12},{5,13},{6,14},{7,15},{8,0},{9,1},... | collective-permute-start | bytes 786440 | tf_op jit(solution)/shard_map/ppermute | solution.py:77
  16.9 11.5 %collective-permute-start.5 = (bf16[256,128]{1,0:T(8,128)(2,1)S(1)}, bf16[256,128]{1,0:T(8,128)(2,1)S(1)}, u32[]{:S(2)}, u32[]{:S(2)}) collective-permute-start(bf16[256,128]{1,0:T(8,128)(2,1)S(1)} %broadcast_select_fusion.20), channel_id=1, source_target_pairs={{0,4},{1,5},{2,6},{3,7},{4,0},{5,1},{6,2},{7,3},{8,12},{9,13},{10,... | collective-permute-start | bytes 196616 | tf_op jit(solution)/shard_map/ppermute | solution.py:68
  28.5 12.5 %collective-permute-start.6 = (bf16[1024,128]{1,0:T(8,128)(2,1)S(1)}, bf16[1024,128]{1,0:T(8,128)(2,1)S(1)}, u32[]{:S(2)}, u32[]{:S(2)}) collective-permute-start(bf16[1024,128]{1,0:T(8,128)(2,1)S(1)} %broadcast_select_fusion.15), channel_id=1, source_target_pairs={{0,4},{1,5},{2,6},{3,7},{4,0},{5,1},{6,2},{7,3},{8,12},{9,13},{10,... | collective-permute-start | bytes 786440 | tf_op jit(solution)/shard_map/ppermute | solution.py:68
  29.3 16.9 %collective-permute-start.7 = (bf16[1024,128]{1,0:T(8,128)(2,1)S(1)}, bf16[1024,128]{1,0:T(8,128)(2,1)S(1)}, u32[]{:S(2)}, u32[]{:S(2)}) collective-permute-start(bf16[1024,128]{1,0:T(8,128)(2,1)S(1)} %get-tuple-element.130), channel_id=1, source_target_pairs={{0,8},{1,9},{2,10},{3,11},{4,12},{5,13},{6,14},{7,15},{8,0},{9,1},... | collective-permute-start | bytes 786440 | tf_op jit(solution)/shard_map/ppermute | solution.py:77
  32.8 13.4 %collective-permute-start.8 = (bf16[1024,256]{1,0:T(8,128)(2,1)S(1)}, bf16[1024,256]{1,0:T(8,128)(2,1)S(1)}, u32[]{:S(2)}, u32[]{:S(2)}) collective-permute-start(bf16[1024,256]{1,0:T(8,128)(2,1)S(1)} %pad_maximum_fusion.4), channel_id=1, source_target_pairs={{0,2},{1,3},{2,0},{3,1},{4,6},{5,7},{6,4},{7,5},{8,10},{9,11},{10,... | collective-permute-start | bytes 1572872 | tf_op jit(solution)/shard_map/ppermute | solution.py:65
  42.5 4.7 %copy-start = (bf16[1024,512]{1,0:T(8,128)(2,1)S(1)}, bf16[1024,512]{1,0:T(8,128)(2,1)}, u32[]{:S(2)}) copy-start(bf16[1024,512]{1,0:T(8,128)(2,1)} %param.5) | copy-start | bytes 3145732
  46.2 6.8 %collective-permute-start.11 = (bf16[1024,128]{1,0:T(8,128)(2,1)S(1)}, bf16[1024,128]{1,0:T(8,128)(2,1)S(1)}, u32[]{:S(2)}, u32[]{:S(2)}) collective-permute-start(bf16[1024,128]{1,0:T(8,128)(2,1)S(1)} %broadcast_select_fusion.12), channel_id=1, source_target_pairs={{0,2},{1,3},{2,0},{3,1},{4,6},{5,7},{6,4},{7,5},{8,10},{9,11},{10,... | collective-permute-start | bytes 786440 | tf_op jit(solution)/shard_map/ppermute | solution.py:65
  46.9 10.9 %collective-permute-start.9 = (bf16[1024,128]{1,0:T(8,128)(2,1)S(1)}, bf16[1024,128]{1,0:T(8,128)(2,1)S(1)}, u32[]{:S(2)}, u32[]{:S(2)}) collective-permute-start(bf16[1024,128]{1,0:T(8,128)(2,1)S(1)} %broadcast_select_fusion.13), channel_id=1, source_target_pairs={{0,4},{1,5},{2,6},{3,7},{4,0},{5,1},{6,2},{7,3},{8,12},{9,13},{10,... | collective-permute-start | bytes 786440 | tf_op jit(solution)/shard_map/ppermute | solution.py:68
  47.3 13.1 %collective-permute-start.10 = (bf16[1024,128]{1,0:T(8,128)(2,1)S(1)}, bf16[1024,128]{1,0:T(8,128)(2,1)S(1)}, u32[]{:S(2)}, u32[]{:S(2)}) collective-permute-start(bf16[1024,128]{1,0:T(8,128)(2,1)S(1)} %get-tuple-element.127), channel_id=1, source_target_pairs={{0,8},{1,9},{2,10},{3,11},{4,12},{5,13},{6,14},{7,15},{8,0},{9,1},... | collective-permute-start | bytes 786440 | tf_op jit(solution)/shard_map/ppermute | solution.py:77
  53.0 13.7 %collective-permute-start.14 = (f32[1024,128]{1,0:T(8,128)S(1)}, f32[1024,128]{1,0:T(8,128)S(1)}, u32[]{:S(2)}, u32[]{:S(2)}) collective-permute-start(f32[1024,128]{1,0:T(8,128)S(1)} %convolution_add_fusion.5), channel_id=1, source_target_pairs={{0,2},{1,3},{2,0},{3,1},{4,6},{5,7},{6,4},{7,5},{8,10},{9,11},{10,... | collective-permute-start | bytes 1572872 | tf_op jit(solution)/shard_map/ppermute | solution.py:65
  60.6 17.0 %collective-permute-start.12 = (bf16[1024,256]{1,0:T(8,128)(2,1)S(1)}, bf16[1024,256]{1,0:T(8,128)(2,1)S(1)}, u32[]{:S(2)}, u32[]{:S(2)}) collective-permute-start(bf16[1024,256]{1,0:T(8,128)(2,1)S(1)} %maximum_select_fusion), channel_id=1, source_target_pairs={{0,4},{1,5},{2,6},{3,7},{4,0},{5,1},{6,2},{7,3},{8,12},{9,13},{10,... | collective-permute-start | bytes 1572872 | tf_op jit(solution)/shard_map/ppermute | solution.py:68
  61.4 17.7 %collective-permute-start.13 = (bf16[1024,128]{1,0:T(8,128)(2,1)S(1)}, bf16[1024,128]{1,0:T(8,128)(2,1)S(1)}, u32[]{:S(2)}, u32[]{:S(2)}) collective-permute-start(bf16[1024,128]{1,0:T(8,128)(2,1)S(1)} %broadcast_select_fusion.11), channel_id=1, source_target_pairs={{0,8},{1,9},{2,10},{3,11},{4,12},{5,13},{6,14},{7,15},{8,0},{9,1},... | collective-permute-start | bytes 786440 | tf_op jit(solution)/shard_map/ppermute | solution.py:77
  63.5 33.8 %collective-permute-start.18 = (bf16[1792,128]{1,0:T(8,128)(2,1)S(1)}, bf16[1792,128]{1,0:T(8,128)(2,1)S(1)}, u32[]{:S(2)}, u32[]{:S(2)}) collective-permute-start(bf16[1792,128]{1,0:T(8,128)(2,1)S(1)} %pad_maximum_fusion.7), channel_id=1, source_target_pairs={{0,8},{1,9},{4,12},{5,13},{10,2},{11,3},{14,6},{15,7},{16,24},{17,... | collective-permute-start | bytes 1376264 | tf_op jit(solution)/shard_map/ppermute | solution.py:74
  66.8 13.6 %collective-permute-start.16 = (f32[1024,128]{1,0:T(8,128)S(1)}, f32[1024,128]{1,0:T(8,128)S(1)}, u32[]{:S(2)}, u32[]{:S(2)}) collective-permute-start(f32[1024,128]{1,0:T(8,128)S(1)} %convolution_add_fusion.4), channel_id=1, source_target_pairs={{0,2},{1,3},{2,0},{3,1},{4,6},{5,7},{6,4},{7,5},{8,10},{9,11},{10,... | collective-permute-start | bytes 1572872 | tf_op jit(solution)/shard_map/ppermute | solution.py:65
  79.3 17.2 %collective-permute-start.15 = (bf16[1024,256]{1,0:T(8,128)(2,1)S(1)}, bf16[1024,256]{1,0:T(8,128)(2,1)S(1)}, u32[]{:S(2)}, u32[]{:S(2)}) collective-permute-start(bf16[1024,256]{1,0:T(8,128)(2,1)S(1)} %maximum_select_fusion.1), channel_id=1, source_target_pairs={{0,4},{1,5},{2,6},{3,7},{4,0},{5,1},{6,2},{7,3},{8,12},{9,13},{10,... | collective-permute-start | bytes 1572872 | tf_op jit(solution)/shard_map/ppermute | solution.py:68
  79.5 22.3 %collective-permute-start.21 = (bf16[1024,512]{1,0:T(8,128)(2,1)S(1)}, bf16[1024,512]{1,0:T(8,128)(2,1)S(1)}, u32[]{:S(2)}, u32[]{:S(2)}) collective-permute-start(bf16[1024,512]{1,0:T(8,128)(2,1)S(1)} %pad_maximum_fusion.2), channel_id=1, source_target_pairs={{0,1},{1,0},{2,3},{3,2},{4,5},{5,4},{6,7},{7,6},{8,9},{9,8},{10,11... | collective-permute-start | bytes 3145736 | tf_op jit(solution)/shard_map/ppermute | solution.py:71
  79.6 21.1 %collective-permute-start.23 = (bf16[1024,512]{1,0:T(8,128)(2,1)S(1)}, bf16[1024,512]{1,0:T(8,128)(2,1)S(1)}, u32[]{:S(2)}, u32[]{:S(2)}) collective-permute-start(bf16[1024,512]{1,0:T(8,128)(2,1)S(1)} %copy-done), channel_id=1, source_target_pairs={{0,1},{1,0},{2,3},{3,2},{4,5},{5,4},{6,7},{7,6},{8,9},{9,8},{10,11... | collective-permute-start | bytes 3145736 | tf_op jit(solution)/shard_map/ppermute | solution.py:71
  80.3 20.4 %collective-permute-start.17 = (f32[1024,128]{1,0:T(8,128)S(1)}, f32[1024,128]{1,0:T(8,128)S(1)}, u32[]{:S(2)}, u32[]{:S(2)}) collective-permute-start(f32[1024,128]{1,0:T(8,128)S(1)} %convolution_add_fusion.3), channel_id=1, source_target_pairs={{0,2},{1,3},{2,0},{3,1},{4,6},{5,7},{6,4},{7,5},{8,10},{9,11},{10,... | collective-permute-start | bytes 1572872 | tf_op jit(solution)/shard_map/ppermute | solution.py:65
  98.1 13.7 %collective-permute-start.19 = (bf16[1792,128]{1,0:T(8,128)(2,1)S(1)}, bf16[1792,128]{1,0:T(8,128)(2,1)S(1)}, u32[]{:S(2)}, u32[]{:S(2)}) collective-permute-start(bf16[1792,128]{1,0:T(8,128)(2,1)S(1)} %broadcast_select_fusion.8), channel_id=1, source_target_pairs={{0,4},{1,5},{2,6},{3,7},{4,0},{5,1},{6,2},{7,3},{8,12},{9,13},{10,... | collective-permute-start | bytes 1376264 | tf_op jit(solution)/shard_map/ppermute | solution.py:68
  101.8 7.7 %collective-permute-start.20 = (bf16[1024,512]{1,0:T(8,128)(2,1)S(1)}, bf16[1024,512]{1,0:T(8,128)(2,1)S(1)}, u32[]{:S(2)}, u32[]{:S(2)}) collective-permute-start(bf16[1024,512]{1,0:T(8,128)(2,1)S(1)} %get-tuple-element.101), channel_id=1, source_target_pairs={{0,1},{1,0},{2,3},{3,2},{4,5},{5,4},{6,7},{7,6},{8,9},{9,8},{10,11... | collective-permute-start | bytes 3145736 | tf_op jit(solution)/shard_map/ppermute | solution.py:71
  102.2 5.9 %collective-permute-start.22 = (bf16[1024,256]{1,0:T(8,128)(2,1)S(1)}, bf16[1024,256]{1,0:T(8,128)(2,1)S(1)}, u32[]{:S(2)}, u32[]{:S(2)}) collective-permute-start(bf16[1024,256]{1,0:T(8,128)(2,1)S(1)} %get-tuple-element.109), channel_id=1, source_target_pairs={{0,1},{1,0},{2,3},{3,2},{4,5},{5,4},{6,7},{7,6},{8,9},{9,8},{10,11... | collective-permute-start | bytes 1572872 | tf_op jit(solution)/shard_map/ppermute | solution.py:71
  102.8 16.0 %collective-permute-start.24 = (f32[1024,128]{1,0:T(8,128)S(1)}, f32[1024,128]{1,0:T(8,128)S(1)}, u32[]{:S(2)}, u32[]{:S(2)}) collective-permute-start(f32[1024,128]{1,0:T(8,128)S(1)} %convolution_add_fusion.2), channel_id=1, source_target_pairs={{0,2},{1,3},{2,0},{3,1},{4,6},{5,7},{6,4},{7,5},{8,10},{9,11},{10,... | collective-permute-start | bytes 1572872 | tf_op jit(solution)/shard_map/ppermute | solution.py:65
  112.2 2.0 %collective-permute-start.25 = (bf16[1024,256]{1,0:T(8,128)(2,1)S(1)}, bf16[1024,256]{1,0:T(8,128)(2,1)S(1)}, u32[]{:S(2)}, u32[]{:S(2)}) collective-permute-start(bf16[1024,256]{1,0:T(8,128)(2,1)S(1)} %get-tuple-element.107), channel_id=1, source_target_pairs={{0,1},{1,0},{2,3},{3,2},{4,5},{5,4},{6,7},{7,6},{8,9},{9,8},{10,11... | collective-permute-start | bytes 1572872 | tf_op jit(solution)/shard_map/ppermute | solution.py:71

commit v21 on v20

--- a/solution.py
+++ b/solution.py
@@ -94,7 +94,7 @@
         v = [columns(value_next, i, i + 1) for i in range(4)]
         x1 = cross(jnp.where(home, v[0], e[0]))
         height = e[3].shape[0]
-        rows = height // 4
+        rows = height * 3 // 4
         j0 = home_jump(e[3][:rows])
         t_other = swap(transition)
         e2 = after(e[2], x1)

time: 121 us -> 120 us (level)
    ppermute x6, waiting for transfers between devices: 33.4 us -> 31 us  [step(): return lax.ppermute(a, AXES, step_pairs)]
    ppermute x4, starting transfers between devices: 9.24 us -> 7 us  [jump(): return lax.ppermute(a, AXES, jump_pairs)]
    ppermute x2, waiting for transfers between devices: 0.01 us -> 1.96 us  [home_jump(): return lax.ppermute(a, AXES, home_jump_pairs)]
    ppermute x6, starting transfers between devices: 5.43 us -> 7.12 us  [step(): return lax.ppermute(a, AXES, step_pairs)]
    ppermute x8, starting transfers between devices: 15.3 us -> 16.6 us  [cross(): return lax.ppermute(a, AXES, cross_pairs)]
  transfers between devices with their start and end apart: 26 -> 26, of which waited for: 11 -> 12; matrix products, arithmetic and copies ran while one was open for 19% -> 20% of each run, Pallas kernels for 0% -> 0%
where the time goes in v21:
time: 120 us
  waiting for transfers between devices  53.1 us (44%)
  starting transfers between devices  39.7 us (33%)
  matrix products  16 us (13%)
  other arithmetic  8.9 us (7%)
  between operations  1.84 us (2%)
    ppermute x6, waiting for transfers between devices, step(): return lax.ppermute(a, AXES, step_pairs)  31 us
    ppermute x8, starting transfers between devices, cross(): return lax.ppermute(a, AXES, cross_pairs)  16.6 us
    ppermute x8, waiting for transfers between devices, cross(): return lax.ppermute(a, AXES, cross_pairs)  16.6 us
    dot_general x12, matrix products, tdot(): lax.dot_general(a, b, (((0,), (0,)), ((), ())), preferred_element_type=jn...  9.04 us
    ppermute x2, starting transfers between devices, home_jump(): return lax.ppermute(a, AXES, home_jump_pairs)  7.2 us
    ppermute x6, starting transfers between devices, step(): return lax.ppermute(a, AXES, step_pairs)  7.12 us
    ppermute x4, starting transfers between devices, jump(): return lax.ppermute(a, AXES, jump_pairs)  7 us
    dot_general x3, matrix products, dott(): lax.dot_general(a, b, (((1,), (1,)), ((), ())), preferred_element_type=jn...  6.97 us
  transfers between devices with their start and end apart: 26, of which 12 were waited for; matrix products, arithmetic and copies ran while one was open for 20% of the time, Pallas kernels for 0%

profile of v21, /device:TPU:0, one launch (start us, length us, event | category | flops | bytes accessed | tf_op | source)
XLA Modules:
  0.0 120.3 jit_solution(8497174169613708105)
XLA Ops:
  0.6 0.5 collective-permute-start
  1.2 2.3 %fusion.36 = (bf16[1024,128]{1,0:T(8,128)(2,1)S(1)}, bf16[1024,128]{1,0:T(8,128)(2,1)}, bf16[1024,128]{1,0:T(8,128)(2,1)S(1)}, bf16[1024,128]{1,0:T(8,128)(2,1)S...) fusion(bf16[1024,512]{1,0:T(8,128)(2,1)} %param.4, ...), kind=kLoop, calls=%fused_computation.81 | loop fusion | flops 131072 | bytes 3932161 | tf_op jit(solution)/shard_map/slice | solution.py:88
  3.5 2.6 %collective-permute-start.1 = (bf16[1024,128]{1,0:T(8,128)(2,1)}, bf16[1024,128]{1,0:T(8,128)(2,1)S(1)}, u32[]{:S(2)}, u32[]{:S(2)}) collective-permute-start(bf16[1024,128]{1,0:T(8,128)(2,1)} %get-tuple-element.111), channel_id=1, source_target_pairs={{0,2},{1,3},{2,0},{3,1},{4,6},{5,7},{6,4},{7,5},{8,10},{9,11},{10,... | collective-permute-start | bytes 786440 | tf_op jit(solution)/shard_map/ppermute | solution.py:65
  6.1 4.5 %collective-permute-start.3 = (bf16[768,128]{1,0:T(8,128)(2,1)S(1)}, bf16[768,128]{1,0:T(8,128)(2,1)S(1)}, u32[]{:S(2)}, u32[]{:S(2)}) collective-permute-start(bf16[768,128]{1,0:T(8,128)(2,1)S(1)} %slice.106), channel_id=1, source_target_pairs={{0,8},{1,9},{4,12},{5,13},{10,2},{11,3},{14,6},{15,7},{16,24},{17,... | collective-permute-start | bytes 589832 | tf_op jit(solution)/shard_map/ppermute | solution.py:74
  10.6 2.5 %broadcast_select_fusion.1 = (bf16[1024,1024]{1,0:T(8,128)(2,1)S(1)}, bf16[1024,1024]{1,0:T(8,128)(2,1)S(1)}) fusion(bf16[1024,1024]{1,0:T(8,128)(2,1)} %param.6, bf16[1024,1024]{1,0:T(8,128)(2,1)} %collective-permute-done, pred[]{:T(512)S(6)} %eq.8), kind=kLoop, calls=%fused_computation.8 | loop fusion | flops 2097152 | bytes 8388609 | tf_op jit(solution)/shard_map/jit(_where)/select_n | solution.py:102
  13.1 2.0 %collective-permute-done.3 = bf16[768,128]{1,0:T(8,128)(2,1)S(1)} collective-permute-done((bf16[768,128]{1,0:T(8,128)(2,1)S(1)}, bf16[768,128]{1,0:T(8,128)(2,1)S(1)}, u32[]{:S(2)}, u32[]{:S(2)}) %collective-permute-start.3) | collective-permute-done | bytes 196640 | tf_op jit(solution)/shard_map/ppermute | solution.py:74
  15.2 5.3 %collective-permute-start.4 = (bf16[1024,256]{1,0:T(8,128)(2,1)S(1)}, bf16[1024,256]{1,0:T(8,128)(2,1)S(1)}, u32[]{:S(2)}, u32[]{:S(2)}) collective-permute-start(bf16[1024,256]{1,0:T(8,128)(2,1)S(1)} %pad_maximum_fusion.3), channel_id=1, source_target_pairs={{0,2},{1,3},{2,0},{3,1},{4,6},{5,7},{6,4},{7,5},{8,10},{9,11},{10,... | collective-permute-start | bytes 1572872 | tf_op jit(solution)/shard_map/ppermute | solution.py:65
  20.6 0.1 collective-permute-start.2
  20.7 3.8 %collective-permute-start.5 = (bf16[768,128]{1,0:T(8,128)(2,1)S(1)}, bf16[768,128]{1,0:T(8,128)(2,1)S(1)}, u32[]{:S(2)}, u32[]{:S(2)}) collective-permute-start(bf16[768,128]{1,0:T(8,128)(2,1)S(1)} %broadcast_select_fusion.20), channel_id=1, source_target_pairs={{0,4},{1,5},{2,6},{3,7},{4,0},{5,1},{6,2},{7,3},{8,12},{9,13},{10,... | collective-permute-start | bytes 589832 | tf_op jit(solution)/shard_map/ppermute | solution.py:68
  24.5 7.7 %collective-permute-done.4 = bf16[1024,256]{1,0:T(8,128)(2,1)S(1)} collective-permute-done((bf16[1024,256]{1,0:T(8,128)(2,1)S(1)}, bf16[1024,256]{1,0:T(8,128)(2,1)S(1)}, u32[]{:S(2)}, u32[]{:S(2)}) %collective-permute-start.4) | collective-permute-done | bytes 524320 | tf_op jit(solution)/shard_map/ppermute | solution.py:65
  32.3 2.4 %collective-permute-done.2 = bf16[1024,128]{1,0:T(8,128)(2,1)S(1)} collective-permute-done((bf16[1024,128]{1,0:T(8,128)(2,1)S(1)}, bf16[1024,128]{1,0:T(8,128)(2,1)S(1)}, u32[]{:S(2)}, u32[]{:S(2)}) %collective-permute-start.2) | collective-permute-done | bytes 262176 | tf_op jit(solution)/shard_map/ppermute | solution.py:77
  34.8 0.2 collective-permute-start.6
  35.0 3.4 %collective-permute-start.7 = (bf16[1024,128]{1,0:T(8,128)(2,1)S(1)}, bf16[1024,128]{1,0:T(8,128)(2,1)S(1)}, u32[]{:S(2)}, u32[]{:S(2)}) collective-permute-start(bf16[1024,128]{1,0:T(8,128)(2,1)S(1)} %get-tuple-element.130), channel_id=1, source_target_pairs={{0,8},{1,9},{2,10},{3,11},{4,12},{5,13},{6,14},{7,15},{8,0},{9,1},... | collective-permute-start | bytes 786440 | tf_op jit(solution)/shard_map/ppermute | solution.py:77
  38.5 0.5 collective-permute-start.8
  39.0 8.0 %collective-permute-done.6 = bf16[1024,128]{1,0:T(8,128)(2,1)S(1)} collective-permute-done((bf16[1024,128]{1,0:T(8,128)(2,1)S(1)}, bf16[1024,128]{1,0:T(8,128)(2,1)S(1)}, u32[]{:S(2)}, u32[]{:S(2)}) %collective-permute-start.6) | collective-permute-done | bytes 262176 | tf_op jit(solution)/shard_map/ppermute | solution.py:68
  47.1 0.7 fusion.43
  47.8 0.8 convolution_add_fusion.5
  48.6 2.5 %collective-permute-done.8 = bf16[1024,256]{1,0:T(8,128)(2,1)S(1)} collective-permute-done((bf16[1024,256]{1,0:T(8,128)(2,1)S(1)}, bf16[1024,256]{1,0:T(8,128)(2,1)S(1)}, u32[]{:S(2)}, u32[]{:S(2)}) %collective-permute-start.8) | collective-permute-done | bytes 524320 | tf_op jit(solution)/shard_map/ppermute | solution.py:65
  51.1 0.7 collective-permute-start.11
  51.9 0.4 collective-permute-start.9
  52.3 1.1 collective-permute-start.10
  53.4 5.0 %collective-permute-done.11 = bf16[1024,128]{1,0:T(8,128)(2,1)S(1)} collective-permute-done((bf16[1024,128]{1,0:T(8,128)(2,1)S(1)}, bf16[1024,128]{1,0:T(8,128)(2,1)S(1)}, u32[]{:S(2)}, u32[]{:S(2)}) %collective-permute-start.11) | collective-permute-done | bytes 262176 | tf_op jit(solution)/shard_map/ppermute | solution.py:65
  58.4 0.4 collective-permute-start.14
  58.8 3.4 %collective-permute-done.9 = bf16[1024,128]{1,0:T(8,128)(2,1)S(1)} collective-permute-done((bf16[1024,128]{1,0:T(8,128)(2,1)S(1)}, bf16[1024,128]{1,0:T(8,128)(2,1)S(1)}, u32[]{:S(2)}, u32[]{:S(2)}) %collective-permute-start.9) | collective-permute-done | bytes 262176 | tf_op jit(solution)/shard_map/ppermute | solution.py:68
  62.2 0.7 fusion.44
  62.9 0.8 convolution_add_fusion.4
  63.7 0.8 collective-permute-done.10
  64.5 0.2 maximum_select_fusion
  64.7 0.1 collective-permute-start.12
  65.5 2.4 %collective-permute-start.13 = (bf16[1024,128]{1,0:T(8,128)(2,1)S(1)}, bf16[1024,128]{1,0:T(8,128)(2,1)S(1)}, u32[]{:S(2)}, u32[]{:S(2)}) collective-permute-start(bf16[1024,128]{1,0:T(8,128)(2,1)S(1)} %broadcast_select_fusion.11), channel_id=1, source_target_pairs={{0,8},{1,9},{2,10},{3,11},{4,12},{5,13},{6,14},{7,15},{8,0},{9,1},... | collective-permute-start | bytes 786440 | tf_op jit(solution)/shard_map/ppermute | solution.py:77
  67.9 2.7 %collective-permute-start.18 = (bf16[1280,128]{1,0:T(8,128)(2,1)S(1)}, bf16[1280,128]{1,0:T(8,128)(2,1)S(1)}, u32[]{:S(2)}, u32[]{:S(2)}) collective-permute-start(bf16[1280,128]{1,0:T(8,128)(2,1)S(1)} %pad_maximum_fusion.7), channel_id=1, source_target_pairs={{0,8},{1,9},{4,12},{5,13},{10,2},{11,3},{14,6},{15,7},{16,24},{17,... | collective-permute-start | bytes 983048 | tf_op jit(solution)/shard_map/ppermute | solution.py:74
  70.6 0.1 constant_dynamic-update-slice_fusion.4
  70.7 0.1 constant_dynamic-update-slice_fusion.3
  70.8 0.1 collective-permute-start.16
  70.9 10.6 %collective-permute-done.12 = bf16[1024,256]{1,0:T(8,128)(2,1)S(1)} collective-permute-done((bf16[1024,256]{1,0:T(8,128)(2,1)S(1)}, bf16[1024,256]{1,0:T(8,128)(2,1)S(1)}, u32[]{:S(2)}, u32[]{:S(2)}) %collective-permute-start.12) | collective-permute-done | bytes 524320 | tf_op jit(solution)/shard_map/ppermute | solution.py:68
  81.5 0.8 fusion.21
  82.2 0.8 convolution_add_fusion.3
  83.0 0.2 maximum_select_fusion.1
  83.3 0.1 pad_maximum_fusion.2
  83.5 0.5 collective-permute-start.23
  84.0 0.1 constant_dynamic-update-slice_fusion.2
  84.1 0.1 constant_dynamic-update-slice_fusion.1
  84.2 4.4 %collective-permute-start.17 = (f32[1024,128]{1,0:T(8,128)S(1)}, f32[1024,128]{1,0:T(8,128)S(1)}, u32[]{:S(2)}, u32[]{:S(2)}) collective-permute-start(f32[1024,128]{1,0:T(8,128)S(1)} %convolution_add_fusion.3), channel_id=1, source_target_pairs={{0,2},{1,3},{2,0},{3,1},{4,6},{5,7},{6,4},{7,5},{8,10},{9,11},{10,... | collective-permute-start | bytes 1572872 | tf_op jit(solution)/shard_map/ppermute | solution.py:65
  88.7 8.9 %collective-permute-done.15 = bf16[1024,256]{1,0:T(8,128)(2,1)S(1)} collective-permute-done((bf16[1024,256]{1,0:T(8,128)(2,1)S(1)}, bf16[1024,256]{1,0:T(8,128)(2,1)S(1)}, u32[]{:S(2)}, u32[]{:S(2)}) %collective-permute-start.15) | collective-permute-done | bytes 524320 | tf_op jit(solution)/shard_map/ppermute | solution.py:68
  97.6 0.8 fusion.30
  98.4 0.8 convolution_add_fusion.2
  99.2 2.6 %collective-permute-start.19 = (bf16[1280,128]{1,0:T(8,128)(2,1)S(1)}, bf16[1280,128]{1,0:T(8,128)(2,1)S(1)}, u32[]{:S(2)}, u32[]{:S(2)}) collective-permute-start(bf16[1280,128]{1,0:T(8,128)(2,1)S(1)} %broadcast_select_fusion.8), channel_id=1, source_target_pairs={{0,4},{1,5},{2,6},{3,7},{4,0},{5,1},{6,2},{7,3},{8,12},{9,13},{10,... | collective-permute-start | bytes 983048 | tf_op jit(solution)/shard_map/ppermute | solution.py:68
  101.9 0.2 fusion.37
  102.1 0.8 broadcast_select_fusion.3
  102.9 0.1 constant_dynamic-update-slice_fusion
  103.1 0.2 broadcast_select_fusion.7
  103.3 0.6 collective-permute-start.22
  103.9 2.6 %collective-permute-start.24 = (f32[1024,128]{1,0:T(8,128)S(1)}, f32[1024,128]{1,0:T(8,128)S(1)}, u32[]{:S(2)}, u32[]{:S(2)}) collective-permute-start(f32[1024,128]{1,0:T(8,128)S(1)} %convolution_add_fusion.2), channel_id=1, source_target_pairs={{0,2},{1,3},{2,0},{3,1},{4,6},{5,7},{6,4},{7,5},{8,10},{9,11},{10,... | collective-permute-start | bytes 1572872 | tf_op jit(solution)/shard_map/ppermute | solution.py:65
  106.5 0.7 fusion.24
  107.2 0.8 convolution_add_fusion.1
  108.0 1.3 %fusion.8 = f32[1024,1024]{1,0:T(8,128)S(1)} fusion(bf16[1024,256]{1,0:T(8,128)(2,1)S(1)} %collective-permute-done.22, bf16[1024,256]{1,0:T(8,128)(2,1)S(1)} %get-tuple-element.108, bf16[1024,256]{1,0:T(8,128)(2,1)S(1)} %get-tuple-element.105, bf16[1024,256]{1,0:T(8,128)(2,1)S(1)} %get-tuple-element.103), kind=kOutput, calls=%fused_computation.19 | convolution fusion | flops 1077936128 | bytes 6291456 | tf_op jit(solution)/shard_map/dot_general | solution.py:38
  109.3 2.4 %fusion.5 = f32[1024,1024]{1,0:T(8,128)S(1)} fusion(f32[1024,1024]{1,0:T(8,128)S(1)} %fusion.8, bf16[1024,1024]{1,0:T(8,128)(2,1)S(1)} %constant_dynamic-update-slice_fusion, bf16[1024,512]{1,0:T(8,128)(2,1)S(1)} %collective-permute-done.20, bf16[1024,512]{1,0:T(8,128)(2,1)S(1)} %get-tuple-element.100), kind=kOutput, calls=%fused_computation.9 | convolution fusion | flops 2152726528 | bytes 12582912 | tf_op jit(solution)/shard_map/dot_general | solution.py:38
  111.8 0.3 broadcast_select_fusion.5
  112.1 0.7 fusion.33
  112.9 0.8 convolution_add_fusion
  113.6 0.4 collective-permute-done.25
  114.0 3.3 %add_multiply_fusion = f32[1024,1024]{1,0:T(8,128)} fusion(f32[1024,1024]{1,0:T(8,128)S(1)} %fusion.5, f32[]{:T(128)} %bitcast, bf16[1024,256]{1,0:T(8,128)(2,1)S(1)} %collective-permute-done.25, bf16[1024,256]{1,0:T(8,128)(2,1)S(1)} %get-tuple-element.106, bf16[1024,256]{1,0:T(8,128)(2,1)S(1)} %get-tuple-element.104, bf16[1024,256]{1,0:T(8,128)(2,1)S(1)} %get-tuple-element.102), kind=kOutput, calls=%fused_computation | convolution fusion | flops 1080033280 | bytes 10485764 | tf_op jit(solution)/shard_map/dot_general | solution.py:38
  117.3 1.3 %collective-permute-done.24 = f32[1024,128]{1,0:T(8,128)S(1)} collective-permute-done((f32[1024,128]{1,0:T(8,128)S(1)}, f32[1024,128]{1,0:T(8,128)S(1)}, u32[]{:S(2)}, u32[]{:S(2)}) %collective-permute-start.24) | collective-permute-done | bytes 524320 | tf_op jit(solution)/shard_map/ppermute | solution.py:65
  118.7 1.6 %fusion.4 = f32[1024,512]{1,0:T(8,128)} fusion(f32[1024,256]{1,0:T(8,128)S(1)} %convolution_add_fusion, f32[1024,256]{1,0:T(8,128)S(1)} %convolution_add_fusion.1, f32[1024,128]{1,0:T(8,128)S(1)} %collective-permute-done.24, f32[1024,128]{1,0:T(8,128)S(1)} %collective-permute-done.17, f32[1024,128]{1,0:T(8,128)S(1)} %collective-permute-done.16, ...), kind=kLoop, calls=%fused_computation.6 | loop fusion | flops 3145728 | bytes 6291460 | tf_op jit(solution)/shard_map/mul | solution.py:192
  (46 shorter events, 1.2 us)
Async XLA Ops:
  0.6 5.4 %copy-start.1 = (bf16[1024,512]{1,0:T(8,128)(2,1)S(1)}, bf16[1024,512]{1,0:T(8,128)(2,1)}, u32[]{:S(2)}) copy-start(bf16[1024,512]{1,0:T(8,128)(2,1)} %param.4) | copy-start | bytes 3145732
  0.6 10.0 %collective-permute-start = (bf16[1024,1024]{1,0:T(8,128)(2,1)}, bf16[1024,1024]{1,0:T(8,128)(2,1)}, u32[]{:S(2)}, u32[]{:S(2)}) collective-permute-start(bf16[1024,1024]{1,0:T(8,128)(2,1)} %param.6), channel_id=1, source_target_pairs={{0,1},{1,0},{2,3},{3,2},{4,5},{5,4},{6,7},{7,6},{8,9},{9,8},{10,11... | collective-permute-start | bytes 6291464 | tf_op jit(solution)/shard_map/ppermute | solution.py:71
  3.5 11.6 %collective-permute-start.1 = (bf16[1024,128]{1,0:T(8,128)(2,1)}, bf16[1024,128]{1,0:T(8,128)(2,1)S(1)}, u32[]{:S(2)}, u32[]{:S(2)}) collective-permute-start(bf16[1024,128]{1,0:T(8,128)(2,1)} %get-tuple-element.111), channel_id=1, source_target_pairs={{0,2},{1,3},{2,0},{3,1},{4,6},{5,7},{6,4},{7,5},{8,10},{9,11},{10,... | collective-permute-start | bytes 786440 | tf_op jit(solution)/shard_map/ppermute | solution.py:65
  6.1 9.0 %collective-permute-start.3 = (bf16[768,128]{1,0:T(8,128)(2,1)S(1)}, bf16[768,128]{1,0:T(8,128)(2,1)S(1)}, u32[]{:S(2)}, u32[]{:S(2)}) collective-permute-start(bf16[768,128]{1,0:T(8,128)(2,1)S(1)} %slice.106), channel_id=1, source_target_pairs={{0,8},{1,9},{4,12},{5,13},{10,2},{11,3},{14,6},{15,7},{16,24},{17,... | collective-permute-start | bytes 589832 | tf_op jit(solution)/shard_map/ppermute | solution.py:74
  15.2 17.0 %collective-permute-start.4 = (bf16[1024,256]{1,0:T(8,128)(2,1)S(1)}, bf16[1024,256]{1,0:T(8,128)(2,1)S(1)}, u32[]{:S(2)}, u32[]{:S(2)}) collective-permute-start(bf16[1024,256]{1,0:T(8,128)(2,1)S(1)} %pad_maximum_fusion.3), channel_id=1, source_target_pairs={{0,2},{1,3},{2,0},{3,1},{4,6},{5,7},{6,4},{7,5},{8,10},{9,11},{10,... | collective-permute-start | bytes 1572872 | tf_op jit(solution)/shard_map/ppermute | solution.py:65
  20.6 14.2 %collective-permute-start.2 = (bf16[1024,128]{1,0:T(8,128)(2,1)S(1)}, bf16[1024,128]{1,0:T(8,128)(2,1)S(1)}, u32[]{:S(2)}, u32[]{:S(2)}) collective-permute-start(bf16[1024,128]{1,0:T(8,128)(2,1)S(1)} %broadcast_select_fusion.18), channel_id=1, source_target_pairs={{0,8},{1,9},{2,10},{3,11},{4,12},{5,13},{6,14},{7,15},{8,0},{9,1},... | collective-permute-start | bytes 786440 | tf_op jit(solution)/shard_map/ppermute | solution.py:77
  20.7 14.1 %collective-permute-start.5 = (bf16[768,128]{1,0:T(8,128)(2,1)S(1)}, bf16[768,128]{1,0:T(8,128)(2,1)S(1)}, u32[]{:S(2)}, u32[]{:S(2)}) collective-permute-start(bf16[768,128]{1,0:T(8,128)(2,1)S(1)} %broadcast_select_fusion.20), channel_id=1, source_target_pairs={{0,4},{1,5},{2,6},{3,7},{4,0},{5,1},{6,2},{7,3},{8,12},{9,13},{10,... | collective-permute-start | bytes 589832 | tf_op jit(solution)/shard_map/ppermute | solution.py:68
  34.8 12.3 %collective-permute-start.6 = (bf16[1024,128]{1,0:T(8,128)(2,1)S(1)}, bf16[1024,128]{1,0:T(8,128)(2,1)S(1)}, u32[]{:S(2)}, u32[]{:S(2)}) collective-permute-start(bf16[1024,128]{1,0:T(8,128)(2,1)S(1)} %broadcast_select_fusion.15), channel_id=1, source_target_pairs={{0,4},{1,5},{2,6},{3,7},{4,0},{5,1},{6,2},{7,3},{8,12},{9,13},{10,... | collective-permute-start | bytes 786440 | tf_op jit(solution)/shard_map/ppermute | solution.py:68
  35.0 16.1 %collective-permute-start.7 = (bf16[1024,128]{1,0:T(8,128)(2,1)S(1)}, bf16[1024,128]{1,0:T(8,128)(2,1)S(1)}, u32[]{:S(2)}, u32[]{:S(2)}) collective-permute-start(bf16[1024,128]{1,0:T(8,128)(2,1)S(1)} %get-tuple-element.130), channel_id=1, source_target_pairs={{0,8},{1,9},{2,10},{3,11},{4,12},{5,13},{6,14},{7,15},{8,0},{9,1},... | collective-permute-start | bytes 786440 | tf_op jit(solution)/shard_map/ppermute | solution.py:77
  38.5 12.5 %collective-permute-start.8 = (bf16[1024,256]{1,0:T(8,128)(2,1)S(1)}, bf16[1024,256]{1,0:T(8,128)(2,1)S(1)}, u32[]{:S(2)}, u32[]{:S(2)}) collective-permute-start(bf16[1024,256]{1,0:T(8,128)(2,1)S(1)} %pad_maximum_fusion.4), channel_id=1, source_target_pairs={{0,2},{1,3},{2,0},{3,1},{4,6},{5,7},{6,4},{7,5},{8,10},{9,11},{10,... | collective-permute-start | bytes 1572872 | tf_op jit(solution)/shard_map/ppermute | solution.py:65
  48.6 3.7 %copy-start = (bf16[1024,512]{1,0:T(8,128)(2,1)S(1)}, bf16[1024,512]{1,0:T(8,128)(2,1)}, u32[]{:S(2)}) copy-start(bf16[1024,512]{1,0:T(8,128)(2,1)} %param.5) | copy-start | bytes 3145732
  51.1 7.2 %collective-permute-start.11 = (bf16[1024,128]{1,0:T(8,128)(2,1)S(1)}, bf16[1024,128]{1,0:T(8,128)(2,1)S(1)}, u32[]{:S(2)}, u32[]{:S(2)}) collective-permute-start(bf16[1024,128]{1,0:T(8,128)(2,1)S(1)} %broadcast_select_fusion.12), channel_id=1, source_target_pairs={{0,2},{1,3},{2,0},{3,1},{4,6},{5,7},{6,4},{7,5},{8,10},{9,11},{10,... | collective-permute-start | bytes 786440 | tf_op jit(solution)/shard_map/ppermute | solution.py:65
  51.9 10.3 %collective-permute-start.9 = (bf16[1024,128]{1,0:T(8,128)(2,1)S(1)}, bf16[1024,128]{1,0:T(8,128)(2,1)S(1)}, u32[]{:S(2)}, u32[]{:S(2)}) collective-permute-start(bf16[1024,128]{1,0:T(8,128)(2,1)S(1)} %broadcast_select_fusion.13), channel_id=1, source_target_pairs={{0,4},{1,5},{2,6},{3,7},{4,0},{5,1},{6,2},{7,3},{8,12},{9,13},{10,... | collective-permute-start | bytes 786440 | tf_op jit(solution)/shard_map/ppermute | solution.py:68
  52.3 12.2 %collective-permute-start.10 = (bf16[1024,128]{1,0:T(8,128)(2,1)S(1)}, bf16[1024,128]{1,0:T(8,128)(2,1)S(1)}, u32[]{:S(2)}, u32[]{:S(2)}) collective-permute-start(bf16[1024,128]{1,0:T(8,128)(2,1)S(1)} %get-tuple-element.127), channel_id=1, source_target_pairs={{0,8},{1,9},{2,10},{3,11},{4,12},{5,13},{6,14},{7,15},{8,0},{9,1},... | collective-permute-start | bytes 786440 | tf_op jit(solution)/shard_map/ppermute | solution.py:77
  58.4 12.5 %collective-permute-start.14 = (f32[1024,128]{1,0:T(8,128)S(1)}, f32[1024,128]{1,0:T(8,128)S(1)}, u32[]{:S(2)}, u32[]{:S(2)}) collective-permute-start(f32[1024,128]{1,0:T(8,128)S(1)} %convolution_add_fusion.5), channel_id=1, source_target_pairs={{0,2},{1,3},{2,0},{3,1},{4,6},{5,7},{6,4},{7,5},{8,10},{9,11},{10,... | collective-permute-start | bytes 1572872 | tf_op jit(solution)/shard_map/ppermute | solution.py:65
  64.7 16.8 %collective-permute-start.12 = (bf16[1024,256]{1,0:T(8,128)(2,1)S(1)}, bf16[1024,256]{1,0:T(8,128)(2,1)S(1)}, u32[]{:S(2)}, u32[]{:S(2)}) collective-permute-start(bf16[1024,256]{1,0:T(8,128)(2,1)S(1)} %maximum_select_fusion), channel_id=1, source_target_pairs={{0,4},{1,5},{2,6},{3,7},{4,0},{5,1},{6,2},{7,3},{8,12},{9,13},{10,... | collective-permute-start | bytes 1572872 | tf_op jit(solution)/shard_map/ppermute | solution.py:68
  65.5 17.5 %collective-permute-start.13 = (bf16[1024,128]{1,0:T(8,128)(2,1)S(1)}, bf16[1024,128]{1,0:T(8,128)(2,1)S(1)}, u32[]{:S(2)}, u32[]{:S(2)}) collective-permute-start(bf16[1024,128]{1,0:T(8,128)(2,1)S(1)} %broadcast_select_fusion.11), channel_id=1, source_target_pairs={{0,8},{1,9},{2,10},{3,11},{4,12},{5,13},{6,14},{7,15},{8,0},{9,1},... | collective-permute-start | bytes 786440 | tf_op jit(solution)/shard_map/ppermute | solution.py:77
  67.9 30.5 %collective-permute-start.18 = (bf16[1280,128]{1,0:T(8,128)(2,1)S(1)}, bf16[1280,128]{1,0:T(8,128)(2,1)S(1)}, u32[]{:S(2)}, u32[]{:S(2)}) collective-permute-start(bf16[1280,128]{1,0:T(8,128)(2,1)S(1)} %pad_maximum_fusion.7), channel_id=1, source_target_pairs={{0,8},{1,9},{4,12},{5,13},{10,2},{11,3},{14,6},{15,7},{16,24},{17,... | collective-permute-start | bytes 983048 | tf_op jit(solution)/shard_map/ppermute | solution.py:74
  70.8 13.4 %collective-permute-start.16 = (f32[1024,128]{1,0:T(8,128)S(1)}, f32[1024,128]{1,0:T(8,128)S(1)}, u32[]{:S(2)}, u32[]{:S(2)}) collective-permute-start(f32[1024,128]{1,0:T(8,128)S(1)} %convolution_add_fusion.4), channel_id=1, source_target_pairs={{0,2},{1,3},{2,0},{3,1},{4,6},{5,7},{6,4},{7,5},{8,10},{9,11},{10,... | collective-permute-start | bytes 1572872 | tf_op jit(solution)/shard_map/ppermute | solution.py:65
  83.2 14.4 %collective-permute-start.15 = (bf16[1024,256]{1,0:T(8,128)(2,1)S(1)}, bf16[1024,256]{1,0:T(8,128)(2,1)S(1)}, u32[]{:S(2)}, u32[]{:S(2)}) collective-permute-start(bf16[1024,256]{1,0:T(8,128)(2,1)S(1)} %maximum_select_fusion.1), channel_id=1, source_target_pairs={{0,4},{1,5},{2,6},{3,7},{4,0},{5,1},{6,2},{7,3},{8,12},{9,13},{10,... | collective-permute-start | bytes 1572872 | tf_op jit(solution)/shard_map/ppermute | solution.py:68
  83.4 19.5 %collective-permute-start.21 = (bf16[1024,512]{1,0:T(8,128)(2,1)S(1)}, bf16[1024,512]{1,0:T(8,128)(2,1)S(1)}, u32[]{:S(2)}, u32[]{:S(2)}) collective-permute-start(bf16[1024,512]{1,0:T(8,128)(2,1)S(1)} %pad_maximum_fusion.2), channel_id=1, source_target_pairs={{0,1},{1,0},{2,3},{3,2},{4,5},{5,4},{6,7},{7,6},{8,9},{9,8},{10,11... | collective-permute-start | bytes 3145736 | tf_op jit(solution)/shard_map/ppermute | solution.py:71
  83.5 18.3 %collective-permute-start.23 = (bf16[1024,512]{1,0:T(8,128)(2,1)S(1)}, bf16[1024,512]{1,0:T(8,128)(2,1)S(1)}, u32[]{:S(2)}, u32[]{:S(2)}) collective-permute-start(bf16[1024,512]{1,0:T(8,128)(2,1)S(1)} %copy-done), channel_id=1, source_target_pairs={{0,1},{1,0},{2,3},{3,2},{4,5},{5,4},{6,7},{7,6},{8,9},{9,8},{10,11... | collective-permute-start | bytes 3145736 | tf_op jit(solution)/shard_map/ppermute | solution.py:71
  84.2 17.6 %collective-permute-start.17 = (f32[1024,128]{1,0:T(8,128)S(1)}, f32[1024,128]{1,0:T(8,128)S(1)}, u32[]{:S(2)}, u32[]{:S(2)}) collective-permute-start(f32[1024,128]{1,0:T(8,128)S(1)} %convolution_add_fusion.3), channel_id=1, source_target_pairs={{0,2},{1,3},{2,0},{3,1},{4,6},{5,7},{6,4},{7,5},{8,10},{9,11},{10,... | collective-permute-start | bytes 1572872 | tf_op jit(solution)/shard_map/ppermute | solution.py:65
  99.2 12.5 %collective-permute-start.19 = (bf16[1280,128]{1,0:T(8,128)(2,1)S(1)}, bf16[1280,128]{1,0:T(8,128)(2,1)S(1)}, u32[]{:S(2)}, u32[]{:S(2)}) collective-permute-start(bf16[1280,128]{1,0:T(8,128)(2,1)S(1)} %broadcast_select_fusion.8), channel_id=1, source_target_pairs={{0,4},{1,5},{2,6},{3,7},{4,0},{5,1},{6,2},{7,3},{8,12},{9,13},{10,... | collective-permute-start | bytes 983048 | tf_op jit(solution)/shard_map/ppermute | solution.py:68
  102.8 6.5 %collective-permute-start.20 = (bf16[1024,512]{1,0:T(8,128)(2,1)S(1)}, bf16[1024,512]{1,0:T(8,128)(2,1)S(1)}, u32[]{:S(2)}, u32[]{:S(2)}) collective-permute-start(bf16[1024,512]{1,0:T(8,128)(2,1)S(1)} %get-tuple-element.101), channel_id=1, source_target_pairs={{0,1},{1,0},{2,3},{3,2},{4,5},{5,4},{6,7},{7,6},{8,9},{9,8},{10,11... | collective-permute-start | bytes 3145736 | tf_op jit(solution)/shard_map/ppermute | solution.py:71
  103.3 4.7 %collective-permute-start.22 = (bf16[1024,256]{1,0:T(8,128)(2,1)S(1)}, bf16[1024,256]{1,0:T(8,128)(2,1)S(1)}, u32[]{:S(2)}, u32[]{:S(2)}) collective-permute-start(bf16[1024,256]{1,0:T(8,128)(2,1)S(1)} %get-tuple-element.109), channel_id=1, source_target_pairs={{0,1},{1,0},{2,3},{3,2},{4,5},{5,4},{6,7},{7,6},{8,9},{9,8},{10,11... | collective-permute-start | bytes 1572872 | tf_op jit(solution)/shard_map/ppermute | solution.py:71
  103.9 14.8 %collective-permute-start.24 = (f32[1024,128]{1,0:T(8,128)S(1)}, f32[1024,128]{1,0:T(8,128)S(1)}, u32[]{:S(2)}, u32[]{:S(2)}) collective-permute-start(f32[1024,128]{1,0:T(8,128)S(1)} %convolution_add_fusion.2), channel_id=1, source_target_pairs={{0,2},{1,3},{2,0},{3,1},{4,6},{5,7},{6,4},{7,5},{8,10},{9,11},{10,... | collective-permute-start | bytes 1572872 | tf_op jit(solution)/shard_map/ppermute | solution.py:65
  112.0 2.0 %collective-permute-start.25 = (bf16[1024,256]{1,0:T(8,128)(2,1)S(1)}, bf16[1024,256]{1,0:T(8,128)(2,1)S(1)}, u32[]{:S(2)}, u32[]{:S(2)}) collective-permute-start(bf16[1024,256]{1,0:T(8,128)(2,1)S(1)} %get-tuple-element.107), channel_id=1, source_target_pairs={{0,1},{1,0},{2,3},{3,2},{4,5},{5,4},{6,7},{7,6},{8,9},{9,8},{10,11... | collective-permute-start | bytes 1572872 | tf_op jit(solution)/shard_map/ppermute | solution.py:71

commit v22 on v18

--- a/solution.py
+++ b/solution.py
@@ -96,14 +96,14 @@
         rows = e[3].shape[0] // 2
         j0 = home_jump(e[3][:rows])
         t_other = swap(transition)
-        e2 = after(e[2], x1)
+        e2 = after(e[2], x1, j0)
         j1 = jump(jnp.where(home, x1, e2))
         t_near, t_next = jnp.where(mine, transition, t_other), jnp.where(mine, t_other, transition)
 
         def adjoint_of(near, far):
             return tdot(t_near, near) + tdot(t_next, far)
 
-        v1, e1 = together((v[1], e[1]), x1, t_near, j0)
+        v1, e1 = together((v[1], e[1]), x1, t_near)
         x2 = cross(jnp.concatenate([jnp.where(home, v1, e1), v[2]], 1))
         x2, v_across2 = columns(x2, 0, 1), columns(x2, 1, 2)
         near, far = together((e[3][:rows], j0), x1)

time: 120 us -> 120 us (level)
  starting transfers between devices: 38.9 us -> 41.9 us
  waiting for transfers between devices: 52.8 us -> 50 us
    ppermute x4, starting transfers between devices: 6.45 us -> 9.65 us  [jump(): return lax.ppermute(a, AXES, jump_pairs)]
    ppermute x8, waiting for transfers between devices: 16.3 us -> 14.4 us  [cross(): return lax.ppermute(a, AXES, cross_pairs)]
  transfers between devices with their start and end apart: 26 -> 26, of which waited for: 12 -> 11; matrix products, arithmetic and copies ran while one was open for 20% -> 20% of each run, Pallas kernels for 0% -> 0%
where the time goes in v22:
time: 120 us; the launch traced here: 119 us
  waiting for transfers between devices  50 us (42%)
  starting transfers between devices  41.9 us (35%)
  matrix products  16 us (13%)
  other arithmetic  8.9 us (7%)
  between operations  1.83 us (2%)
    ppermute x6, waiting for transfers between devices, step(): return lax.ppermute(a, AXES, step_pairs)  31.8 us
    ppermute x8, starting transfers between devices, cross(): return lax.ppermute(a, AXES, cross_pairs)  15.3 us
    ppermute x8, waiting for transfers between devices, cross(): return lax.ppermute(a, AXES, cross_pairs)  14.4 us
    ppermute x4, starting transfers between devices, jump(): return lax.ppermute(a, AXES, jump_pairs)  9.65 us
    dot_general x12, matrix products, tdot(): lax.dot_general(a, b, (((0,), (0,)), ((), ())), preferred_element_type=jn...  9.04 us
    ppermute x2, starting transfers between devices, home_jump(): return lax.ppermute(a, AXES, home_jump_pairs)  7.59 us
    ppermute x6, starting transfers between devices, step(): return lax.ppermute(a, AXES, step_pairs)  7.56 us
    dot_general x3, matrix products, dott(): lax.dot_general(a, b, (((1,), (1,)), ((), ())), preferred_element_type=jn...  6.98 us
  transfers between devices with their start and end apart: 26, of which 11 were waited for; matrix products, arithmetic and copies ran while one was open for 20% of the time, Pallas kernels for 0%

profile of v22, /device:TPU:0, one launch (start us, length us, event | category | flops | bytes accessed | tf_op | source)
XLA Modules:
  0.0 119.4 jit_solution(15708735092964367578)
XLA Ops:
  0.6 0.5 collective-permute-start
  1.2 2.3 %fusion.36 = (bf16[1024,128]{1,0:T(8,128)(2,1)S(1)}, bf16[1024,128]{1,0:T(8,128)(2,1)}, bf16[1024,128]{1,0:T(8,128)(2,1)S(1)}, bf16[1024,128]{1,0:T(8,128)(2,1)S...) fusion(bf16[1024,512]{1,0:T(8,128)(2,1)} %param.4, ...), kind=kLoop, calls=%fused_computation.81 | loop fusion | flops 131072 | bytes 3932161 | tf_op jit(solution)/shard_map/slice | solution.py:88
  3.5 2.6 %collective-permute-start.1 = (bf16[1024,128]{1,0:T(8,128)(2,1)}, bf16[1024,128]{1,0:T(8,128)(2,1)S(1)}, u32[]{:S(2)}, u32[]{:S(2)}) collective-permute-start(bf16[1024,128]{1,0:T(8,128)(2,1)} %get-tuple-element.111), channel_id=1, source_target_pairs={{0,2},{1,3},{2,0},{3,1},{4,6},{5,7},{6,4},{7,5},{8,10},{9,11},{10,... | collective-permute-start | bytes 786440 | tf_op jit(solution)/shard_map/ppermute | solution.py:65
  6.1 4.5 %collective-permute-start.2 = (bf16[512,128]{1,0:T(8,128)(2,1)S(1)}, bf16[512,128]{1,0:T(8,128)(2,1)S(1)}, u32[]{:S(2)}, u32[]{:S(2)}) collective-permute-start(bf16[512,128]{1,0:T(8,128)(2,1)S(1)} %get-tuple-element.53), channel_id=1, source_target_pairs={{0,8},{1,9},{4,12},{5,13},{10,2},{11,3},{14,6},{15,7},{16,24},{17,... | collective-permute-start | bytes 393224 | tf_op jit(solution)/shard_map/ppermute | solution.py:74
  10.6 2.5 %broadcast_select_fusion.1 = (bf16[1024,1024]{1,0:T(8,128)(2,1)S(1)}, bf16[1024,1024]{1,0:T(8,128)(2,1)S(1)}) fusion(bf16[1024,1024]{1,0:T(8,128)(2,1)} %param.6, bf16[1024,1024]{1,0:T(8,128)(2,1)} %collective-permute-done, pred[]{:T(512)S(6)} %eq.8), kind=kLoop, calls=%fused_computation.8 | loop fusion | flops 2097152 | bytes 8388609 | tf_op jit(solution)/shard_map/jit(_where)/select_n | solution.py:101
  13.3 1.8 %collective-permute-start.4 = (bf16[1024,256]{1,0:T(8,128)(2,1)S(1)}, bf16[1024,256]{1,0:T(8,128)(2,1)S(1)}, u32[]{:S(2)}, u32[]{:S(2)}) collective-permute-start(bf16[1024,256]{1,0:T(8,128)(2,1)S(1)} %pad_maximum_fusion.3), channel_id=1, source_target_pairs={{0,2},{1,3},{2,0},{3,1},{4,6},{5,7},{6,4},{7,5},{8,10},{9,11},{10,... | collective-permute-start | bytes 1572872 | tf_op jit(solution)/shard_map/ppermute | solution.py:65
  15.1 2.7 %collective-permute-start.3 = (bf16[1024,128]{1,0:T(8,128)(2,1)S(1)}, bf16[1024,128]{1,0:T(8,128)(2,1)S(1)}, u32[]{:S(2)}, u32[]{:S(2)}) collective-permute-start(bf16[1024,128]{1,0:T(8,128)(2,1)S(1)} %broadcast_select_fusion.18), channel_id=1, source_target_pairs={{0,8},{1,9},{2,10},{3,11},{4,12},{5,13},{6,14},{7,15},{8,0},{9,1},... | collective-permute-start | bytes 786440 | tf_op jit(solution)/shard_map/ppermute | solution.py:77
  17.8 3.7 %collective-permute-start.5 = (bf16[512,128]{1,0:T(8,128)(2,1)S(1)}, bf16[512,128]{1,0:T(8,128)(2,1)S(1)}, u32[]{:S(2)}, u32[]{:S(2)}) collective-permute-start(bf16[512,128]{1,0:T(8,128)(2,1)S(1)} %broadcast_select_fusion.20), channel_id=1, source_target_pairs={{0,4},{1,5},{2,6},{3,7},{4,0},{5,1},{6,2},{7,3},{8,12},{9,13},{10,... | collective-permute-start | bytes 393224 | tf_op jit(solution)/shard_map/ppermute | solution.py:68
  21.5 5.5 %collective-permute-done.4 = bf16[1024,256]{1,0:T(8,128)(2,1)S(1)} collective-permute-done((bf16[1024,256]{1,0:T(8,128)(2,1)S(1)}, bf16[1024,256]{1,0:T(8,128)(2,1)S(1)}, u32[]{:S(2)}, u32[]{:S(2)}) %collective-permute-start.4) | collective-permute-done | bytes 524320 | tf_op jit(solution)/shard_map/ppermute | solution.py:65
  27.1 2.2 %collective-permute-done.3 = bf16[1024,128]{1,0:T(8,128)(2,1)S(1)} collective-permute-done((bf16[1024,128]{1,0:T(8,128)(2,1)S(1)}, bf16[1024,128]{1,0:T(8,128)(2,1)S(1)}, u32[]{:S(2)}, u32[]{:S(2)}) %collective-permute-start.3) | collective-permute-done | bytes 262176 | tf_op jit(solution)/shard_map/ppermute | solution.py:77
  29.4 0.7 collective-permute-start.6
  30.1 3.4 %collective-permute-start.7 = (bf16[1024,128]{1,0:T(8,128)(2,1)S(1)}, bf16[1024,128]{1,0:T(8,128)(2,1)S(1)}, u32[]{:S(2)}, u32[]{:S(2)}) collective-permute-start(bf16[1024,128]{1,0:T(8,128)(2,1)S(1)} %get-tuple-element.132), channel_id=1, source_target_pairs={{0,8},{1,9},{2,10},{3,11},{4,12},{5,13},{6,14},{7,15},{8,0},{9,1},... | collective-permute-start | bytes 786440 | tf_op jit(solution)/shard_map/ppermute | solution.py:77
  33.5 0.6 collective-permute-start.8
  34.1 7.8 %collective-permute-done.6 = bf16[1024,128]{1,0:T(8,128)(2,1)S(1)} collective-permute-done((bf16[1024,128]{1,0:T(8,128)(2,1)S(1)}, bf16[1024,128]{1,0:T(8,128)(2,1)S(1)}, u32[]{:S(2)}, u32[]{:S(2)}) %collective-permute-start.6) | collective-permute-done | bytes 262176 | tf_op jit(solution)/shard_map/ppermute | solution.py:68
  42.0 0.7 fusion.44
  42.7 0.8 convolution_add_fusion.5
  43.5 3.4 %collective-permute-done.8 = bf16[1024,256]{1,0:T(8,128)(2,1)S(1)} collective-permute-done((bf16[1024,256]{1,0:T(8,128)(2,1)S(1)}, bf16[1024,256]{1,0:T(8,128)(2,1)S(1)}, u32[]{:S(2)}, u32[]{:S(2)}) %collective-permute-start.8) | collective-permute-done | bytes 524320 | tf_op jit(solution)/shard_map/ppermute | solution.py:65
  47.0 0.6 collective-permute-start.11
  47.6 0.4 collective-permute-start.9
  48.1 1.6 %collective-permute-start.10 = (bf16[1024,128]{1,0:T(8,128)(2,1)S(1)}, bf16[1024,128]{1,0:T(8,128)(2,1)S(1)}, u32[]{:S(2)}, u32[]{:S(2)}) collective-permute-start(bf16[1024,128]{1,0:T(8,128)(2,1)S(1)} %get-tuple-element.129), channel_id=1, source_target_pairs={{0,8},{1,9},{2,10},{3,11},{4,12},{5,13},{6,14},{7,15},{8,0},{9,1},... | collective-permute-start | bytes 786440 | tf_op jit(solution)/shard_map/ppermute | solution.py:77
  49.7 4.1 %collective-permute-done.11 = bf16[1024,128]{1,0:T(8,128)(2,1)S(1)} collective-permute-done((bf16[1024,128]{1,0:T(8,128)(2,1)S(1)}, bf16[1024,128]{1,0:T(8,128)(2,1)S(1)}, u32[]{:S(2)}, u32[]{:S(2)}) %collective-permute-start.11) | collective-permute-done | bytes 262176 | tf_op jit(solution)/shard_map/ppermute | solution.py:65
  53.8 0.5 collective-permute-start.14
  54.3 4.1 %collective-permute-done.9 = bf16[1024,128]{1,0:T(8,128)(2,1)S(1)} collective-permute-done((bf16[1024,128]{1,0:T(8,128)(2,1)S(1)}, bf16[1024,128]{1,0:T(8,128)(2,1)S(1)}, u32[]{:S(2)}, u32[]{:S(2)}) %collective-permute-start.9) | collective-permute-done | bytes 262176 | tf_op jit(solution)/shard_map/ppermute | solution.py:68
  58.4 0.7 fusion.45
  59.2 0.8 convolution_add_fusion.4
  60.0 1.3 %collective-permute-done.10 = bf16[1024,128]{1,0:T(8,128)(2,1)S(1)} collective-permute-done((bf16[1024,128]{1,0:T(8,128)(2,1)S(1)}, bf16[1024,128]{1,0:T(8,128)(2,1)S(1)}, u32[]{:S(2)}, u32[]{:S(2)}) %collective-permute-start.10) | collective-permute-done | bytes 262176 | tf_op jit(solution)/shard_map/ppermute | solution.py:77
  61.2 0.2 maximum_select_fusion
  61.4 0.1 collective-permute-start.12
  62.2 2.0 %collective-permute-start.13 = (bf16[1024,128]{1,0:T(8,128)(2,1)S(1)}, bf16[1024,128]{1,0:T(8,128)(2,1)S(1)}, u32[]{:S(2)}, u32[]{:S(2)}) collective-permute-start(bf16[1024,128]{1,0:T(8,128)(2,1)S(1)} %broadcast_select_fusion.11), channel_id=1, source_target_pairs={{0,8},{1,9},{2,10},{3,11},{4,12},{5,13},{6,14},{7,15},{8,0},{9,1},... | collective-permute-start | bytes 786440 | tf_op jit(solution)/shard_map/ppermute | solution.py:77
  64.2 3.1 %collective-permute-start.18 = (bf16[1536,128]{1,0:T(8,128)(2,1)S(1)}, bf16[1536,128]{1,0:T(8,128)(2,1)S(1)}, u32[]{:S(2)}, u32[]{:S(2)}) collective-permute-start(bf16[1536,128]{1,0:T(8,128)(2,1)S(1)} %pad_maximum_fusion.7), channel_id=1, source_target_pairs={{0,8},{1,9},{4,12},{5,13},{10,2},{11,3},{14,6},{15,7},{16,24},{17,... | collective-permute-start | bytes 1179656 | tf_op jit(solution)/shard_map/ppermute | solution.py:74
  67.3 0.1 constant_dynamic-update-slice_fusion.4
  67.4 0.1 constant_dynamic-update-slice_fusion.3
  67.6 0.1 collective-permute-start.16
  67.6 10.6 %collective-permute-done.12 = bf16[1024,256]{1,0:T(8,128)(2,1)S(1)} collective-permute-done((bf16[1024,256]{1,0:T(8,128)(2,1)S(1)}, bf16[1024,256]{1,0:T(8,128)(2,1)S(1)}, u32[]{:S(2)}, u32[]{:S(2)}) %collective-permute-start.12) | collective-permute-done | bytes 524320 | tf_op jit(solution)/shard_map/ppermute | solution.py:68
  78.2 0.8 fusion.21
  79.0 0.8 convolution_add_fusion.3
  79.8 0.2 maximum_select_fusion.1
  80.0 0.1 pad_maximum_fusion.2
  80.2 0.5 collective-permute-start.23
  80.7 0.1 constant_dynamic-update-slice_fusion.2
  80.8 0.1 constant_dynamic-update-slice_fusion.1
  81.0 5.5 %collective-permute-start.17 = (f32[1024,128]{1,0:T(8,128)S(1)}, f32[1024,128]{1,0:T(8,128)S(1)}, u32[]{:S(2)}, u32[]{:S(2)}) collective-permute-start(f32[1024,128]{1,0:T(8,128)S(1)} %convolution_add_fusion.3), channel_id=1, source_target_pairs={{0,2},{1,3},{2,0},{3,1},{4,6},{5,7},{6,4},{7,5},{8,10},{9,11},{10,... | collective-permute-start | bytes 1572872 | tf_op jit(solution)/shard_map/ppermute | solution.py:65
  86.4 9.3 %collective-permute-done.15 = bf16[1024,256]{1,0:T(8,128)(2,1)S(1)} collective-permute-done((bf16[1024,256]{1,0:T(8,128)(2,1)S(1)}, bf16[1024,256]{1,0:T(8,128)(2,1)S(1)}, u32[]{:S(2)}, u32[]{:S(2)}) %collective-permute-start.15) | collective-permute-done | bytes 524320 | tf_op jit(solution)/shard_map/ppermute | solution.py:68
  95.7 0.8 fusion.30
  96.5 0.8 convolution_add_fusion.2
  97.3 2.6 %collective-permute-start.19 = (bf16[1536,128]{1,0:T(8,128)(2,1)S(1)}, bf16[1536,128]{1,0:T(8,128)(2,1)S(1)}, u32[]{:S(2)}, u32[]{:S(2)}) collective-permute-start(bf16[1536,128]{1,0:T(8,128)(2,1)S(1)} %broadcast_select_fusion.8), channel_id=1, source_target_pairs={{0,4},{1,5},{2,6},{3,7},{4,0},{5,1},{6,2},{7,3},{8,12},{9,13},{10,... | collective-permute-start | bytes 1179656 | tf_op jit(solution)/shard_map/ppermute | solution.py:68
  100.0 0.2 fusion.38
  100.2 0.8 broadcast_select_fusion.3
  101.1 0.1 constant_dynamic-update-slice_fusion
  101.2 0.2 broadcast_select_fusion.7
  101.5 0.6 collective-permute-start.22
  102.0 3.6 %collective-permute-start.24 = (f32[1024,128]{1,0:T(8,128)S(1)}, f32[1024,128]{1,0:T(8,128)S(1)}, u32[]{:S(2)}, u32[]{:S(2)}) collective-permute-start(f32[1024,128]{1,0:T(8,128)S(1)} %convolution_add_fusion.2), channel_id=1, source_target_pairs={{0,2},{1,3},{2,0},{3,1},{4,6},{5,7},{6,4},{7,5},{8,10},{9,11},{10,... | collective-permute-start | bytes 1572872 | tf_op jit(solution)/shard_map/ppermute | solution.py:65
  105.6 0.7 fusion.24
  106.4 0.7 convolution_add_fusion.1
  107.1 1.3 %fusion.8 = f32[1024,1024]{1,0:T(8,128)S(1)} fusion(bf16[1024,256]{1,0:T(8,128)(2,1)S(1)} %collective-permute-done.22, bf16[1024,256]{1,0:T(8,128)(2,1)S(1)} %get-tuple-element.108, bf16[1024,256]{1,0:T(8,128)(2,1)S(1)} %get-tuple-element.105, bf16[1024,256]{1,0:T(8,128)(2,1)S(1)} %get-tuple-element.103), kind=kOutput, calls=%fused_computation.19 | convolution fusion | flops 1077936128 | bytes 6291456 | tf_op jit(solution)/shard_map/dot_general | solution.py:38
  108.4 2.4 %fusion.5 = f32[1024,1024]{1,0:T(8,128)S(1)} fusion(f32[1024,1024]{1,0:T(8,128)S(1)} %fusion.8, bf16[1024,1024]{1,0:T(8,128)(2,1)S(1)} %constant_dynamic-update-slice_fusion, bf16[1024,512]{1,0:T(8,128)(2,1)S(1)} %collective-permute-done.20, bf16[1024,512]{1,0:T(8,128)(2,1)S(1)} %get-tuple-element.100), kind=kOutput, calls=%fused_computation.9 | convolution fusion | flops 2152726528 | bytes 12582912 | tf_op jit(solution)/shard_map/dot_general | solution.py:38
  110.9 0.2 broadcast_select_fusion.5
  111.2 0.1 collective-permute-start.25
  111.2 0.7 fusion.33
  112.0 0.8 convolution_add_fusion
  112.8 0.4 collective-permute-done.25
  113.1 3.3 %add_multiply_fusion = f32[1024,1024]{1,0:T(8,128)} fusion(f32[1024,1024]{1,0:T(8,128)S(1)} %fusion.5, f32[]{:T(128)} %bitcast, bf16[1024,256]{1,0:T(8,128)(2,1)S(1)} %collective-permute-done.25, bf16[1024,256]{1,0:T(8,128)(2,1)S(1)} %get-tuple-element.106, bf16[1024,256]{1,0:T(8,128)(2,1)S(1)} %get-tuple-element.104, bf16[1024,256]{1,0:T(8,128)(2,1)S(1)} %get-tuple-element.102), kind=kOutput, calls=%fused_computation | convolution fusion | flops 1080033280 | bytes 10485764 | tf_op jit(solution)/shard_map/dot_general | solution.py:38
  116.5 1.3 %collective-permute-done.24 = f32[1024,128]{1,0:T(8,128)S(1)} collective-permute-done((f32[1024,128]{1,0:T(8,128)S(1)}, f32[1024,128]{1,0:T(8,128)S(1)}, u32[]{:S(2)}, u32[]{:S(2)}) %collective-permute-start.24) | collective-permute-done | bytes 524320 | tf_op jit(solution)/shard_map/ppermute | solution.py:65
  117.8 1.6 %fusion.4 = f32[1024,512]{1,0:T(8,128)} fusion(f32[1024,256]{1,0:T(8,128)S(1)} %convolution_add_fusion, f32[1024,256]{1,0:T(8,128)S(1)} %convolution_add_fusion.1, f32[1024,128]{1,0:T(8,128)S(1)} %collective-permute-done.24, f32[1024,128]{1,0:T(8,128)S(1)} %collective-permute-done.17, f32[1024,128]{1,0:T(8,128)S(1)} %collective-permute-done.16, ...), kind=kLoop, calls=%fused_computation.6 | loop fusion | flops 3145728 | bytes 6291460 | tf_op jit(solution)/shard_map/mul | solution.py:191
  (45 shorter events, 1.1 us)
Async XLA Ops:
  0.6 5.4 %copy-start.1 = (bf16[1024,512]{1,0:T(8,128)(2,1)S(1)}, bf16[1024,512]{1,0:T(8,128)(2,1)}, u32[]{:S(2)}) copy-start(bf16[1024,512]{1,0:T(8,128)(2,1)} %param.4) | copy-start | bytes 3145732
  0.6 10.0 %collective-permute-start = (bf16[1024,1024]{1,0:T(8,128)(2,1)}, bf16[1024,1024]{1,0:T(8,128)(2,1)}, u32[]{:S(2)}, u32[]{:S(2)}) collective-permute-start(bf16[1024,1024]{1,0:T(8,128)(2,1)} %param.6), channel_id=1, source_target_pairs={{0,1},{1,0},{2,3},{3,2},{4,5},{5,4},{6,7},{7,6},{8,9},{9,8},{10,11... | collective-permute-start | bytes 6291464 | tf_op jit(solution)/shard_map/ppermute | solution.py:71
  3.5 9.7 %collective-permute-start.1 = (bf16[1024,128]{1,0:T(8,128)(2,1)}, bf16[1024,128]{1,0:T(8,128)(2,1)S(1)}, u32[]{:S(2)}, u32[]{:S(2)}) collective-permute-start(bf16[1024,128]{1,0:T(8,128)(2,1)} %get-tuple-element.111), channel_id=1, source_target_pairs={{0,2},{1,3},{2,0},{3,1},{4,6},{5,7},{6,4},{7,5},{8,10},{9,11},{10,... | collective-permute-start | bytes 786440 | tf_op jit(solution)/shard_map/ppermute | solution.py:65
  6.1 9.0 %collective-permute-start.2 = (bf16[512,128]{1,0:T(8,128)(2,1)S(1)}, bf16[512,128]{1,0:T(8,128)(2,1)S(1)}, u32[]{:S(2)}, u32[]{:S(2)}) collective-permute-start(bf16[512,128]{1,0:T(8,128)(2,1)S(1)} %get-tuple-element.53), channel_id=1, source_target_pairs={{0,8},{1,9},{4,12},{5,13},{10,2},{11,3},{14,6},{15,7},{16,24},{17,... | collective-permute-start | bytes 393224 | tf_op jit(solution)/shard_map/ppermute | solution.py:74
  13.3 13.8 %collective-permute-start.4 = (bf16[1024,256]{1,0:T(8,128)(2,1)S(1)}, bf16[1024,256]{1,0:T(8,128)(2,1)S(1)}, u32[]{:S(2)}, u32[]{:S(2)}) collective-permute-start(bf16[1024,256]{1,0:T(8,128)(2,1)S(1)} %pad_maximum_fusion.3), channel_id=1, source_target_pairs={{0,2},{1,3},{2,0},{3,1},{4,6},{5,7},{6,4},{7,5},{8,10},{9,11},{10,... | collective-permute-start | bytes 1572872 | tf_op jit(solution)/shard_map/ppermute | solution.py:65
  15.1 14.2 %collective-permute-start.3 = (bf16[1024,128]{1,0:T(8,128)(2,1)S(1)}, bf16[1024,128]{1,0:T(8,128)(2,1)S(1)}, u32[]{:S(2)}, u32[]{:S(2)}) collective-permute-start(bf16[1024,128]{1,0:T(8,128)(2,1)S(1)} %broadcast_select_fusion.18), channel_id=1, source_target_pairs={{0,8},{1,9},{2,10},{3,11},{4,12},{5,13},{6,14},{7,15},{8,0},{9,1},... | collective-permute-start | bytes 786440 | tf_op jit(solution)/shard_map/ppermute | solution.py:77
  17.8 11.5 %collective-permute-start.5 = (bf16[512,128]{1,0:T(8,128)(2,1)S(1)}, bf16[512,128]{1,0:T(8,128)(2,1)S(1)}, u32[]{:S(2)}, u32[]{:S(2)}) collective-permute-start(bf16[512,128]{1,0:T(8,128)(2,1)S(1)} %broadcast_select_fusion.20), channel_id=1, source_target_pairs={{0,4},{1,5},{2,6},{3,7},{4,0},{5,1},{6,2},{7,3},{8,12},{9,13},{10,... | collective-permute-start | bytes 393224 | tf_op jit(solution)/shard_map/ppermute | solution.py:68
  29.4 12.6 %collective-permute-start.6 = (bf16[1024,128]{1,0:T(8,128)(2,1)S(1)}, bf16[1024,128]{1,0:T(8,128)(2,1)S(1)}, u32[]{:S(2)}, u32[]{:S(2)}) collective-permute-start(bf16[1024,128]{1,0:T(8,128)(2,1)S(1)} %broadcast_select_fusion.15), channel_id=1, source_target_pairs={{0,4},{1,5},{2,6},{3,7},{4,0},{5,1},{6,2},{7,3},{8,12},{9,13},{10,... | collective-permute-start | bytes 786440 | tf_op jit(solution)/shard_map/ppermute | solution.py:68
  30.1 16.9 %collective-permute-start.7 = (bf16[1024,128]{1,0:T(8,128)(2,1)S(1)}, bf16[1024,128]{1,0:T(8,128)(2,1)S(1)}, u32[]{:S(2)}, u32[]{:S(2)}) collective-permute-start(bf16[1024,128]{1,0:T(8,128)(2,1)S(1)} %get-tuple-element.132), channel_id=1, source_target_pairs={{0,8},{1,9},{2,10},{3,11},{4,12},{5,13},{6,14},{7,15},{8,0},{9,1},... | collective-permute-start | bytes 786440 | tf_op jit(solution)/shard_map/ppermute | solution.py:77
  33.5 13.4 %collective-permute-start.8 = (bf16[1024,256]{1,0:T(8,128)(2,1)S(1)}, bf16[1024,256]{1,0:T(8,128)(2,1)S(1)}, u32[]{:S(2)}, u32[]{:S(2)}) collective-permute-start(bf16[1024,256]{1,0:T(8,128)(2,1)S(1)} %pad_maximum_fusion.4), channel_id=1, source_target_pairs={{0,2},{1,3},{2,0},{3,1},{4,6},{5,7},{6,4},{7,5},{8,10},{9,11},{10,... | collective-permute-start | bytes 1572872 | tf_op jit(solution)/shard_map/ppermute | solution.py:65
  43.5 4.6 %copy-start = (bf16[1024,512]{1,0:T(8,128)(2,1)S(1)}, bf16[1024,512]{1,0:T(8,128)(2,1)}, u32[]{:S(2)}) copy-start(bf16[1024,512]{1,0:T(8,128)(2,1)} %param.5) | copy-start | bytes 3145732
  47.0 6.8 %collective-permute-start.11 = (bf16[1024,128]{1,0:T(8,128)(2,1)S(1)}, bf16[1024,128]{1,0:T(8,128)(2,1)S(1)}, u32[]{:S(2)}, u32[]{:S(2)}) collective-permute-start(bf16[1024,128]{1,0:T(8,128)(2,1)S(1)} %broadcast_select_fusion.12), channel_id=1, source_target_pairs={{0,2},{1,3},{2,0},{3,1},{4,6},{5,7},{6,4},{7,5},{8,10},{9,11},{10,... | collective-permute-start | bytes 786440 | tf_op jit(solution)/shard_map/ppermute | solution.py:65
  47.6 10.8 %collective-permute-start.9 = (bf16[1024,128]{1,0:T(8,128)(2,1)S(1)}, bf16[1024,128]{1,0:T(8,128)(2,1)S(1)}, u32[]{:S(2)}, u32[]{:S(2)}) collective-permute-start(bf16[1024,128]{1,0:T(8,128)(2,1)S(1)} %broadcast_select_fusion.13), channel_id=1, source_target_pairs={{0,4},{1,5},{2,6},{3,7},{4,0},{5,1},{6,2},{7,3},{8,12},{9,13},{10,... | collective-permute-start | bytes 786440 | tf_op jit(solution)/shard_map/ppermute | solution.py:68
  48.1 13.1 %collective-permute-start.10 = (bf16[1024,128]{1,0:T(8,128)(2,1)S(1)}, bf16[1024,128]{1,0:T(8,128)(2,1)S(1)}, u32[]{:S(2)}, u32[]{:S(2)}) collective-permute-start(bf16[1024,128]{1,0:T(8,128)(2,1)S(1)} %get-tuple-element.129), channel_id=1, source_target_pairs={{0,8},{1,9},{2,10},{3,11},{4,12},{5,13},{6,14},{7,15},{8,0},{9,1},... | collective-permute-start | bytes 786440 | tf_op jit(solution)/shard_map/ppermute | solution.py:77
  53.8 13.7 %collective-permute-start.14 = (f32[1024,128]{1,0:T(8,128)S(1)}, f32[1024,128]{1,0:T(8,128)S(1)}, u32[]{:S(2)}, u32[]{:S(2)}) collective-permute-start(f32[1024,128]{1,0:T(8,128)S(1)} %convolution_add_fusion.5), channel_id=1, source_target_pairs={{0,2},{1,3},{2,0},{3,1},{4,6},{5,7},{6,4},{7,5},{8,10},{9,11},{10,... | collective-permute-start | bytes 1572872 | tf_op jit(solution)/shard_map/ppermute | solution.py:65
  61.4 16.8 %collective-permute-start.12 = (bf16[1024,256]{1,0:T(8,128)(2,1)S(1)}, bf16[1024,256]{1,0:T(8,128)(2,1)S(1)}, u32[]{:S(2)}, u32[]{:S(2)}) collective-permute-start(bf16[1024,256]{1,0:T(8,128)(2,1)S(1)} %maximum_select_fusion), channel_id=1, source_target_pairs={{0,4},{1,5},{2,6},{3,7},{4,0},{5,1},{6,2},{7,3},{8,12},{9,13},{10,... | collective-permute-start | bytes 1572872 | tf_op jit(solution)/shard_map/ppermute | solution.py:68
  62.2 17.5 %collective-permute-start.13 = (bf16[1024,128]{1,0:T(8,128)(2,1)S(1)}, bf16[1024,128]{1,0:T(8,128)(2,1)S(1)}, u32[]{:S(2)}, u32[]{:S(2)}) collective-permute-start(bf16[1024,128]{1,0:T(8,128)(2,1)S(1)} %broadcast_select_fusion.11), channel_id=1, source_target_pairs={{0,8},{1,9},{2,10},{3,11},{4,12},{5,13},{6,14},{7,15},{8,0},{9,1},... | collective-permute-start | bytes 786440 | tf_op jit(solution)/shard_map/ppermute | solution.py:77
  64.2 32.3 %collective-permute-start.18 = (bf16[1536,128]{1,0:T(8,128)(2,1)S(1)}, bf16[1536,128]{1,0:T(8,128)(2,1)S(1)}, u32[]{:S(2)}, u32[]{:S(2)}) collective-permute-start(bf16[1536,128]{1,0:T(8,128)(2,1)S(1)} %pad_maximum_fusion.7), channel_id=1, source_target_pairs={{0,8},{1,9},{4,12},{5,13},{10,2},{11,3},{14,6},{15,7},{16,24},{17,... | collective-permute-start | bytes 1179656 | tf_op jit(solution)/shard_map/ppermute | solution.py:74
  67.6 13.4 %collective-permute-start.16 = (f32[1024,128]{1,0:T(8,128)S(1)}, f32[1024,128]{1,0:T(8,128)S(1)}, u32[]{:S(2)}, u32[]{:S(2)}) collective-permute-start(f32[1024,128]{1,0:T(8,128)S(1)} %convolution_add_fusion.4), channel_id=1, source_target_pairs={{0,2},{1,3},{2,0},{3,1},{4,6},{5,7},{6,4},{7,5},{8,10},{9,11},{10,... | collective-permute-start | bytes 1572872 | tf_op jit(solution)/shard_map/ppermute | solution.py:65
  79.9 15.8 %collective-permute-start.15 = (bf16[1024,256]{1,0:T(8,128)(2,1)S(1)}, bf16[1024,256]{1,0:T(8,128)(2,1)S(1)}, u32[]{:S(2)}, u32[]{:S(2)}) collective-permute-start(bf16[1024,256]{1,0:T(8,128)(2,1)S(1)} %maximum_select_fusion.1), channel_id=1, source_target_pairs={{0,4},{1,5},{2,6},{3,7},{4,0},{5,1},{6,2},{7,3},{8,12},{9,13},{10,... | collective-permute-start | bytes 1572872 | tf_op jit(solution)/shard_map/ppermute | solution.py:68
  80.1 20.9 %collective-permute-start.21 = (bf16[1024,512]{1,0:T(8,128)(2,1)S(1)}, bf16[1024,512]{1,0:T(8,128)(2,1)S(1)}, u32[]{:S(2)}, u32[]{:S(2)}) collective-permute-start(bf16[1024,512]{1,0:T(8,128)(2,1)S(1)} %pad_maximum_fusion.2), channel_id=1, source_target_pairs={{0,1},{1,0},{2,3},{3,2},{4,5},{5,4},{6,7},{7,6},{8,9},{9,8},{10,11... | collective-permute-start | bytes 3145736 | tf_op jit(solution)/shard_map/ppermute | solution.py:71
  80.2 19.7 %collective-permute-start.23 = (bf16[1024,512]{1,0:T(8,128)(2,1)S(1)}, bf16[1024,512]{1,0:T(8,128)(2,1)S(1)}, u32[]{:S(2)}, u32[]{:S(2)}) collective-permute-start(bf16[1024,512]{1,0:T(8,128)(2,1)S(1)} %copy-done), channel_id=1, source_target_pairs={{0,1},{1,0},{2,3},{3,2},{4,5},{5,4},{6,7},{7,6},{8,9},{9,8},{10,11... | collective-permute-start | bytes 3145736 | tf_op jit(solution)/shard_map/ppermute | solution.py:71
  81.0 19.0 %collective-permute-start.17 = (f32[1024,128]{1,0:T(8,128)S(1)}, f32[1024,128]{1,0:T(8,128)S(1)}, u32[]{:S(2)}, u32[]{:S(2)}) collective-permute-start(f32[1024,128]{1,0:T(8,128)S(1)} %convolution_add_fusion.3), channel_id=1, source_target_pairs={{0,2},{1,3},{2,0},{3,1},{4,6},{5,7},{6,4},{7,5},{8,10},{9,11},{10,... | collective-permute-start | bytes 1572872 | tf_op jit(solution)/shard_map/ppermute | solution.py:65
  97.3 13.5 %collective-permute-start.19 = (bf16[1536,128]{1,0:T(8,128)(2,1)S(1)}, bf16[1536,128]{1,0:T(8,128)(2,1)S(1)}, u32[]{:S(2)}, u32[]{:S(2)}) collective-permute-start(bf16[1536,128]{1,0:T(8,128)(2,1)S(1)} %broadcast_select_fusion.8), channel_id=1, source_target_pairs={{0,4},{1,5},{2,6},{3,7},{4,0},{5,1},{6,2},{7,3},{8,12},{9,13},{10,... | collective-permute-start | bytes 1179656 | tf_op jit(solution)/shard_map/ppermute | solution.py:68
  101.0 7.5 %collective-permute-start.20 = (bf16[1024,512]{1,0:T(8,128)(2,1)S(1)}, bf16[1024,512]{1,0:T(8,128)(2,1)S(1)}, u32[]{:S(2)}, u32[]{:S(2)}) collective-permute-start(bf16[1024,512]{1,0:T(8,128)(2,1)S(1)} %get-tuple-element.101), channel_id=1, source_target_pairs={{0,1},{1,0},{2,3},{3,2},{4,5},{5,4},{6,7},{7,6},{8,9},{9,8},{10,11... | collective-permute-start | bytes 3145736 | tf_op jit(solution)/shard_map/ppermute | solution.py:71
  101.5 5.7 %collective-permute-start.22 = (bf16[1024,256]{1,0:T(8,128)(2,1)S(1)}, bf16[1024,256]{1,0:T(8,128)(2,1)S(1)}, u32[]{:S(2)}, u32[]{:S(2)}) collective-permute-start(bf16[1024,256]{1,0:T(8,128)(2,1)S(1)} %get-tuple-element.109), channel_id=1, source_target_pairs={{0,1},{1,0},{2,3},{3,2},{4,5},{5,4},{6,7},{7,6},{8,9},{9,8},{10,11... | collective-permute-start | bytes 1572872 | tf_op jit(solution)/shard_map/ppermute | solution.py:71
  102.0 15.8 %collective-permute-start.24 = (f32[1024,128]{1,0:T(8,128)S(1)}, f32[1024,128]{1,0:T(8,128)S(1)}, u32[]{:S(2)}, u32[]{:S(2)}) collective-permute-start(f32[1024,128]{1,0:T(8,128)S(1)} %convolution_add_fusion.2), channel_id=1, source_target_pairs={{0,2},{1,3},{2,0},{3,1},{4,6},{5,7},{6,4},{7,5},{8,10},{9,11},{10,... | collective-permute-start | bytes 1572872 | tf_op jit(solution)/shard_map/ppermute | solution.py:65
  111.2 2.0 %collective-permute-start.25 = (bf16[1024,256]{1,0:T(8,128)(2,1)S(1)}, bf16[1024,256]{1,0:T(8,128)(2,1)S(1)}, u32[]{:S(2)}, u32[]{:S(2)}) collective-permute-start(bf16[1024,256]{1,0:T(8,128)(2,1)S(1)} %get-tuple-element.107), channel_id=1, source_target_pairs={{0,1},{1,0},{2,3},{3,2},{4,5},{5,4},{6,7},{7,6},{8,9},{9,8},{10,11... | collective-permute-start | bytes 1572872 | tf_op jit(solution)/shard_map/ppermute | solution.py:71

commit v23 on v22

--- a/solution.py
+++ b/solution.py
@@ -93,7 +93,8 @@
         e = [columns(expected_cot, i, i + 1) for i in range(4)]
         v = [columns(value_next, i, i + 1) for i in range(4)]
         x1 = cross(jnp.where(home, v[0], e[0]))
-        rows = e[3].shape[0] // 2
+        height = e[3].shape[0]
+        rows = height * 5 // 8
         j0 = home_jump(e[3][:rows])
         t_other = swap(transition)
         e2 = after(e[2], x1, j0)
@@ -178,7 +179,7 @@
         near, far, near_top, far_top = together((a_rest, a_rest_next, a3_top, a3_top_next), grad, own01)
 
         def two_quarters(rest, top):
-            return jnp.concatenate([rest[: 2 * rows], jnp.concatenate([top, rest[2 * rows :]], 0)], 1)
+            return jnp.concatenate([rest[:height], jnp.concatenate([top, rest[height:]], 0)], 1)
 
         near, far = two_quarters(near, near_top), two_quarters(far, far_top)
         a23_own, a23_swapped = own_and_swapped(near, far)

time: 120 us -> 123 us (1.025)
  starting transfers between devices: 41.9 us -> 50 us
  waiting for transfers between devices: 50 us -> 45.3 us
    ppermute x6, starting transfers between devices: 7.56 us -> 17.4 us  [step(): return lax.ppermute(a, AXES, step_pairs)]
    ppermute x8, starting transfers between devices: 15.3 us -> 12.8 us  [cross(): return lax.ppermute(a, AXES, cross_pairs)]
    ppermute x4, waiting for transfers between devices: 3.46 us -> 1.63 us  [jump(): return lax.ppermute(a, AXES, jump_pairs)]
    ppermute x6, waiting for transfers between devices: 31.8 us -> 30.1 us  [step(): return lax.ppermute(a, AXES, step_pairs)]
where the time goes in v23:
time: 123 us
  starting transfers between devices  50 us (41%)
  waiting for transfers between devices  45.3 us (37%)
  matrix products  16 us (13%)
  other arithmetic  8.9 us (7%)
  between operations  1.81 us (1%)
    ppermute x6, waiting for transfers between devices, step(): return lax.ppermute(a, AXES, step_pairs)  30.1 us
    ppermute x6, starting transfers between devices, step(): return lax.ppermute(a, AXES, step_pairs)  17.4 us
    ppermute x8, waiting for transfers between devices, cross(): return lax.ppermute(a, AXES, cross_pairs)  13.2 us
    ppermute x8, starting transfers between devices, cross(): return lax.ppermute(a, AXES, cross_pairs)  12.8 us
    ppermute x4, starting transfers between devices, jump(): return lax.ppermute(a, AXES, jump_pairs)  10.2 us
    dot_general x12, matrix products, tdot(): lax.dot_general(a, b, (((0,), (0,)), ((), ())), preferred_element_type=jn...  9.04 us
    ppermute x2, starting transfers between devices, home_jump(): return lax.ppermute(a, AXES, home_jump_pairs)  7.77 us
    dot_general x3, matrix products, dott(): lax.dot_general(a, b, (((1,), (1,)), ((), ())), preferred_element_type=jn...  6.96 us
  transfers between devices with their start and end apart: 26, of which 11 were waited for; matrix products, arithmetic and copies ran while one was open for 20% of the time, Pallas kernels for 0%

profile of v23, /device:TPU:0, one launch (start us, length us, event | category | flops | bytes accessed | tf_op | source)
XLA Modules:
  0.0 122.8 jit_solution(6404434561220708275)
XLA Ops:
  0.6 0.5 collective-permute-start
  1.2 2.3 %fusion.36 = (bf16[1024,128]{1,0:T(8,128)(2,1)S(1)}, bf16[1024,128]{1,0:T(8,128)(2,1)}, bf16[1024,128]{1,0:T(8,128)(2,1)S(1)}, bf16[1024,128]{1,0:T(8,128)(2,1)S...) fusion(bf16[1024,512]{1,0:T(8,128)(2,1)} %param.4, ...), kind=kLoop, calls=%fused_computation.81 | loop fusion | flops 131072 | bytes 3932161 | tf_op jit(solution)/shard_map/slice | solution.py:88
  3.5 2.6 %collective-permute-start.1 = (bf16[1024,128]{1,0:T(8,128)(2,1)}, bf16[1024,128]{1,0:T(8,128)(2,1)S(1)}, u32[]{:S(2)}, u32[]{:S(2)}) collective-permute-start(bf16[1024,128]{1,0:T(8,128)(2,1)} %get-tuple-element.111), channel_id=1, source_target_pairs={{0,2},{1,3},{2,0},{3,1},{4,6},{5,7},{6,4},{7,5},{8,10},{9,11},{10,... | collective-permute-start | bytes 786440 | tf_op jit(solution)/shard_map/ppermute | solution.py:65
  6.1 4.5 %collective-permute-start.2 = (bf16[640,128]{1,0:T(8,128)(2,1)S(1)}, bf16[640,128]{1,0:T(8,128)(2,1)S(1)}, u32[]{:S(2)}, u32[]{:S(2)}) collective-permute-start(bf16[640,128]{1,0:T(8,128)(2,1)S(1)} %slice.104), channel_id=1, source_target_pairs={{0,8},{1,9},{4,12},{5,13},{10,2},{11,3},{14,6},{15,7},{16,24},{17,... | collective-permute-start | bytes 491528 | tf_op jit(solution)/shard_map/ppermute | solution.py:74
  10.6 2.5 %broadcast_select_fusion.1 = (bf16[1024,1024]{1,0:T(8,128)(2,1)S(1)}, bf16[1024,1024]{1,0:T(8,128)(2,1)S(1)}) fusion(bf16[1024,1024]{1,0:T(8,128)(2,1)} %param.6, bf16[1024,1024]{1,0:T(8,128)(2,1)} %collective-permute-done, pred[]{:T(512)S(6)} %eq.8), kind=kLoop, calls=%fused_computation.8 | loop fusion | flops 2097152 | bytes 8388609 | tf_op jit(solution)/shard_map/jit(_where)/select_n | solution.py:102
  13.3 1.8 %collective-permute-start.4 = (bf16[1024,256]{1,0:T(8,128)(2,1)S(1)}, bf16[1024,256]{1,0:T(8,128)(2,1)S(1)}, u32[]{:S(2)}, u32[]{:S(2)}) collective-permute-start(bf16[1024,256]{1,0:T(8,128)(2,1)S(1)} %pad_maximum_fusion.3), channel_id=1, source_target_pairs={{0,2},{1,3},{2,0},{3,1},{4,6},{5,7},{6,4},{7,5},{8,10},{9,11},{10,... | collective-permute-start | bytes 1572872 | tf_op jit(solution)/shard_map/ppermute | solution.py:65
  15.1 2.8 %collective-permute-start.3 = (bf16[1024,128]{1,0:T(8,128)(2,1)S(1)}, bf16[1024,128]{1,0:T(8,128)(2,1)S(1)}, u32[]{:S(2)}, u32[]{:S(2)}) collective-permute-start(bf16[1024,128]{1,0:T(8,128)(2,1)S(1)} %broadcast_select_fusion.18), channel_id=1, source_target_pairs={{0,8},{1,9},{2,10},{3,11},{4,12},{5,13},{6,14},{7,15},{8,0},{9,1},... | collective-permute-start | bytes 786440 | tf_op jit(solution)/shard_map/ppermute | solution.py:77
  18.0 10.6 %collective-permute-start.5 = (bf16[640,128]{1,0:T(8,128)(2,1)S(1)}, bf16[640,128]{1,0:T(8,128)(2,1)S(1)}, u32[]{:S(2)}, u32[]{:S(2)}) collective-permute-start(bf16[640,128]{1,0:T(8,128)(2,1)S(1)} %broadcast_select_fusion.20), channel_id=1, source_target_pairs={{0,4},{1,5},{2,6},{3,7},{4,0},{5,1},{6,2},{7,3},{8,12},{9,13},{10,... | collective-permute-start | bytes 491528 | tf_op jit(solution)/shard_map/ppermute | solution.py:68
  28.6 4.0 %collective-permute-done.5 = bf16[640,128]{1,0:T(8,128)(2,1)S(1)} collective-permute-done((bf16[640,128]{1,0:T(8,128)(2,1)S(1)}, bf16[640,128]{1,0:T(8,128)(2,1)S(1)}, u32[]{:S(2)}, u32[]{:S(2)}) %collective-permute-start.5) | collective-permute-done | bytes 163872 | tf_op jit(solution)/shard_map/ppermute | solution.py:68
  32.7 3.0 %collective-permute-start.6 = (bf16[1024,128]{1,0:T(8,128)(2,1)S(1)}, bf16[1024,128]{1,0:T(8,128)(2,1)S(1)}, u32[]{:S(2)}, u32[]{:S(2)}) collective-permute-start(bf16[1024,128]{1,0:T(8,128)(2,1)S(1)} %broadcast_select_fusion.15), channel_id=1, source_target_pairs={{0,4},{1,5},{2,6},{3,7},{4,0},{5,1},{6,2},{7,3},{8,12},{9,13},{10,... | collective-permute-start | bytes 786440 | tf_op jit(solution)/shard_map/ppermute | solution.py:68
  35.7 4.8 %collective-permute-start.7 = (bf16[1024,128]{1,0:T(8,128)(2,1)S(1)}, bf16[1024,128]{1,0:T(8,128)(2,1)S(1)}, u32[]{:S(2)}, u32[]{:S(2)}) collective-permute-start(bf16[1024,128]{1,0:T(8,128)(2,1)S(1)} %get-tuple-element.130), channel_id=1, source_target_pairs={{0,8},{1,9},{2,10},{3,11},{4,12},{5,13},{6,14},{7,15},{8,0},{9,1},... | collective-permute-start | bytes 786440 | tf_op jit(solution)/shard_map/ppermute | solution.py:77
  40.5 0.1 collective-permute-start.8
  40.6 5.1 %collective-permute-done.6 = bf16[1024,128]{1,0:T(8,128)(2,1)S(1)} collective-permute-done((bf16[1024,128]{1,0:T(8,128)(2,1)S(1)}, bf16[1024,128]{1,0:T(8,128)(2,1)S(1)}, u32[]{:S(2)}, u32[]{:S(2)}) %collective-permute-start.6) | collective-permute-done | bytes 262176 | tf_op jit(solution)/shard_map/ppermute | solution.py:68
  45.7 0.7 fusion.43
  46.4 0.8 convolution_add_fusion.5
  47.2 5.9 %collective-permute-done.8 = bf16[1024,256]{1,0:T(8,128)(2,1)S(1)} collective-permute-done((bf16[1024,256]{1,0:T(8,128)(2,1)S(1)}, bf16[1024,256]{1,0:T(8,128)(2,1)S(1)}, u32[]{:S(2)}, u32[]{:S(2)}) %collective-permute-start.8) | collective-permute-done | bytes 524320 | tf_op jit(solution)/shard_map/ppermute | solution.py:65
  53.2 0.4 collective-permute-start.11
  53.6 0.5 collective-permute-start.9
  54.2 0.8 collective-permute-start.10
  55.0 5.4 %collective-permute-done.11 = bf16[1024,128]{1,0:T(8,128)(2,1)S(1)} collective-permute-done((bf16[1024,128]{1,0:T(8,128)(2,1)S(1)}, bf16[1024,128]{1,0:T(8,128)(2,1)S(1)}, u32[]{:S(2)}, u32[]{:S(2)}) %collective-permute-start.11) | collective-permute-done | bytes 262176 | tf_op jit(solution)/shard_map/ppermute | solution.py:65
  60.4 3.3 %collective-permute-done.9 = bf16[1024,128]{1,0:T(8,128)(2,1)S(1)} collective-permute-done((bf16[1024,128]{1,0:T(8,128)(2,1)S(1)}, bf16[1024,128]{1,0:T(8,128)(2,1)S(1)}, u32[]{:S(2)}, u32[]{:S(2)}) %collective-permute-start.9) | collective-permute-done | bytes 262176 | tf_op jit(solution)/shard_map/ppermute | solution.py:68
  63.7 0.7 fusion.44
  64.4 0.8 convolution_add_fusion.4
  65.3 1.6 %collective-permute-done.10 = bf16[1024,128]{1,0:T(8,128)(2,1)S(1)} collective-permute-done((bf16[1024,128]{1,0:T(8,128)(2,1)S(1)}, bf16[1024,128]{1,0:T(8,128)(2,1)S(1)}, u32[]{:S(2)}, u32[]{:S(2)}) %collective-permute-start.10) | collective-permute-done | bytes 262176 | tf_op jit(solution)/shard_map/ppermute | solution.py:77
  66.9 0.2 maximum_select_fusion
  67.9 1.8 %collective-permute-start.13 = (bf16[1024,128]{1,0:T(8,128)(2,1)S(1)}, bf16[1024,128]{1,0:T(8,128)(2,1)S(1)}, u32[]{:S(2)}, u32[]{:S(2)}) collective-permute-start(bf16[1024,128]{1,0:T(8,128)(2,1)S(1)} %broadcast_select_fusion.11), channel_id=1, source_target_pairs={{0,8},{1,9},{2,10},{3,11},{4,12},{5,13},{6,14},{7,15},{8,0},{9,1},... | collective-permute-start | bytes 786440 | tf_op jit(solution)/shard_map/ppermute | solution.py:77
  69.7 3.3 %collective-permute-start.18 = (bf16[1408,128]{1,0:T(8,128)(2,1)S(1)}, bf16[1408,128]{1,0:T(8,128)(2,1)S(1)}, u32[]{:S(2)}, u32[]{:S(2)}) collective-permute-start(bf16[1408,128]{1,0:T(8,128)(2,1)S(1)} %pad_maximum_fusion.7), channel_id=1, source_target_pairs={{0,8},{1,9},{4,12},{5,13},{10,2},{11,3},{14,6},{15,7},{16,24},{17,... | collective-permute-start | bytes 1081352 | tf_op jit(solution)/shard_map/ppermute | solution.py:74
  73.0 0.1 constant_dynamic-update-slice_fusion.4
  73.0 0.1 constant_dynamic-update-slice_fusion.3
  73.3 10.4 %collective-permute-done.12 = bf16[1024,256]{1,0:T(8,128)(2,1)S(1)} collective-permute-done((bf16[1024,256]{1,0:T(8,128)(2,1)S(1)}, bf16[1024,256]{1,0:T(8,128)(2,1)S(1)}, u32[]{:S(2)}, u32[]{:S(2)}) %collective-permute-start.12) | collective-permute-done | bytes 524320 | tf_op jit(solution)/shard_map/ppermute | solution.py:68
  83.6 0.8 fusion.21
  84.4 0.8 convolution_add_fusion.3
  85.2 0.2 maximum_select_fusion.1
  85.4 0.7 collective-permute-start.15
  86.1 0.1 pad_maximum_fusion.2
  86.2 0.1 collective-permute-start.21
  86.2 0.5 collective-permute-start.23
  86.7 0.1 constant_dynamic-update-slice_fusion.2
  86.8 0.1 constant_dynamic-update-slice_fusion.1
  87.0 5.0 %collective-permute-start.17 = (f32[1024,128]{1,0:T(8,128)S(1)}, f32[1024,128]{1,0:T(8,128)S(1)}, u32[]{:S(2)}, u32[]{:S(2)}) collective-permute-start(f32[1024,128]{1,0:T(8,128)S(1)} %convolution_add_fusion.3), channel_id=1, source_target_pairs={{0,2},{1,3},{2,0},{3,1},{4,6},{5,7},{6,4},{7,5},{8,10},{9,11},{10,... | collective-permute-start | bytes 1572872 | tf_op jit(solution)/shard_map/ppermute | solution.py:65
  92.0 7.3 %collective-permute-done.15 = bf16[1024,256]{1,0:T(8,128)(2,1)S(1)} collective-permute-done((bf16[1024,256]{1,0:T(8,128)(2,1)S(1)}, bf16[1024,256]{1,0:T(8,128)(2,1)S(1)}, u32[]{:S(2)}, u32[]{:S(2)}) %collective-permute-start.15) | collective-permute-done | bytes 524320 | tf_op jit(solution)/shard_map/ppermute | solution.py:68
  99.3 0.8 fusion.30
  100.2 0.8 convolution_add_fusion.2
  100.9 2.6 %collective-permute-start.19 = (bf16[1408,128]{1,0:T(8,128)(2,1)S(1)}, bf16[1408,128]{1,0:T(8,128)(2,1)S(1)}, u32[]{:S(2)}, u32[]{:S(2)}) collective-permute-start(bf16[1408,128]{1,0:T(8,128)(2,1)S(1)} %broadcast_select_fusion.8), channel_id=1, source_target_pairs={{0,4},{1,5},{2,6},{3,7},{4,0},{5,1},{6,2},{7,3},{8,12},{9,13},{10,... | collective-permute-start | bytes 1081352 | tf_op jit(solution)/shard_map/ppermute | solution.py:68
  103.7 0.5 collective-permute-done.17
  104.2 0.2 fusion.37
  104.4 0.8 broadcast_select_fusion.3
  105.1 0.1 collective-permute-start.20
  105.2 0.1 constant_dynamic-update-slice_fusion
  105.4 0.2 broadcast_select_fusion.7
  105.6 0.6 collective-permute-start.22
  106.2 2.8 %collective-permute-start.24 = (f32[1024,128]{1,0:T(8,128)S(1)}, f32[1024,128]{1,0:T(8,128)S(1)}, u32[]{:S(2)}, u32[]{:S(2)}) collective-permute-start(f32[1024,128]{1,0:T(8,128)S(1)} %convolution_add_fusion.2), channel_id=1, source_target_pairs={{0,2},{1,3},{2,0},{3,1},{4,6},{5,7},{6,4},{7,5},{8,10},{9,11},{10,... | collective-permute-start | bytes 1572872 | tf_op jit(solution)/shard_map/ppermute | solution.py:65
  109.0 0.7 fusion.24
  109.7 0.7 convolution_add_fusion.1
  110.5 1.3 %fusion.8 = f32[1024,1024]{1,0:T(8,128)S(1)} fusion(bf16[1024,256]{1,0:T(8,128)(2,1)S(1)} %collective-permute-done.22, bf16[1024,256]{1,0:T(8,128)(2,1)S(1)} %get-tuple-element.108, bf16[1024,256]{1,0:T(8,128)(2,1)S(1)} %get-tuple-element.105, bf16[1024,256]{1,0:T(8,128)(2,1)S(1)} %get-tuple-element.103), kind=kOutput, calls=%fused_computation.19 | convolution fusion | flops 1077936128 | bytes 6291456 | tf_op jit(solution)/shard_map/dot_general | solution.py:38
  111.8 2.4 %fusion.5 = f32[1024,1024]{1,0:T(8,128)S(1)} fusion(f32[1024,1024]{1,0:T(8,128)S(1)} %fusion.8, bf16[1024,1024]{1,0:T(8,128)(2,1)S(1)} %constant_dynamic-update-slice_fusion, bf16[1024,512]{1,0:T(8,128)(2,1)S(1)} %collective-permute-done.20, bf16[1024,512]{1,0:T(8,128)(2,1)S(1)} %get-tuple-element.100), kind=kOutput, calls=%fused_computation.9 | convolution fusion | flops 2152726528 | bytes 12582912 | tf_op jit(solution)/shard_map/dot_general | solution.py:38
  114.3 0.3 broadcast_select_fusion.5
  114.5 0.1 collective-permute-start.25
  114.6 0.7 fusion.33
  115.4 0.8 convolution_add_fusion
  116.1 0.4 collective-permute-done.25
  116.5 3.3 %add_multiply_fusion = f32[1024,1024]{1,0:T(8,128)} fusion(f32[1024,1024]{1,0:T(8,128)S(1)} %fusion.5, f32[]{:T(128)} %bitcast, bf16[1024,256]{1,0:T(8,128)(2,1)S(1)} %collective-permute-done.25, bf16[1024,256]{1,0:T(8,128)(2,1)S(1)} %get-tuple-element.106, bf16[1024,256]{1,0:T(8,128)(2,1)S(1)} %get-tuple-element.104, bf16[1024,256]{1,0:T(8,128)(2,1)S(1)} %get-tuple-element.102), kind=kOutput, calls=%fused_computation | convolution fusion | flops 1080033280 | bytes 10485764 | tf_op jit(solution)/shard_map/dot_general | solution.py:38
  119.8 1.3 %collective-permute-done.24 = f32[1024,128]{1,0:T(8,128)S(1)} collective-permute-done((f32[1024,128]{1,0:T(8,128)S(1)}, f32[1024,128]{1,0:T(8,128)S(1)}, u32[]{:S(2)}, u32[]{:S(2)}) %collective-permute-start.24) | collective-permute-done | bytes 524320 | tf_op jit(solution)/shard_map/ppermute | solution.py:65
  121.2 1.6 %fusion.4 = f32[1024,512]{1,0:T(8,128)} fusion(f32[1024,256]{1,0:T(8,128)S(1)} %convolution_add_fusion, f32[1024,256]{1,0:T(8,128)S(1)} %convolution_add_fusion.1, f32[1024,128]{1,0:T(8,128)S(1)} %collective-permute-done.24, f32[1024,128]{1,0:T(8,128)S(1)} %collective-permute-done.17, f32[1024,128]{1,0:T(8,128)S(1)} %collective-permute-done.16, ...), kind=kLoop, calls=%fused_computation.6 | loop fusion | flops 3145728 | bytes 6291460 | tf_op jit(solution)/shard_map/mul | solution.py:192
  (46 shorter events, 1.0 us)
Async XLA Ops:
  0.6 5.4 %copy-start.1 = (bf16[1024,512]{1,0:T(8,128)(2,1)S(1)}, bf16[1024,512]{1,0:T(8,128)(2,1)}, u32[]{:S(2)}) copy-start(bf16[1024,512]{1,0:T(8,128)(2,1)} %param.4) | copy-start | bytes 3145732
  0.6 10.0 %collective-permute-start = (bf16[1024,1024]{1,0:T(8,128)(2,1)}, bf16[1024,1024]{1,0:T(8,128)(2,1)}, u32[]{:S(2)}, u32[]{:S(2)}) collective-permute-start(bf16[1024,1024]{1,0:T(8,128)(2,1)} %param.6), channel_id=1, source_target_pairs={{0,1},{1,0},{2,3},{3,2},{4,5},{5,4},{6,7},{7,6},{8,9},{9,8},{10,11... | collective-permute-start | bytes 6291464 | tf_op jit(solution)/shard_map/ppermute | solution.py:71
  3.5 9.7 %collective-permute-start.1 = (bf16[1024,128]{1,0:T(8,128)(2,1)}, bf16[1024,128]{1,0:T(8,128)(2,1)S(1)}, u32[]{:S(2)}, u32[]{:S(2)}) collective-permute-start(bf16[1024,128]{1,0:T(8,128)(2,1)} %get-tuple-element.111), channel_id=1, source_target_pairs={{0,2},{1,3},{2,0},{3,1},{4,6},{5,7},{6,4},{7,5},{8,10},{9,11},{10,... | collective-permute-start | bytes 786440 | tf_op jit(solution)/shard_map/ppermute | solution.py:65
  6.1 9.0 %collective-permute-start.2 = (bf16[640,128]{1,0:T(8,128)(2,1)S(1)}, bf16[640,128]{1,0:T(8,128)(2,1)S(1)}, u32[]{:S(2)}, u32[]{:S(2)}) collective-permute-start(bf16[640,128]{1,0:T(8,128)(2,1)S(1)} %slice.104), channel_id=1, source_target_pairs={{0,8},{1,9},{4,12},{5,13},{10,2},{11,3},{14,6},{15,7},{16,24},{17,... | collective-permute-start | bytes 491528 | tf_op jit(solution)/shard_map/ppermute | solution.py:74
  13.3 15.3 %collective-permute-start.4 = (bf16[1024,256]{1,0:T(8,128)(2,1)S(1)}, bf16[1024,256]{1,0:T(8,128)(2,1)S(1)}, u32[]{:S(2)}, u32[]{:S(2)}) collective-permute-start(bf16[1024,256]{1,0:T(8,128)(2,1)S(1)} %pad_maximum_fusion.3), channel_id=1, source_target_pairs={{0,2},{1,3},{2,0},{3,1},{4,6},{5,7},{6,4},{7,5},{8,10},{9,11},{10,... | collective-permute-start | bytes 1572872 | tf_op jit(solution)/shard_map/ppermute | solution.py:65
  15.1 13.5 %collective-permute-start.3 = (bf16[1024,128]{1,0:T(8,128)(2,1)S(1)}, bf16[1024,128]{1,0:T(8,128)(2,1)S(1)}, u32[]{:S(2)}, u32[]{:S(2)}) collective-permute-start(bf16[1024,128]{1,0:T(8,128)(2,1)S(1)} %broadcast_select_fusion.18), channel_id=1, source_target_pairs={{0,8},{1,9},{2,10},{3,11},{4,12},{5,13},{6,14},{7,15},{8,0},{9,1},... | collective-permute-start | bytes 786440 | tf_op jit(solution)/shard_map/ppermute | solution.py:77
  18.0 14.7 %collective-permute-start.5 = (bf16[640,128]{1,0:T(8,128)(2,1)S(1)}, bf16[640,128]{1,0:T(8,128)(2,1)S(1)}, u32[]{:S(2)}, u32[]{:S(2)}) collective-permute-start(bf16[640,128]{1,0:T(8,128)(2,1)S(1)} %broadcast_select_fusion.20), channel_id=1, source_target_pairs={{0,4},{1,5},{2,6},{3,7},{4,0},{5,1},{6,2},{7,3},{8,12},{9,13},{10,... | collective-permute-start | bytes 491528 | tf_op jit(solution)/shard_map/ppermute | solution.py:68
  32.7 13.0 %collective-permute-start.6 = (bf16[1024,128]{1,0:T(8,128)(2,1)S(1)}, bf16[1024,128]{1,0:T(8,128)(2,1)S(1)}, u32[]{:S(2)}, u32[]{:S(2)}) collective-permute-start(bf16[1024,128]{1,0:T(8,128)(2,1)S(1)} %broadcast_select_fusion.15), channel_id=1, source_target_pairs={{0,4},{1,5},{2,6},{3,7},{4,0},{5,1},{6,2},{7,3},{8,12},{9,13},{10,... | collective-permute-start | bytes 786440 | tf_op jit(solution)/shard_map/ppermute | solution.py:68
  35.7 17.5 %collective-permute-start.7 = (bf16[1024,128]{1,0:T(8,128)(2,1)S(1)}, bf16[1024,128]{1,0:T(8,128)(2,1)S(1)}, u32[]{:S(2)}, u32[]{:S(2)}) collective-permute-start(bf16[1024,128]{1,0:T(8,128)(2,1)S(1)} %get-tuple-element.130), channel_id=1, source_target_pairs={{0,8},{1,9},{2,10},{3,11},{4,12},{5,13},{6,14},{7,15},{8,0},{9,1},... | collective-permute-start | bytes 786440 | tf_op jit(solution)/shard_map/ppermute | solution.py:77
  40.5 12.6 %collective-permute-start.8 = (bf16[1024,256]{1,0:T(8,128)(2,1)S(1)}, bf16[1024,256]{1,0:T(8,128)(2,1)S(1)}, u32[]{:S(2)}, u32[]{:S(2)}) collective-permute-start(bf16[1024,256]{1,0:T(8,128)(2,1)S(1)} %pad_maximum_fusion.4), channel_id=1, source_target_pairs={{0,2},{1,3},{2,0},{3,1},{4,6},{5,7},{6,4},{7,5},{8,10},{9,11},{10,... | collective-permute-start | bytes 1572872 | tf_op jit(solution)/shard_map/ppermute | solution.py:65
  47.2 7.0 %copy-start = (bf16[1024,512]{1,0:T(8,128)(2,1)S(1)}, bf16[1024,512]{1,0:T(8,128)(2,1)}, u32[]{:S(2)}) copy-start(bf16[1024,512]{1,0:T(8,128)(2,1)} %param.5) | copy-start | bytes 3145732
  53.2 7.2 %collective-permute-start.11 = (bf16[1024,128]{1,0:T(8,128)(2,1)S(1)}, bf16[1024,128]{1,0:T(8,128)(2,1)S(1)}, u32[]{:S(2)}, u32[]{:S(2)}) collective-permute-start(bf16[1024,128]{1,0:T(8,128)(2,1)S(1)} %broadcast_select_fusion.12), channel_id=1, source_target_pairs={{0,2},{1,3},{2,0},{3,1},{4,6},{5,7},{6,4},{7,5},{8,10},{9,11},{10,... | collective-permute-start | bytes 786440 | tf_op jit(solution)/shard_map/ppermute | solution.py:65
  53.6 10.1 %collective-permute-start.9 = (bf16[1024,128]{1,0:T(8,128)(2,1)S(1)}, bf16[1024,128]{1,0:T(8,128)(2,1)S(1)}, u32[]{:S(2)}, u32[]{:S(2)}) collective-permute-start(bf16[1024,128]{1,0:T(8,128)(2,1)S(1)} %broadcast_select_fusion.13), channel_id=1, source_target_pairs={{0,4},{1,5},{2,6},{3,7},{4,0},{5,1},{6,2},{7,3},{8,12},{9,13},{10,... | collective-permute-start | bytes 786440 | tf_op jit(solution)/shard_map/ppermute | solution.py:68
  54.2 12.7 %collective-permute-start.10 = (bf16[1024,128]{1,0:T(8,128)(2,1)S(1)}, bf16[1024,128]{1,0:T(8,128)(2,1)S(1)}, u32[]{:S(2)}, u32[]{:S(2)}) collective-permute-start(bf16[1024,128]{1,0:T(8,128)(2,1)S(1)} %get-tuple-element.127), channel_id=1, source_target_pairs={{0,8},{1,9},{2,10},{3,11},{4,12},{5,13},{6,14},{7,15},{8,0},{9,1},... | collective-permute-start | bytes 786440 | tf_op jit(solution)/shard_map/ppermute | solution.py:77
  60.4 12.8 %collective-permute-start.14 = (f32[1024,128]{1,0:T(8,128)S(1)}, f32[1024,128]{1,0:T(8,128)S(1)}, u32[]{:S(2)}, u32[]{:S(2)}) collective-permute-start(f32[1024,128]{1,0:T(8,128)S(1)} %convolution_add_fusion.5), channel_id=1, source_target_pairs={{0,2},{1,3},{2,0},{3,1},{4,6},{5,7},{6,4},{7,5},{8,10},{9,11},{10,... | collective-permute-start | bytes 1572872 | tf_op jit(solution)/shard_map/ppermute | solution.py:65
  67.1 16.6 %collective-permute-start.12 = (bf16[1024,256]{1,0:T(8,128)(2,1)S(1)}, bf16[1024,256]{1,0:T(8,128)(2,1)S(1)}, u32[]{:S(2)}, u32[]{:S(2)}) collective-permute-start(bf16[1024,256]{1,0:T(8,128)(2,1)S(1)} %maximum_select_fusion), channel_id=1, source_target_pairs={{0,4},{1,5},{2,6},{3,7},{4,0},{5,1},{6,2},{7,3},{8,12},{9,13},{10,... | collective-permute-start | bytes 1572872 | tf_op jit(solution)/shard_map/ppermute | solution.py:68
  67.9 17.3 %collective-permute-start.13 = (bf16[1024,128]{1,0:T(8,128)(2,1)S(1)}, bf16[1024,128]{1,0:T(8,128)(2,1)S(1)}, u32[]{:S(2)}, u32[]{:S(2)}) collective-permute-start(bf16[1024,128]{1,0:T(8,128)(2,1)S(1)} %broadcast_select_fusion.11), channel_id=1, source_target_pairs={{0,8},{1,9},{2,10},{3,11},{4,12},{5,13},{6,14},{7,15},{8,0},{9,1},... | collective-permute-start | bytes 786440 | tf_op jit(solution)/shard_map/ppermute | solution.py:77
  69.7 30.4 %collective-permute-start.18 = (bf16[1408,128]{1,0:T(8,128)(2,1)S(1)}, bf16[1408,128]{1,0:T(8,128)(2,1)S(1)}, u32[]{:S(2)}, u32[]{:S(2)}) collective-permute-start(bf16[1408,128]{1,0:T(8,128)(2,1)S(1)} %pad_maximum_fusion.7), channel_id=1, source_target_pairs={{0,8},{1,9},{4,12},{5,13},{10,2},{11,3},{14,6},{15,7},{16,24},{17,... | collective-permute-start | bytes 1081352 | tf_op jit(solution)/shard_map/ppermute | solution.py:74
  73.2 13.8 %collective-permute-start.16 = (f32[1024,128]{1,0:T(8,128)S(1)}, f32[1024,128]{1,0:T(8,128)S(1)}, u32[]{:S(2)}, u32[]{:S(2)}) collective-permute-start(f32[1024,128]{1,0:T(8,128)S(1)} %convolution_add_fusion.4), channel_id=1, source_target_pairs={{0,2},{1,3},{2,0},{3,1},{4,6},{5,7},{6,4},{7,5},{8,10},{9,11},{10,... | collective-permute-start | bytes 1572872 | tf_op jit(solution)/shard_map/ppermute | solution.py:65
  85.4 14.0 %collective-permute-start.15 = (bf16[1024,256]{1,0:T(8,128)(2,1)S(1)}, bf16[1024,256]{1,0:T(8,128)(2,1)S(1)}, u32[]{:S(2)}, u32[]{:S(2)}) collective-permute-start(bf16[1024,256]{1,0:T(8,128)(2,1)S(1)} %maximum_select_fusion.1), channel_id=1, source_target_pairs={{0,4},{1,5},{2,6},{3,7},{4,0},{5,1},{6,2},{7,3},{8,12},{9,13},{10,... | collective-permute-start | bytes 1572872 | tf_op jit(solution)/shard_map/ppermute | solution.py:68
  86.2 19.1 %collective-permute-start.21 = (bf16[1024,512]{1,0:T(8,128)(2,1)S(1)}, bf16[1024,512]{1,0:T(8,128)(2,1)S(1)}, u32[]{:S(2)}, u32[]{:S(2)}) collective-permute-start(bf16[1024,512]{1,0:T(8,128)(2,1)S(1)} %pad_maximum_fusion.2), channel_id=1, source_target_pairs={{0,1},{1,0},{2,3},{3,2},{4,5},{5,4},{6,7},{7,6},{8,9},{9,8},{10,11... | collective-permute-start | bytes 3145736 | tf_op jit(solution)/shard_map/ppermute | solution.py:71
  86.2 17.3 %collective-permute-start.23 = (bf16[1024,512]{1,0:T(8,128)(2,1)S(1)}, bf16[1024,512]{1,0:T(8,128)(2,1)S(1)}, u32[]{:S(2)}, u32[]{:S(2)}) collective-permute-start(bf16[1024,512]{1,0:T(8,128)(2,1)S(1)} %copy-done), channel_id=1, source_target_pairs={{0,1},{1,0},{2,3},{3,2},{4,5},{5,4},{6,7},{7,6},{8,9},{9,8},{10,11... | collective-permute-start | bytes 3145736 | tf_op jit(solution)/shard_map/ppermute | solution.py:71
  87.0 17.2 %collective-permute-start.17 = (f32[1024,128]{1,0:T(8,128)S(1)}, f32[1024,128]{1,0:T(8,128)S(1)}, u32[]{:S(2)}, u32[]{:S(2)}) collective-permute-start(f32[1024,128]{1,0:T(8,128)S(1)} %convolution_add_fusion.3), channel_id=1, source_target_pairs={{0,2},{1,3},{2,0},{3,1},{4,6},{5,7},{6,4},{7,5},{8,10},{9,11},{10,... | collective-permute-start | bytes 1572872 | tf_op jit(solution)/shard_map/ppermute | solution.py:65
  100.9 13.2 %collective-permute-start.19 = (bf16[1408,128]{1,0:T(8,128)(2,1)S(1)}, bf16[1408,128]{1,0:T(8,128)(2,1)S(1)}, u32[]{:S(2)}, u32[]{:S(2)}) collective-permute-start(bf16[1408,128]{1,0:T(8,128)(2,1)S(1)} %broadcast_select_fusion.8), channel_id=1, source_target_pairs={{0,4},{1,5},{2,6},{3,7},{4,0},{5,1},{6,2},{7,3},{8,12},{9,13},{10,... | collective-permute-start | bytes 1081352 | tf_op jit(solution)/shard_map/ppermute | solution.py:68
  105.1 6.7 %collective-permute-start.20 = (bf16[1024,512]{1,0:T(8,128)(2,1)S(1)}, bf16[1024,512]{1,0:T(8,128)(2,1)S(1)}, u32[]{:S(2)}, u32[]{:S(2)}) collective-permute-start(bf16[1024,512]{1,0:T(8,128)(2,1)S(1)} %get-tuple-element.101), channel_id=1, source_target_pairs={{0,1},{1,0},{2,3},{3,2},{4,5},{5,4},{6,7},{7,6},{8,9},{9,8},{10,11... | collective-permute-start | bytes 3145736 | tf_op jit(solution)/shard_map/ppermute | solution.py:71
  105.6 4.9 %collective-permute-start.22 = (bf16[1024,256]{1,0:T(8,128)(2,1)S(1)}, bf16[1024,256]{1,0:T(8,128)(2,1)S(1)}, u32[]{:S(2)}, u32[]{:S(2)}) collective-permute-start(bf16[1024,256]{1,0:T(8,128)(2,1)S(1)} %get-tuple-element.109), channel_id=1, source_target_pairs={{0,1},{1,0},{2,3},{3,2},{4,5},{5,4},{6,7},{7,6},{8,9},{9,8},{10,11... | collective-permute-start | bytes 1572872 | tf_op jit(solution)/shard_map/ppermute | solution.py:71
  106.2 15.0 %collective-permute-start.24 = (f32[1024,128]{1,0:T(8,128)S(1)}, f32[1024,128]{1,0:T(8,128)S(1)}, u32[]{:S(2)}, u32[]{:S(2)}) collective-permute-start(f32[1024,128]{1,0:T(8,128)S(1)} %convolution_add_fusion.2), channel_id=1, source_target_pairs={{0,2},{1,3},{2,0},{3,1},{4,6},{5,7},{6,4},{7,5},{8,10},{9,11},{10,... | collective-permute-start | bytes 1572872 | tf_op jit(solution)/shard_map/ppermute | solution.py:65
  114.5 2.0 %collective-permute-start.25 = (bf16[1024,256]{1,0:T(8,128)(2,1)S(1)}, bf16[1024,256]{1,0:T(8,128)(2,1)S(1)}, u32[]{:S(2)}, u32[]{:S(2)}) collective-permute-start(bf16[1024,256]{1,0:T(8,128)(2,1)S(1)} %get-tuple-element.107), channel_id=1, source_target_pairs={{0,1},{1,0},{2,3},{3,2},{4,5},{5,4},{6,7},{7,6},{8,9},{9,8},{10,11... | collective-permute-start | bytes 1572872 | tf_op jit(solution)/shard_map/ppermute | solution.py:71
